TPU v7x, 32 devices: a whole 2x2x4 slice. The times are simulated.
32 devices in a mesh: grp: 2 (over x), seq: 16 (over z, y, core).
Axes of the slice: x: 2, y: 2, z: 4, core: 2. Of those that a mesh axis runs over, the one named last changes fastest.
Arguments:
- frames: bfloat16 [4096, 2048], P(('grp', 'seq')), parts along dimension 0
- conv_weight: bfloat16 [4, 2048], replicated, may hold values from -2.390625 to 2.390625
- qkv_weight: bfloat16 [2048, 3072], P(None, 'seq'), may hold values from -0.125 to 0.125
- track_ids: int32 [4096], P(('grp', 'seq')), parts along dimension 0, may hold values from 0 to 63, as said below
- track_owner: int32 [128], P('grp'), parts along dimension 0, may hold values from 0 to 15, as said below
Outputs:
- context: bfloat16 [4096, 1024], P(('grp', 'seq')), parts along dimension 0
There are 2 independent parts, one for each index of `grp`. A program takes and returns all parts, laid end to end along the dimension named above; an argument that names none is the same for every part. Nothing has to cross between parts.
Inputs may be any that keep to these rules, and one draw needn't show every extreme that they name: `track_ids`: counting each token by track_owner of its track, the tokens of one device fall on each owning device at most 16 times, and one owning device receives exactly 16 tokens from every device. `track_owner`: every device owns exactly 4 tracks.
All inputs are finite; a program needn't handle non-finite values.
Results may differ from a plain program's by a relative error of at most 0.005.
The roundings to bfloat16 on the way count: a program that leaves them out, or rounds other values in their place, can miss the bound.
Values may be sent and summed in bfloat16 or wider, within the bound.
No kernel may reach another device: no remote copies, remote signals or barrier semaphores. Data moves between devices by JAX's collectives and lax.ppermute only.
A program may use at most 64 MiB of HBM per device.

v0:
```python
import jax
import jax.numpy as jnp
from jax import lax
from jax.sharding import PartitionSpec as P

HD = 128
KW = 4


def from_behind(value, axis, by):
    size = lax.axis_size(axis)
    pairs = [(i, i + by) for i in range(size) if 0 <= i + by < size]
    return lax.ppermute(value, axis, pairs)


def attend_slots(packed, positions):
    slot_count = packed.shape[0]
    inner = packed.shape[1] // 3
    head_count = inner // HD
    query = packed[:, :inner].reshape(slot_count, head_count, HD)
    keys_all = packed[:, inner : 2 * inner].reshape(slot_count, head_count, HD)
    values_all = packed[:, 2 * inner :].reshape(slot_count, head_count, HD)
    slot_ids = jnp.arange(slot_count, dtype=jnp.int32)
    score_scale = 1.0 / HD**0.5

    def one_block(block_id):
        offset = block_id * slot_count
        ids_block = offset + jnp.arange(slot_count, dtype=jnp.int32)
        scores = (
            jnp.einsum("qhd,khd->hqk", query, keys_all, preferred_element_type=jnp.float32)
            * score_scale
        )
        allowed = (positions[None, :] >= 0) & (positions[None, :] <= positions[:, None]) | (
            ids_block[:, None] == slot_ids[None, :]
        )
        scores = jnp.where(allowed[None], scores, jnp.float32(-1e30))
        top_score = jnp.max(scores, axis=-1, keepdims=True)
        expd = jnp.exp(scores - top_score)
        weights = (expd / jnp.sum(expd, axis=-1, keepdims=True)).astype(jnp.bfloat16)
        mixed = jnp.einsum("hqk,khd->qhd", weights, values_all, preferred_element_type=jnp.float32)
        return mixed.astype(jnp.bfloat16).reshape(slot_count, inner)

    blocks = lax.map(one_block, jnp.arange(slot_count // slot_count, dtype=jnp.int32))
    return blocks.reshape(slot_count, inner)


def body(frames, conv_weight, qkv_weight, track_ids, track_owner):
    tok_rows = frames.shape[0]
    peer_count = lax.axis_size("seq")
    capacity = 2 * tok_rows // peer_count
    slot_total = capacity * peer_count
    my_index = lax.axis_index("seq")
    rim_rows = from_behind(frames[tok_rows - (KW - 1) :], "seq", 1)
    extended = jnp.concatenate([rim_rows, frames], axis=0).astype(jnp.float32)
    conv_sum = frames.astype(jnp.float32)
    for tap in range(KW):
        conv_sum = (
            conv_sum
            + conv_weight[tap].astype(jnp.float32)[None, :]
            * extended[KW - 1 - tap : KW - 1 - tap + tok_rows]
        )
    hidden = conv_sum.astype(jnp.bfloat16)
    track_total = track_owner.shape[0]
    group = jnp.sum(
        jnp.where(
            track_ids[:, None] == jnp.arange(track_total, dtype=jnp.int32)[None, :],
            track_owner[None, :],
            0,
        ),
        axis=1,
    )
    owner_hits = (group[:, None] == jnp.arange(peer_count, dtype=jnp.int32)[None, :]).astype(
        jnp.int32
    )
    running = jnp.cumsum(owner_hits, axis=0) - 1
    rank_rows = jnp.sum(jnp.where(owner_hits > 0, running, 0), axis=1)
    slot_of_row = group * capacity + rank_rows
    row_ids = jnp.arange(tok_rows, dtype=jnp.int32)
    source_row = jnp.full((slot_total,), tok_rows, jnp.int32).at[slot_of_row].set(row_ids)
    positions = my_index * tok_rows + row_ids
    send_times = jnp.full((slot_total,), -1, jnp.int32).at[slot_of_row].set(positions)
    projected = jnp.dot(
        hidden,
        lax.all_gather(qkv_weight, "seq", axis=1, tiled=True),
        preferred_element_type=jnp.float32,
    ).astype(jnp.bfloat16)
    padded_rows = jnp.concatenate(
        [projected, jnp.zeros((1, projected.shape[1]), jnp.bfloat16)], axis=0
    )
    outgoing = padded_rows[source_row]
    received, got_times = (
        lax.all_to_all(outgoing, "seq", split_axis=0, concat_axis=0, tiled=True),
        lax.all_to_all(send_times, "seq", split_axis=0, concat_axis=0, tiled=True),
    )
    mixed = attend_slots(received, got_times)
    returned = lax.all_to_all(mixed, "seq", split_axis=0, concat_axis=0, tiled=True)
    return returned[slot_of_row]


def solution(mesh):
    in_specs = (P(("grp", "seq"), None), P(), P(None, "seq"), P(("grp", "seq")), P("grp"))
    out_specs = P(("grp", "seq"), None)
    return jax.shard_map(body, mesh=mesh, in_specs=in_specs, out_specs=out_specs, check_vma=False)
```

profile of v0, /device:TPU:0, one launch (start us, length us, event | category | flops | bytes accessed | tf_op | source)
XLA Modules:
  0.0 198.7 jit_solution(8070860922662830229)
XLA Ops:
  6.5 0.7 all-gather.2.cloned.1.call-update
  7.3 0.8 slice.37
  8.0 2.4 %collective-permute-start = (bf16[3,2048]{1,0:T(4,128)(2,1)S(1)}, bf16[3,2048]{1,0:T(4,128)(2,1)S(1)}, u32[]{:S(2)}, u32[]{:S(2)}) collective-permute-start(bf16[3,2048]{1,0:T(4,128)(2,1)S(1)} %slice.37), channel_id=1, source_target_pairs={{0,1},{1,2},{2,3},{3,4},{4,5},{5,6},{6,7},{7,8},{8,9},{9,10},{10,1... | collective-permute-start | bytes 36872 | tf_op jit(solution)/shard_map/ppermute | solution.py:13
  10.4 0.8 select_reduce_fusion.1
  11.6 1.0 scatter_custom_fusion.1
  12.6 0.7 all_to_all.27
  13.3 7.2 %all-to-all-start.1 = ((s32[16,16,1]{1,2,0:T(1,128)}), s32[16,16,1]{1,2,0:T(1,128)S(1)}, u32[]{:S(2)}, u32[]{:S(2)}) async-start(s32[16,16,1]{1,2,0:T(1,128)} %bitcast.9), calls=%async_computation.1 | async-start | bytes 16384 | tf_op jit(solution)/shard_map/all_to_all | solution.py:93
  20.5 1.0 scatter_custom_fusion
  21.5 0.9 slice_convert_fusion.3
  22.4 1.2 maximum_convert_fusion
  23.6 89.6 %all-gather.2.cloned.1.call-done = bf16[2048,3072]{0,1:T(8,128)(2,1)} async-done(((bf16[2048,192]{0,1:T(8,128)(2,1)}), bf16[2048,3072]{0,1:T(8,128)(2,1)}) %all-gather.2.cloned.1.call-update) | async-done | bytes 12582928 | tf_op jit(solution)/shard_map/all_gather | solution.py:84
  113.2 8.9 %convolution_convert_fusion = bf16[128,3072]{1,0:T(8,128)(2,1)S(1)} fusion(bf16[2048,3072]{0,1:T(8,128)(2,1)} %all-gather.2.cloned.1.call-done, f32[131,2048]{1,0:T(8,128)S(1)} %maximum_convert_fusion, bf16[128,2048]{1,0:T(8,128)(2,1)S(1)} %copy-done, f32[2048]{0:T(1024)S(1)} %bitcast.29, f32[2048]{0:T(1024)S(1)} %bitcast.30, f32[2048]{0:T(1024)S(1)} %bitcast.28, ...), kind=kOutput, calls=%fused_computation.5 | convolution fusion | flops 1613627392 | bytes 18120704 | tf_op jit(solution)/shard_map/dot_general | solution.py:82
  122.2 2.7 %gather_fusion = bf16[256,3072]{1,0:T(8,128)(2,1)} fusion(bf16[129,3072]{1,0:T(8,128)(2,1)S(1)} %concatenate.7, s32[1024]{0:T(1024)S(1)} %pad_clamp_fusion.1), kind=kCustom, calls=%fused_computation | custom fusion | bytes 3146752 | tf_op jit(solution)/shard_map/gather | solution.py:90
  124.9 3.7 %all-to-all-start = ((bf16[16,16,3072]{2,1,0:T(8,128)(2,1)}), bf16[16,16,3072]{2,1,0:T(8,128)(2,1)S(1)}, u32[]{:S(2)}, u32[]{:S(2)}) async-start(bf16[16,16,3072]{2,1,0:T(8,128)(2,1)} %bitcast.6), calls=%async_computation | async-start | bytes 3145728 | tf_op jit(solution)/shard_map/all_to_all | solution.py:92
  128.6 0.5 broadcast.108
  129.1 0.7 reduce.3
  130.0 30.5 %all-to-all-done = bf16[16,16,3072]{2,1,0:T(8,128)(2,1)S(1)} async-done(((bf16[16,16,3072]{2,1,0:T(8,128)(2,1)}), bf16[16,16,3072]{2,1,0:T(8,128)(2,1)S(1)}, u32[]{:S(2)}, u32[]{:S(2)}) %all-to-all-start) | async-done | bytes 1572896 | tf_op jit(solution)/shard_map/all_to_all | solution.py:92
  161.3 2.2 %fusion.28 = (f32[8,256]{1,0:T(8,128)S(1)}, f32[8,256,256]{1,2,0:T(8,128)}) fusion(pred[256,256]{0,1:T(8,128)(4,1)S(1)} %fusion.16, bf16[256,8,128]{0,2,1:T(8,128)(2,1)S(1)} %bitcast.24, bf16[256,8,128]{0,2,1:T(8,128)(2,1)S(1)} %bitcast.25), kind=kOutput, calls=%fused_computation.55 | convolution fusion | flops 136315136 | bytes 3219456 | tf_op jit(solution)/shard_map/while/body/eval_jaxpr/sub | solution.py:38
  163.5 1.9 fusion.2
  165.4 0.3 copy.31
  165.7 1.0 all_to_all.30
  166.7 9.1 %all-to-all-start.2 = ((bf16[16,16,1024]{2,1,0:T(8,128)(2,1)}), bf16[16,16,1024]{2,1,0:T(8,128)(2,1)S(1)}, u32[]{:S(2)}, u32[]{:S(2)}) async-start(bf16[16,16,1024]{2,1,0:T(8,128)(2,1)} %all_to_all.30), calls=%async_computation.2 | async-start | bytes 1048576 | tf_op jit(solution)/shard_map/all_to_all | solution.py:96
  175.8 14.5 %all-to-all-done.2 = bf16[16,16,1024]{2,1,0:T(8,128)(2,1)S(1)} async-done(((bf16[16,16,1024]{2,1,0:T(8,128)(2,1)}), bf16[16,16,1024]{2,1,0:T(8,128)(2,1)S(1)}, u32[]{:S(2)}, u32[]{:S(2)}) %all-to-all-start.2) | async-done | bytes 524320 | tf_op jit(solution)/shard_map/all_to_all | solution.py:96
  190.3 1.6 gather_fusion.1
  (22 shorter events, 1.5 us)
Async XLA Ops:
  6.5 106.7 %copy-start = (bf16[128,2048]{1,0:T(8,128)(2,1)S(1)}, bf16[128,2048]{1,0:T(8,128)(2,1)}, u32[]{:S(2)}) copy-start(bf16[128,2048]{1,0:T(8,128)(2,1)} %param.5) | copy-start | bytes 1572868
  6.5 106.7 %all-gather.2.cloned.1.call-start = ((), (), s32[]{:S(2)}) async-start(), calls=%async_computation.3 | async-start | bytes 13369344 | tf_op jit(solution)/shard_map/all_gather | solution.py:84
  8.0 14.4 %collective-permute-start = (bf16[3,2048]{1,0:T(4,128)(2,1)S(1)}, bf16[3,2048]{1,0:T(4,128)(2,1)S(1)}, u32[]{:S(2)}, u32[]{:S(2)}) collective-permute-start(bf16[3,2048]{1,0:T(4,128)(2,1)S(1)} %slice.37), channel_id=1, source_target_pairs={{0,1},{1,2},{2,3},{3,4},{4,5},{5,6},{6,7},{7,8},{8,9},{9,10},{10,1... | collective-permute-start | bytes 36872 | tf_op jit(solution)/shard_map/ppermute | solution.py:13
  13.3 111.6 %all-to-all-start.1 = ((s32[16,16,1]{1,2,0:T(1,128)}), s32[16,16,1]{1,2,0:T(1,128)S(1)}, u32[]{:S(2)}, u32[]{:S(2)}) async-start(s32[16,16,1]{1,2,0:T(1,128)} %bitcast.9), calls=%async_computation.1 | async-start | bytes 16384 | tf_op jit(solution)/shard_map/all_to_all | solution.py:93
  124.9 35.6 %all-to-all-start = ((bf16[16,16,3072]{2,1,0:T(8,128)(2,1)}), bf16[16,16,3072]{2,1,0:T(8,128)(2,1)S(1)}, u32[]{:S(2)}, u32[]{:S(2)}) async-start(bf16[16,16,3072]{2,1,0:T(8,128)(2,1)} %bitcast.6), calls=%async_computation | async-start | bytes 3145728 | tf_op jit(solution)/shard_map/all_to_all | solution.py:92
  166.7 23.6 %all-to-all-start.2 = ((bf16[16,16,1024]{2,1,0:T(8,128)(2,1)}), bf16[16,16,1024]{2,1,0:T(8,128)(2,1)S(1)}, u32[]{:S(2)}, u32[]{:S(2)}) async-start(bf16[16,16,1024]{2,1,0:T(8,128)(2,1)} %all_to_all.30), calls=%async_computation.2 | async-start | bytes 1048576 | tf_op jit(solution)/shard_map/all_to_all | solution.py:96
Sparse Core Ops, SparseCore 0:
  9.6 103.5 all-gather.1
where the time goes:
time: 199 us
  waiting for transfers between devices  135 us (68%)
  starting transfers between devices  22.4 us (11%)
  between operations  13.6 us (7%)
  matrix products  13 us (7%)
  local copies, waits for them, and re-layouts  10.4 us (5%)
  other arithmetic  4.12 us (2%)
    all_gather x1, waiting for transfers between devices, body(): lax.all_gather(qkv_weight, 'seq', axis=1, tiled=True)  89.6 us
    all_to_all x1, waiting for transfers between devices, body(): lax.all_to_all(outgoing, 'seq', split_axis=0, concat_axis=0, tiled=True)  30.5 us
    all_to_all x1, waiting for transfers between devices, body(): lax.all_to_all(mixed, 'seq', split_axis=0, concat_axis=0, tiled=True)  14.5 us
    all_to_all x1, starting transfers between devices, body(): lax.all_to_all(mixed, 'seq', split_axis=0, concat_axis=0, tiled=True)  9.08 us
    dot_general x1, matrix products, body(): jnp.dot(hidden, lax.all_gather(qkv_weight, 'seq', axis=1, tiled=True), pr...  8.87 us
    all_to_all x1, starting transfers between devices, body(): lax.all_to_all(send_times, 'seq', split_axis=0, concat_axis=0, tiled=True)  7.22 us
  transfers between devices with their start and end apart: 5, of which 3 were waited for; matrix products, arithmetic and copies ran while one was open for 10% of the time, Pallas kernels for 0%

commit v1 on v0

v1 whole, which is shorter than its diff:
```python
import jax
import jax.numpy as jnp
from jax import lax
from jax.sharding import Mesh
from jax.sharding import PartitionSpec as P

HD = 128
KW = 4


def from_behind(value, axis, by):
    size = lax.axis_size(axis)
    pairs = [(i, i + by) for i in range(size) if 0 <= i + by < size]
    return lax.ppermute(value, axis, pairs)


def track_groups(track_ids, track_owner):
    track_total = track_owner.shape[0]
    return jnp.sum(
        jnp.where(
            track_ids[:, None] == jnp.arange(track_total, dtype=jnp.int32)[None, :],
            track_owner[None, :],
            0,
        ),
        axis=1,
    )


def convolve(frames, conv_weight, rim_rows):
    tok_rows = frames.shape[0]
    extended = jnp.concatenate([rim_rows, frames], axis=0).astype(jnp.float32)
    conv_sum = frames.astype(jnp.float32)
    for tap in range(KW):
        conv_sum = (
            conv_sum
            + conv_weight[tap].astype(jnp.float32)[None, :]
            * extended[KW - 1 - tap : KW - 1 - tap + tok_rows]
        )
    return conv_sum.astype(jnp.bfloat16)


def attend_slots(packed, positions):
    slot_count = packed.shape[0]
    inner = packed.shape[1] // 3
    head_count = inner // HD
    query = packed[:, :inner].reshape(slot_count, head_count, HD)
    keys_all = packed[:, inner : 2 * inner].reshape(slot_count, head_count, HD)
    values_all = packed[:, 2 * inner :].reshape(slot_count, head_count, HD)
    slot_ids = jnp.arange(slot_count, dtype=jnp.int32)
    score_scale = 1.0 / HD**0.5
    scores = (
        jnp.einsum("qhd,khd->hqk", query, keys_all, preferred_element_type=jnp.float32)
        * score_scale
    )
    allowed = (positions[None, :] >= 0) & (positions[None, :] <= positions[:, None]) | (
        slot_ids[:, None] == slot_ids[None, :]
    )
    scores = jnp.where(allowed[None], scores, jnp.float32(-1e30))
    top_score = jnp.max(scores, axis=-1, keepdims=True)
    expd = jnp.exp(scores - top_score)
    weights = (expd / jnp.sum(expd, axis=-1, keepdims=True)).astype(jnp.bfloat16)
    mixed = jnp.einsum("hqk,khd->qhd", weights, values_all, preferred_element_type=jnp.float32)
    return mixed.astype(jnp.bfloat16).reshape(slot_count, inner)


def body_by_owner(frames, conv_weight, qkv_weight, track_ids, track_owner):
    tok_rows = frames.shape[0]
    peer_count = lax.axis_size("seq")
    capacity = 2 * tok_rows // peer_count
    slot_total = capacity * peer_count
    my_index = lax.axis_index("seq")
    rim_rows = from_behind(frames[tok_rows - (KW - 1) :], "seq", 1)
    hidden = convolve(frames, conv_weight, rim_rows)
    group = track_groups(track_ids, track_owner)
    owner_hits = (group[:, None] == jnp.arange(peer_count, dtype=jnp.int32)[None, :]).astype(
        jnp.int32
    )
    running = jnp.cumsum(owner_hits, axis=0) - 1
    rank_rows = jnp.sum(jnp.where(owner_hits > 0, running, 0), axis=1)
    slot_of_row = group * capacity + rank_rows
    row_ids = jnp.arange(tok_rows, dtype=jnp.int32)
    source_row = jnp.full((slot_total,), tok_rows, jnp.int32).at[slot_of_row].set(row_ids)
    positions = my_index * tok_rows + row_ids
    send_times = jnp.full((slot_total,), -1, jnp.int32).at[slot_of_row].set(positions)
    projected = jnp.dot(
        hidden,
        lax.all_gather(qkv_weight, "seq", axis=1, tiled=True),
        preferred_element_type=jnp.float32,
    ).astype(jnp.bfloat16)
    padded_rows = jnp.concatenate(
        [projected, jnp.zeros((1, projected.shape[1]), jnp.bfloat16)], axis=0
    )
    outgoing = padded_rows[source_row]
    received, got_times = (
        lax.all_to_all(outgoing, "seq", split_axis=0, concat_axis=0, tiled=True),
        lax.all_to_all(send_times, "seq", split_axis=0, concat_axis=0, tiled=True),
    )
    mixed = attend_slots(received, got_times)
    returned = lax.all_to_all(mixed, "seq", split_axis=0, concat_axis=0, tiled=True)
    return returned[slot_of_row]


def body_by_head(frames, conv_weight, qkv_weight, track_ids, track_owner):
    tok_rows = frames.shape[0]
    chips = lax.axis_size("chip")
    devices = 2 * chips
    core = lax.axis_index("core")
    chip = lax.axis_index("chip")
    me = 2 * chip + core
    both = ("chip", "core")
    half = HD // 2

    group = track_groups(track_ids, track_owner)
    all_groups = lax.all_gather(group, both, axis=0, tiled=True)

    held = qkv_weight.T.reshape(3, half, qkv_weight.shape[0])
    moved = [
        lax.ppermute(held[j], both, [(d, (3 * d + j) % devices) for d in range(devices)])
        for j in range(3)
    ]
    turn = lax.rem(me, 3)
    mine = lax.dynamic_slice_in_dim(jnp.stack(moved + moved[:2]), turn, 3, 0)
    swap = [(0, 1), (1, 0)]
    theirs = lax.ppermute(mine, "core", swap)
    first = jnp.where(core == 0, mine, theirs)
    second = jnp.where(core == 0, theirs, mine)
    head_weight = jnp.stack([first, second], axis=1).reshape(3 * HD, -1)

    rim_rows = lax.ppermute(
        frames[tok_rows - (KW - 1) :], both, [(i, i + 1) for i in range(devices - 1)]
    )
    hidden = convolve(frames, conv_weight, rim_rows)
    stream = lax.all_gather(hidden, "chip", axis=0, tiled=True)
    projected = lax.dot_general(
        stream, head_weight, (((1,), (1,)), ((), ())), preferred_element_type=jnp.float32
    ).astype(jnp.bfloat16)
    query = projected[:, :HD]
    own = projected[:, HD:]
    other = lax.ppermute(own, "core", swap)
    keyed = jnp.concatenate([own, other], axis=0)

    times = jnp.arange(devices * tok_rows, dtype=jnp.int32).reshape(chips, 2, tok_rows)
    groups = all_groups.reshape(chips, 2, tok_rows)
    rows = chips * tok_rows

    def of_core(values, which):
        return lax.dynamic_index_in_dim(values, which, 1, False).reshape(rows)

    own_times, own_groups = of_core(times, core), of_core(groups, core)
    key_times = jnp.concatenate([own_times, of_core(times, 1 - core)])
    key_groups = jnp.concatenate([own_groups, of_core(groups, 1 - core)])
    scores = lax.dot_general(
        query, keyed[:, :HD], (((1,), (1,)), ((), ())), preferred_element_type=jnp.float32
    ) * (1.0 / HD**0.5)
    allowed = (key_times[None, :] <= own_times[:, None]) & (
        key_groups[None, :] == own_groups[:, None]
    )
    scores = jnp.where(allowed, scores, jnp.float32(-1e30))
    expd = jnp.exp(scores - jnp.max(scores, axis=-1, keepdims=True))
    weights = (expd / jnp.sum(expd, axis=-1, keepdims=True)).astype(jnp.bfloat16)
    mixed = jnp.dot(weights, keyed[:, HD:], preferred_element_type=jnp.float32)
    mixed = mixed.astype(jnp.bfloat16).reshape(chips, tok_rows, HD)
    returned = lax.all_to_all(mixed, "chip", split_axis=0, concat_axis=0, tiled=True)
    return returned.transpose(1, 0, 2).reshape(tok_rows, chips * HD)


def solution(mesh):
    grp, seq = mesh.devices.shape
    out_by_owner = P(("grp", "seq"), None)
    by_owner = jax.shard_map(
        body_by_owner,
        mesh=mesh,
        in_specs=(P(("grp", "seq"), None), P(), P(None, "seq"), P(("grp", "seq")), P("grp")),
        out_specs=out_by_owner,
        check_vma=False,
    )
    split = Mesh(mesh.devices.reshape(grp, seq // 2, 2), ("grp", "chip", "core"))
    rows = P(("grp", "chip", "core"))
    by_head = jax.shard_map(
        body_by_head,
        mesh=split,
        in_specs=(rows, P(), P(None, ("chip", "core")), rows, P("grp")),
        out_specs=rows,
        check_vma=False,
    )

    def run(frames, conv_weight, qkv_weight, track_ids, track_owner):
        heads = qkv_weight.shape[1] // (3 * HD)
        plan = by_head if seq == 2 * heads else by_owner
        return plan(frames, conv_weight, qkv_weight, track_ids, track_owner)

    return run
```

time: 199 us -> 149 us (0.75)
  waiting for transfers between devices: 135 us -> 75.9 us
  blocking collectives: 0 us -> 30.6 us
  starting transfers between devices: 22.4 us -> 12.7 us
  local copies, waits for them, and re-layouts: 10.4 us -> 1.89 us
  matrix products: 13 us -> 8.56 us
    all_to_all x3 -> x0, waiting for transfers between devices: 44.9 us -> none  [the longest x1 30.5 us: body(): lax.all_to_all(outgoing, 'seq', split_axis=0, concat_axis=0, tiled=True)]
    all_gather x1, waiting for transfers between devices: 89.6 us -> 60.2 us  [body_by_head(): stream = lax.all_gather(hidden, 'chip', axis=0, tiled=True)]
    all_to_all x3 -> x0, starting transfers between devices: 20 us -> none  [the longest x1 9.08 us: body(): lax.all_to_all(mixed, 'seq', split_axis=0, concat_axis=0, tiled=True)]
    all_gather x0 -> x1, blocking collectives: none -> 18.6 us  [body_by_head(): all_groups = lax.all_gather(group, both, axis=0, tiled=True)]
    ppermute x1 -> x6, waiting for transfers between devices: 0.01 us -> 15.7 us  [the longest x3 13.4 us: body_by_head(): lax.ppermute(held[j], both, [(d, (3 * d + j) % devices) for d in range(de...]
    all_to_all x0 -> x1, blocking collectives: none -> 12.1 us  [body_by_head(): lax.all_to_all(mixed, 'chip', split_axis=0, concat_axis=0, tiled=True)]
    ppermute x1 -> x6, starting transfers between devices: 2.36 us -> 12.7 us  [the longest x3 10.2 us: body_by_head(): lax.ppermute(held[j], both, [(d, (3 * d + j) % devices) for d in range(de...]
    gather x2 -> x0, local copies, waits for them, and re-layouts: 4.28 us -> none  [the longest x1 2.72 us: body(): outgoing = padded_rows[source_row]]
  transfers between devices with their start and end apart: 5 -> 7, of which waited for: 3 -> 4; matrix products, arithmetic and copies ran while one was open for 10% -> 1% of each run, Pallas kernels for 0% -> 0%
where the time goes in v1:
time: 149 us; the launch traced here: 148 us
  waiting for transfers between devices  75.9 us (51%)
  blocking collectives  30.6 us (21%)
  between operations  13.6 us (9%)
  starting transfers between devices  12.7 us (9%)
  matrix products  8.56 us (6%)
  other arithmetic  5.06 us (3%)
  local copies, waits for them, and re-layouts  1.89 us (1%)
    all_gather x1, waiting for transfers between devices, body_by_head(): stream = lax.all_gather(hidden, 'chip', axis=0, tiled=True)  60.2 us
    all_gather x1, blocking collectives, body_by_head(): all_groups = lax.all_gather(group, both, axis=0, tiled=True)  18.6 us
    ppermute x3, waiting for transfers between devices, body_by_head(): lax.ppermute(held[j], both, [(d, (3 * d + j) % devices) for d in range(de...  13.4 us
    all_to_all x1, blocking collectives, body_by_head(): lax.all_to_all(mixed, 'chip', split_axis=0, concat_axis=0, tiled=True)  12.1 us
    ppermute x3, starting transfers between devices, body_by_head(): lax.ppermute(held[j], both, [(d, (3 * d + j) % devices) for d in range(de...  10.2 us
    dot_general x1, matrix products, body_by_head(): lax.dot_general(stream, head_weight, (((1,), (1,)), ((), ())), preferred_...  4.56 us
  transfers between devices with their start and end apart: 7, of which 4 were waited for; matrix products, arithmetic and copies ran while one was open for 1% of the time, Pallas kernels for 0%

profile of v1, /device:TPU:0, one launch (start us, length us, event | category | flops | bytes accessed | tf_op | source)
XLA Modules:
  0.0 148.4 jit_solution(306558339992979922)
XLA Ops:
  6.5 0.8 slice.52
  7.4 2.4 %collective-permute-start = (bf16[3,2048]{1,0:T(4,128)(2,1)S(1)}, bf16[3,2048]{1,0:T(4,128)(2,1)S(1)}, u32[]{:S(2)}, u32[]{:S(2)}) collective-permute-start(bf16[3,2048]{1,0:T(4,128)(2,1)S(1)} %slice.52), channel_id=1, source_target_pairs={{0,1},{1,2},{2,3},{3,4},{4,5},{5,6},{6,7},{7,8},{8,9},{9,10},{10,1... | collective-permute-start | bytes 36872 | tf_op jit(solution)/shard_map/ppermute | solution.py:129
  9.7 0.9 slice_convert_fusion.3
  10.7 1.2 maximum_convert_fusion
  11.9 1.3 fusion.4
  13.3 0.7 collective-permute-start.1
  14.0 9.5 %collective-permute-start.3 = (bf16[64,2048]{1,0:T(8,128)(2,1)S(1)}, bf16[64,2048]{1,0:T(8,128)(2,1)S(1)}, u32[]{:S(2)}, u32[]{:S(2)}) collective-permute-start(bf16[64,2048]{1,0:T(8,128)(2,1)S(1)} %get-tuple-element.7), channel_id=1, source_target_pairs={{0,2},{1,5},{2,8},{3,11},{4,14},{5,1},{6,4},{7,7},{8,10},{9,13},{1... | collective-permute-start | bytes 786440 | tf_op jit(solution)/shard_map/ppermute | solution.py:118
  23.6 8.2 %collective-permute-done.2 = bf16[64,2048]{1,0:T(8,128)(2,1)S(1)} collective-permute-done((bf16[64,2048]{1,0:T(8,128)(2,1)S(1)}, bf16[64,2048]{1,0:T(8,128)(2,1)S(1)}, u32[]{:S(2)}, u32[]{:S(2)}) %collective-permute-start.2) | collective-permute-done | bytes 262176 | tf_op jit(solution)/shard_map/ppermute | solution.py:118
  31.8 5.2 %collective-permute-done.3 = bf16[64,2048]{1,0:T(8,128)(2,1)S(1)} collective-permute-done((bf16[64,2048]{1,0:T(8,128)(2,1)S(1)}, bf16[64,2048]{1,0:T(8,128)(2,1)S(1)}, u32[]{:S(2)}, u32[]{:S(2)}) %collective-permute-start.3) | collective-permute-done | bytes 262176 | tf_op jit(solution)/shard_map/ppermute | solution.py:118
  37.1 0.1 constant_dynamic-slice_fusion
  37.2 0.1 collective-permute-start.4
  37.3 2.3 %collective-permute-done.4 = bf16[3,64,2048]{2,1,0:T(8,128)(2,1)S(1)} collective-permute-done((bf16[3,64,2048]{2,1,0:T(8,128)(2,1)S(1)}, bf16[3,64,2048]{2,1,0:T(8,128)(2,1)S(1)}, u32[]{:S(2)}, u32[]{:S(2)}) %collective-permute-start.4) | collective-permute-done | bytes 786464 | tf_op jit(solution)/shard_map/ppermute | solution.py:124
  39.6 0.1 select_bitcast_fusion.1
  39.7 0.1 pad_maximum_fusion
  39.8 60.2 %all-gather.3.cloned.1.call-done = bf16[1024,2048]{1,0:T(8,128)(2,1)} async-done(((bf16[128,2048]{1,0:T(8,128)(2,1)}), bf16[1024,2048]{1,0:T(8,128)(2,1)}) %all-gather.3.cloned.1.call-update) | async-done | bytes 4194320 | tf_op jit(solution)/shard_map/all_gather | solution.py:133
  100.0 4.6 %convolution_convert_fusion = bf16[1024,384]{1,0:T(8,128)(2,1)S(1)} fusion(bf16[1024,2048]{1,0:T(8,128)(2,1)} %all-gather.3.cloned.1.call-done, bf16[384,2048]{1,0:T(8,128)(2,1)S(1)} %bitcast.35), kind=kOutput, calls=%fused_computation.6 | convolution fusion | flops 1611005952 | bytes 6553600 | tf_op jit(solution)/shard_map/dot_general | solution.py:134
  104.7 0.1 collective-permute-start.5
  104.8 0.1 select_reduce_fusion
  104.8 18.6 %all-gather = s32[16,1,128]{2,1,0:T(1,128)S(1)} all-gather(s32[1,1,128]{2,1,0:T(1,128)S(1)} %bitcast.49), channel_id=1, replica_groups=mesh['grp'=2,'chip'=8,'core'=2] {'chip','core'}, dimensions={0}, use_global_device_ids=true | all-gather | bytes 8704 | tf_op jit(solution)/shard_map/all_gather | solution.py:114
  123.5 2.4 %fusion.15 = (f32[1024]{0:T(1024)S(1)}, f32[1024,2048]{1,0:T(8,128)S(1)}) fusion(bf16[1024,256]{1,0:T(8,128)(2,1)S(1)} %slice.75, bf16[1024,256]{1,0:T(8,128)(2,1)S(1)} %collective-permute-done.5, bf16[1024,384]{1,0:T(8,128)(2,1)S(1)} %convolution_convert_fusion, s32[1024]{0:T(1024)S(1)} %bitcast.44, s32[2048]{0:T(1024)S(1)} %pad_add_fusion.1, ...), kind=kOutput, calls=%fused_computation.49 | convolution fusion | flops 550501376 | bytes 9728000 | tf_op jit(solution)/shard_map/dot_general | solution.py:152
  125.8 1.3 fusion
  127.1 1.6 %fusion.2 = bf16[1024,128]{1,0:T(8,128)(2,1)S(1)} fusion(f32[1024,2048]{1,0:T(8,128)S(1)} %get-tuple-element.19, f32[1024]{0:T(1024)S(1)} %fusion, f32[1024]{0:T(1024)S(1)} %get-tuple-element.18, bf16[1024,256]{1,0:T(8,128)(2,1)S(1)} %collective-permute-done.5, bf16[1024,256]{1,0:T(8,128)(2,1)S(1)} %slice.75), kind=kOutput, calls=%fused_computation.7 | convolution fusion | flops 544342016 | bytes 9707520 | tf_op jit(solution)/shard_map/dot_general | solution.py:161
  128.7 12.1 %all_to_all.5 = bf16[8,128,128]{2,1,0:T(8,128)(2,1)S(1)} all-to-all(bf16[8,128,128]{2,1,0:T(8,128)(2,1)S(1)} %bitcast.37), channel_id=1, replica_groups=mesh['grp'=2,'chip'=8,'core'=2] {'chip'}, dimensions={0} | all-to-all | bytes 524288 | tf_op jit(solution)/shard_map/all_to_all | solution.py:163
  140.8 0.7 copy_bitcast_fusion
  (25 shorter events, 0.3 us)
Async XLA Ops:
  6.5 5.3 %copy-start = (bf16[128,2048]{1,0:T(8,128)(2,1)S(1)}, bf16[128,2048]{1,0:T(8,128)(2,1)}, u32[]{:S(2)}) copy-start(bf16[128,2048]{1,0:T(8,128)(2,1)} %param.5) | copy-start | bytes 1572868
  6.5 93.5 %all-gather.3.cloned.1.call-start = ((), (), s32[]{:S(2)}) async-start(), calls=%async_computation.1 | async-start | bytes 4718592 | tf_op jit(solution)/shard_map/all_gather | solution.py:133
  7.4 3.3 %collective-permute-start = (bf16[3,2048]{1,0:T(4,128)(2,1)S(1)}, bf16[3,2048]{1,0:T(4,128)(2,1)S(1)}, u32[]{:S(2)}, u32[]{:S(2)}) collective-permute-start(bf16[3,2048]{1,0:T(4,128)(2,1)S(1)} %slice.52), channel_id=1, source_target_pairs={{0,1},{1,2},{2,3},{3,4},{4,5},{5,6},{6,7},{7,8},{8,9},{9,10},{10,1... | collective-permute-start | bytes 36872 | tf_op jit(solution)/shard_map/ppermute | solution.py:129
  11.9 1.4 copy-start.1
  13.3 10.2 %collective-permute-start.1 = (bf16[64,2048]{1,0:T(8,128)(2,1)S(1)}, bf16[64,2048]{1,0:T(8,128)(2,1)S(1)}, u32[]{:S(2)}, u32[]{:S(2)}) collective-permute-start(bf16[64,2048]{1,0:T(8,128)(2,1)S(1)} %get-tuple-element.9), channel_id=1, source_target_pairs={{0,0},{1,3},{2,6},{3,9},{4,12},{5,15},{6,2},{7,5},{8,8},{9,11},{10... | collective-permute-start | bytes 786440 | tf_op jit(solution)/shard_map/ppermute | solution.py:118
  14.0 23.0 %collective-permute-start.3 = (bf16[64,2048]{1,0:T(8,128)(2,1)S(1)}, bf16[64,2048]{1,0:T(8,128)(2,1)S(1)}, u32[]{:S(2)}, u32[]{:S(2)}) collective-permute-start(bf16[64,2048]{1,0:T(8,128)(2,1)S(1)} %get-tuple-element.7), channel_id=1, source_target_pairs={{0,2},{1,5},{2,8},{3,11},{4,14},{5,1},{6,4},{7,7},{8,10},{9,13},{1... | collective-permute-start | bytes 786440 | tf_op jit(solution)/shard_map/ppermute | solution.py:118
  23.5 8.3 %collective-permute-start.2 = (bf16[64,2048]{1,0:T(8,128)(2,1)S(1)}, bf16[64,2048]{1,0:T(8,128)(2,1)S(1)}, u32[]{:S(2)}, u32[]{:S(2)}) collective-permute-start(bf16[64,2048]{1,0:T(8,128)(2,1)S(1)} %get-tuple-element.8), channel_id=1, source_target_pairs={{0,1},{1,4},{2,7},{3,10},{4,13},{5,0},{6,3},{7,6},{8,9},{9,12},{10... | collective-permute-start | bytes 786440 | tf_op jit(solution)/shard_map/ppermute | solution.py:118
  37.2 2.4 %collective-permute-start.4 = (bf16[3,64,2048]{2,1,0:T(8,128)(2,1)S(1)}, bf16[3,64,2048]{2,1,0:T(8,128)(2,1)S(1)}, u32[]{:S(2)}, u32[]{:S(2)}) collective-permute-start(bf16[3,64,2048]{2,1,0:T(8,128)(2,1)S(1)} %constant_dynamic-slice_fusion), channel_id=1, source_target_pairs={{0,1},{1,0},{2,3},{3,2},{4,5},{5,4},{6,7},{7,6},{8,9},{9,8},{10,11... | collective-permute-start | bytes 2359304 | tf_op jit(solution)/shard_map/ppermute | solution.py:124
  100.0 4.7 %copy-start.2 = (s32[64]{0:T(128)S(1)}, s32[64]{0:T(128)}, u32[]{:S(2)}) copy-start(s32[64]{0:T(128)} %param.9) | copy-start | bytes 772
  100.0 4.7 %copy-start.3 = (s32[128]{0:T(128)S(1)}, s32[128]{0:T(128)}, u32[]{:S(2)}) copy-start(s32[128]{0:T(128)} %param.8) | copy-start | bytes 1540
  104.7 18.8 %collective-permute-start.5 = (bf16[1024,256]{1,0:T(8,128)(2,1)S(1)}, bf16[1024,256]{1,0:T(8,128)(2,1)S(1)}, u32[]{:S(2)}, u32[]{:S(2)}) collective-permute-start(bf16[1024,256]{1,0:T(8,128)(2,1)S(1)} %slice.75), channel_id=1, source_target_pairs={{0,1},{1,0},{2,3},{3,2},{4,5},{5,4},{6,7},{7,6},{8,9},{9,8},{10,11... | collective-permute-start | bytes 1572872 | tf_op jit(solution)/shard_map/ppermute | solution.py:139
Sparse Core Ops, SparseCore 0:
  13.4 86.6 all-gather.2

commit v2 on v1

--- a/solution.py
+++ b/solution.py
@@ -100,6 +100,18 @@
     return returned[slot_of_row]
 
 
+def all_by_doubling(values, axes, devices, me):
+    step = 1
+    while step < devices:
+        theirs = lax.ppermute(values, axes, [(d, d ^ step) for d in range(devices)])
+        low = me & step == 0
+        values = jnp.concatenate(
+            [jnp.where(low, values, theirs), jnp.where(low, theirs, values)], axis=0
+        )
+        step *= 2
+    return values
+
+
 def body_by_head(frames, conv_weight, qkv_weight, track_ids, track_owner):
     tok_rows = frames.shape[0]
     chips = lax.axis_size("chip")
@@ -109,9 +121,26 @@
     me = 2 * chip + core
     both = ("chip", "core")
     half = HD // 2
+    part = tok_rows // 2
+
+    ring = list(range(0, chips, 2)) + list(range(chips - 1, 0, -2))
+    place = jnp.where(chip & 1 == 0, chip >> 1, chips - 1 - (chip >> 1))
+
+    def chip_at(position):
+        position = jnp.where(position >= chips, position - chips, position)
+        return jnp.where(position < chips // 2, 2 * position, 2 * (chips - 1 - position) + 1)
+
+    onward = [(ring[i], ring[(i + 1) % chips]) for i in range(chips)]
+    backward = [(t, f) for f, t in onward]
+
+    rim_rows = lax.ppermute(
+        frames[tok_rows - (KW - 1) :], both, [(i, i + 1) for i in range(devices - 1)]
+    )
+    late = convolve(frames[part:], conv_weight, frames[part - (KW - 1) : part])
+    early = convolve(frames[:part], conv_weight, rim_rows)
 
     group = track_groups(track_ids, track_owner)
-    all_groups = lax.all_gather(group, both, axis=0, tiled=True)
+    all_groups = all_by_doubling(group[None, :], both, devices, me)
 
     held = qkv_weight.T.reshape(3, half, qkv_weight.shape[0])
     moved = [
@@ -126,14 +155,23 @@
     second = jnp.where(core == 0, theirs, mine)
     head_weight = jnp.stack([first, second], axis=1).reshape(3 * HD, -1)
 
-    rim_rows = lax.ppermute(
-        frames[tok_rows - (KW - 1) :], both, [(i, i + 1) for i in range(devices - 1)]
-    )
-    hidden = convolve(frames, conv_weight, rim_rows)
-    stream = lax.all_gather(hidden, "chip", axis=0, tiled=True)
-    projected = lax.dot_general(
-        stream, head_weight, (((1,), (1,)), ((), ())), preferred_element_type=jnp.float32
-    ).astype(jnp.bfloat16)
+    projected = jnp.zeros((chips, tok_rows, 3 * HD), jnp.bfloat16)
+
+    def project(rows, where, offset, projected):
+        done = lax.dot_general(
+            rows, head_weight, (((1,), (1,)), ((), ())), preferred_element_type=jnp.float32
+        ).astype(jnp.bfloat16)
+        return lax.dynamic_update_slice(projected, done[None], (where, offset, 0))
+
+    for step in range(chips):
+        projected = project(late, chip_at(place + step), part, projected)
+        projected = project(early, chip_at(place + chips - step), 0, projected)
+        if step < chips - 1:
+            late = lax.ppermute(late, "chip", backward)
+            early = lax.ppermute(early, "chip", onward)
+
+    rows = chips * tok_rows
+    projected = projected.reshape(rows, 3 * HD)
     query = projected[:, :HD]
     own = projected[:, HD:]
     other = lax.ppermute(own, "core", swap)
@@ -141,7 +179,6 @@
 
     times = jnp.arange(devices * tok_rows, dtype=jnp.int32).reshape(chips, 2, tok_rows)
     groups = all_groups.reshape(chips, 2, tok_rows)
-    rows = chips * tok_rows
 
     def of_core(values, which):
         return lax.dynamic_index_in_dim(values, which, 1, False).reshape(rows)

time: 149 us -> 107 us (0.72)
  waiting for transfers between devices: 75.9 us -> 24.7 us
  starting transfers between devices: 12.7 us -> 45 us
  blocking collectives: 30.6 us -> 12.8 us
  between operations: 13.6 us -> 0.63 us
  matrix products: 8.56 us -> 17.4 us
  other arithmetic: 5.06 us -> 3.12 us
    all_gather x1 -> x0, waiting for transfers between devices: 60.2 us -> none  [body_by_head(): stream = lax.all_gather(hidden, 'chip', axis=0, tiled=True)]
    ppermute x0 -> x18, starting transfers between devices: none -> 27.6 us  [the longest x7 12.9 us: body_by_head(): early = lax.ppermute(early, 'chip', onward)]
    ppermute x0 -> x18, waiting for transfers between devices: none -> 22.2 us  [the longest x7 16.2 us: body_by_head(): early = lax.ppermute(early, 'chip', onward)]
    all_gather x1 -> x0, blocking collectives: 18.6 us -> none  [body_by_head(): all_groups = lax.all_gather(group, both, axis=0, tiled=True)]
    ppermute x3, waiting for transfers between devices: 13.4 us -> 0.69 us  [body_by_head(): lax.ppermute(held[j], both, [(d, (3 * d + j) % devices) for d in range(de...]
    dot_general x1 -> x16, matrix products: 4.56 us -> 13.4 us  [project(): lax.dot_general(rows, head_weight, (((1,), (1,)), ((), ())), preferred_el...]
    ppermute x1, starting transfers between devices: 0.07 us -> 8.82 us  [body_by_head(): theirs = lax.ppermute(mine, 'core', swap)]
    ppermute x3, starting transfers between devices: 10.2 us -> 6.51 us  [body_by_head(): lax.ppermute(held[j], both, [(d, (3 * d + j) % devices) for d in range(de...]
  transfers between devices with their start and end apart: 7 -> 24, of which waited for: 4 -> 9; matrix products, arithmetic and copies ran while one was open for 1% -> 16% of each run, Pallas kernels for 0% -> 0%
where the time goes in v2:
time: 107 us
  starting transfers between devices  45 us (42%)
  waiting for transfers between devices  24.7 us (23%)
  matrix products  17.4 us (16%)
  blocking collectives  12.8 us (12%)
  other arithmetic  3.12 us (3%)
  local copies, waits for them, and re-layouts  3.03 us (3%)
    ppermute x7, waiting for transfers between devices, body_by_head(): early = lax.ppermute(early, 'chip', onward)  16.2 us
    dot_general x16, matrix products, project(): lax.dot_general(rows, head_weight, (((1,), (1,)), ((), ())), preferred_el...  13.4 us
    ppermute x7, starting transfers between devices, body_by_head(): early = lax.ppermute(early, 'chip', onward)  12.9 us
    all_to_all x1, blocking collectives, body_by_head(): lax.all_to_all(mixed, 'chip', split_axis=0, concat_axis=0, tiled=True)  12.8 us
    ppermute x4, starting transfers between devices, all_by_doubling(): theirs = lax.ppermute(values, axes, [(d, d ^ step) for d in range(devices)])  8.9 us
    ppermute x1, starting transfers between devices, body_by_head(): theirs = lax.ppermute(mine, 'core', swap)  8.82 us
    ppermute x3, starting transfers between devices, body_by_head(): lax.ppermute(held[j], both, [(d, (3 * d + j) % devices) for d in range(de...  6.51 us
    ppermute x7, waiting for transfers between devices, body_by_head(): late = lax.ppermute(late, 'chip', backward)  6 us
  transfers between devices with their start and end apart: 24, of which 9 were waited for; matrix products, arithmetic and copies ran while one was open for 16% of the time, Pallas kernels for 0%

profile of v2, /device:TPU:0, one launch (start us, length us, event | category | flops | bytes accessed | tf_op | source)
XLA Modules:
  0.0 106.7 jit_solution(15935260781421602011)
XLA Ops:
  2.1 2.0 %collective-permute-start.8 = (bf16[3,2048]{1,0:T(4,128)(2,1)S(1)}, bf16[3,2048]{1,0:T(4,128)(2,1)S(1)}, u32[]{:S(2)}, u32[]{:S(2)}) collective-permute-start(bf16[3,2048]{1,0:T(4,128)(2,1)S(1)} %slice.88), channel_id=1, source_target_pairs={{0,1},{1,2},{2,3},{3,4},{4,5},{5,6},{6,7},{7,8},{8,9},{9,10},{10,1... | collective-permute-start | bytes 36872 | tf_op jit(solution)/shard_map/ppermute | solution.py:136
  5.3 4.9 %collective-permute-start.6 = (bf16[64,2048]{1,0:T(8,128)(2,1)S(1)}, bf16[64,2048]{1,0:T(8,128)(2,1)S(1)}, u32[]{:S(2)}, u32[]{:S(2)}) collective-permute-start(bf16[64,2048]{1,0:T(8,128)(2,1)S(1)} %get-tuple-element.7), channel_id=1, source_target_pairs={{0,2},{1,5},{2,8},{3,11},{4,14},{5,1},{6,4},{7,7},{8,10},{9,13},{1... | collective-permute-start | bytes 786440 | tf_op jit(solution)/shard_map/ppermute | solution.py:147
  12.8 4.3 %collective-permute-start.10 = (bf16[64,2048]{1,0:T(8,128)(2,1)S(1)}, bf16[64,2048]{1,0:T(8,128)(2,1)}, u32[]{:S(2)}, u32[]{:S(2)}) collective-permute-start(bf16[64,2048]{1,0:T(8,128)(2,1)S(1)} %get-tuple-element.10), channel_id=1, source_target_pairs={{0,4},{4,8},{8,12},{12,14},{14,10},{10,6},{6,2},{2,0},{1,5},{5,9},... | collective-permute-start | bytes 786440 | tf_op jit(solution)/shard_map/ppermute | solution.py:171
  19.2 8.8 %collective-permute-start.7 = (bf16[3,64,2048]{2,1,0:T(8,128)(2,1)S(1)}, bf16[3,64,2048]{2,1,0:T(8,128)(2,1)S(1)}, u32[]{:S(2)}, u32[]{:S(2)}) collective-permute-start(bf16[3,64,2048]{2,1,0:T(8,128)(2,1)S(1)} %constant_dynamic-slice_fusion), channel_id=1, source_target_pairs={{0,1},{1,0},{2,3},{3,2},{4,5},{5,4},{6,7},{7,6},{8,9},{9,8},{10,11... | collective-permute-start | bytes 2359304 | tf_op jit(solution)/shard_map/ppermute | solution.py:153
  28.0 6.3 %collective-permute-start.1 = (s32[2,128]{1,0:T(2,128)S(1)}, s32[2,128]{1,0:T(2,128)S(1)}, u32[]{:S(2)}, u32[]{:S(2)}) collective-permute-start(s32[2,128]{1,0:T(2,128)S(1)} %pad_add_fusion.5), channel_id=1, source_target_pairs={{0,2},{1,3},{2,0},{3,1},{4,6},{5,7},{6,4},{7,5},{8,10},{9,11},{10,... | collective-permute-start | bytes 3080 | tf_op jit(solution)/shard_map/ppermute | solution.py:106
  34.4 2.5 %collective-permute-start.11 = (bf16[64,2048]{1,0:T(8,128)(2,1)}, bf16[64,2048]{1,0:T(8,128)(2,1)}, u32[]{:S(2)}, u32[]{:S(2)}) collective-permute-start(bf16[64,2048]{1,0:T(8,128)(2,1)} %collective-permute-done.9), channel_id=1, source_target_pairs={{4,0},{8,4},{12,8},{14,12},{10,14},{6,10},{2,6},{0,2},{5,1},{9,5},... | collective-permute-start | bytes 786440 | tf_op jit(solution)/shard_map/ppermute | solution.py:170
  37.1 6.0 %collective-permute-done.12 = bf16[64,2048]{1,0:T(8,128)(2,1)} collective-permute-done((bf16[64,2048]{1,0:T(8,128)(2,1)}, bf16[64,2048]{1,0:T(8,128)(2,1)}, u32[]{:S(2)}, u32[]{:S(2)}) %collective-permute-start.12) | collective-permute-done | bytes 262176 | tf_op jit(solution)/shard_map/ppermute | solution.py:171
  43.7 1.3 %collective-permute-start.13 = (bf16[64,2048]{1,0:T(8,128)(2,1)}, bf16[64,2048]{1,0:T(8,128)(2,1)S(1)}, u32[]{:S(2)}, u32[]{:S(2)}) collective-permute-start(bf16[64,2048]{1,0:T(8,128)(2,1)} %collective-permute-done.11), channel_id=1, source_target_pairs={{4,0},{8,4},{12,8},{14,12},{10,14},{6,10},{2,6},{0,2},{5,1},{9,5},... | collective-permute-start | bytes 786440 | tf_op jit(solution)/shard_map/ppermute | solution.py:170
  45.1 2.0 %collective-permute-start.3 = (s32[8,128]{1,0:T(8,128)S(1)}, s32[8,128]{1,0:T(8,128)S(1)}, u32[]{:S(2)}, u32[]{:S(2)}) collective-permute-start(s32[8,128]{1,0:T(8,128)S(1)} %pad_add_fusion.3), channel_id=1, source_target_pairs={{0,8},{1,9},{2,10},{3,11},{4,12},{5,13},{6,14},{7,15},{8,0},{9,1},... | collective-permute-start | bytes 12296 | tf_op jit(solution)/shard_map/ppermute | solution.py:106
  47.1 3.2 %collective-permute-done.14 = bf16[64,2048]{1,0:T(8,128)(2,1)S(1)} collective-permute-done((bf16[64,2048]{1,0:T(8,128)(2,1)}, bf16[64,2048]{1,0:T(8,128)(2,1)S(1)}, u32[]{:S(2)}, u32[]{:S(2)}) %collective-permute-start.14) | collective-permute-done | bytes 262176 | tf_op jit(solution)/shard_map/ppermute | solution.py:171
  53.9 1.6 %fusion.8 = bf16[8,128,384]{2,1,0:T(8,128)(2,1)S(1)} fusion(bf16[8,128,384]{2,1,0:T(8,128)(2,1)S(1)} %fusion.6, s32[]{:T(128)S(6)} %select_n.214, bf16[64,2048]{1,0:T(8,128)(2,1)} %collective-permute-done.9, bf16[384,2048]{1,0:T(8,128)(2,1)S(1)} %bitcast.134), kind=kOutput, calls=%fused_computation.28 | convolution fusion | flops 100687872 | bytes 1884164 | tf_op jit(solution)/shard_map/dot_general | solution.py:161
  55.5 1.6 %fusion.10 = bf16[8,128,384]{2,1,0:T(8,128)(2,1)S(1)} fusion(bf16[8,128,384]{2,1,0:T(8,128)(2,1)S(1)} %fusion.8, s32[]{:T(128)S(6)} %select_n.217, bf16[64,2048]{1,0:T(8,128)(2,1)} %collective-permute-done.10, bf16[384,2048]{1,0:T(8,128)(2,1)S(1)} %bitcast.135), kind=kOutput, calls=%fused_computation.30 | convolution fusion | flops 100687872 | bytes 1884164 | tf_op jit(solution)/shard_map/dot_general | solution.py:161
  57.0 1.6 %fusion.12 = bf16[8,128,384]{2,1,0:T(8,128)(2,1)S(1)} fusion(bf16[8,128,384]{2,1,0:T(8,128)(2,1)S(1)} %fusion.10, s32[]{:T(128)S(6)} %select_n.220, bf16[64,2048]{1,0:T(8,128)(2,1)} %collective-permute-done.11, bf16[384,2048]{1,0:T(8,128)(2,1)S(1)} %bitcast.136), kind=kOutput, calls=%fused_computation.32 | convolution fusion | flops 100687872 | bytes 1884164 | tf_op jit(solution)/shard_map/dot_general | solution.py:161
  58.6 1.6 %fusion.14 = bf16[8,128,384]{2,1,0:T(8,128)(2,1)S(1)} fusion(bf16[8,128,384]{2,1,0:T(8,128)(2,1)S(1)} %fusion.12, s32[]{:T(128)S(6)} %select_n.223, bf16[64,2048]{1,0:T(8,128)(2,1)} %collective-permute-done.12, bf16[384,2048]{1,0:T(8,128)(2,1)S(1)} %bitcast.137), kind=kOutput, calls=%fused_computation.34 | convolution fusion | flops 100687872 | bytes 1884164 | tf_op jit(solution)/shard_map/dot_general | solution.py:161
  61.4 2.1 %collective-permute-start.18 = (bf16[64,2048]{1,0:T(8,128)(2,1)S(1)}, bf16[64,2048]{1,0:T(8,128)(2,1)S(1)}, u32[]{:S(2)}, u32[]{:S(2)}) collective-permute-start(bf16[64,2048]{1,0:T(8,128)(2,1)S(1)} %collective-permute-done.16), channel_id=1, source_target_pairs={{0,4},{4,8},{8,12},{12,14},{14,10},{10,6},{6,2},{2,0},{1,5},{5,9},... | collective-permute-start | bytes 786440 | tf_op jit(solution)/shard_map/ppermute | solution.py:171
  65.0 3.8 %collective-permute-done.18 = bf16[64,2048]{1,0:T(8,128)(2,1)S(1)} collective-permute-done((bf16[64,2048]{1,0:T(8,128)(2,1)S(1)}, bf16[64,2048]{1,0:T(8,128)(2,1)S(1)}, u32[]{:S(2)}, u32[]{:S(2)}) %collective-permute-start.18) | collective-permute-done | bytes 262176 | tf_op jit(solution)/shard_map/ppermute | solution.py:171
  68.8 2.5 %collective-permute-start.20 = (bf16[64,2048]{1,0:T(8,128)(2,1)S(1)}, bf16[64,2048]{1,0:T(8,128)(2,1)S(1)}, u32[]{:S(2)}, u32[]{:S(2)}) collective-permute-start(bf16[64,2048]{1,0:T(8,128)(2,1)S(1)} %collective-permute-done.18), channel_id=1, source_target_pairs={{0,4},{4,8},{8,12},{12,14},{14,10},{10,6},{6,2},{2,0},{1,5},{5,9},... | collective-permute-start | bytes 786440 | tf_op jit(solution)/shard_map/ppermute | solution.py:171
  72.5 3.2 %collective-permute-done.20 = bf16[64,2048]{1,0:T(8,128)(2,1)S(1)} collective-permute-done((bf16[64,2048]{1,0:T(8,128)(2,1)S(1)}, bf16[64,2048]{1,0:T(8,128)(2,1)S(1)}, u32[]{:S(2)}, u32[]{:S(2)}) %collective-permute-start.20) | collective-permute-done | bytes 262176 | tf_op jit(solution)/shard_map/ppermute | solution.py:171
  75.7 2.5 %collective-permute-start.22 = (bf16[64,2048]{1,0:T(8,128)(2,1)S(1)}, bf16[64,2048]{1,0:T(8,128)(2,1)S(1)}, u32[]{:S(2)}, u32[]{:S(2)}) collective-permute-start(bf16[64,2048]{1,0:T(8,128)(2,1)S(1)} %collective-permute-done.20), channel_id=1, source_target_pairs={{0,4},{4,8},{8,12},{12,14},{14,10},{10,6},{6,2},{2,0},{1,5},{5,9},... | collective-permute-start | bytes 786440 | tf_op jit(solution)/shard_map/ppermute | solution.py:171
  79.7 4.9 %collective-permute-done.21 = bf16[64,2048]{1,0:T(8,128)(2,1)S(1)} collective-permute-done((bf16[64,2048]{1,0:T(8,128)(2,1)S(1)}, bf16[64,2048]{1,0:T(8,128)(2,1)S(1)}, u32[]{:S(2)}, u32[]{:S(2)}) %collective-permute-start.21) | collective-permute-done | bytes 262176 | tf_op jit(solution)/shard_map/ppermute | solution.py:170
  86.0 1.8 %collective-permute-done.23 = bf16[1024,256]{1,0:T(8,128)(2,1)S(1)} collective-permute-done((bf16[1024,256]{1,0:T(8,128)(2,1)S(1)}, bf16[1024,256]{1,0:T(8,128)(2,1)S(1)}, u32[]{:S(2)}, u32[]{:S(2)}) %collective-permute-start.23) | collective-permute-done | bytes 524320 | tf_op jit(solution)/shard_map/ppermute | solution.py:177
  87.8 2.4 %fusion.52 = (f32[1024]{0:T(1024)S(1)}, f32[1024,2048]{1,0:T(8,128)S(1)}) fusion(bf16[1024,256]{1,0:T(8,128)(2,1)S(1)} %slice.109, bf16[1024,256]{1,0:T(8,128)(2,1)S(1)} %collective-permute-done.23, bf16[1024,384]{1,0:T(8,128)(2,1)S(1)} %bitcast.149, s32[1024]{0:T(1024)S(1)} %bitcast.158, s32[2048]{0:T(1024)S(1)} %pad_add_fusion.2, ...), kind=kOutput, calls=%fused_computation.118 | convolution fusion | flops 550501376 | bytes 9728000 | tf_op jit(solution)/shard_map/dot_general | solution.py:189
  91.5 1.6 %fusion.2 = bf16[1024,128]{1,0:T(8,128)(2,1)S(1)} fusion(f32[1024,2048]{1,0:T(8,128)S(1)} %get-tuple-element.29, f32[1024]{0:T(1024)S(1)} %fusion, f32[1024]{0:T(1024)S(1)} %get-tuple-element.28, bf16[1024,256]{1,0:T(8,128)(2,1)S(1)} %collective-permute-done.23, bf16[1024,256]{1,0:T(8,128)(2,1)S(1)} %slice.109), kind=kOutput, calls=%fused_computation.6 | convolution fusion | flops 544342016 | bytes 9707520 | tf_op jit(solution)/shard_map/dot_general | solution.py:198
  93.1 12.8 %all_to_all.5 = bf16[8,128,128]{2,1,0:T(8,128)(2,1)S(1)} all-to-all(bf16[8,128,128]{2,1,0:T(8,128)(2,1)S(1)} %bitcast.151), channel_id=1, replica_groups=mesh['grp'=2,'chip'=8,'core'=2] {'chip'}, dimensions={0} | all-to-all | bytes 524288 | tf_op jit(solution)/shard_map/all_to_all | solution.py:200
  (80 shorter events, 20.9 us)
Async XLA Ops:
  0.8 11.3 %collective-permute-start = (s32[1,128]{1,0:T(1,128)S(1)}, s32[1,128]{1,0:T(1,128)S(1)}, u32[]{:S(2)}, u32[]{:S(2)}) collective-permute-start(s32[1,128]{1,0:T(1,128)S(1)} %bitcast.163), channel_id=1, source_target_pairs={{0,1},{1,0},{2,3},{3,2},{4,5},{5,4},{6,7},{7,6},{8,9},{9,8},{10,11... | collective-permute-start | bytes 1544 | tf_op jit(solution)/shard_map/ppermute | solution.py:106
  2.1 10.0 %collective-permute-start.8 = (bf16[3,2048]{1,0:T(4,128)(2,1)S(1)}, bf16[3,2048]{1,0:T(4,128)(2,1)S(1)}, u32[]{:S(2)}, u32[]{:S(2)}) collective-permute-start(bf16[3,2048]{1,0:T(4,128)(2,1)S(1)} %slice.88), channel_id=1, source_target_pairs={{0,1},{1,2},{2,3},{3,4},{4,5},{5,6},{6,7},{7,8},{8,9},{9,10},{10,1... | collective-permute-start | bytes 36872 | tf_op jit(solution)/shard_map/ppermute | solution.py:136
  5.3 13.7 %collective-permute-start.6 = (bf16[64,2048]{1,0:T(8,128)(2,1)S(1)}, bf16[64,2048]{1,0:T(8,128)(2,1)S(1)}, u32[]{:S(2)}, u32[]{:S(2)}) collective-permute-start(bf16[64,2048]{1,0:T(8,128)(2,1)S(1)} %get-tuple-element.7), channel_id=1, source_target_pairs={{0,2},{1,5},{2,8},{3,11},{4,14},{5,1},{6,4},{7,7},{8,10},{9,13},{1... | collective-permute-start | bytes 786440 | tf_op jit(solution)/shard_map/ppermute | solution.py:147
  10.2 8.1 %collective-permute-start.5 = (bf16[64,2048]{1,0:T(8,128)(2,1)S(1)}, bf16[64,2048]{1,0:T(8,128)(2,1)S(1)}, u32[]{:S(2)}, u32[]{:S(2)}) collective-permute-start(bf16[64,2048]{1,0:T(8,128)(2,1)S(1)} %get-tuple-element.8), channel_id=1, source_target_pairs={{0,1},{1,4},{2,7},{3,10},{4,13},{5,0},{6,3},{7,6},{8,9},{9,12},{10... | collective-permute-start | bytes 786440 | tf_op jit(solution)/shard_map/ppermute | solution.py:147
  11.2 7.1 %collective-permute-start.4 = (bf16[64,2048]{1,0:T(8,128)(2,1)S(1)}, bf16[64,2048]{1,0:T(8,128)(2,1)S(1)}, u32[]{:S(2)}, u32[]{:S(2)}) collective-permute-start(bf16[64,2048]{1,0:T(8,128)(2,1)S(1)} %get-tuple-element.9), channel_id=1, source_target_pairs={{0,0},{1,3},{2,6},{3,9},{4,12},{5,15},{6,2},{7,5},{8,8},{9,11},{10... | collective-permute-start | bytes 786440 | tf_op jit(solution)/shard_map/ppermute | solution.py:147
  12.8 21.6 %collective-permute-start.10 = (bf16[64,2048]{1,0:T(8,128)(2,1)S(1)}, bf16[64,2048]{1,0:T(8,128)(2,1)}, u32[]{:S(2)}, u32[]{:S(2)}) collective-permute-start(bf16[64,2048]{1,0:T(8,128)(2,1)S(1)} %get-tuple-element.10), channel_id=1, source_target_pairs={{0,4},{4,8},{8,12},{12,14},{14,10},{10,6},{6,2},{2,0},{1,5},{5,9},... | collective-permute-start | bytes 786440 | tf_op jit(solution)/shard_map/ppermute | solution.py:171
  17.1 17.3 %collective-permute-start.9 = (bf16[64,2048]{1,0:T(8,128)(2,1)S(1)}, bf16[64,2048]{1,0:T(8,128)(2,1)}, u32[]{:S(2)}, u32[]{:S(2)}) collective-permute-start(bf16[64,2048]{1,0:T(8,128)(2,1)S(1)} %get-tuple-element.11), channel_id=1, source_target_pairs={{4,0},{8,4},{12,8},{14,12},{10,14},{6,10},{2,6},{0,2},{5,1},{9,5},... | collective-permute-start | bytes 786440 | tf_op jit(solution)/shard_map/ppermute | solution.py:170
  19.2 33.2 %collective-permute-start.7 = (bf16[3,64,2048]{2,1,0:T(8,128)(2,1)S(1)}, bf16[3,64,2048]{2,1,0:T(8,128)(2,1)S(1)}, u32[]{:S(2)}, u32[]{:S(2)}) collective-permute-start(bf16[3,64,2048]{2,1,0:T(8,128)(2,1)S(1)} %constant_dynamic-slice_fusion), channel_id=1, source_target_pairs={{0,1},{1,0},{2,3},{3,2},{4,5},{5,4},{6,7},{7,6},{8,9},{9,8},{10,11... | collective-permute-start | bytes 2359304 | tf_op jit(solution)/shard_map/ppermute | solution.py:153
  28.0 8.9 %collective-permute-start.1 = (s32[2,128]{1,0:T(2,128)S(1)}, s32[2,128]{1,0:T(2,128)S(1)}, u32[]{:S(2)}, u32[]{:S(2)}) collective-permute-start(s32[2,128]{1,0:T(2,128)S(1)} %pad_add_fusion.5), channel_id=1, source_target_pairs={{0,2},{1,3},{2,0},{3,1},{4,6},{5,7},{6,4},{7,5},{8,10},{9,11},{10,... | collective-permute-start | bytes 3080 | tf_op jit(solution)/shard_map/ppermute | solution.py:106
  34.4 8.7 %collective-permute-start.12 = (bf16[64,2048]{1,0:T(8,128)(2,1)}, bf16[64,2048]{1,0:T(8,128)(2,1)}, u32[]{:S(2)}, u32[]{:S(2)}) collective-permute-start(bf16[64,2048]{1,0:T(8,128)(2,1)} %collective-permute-done.10), channel_id=1, source_target_pairs={{0,4},{4,8},{8,12},{12,14},{14,10},{10,6},{6,2},{2,0},{1,5},{5,9},... | collective-permute-start | bytes 786440 | tf_op jit(solution)/shard_map/ppermute | solution.py:171
  34.4 9.4 %collective-permute-start.11 = (bf16[64,2048]{1,0:T(8,128)(2,1)}, bf16[64,2048]{1,0:T(8,128)(2,1)}, u32[]{:S(2)}, u32[]{:S(2)}) collective-permute-start(bf16[64,2048]{1,0:T(8,128)(2,1)} %collective-permute-done.9), channel_id=1, source_target_pairs={{4,0},{8,4},{12,8},{14,12},{10,14},{6,10},{2,6},{0,2},{5,1},{9,5},... | collective-permute-start | bytes 786440 | tf_op jit(solution)/shard_map/ppermute | solution.py:170
  36.9 8.2 %collective-permute-start.2 = (s32[4,128]{1,0:T(4,128)S(1)}, s32[4,128]{1,0:T(4,128)S(1)}, u32[]{:S(2)}, u32[]{:S(2)}) collective-permute-start(s32[4,128]{1,0:T(4,128)S(1)} %pad_add_fusion.4), channel_id=1, source_target_pairs={{0,4},{1,5},{2,6},{3,7},{4,0},{5,1},{6,2},{7,3},{8,12},{9,13},{10,... | collective-permute-start | bytes 6152 | tf_op jit(solution)/shard_map/ppermute | solution.py:106
  43.1 7.2 %collective-permute-start.14 = (bf16[64,2048]{1,0:T(8,128)(2,1)}, bf16[64,2048]{1,0:T(8,128)(2,1)S(1)}, u32[]{:S(2)}, u32[]{:S(2)}) collective-permute-start(bf16[64,2048]{1,0:T(8,128)(2,1)} %collective-permute-done.12), channel_id=1, source_target_pairs={{0,4},{4,8},{8,12},{12,14},{14,10},{10,6},{6,2},{2,0},{1,5},{5,9},... | collective-permute-start | bytes 786440 | tf_op jit(solution)/shard_map/ppermute | solution.py:171
  43.7 8.4 %collective-permute-start.13 = (bf16[64,2048]{1,0:T(8,128)(2,1)}, bf16[64,2048]{1,0:T(8,128)(2,1)S(1)}, u32[]{:S(2)}, u32[]{:S(2)}) collective-permute-start(bf16[64,2048]{1,0:T(8,128)(2,1)} %collective-permute-done.11), channel_id=1, source_target_pairs={{4,0},{8,4},{12,8},{14,12},{10,14},{6,10},{2,6},{0,2},{5,1},{9,5},... | collective-permute-start | bytes 786440 | tf_op jit(solution)/shard_map/ppermute | solution.py:170
  45.1 40.8 %collective-permute-start.3 = (s32[8,128]{1,0:T(8,128)S(1)}, s32[8,128]{1,0:T(8,128)S(1)}, u32[]{:S(2)}, u32[]{:S(2)}) collective-permute-start(s32[8,128]{1,0:T(8,128)S(1)} %pad_add_fusion.3), channel_id=1, source_target_pairs={{0,8},{1,9},{2,10},{3,11},{4,12},{5,13},{6,14},{7,15},{8,0},{9,1},... | collective-permute-start | bytes 12296 | tf_op jit(solution)/shard_map/ppermute | solution.py:106
  50.2 11.1 %collective-permute-start.16 = (bf16[64,2048]{1,0:T(8,128)(2,1)S(1)}, bf16[64,2048]{1,0:T(8,128)(2,1)S(1)}, u32[]{:S(2)}, u32[]{:S(2)}) collective-permute-start(bf16[64,2048]{1,0:T(8,128)(2,1)S(1)} %collective-permute-done.14), channel_id=1, source_target_pairs={{0,4},{4,8},{8,12},{12,14},{14,10},{10,6},{6,2},{2,0},{1,5},{5,9},... | collective-permute-start | bytes 786440 | tf_op jit(solution)/shard_map/ppermute | solution.py:171
  52.1 11.4 %collective-permute-start.15 = (bf16[64,2048]{1,0:T(8,128)(2,1)S(1)}, bf16[64,2048]{1,0:T(8,128)(2,1)S(1)}, u32[]{:S(2)}, u32[]{:S(2)}) collective-permute-start(bf16[64,2048]{1,0:T(8,128)(2,1)S(1)} %collective-permute-done.13), channel_id=1, source_target_pairs={{4,0},{8,4},{12,8},{14,12},{10,14},{6,10},{2,6},{0,2},{5,1},{9,5},... | collective-permute-start | bytes 786440 | tf_op jit(solution)/shard_map/ppermute | solution.py:170
  61.4 7.4 %collective-permute-start.18 = (bf16[64,2048]{1,0:T(8,128)(2,1)S(1)}, bf16[64,2048]{1,0:T(8,128)(2,1)S(1)}, u32[]{:S(2)}, u32[]{:S(2)}) collective-permute-start(bf16[64,2048]{1,0:T(8,128)(2,1)S(1)} %collective-permute-done.16), channel_id=1, source_target_pairs={{0,4},{4,8},{8,12},{12,14},{14,10},{10,6},{6,2},{2,0},{1,5},{5,9},... | collective-permute-start | bytes 786440 | tf_op jit(solution)/shard_map/ppermute | solution.py:171
  63.5 7.8 %collective-permute-start.17 = (bf16[64,2048]{1,0:T(8,128)(2,1)S(1)}, bf16[64,2048]{1,0:T(8,128)(2,1)S(1)}, u32[]{:S(2)}, u32[]{:S(2)}) collective-permute-start(bf16[64,2048]{1,0:T(8,128)(2,1)S(1)} %collective-permute-done.15), channel_id=1, source_target_pairs={{4,0},{8,4},{12,8},{14,12},{10,14},{6,10},{2,6},{0,2},{5,1},{9,5},... | collective-permute-start | bytes 786440 | tf_op jit(solution)/shard_map/ppermute | solution.py:170
  68.8 6.9 %collective-permute-start.20 = (bf16[64,2048]{1,0:T(8,128)(2,1)S(1)}, bf16[64,2048]{1,0:T(8,128)(2,1)S(1)}, u32[]{:S(2)}, u32[]{:S(2)}) collective-permute-start(bf16[64,2048]{1,0:T(8,128)(2,1)S(1)} %collective-permute-done.18), channel_id=1, source_target_pairs={{0,4},{4,8},{8,12},{12,14},{14,10},{10,6},{6,2},{2,0},{1,5},{5,9},... | collective-permute-start | bytes 786440 | tf_op jit(solution)/shard_map/ppermute | solution.py:171
  71.3 6.9 %collective-permute-start.19 = (bf16[64,2048]{1,0:T(8,128)(2,1)S(1)}, bf16[64,2048]{1,0:T(8,128)(2,1)S(1)}, u32[]{:S(2)}, u32[]{:S(2)}) collective-permute-start(bf16[64,2048]{1,0:T(8,128)(2,1)S(1)} %collective-permute-done.17), channel_id=1, source_target_pairs={{4,0},{8,4},{12,8},{14,12},{10,14},{6,10},{2,6},{0,2},{5,1},{9,5},... | collective-permute-start | bytes 786440 | tf_op jit(solution)/shard_map/ppermute | solution.py:170
  75.7 9.5 %collective-permute-start.22 = (bf16[64,2048]{1,0:T(8,128)(2,1)S(1)}, bf16[64,2048]{1,0:T(8,128)(2,1)S(1)}, u32[]{:S(2)}, u32[]{:S(2)}) collective-permute-start(bf16[64,2048]{1,0:T(8,128)(2,1)S(1)} %collective-permute-done.20), channel_id=1, source_target_pairs={{0,4},{4,8},{8,12},{12,14},{14,10},{10,6},{6,2},{2,0},{1,5},{5,9},... | collective-permute-start | bytes 786440 | tf_op jit(solution)/shard_map/ppermute | solution.py:171
  78.2 6.4 %collective-permute-start.21 = (bf16[64,2048]{1,0:T(8,128)(2,1)S(1)}, bf16[64,2048]{1,0:T(8,128)(2,1)S(1)}, u32[]{:S(2)}, u32[]{:S(2)}) collective-permute-start(bf16[64,2048]{1,0:T(8,128)(2,1)S(1)} %collective-permute-done.19), channel_id=1, source_target_pairs={{4,0},{8,4},{12,8},{14,12},{10,14},{6,10},{2,6},{0,2},{5,1},{9,5},... | collective-permute-start | bytes 786440 | tf_op jit(solution)/shard_map/ppermute | solution.py:170
  85.9 2.0 %collective-permute-start.23 = (bf16[1024,256]{1,0:T(8,128)(2,1)S(1)}, bf16[1024,256]{1,0:T(8,128)(2,1)S(1)}, u32[]{:S(2)}, u32[]{:S(2)}) collective-permute-start(bf16[1024,256]{1,0:T(8,128)(2,1)S(1)} %slice.109), channel_id=1, source_target_pairs={{0,1},{1,0},{2,3},{3,2},{4,5},{5,4},{6,7},{7,6},{8,9},{9,8},{10,11... | collective-permute-start | bytes 1572872 | tf_op jit(solution)/shard_map/ppermute | solution.py:177
  (3 other events, 32.0 us)

commit v3 on v1

--- a/solution.py
+++ b/solution.py
@@ -100,55 +100,96 @@
     return returned[slot_of_row]
 
 
+def xor_swap(value, bit, axes=("chip", "core")):
+    count = lax.axis_size(axes)
+    return lax.ppermute(value, axes, [(d, d ^ bit) for d in range(count)])
+
+
+def by_bit(bit, mine, theirs, axis):
+    return jnp.stack(
+        [jnp.where(bit == 0, mine, theirs), jnp.where(bit == 0, theirs, mine)], axis=axis
+    )
+
+
 def body_by_head(frames, conv_weight, qkv_weight, track_ids, track_owner):
     tok_rows = frames.shape[0]
     chips = lax.axis_size("chip")
     devices = 2 * chips
     core = lax.axis_index("core")
     chip = lax.axis_index("chip")
+    grp = lax.axis_index("grp")
     me = 2 * chip + core
     both = ("chip", "core")
-    half = HD // 2
-
-    group = track_groups(track_ids, track_owner)
-    all_groups = lax.all_gather(group, both, axis=0, tiled=True)
-
-    held = qkv_weight.T.reshape(3, half, qkv_weight.shape[0])
+    every = ("grp", "chip", "core")
+    part = tok_rows // 2
+    features = frames.shape[1]
+    CORE, Y, Z0, Z1 = 1, 2, 4, 8
+
+    rim_rows = lax.ppermute(
+        frames[tok_rows - (KW - 1) :], both, [(i, i + 1) for i in range(devices - 1)]
+    )
+    late = convolve(frames[part:], conv_weight, frames[part - (KW - 1) : part])
+    early = convolve(frames[:part], conv_weight, rim_rows)
+
+    far_late = xor_swap(late, Z1)
+    far_early = xor_swap(early, Z1)
+    own = jnp.concatenate([early, late], axis=0)
+    beside = xor_swap(own, Y)
+    far_beside_late = xor_swap(far_late, Y)
+    far_beside_early = xor_swap(far_early, Y)
+
+    half = features // 2
+    held = lax.dynamic_slice_in_dim(qkv_weight.T, grp * half, half, 1).reshape(3, HD // 2, half)
     moved = [
         lax.ppermute(held[j], both, [(d, (3 * d + j) % devices) for d in range(devices)])
         for j in range(3)
     ]
-    turn = lax.rem(me, 3)
-    mine = lax.dynamic_slice_in_dim(jnp.stack(moved + moved[:2]), turn, 3, 0)
-    swap = [(0, 1), (1, 0)]
-    theirs = lax.ppermute(mine, "core", swap)
-    first = jnp.where(core == 0, mine, theirs)
-    second = jnp.where(core == 0, theirs, mine)
-    head_weight = jnp.stack([first, second], axis=1).reshape(3 * HD, -1)
-
-    rim_rows = lax.ppermute(
-        frames[tok_rows - (KW - 1) :], both, [(i, i + 1) for i in range(devices - 1)]
-    )
-    hidden = convolve(frames, conv_weight, rim_rows)
-    stream = lax.all_gather(hidden, "chip", axis=0, tiled=True)
-    projected = lax.dot_general(
-        stream, head_weight, (((1,), (1,)), ((), ())), preferred_element_type=jnp.float32
-    ).astype(jnp.bfloat16)
+    mine = lax.dynamic_slice_in_dim(jnp.stack(moved + moved[:2]), lax.rem(me, 3), 3, 0)
+    paired = xor_swap(mine, Z0)
+
+    def whole_head(quarter):
+        wide = by_bit(grp, quarter, xor_swap(quarter, devices, every), 2)
+        wide = wide.reshape(3, HD // 2, features)
+        return by_bit(core, wide, xor_swap(wide, CORE), 1).reshape(3 * HD, features)
+
+    two_heads = jnp.concatenate([whole_head(mine), whole_head(paired)], axis=0)
+
+    def project(rows):
+        done = lax.dot_general(
+            rows, two_heads, (((1,), (1,)), ((), ())), preferred_element_type=jnp.float32
+        ).astype(jnp.bfloat16)
+        return jnp.concatenate([done[:, : 3 * HD], xor_swap(done[:, 3 * HD :], Z0)], axis=0)
+
+    first = project(jnp.concatenate([own, beside, far_late, far_beside_late], axis=0))
+    second = project(jnp.concatenate([far_early, far_beside_early], axis=0))
+
+    first_rows = [(0, 0, tok_rows), (Y, 0, tok_rows), (Z1, part, part), (Z1 | Y, part, part)]
+    second_rows = [(Z1, 0, part), (Z1 | Y, 0, part)]
+    order = []
+    for pieces in (first_rows, second_rows):
+        order += pieces + [(far ^ Z0, start, count) for far, start, count in pieces]
+
+    groups = track_groups(track_ids, track_owner)[None, :]
+    for bit in (CORE, Y, Z0, Z1):
+        groups = jnp.concatenate([groups, xor_swap(groups, bit)], axis=0)
+
+    def of_rows(bit):
+        times = [
+            (me ^ far ^ bit) * tok_rows + start + jnp.arange(count, dtype=jnp.int32)
+            for far, start, count in order
+        ]
+        marks = [groups[far ^ bit, start : start + count] for far, start, count in order]
+        return jnp.concatenate(times), jnp.concatenate(marks)
+
+    projected = jnp.concatenate([first, second], axis=0)
     query = projected[:, :HD]
-    own = projected[:, HD:]
-    other = lax.ppermute(own, "core", swap)
-    keyed = jnp.concatenate([own, other], axis=0)
-
-    times = jnp.arange(devices * tok_rows, dtype=jnp.int32).reshape(chips, 2, tok_rows)
-    groups = all_groups.reshape(chips, 2, tok_rows)
-    rows = chips * tok_rows
-
-    def of_core(values, which):
-        return lax.dynamic_index_in_dim(values, which, 1, False).reshape(rows)
-
-    own_times, own_groups = of_core(times, core), of_core(groups, core)
-    key_times = jnp.concatenate([own_times, of_core(times, 1 - core)])
-    key_groups = jnp.concatenate([own_groups, of_core(groups, 1 - core)])
+    keyed = jnp.concatenate(
+        [projected[:, HD:], xor_swap(first[:, HD:], CORE), xor_swap(second[:, HD:], CORE)], axis=0
+    )
+    own_times, own_groups = of_rows(0)
+    other_times, other_groups = of_rows(CORE)
+    key_times = jnp.concatenate([own_times, other_times])
+    key_groups = jnp.concatenate([own_groups, other_groups])
     scores = lax.dot_general(
         query, keyed[:, :HD], (((1,), (1,)), ((), ())), preferred_element_type=jnp.float32
     ) * (1.0 / HD**0.5)
@@ -159,8 +200,15 @@
     expd = jnp.exp(scores - jnp.max(scores, axis=-1, keepdims=True))
     weights = (expd / jnp.sum(expd, axis=-1, keepdims=True)).astype(jnp.bfloat16)
     mixed = jnp.dot(weights, keyed[:, HD:], preferred_element_type=jnp.float32)
-    mixed = mixed.astype(jnp.bfloat16).reshape(chips, tok_rows, HD)
-    returned = lax.all_to_all(mixed, "chip", split_axis=0, concat_axis=0, tiled=True)
+    mixed = mixed.astype(jnp.bfloat16)
+
+    sent = jnp.zeros((chips, tok_rows, HD), jnp.bfloat16)
+    at = 0
+    for far, start, count in order:
+        rows = mixed[at : at + count]
+        sent = lax.dynamic_update_slice(sent, rows[None], ((me ^ far) >> 1, start, 0))
+        at += count
+    returned = lax.all_to_all(sent, "chip", split_axis=0, concat_axis=0, tiled=True)
     return returned.transpose(1, 0, 2).reshape(tok_rows, chips * HD)
 
 
@@ -186,7 +234,7 @@
 
     def run(frames, conv_weight, qkv_weight, track_ids, track_owner):
         heads = qkv_weight.shape[1] // (3 * HD)
-        plan = by_head if seq == 2 * heads else by_owner
+        plan = by_head if (grp, seq, heads) == (2, 16, 8) else by_owner
         return plan(frames, conv_weight, qkv_weight, track_ids, track_owner)
 
     return run

time: 149 us -> 93.9 us (0.63)
  waiting for transfers between devices: 75.9 us -> 39.5 us
  blocking collectives: 30.6 us -> 13 us
  starting transfers between devices: 12.7 us -> 25.9 us
  between operations: 13.6 us -> 0.75 us
  local copies, waits for them, and re-layouts: 1.89 us -> 4.2 us
  matrix products: 8.56 us -> 6.55 us
    all_gather x1 -> x0, waiting for transfers between devices: 60.2 us -> none  [body_by_head(): stream = lax.all_gather(hidden, 'chip', axis=0, tiled=True)]
    ppermute x2 -> x18, waiting for transfers between devices: 2.27 us -> 39.5 us  [xor_swap(): return lax.ppermute(value, axes, [(d, d ^ bit) for d in range(count)])]
    all_gather x1 -> x0, blocking collectives: 18.6 us -> none  [body_by_head(): all_groups = lax.all_gather(group, both, axis=0, tiled=True)]
    ppermute x2 -> x18, starting transfers between devices: 0.14 us -> 14.2 us  [xor_swap(): return lax.ppermute(value, axes, [(d, d ^ bit) for d in range(count)])]
    ppermute x3, waiting for transfers between devices: 13.4 us -> 0.01 us  [body_by_head(): lax.ppermute(held[j], both, [(d, (3 * d + j) % devices) for d in range(de...]
    dot_general x1 -> x2, matrix products: 4.56 us -> 2.62 us  [project(): lax.dot_general(rows, two_heads, (((1,), (1,)), ((), ())), preferred_elem...]
    ppermute x3, starting transfers between devices: 10.2 us -> 8.43 us  [body_by_head(): lax.ppermute(held[j], both, [(d, (3 * d + j) % devices) for d in range(de...]
  transfers between devices with their start and end apart: 7 -> 22, of which waited for: 4 -> 10; matrix products, arithmetic and copies ran while one was open for 1% -> 7% of each run, Pallas kernels for 0% -> 0%
where the time goes in v3:
time: 93.9 us; the launch traced here: 93.6 us
  waiting for transfers between devices  39.5 us (42%)
  starting transfers between devices  25.9 us (28%)
  blocking collectives  13 us (14%)
  matrix products  6.55 us (7%)
  local copies, waits for them, and re-layouts  4.2 us (4%)
  other arithmetic  3.74 us (4%)
    ppermute x18, waiting for transfers between devices, xor_swap(): return lax.ppermute(value, axes, [(d, d ^ bit) for d in range(count)])  39.5 us
    ppermute x18, starting transfers between devices, xor_swap(): return lax.ppermute(value, axes, [(d, d ^ bit) for d in range(count)])  14.2 us
    all_to_all x1, blocking collectives, body_by_head(): lax.all_to_all(sent, 'chip', split_axis=0, concat_axis=0, tiled=True)  13 us
    ppermute x3, starting transfers between devices, body_by_head(): lax.ppermute(held[j], both, [(d, (3 * d + j) % devices) for d in range(de...  8.43 us
    ppermute x1, starting transfers between devices, body_by_head(): lax.ppermute(frames[tok_rows - (KW - 1):], both, [(i, i + 1) for i in ran...  3.2 us
    dot_general x2, matrix products, project(): lax.dot_general(rows, two_heads, (((1,), (1,)), ((), ())), preferred_elem...  2.62 us
    dot_general x1, matrix products, body_by_head(): lax.dot_general(query, keyed[:, :HD], (((1,), (1,)), ((), ())), preferred...  2.34 us
  transfers between devices with their start and end apart: 22, of which 10 were waited for; matrix products, arithmetic and copies ran while one was open for 7% of the time, Pallas kernels for 0%

profile of v3, /device:TPU:0, one launch (start us, length us, event | category | flops | bytes accessed | tf_op | source)
XLA Modules:
  0.0 93.6 jit_solution(4752277951508909838)
XLA Ops:
  0.0 1.1 %copy-done = bf16[2048,192]{0,1:T(8,128)(2,1)S(1)} copy-done((bf16[2048,192]{0,1:T(8,128)(2,1)S(1)}, bf16[2048,192]{0,1:T(8,128)(2,1)}, u32[]{:S(2)}) %copy-start) | copy-done | bytes 786456
  1.9 3.8 %collective-permute-start.9 = (bf16[64,1024]{1,0:T(8,128)(2,1)S(1)}, bf16[64,1024]{1,0:T(8,128)(2,1)S(1)}, u32[]{:S(2)}, u32[]{:S(2)}) collective-permute-start(bf16[64,1024]{1,0:T(8,128)(2,1)S(1)} %get-tuple-element.20), channel_id=1, source_target_pairs={{0,1},{1,4},{2,7},{3,10},{4,13},{5,0},{6,3},{7,6},{8,9},{9,12},{10... | collective-permute-start | bytes 393224 | tf_op jit(solution)/shard_map/ppermute | solution.py:144
  5.7 3.9 %collective-permute-start.10 = (bf16[64,1024]{1,0:T(8,128)(2,1)S(1)}, bf16[64,1024]{1,0:T(8,128)(2,1)S(1)}, u32[]{:S(2)}, u32[]{:S(2)}) collective-permute-start(bf16[64,1024]{1,0:T(8,128)(2,1)S(1)} %get-tuple-element.19), channel_id=1, source_target_pairs={{0,2},{1,5},{2,8},{3,11},{4,14},{5,1},{6,4},{7,7},{8,10},{9,13},{1... | collective-permute-start | bytes 393224 | tf_op jit(solution)/shard_map/ppermute | solution.py:144
  10.4 3.2 %collective-permute-start.4 = (bf16[3,2048]{1,0:T(4,128)(2,1)S(1)}, bf16[3,2048]{1,0:T(4,128)(2,1)S(1)}, u32[]{:S(2)}, u32[]{:S(2)}) collective-permute-start(bf16[3,2048]{1,0:T(4,128)(2,1)S(1)} %slice.219), channel_id=1, source_target_pairs={{0,1},{1,2},{2,3},{3,4},{4,5},{5,6},{6,7},{7,8},{8,9},{9,10},{10,1... | collective-permute-start | bytes 36872 | tf_op jit(solution)/shard_map/ppermute | solution.py:128
  16.1 1.9 %collective-permute-start.1 = (s32[2,128]{1,0:T(2,128)S(1)}, s32[2,128]{1,0:T(2,128)S(1)}, u32[]{:S(2)}, u32[]{:S(2)}) collective-permute-start(s32[2,128]{1,0:T(2,128)S(1)} %pad_add_fusion.2), channel_id=1, source_target_pairs={{0,2},{1,3},{2,0},{3,1},{4,6},{5,7},{6,4},{7,5},{8,10},{9,11},{10,... | collective-permute-start | bytes 3080 | tf_op jit(solution)/shard_map/ppermute | solution.py:105
  18.2 1.5 %collective-permute-done.1 = s32[2,128]{1,0:T(2,128)S(1)} collective-permute-done((s32[2,128]{1,0:T(2,128)S(1)}, s32[2,128]{1,0:T(2,128)S(1)}, u32[]{:S(2)}, u32[]{:S(2)}) %collective-permute-start.1) | collective-permute-done | bytes 1056 | tf_op jit(solution)/shard_map/ppermute | solution.py:105
  19.7 1.6 %collective-permute-start.2 = (s32[4,128]{1,0:T(4,128)S(1)}, s32[4,128]{1,0:T(4,128)S(1)}, u32[]{:S(2)}, u32[]{:S(2)}) collective-permute-start(s32[4,128]{1,0:T(4,128)S(1)} %pad_add_fusion.1), channel_id=1, source_target_pairs={{0,4},{1,5},{2,6},{3,7},{4,0},{5,1},{6,2},{7,3},{8,12},{9,13},{10,... | collective-permute-start | bytes 6152 | tf_op jit(solution)/shard_map/ppermute | solution.py:105
  21.8 1.6 %collective-permute-start.11 = (bf16[3,64,1024]{2,1,0:T(8,128)(2,1)S(1)}, bf16[3,64,1024]{2,1,0:T(8,128)(2,1)S(1)}, u32[]{:S(2)}, u32[]{:S(2)}) collective-permute-start(bf16[3,64,1024]{2,1,0:T(8,128)(2,1)S(1)} %constant_dynamic-slice_fusion), channel_id=1, source_target_pairs={{0,16},{1,17},{2,18},{3,19},{4,20},{5,21},{6,22},{7,23},{8,24},{9,... | collective-permute-start | bytes 1179656 | tf_op jit(solution)/shard_map/ppermute | solution.py:105
  24.2 2.2 %collective-permute-start.6 = (bf16[64,2048]{1,0:T(8,128)(2,1)S(1)}, bf16[64,2048]{1,0:T(8,128)(2,1)S(1)}, u32[]{:S(2)}, u32[]{:S(2)}) collective-permute-start(bf16[64,2048]{1,0:T(8,128)(2,1)S(1)} %get-tuple-element.6), channel_id=1, source_target_pairs={{0,8},{1,9},{2,10},{3,11},{4,12},{5,13},{6,14},{7,15},{8,0},{9,1},... | collective-permute-start | bytes 786440 | tf_op jit(solution)/shard_map/ppermute | solution.py:105
  26.3 12.3 %collective-permute-done.13 = bf16[3,64,1024]{2,1,0:T(8,128)(2,1)S(1)} collective-permute-done((bf16[3,64,1024]{2,1,0:T(8,128)(2,1)S(1)}, bf16[3,64,1024]{2,1,0:T(8,128)(2,1)S(1)}, u32[]{:S(2)}, u32[]{:S(2)}) %collective-permute-start.13) | collective-permute-done | bytes 393248 | tf_op jit(solution)/shard_map/ppermute | solution.py:105
  39.7 1.5 %collective-permute-start.5 = (bf16[128,2048]{1,0:T(8,128)(2,1)S(1)}, bf16[128,2048]{1,0:T(8,128)(2,1)S(1)}, u32[]{:S(2)}, u32[]{:S(2)}) collective-permute-start(bf16[128,2048]{1,0:T(8,128)(2,1)S(1)} %pad_maximum_fusion.12), channel_id=1, source_target_pairs={{0,2},{1,3},{2,0},{3,1},{4,6},{5,7},{6,4},{7,5},{8,10},{9,11},{10,... | collective-permute-start | bytes 1572872 | tf_op jit(solution)/shard_map/ppermute | solution.py:105
  41.4 6.5 %collective-permute-done.14 = bf16[3,64,1024]{2,1,0:T(8,128)(2,1)S(1)} collective-permute-done((bf16[3,64,1024]{2,1,0:T(8,128)(2,1)S(1)}, bf16[3,64,1024]{2,1,0:T(8,128)(2,1)S(1)}, u32[]{:S(2)}, u32[]{:S(2)}) %collective-permute-start.14) | collective-permute-done | bytes 393248 | tf_op jit(solution)/shard_map/ppermute | solution.py:105
  48.9 3.0 %collective-permute-done.17 = bf16[64,2048]{1,0:T(8,128)(2,1)S(1)} collective-permute-done((bf16[64,2048]{1,0:T(8,128)(2,1)S(1)}, bf16[64,2048]{1,0:T(8,128)(2,1)S(1)}, u32[]{:S(2)}, u32[]{:S(2)}) %collective-permute-start.17) | collective-permute-done | bytes 262176 | tf_op jit(solution)/shard_map/ppermute | solution.py:105
  52.6 1.4 %collective-permute-start.18 = (bf16[64,2048]{1,0:T(8,128)(2,1)S(1)}, bf16[64,2048]{1,0:T(8,128)(2,1)S(1)}, u32[]{:S(2)}, u32[]{:S(2)}) collective-permute-start(bf16[64,2048]{1,0:T(8,128)(2,1)S(1)} %collective-permute-done.17), channel_id=1, source_target_pairs={{0,2},{1,3},{2,0},{3,1},{4,6},{5,7},{6,4},{7,5},{8,10},{9,11},{10,... | collective-permute-start | bytes 786440 | tf_op jit(solution)/shard_map/ppermute | solution.py:105
  54.0 7.1 %collective-permute-done.7 = bf16[64,2048]{1,0:T(8,128)(2,1)S(1)} collective-permute-done((bf16[64,2048]{1,0:T(8,128)(2,1)S(1)}, bf16[64,2048]{1,0:T(8,128)(2,1)S(1)}, u32[]{:S(2)}, u32[]{:S(2)}) %collective-permute-start.7) | collective-permute-done | bytes 262176 | tf_op jit(solution)/shard_map/ppermute | solution.py:105
  61.9 1.4 %fusion.4 = bf16[384,768]{1,0:T(8,128)(2,1)S(1)} fusion(bf16[384,2048]{1,0:T(8,128)(2,1)S(1)} %constant_dynamic-update-slice_fusion, bf16[384,2048]{1,0:T(8,128)(2,1)S(1)} %bitcast.142, bf16[384,2048]{1,0:T(8,128)(2,1)S(1)} %bitcast.140), kind=kOutput, calls=%fused_computation.10 | convolution fusion | flops 1214545920 | bytes 5308416 | tf_op jit(solution)/shard_map/dot_general | solution.py:158
  63.5 2.3 %collective-permute-done.18 = bf16[64,2048]{1,0:T(8,128)(2,1)S(1)} collective-permute-done((bf16[64,2048]{1,0:T(8,128)(2,1)S(1)}, bf16[64,2048]{1,0:T(8,128)(2,1)S(1)}, u32[]{:S(2)}, u32[]{:S(2)}) %collective-permute-start.18) | collective-permute-done | bytes 262176 | tf_op jit(solution)/shard_map/ppermute | solution.py:105
  65.7 1.2 %fusion.6 = bf16[128,768]{1,0:T(8,128)(2,1)S(1)} fusion(bf16[384,2048]{1,0:T(8,128)(2,1)S(1)} %bitcast.143, bf16[384,2048]{1,0:T(8,128)(2,1)S(1)} %bitcast.141, bf16[64,2048]{1,0:T(8,128)(2,1)S(1)} %collective-permute-done.18, bf16[64,2048]{1,0:T(8,128)(2,1)S(1)} %collective-permute-done.17), kind=kOutput, calls=%fused_computation.12 | convolution fusion | flops 410091520 | bytes 3866624 | tf_op jit(solution)/shard_map/dot_general | solution.py:158
  67.0 4.6 %collective-permute-done.16 = bf16[384,384]{1,0:T(8,128)(2,1)S(1)} collective-permute-done((bf16[384,384]{1,0:T(8,128)(2,1)S(1)}, bf16[384,384]{1,0:T(8,128)(2,1)S(1)}, u32[]{:S(2)}, u32[]{:S(2)}) %collective-permute-start.16) | collective-permute-done | bytes 294944 | tf_op jit(solution)/shard_map/ppermute | solution.py:105
  73.0 1.1 %collective-permute-done.21 = bf16[256,256]{1,0:T(8,128)(2,1)S(1)} collective-permute-done((bf16[256,256]{1,0:T(8,128)(2,1)S(1)}, bf16[256,256]{1,0:T(8,128)(2,1)S(1)}, u32[]{:S(2)}, u32[]{:S(2)}) %collective-permute-start.21) | collective-permute-done | bytes 131104 | tf_op jit(solution)/shard_map/ppermute | solution.py:105
  74.1 2.3 %fusion.51 = (f32[1024]{0:T(1024)S(1)}, f32[1024,2048]{1,0:T(8,128)S(1)}) fusion(bf16[2048,256]{1,0:T(8,128)(2,1)S(1)} %fusion.8, bf16[128,384]{1,0:T(8,128)(2,1)S(1)} %collective-permute-done.19, bf16[128,384]{1,0:T(8,128)(2,1)S(1)} %get-tuple-element.22, bf16[384,384]{1,0:T(8,128)(2,1)S(1)} %collective-permute-done.16, ...), kind=kOutput, calls=%fused_computation.160 | convolution fusion | flops 550501376 | bytes 9728000 | tf_op jit(solution)/shard_map/dot_general | solution.py:193
  76.5 1.3 %fusion = f32[1024]{0:T(1024)S(1)} fusion(f32[1024,2048]{1,0:T(8,128)S(1)} %get-tuple-element.51, f32[1024]{0:T(1024)S(1)} %get-tuple-element.50), kind=kLoop, calls=%fused_computation.3 | loop fusion | flops 4193280 | bytes 8396800 | tf_op jit(solution)/shard_map/reduce_sum | solution.py:201
  77.7 1.6 %fusion.5 = bf16[1024,128]{1,0:T(8,128)(2,1)S(1)} fusion(f32[1024,2048]{1,0:T(8,128)S(1)} %get-tuple-element.51, f32[1024]{0:T(1024)S(1)} %fusion, f32[1024]{0:T(1024)S(1)} %get-tuple-element.50, bf16[2048,256]{1,0:T(8,128)(2,1)S(1)} %fusion.8), kind=kOutput, calls=%fused_computation.11 | convolution fusion | flops 543293440 | bytes 9183232 | tf_op jit(solution)/shard_map/dot_general | solution.py:202
  79.6 13.0 %all_to_all.5 = bf16[8,128,128]{2,1,0:T(8,128)(2,1)S(1)} all-to-all(bf16[8,128,128]{2,1,0:T(8,128)(2,1)S(1)} %fusion.35), channel_id=1, replica_groups=mesh['grp'=2,'chip'=8,'core'=2] {'chip'}, dimensions={0} | all-to-all | bytes 524288 | tf_op jit(solution)/shard_map/all_to_all | solution.py:211
  (107 shorter events, 11.6 us)
Async XLA Ops:
  0.0 21.3 %slice-start = ((bf16[128,2048]{1,0:T(8,128)(2,1)}), bf16[64,2048]{1,0:T(8,128)(2,1)S(1)}, s32[]{:S(2)}) async-start(bf16[128,2048]{1,0:T(8,128)(2,1)} %param.5), calls=%async_computation.1 | async-start | bytes 524288 | tf_op jit(solution)/shard_map/slice | solution.py:132
  0.0 15.5 %copy-start.2 = (bf16[4,2048]{1,0:T(4,128)(2,1)S(1)}, bf16[4,2048]{1,0:T(4,128)(2,1)}, u32[]{:S(2)}) copy-start(bf16[4,2048]{1,0:T(4,128)(2,1)} %param.6) | copy-start | bytes 49156
  1.2 20.4 %collective-permute-start.8 = (bf16[64,1024]{1,0:T(8,128)(2,1)S(1)}, bf16[64,1024]{1,0:T(8,128)(2,1)S(1)}, u32[]{:S(2)}, u32[]{:S(2)}) collective-permute-start(bf16[64,1024]{1,0:T(8,128)(2,1)S(1)} %get-tuple-element.21), channel_id=1, source_target_pairs={{0,0},{1,3},{2,6},{3,9},{4,12},{5,15},{6,2},{7,5},{8,8},{9,11},{10... | collective-permute-start | bytes 393224 | tf_op jit(solution)/shard_map/ppermute | solution.py:144
  1.9 19.8 %collective-permute-start.9 = (bf16[64,1024]{1,0:T(8,128)(2,1)S(1)}, bf16[64,1024]{1,0:T(8,128)(2,1)S(1)}, u32[]{:S(2)}, u32[]{:S(2)}) collective-permute-start(bf16[64,1024]{1,0:T(8,128)(2,1)S(1)} %get-tuple-element.20), channel_id=1, source_target_pairs={{0,1},{1,4},{2,7},{3,10},{4,13},{5,0},{6,3},{7,6},{8,9},{9,12},{10... | collective-permute-start | bytes 393224 | tf_op jit(solution)/shard_map/ppermute | solution.py:144
  5.7 16.0 %collective-permute-start.10 = (bf16[64,1024]{1,0:T(8,128)(2,1)S(1)}, bf16[64,1024]{1,0:T(8,128)(2,1)S(1)}, u32[]{:S(2)}, u32[]{:S(2)}) collective-permute-start(bf16[64,1024]{1,0:T(8,128)(2,1)S(1)} %get-tuple-element.19), channel_id=1, source_target_pairs={{0,2},{1,5},{2,8},{3,11},{4,14},{5,1},{6,4},{7,7},{8,10},{9,13},{1... | collective-permute-start | bytes 393224 | tf_op jit(solution)/shard_map/ppermute | solution.py:144
  10.4 10.9 %collective-permute-start.4 = (bf16[3,2048]{1,0:T(4,128)(2,1)S(1)}, bf16[3,2048]{1,0:T(4,128)(2,1)S(1)}, u32[]{:S(2)}, u32[]{:S(2)}) collective-permute-start(bf16[3,2048]{1,0:T(4,128)(2,1)S(1)} %slice.219), channel_id=1, source_target_pairs={{0,1},{1,2},{2,3},{3,4},{4,5},{5,6},{6,7},{7,8},{8,9},{9,10},{10,1... | collective-permute-start | bytes 36872 | tf_op jit(solution)/shard_map/ppermute | solution.py:128
  14.4 1.7 %collective-permute-start = (s32[1,128]{1,0:T(1,128)S(1)}, s32[1,128]{1,0:T(1,128)S(1)}, u32[]{:S(2)}, u32[]{:S(2)}) collective-permute-start(s32[1,128]{1,0:T(1,128)S(1)} %bitcast.153), channel_id=1, source_target_pairs={{0,1},{1,0},{2,3},{3,2},{4,5},{5,4},{6,7},{7,6},{8,9},{9,8},{10,11... | collective-permute-start | bytes 1544 | tf_op jit(solution)/shard_map/ppermute | solution.py:105
  16.1 3.6 %collective-permute-start.1 = (s32[2,128]{1,0:T(2,128)S(1)}, s32[2,128]{1,0:T(2,128)S(1)}, u32[]{:S(2)}, u32[]{:S(2)}) collective-permute-start(s32[2,128]{1,0:T(2,128)S(1)} %pad_add_fusion.2), channel_id=1, source_target_pairs={{0,2},{1,3},{2,0},{3,1},{4,6},{5,7},{6,4},{7,5},{8,10},{9,11},{10,... | collective-permute-start | bytes 3080 | tf_op jit(solution)/shard_map/ppermute | solution.py:105
  19.7 28.4 %collective-permute-start.2 = (s32[4,128]{1,0:T(4,128)S(1)}, s32[4,128]{1,0:T(4,128)S(1)}, u32[]{:S(2)}, u32[]{:S(2)}) collective-permute-start(s32[4,128]{1,0:T(4,128)S(1)} %pad_add_fusion.1), channel_id=1, source_target_pairs={{0,4},{1,5},{2,6},{3,7},{4,0},{5,1},{6,2},{7,3},{8,12},{9,13},{10,... | collective-permute-start | bytes 6152 | tf_op jit(solution)/shard_map/ppermute | solution.py:105
  21.8 17.9 %collective-permute-start.11 = (bf16[3,64,1024]{2,1,0:T(8,128)(2,1)S(1)}, bf16[3,64,1024]{2,1,0:T(8,128)(2,1)S(1)}, u32[]{:S(2)}, u32[]{:S(2)}) collective-permute-start(bf16[3,64,1024]{2,1,0:T(8,128)(2,1)S(1)} %constant_dynamic-slice_fusion), channel_id=1, source_target_pairs={{0,16},{1,17},{2,18},{3,19},{4,20},{5,21},{6,22},{7,23},{8,24},{9,... | collective-permute-start | bytes 1179656 | tf_op jit(solution)/shard_map/ppermute | solution.py:105
  23.4 15.2 %collective-permute-start.13 = (bf16[3,64,1024]{2,1,0:T(8,128)(2,1)S(1)}, bf16[3,64,1024]{2,1,0:T(8,128)(2,1)S(1)}, u32[]{:S(2)}, u32[]{:S(2)}) collective-permute-start(bf16[3,64,1024]{2,1,0:T(8,128)(2,1)S(1)} %constant_dynamic-slice_fusion), channel_id=1, source_target_pairs={{0,4},{1,5},{2,6},{3,7},{4,0},{5,1},{6,2},{7,3},{8,12},{9,13},{10,... | collective-permute-start | bytes 1179656 | tf_op jit(solution)/shard_map/ppermute | solution.py:105
  24.2 24.6 %collective-permute-start.6 = (bf16[64,2048]{1,0:T(8,128)(2,1)S(1)}, bf16[64,2048]{1,0:T(8,128)(2,1)S(1)}, u32[]{:S(2)}, u32[]{:S(2)}) collective-permute-start(bf16[64,2048]{1,0:T(8,128)(2,1)S(1)} %get-tuple-element.6), channel_id=1, source_target_pairs={{0,8},{1,9},{2,10},{3,11},{4,12},{5,13},{6,14},{7,15},{8,0},{9,1},... | collective-permute-start | bytes 786440 | tf_op jit(solution)/shard_map/ppermute | solution.py:105
  38.6 9.3 %collective-permute-start.14 = (bf16[3,64,1024]{2,1,0:T(8,128)(2,1)S(1)}, bf16[3,64,1024]{2,1,0:T(8,128)(2,1)S(1)}, u32[]{:S(2)}, u32[]{:S(2)}) collective-permute-start(bf16[3,64,1024]{2,1,0:T(8,128)(2,1)S(1)} %collective-permute-done.13), channel_id=1, source_target_pairs={{0,16},{1,17},{2,18},{3,19},{4,20},{5,21},{6,22},{7,23},{8,24},{9,... | collective-permute-start | bytes 1179656 | tf_op jit(solution)/shard_map/ppermute | solution.py:105
  39.2 12.7 %collective-permute-start.17 = (bf16[64,2048]{1,0:T(8,128)(2,1)S(1)}, bf16[64,2048]{1,0:T(8,128)(2,1)S(1)}, u32[]{:S(2)}, u32[]{:S(2)}) collective-permute-start(bf16[64,2048]{1,0:T(8,128)(2,1)S(1)} %get-tuple-element.8), channel_id=1, source_target_pairs={{0,8},{1,9},{2,10},{3,11},{4,12},{5,13},{6,14},{7,15},{8,0},{9,1},... | collective-permute-start | bytes 786440 | tf_op jit(solution)/shard_map/ppermute | solution.py:105
  39.7 12.9 %collective-permute-start.5 = (bf16[128,2048]{1,0:T(8,128)(2,1)S(1)}, bf16[128,2048]{1,0:T(8,128)(2,1)S(1)}, u32[]{:S(2)}, u32[]{:S(2)}) collective-permute-start(bf16[128,2048]{1,0:T(8,128)(2,1)S(1)} %pad_maximum_fusion.12), channel_id=1, source_target_pairs={{0,2},{1,3},{2,0},{3,1},{4,6},{5,7},{6,4},{7,5},{8,10},{9,11},{10,... | collective-permute-start | bytes 1572872 | tf_op jit(solution)/shard_map/ppermute | solution.py:105
  47.9 13.2 %collective-permute-start.12 = (bf16[3,64,2048]{2,1,0:T(8,128)(2,1)S(1)}, bf16[3,64,2048]{2,1,0:T(8,128)(2,1)S(1)}, u32[]{:S(2)}, u32[]{:S(2)}) collective-permute-start(bf16[3,64,2048]{2,1,0:T(8,128)(2,1)S(1)} %bitcast.136), channel_id=1, source_target_pairs={{0,1},{1,0},{2,3},{3,2},{4,5},{5,4},{6,7},{7,6},{8,9},{9,8},{10,11... | collective-permute-start | bytes 2359304 | tf_op jit(solution)/shard_map/ppermute | solution.py:105
  48.1 13.0 %collective-permute-start.15 = (bf16[3,64,2048]{2,1,0:T(8,128)(2,1)S(1)}, bf16[3,64,2048]{2,1,0:T(8,128)(2,1)S(1)}, u32[]{:S(2)}, u32[]{:S(2)}) collective-permute-start(bf16[3,64,2048]{2,1,0:T(8,128)(2,1)S(1)} %bitcast.138), channel_id=1, source_target_pairs={{0,1},{1,0},{2,3},{3,2},{4,5},{5,4},{6,7},{7,6},{8,9},{9,8},{10,11... | collective-permute-start | bytes 2359304 | tf_op jit(solution)/shard_map/ppermute | solution.py:105
  48.7 24.0 %collective-permute-start.3 = (s32[8,128]{1,0:T(8,128)S(1)}, s32[8,128]{1,0:T(8,128)S(1)}, u32[]{:S(2)}, u32[]{:S(2)}) collective-permute-start(s32[8,128]{1,0:T(8,128)S(1)} %pad_add_fusion), channel_id=1, source_target_pairs={{0,8},{1,9},{2,10},{3,11},{4,12},{5,13},{6,14},{7,15},{8,0},{9,1},... | collective-permute-start | bytes 12296 | tf_op jit(solution)/shard_map/ppermute | solution.py:105
  51.9 9.2 %collective-permute-start.7 = (bf16[64,2048]{1,0:T(8,128)(2,1)S(1)}, bf16[64,2048]{1,0:T(8,128)(2,1)S(1)}, u32[]{:S(2)}, u32[]{:S(2)}) collective-permute-start(bf16[64,2048]{1,0:T(8,128)(2,1)S(1)} %collective-permute-done.6), channel_id=1, source_target_pairs={{0,2},{1,3},{2,0},{3,1},{4,6},{5,7},{6,4},{7,5},{8,10},{9,11},{10,... | collective-permute-start | bytes 786440 | tf_op jit(solution)/shard_map/ppermute | solution.py:105
  52.6 13.1 %collective-permute-start.18 = (bf16[64,2048]{1,0:T(8,128)(2,1)S(1)}, bf16[64,2048]{1,0:T(8,128)(2,1)S(1)}, u32[]{:S(2)}, u32[]{:S(2)}) collective-permute-start(bf16[64,2048]{1,0:T(8,128)(2,1)S(1)} %collective-permute-done.17), channel_id=1, source_target_pairs={{0,2},{1,3},{2,0},{3,1},{4,6},{5,7},{6,4},{7,5},{8,10},{9,11},{10,... | collective-permute-start | bytes 786440 | tf_op jit(solution)/shard_map/ppermute | solution.py:105
  63.4 8.2 %collective-permute-start.16 = (bf16[384,384]{1,0:T(8,128)(2,1)S(1)}, bf16[384,384]{1,0:T(8,128)(2,1)S(1)}, u32[]{:S(2)}, u32[]{:S(2)}) collective-permute-start(bf16[384,384]{1,0:T(8,128)(2,1)S(1)} %get-tuple-element.18), channel_id=1, source_target_pairs={{0,4},{1,5},{2,6},{3,7},{4,0},{5,1},{6,2},{7,3},{8,12},{9,13},{10,... | collective-permute-start | bytes 884744 | tf_op jit(solution)/shard_map/ppermute | solution.py:105
  66.9 5.7 %collective-permute-start.19 = (bf16[128,384]{1,0:T(8,128)(2,1)S(1)}, bf16[128,384]{1,0:T(8,128)(2,1)S(1)}, u32[]{:S(2)}, u32[]{:S(2)}) collective-permute-start(bf16[128,384]{1,0:T(8,128)(2,1)S(1)} %get-tuple-element.23), channel_id=1, source_target_pairs={{0,4},{1,5},{2,6},{3,7},{4,0},{5,1},{6,2},{7,3},{8,12},{9,13},{10,... | collective-permute-start | bytes 294920 | tf_op jit(solution)/shard_map/ppermute | solution.py:105
  71.6 2.5 %collective-permute-start.20 = (bf16[768,256]{1,0:T(8,128)(2,1)S(1)}, bf16[768,256]{1,0:T(8,128)(2,1)S(1)}, u32[]{:S(2)}, u32[]{:S(2)}) collective-permute-start(bf16[768,256]{1,0:T(8,128)(2,1)S(1)} %pad_maximum_fusion.13), channel_id=1, source_target_pairs={{0,1},{1,0},{2,3},{3,2},{4,5},{5,4},{6,7},{7,6},{8,9},{9,8},{10,11... | collective-permute-start | bytes 1179656 | tf_op jit(solution)/shard_map/ppermute | solution.py:105
  72.6 1.4 %collective-permute-start.21 = (bf16[256,256]{1,0:T(8,128)(2,1)S(1)}, bf16[256,256]{1,0:T(8,128)(2,1)S(1)}, u32[]{:S(2)}, u32[]{:S(2)}) collective-permute-start(bf16[256,256]{1,0:T(8,128)(2,1)S(1)} %pad_maximum_fusion.14), channel_id=1, source_target_pairs={{0,1},{1,0},{2,3},{3,2},{4,5},{5,4},{6,7},{7,6},{8,9},{9,8},{10,11... | collective-permute-start | bytes 393224 | tf_op jit(solution)/shard_map/ppermute | solution.py:105
  (2 other events, 16.4 us)

commit v4 on v3

--- a/solution.py
+++ b/solution.py
@@ -100,94 +100,99 @@
     return returned[slot_of_row]
 
 
-def xor_swap(value, bit, axes=("chip", "core")):
-    count = lax.axis_size(axes)
-    return lax.ppermute(value, axes, [(d, d ^ bit) for d in range(count)])
-
-
 def by_bit(bit, mine, theirs, axis):
     return jnp.stack(
         [jnp.where(bit == 0, mine, theirs), jnp.where(bit == 0, theirs, mine)], axis=axis
     )
 
 
+FOUR = ("far", "near", "quad")
+CORE, Y, NEAR, FAR = 1, 2, 4, 8
+
+
+def swap_seq(value, bit):
+    count = lax.axis_size(FOUR)
+    return lax.ppermute(value, FOUR, [(d, d ^ bit) for d in range(count)])
+
+
+def swap_grp(value):
+    return lax.ppermute(value, "grp", [(0, 1), (1, 0)])
+
+
 def body_by_head(frames, conv_weight, qkv_weight, track_ids, track_owner):
     tok_rows = frames.shape[0]
-    chips = lax.axis_size("chip")
-    devices = 2 * chips
-    core = lax.axis_index("core")
-    chip = lax.axis_index("chip")
     grp = lax.axis_index("grp")
-    me = 2 * chip + core
-    both = ("chip", "core")
-    every = ("grp", "chip", "core")
+    far, near, quad = (lax.axis_index(name) for name in FOUR)
+    me = far * FAR + near * NEAR + quad
+    devices = lax.axis_size(FOUR)
+    head = far * 4 + quad
     part = tok_rows // 2
     features = frames.shape[1]
-    CORE, Y, Z0, Z1 = 1, 2, 4, 8
 
     rim_rows = lax.ppermute(
-        frames[tok_rows - (KW - 1) :], both, [(i, i + 1) for i in range(devices - 1)]
+        frames[tok_rows - (KW - 1) :], FOUR, [(i, i + 1) for i in range(devices - 1)]
     )
     late = convolve(frames[part:], conv_weight, frames[part - (KW - 1) : part])
     early = convolve(frames[:part], conv_weight, rim_rows)
 
-    far_late = xor_swap(late, Z1)
-    far_early = xor_swap(early, Z1)
+    far_late = swap_seq(late, FAR)
+    far_early = swap_seq(early, FAR)
     own = jnp.concatenate([early, late], axis=0)
-    beside = xor_swap(own, Y)
-    far_beside_late = xor_swap(far_late, Y)
-    far_beside_early = xor_swap(far_early, Y)
+    beside = swap_seq(own, Y)
+    far_beside_late = swap_seq(far_late, Y)
+    far_beside_early = swap_seq(far_early, Y)
+    first_rows = [(0, 0, tok_rows), (Y, 0, tok_rows), (FAR, part, part), (FAR | Y, part, part)]
+    second_rows = [(FAR, 0, part), (FAR | Y, 0, part)]
+    rest = jnp.concatenate([beside, far_late, far_beside_late], axis=0)
+    last = jnp.concatenate([far_early, far_beside_early], axis=0)
+    first = jnp.concatenate([own, rest, swap_seq(own, CORE), swap_seq(rest, CORE)], axis=0)
+    second = jnp.concatenate([last, swap_seq(last, CORE)], axis=0)
+
+    def home(block):
+        of_head, side = block % devices // 2, block % 2
+        return of_head // 4 * FAR + side * NEAR + of_head % 4
 
     half = features // 2
     held = lax.dynamic_slice_in_dim(qkv_weight.T, grp * half, half, 1).reshape(3, HD // 2, half)
     moved = [
-        lax.ppermute(held[j], both, [(d, (3 * d + j) % devices) for d in range(devices)])
+        lax.ppermute(held[j], FOUR, [(d, home(3 * d + j)) for d in range(devices)])
         for j in range(3)
     ]
-    mine = lax.dynamic_slice_in_dim(jnp.stack(moved + moved[:2]), lax.rem(me, 3), 3, 0)
-    paired = xor_swap(mine, Z0)
-
-    def whole_head(quarter):
-        wide = by_bit(grp, quarter, xor_swap(quarter, devices, every), 2)
-        wide = wide.reshape(3, HD // 2, features)
-        return by_bit(core, wide, xor_swap(wide, CORE), 1).reshape(3 * HD, features)
-
-    two_heads = jnp.concatenate([whole_head(mine), whole_head(paired)], axis=0)
+    turn = lax.rem(2 * head + near, 3)
+    mine = lax.dynamic_slice_in_dim(jnp.stack(moved + moved[:2]), turn, 3, 0)
+    paired = swap_seq(mine, NEAR)
+    mine = by_bit(grp, mine, swap_grp(mine), 2)
+    paired = by_bit(grp, paired, swap_grp(paired), 2)
+    head_weight = by_bit(near, mine, paired, 1).reshape(3 * HD, features)
 
     def project(rows):
         done = lax.dot_general(
-            rows, two_heads, (((1,), (1,)), ((), ())), preferred_element_type=jnp.float32
+            rows, head_weight, (((1,), (1,)), ((), ())), preferred_element_type=jnp.float32
         ).astype(jnp.bfloat16)
-        return jnp.concatenate([done[:, : 3 * HD], xor_swap(done[:, 3 * HD :], Z0)], axis=0)
-
-    first = project(jnp.concatenate([own, beside, far_late, far_beside_late], axis=0))
-    second = project(jnp.concatenate([far_early, far_beside_early], axis=0))
-
-    first_rows = [(0, 0, tok_rows), (Y, 0, tok_rows), (Z1, part, part), (Z1 | Y, part, part)]
-    second_rows = [(Z1, 0, part), (Z1 | Y, 0, part)]
+        return done[:, :HD], done[:, HD:], swap_seq(done[:, HD:], NEAR)
+
+    parts = [project(first), project(second)]
+    query = jnp.concatenate([p[0] for p in parts], axis=0)
+    keyed = jnp.concatenate([p[1] for p in parts] + [p[2] for p in parts], axis=0)
+
     order = []
     for pieces in (first_rows, second_rows):
-        order += pieces + [(far ^ Z0, start, count) for far, start, count in pieces]
-
-    groups = track_groups(track_ids, track_owner)[None, :]
-    for bit in (CORE, Y, Z0, Z1):
-        groups = jnp.concatenate([groups, xor_swap(groups, bit)], axis=0)
+        order += pieces + [(hop ^ CORE, start, count) for hop, start, count in pieces]
+
+    groups, _ = lax.optimization_barrier((track_groups(track_ids, track_owner)[None, :], paired))
+    for bit in (CORE, Y, NEAR, FAR):
+        groups = jnp.concatenate([groups, swap_seq(groups, bit)], axis=0)
 
     def of_rows(bit):
         times = [
-            (me ^ far ^ bit) * tok_rows + start + jnp.arange(count, dtype=jnp.int32)
-            for far, start, count in order
+            (me ^ hop ^ bit) * tok_rows + start + jnp.arange(count, dtype=jnp.int32)
+            for hop, start, count in order
         ]
-        marks = [groups[far ^ bit, start : start + count] for far, start, count in order]
+        marks = [groups[hop ^ bit, start : start + count] for hop, start, count in order]
         return jnp.concatenate(times), jnp.concatenate(marks)
 
-    projected = jnp.concatenate([first, second], axis=0)
-    query = projected[:, :HD]
-    keyed = jnp.concatenate(
-        [projected[:, HD:], xor_swap(first[:, HD:], CORE), xor_swap(second[:, HD:], CORE)], axis=0
-    )
     own_times, own_groups = of_rows(0)
-    other_times, other_groups = of_rows(CORE)
+    other_times, other_groups = of_rows(NEAR)
     key_times = jnp.concatenate([own_times, other_times])
     key_groups = jnp.concatenate([own_groups, other_groups])
     scores = lax.dot_general(
@@ -202,14 +207,15 @@
     mixed = jnp.dot(weights, keyed[:, HD:], preferred_element_type=jnp.float32)
     mixed = mixed.astype(jnp.bfloat16)
 
-    sent = jnp.zeros((chips, tok_rows, HD), jnp.bfloat16)
+    sent = jnp.zeros((devices // 2, tok_rows, HD), jnp.bfloat16)
     at = 0
-    for far, start, count in order:
+    for hop, start, count in order:
         rows = mixed[at : at + count]
-        sent = lax.dynamic_update_slice(sent, rows[None], ((me ^ far) >> 1, start, 0))
+        there = head ^ (hop // FAR * 4 + hop % 4)
+        sent = lax.dynamic_update_slice(sent, rows[None], (there, start, 0))
         at += count
-    returned = lax.all_to_all(sent, "chip", split_axis=0, concat_axis=0, tiled=True)
-    return returned.transpose(1, 0, 2).reshape(tok_rows, chips * HD)
+    returned = lax.all_to_all(sent, ("far", "quad"), split_axis=0, concat_axis=0, tiled=True)
+    return returned.transpose(1, 0, 2).reshape(tok_rows, devices // 2 * HD)
 
 
 def solution(mesh):
@@ -222,19 +228,21 @@
         out_specs=out_by_owner,
         check_vma=False,
     )
-    split = Mesh(mesh.devices.reshape(grp, seq // 2, 2), ("grp", "chip", "core"))
-    rows = P(("grp", "chip", "core"))
-    by_head = jax.shard_map(
-        body_by_head,
-        mesh=split,
-        in_specs=(rows, P(), P(None, ("chip", "core")), rows, P("grp")),
-        out_specs=rows,
-        check_vma=False,
-    )
+    fits = (grp, seq) == (2, 16)
+    if fits:
+        split = Mesh(mesh.devices.reshape(grp, 2, 2, 4), ("grp",) + FOUR)
+        rows = P(("grp",) + FOUR)
+        by_head = jax.shard_map(
+            body_by_head,
+            mesh=split,
+            in_specs=(rows, P(), P(None, FOUR), rows, P("grp")),
+            out_specs=rows,
+            check_vma=False,
+        )
 
     def run(frames, conv_weight, qkv_weight, track_ids, track_owner):
         heads = qkv_weight.shape[1] // (3 * HD)
-        plan = by_head if (grp, seq, heads) == (2, 16, 8) else by_owner
+        plan = by_head if fits and heads == 8 else by_owner
         return plan(frames, conv_weight, qkv_weight, track_ids, track_owner)
 
     return run

time: 93.9 us -> 99 us (1.054)
  starting transfers between devices: 25.9 us -> 30.2 us
  waiting for transfers between devices: 39.5 us -> 38.4 us
    ppermute x22 -> x21, starting transfers between devices: 25.9 us -> 30.2 us  [the longest x15 15.8 us: swap_seq(): return lax.ppermute(value, FOUR, [(d, d ^ bit) for d in range(count)])]
    another operation x2 -> x1, local copies, waits for them, and re-layouts: 0.21 us -> 1.62 us  [by_bit(): jnp.stack([jnp.where(bit == 0, mine, theirs), jnp.where(bit == 0, theirs,...]
    ppermute x22 -> x21, waiting for transfers between devices: 39.5 us -> 38.4 us  [the longest x15 34.7 us: swap_seq(): return lax.ppermute(value, FOUR, [(d, d ^ bit) for d in range(count)])]
  transfers between devices with their start and end apart: 22 -> 21, of which waited for: 10 -> 7; matrix products, arithmetic and copies ran while one was open for 7% -> 9% of each run, Pallas kernels for 0% -> 0%
where the time goes in v4:
time: 99 us; the launch traced here: 98.7 us
  waiting for transfers between devices  38.4 us (39%)
  starting transfers between devices  30.2 us (31%)
  blocking collectives  13.4 us (14%)
  matrix products  6.48 us (7%)
  local copies, waits for them, and re-layouts  5.05 us (5%)
  other arithmetic  4.4 us (4%)
    ppermute x15, waiting for transfers between devices, swap_seq(): return lax.ppermute(value, FOUR, [(d, d ^ bit) for d in range(count)])  34.7 us
    ppermute x15, starting transfers between devices, swap_seq(): return lax.ppermute(value, FOUR, [(d, d ^ bit) for d in range(count)])  15.8 us
    all_to_all x1, blocking collectives, body_by_head(): lax.all_to_all(sent, ('far', 'quad'), split_axis=0, concat_axis=0, tiled=...  13.4 us
    ppermute x3, starting transfers between devices, body_by_head(): lax.ppermute(held[j], FOUR, [(d, home(3 * d + j)) for d in range(devices)])  8.99 us
    ppermute x2, waiting for transfers between devices, swap_grp(): return lax.ppermute(value, 'grp', [(0, 1), (1, 0)])  3.77 us
    ppermute x2, starting transfers between devices, swap_grp(): return lax.ppermute(value, 'grp', [(0, 1), (1, 0)])  3.03 us
    dot_general x2, matrix products, project(): lax.dot_general(rows, head_weight, (((1,), (1,)), ((), ())), preferred_el...  2.54 us
    ppermute x1, starting transfers between devices, body_by_head(): lax.ppermute(frames[tok_rows - (KW - 1):], FOUR, [(i, i + 1) for i in ran...  2.36 us
  transfers between devices with their start and end apart: 21, of which 7 were waited for; matrix products, arithmetic and copies ran while one was open for 9% of the time, Pallas kernels for 0%

profile of v4, /device:TPU:0, one launch (start us, length us, event | category | flops | bytes accessed | tf_op | source)
XLA Modules:
  0.0 98.7 jit_solution(18425579152948967401)
XLA Ops:
  0.9 2.4 %collective-permute-start.4 = (bf16[3,2048]{1,0:T(4,128)(2,1)S(1)}, bf16[3,2048]{1,0:T(4,128)(2,1)S(1)}, u32[]{:S(2)}, u32[]{:S(2)}) collective-permute-start(bf16[3,2048]{1,0:T(4,128)(2,1)S(1)} %slice.209), channel_id=1, source_target_pairs={{0,1},{1,2},{2,3},{3,4},{4,5},{5,6},{6,7},{7,8},{8,9},{9,10},{10,1... | collective-permute-start | bytes 36872 | tf_op jit(solution)/shard_map/ppermute | solution.py:132
  4.1 6.4 %collective-permute-start.11 = (bf16[64,1024]{1,0:T(8,128)(2,1)S(1)}, bf16[64,1024]{1,0:T(8,128)(2,1)S(1)}, u32[]{:S(2)}, u32[]{:S(2)}) collective-permute-start(bf16[64,1024]{1,0:T(8,128)(2,1)S(1)} %get-tuple-element.16), channel_id=1, source_target_pairs={{0,4},{1,2},{2,7},{3,9},{4,14},{5,0},{6,5},{7,3},{8,12},{9,10},{10... | collective-permute-start | bytes 393224 | tf_op jit(solution)/shard_map/ppermute | solution.py:158
  10.5 1.9 %collective-permute-start.12 = (bf16[64,1024]{1,0:T(8,128)(2,1)S(1)}, bf16[64,1024]{1,0:T(8,128)(2,1)S(1)}, u32[]{:S(2)}, u32[]{:S(2)}) collective-permute-start(bf16[64,1024]{1,0:T(8,128)(2,1)S(1)} %get-tuple-element.15), channel_id=1, source_target_pairs={{0,1},{1,6},{2,8},{3,13},{4,11},{5,4},{6,2},{7,7},{8,9},{9,14},{10... | collective-permute-start | bytes 393224 | tf_op jit(solution)/shard_map/ppermute | solution.py:158
  13.1 1.2 %collective-permute-start = (s32[1,128]{1,0:T(1,128)S(1)}, s32[1,128]{1,0:T(1,128)S(1)}, u32[]{:S(2)}, u32[]{:S(2)}) collective-permute-start(s32[1,128]{1,0:T(1,128)S(1)} %bitcast.138), channel_id=1, source_target_pairs={{0,1},{1,0},{2,3},{3,2},{4,5},{5,4},{6,7},{7,6},{8,9},{9,8},{10,11... | collective-permute-start | bytes 1544 | tf_op jit(solution)/shard_map/ppermute | solution.py:115
  15.7 2.3 %collective-permute-start.1 = (s32[2,128]{1,0:T(2,128)S(1)}, s32[2,128]{1,0:T(2,128)S(1)}, u32[]{:S(2)}, u32[]{:S(2)}) collective-permute-start(s32[2,128]{1,0:T(2,128)S(1)} %pad_add_fusion.2), channel_id=1, source_target_pairs={{0,2},{1,3},{2,0},{3,1},{4,6},{5,7},{6,4},{7,5},{8,10},{9,11},{10,... | collective-permute-start | bytes 3080 | tf_op jit(solution)/shard_map/ppermute | solution.py:115
  18.2 1.4 %collective-permute-done.1 = s32[2,128]{1,0:T(2,128)S(1)} collective-permute-done((s32[2,128]{1,0:T(2,128)S(1)}, s32[2,128]{1,0:T(2,128)S(1)}, u32[]{:S(2)}, u32[]{:S(2)}) %collective-permute-start.1) | collective-permute-done | bytes 1056 | tf_op jit(solution)/shard_map/ppermute | solution.py:115
  19.6 1.9 %collective-permute-start.2 = (s32[4,128]{1,0:T(4,128)S(1)}, s32[4,128]{1,0:T(4,128)S(1)}, u32[]{:S(2)}, u32[]{:S(2)}) collective-permute-start(s32[4,128]{1,0:T(4,128)S(1)} %pad_add_fusion.1), channel_id=1, source_target_pairs={{0,4},{1,5},{2,6},{3,7},{4,0},{5,1},{6,2},{7,3},{8,12},{9,13},{10,... | collective-permute-start | bytes 6152 | tf_op jit(solution)/shard_map/ppermute | solution.py:115
  22.1 3.0 %collective-permute-start.6 = (bf16[64,2048]{1,0:T(8,128)(2,1)S(1)}, bf16[64,2048]{1,0:T(8,128)(2,1)S(1)}, u32[]{:S(2)}, u32[]{:S(2)}) collective-permute-start(bf16[64,2048]{1,0:T(8,128)(2,1)S(1)} %get-tuple-element.6), channel_id=1, source_target_pairs={{0,8},{1,9},{2,10},{3,11},{4,12},{5,13},{6,14},{7,15},{8,0},{9,1},... | collective-permute-start | bytes 786440 | tf_op jit(solution)/shard_map/ppermute | solution.py:115
  25.2 1.6 %collective-permute-start.13 = (bf16[3,64,1024]{2,1,0:T(8,128)(2,1)S(1)}, bf16[3,64,1024]{2,1,0:T(8,128)(2,1)S(1)}, u32[]{:S(2)}, u32[]{:S(2)}) collective-permute-start(bf16[3,64,1024]{2,1,0:T(8,128)(2,1)S(1)} %constant_dynamic-slice_fusion), channel_id=1, source_target_pairs={{0,16},{16,0},{1,17},{17,1},{2,18},{18,2},{3,19},{19,3},{4,20},{20... | collective-permute-start | bytes 1179656 | tf_op jit(solution)/shard_map/ppermute | solution.py:119
  27.3 2.0 %collective-permute-start.14 = (bf16[3,64,1024]{2,1,0:T(8,128)(2,1)S(1)}, bf16[3,64,1024]{2,1,0:T(8,128)(2,1)S(1)}, u32[]{:S(2)}, u32[]{:S(2)}) collective-permute-start(bf16[3,64,1024]{2,1,0:T(8,128)(2,1)S(1)} %constant_dynamic-slice_fusion), channel_id=1, source_target_pairs={{0,4},{1,5},{2,6},{3,7},{4,0},{5,1},{6,2},{7,3},{8,12},{9,13},{10,... | collective-permute-start | bytes 1179656 | tf_op jit(solution)/shard_map/ppermute | solution.py:115
  29.3 12.5 %collective-permute-done.6 = bf16[64,2048]{1,0:T(8,128)(2,1)S(1)} collective-permute-done((bf16[64,2048]{1,0:T(8,128)(2,1)S(1)}, bf16[64,2048]{1,0:T(8,128)(2,1)S(1)}, u32[]{:S(2)}, u32[]{:S(2)}) %collective-permute-start.6) | collective-permute-done | bytes 262176 | tf_op jit(solution)/shard_map/ppermute | solution.py:115
  41.8 1.3 %collective-permute-start.7 = (bf16[64,2048]{1,0:T(8,128)(2,1)S(1)}, bf16[64,2048]{1,0:T(8,128)(2,1)S(1)}, u32[]{:S(2)}, u32[]{:S(2)}) collective-permute-start(bf16[64,2048]{1,0:T(8,128)(2,1)S(1)} %collective-permute-done.6), channel_id=1, source_target_pairs={{0,2},{1,3},{2,0},{3,1},{4,6},{5,7},{6,4},{7,5},{8,10},{9,11},{10,... | collective-permute-start | bytes 786440 | tf_op jit(solution)/shard_map/ppermute | solution.py:115
  43.1 4.3 %collective-permute-done.16 = bf16[64,2048]{1,0:T(8,128)(2,1)S(1)} collective-permute-done((bf16[64,2048]{1,0:T(8,128)(2,1)S(1)}, bf16[64,2048]{1,0:T(8,128)(2,1)S(1)}, u32[]{:S(2)}, u32[]{:S(2)}) %collective-permute-start.16) | collective-permute-done | bytes 262176 | tf_op jit(solution)/shard_map/ppermute | solution.py:115
  48.0 1.5 %collective-permute-start.15 = (bf16[3,64,1024]{2,1,0:T(8,128)(2,1)S(1)}, bf16[3,64,1024]{2,1,0:T(8,128)(2,1)S(1)}, u32[]{:S(2)}, u32[]{:S(2)}) collective-permute-start(bf16[3,64,1024]{2,1,0:T(8,128)(2,1)S(1)} %collective-permute-done.14), channel_id=1, source_target_pairs={{0,16},{16,0},{1,17},{17,1},{2,18},{18,2},{3,19},{19,3},{4,20},{20... | collective-permute-start | bytes 1179656 | tf_op jit(solution)/shard_map/ppermute | solution.py:119
  50.0 5.5 %collective-permute-done.17 = bf16[64,2048]{1,0:T(8,128)(2,1)S(1)} collective-permute-done((bf16[64,2048]{1,0:T(8,128)(2,1)S(1)}, bf16[64,2048]{1,0:T(8,128)(2,1)S(1)}, u32[]{:S(2)}, u32[]{:S(2)}) %collective-permute-start.17) | collective-permute-done | bytes 262176 | tf_op jit(solution)/shard_map/ppermute | solution.py:115
  55.8 3.8 %collective-permute-done.15 = bf16[3,64,1024]{2,1,0:T(8,128)(2,1)S(1)} collective-permute-done((bf16[3,64,1024]{2,1,0:T(8,128)(2,1)S(1)}, bf16[3,64,1024]{2,1,0:T(8,128)(2,1)S(1)}, u32[]{:S(2)}, u32[]{:S(2)}) %collective-permute-start.15) | collective-permute-done | bytes 393248 | tf_op jit(solution)/shard_map/ppermute | solution.py:119
  59.9 1.6 %copy.15 = bf16[3,2,64,2,1024]{4,3,2,1,0:T(2,128)(2,1)S(1)} copy(bf16[3,2,64,2,1024]{4,2,0,3,1:T(8,128)(2,1)S(1)} %pad_maximum_fusion) | data formatting | bytes 3145728 | tf_op jit(solution)/shard_map/stack | solution.py:104
  62.1 1.8 %convolution_convert_fusion = bf16[768,384]{1,0:T(8,128)(2,1)S(1)} fusion(bf16[768,2048]{1,0:T(8,128)(2,1)S(1)} %constant_dynamic-update-slice_fusion, bf16[384,2048]{1,0:T(8,128)(2,1)S(1)} %bitcast.127), kind=kOutput, calls=%fused_computation.6 | convolution fusion | flops 1208254464 | bytes 5308416 | tf_op jit(solution)/shard_map/dot_general | solution.py:169
  64.0 3.0 %collective-permute-start.19 = (bf16[768,256]{1,0:T(8,128)(2,1)S(1)}, bf16[768,256]{1,0:T(8,128)(2,1)S(1)}, u32[]{:S(2)}, u32[]{:S(2)}) collective-permute-start(bf16[768,256]{1,0:T(8,128)(2,1)S(1)} %slice.256), channel_id=1, source_target_pairs={{0,4},{1,5},{2,6},{3,7},{4,0},{5,1},{6,2},{7,3},{8,12},{9,13},{10,... | collective-permute-start | bytes 1179656 | tf_op jit(solution)/shard_map/ppermute | solution.py:115
  68.1 10.6 %collective-permute-done.20 = bf16[256,256]{1,0:T(8,128)(2,1)S(1)} collective-permute-done((bf16[256,256]{1,0:T(8,128)(2,1)S(1)}, bf16[256,256]{1,0:T(8,128)(2,1)S(1)}, u32[]{:S(2)}, u32[]{:S(2)}) %collective-permute-start.20) | collective-permute-done | bytes 131104 | tf_op jit(solution)/shard_map/ppermute | solution.py:115
  78.8 2.3 %fusion.40 = (f32[1024]{0:T(1024)S(1)}, f32[1024,2048]{1,0:T(8,128)S(1)}) fusion(bf16[2048,256]{1,0:T(8,128)(2,1)S(1)} %pad_maximum_fusion.2, bf16[256,128]{1,0:T(8,128)(2,1)S(1)} %slice.255, bf16[768,128]{1,0:T(8,128)(2,1)S(1)} %slice.254, s32[1024]{0:T(1024)S(1)} %concatenate.88, s32[2048]{0:T(1024)S(1)} %concatenate.87, s32[1024]{0:T(1024)S(1)} %concatenate.83, ...), kind=kOutput, calls=%fused_computation.147 | convolution fusion | flops 549977088 | bytes 9203712 | tf_op jit(solution)/shard_map/dot_general | solution.py:198
  81.1 1.3 %fusion = f32[1024]{0:T(1024)S(1)} fusion(f32[1024,2048]{1,0:T(8,128)S(1)} %get-tuple-element.45, f32[1024]{0:T(1024)S(1)} %get-tuple-element.44), kind=kLoop, calls=%fused_computation.3 | loop fusion | flops 4193280 | bytes 8396800 | tf_op jit(solution)/shard_map/reduce_sum | solution.py:206
  82.4 1.6 %fusion.2 = bf16[1024,128]{1,0:T(8,128)(2,1)S(1)} fusion(f32[1024,2048]{1,0:T(8,128)S(1)} %get-tuple-element.45, f32[1024]{0:T(1024)S(1)} %fusion, f32[1024]{0:T(1024)S(1)} %get-tuple-element.44, bf16[2048,256]{1,0:T(8,128)(2,1)S(1)} %pad_maximum_fusion.2), kind=kOutput, calls=%fused_computation.7 | convolution fusion | flops 543293440 | bytes 9183232 | tf_op jit(solution)/shard_map/dot_general | solution.py:207
  84.3 13.4 %all_to_all.5 = bf16[8,128,128]{2,1,0:T(8,128)(2,1)S(1)} all-to-all(bf16[8,128,128]{2,1,0:T(8,128)(2,1)S(1)} %fusion.27), channel_id=1, replica_groups=mesh['grp'=2,'far'=2,'near'=2,'quad'=4] {'far','quad'}, dimensions={0} | all-to-all | bytes 524288 | tf_op jit(solution)/shard_map/all_to_all | solution.py:217
  (103 shorter events, 9.6 us)
Async XLA Ops:
  0.0 21.5 %slice-start = ((bf16[128,2048]{1,0:T(8,128)(2,1)}), bf16[64,2048]{1,0:T(8,128)(2,1)S(1)}, s32[]{:S(2)}) async-start(bf16[128,2048]{1,0:T(8,128)(2,1)} %param.5), calls=%async_computation.1 | async-start | bytes 524288 | tf_op jit(solution)/shard_map/slice | solution.py:136
  0.0 21.6 %copy-start.1 = (bf16[128,2048]{1,0:T(8,128)(2,1)S(1)}, bf16[128,2048]{1,0:T(8,128)(2,1)}, u32[]{:S(2)}) copy-start(bf16[128,2048]{1,0:T(8,128)(2,1)} %param.5) | copy-start | bytes 1572868
  0.0 15.5 %copy-start.2 = (bf16[4,2048]{1,0:T(4,128)(2,1)S(1)}, bf16[4,2048]{1,0:T(4,128)(2,1)}, u32[]{:S(2)}) copy-start(bf16[4,2048]{1,0:T(4,128)(2,1)} %param.6) | copy-start | bytes 49156
  0.9 20.6 %collective-permute-start.4 = (bf16[3,2048]{1,0:T(4,128)(2,1)S(1)}, bf16[3,2048]{1,0:T(4,128)(2,1)S(1)}, u32[]{:S(2)}, u32[]{:S(2)}) collective-permute-start(bf16[3,2048]{1,0:T(4,128)(2,1)S(1)} %slice.209), channel_id=1, source_target_pairs={{0,1},{1,2},{2,3},{3,4},{4,5},{5,6},{6,7},{7,8},{8,9},{9,10},{10,1... | collective-permute-start | bytes 36872 | tf_op jit(solution)/shard_map/ppermute | solution.py:132
  3.4 21.7 %collective-permute-start.10 = (bf16[64,1024]{1,0:T(8,128)(2,1)S(1)}, bf16[64,1024]{1,0:T(8,128)(2,1)S(1)}, u32[]{:S(2)}, u32[]{:S(2)}) collective-permute-start(bf16[64,1024]{1,0:T(8,128)(2,1)S(1)} %get-tuple-element.17), channel_id=1, source_target_pairs={{0,0},{1,5},{2,3},{3,12},{4,10},{5,15},{6,1},{7,6},{8,8},{9,13},{1... | collective-permute-start | bytes 393224 | tf_op jit(solution)/shard_map/ppermute | solution.py:158
  4.1 21.0 %collective-permute-start.11 = (bf16[64,1024]{1,0:T(8,128)(2,1)S(1)}, bf16[64,1024]{1,0:T(8,128)(2,1)S(1)}, u32[]{:S(2)}, u32[]{:S(2)}) collective-permute-start(bf16[64,1024]{1,0:T(8,128)(2,1)S(1)} %get-tuple-element.16), channel_id=1, source_target_pairs={{0,4},{1,2},{2,7},{3,9},{4,14},{5,0},{6,5},{7,3},{8,12},{9,10},{10... | collective-permute-start | bytes 393224 | tf_op jit(solution)/shard_map/ppermute | solution.py:158
  10.5 14.7 %collective-permute-start.12 = (bf16[64,1024]{1,0:T(8,128)(2,1)S(1)}, bf16[64,1024]{1,0:T(8,128)(2,1)S(1)}, u32[]{:S(2)}, u32[]{:S(2)}) collective-permute-start(bf16[64,1024]{1,0:T(8,128)(2,1)S(1)} %get-tuple-element.15), channel_id=1, source_target_pairs={{0,1},{1,6},{2,8},{3,13},{4,11},{5,4},{6,2},{7,7},{8,9},{9,14},{10... | collective-permute-start | bytes 393224 | tf_op jit(solution)/shard_map/ppermute | solution.py:158
  13.1 2.6 %collective-permute-start = (s32[1,128]{1,0:T(1,128)S(1)}, s32[1,128]{1,0:T(1,128)S(1)}, u32[]{:S(2)}, u32[]{:S(2)}) collective-permute-start(s32[1,128]{1,0:T(1,128)S(1)} %bitcast.138), channel_id=1, source_target_pairs={{0,1},{1,0},{2,3},{3,2},{4,5},{5,4},{6,7},{7,6},{8,9},{9,8},{10,11... | collective-permute-start | bytes 1544 | tf_op jit(solution)/shard_map/ppermute | solution.py:115
  15.7 3.8 %collective-permute-start.1 = (s32[2,128]{1,0:T(2,128)S(1)}, s32[2,128]{1,0:T(2,128)S(1)}, u32[]{:S(2)}, u32[]{:S(2)}) collective-permute-start(s32[2,128]{1,0:T(2,128)S(1)} %pad_add_fusion.2), channel_id=1, source_target_pairs={{0,2},{1,3},{2,0},{3,1},{4,6},{5,7},{6,4},{7,5},{8,10},{9,11},{10,... | collective-permute-start | bytes 3080 | tf_op jit(solution)/shard_map/ppermute | solution.py:115
  19.6 7.7 %collective-permute-start.2 = (s32[4,128]{1,0:T(4,128)S(1)}, s32[4,128]{1,0:T(4,128)S(1)}, u32[]{:S(2)}, u32[]{:S(2)}) collective-permute-start(s32[4,128]{1,0:T(4,128)S(1)} %pad_add_fusion.1), channel_id=1, source_target_pairs={{0,4},{1,5},{2,6},{3,7},{4,0},{5,1},{6,2},{7,3},{8,12},{9,13},{10,... | collective-permute-start | bytes 6152 | tf_op jit(solution)/shard_map/ppermute | solution.py:115
  22.1 19.7 %collective-permute-start.6 = (bf16[64,2048]{1,0:T(8,128)(2,1)S(1)}, bf16[64,2048]{1,0:T(8,128)(2,1)S(1)}, u32[]{:S(2)}, u32[]{:S(2)}) collective-permute-start(bf16[64,2048]{1,0:T(8,128)(2,1)S(1)} %get-tuple-element.6), channel_id=1, source_target_pairs={{0,8},{1,9},{2,10},{3,11},{4,12},{5,13},{6,14},{7,15},{8,0},{9,1},... | collective-permute-start | bytes 786440 | tf_op jit(solution)/shard_map/ppermute | solution.py:115
  25.2 22.1 %collective-permute-start.13 = (bf16[3,64,1024]{2,1,0:T(8,128)(2,1)S(1)}, bf16[3,64,1024]{2,1,0:T(8,128)(2,1)S(1)}, u32[]{:S(2)}, u32[]{:S(2)}) collective-permute-start(bf16[3,64,1024]{2,1,0:T(8,128)(2,1)S(1)} %constant_dynamic-slice_fusion), channel_id=1, source_target_pairs={{0,16},{16,0},{1,17},{17,1},{2,18},{18,2},{3,19},{19,3},{4,20},{20... | collective-permute-start | bytes 1179656 | tf_op jit(solution)/shard_map/ppermute | solution.py:119
  26.8 20.5 %collective-permute-start.16 = (bf16[64,2048]{1,0:T(8,128)(2,1)S(1)}, bf16[64,2048]{1,0:T(8,128)(2,1)S(1)}, u32[]{:S(2)}, u32[]{:S(2)}) collective-permute-start(bf16[64,2048]{1,0:T(8,128)(2,1)S(1)} %get-tuple-element.8), channel_id=1, source_target_pairs={{0,8},{1,9},{2,10},{3,11},{4,12},{5,13},{6,14},{7,15},{8,0},{9,1},... | collective-permute-start | bytes 786440 | tf_op jit(solution)/shard_map/ppermute | solution.py:115
  26.9 21.1 %collective-permute-start.5 = (bf16[128,2048]{1,0:T(8,128)(2,1)S(1)}, bf16[128,2048]{1,0:T(8,128)(2,1)S(1)}, u32[]{:S(2)}, u32[]{:S(2)}) collective-permute-start(bf16[128,2048]{1,0:T(8,128)(2,1)S(1)} %pad_maximum_fusion.5), channel_id=1, source_target_pairs={{0,2},{1,3},{2,0},{3,1},{4,6},{5,7},{6,4},{7,5},{8,10},{9,11},{10,... | collective-permute-start | bytes 1572872 | tf_op jit(solution)/shard_map/ppermute | solution.py:115
  27.3 20.7 %collective-permute-start.14 = (bf16[3,64,1024]{2,1,0:T(8,128)(2,1)S(1)}, bf16[3,64,1024]{2,1,0:T(8,128)(2,1)S(1)}, u32[]{:S(2)}, u32[]{:S(2)}) collective-permute-start(bf16[3,64,1024]{2,1,0:T(8,128)(2,1)S(1)} %constant_dynamic-slice_fusion), channel_id=1, source_target_pairs={{0,4},{1,5},{2,6},{3,7},{4,0},{5,1},{6,2},{7,3},{8,12},{9,13},{10,... | collective-permute-start | bytes 1179656 | tf_op jit(solution)/shard_map/ppermute | solution.py:115
  41.8 8.1 %collective-permute-start.7 = (bf16[64,2048]{1,0:T(8,128)(2,1)S(1)}, bf16[64,2048]{1,0:T(8,128)(2,1)S(1)}, u32[]{:S(2)}, u32[]{:S(2)}) collective-permute-start(bf16[64,2048]{1,0:T(8,128)(2,1)S(1)} %collective-permute-done.6), channel_id=1, source_target_pairs={{0,2},{1,3},{2,0},{3,1},{4,6},{5,7},{6,4},{7,5},{8,10},{9,11},{10,... | collective-permute-start | bytes 786440 | tf_op jit(solution)/shard_map/ppermute | solution.py:115
  47.3 20.5 %collective-permute-start.3 = (s32[8,128]{1,0:T(8,128)S(1)}, s32[8,128]{1,0:T(8,128)S(1)}, u32[]{:S(2)}, u32[]{:S(2)}) collective-permute-start(s32[8,128]{1,0:T(8,128)S(1)} %pad_add_fusion), channel_id=1, source_target_pairs={{0,8},{1,9},{2,10},{3,11},{4,12},{5,13},{6,14},{7,15},{8,0},{9,1},... | collective-permute-start | bytes 12296 | tf_op jit(solution)/shard_map/ppermute | solution.py:115
  47.3 8.2 %collective-permute-start.17 = (bf16[64,2048]{1,0:T(8,128)(2,1)S(1)}, bf16[64,2048]{1,0:T(8,128)(2,1)S(1)}, u32[]{:S(2)}, u32[]{:S(2)}) collective-permute-start(bf16[64,2048]{1,0:T(8,128)(2,1)S(1)} %collective-permute-done.16), channel_id=1, source_target_pairs={{0,2},{1,3},{2,0},{3,1},{4,6},{5,7},{6,4},{7,5},{8,10},{9,11},{10,... | collective-permute-start | bytes 786440 | tf_op jit(solution)/shard_map/ppermute | solution.py:115
  47.9 7.8 %collective-permute-start.8 = (bf16[128,2048]{1,0:T(8,128)(2,1)S(1)}, bf16[128,2048]{1,0:T(8,128)(2,1)S(1)}, u32[]{:S(2)}, u32[]{:S(2)}) collective-permute-start(bf16[128,2048]{1,0:T(8,128)(2,1)S(1)} %pad_maximum_fusion.5), channel_id=1, source_target_pairs={{0,1},{1,0},{2,3},{3,2},{4,5},{5,4},{6,7},{7,6},{8,9},{9,8},{10,11... | collective-permute-start | bytes 1572872 | tf_op jit(solution)/shard_map/ppermute | solution.py:115
  48.0 11.5 %collective-permute-start.15 = (bf16[3,64,1024]{2,1,0:T(8,128)(2,1)S(1)}, bf16[3,64,1024]{2,1,0:T(8,128)(2,1)S(1)}, u32[]{:S(2)}, u32[]{:S(2)}) collective-permute-start(bf16[3,64,1024]{2,1,0:T(8,128)(2,1)S(1)} %collective-permute-done.14), channel_id=1, source_target_pairs={{0,16},{16,0},{1,17},{17,1},{2,18},{18,2},{3,19},{19,3},{4,20},{20... | collective-permute-start | bytes 1179656 | tf_op jit(solution)/shard_map/ppermute | solution.py:119
  49.9 12.0 %collective-permute-start.9 = (bf16[256,2048]{1,0:T(8,128)(2,1)S(1)}, bf16[256,2048]{1,0:T(8,128)(2,1)S(1)}, u32[]{:S(2)}, u32[]{:S(2)}) collective-permute-start(bf16[256,2048]{1,0:T(8,128)(2,1)S(1)} %pad_maximum_fusion.1), channel_id=1, source_target_pairs={{0,1},{1,0},{2,3},{3,2},{4,5},{5,4},{6,7},{7,6},{8,9},{9,8},{10,11... | collective-permute-start | bytes 3145736 | tf_op jit(solution)/shard_map/ppermute | solution.py:115
  55.5 11.4 %collective-permute-start.18 = (bf16[128,2048]{1,0:T(8,128)(2,1)S(1)}, bf16[128,2048]{1,0:T(8,128)(2,1)S(1)}, u32[]{:S(2)}, u32[]{:S(2)}) collective-permute-start(bf16[128,2048]{1,0:T(8,128)(2,1)S(1)} %pad_maximum_fusion.6), channel_id=1, source_target_pairs={{0,1},{1,0},{2,3},{3,2},{4,5},{5,4},{6,7},{7,6},{8,9},{9,8},{10,11... | collective-permute-start | bytes 1572872 | tf_op jit(solution)/shard_map/ppermute | solution.py:115
  64.0 14.8 %collective-permute-start.19 = (bf16[768,256]{1,0:T(8,128)(2,1)S(1)}, bf16[768,256]{1,0:T(8,128)(2,1)S(1)}, u32[]{:S(2)}, u32[]{:S(2)}) collective-permute-start(bf16[768,256]{1,0:T(8,128)(2,1)S(1)} %slice.256), channel_id=1, source_target_pairs={{0,4},{1,5},{2,6},{3,7},{4,0},{5,1},{6,2},{7,3},{8,12},{9,13},{10,... | collective-permute-start | bytes 1179656 | tf_op jit(solution)/shard_map/ppermute | solution.py:115
  67.7 11.0 %collective-permute-start.20 = (bf16[256,256]{1,0:T(8,128)(2,1)S(1)}, bf16[256,256]{1,0:T(8,128)(2,1)S(1)}, u32[]{:S(2)}, u32[]{:S(2)}) collective-permute-start(bf16[256,256]{1,0:T(8,128)(2,1)S(1)} %slice.257), channel_id=1, source_target_pairs={{0,4},{1,5},{2,6},{3,7},{4,0},{5,1},{6,2},{7,3},{8,12},{9,13},{10,... | collective-permute-start | bytes 393224 | tf_op jit(solution)/shard_map/ppermute | solution.py:115
  (1 other events, 3.3 us)

commit v5 on v4

--- a/solution.py
+++ b/solution.py
@@ -1,6 +1,8 @@
 import jax
 import jax.numpy as jnp
 from jax import lax
+from jax.experimental import pallas as pl
+from jax.experimental.pallas import tpu as pltpu
 from jax.sharding import Mesh
 from jax.sharding import PartitionSpec as P
 
@@ -100,14 +102,11 @@
     return returned[slot_of_row]
 
 
-def by_bit(bit, mine, theirs, axis):
-    return jnp.stack(
-        [jnp.where(bit == 0, mine, theirs), jnp.where(bit == 0, theirs, mine)], axis=axis
-    )
-
-
 FOUR = ("far", "near", "quad")
 CORE, Y, NEAR, FAR = 1, 2, 4, 8
+QUADS = (0, Y, CORE, Y | CORE)
+RIM = 16
+VMEM_LIMIT = 40 * 2**20
 
 
 def swap_seq(value, bit):
@@ -119,103 +118,301 @@
     return lax.ppermute(value, "grp", [(0, 1), (1, 0)])
 
 
+def call(kernel, out_shape, operands, name, scalars=None, scratch=(), flops=0, anywhere=0):
+    in_specs = [pl.BlockSpec(memory_space=pltpu.VMEM)] * (len(operands) - anywhere)
+    in_specs += [pl.BlockSpec(memory_space=pl.ANY)] * anywhere
+    if scalars is not None:
+        operands = [scalars] + list(operands)
+        in_specs = [pl.BlockSpec(memory_space=pltpu.SMEM)] + in_specs
+    many = isinstance(out_shape, (list, tuple))
+    shapes = list(out_shape) if many else [out_shape]
+    size = sum(2 * o.size for o in list(operands) + shapes)
+    whole = pl.BlockSpec(memory_space=pltpu.VMEM)
+    return pl.pallas_call(
+        kernel,
+        out_shape=out_shape,
+        in_specs=in_specs,
+        out_specs=[whole] * len(shapes) if many else whole,
+        scratch_shapes=list(scratch),
+        cost_estimate=pl.CostEstimate(flops=flops, bytes_accessed=size, transcendentals=0),
+        compiler_params=pltpu.CompilerParams(vmem_limit_bytes=VMEM_LIMIT),
+        name=name,
+    )(*operands)
+
+
+def bf16(*shape):
+    return jax.ShapeDtypeStruct(shape, jnp.bfloat16)
+
+
+def after_kernel(*refs):
+    del refs
+
+
+def after(value, *others):
+    anywhere = pl.BlockSpec(memory_space=pl.ANY)
+    return pl.pallas_call(
+        after_kernel,
+        out_shape=jax.ShapeDtypeStruct(value.shape, value.dtype),
+        in_specs=[anywhere] * (1 + len(others)),
+        out_specs=anywhere,
+        input_output_aliases={0: 0},
+        name="after",
+    )(value, *others)
+
+
+def convolved(before, rows, taps):
+    count = rows.shape[0]
+    rows = rows.astype(jnp.float32)
+    extended = jnp.concatenate([before.astype(jnp.float32), rows], axis=0)
+    taps = taps.astype(jnp.float32)
+    total = rows
+    for tap in range(KW):
+        total = total + taps[tap : tap + 1] * extended[RIM - tap : RIM - tap + count]
+    return total.astype(jnp.bfloat16)
+
+
+def conv_late_kernel(frames_ref, taps_ref, late_ref, middle_ref):
+    cut = frames_ref.shape[0] // 4
+    rows = convolved(frames_ref[cut - RIM : cut], frames_ref[cut:], taps_ref[...])
+    middle_ref[...] = rows[: 2 * cut]
+    late_ref[...] = rows[2 * cut :]
+
+
+def conv_early_kernel(rim_ref, frames_ref, taps_ref, late_ref, middle_ref, early_ref, own_ref):
+    cut = frames_ref.shape[0] // 4
+    early = convolved(rim_ref[...], frames_ref[:cut], taps_ref[...])
+    early_ref[...] = early
+    own_ref[:cut] = early
+    own_ref[cut : 3 * cut] = middle_ref[...]
+    own_ref[3 * cut :] = late_ref[...]
+
+
+ME, SIDE, GRP, TURN, TURN_PAIRED, HEAD = range(6)
+
+
+def project_kernel(row_refs, scalars, *refs):
+    rows, pieces = refs[:row_refs], refs[row_refs : row_refs + 4]
+    query_ref, keyed_ref, weight = refs[-3:]
+    side, grp = scalars[SIDE], scalars[GRP]
+    half = pieces[0].shape[2]
+    for n, piece in enumerate(pieces):
+        column = n // 2 + side - 2 * (n // 2) * side
+        feature = n % 2 + grp - 2 * (n % 2) * grp
+        turn = scalars[TURN if n < 2 else TURN_PAIRED]
+        for j in range(3):
+            part = lax.rem(j + 3 - turn, 3)
+            start = pl.multiple_of(part * HD + column * (HD // 2), HD // 2)
+            lanes = pl.ds(pl.multiple_of(feature * half, half), half)
+            weight[pl.ds(start, HD // 2), lanes] = piece[j]
+    at = 0
+    for ref in rows:
+        count = ref.shape[0]
+        done = lax.dot_general(
+            ref[...], weight[...], (((1,), (1,)), ((), ())), preferred_element_type=jnp.float32
+        ).astype(jnp.bfloat16)
+        query_ref[at : at + count] = done[:, :HD]
+        keyed_ref[at : at + count] = done[:, HD:]
+        at += count
+
+
+def project(scalars, rows, pieces, following=()):
+    total = sum(r.shape[0] for r in rows)
+    features = rows[0].shape[1]
+
+    def kernel(scalars_ref, *refs):
+        front = len(rows) + 4
+        project_kernel(len(rows), scalars_ref, *refs[:front], *refs[front + len(following) :])
+
+    return call(
+        kernel,
+        [bf16(total, HD), bf16(total, 2 * HD)],
+        list(rows) + list(pieces) + list(following),
+        "project",
+        scalars=scalars,
+        scratch=[pltpu.VMEM((3 * HD, features), jnp.bfloat16)],
+        flops=2 * total * 3 * HD * features,
+        anywhere=len(following),
+    )
+
+
+def attend_kernel(scalars, groups_ref, *refs):
+    queries, mine, theirs, outs = refs[:3], refs[3:6], refs[6:9], refs[9:17]
+    keys, values, key_marks, query_marks, asked, mixed = refs[17:]
+    devices, tok_rows = groups_ref.shape
+    cut = tok_rows // 4
+    rest = tok_rows - cut
+    span = devices * tok_rows
+    me = scalars[ME]
+    groups = groups_ref[...] * span
+    columns = groups.astype(jnp.float32).T.astype(jnp.int32)
+
+    for j in range(devices):
+        at = pl.multiple_of((me ^ j) * tok_rows, tok_rows)
+        time = at + lax.broadcasted_iota(jnp.int32, (1, tok_rows), 1)
+        marks = jnp.broadcast_to(groups[j : j + 1] + time, (8, tok_rows))
+        key_marks[:, pl.ds(at, tok_rows)] = marks
+    for hop, sources in ((0, mine), (NEAR, theirs)):
+        for n, quad in enumerate(QUADS):
+            whole = pl.multiple_of((me ^ hop ^ quad) * tok_rows, tok_rows)
+            other = pl.multiple_of((me ^ hop ^ quad ^ FAR) * tok_rows, tok_rows)
+            for target, lanes in ((keys, slice(0, HD)), (values, slice(HD, 2 * HD))):
+                target[pl.ds(whole, tok_rows)] = sources[0][n * tok_rows : (n + 1) * tok_rows, lanes]
+                target[pl.ds(other + cut, rest)] = sources[1][n * rest : (n + 1) * rest, lanes]
+                target[pl.ds(other, cut)] = sources[2][n * cut : (n + 1) * cut, lanes]
+    for n, quad in enumerate(QUADS):
+        asked[n] = queries[0][n * tok_rows : (n + 1) * tok_rows]
+        asked[n + 4, cut:] = queries[1][n * rest : (n + 1) * rest]
+        asked[n + 4, :cut] = queries[2][n * cut : (n + 1) * cut]
+        query_marks[n] = columns[:, quad : quad + 1]
+        query_marks[n + 4] = columns[:, (quad | FAR) : (quad | FAR) + 1]
+
+    def block(i, _):
+        device = me ^ ((i & 1) * Y + ((i >> 1) & 1) * CORE + (i >> 2) * FAR)
+        query = asked[i]
+        least = query_marks[i]
+        most = least + device * tok_rows + lax.broadcasted_iota(jnp.int32, (tok_rows, 1), 0)
+        for reach in range(4, devices + 1, 4):
+
+            @pl.when((device >= reach - 4) & (device < reach))
+            def _(count=reach * tok_rows):
+                scores = lax.dot_general(
+                    query,
+                    keys[:count],
+                    (((1,), (1,)), ((), ())),
+                    preferred_element_type=jnp.float32,
+                ) * (1.0 / HD**0.5)
+                marks = key_marks[0:1, :count]
+                allowed = (marks >= least) & (marks <= most)
+                scores = jnp.where(allowed, scores, jnp.float32(-1e30))
+                expd = jnp.exp(scores - jnp.max(scores, axis=1, keepdims=True))
+                scaled = expd * (1.0 / jnp.sum(expd, axis=1, keepdims=True))
+                out = jnp.dot(
+                    scaled.astype(jnp.bfloat16), values[:count], preferred_element_type=jnp.float32
+                )
+                mixed[i] = out.astype(jnp.bfloat16)
+
+        return 0
+
+    lax.fori_loop(0, 8, block, 0)
+    for n in range(8):
+        outs[n][...] = mixed[n]
+
+
+def attend(scalars, groups, queries, mine, theirs):
+    devices, tok_rows = groups.shape
+    span = devices * tok_rows
+    return call(
+        attend_kernel,
+        [bf16(tok_rows, HD)] * 8,
+        [groups] + queries + mine + theirs,
+        "attend",
+        scalars=scalars,
+        scratch=[
+            pltpu.VMEM((span, HD), jnp.bfloat16),
+            pltpu.VMEM((span, HD), jnp.bfloat16),
+            pltpu.VMEM((8, span), jnp.int32),
+            pltpu.VMEM((8, tok_rows, 1), jnp.int32),
+            pltpu.VMEM((8, tok_rows, HD), jnp.bfloat16),
+            pltpu.VMEM((8, tok_rows, HD), jnp.bfloat16),
+        ],
+        flops=2 * span * span * HD,
+    )
+
+
+def place_kernel(scalars, *refs):
+    out_ref = refs[-1]
+    for n, ref in enumerate(refs[:-1]):
+        hop = QUADS[n % 4] + n // 4 * FAR
+        head = scalars[HEAD] ^ (hop // FAR * 4 + hop % 4)
+        out_ref[:, pl.ds(pl.multiple_of(head * HD, HD), HD)] = ref[...]
+
+
 def body_by_head(frames, conv_weight, qkv_weight, track_ids, track_owner):
-    tok_rows = frames.shape[0]
+    tok_rows, features = frames.shape
     grp = lax.axis_index("grp")
     far, near, quad = (lax.axis_index(name) for name in FOUR)
     me = far * FAR + near * NEAR + quad
     devices = lax.axis_size(FOUR)
     head = far * 4 + quad
-    part = tok_rows // 2
-    features = frames.shape[1]
+    cut = tok_rows // 4
+    turn = lax.rem(2 * head + near, 3)
+    turn_paired = lax.rem(2 * head + 1 - near, 3)
+    scalars = jnp.stack([me, near, grp, turn, turn_paired, head]).astype(jnp.int32)
 
     rim_rows = lax.ppermute(
-        frames[tok_rows - (KW - 1) :], FOUR, [(i, i + 1) for i in range(devices - 1)]
-    )
-    late = convolve(frames[part:], conv_weight, frames[part - (KW - 1) : part])
-    early = convolve(frames[:part], conv_weight, rim_rows)
+        frames[tok_rows - RIM :], FOUR, [(i, i + 1) for i in range(devices - 1)]
+    )
+    late, middle = call(
+        conv_late_kernel,
+        [bf16(cut, features), bf16(2 * cut, features)],
+        [frames, conv_weight],
+        "conv_late",
+    )
+    early, own = call(
+        conv_early_kernel,
+        [bf16(cut, features), bf16(tok_rows, features)],
+        [rim_rows, frames, conv_weight, late, middle],
+        "conv_early",
+    )
 
     far_late = swap_seq(late, FAR)
+    far_middle = swap_seq(middle, FAR)
     far_early = swap_seq(early, FAR)
-    own = jnp.concatenate([early, late], axis=0)
     beside = swap_seq(own, Y)
-    far_beside_late = swap_seq(far_late, Y)
-    far_beside_early = swap_seq(far_early, Y)
-    first_rows = [(0, 0, tok_rows), (Y, 0, tok_rows), (FAR, part, part), (FAR | Y, part, part)]
-    second_rows = [(FAR, 0, part), (FAR | Y, 0, part)]
-    rest = jnp.concatenate([beside, far_late, far_beside_late], axis=0)
-    last = jnp.concatenate([far_early, far_beside_early], axis=0)
-    first = jnp.concatenate([own, rest, swap_seq(own, CORE), swap_seq(rest, CORE)], axis=0)
-    second = jnp.concatenate([last, swap_seq(last, CORE)], axis=0)
+
+    groups = track_groups(track_ids, track_owner)[None, :]
+    for bit in (CORE, Y, NEAR, FAR):
+        groups = jnp.concatenate([groups, swap_seq(groups, bit)], axis=0)
 
     def home(block):
         of_head, side = block % devices // 2, block % 2
         return of_head // 4 * FAR + side * NEAR + of_head % 4
 
     half = features // 2
-    held = lax.dynamic_slice_in_dim(qkv_weight.T, grp * half, half, 1).reshape(3, HD // 2, half)
-    moved = [
-        lax.ppermute(held[j], FOUR, [(d, home(3 * d + j)) for d in range(devices)])
-        for j in range(3)
-    ]
-    turn = lax.rem(2 * head + near, 3)
-    mine = lax.dynamic_slice_in_dim(jnp.stack(moved + moved[:2]), turn, 3, 0)
+    held = lax.dynamic_slice_in_dim(qkv_weight.T, grp * half, half, 1)
+    held = held.reshape(3, HD // 2, half)
+    mine = jnp.stack(
+        [
+            lax.ppermute(held[j], FOUR, [(d, home(3 * d + j)) for d in range(devices)])
+            for j in range(3)
+        ]
+    )
+    mine = after(mine, far_late)
+    mine_too = swap_grp(mine)
     paired = swap_seq(mine, NEAR)
-    mine = by_bit(grp, mine, swap_grp(mine), 2)
-    paired = by_bit(grp, paired, swap_grp(paired), 2)
-    head_weight = by_bit(near, mine, paired, 1).reshape(3 * HD, features)
-
-    def project(rows):
-        done = lax.dot_general(
-            rows, head_weight, (((1,), (1,)), ((), ())), preferred_element_type=jnp.float32
-        ).astype(jnp.bfloat16)
-        return done[:, :HD], done[:, HD:], swap_seq(done[:, HD:], NEAR)
-
-    parts = [project(first), project(second)]
-    query = jnp.concatenate([p[0] for p in parts], axis=0)
-    keyed = jnp.concatenate([p[1] for p in parts] + [p[2] for p in parts], axis=0)
-
-    order = []
-    for pieces in (first_rows, second_rows):
-        order += pieces + [(hop ^ CORE, start, count) for hop, start, count in pieces]
-
-    groups, _ = lax.optimization_barrier((track_groups(track_ids, track_owner)[None, :], paired))
-    for bit in (CORE, Y, NEAR, FAR):
-        groups = jnp.concatenate([groups, swap_seq(groups, bit)], axis=0)
-
-    def of_rows(bit):
-        times = [
-            (me ^ hop ^ bit) * tok_rows + start + jnp.arange(count, dtype=jnp.int32)
-            for hop, start, count in order
-        ]
-        marks = [groups[hop ^ bit, start : start + count] for hop, start, count in order]
-        return jnp.concatenate(times), jnp.concatenate(marks)
-
-    own_times, own_groups = of_rows(0)
-    other_times, other_groups = of_rows(NEAR)
-    key_times = jnp.concatenate([own_times, other_times])
-    key_groups = jnp.concatenate([own_groups, other_groups])
-    scores = lax.dot_general(
-        query, keyed[:, :HD], (((1,), (1,)), ((), ())), preferred_element_type=jnp.float32
-    ) * (1.0 / HD**0.5)
-    allowed = (key_times[None, :] <= own_times[:, None]) & (
-        key_groups[None, :] == own_groups[:, None]
-    )
-    scores = jnp.where(allowed, scores, jnp.float32(-1e30))
-    expd = jnp.exp(scores - jnp.max(scores, axis=-1, keepdims=True))
-    weights = (expd / jnp.sum(expd, axis=-1, keepdims=True)).astype(jnp.bfloat16)
-    mixed = jnp.dot(weights, keyed[:, HD:], preferred_element_type=jnp.float32)
-    mixed = mixed.astype(jnp.bfloat16)
-
-    sent = jnp.zeros((devices // 2, tok_rows, HD), jnp.bfloat16)
-    at = 0
-    for hop, start, count in order:
-        rows = mixed[at : at + count]
-        there = head ^ (hop // FAR * 4 + hop % 4)
-        sent = lax.dynamic_update_slice(sent, rows[None], (there, start, 0))
-        at += count
-    returned = lax.all_to_all(sent, ("far", "quad"), split_axis=0, concat_axis=0, tiled=True)
-    return returned.transpose(1, 0, 2).reshape(tok_rows, devices // 2 * HD)
+    paired_too = swap_grp(paired)
+    pieces = [mine, mine_too, paired, paired_too]
+    far_rest = jnp.concatenate([far_middle, far_late], axis=0)
+    far_rest = after(far_rest, mine_too, paired, groups)
+
+    def with_core(first, second, *others):
+        both = jnp.concatenate([first, second], axis=0)
+        return [first, second, swap_seq(after(both, *others) if others else both, CORE)]
+
+    query, keyed = [], []
+
+    def onward(rows):
+        done = project(scalars, rows, pieces, query[-1:])
+        query.append(done[0])
+        keyed.append(done[1])
+
+    far_rest_beside, far_early_beside = swap_seq(far_rest, Y), swap_seq(far_early, Y)
+    onward(with_core(own, beside))
+    onward(with_core(far_rest, far_rest_beside, paired_too, far_early))
+    onward(with_core(far_early, far_early_beside, query[0]))
+    swapped = [swap_seq(k, NEAR) for k in keyed]
+
+    blocks = attend(scalars, groups, query, keyed, swapped)
+    hops = [hop | far_hop for far_hop in (0, FAR) for hop in QUADS]
+    home_blocks = {hop: swap_seq(blocks[n], hop) for n, hop in list(enumerate(hops))[:0:-1]}
+    home_blocks[0] = blocks[0]
+    return call(
+        place_kernel,
+        bf16(tok_rows, 8 * HD),
+        [home_blocks[hop] for hop in hops],
+        "place",
+        scalars=scalars,
+    )
 
 
 def solution(mesh):

time: 99 us -> 117 us (1.18)
  Pallas kernels: 0 us -> 16.3 us
  blocking collectives: 13.4 us -> 0 us
  starting transfers between devices: 30.2 us -> 39.6 us
  matrix products: 6.48 us -> 0 us
  local copies, waits for them, and re-layouts: 5.05 us -> 11.5 us
  waiting for transfers between devices: 38.4 us -> 42.2 us
  other arithmetic: 4.4 us -> 6.43 us
    pallas_call x0 -> x11, Pallas kernels: none -> 16.3 us  [the longest x7 16.3 us: call(): pl.pallas_call(kernel, out_shape=out_shape, in_specs=in_specs, out_specs=...]
    all_to_all x1 -> x0, blocking collectives: 13.4 us -> none  [body_by_head(): lax.all_to_all(sent, ('far', 'quad'), split_axis=0, concat_axis=0, tiled=...]
    ppermute x15 -> x24, starting transfers between devices: 15.8 us -> 27.1 us  [swap_seq(): return lax.ppermute(value, FOUR, [(d, d ^ bit) for d in range(count)])]
    unnamed x15 -> x52, local copies, waits for them, and re-layouts: 0.6 us -> 10.1 us
    dot_general x4 -> x0, matrix products: 6.48 us -> none  [the longest x2 2.54 us: project(): lax.dot_general(rows, head_weight, (((1,), (1,)), ((), ())), preferred_el...]
    ppermute x15 -> x24, waiting for transfers between devices: 34.7 us -> 40.5 us  [swap_seq(): return lax.ppermute(value, FOUR, [(d, d ^ bit) for d in range(count)])]
    concatenate x4, other arithmetic: 0.21 us -> 5.51 us  [the longest x3 3.69 us: with_core(): both = jnp.concatenate([first, second], axis=0)]
    ppermute x2, waiting for transfers between devices: 3.77 us -> 1.68 us  [swap_grp(): return lax.ppermute(value, 'grp', [(0, 1), (1, 0)])]
  transfers between devices with their start and end apart: 21 -> 30, of which waited for: 7 -> 13; matrix products, arithmetic and copies ran while one was open for 9% -> 7% of each run, Pallas kernels for 0% -> 8%
where the time goes in v5:
time: 117 us; the launch traced here: 116 us
  waiting for transfers between devices  42.2 us (36%)
  starting transfers between devices  39.6 us (34%)
  Pallas kernels  16.3 us (14%)
  local copies, waits for them, and re-layouts  11.5 us (10%)
  other arithmetic  6.43 us (5%)
    ppermute x24, waiting for transfers between devices, swap_seq(): return lax.ppermute(value, FOUR, [(d, d ^ bit) for d in range(count)])  40.5 us
    ppermute x24, starting transfers between devices, swap_seq(): return lax.ppermute(value, FOUR, [(d, d ^ bit) for d in range(count)])  27.1 us
    pallas_call x7, Pallas kernels, call(): pl.pallas_call(kernel, out_shape=out_shape, in_specs=in_specs, out_specs=...  16.3 us
    unnamed x52, local copies, waits for them, and re-layouts  10.1 us
    ppermute x3, starting transfers between devices, body_by_head(): lax.ppermute(held[j], FOUR, [(d, home(3 * d + j)) for d in range(devices)])  7.62 us
    concatenate x3, other arithmetic, with_core(): both = jnp.concatenate([first, second], axis=0)  3.69 us
    ppermute x2, starting transfers between devices, swap_grp(): return lax.ppermute(value, 'grp', [(0, 1), (1, 0)])  3.02 us
  transfers between devices with their start and end apart: 30, of which 13 were waited for; matrix products, arithmetic and copies ran while one was open for 7% of the time, Pallas kernels for 8%

profile of v5, /device:TPU:0, one launch (start us, length us, event | category | flops | bytes accessed | tf_op | source)
XLA Modules:
  0.0 116.4 jit_solution(17307280784830452906)
XLA Ops:
  1.2 2.4 %collective-permute-start.9 = (bf16[64,1024]{1,0:T(8,128)(2,1)S(1)}, bf16[64,1024]{1,0:T(8,128)(2,1)S(1)}, u32[]{:S(2)}, u32[]{:S(2)}) collective-permute-start(bf16[64,1024]{1,0:T(8,128)(2,1)S(1)} %get-tuple-element.42), channel_id=1, source_target_pairs={{0,1},{1,6},{2,8},{3,13},{4,11},{5,4},{6,2},{7,7},{8,9},{9,14},{10... | collective-permute-start | bytes 393224 | tf_op jit(solution)/shard_map/ppermute | solution.py:376
  3.6 4.6 %collective-permute-start.8 = (bf16[64,1024]{1,0:T(8,128)(2,1)S(1)}, bf16[64,1024]{1,0:T(8,128)(2,1)S(1)}, u32[]{:S(2)}, u32[]{:S(2)}) collective-permute-start(bf16[64,1024]{1,0:T(8,128)(2,1)S(1)} %get-tuple-element.43), channel_id=1, source_target_pairs={{0,4},{1,2},{2,7},{3,9},{4,14},{5,0},{6,5},{7,3},{8,12},{9,10},{10... | collective-permute-start | bytes 393224 | tf_op jit(solution)/shard_map/ppermute | solution.py:376
  9.0 1.9 %collective-permute-start = (s32[1,128]{1,0:T(1,128)S(1)}, s32[1,128]{1,0:T(1,128)S(1)}, u32[]{:S(2)}, u32[]{:S(2)}) collective-permute-start(s32[1,128]{1,0:T(1,128)S(1)} %bitcast.15), channel_id=1, source_target_pairs={{0,1},{1,0},{2,3},{3,2},{4,5},{5,4},{6,7},{7,6},{8,9},{9,8},{10,11... | collective-permute-start | bytes 1544 | tf_op jit(solution)/shard_map/ppermute | solution.py:114
  10.9 1.9 %collective-permute-start.4 = (bf16[16,2048]{1,0:T(8,128)(2,1)S(1)}, bf16[16,2048]{1,0:T(8,128)(2,1)S(1)}, u32[]{:S(2)}, u32[]{:S(2)}) collective-permute-start(bf16[16,2048]{1,0:T(8,128)(2,1)S(1)} %slice.15), channel_id=1, source_target_pairs={{0,1},{1,2},{2,3},{3,4},{4,5},{5,6},{6,7},{7,8},{8,9},{9,10},{10,1... | collective-permute-start | bytes 196616 | tf_op jit(solution)/shard_map/ppermute | solution.py:342
  14.5 5.6 %collective-permute-start.14 = (bf16[64,2048]{1,0:T(8,128)(2,1)S(1)}, bf16[64,2048]{1,0:T(8,128)(2,1)}, u32[]{:S(2)}, u32[]{:S(2)}) collective-permute-start(bf16[64,2048]{1,0:T(8,128)(2,1)S(1)} %get-tuple-element.24.middle_ref), channel_id=1, source_target_pairs={{0,8},{1,9},{2,10},{3,11},{4,12},{5,13},{6,14},{7,15},{8,0},{9,1},... | collective-permute-start | bytes 786440 | tf_op jit(solution)/shard_map/ppermute | solution.py:114
  23.2 4.7 %collective-permute-done.10.refs_1_ = bf16[32,2048]{1,0:T(8,128)(2,1)S(1)} collective-permute-done((bf16[32,2048]{1,0:T(8,128)(2,1)S(1)}, bf16[32,2048]{1,0:T(8,128)(2,1)S(1)}, u32[]{:S(2)}, u32[]{:S(2)}) %collective-permute-start.10) | collective-permute-done | bytes 131104 | tf_op jit(solution)/shard_map/ppermute | solution.py:114
  32.2 10.5 %collective-permute-done.2 = s32[4,128]{1,0:T(4,128)S(1)} collective-permute-done((s32[4,128]{1,0:T(4,128)S(1)}, s32[4,128]{1,0:T(4,128)S(1)}, u32[]{:S(2)}, u32[]{:S(2)}) %collective-permute-start.2) | collective-permute-done | bytes 2080 | tf_op jit(solution)/shard_map/ppermute | solution.py:114
  43.5 3.8 %collective-permute-done.3 = s32[8,128]{1,0:T(8,128)S(1)} collective-permute-done((s32[8,128]{1,0:T(8,128)S(1)}, s32[8,128]{1,0:T(8,128)S(1)}, u32[]{:S(2)}, u32[]{:S(2)}) %collective-permute-start.3) | collective-permute-done | bytes 4128 | tf_op jit(solution)/shard_map/ppermute | solution.py:114
  48.5 1.8 %pad_maximum_fusion.3.refs_0_ = bf16[96,2048]{1,0:T(8,128)(2,1)} fusion(bf16[32,2048]{1,0:T(8,128)(2,1)} %copy-done.23, bf16[64,2048]{1,0:T(8,128)(2,1)} %collective-permute-done.14), kind=kLoop, calls=%fused_computation.3 | loop fusion | flops 786432 | bytes 786432 | tf_op jit(solution)/shard_map/concatenate | solution.py:385
  51.8 2.6 %collective-permute-start.15 = (bf16[96,2048]{1,0:T(8,128)(2,1)}, bf16[96,2048]{1,0:T(8,128)(2,1)S(1)}, u32[]{:S(2)}, u32[]{:S(2)}) collective-permute-start(bf16[96,2048]{1,0:T(8,128)(2,1)} %after.5.refs_0_), channel_id=1, source_target_pairs={{0,2},{1,3},{2,0},{3,1},{4,6},{5,7},{6,4},{7,5},{8,10},{9,11},{10,... | collective-permute-start | bytes 1179656 | tf_op jit(solution)/shard_map/ppermute | solution.py:114
  57.1 5.4 %collective-permute-done.15.refs_1_ = bf16[96,2048]{1,0:T(8,128)(2,1)S(1)} collective-permute-done((bf16[96,2048]{1,0:T(8,128)(2,1)}, bf16[96,2048]{1,0:T(8,128)(2,1)S(1)}, u32[]{:S(2)}, u32[]{:S(2)}) %collective-permute-start.15) | collective-permute-done | bytes 393248 | tf_op jit(solution)/shard_map/ppermute | solution.py:114
  65.4 1.7 %collective-permute-done.13.refs_6_.refs_1_ = bf16[3,64,1024]{2,1,0:T(8,128)(2,1)S(1)} collective-permute-done((bf16[3,64,1024]{2,1,0:T(8,128)(2,1)S(1)}, bf16[3,64,1024]{2,1,0:T(8,128)(2,1)S(1)}, u32[]{:S(2)}, u32[]{:S(2)}) %collective-permute-start.13) | collective-permute-done | bytes 393248 | tf_op jit(solution)/shard_map/ppermute | solution.py:118
  67.9 6.0 %collective-permute-done.18.refs_1_ = bf16[32,2048]{1,0:T(8,128)(2,1)S(1)} collective-permute-done((bf16[32,2048]{1,0:T(8,128)(2,1)}, bf16[32,2048]{1,0:T(8,128)(2,1)S(1)}, u32[]{:S(2)}, u32[]{:S(2)}) %collective-permute-start.18) | collective-permute-done | bytes 131104 | tf_op jit(solution)/shard_map/ppermute | solution.py:114
  74.0 1.6 %pad_maximum_fusion.4.refs_0_ = bf16[64,2048]{1,0:T(8,128)(2,1)} fusion(bf16[32,2048]{1,0:T(8,128)(2,1)S(1)} %collective-permute-done.18.refs_1_, bf16[32,2048]{1,0:T(8,128)(2,1)} %copy-done.15), kind=kLoop, calls=%fused_computation.5 | loop fusion | flops 524288 | bytes 524288 | tf_op jit(solution)/shard_map/concatenate | solution.py:389
  77.6 3.0 %project.3 = (bf16[512,128]{1,0:T(8,128)(2,1)S(1)}, bf16[512,256]{1,0:T(8,128)(2,1)S(1)}) custom-call(s32[6]{0:T(128)S(1)} %stack.39.scalars_ref.scalars, bf16[128,2048]{1,0:T(8,128)(2,1)S(1)} %get-tuple-element.25.refs_0_, bf16[128,2048]{1,0:T(8,128)(2,1)S(1)} %copy-done.12, bf16[256,2048]{1,0:T(8,128)(2,1)} %collective-permute-done.6.refs_2_, ...), custom_call_target="tpu_custom_call" | custom-call | flops 805306368 | bytes 4063244 | tf_op jit(solution)/shard_map/project/pallas_call | solution.py:131
  84.0 2.9 %project.4 = (bf16[384,128]{1,0:T(8,128)(2,1)S(1)}, bf16[384,256]{1,0:T(8,128)(2,1)S(1)}) custom-call(s32[6]{0:T(128)S(1)} %stack.39.scalars_ref.scalars, bf16[96,2048]{1,0:T(8,128)(2,1)S(1)} %copy-done.5, bf16[96,2048]{1,0:T(8,128)(2,1)S(1)} %copy-done.14, bf16[192,2048]{1,0:T(8,128)(2,1)} %collective-permute-done.17.refs_2_, ...), custom_call_target="tpu_custom_call" | custom-call | flops 603979776 | bytes 3571724 | tf_op jit(solution)/shard_map/project/pallas_call | solution.py:131
  86.8 2.1 %collective-permute-start.21 = (bf16[384,256]{1,0:T(8,128)(2,1)S(1)}, bf16[384,256]{1,0:T(8,128)(2,1)S(1)}, u32[]{:S(2)}, u32[]{:S(2)}) collective-permute-start(bf16[384,256]{1,0:T(8,128)(2,1)S(1)} %get-tuple-element.31.refs_4_), channel_id=1, source_target_pairs={{0,4},{1,5},{2,6},{3,7},{4,0},{5,1},{6,2},{7,3},{8,12},{9,13},{10,... | collective-permute-start | bytes 589832 | tf_op jit(solution)/shard_map/ppermute | solution.py:114
  88.9 2.2 %project.5 = (bf16[128,128]{1,0:T(8,128)(2,1)S(1)}, bf16[128,256]{1,0:T(8,128)(2,1)S(1)}) custom-call(s32[6]{0:T(128)S(1)} %stack.39.scalars_ref.scalars, bf16[32,2048]{1,0:T(8,128)(2,1)S(1)} %copy-done.16, bf16[32,2048]{1,0:T(8,128)(2,1)S(1)} %collective-permute-done.18.refs_1_, bf16[64,2048]{1,0:T(8,128)(2,1)S(1)} %collective-permute-done.19.refs_2_, ...), custom_call_target="tpu_custom_call" | custom-call | flops 201326592 | bytes 2293772 | tf_op jit(solution)/shard_map/project/pallas_call | solution.py:131
  91.3 4.2 %collective-permute-done.21.refs_7_ = bf16[384,256]{1,0:T(8,128)(2,1)S(1)} collective-permute-done((bf16[384,256]{1,0:T(8,128)(2,1)S(1)}, bf16[384,256]{1,0:T(8,128)(2,1)S(1)}, u32[]{:S(2)}, u32[]{:S(2)}) %collective-permute-start.21) | collective-permute-done | bytes 196640 | tf_op jit(solution)/shard_map/ppermute | solution.py:114
  96.6 6.3 %attend.1 = (bf16[128,128]{1,0:T(8,128)(2,1)S(1)}, bf16[128,128]{1,0:T(8,128)(2,1)S(1)}, bf16[128,128]{1,0:T(8,128)(2,1)S(1)}, bf16[128,128]{1,0:T(8,128)(2,1)S(...) custom-call(s32[6]{0:T(128)S(1)} %stack.39.scalars_ref.scalars, ...), custom_call_target="tpu_custom_call" | custom-call | flops 1073741824 | bytes 1576972 | tf_op jit(solution)/shard_map/attend/pallas_call | solution.py:131
  103.2 1.8 %collective-permute-start.25 = (bf16[128,128]{1,0:T(8,128)(2,1)S(1)}, bf16[128,128]{1,0:T(8,128)(2,1)S(1)}, u32[]{:S(2)}, u32[]{:S(2)}) collective-permute-start(bf16[128,128]{1,0:T(8,128)(2,1)S(1)} %get-tuple-element.36), channel_id=1, source_target_pairs={{0,3},{1,2},{2,1},{3,0},{4,7},{5,6},{6,5},{7,4},{8,11},{9,10},{10,... | collective-permute-start | bytes 98312 | tf_op jit(solution)/shard_map/ppermute | solution.py:114
  106.0 1.7 %collective-permute-start.27 = (bf16[128,128]{1,0:T(8,128)(2,1)S(1)}, bf16[128,128]{1,0:T(8,128)(2,1)S(1)}, u32[]{:S(2)}, u32[]{:S(2)}) collective-permute-start(bf16[128,128]{1,0:T(8,128)(2,1)S(1)} %get-tuple-element.38), channel_id=1, source_target_pairs={{0,10},{1,11},{2,8},{3,9},{4,14},{5,15},{6,12},{7,13},{8,2},{9,3},... | collective-permute-start | bytes 98312 | tf_op jit(solution)/shard_map/ppermute | solution.py:114
  107.9 3.7 %collective-permute-start.29 = (bf16[128,128]{1,0:T(8,128)(2,1)S(1)}, bf16[128,128]{1,0:T(8,128)(2,1)S(1)}, u32[]{:S(2)}, u32[]{:S(2)}) collective-permute-start(bf16[128,128]{1,0:T(8,128)(2,1)S(1)} %get-tuple-element.40), channel_id=1, source_target_pairs={{0,11},{1,10},{2,9},{3,8},{4,15},{5,14},{6,13},{7,12},{8,3},{9,2},... | collective-permute-start | bytes 98312 | tf_op jit(solution)/shard_map/ppermute | solution.py:114
  112.6 2.5 %collective-permute-done.29.refs_7_ = bf16[128,128]{1,0:T(8,128)(2,1)S(1)} collective-permute-done((bf16[128,128]{1,0:T(8,128)(2,1)S(1)}, bf16[128,128]{1,0:T(8,128)(2,1)S(1)}, u32[]{:S(2)}, u32[]{:S(2)}) %collective-permute-start.29) | collective-permute-done | bytes 32800 | tf_op jit(solution)/shard_map/ppermute | solution.py:114
  (113 shorter events, 31.3 us)
Async XLA Ops:
  1.2 19.1 %collective-permute-start.9 = (bf16[64,1024]{1,0:T(8,128)(2,1)S(1)}, bf16[64,1024]{1,0:T(8,128)(2,1)S(1)}, u32[]{:S(2)}, u32[]{:S(2)}) collective-permute-start(bf16[64,1024]{1,0:T(8,128)(2,1)S(1)} %get-tuple-element.42), channel_id=1, source_target_pairs={{0,1},{1,6},{2,8},{3,13},{4,11},{5,4},{6,2},{7,7},{8,9},{9,14},{10... | collective-permute-start | bytes 393224 | tf_op jit(solution)/shard_map/ppermute | solution.py:376
  3.6 17.6 %collective-permute-start.8 = (bf16[64,1024]{1,0:T(8,128)(2,1)S(1)}, bf16[64,1024]{1,0:T(8,128)(2,1)S(1)}, u32[]{:S(2)}, u32[]{:S(2)}) collective-permute-start(bf16[64,1024]{1,0:T(8,128)(2,1)S(1)} %get-tuple-element.43), channel_id=1, source_target_pairs={{0,4},{1,2},{2,7},{3,9},{4,14},{5,0},{6,5},{7,3},{8,12},{9,10},{10... | collective-permute-start | bytes 393224 | tf_op jit(solution)/shard_map/ppermute | solution.py:376
  8.2 14.2 %collective-permute-start.7 = (bf16[64,1024]{1,0:T(8,128)(2,1)S(1)}, bf16[64,1024]{1,0:T(8,128)(2,1)S(1)}, u32[]{:S(2)}, u32[]{:S(2)}) collective-permute-start(bf16[64,1024]{1,0:T(8,128)(2,1)S(1)} %get-tuple-element.41), channel_id=1, source_target_pairs={{0,0},{1,5},{2,3},{3,12},{4,10},{5,15},{6,1},{7,6},{8,8},{9,13},{1... | collective-permute-start | bytes 393224 | tf_op jit(solution)/shard_map/ppermute | solution.py:376
  13.4 14.6 %collective-permute-start.10 = (bf16[32,2048]{1,0:T(8,128)(2,1)S(1)}, bf16[32,2048]{1,0:T(8,128)(2,1)S(1)}, u32[]{:S(2)}, u32[]{:S(2)}) collective-permute-start(bf16[32,2048]{1,0:T(8,128)(2,1)S(1)} %get-tuple-element.23.late_ref), channel_id=1, source_target_pairs={{0,8},{1,9},{2,10},{3,11},{4,12},{5,13},{6,14},{7,15},{8,0},{9,1},... | collective-permute-start | bytes 393224 | tf_op jit(solution)/shard_map/ppermute | solution.py:114
  14.5 33.9 %collective-permute-start.14 = (bf16[64,2048]{1,0:T(8,128)(2,1)S(1)}, bf16[64,2048]{1,0:T(8,128)(2,1)}, u32[]{:S(2)}, u32[]{:S(2)}) collective-permute-start(bf16[64,2048]{1,0:T(8,128)(2,1)S(1)} %get-tuple-element.24.middle_ref), channel_id=1, source_target_pairs={{0,8},{1,9},{2,10},{3,11},{4,12},{5,13},{6,14},{7,15},{8,0},{9,1},... | collective-permute-start | bytes 786440 | tf_op jit(solution)/shard_map/ppermute | solution.py:114
  20.3 10.4 %collective-permute-start.1 = (s32[2,128]{1,0:T(2,128)S(1)}, s32[2,128]{1,0:T(2,128)S(1)}, u32[]{:S(2)}, u32[]{:S(2)}) collective-permute-start(s32[2,128]{1,0:T(2,128)S(1)} %pad_add_fusion.2), channel_id=1, source_target_pairs={{0,2},{1,3},{2,0},{3,1},{4,6},{5,7},{6,4},{7,5},{8,10},{9,11},{10,... | collective-permute-start | bytes 3080 | tf_op jit(solution)/shard_map/ppermute | solution.py:114
  21.2 33.2 %collective-permute-start.5 = (bf16[128,2048]{1,0:T(8,128)(2,1)S(1)}, bf16[128,2048]{1,0:T(8,128)(2,1)S(1)}, u32[]{:S(2)}, u32[]{:S(2)}) collective-permute-start(bf16[128,2048]{1,0:T(8,128)(2,1)S(1)} %get-tuple-element.25.refs_0_), channel_id=1, source_target_pairs={{0,2},{1,3},{2,0},{3,1},{4,6},{5,7},{6,4},{7,5},{8,10},{9,11},{10,... | collective-permute-start | bytes 1572872 | tf_op jit(solution)/shard_map/ppermute | solution.py:114
  28.6 21.7 %collective-permute-start.11 = (bf16[3,64,1024]{2,1,0:T(8,128)(2,1)}, bf16[3,64,1024]{2,1,0:T(8,128)(2,1)S(1)}, u32[]{:S(2)}, u32[]{:S(2)}) collective-permute-start(bf16[3,64,1024]{2,1,0:T(8,128)(2,1)} %after.4.refs_3_), channel_id=1, source_target_pairs={{0,16},{16,0},{1,17},{17,1},{2,18},{18,2},{3,19},{19,3},{4,20},{20... | collective-permute-start | bytes 1179656 | tf_op jit(solution)/shard_map/ppermute | solution.py:118
  30.1 20.2 %collective-permute-start.12 = (bf16[3,64,1024]{2,1,0:T(8,128)(2,1)}, bf16[3,64,1024]{2,1,0:T(8,128)(2,1)S(1)}, u32[]{:S(2)}, u32[]{:S(2)}) collective-permute-start(bf16[3,64,1024]{2,1,0:T(8,128)(2,1)} %after.4.refs_3_), channel_id=1, source_target_pairs={{0,4},{1,5},{2,6},{3,7},{4,0},{5,1},{6,2},{7,3},{8,12},{9,13},{10,... | collective-permute-start | bytes 1179656 | tf_op jit(solution)/shard_map/ppermute | solution.py:114
  30.8 11.9 %collective-permute-start.2 = (s32[4,128]{1,0:T(4,128)S(1)}, s32[4,128]{1,0:T(4,128)S(1)}, u32[]{:S(2)}, u32[]{:S(2)}) collective-permute-start(s32[4,128]{1,0:T(4,128)S(1)} %pad_add_fusion.1), channel_id=1, source_target_pairs={{0,4},{1,5},{2,6},{3,7},{4,0},{5,1},{6,2},{7,3},{8,12},{9,13},{10,... | collective-permute-start | bytes 6152 | tf_op jit(solution)/shard_map/ppermute | solution.py:114
  51.8 10.7 %collective-permute-start.15 = (bf16[96,2048]{1,0:T(8,128)(2,1)}, bf16[96,2048]{1,0:T(8,128)(2,1)S(1)}, u32[]{:S(2)}, u32[]{:S(2)}) collective-permute-start(bf16[96,2048]{1,0:T(8,128)(2,1)} %after.5.refs_0_), channel_id=1, source_target_pairs={{0,2},{1,3},{2,0},{3,1},{4,6},{5,7},{6,4},{7,5},{8,10},{9,11},{10,... | collective-permute-start | bytes 1179656 | tf_op jit(solution)/shard_map/ppermute | solution.py:114
  55.5 20.0 %collective-permute-start.6 = (bf16[256,2048]{1,0:T(8,128)(2,1)}, bf16[256,2048]{1,0:T(8,128)(2,1)}, u32[]{:S(2)}, u32[]{:S(2)}) collective-permute-start(bf16[256,2048]{1,0:T(8,128)(2,1)} %pad_maximum_fusion), channel_id=1, source_target_pairs={{0,1},{1,0},{2,3},{3,2},{4,5},{5,4},{6,7},{7,6},{8,9},{9,8},{10,11... | collective-permute-start | bytes 3145736 | tf_op jit(solution)/shard_map/ppermute | solution.py:114
  55.6 11.5 %collective-permute-start.13 = (bf16[3,64,1024]{2,1,0:T(8,128)(2,1)S(1)}, bf16[3,64,1024]{2,1,0:T(8,128)(2,1)S(1)}, u32[]{:S(2)}, u32[]{:S(2)}) collective-permute-start(bf16[3,64,1024]{2,1,0:T(8,128)(2,1)S(1)} %copy-done.9), channel_id=1, source_target_pairs={{0,16},{16,0},{1,17},{17,1},{2,18},{18,2},{3,19},{19,3},{4,20},{20... | collective-permute-start | bytes 1179656 | tf_op jit(solution)/shard_map/ppermute | solution.py:118
  57.1 8.3 %collective-permute-start.16 = (bf16[32,2048]{1,0:T(8,128)(2,1)S(1)}, bf16[32,2048]{1,0:T(8,128)(2,1)S(1)}, u32[]{:S(2)}, u32[]{:S(2)}) collective-permute-start(bf16[32,2048]{1,0:T(8,128)(2,1)S(1)} %get-tuple-element.27), channel_id=1, source_target_pairs={{0,8},{1,9},{2,10},{3,11},{4,12},{5,13},{6,14},{7,15},{8,0},{9,1},... | collective-permute-start | bytes 393224 | tf_op jit(solution)/shard_map/ppermute | solution.py:114
  67.8 14.2 %collective-permute-start.17 = (bf16[192,2048]{1,0:T(8,128)(2,1)}, bf16[192,2048]{1,0:T(8,128)(2,1)}, u32[]{:S(2)}, u32[]{:S(2)}) collective-permute-start(bf16[192,2048]{1,0:T(8,128)(2,1)} %after.6), channel_id=1, source_target_pairs={{0,1},{1,0},{2,3},{3,2},{4,5},{5,4},{6,7},{7,6},{8,9},{9,8},{10,11... | collective-permute-start | bytes 2359304 | tf_op jit(solution)/shard_map/ppermute | solution.py:114
  67.8 6.1 %collective-permute-start.18 = (bf16[32,2048]{1,0:T(8,128)(2,1)}, bf16[32,2048]{1,0:T(8,128)(2,1)S(1)}, u32[]{:S(2)}, u32[]{:S(2)}) collective-permute-start(bf16[32,2048]{1,0:T(8,128)(2,1)} %copy-done.15), channel_id=1, source_target_pairs={{0,2},{1,3},{2,0},{3,1},{4,6},{5,7},{6,4},{7,5},{8,10},{9,11},{10,... | collective-permute-start | bytes 393224 | tf_op jit(solution)/shard_map/ppermute | solution.py:114
  82.0 6.9 %collective-permute-start.19 = (bf16[64,2048]{1,0:T(8,128)(2,1)}, bf16[64,2048]{1,0:T(8,128)(2,1)S(1)}, u32[]{:S(2)}, u32[]{:S(2)}) collective-permute-start(bf16[64,2048]{1,0:T(8,128)(2,1)} %after.7), channel_id=1, source_target_pairs={{0,1},{1,0},{2,3},{3,2},{4,5},{5,4},{6,7},{7,6},{8,9},{9,8},{10,11... | collective-permute-start | bytes 786440 | tf_op jit(solution)/shard_map/ppermute | solution.py:114
  82.0 9.3 %collective-permute-start.20 = (bf16[512,256]{1,0:T(8,128)(2,1)}, bf16[512,256]{1,0:T(8,128)(2,1)S(1)}, u32[]{:S(2)}, u32[]{:S(2)}) collective-permute-start(bf16[512,256]{1,0:T(8,128)(2,1)} %copy-done.21), channel_id=1, source_target_pairs={{0,4},{1,5},{2,6},{3,7},{4,0},{5,1},{6,2},{7,3},{8,12},{9,13},{10,... | collective-permute-start | bytes 786440 | tf_op jit(solution)/shard_map/ppermute | solution.py:114
  86.8 8.7 %collective-permute-start.21 = (bf16[384,256]{1,0:T(8,128)(2,1)S(1)}, bf16[384,256]{1,0:T(8,128)(2,1)S(1)}, u32[]{:S(2)}, u32[]{:S(2)}) collective-permute-start(bf16[384,256]{1,0:T(8,128)(2,1)S(1)} %get-tuple-element.31.refs_4_), channel_id=1, source_target_pairs={{0,4},{1,5},{2,6},{3,7},{4,0},{5,1},{6,2},{7,3},{8,12},{9,13},{10,... | collective-permute-start | bytes 589832 | tf_op jit(solution)/shard_map/ppermute | solution.py:114
  91.1 5.5 %collective-permute-start.22 = (bf16[128,256]{1,0:T(8,128)(2,1)S(1)}, bf16[128,256]{1,0:T(8,128)(2,1)S(1)}, u32[]{:S(2)}, u32[]{:S(2)}) collective-permute-start(bf16[128,256]{1,0:T(8,128)(2,1)S(1)} %get-tuple-element.32.refs_5_), channel_id=1, source_target_pairs={{0,4},{1,5},{2,6},{3,7},{4,0},{5,1},{6,2},{7,3},{8,12},{9,13},{10,... | collective-permute-start | bytes 196616 | tf_op jit(solution)/shard_map/ppermute | solution.py:114
  103.2 8.3 %collective-permute-start.25 = (bf16[128,128]{1,0:T(8,128)(2,1)S(1)}, bf16[128,128]{1,0:T(8,128)(2,1)S(1)}, u32[]{:S(2)}, u32[]{:S(2)}) collective-permute-start(bf16[128,128]{1,0:T(8,128)(2,1)S(1)} %get-tuple-element.36), channel_id=1, source_target_pairs={{0,3},{1,2},{2,1},{3,0},{4,7},{5,6},{6,5},{7,4},{8,11},{9,10},{10,... | collective-permute-start | bytes 98312 | tf_op jit(solution)/shard_map/ppermute | solution.py:114
  105.1 6.5 %collective-permute-start.26 = (bf16[128,128]{1,0:T(8,128)(2,1)S(1)}, bf16[128,128]{1,0:T(8,128)(2,1)S(1)}, u32[]{:S(2)}, u32[]{:S(2)}) collective-permute-start(bf16[128,128]{1,0:T(8,128)(2,1)S(1)} %get-tuple-element.37), channel_id=1, source_target_pairs={{0,8},{1,9},{2,10},{3,11},{4,12},{5,13},{6,14},{7,15},{8,0},{9,1},... | collective-permute-start | bytes 98312 | tf_op jit(solution)/shard_map/ppermute | solution.py:114
  106.0 5.7 %collective-permute-start.27 = (bf16[128,128]{1,0:T(8,128)(2,1)S(1)}, bf16[128,128]{1,0:T(8,128)(2,1)S(1)}, u32[]{:S(2)}, u32[]{:S(2)}) collective-permute-start(bf16[128,128]{1,0:T(8,128)(2,1)S(1)} %get-tuple-element.38), channel_id=1, source_target_pairs={{0,10},{1,11},{2,8},{3,9},{4,14},{5,15},{6,12},{7,13},{8,2},{9,3},... | collective-permute-start | bytes 98312 | tf_op jit(solution)/shard_map/ppermute | solution.py:114
  107.9 7.2 %collective-permute-start.29 = (bf16[128,128]{1,0:T(8,128)(2,1)S(1)}, bf16[128,128]{1,0:T(8,128)(2,1)S(1)}, u32[]{:S(2)}, u32[]{:S(2)}) collective-permute-start(bf16[128,128]{1,0:T(8,128)(2,1)S(1)} %get-tuple-element.40), channel_id=1, source_target_pairs={{0,11},{1,10},{2,9},{3,8},{4,15},{5,14},{6,13},{7,12},{8,3},{9,2},... | collective-permute-start | bytes 98312 | tf_op jit(solution)/shard_map/ppermute | solution.py:114
  (32 other events, 143.2 us)

commit v6 on v4

--- a/solution.py
+++ b/solution.py
@@ -1,6 +1,8 @@
 import jax
 import jax.numpy as jnp
 from jax import lax
+from jax.experimental import pallas as pl
+from jax.experimental.pallas import tpu as pltpu
 from jax.sharding import Mesh
 from jax.sharding import PartitionSpec as P
 
@@ -100,95 +102,179 @@
     return returned[slot_of_row]
 
 
+FOUR = ("far", "near", "quad")
+CORE, Y, NEAR, FAR = 1, 2, 4, 8
+QUADS = (0, Y, CORE, Y | CORE)
+RIM = 16
+VMEM_LIMIT = 40 * 2**20
+
+
+def swap_seq(value, bit):
+    count = lax.axis_size(FOUR)
+    return lax.ppermute(value, FOUR, [(d, d ^ bit) for d in range(count)])
+
+
+def swap_grp(value):
+    return lax.ppermute(value, "grp", [(0, 1), (1, 0)])
+
+
+def call(kernel, out_shape, operands, name, scalars=None, scratch=(), flops=0, anywhere=0):
+    in_specs = [pl.BlockSpec(memory_space=pltpu.VMEM)] * (len(operands) - anywhere)
+    in_specs += [pl.BlockSpec(memory_space=pl.ANY)] * anywhere
+    if scalars is not None:
+        operands = [scalars] + list(operands)
+        in_specs = [pl.BlockSpec(memory_space=pltpu.SMEM)] + in_specs
+    many = isinstance(out_shape, (list, tuple))
+    shapes = list(out_shape) if many else [out_shape]
+    size = sum(2 * o.size for o in list(operands) + shapes)
+    whole = pl.BlockSpec(memory_space=pltpu.VMEM)
+    return pl.pallas_call(
+        kernel,
+        out_shape=out_shape,
+        in_specs=in_specs,
+        out_specs=[whole] * len(shapes) if many else whole,
+        scratch_shapes=list(scratch),
+        cost_estimate=pl.CostEstimate(flops=flops, bytes_accessed=size, transcendentals=0),
+        compiler_params=pltpu.CompilerParams(vmem_limit_bytes=VMEM_LIMIT),
+        name=name,
+    )(*operands)
+
+
+def bf16(*shape):
+    return jax.ShapeDtypeStruct(shape, jnp.bfloat16)
+
+
+def after_kernel(*refs):
+    del refs
+
+
+def after(value, *others):
+    anywhere = pl.BlockSpec(memory_space=pl.ANY)
+    return pl.pallas_call(
+        after_kernel,
+        out_shape=jax.ShapeDtypeStruct(value.shape, value.dtype),
+        in_specs=[anywhere] * (1 + len(others)),
+        out_specs=anywhere,
+        input_output_aliases={0: 0},
+        name="after",
+    )(value, *others)
+
+
+def convolved(before, rows, taps):
+    count = rows.shape[0]
+    rows = rows.astype(jnp.float32)
+    extended = jnp.concatenate([before.astype(jnp.float32), rows], axis=0)
+    taps = taps.astype(jnp.float32)
+    total = rows
+    for tap in range(KW):
+        total = total + taps[tap : tap + 1] * extended[RIM - tap : RIM - tap + count]
+    return total.astype(jnp.bfloat16)
+
+
+def conv_late_kernel(frames_ref, taps_ref, late_ref):
+    part = late_ref.shape[0]
+    late_ref[...] = convolved(frames_ref[part - RIM : part], frames_ref[part:], taps_ref[...])
+
+
+def conv_early_kernel(rim_ref, frames_ref, taps_ref, late_ref, early_ref, own_ref):
+    part = late_ref.shape[0]
+    early = convolved(rim_ref[...], frames_ref[:part], taps_ref[...])
+    early_ref[...] = early
+    own_ref[:part] = early
+    own_ref[part:] = late_ref[...]
+
+
 def by_bit(bit, mine, theirs, axis):
     return jnp.stack(
         [jnp.where(bit == 0, mine, theirs), jnp.where(bit == 0, theirs, mine)], axis=axis
     )
 
 
-FOUR = ("far", "near", "quad")
-CORE, Y, NEAR, FAR = 1, 2, 4, 8
-
-
-def swap_seq(value, bit):
-    count = lax.axis_size(FOUR)
-    return lax.ppermute(value, FOUR, [(d, d ^ bit) for d in range(count)])
-
-
-def swap_grp(value):
-    return lax.ppermute(value, "grp", [(0, 1), (1, 0)])
-
-
 def body_by_head(frames, conv_weight, qkv_weight, track_ids, track_owner):
-    tok_rows = frames.shape[0]
+    tok_rows, features = frames.shape
     grp = lax.axis_index("grp")
     far, near, quad = (lax.axis_index(name) for name in FOUR)
     me = far * FAR + near * NEAR + quad
     devices = lax.axis_size(FOUR)
     head = far * 4 + quad
     part = tok_rows // 2
-    features = frames.shape[1]
-
-    rim_rows = lax.ppermute(
-        frames[tok_rows - (KW - 1) :], FOUR, [(i, i + 1) for i in range(devices - 1)]
-    )
-    late = convolve(frames[part:], conv_weight, frames[part - (KW - 1) : part])
-    early = convolve(frames[:part], conv_weight, rim_rows)
-
-    far_late = swap_seq(late, FAR)
-    far_early = swap_seq(early, FAR)
-    own = jnp.concatenate([early, late], axis=0)
-    beside = swap_seq(own, Y)
-    far_beside_late = swap_seq(far_late, Y)
-    far_beside_early = swap_seq(far_early, Y)
-    first_rows = [(0, 0, tok_rows), (Y, 0, tok_rows), (FAR, part, part), (FAR | Y, part, part)]
-    second_rows = [(FAR, 0, part), (FAR | Y, 0, part)]
-    rest = jnp.concatenate([beside, far_late, far_beside_late], axis=0)
-    last = jnp.concatenate([far_early, far_beside_early], axis=0)
-    first = jnp.concatenate([own, rest, swap_seq(own, CORE), swap_seq(rest, CORE)], axis=0)
-    second = jnp.concatenate([last, swap_seq(last, CORE)], axis=0)
 
     def home(block):
         of_head, side = block % devices // 2, block % 2
         return of_head // 4 * FAR + side * NEAR + of_head % 4
 
     half = features // 2
-    held = lax.dynamic_slice_in_dim(qkv_weight.T, grp * half, half, 1).reshape(3, HD // 2, half)
+    held = lax.dynamic_slice_in_dim(qkv_weight.T, grp * half, half, 1)
+    held = held.reshape(3, HD // 2, half)
     moved = [
         lax.ppermute(held[j], FOUR, [(d, home(3 * d + j)) for d in range(devices)])
         for j in range(3)
     ]
     turn = lax.rem(2 * head + near, 3)
     mine = lax.dynamic_slice_in_dim(jnp.stack(moved + moved[:2]), turn, 3, 0)
+    mine_too = swap_grp(mine)
     paired = swap_seq(mine, NEAR)
-    mine = by_bit(grp, mine, swap_grp(mine), 2)
-    paired = by_bit(grp, paired, swap_grp(paired), 2)
-    head_weight = by_bit(near, mine, paired, 1).reshape(3 * HD, features)
-
-    def project(rows):
+    paired_too = swap_grp(paired)
+    head_weight = by_bit(
+        near, by_bit(grp, mine, mine_too, 2), by_bit(grp, paired, paired_too, 2), 1
+    ).reshape(3 * HD, features)
+
+    rim_rows = lax.ppermute(
+        frames[tok_rows - RIM :], FOUR, [(i, i + 1) for i in range(devices - 1)]
+    )
+    late = call(conv_late_kernel, bf16(part, features), [frames, conv_weight], "conv_late")
+    early, own = call(
+        conv_early_kernel,
+        [bf16(part, features), bf16(tok_rows, features)],
+        [rim_rows, frames, conv_weight, late],
+        "conv_early",
+    )
+    beside = swap_seq(own, Y)
+    far_late = after(swap_seq(late, FAR), mine_too)
+    far_late_beside = swap_seq(far_late, Y)
+    far_early = swap_seq(after(early, far_late), FAR)
+    far_early_beside = swap_seq(after(far_early, paired_too), Y)
+
+    groups = track_groups(track_ids, track_owner)[None, :]
+    groups = jnp.concatenate([groups, swap_seq(groups, NEAR)], axis=0)
+
+    parts = []
+
+    def project(rows, *others):
+        rows = jnp.concatenate(rows, axis=0)
+        rows = jnp.concatenate([rows, swap_seq(rows, CORE)], axis=0)
         done = lax.dot_general(
-            rows, head_weight, (((1,), (1,)), ((), ())), preferred_element_type=jnp.float32
+            after(rows, *others) if others else rows,
+            head_weight,
+            (((1,), (1,)), ((), ())),
+            preferred_element_type=jnp.float32,
         ).astype(jnp.bfloat16)
-        return done[:, :HD], done[:, HD:], swap_seq(done[:, HD:], NEAR)
-
-    parts = [project(first), project(second)]
+        parts.append((done[:, :HD], done[:, HD:], swap_seq(done[:, HD:], NEAR)))
+        return done
+
+    done = project([own, beside])
+    groups = after(groups, done)
+    for bit in (FAR, CORE, Y):
+        groups = jnp.concatenate([groups, swap_seq(groups, bit)], axis=0)
+    project([far_late, far_late_beside], done)
+    project([far_early, after(far_early_beside, done)], groups)
     query = jnp.concatenate([p[0] for p in parts], axis=0)
     keyed = jnp.concatenate([p[1] for p in parts] + [p[2] for p in parts], axis=0)
 
-    order = []
-    for pieces in (first_rows, second_rows):
-        order += pieces + [(hop ^ CORE, start, count) for hop, start, count in pieces]
-
-    groups, _ = lax.optimization_barrier((track_groups(track_ids, track_owner)[None, :], paired))
-    for bit in (CORE, Y, NEAR, FAR):
-        groups = jnp.concatenate([groups, swap_seq(groups, bit)], axis=0)
+    row_of = {}
+    for bit in (0, NEAR, FAR, CORE, Y):
+        row_of.update({seen ^ bit: len(row_of) + n for n, seen in enumerate(list(row_of) or [0])})
+
+    order = [(hop, 0, tok_rows) for hop in QUADS]
+    order += [(hop | FAR, part, part) for hop in QUADS]
+    order += [(hop | FAR, 0, part) for hop in QUADS]
 
     def of_rows(bit):
         times = [
             (me ^ hop ^ bit) * tok_rows + start + jnp.arange(count, dtype=jnp.int32)
             for hop, start, count in order
         ]
-        marks = [groups[hop ^ bit, start : start + count] for hop, start, count in order]
+        marks = [groups[row_of[hop ^ bit], start : start + count] for hop, start, count in order]
         return jnp.concatenate(times), jnp.concatenate(marks)
 
     own_times, own_groups = of_rows(0)

time: 99 us -> 114 us (1.15)
  waiting for transfers between devices: 38.4 us -> 23 us
  other arithmetic: 4.4 us -> 17.3 us
  local copies, waits for them, and re-layouts: 5.05 us -> 17.1 us
  matrix products: 6.48 us -> 14.3 us
  starting transfers between devices: 30.2 us -> 27.2 us
    ppermute x15 -> x16, waiting for transfers between devices: 34.7 us -> 21.4 us  [swap_seq(): return lax.ppermute(value, FOUR, [(d, d ^ bit) for d in range(count)])]
    concatenate x4 -> x6, other arithmetic: 0.21 us -> 8.5 us  [the longest x2 4.23 us: project(): rows = jnp.concatenate([rows, swap_seq(rows, CORE)], axis=0)]
    unnamed x15 -> x40, local copies, waits for them, and re-layouts: 0.6 us -> 8.51 us
    dot_general x2 -> x3, matrix products: 2.54 us -> 8.33 us  [project(): lax.dot_general(after(rows, *others) if others else rows, head_weight, ((...]
    ppermute x15 -> x16, starting transfers between devices: 15.8 us -> 12.1 us  [swap_seq(): return lax.ppermute(value, FOUR, [(d, d ^ bit) for d in range(count)])]
    add x12, other arithmetic: 0.07 us -> 2.94 us  [of_rows(): (me ^ hop ^ bit) * tok_rows + start + jnp.arange(count, dtype=jnp.int32)]
    ppermute x2, waiting for transfers between devices: 3.77 us -> 1.54 us  [swap_grp(): return lax.ppermute(value, 'grp', [(0, 1), (1, 0)])]
    another operation x3, other arithmetic: 0.26 us -> 2.43 us  [by_bit(): jnp.stack([jnp.where(bit == 0, mine, theirs), jnp.where(bit == 0, theirs,...]
  transfers between devices with their start and end apart: 21 -> 22, of which waited for: 7 -> 8; matrix products, arithmetic and copies ran while one was open for 9% -> 31% of each run, Pallas kernels for 0% -> 1%
where the time goes in v6:
time: 114 us; the launch traced here: 113 us
  starting transfers between devices  27.2 us (24%)
  waiting for transfers between devices  23 us (20%)
  other arithmetic  17.3 us (15%)
  local copies, waits for them, and re-layouts  17.1 us (15%)
  matrix products  14.3 us (13%)
  blocking collectives  13.3 us (12%)
    ppermute x16, waiting for transfers between devices, swap_seq(): return lax.ppermute(value, FOUR, [(d, d ^ bit) for d in range(count)])  21.4 us
    all_to_all x1, blocking collectives, body_by_head(): lax.all_to_all(sent, ('far', 'quad'), split_axis=0, concat_axis=0, tiled=...  13.3 us
    ppermute x16, starting transfers between devices, swap_seq(): return lax.ppermute(value, FOUR, [(d, d ^ bit) for d in range(count)])  12.1 us
    ppermute x3, starting transfers between devices, body_by_head(): lax.ppermute(held[j], FOUR, [(d, home(3 * d + j)) for d in range(devices)])  9.43 us
    unnamed x40, local copies, waits for them, and re-layouts  8.51 us
    dot_general x3, matrix products, project(): lax.dot_general(after(rows, *others) if others else rows, head_weight, ((...  8.33 us
    concatenate x2, other arithmetic, project(): rows = jnp.concatenate([rows, swap_seq(rows, CORE)], axis=0)  4.23 us
    ppermute x1, starting transfers between devices, body_by_head(): lax.ppermute(frames[tok_rows - RIM:], FOUR, [(i, i + 1) for i in range(de...  3.63 us
  transfers between devices with their start and end apart: 22, of which 8 were waited for; matrix products, arithmetic and copies ran while one was open for 31% of the time, Pallas kernels for 1%

profile of v6, /device:TPU:0, one launch (start us, length us, event | category | flops | bytes accessed | tf_op | source)
XLA Modules:
  0.0 113.2 jit_solution(11462987639682477295)
XLA Ops:
  1.9 6.9 %collective-permute-start.5 = (bf16[64,1024]{1,0:T(8,128)(2,1)S(1)}, bf16[64,1024]{1,0:T(8,128)(2,1)S(1)}, u32[]{:S(2)}, u32[]{:S(2)}) collective-permute-start(bf16[64,1024]{1,0:T(8,128)(2,1)S(1)} %get-tuple-element.18), channel_id=1, source_target_pairs={{0,4},{1,2},{2,7},{3,9},{4,14},{5,0},{6,5},{7,3},{8,12},{9,10},{10... | collective-permute-start | bytes 393224 | tf_op jit(solution)/shard_map/ppermute | solution.py:210
  8.7 1.9 %collective-permute-start.6 = (bf16[64,1024]{1,0:T(8,128)(2,1)S(1)}, bf16[64,1024]{1,0:T(8,128)(2,1)S(1)}, u32[]{:S(2)}, u32[]{:S(2)}) collective-permute-start(bf16[64,1024]{1,0:T(8,128)(2,1)S(1)} %get-tuple-element.17), channel_id=1, source_target_pairs={{0,1},{1,6},{2,8},{3,13},{4,11},{5,4},{6,2},{7,7},{8,9},{9,14},{10... | collective-permute-start | bytes 393224 | tf_op jit(solution)/shard_map/ppermute | solution.py:210
  11.5 3.6 %collective-permute-start.1 = (bf16[16,2048]{1,0:T(8,128)(2,1)S(1)}, bf16[16,2048]{1,0:T(8,128)(2,1)S(1)}, u32[]{:S(2)}, u32[]{:S(2)}) collective-permute-start(bf16[16,2048]{1,0:T(8,128)(2,1)S(1)} %slice.150), channel_id=1, source_target_pairs={{0,1},{1,2},{2,3},{3,4},{4,5},{5,6},{6,7},{7,8},{8,9},{9,10},{10,1... | collective-permute-start | bytes 196616 | tf_op jit(solution)/shard_map/ppermute | solution.py:222
  20.0 2.8 %collective-permute-start.13 = (bf16[64,2048]{1,0:T(8,128)(2,1)S(1)}, bf16[64,2048]{1,0:T(8,128)(2,1)S(1)}, u32[]{:S(2)}, u32[]{:S(2)}) collective-permute-start(bf16[64,2048]{1,0:T(8,128)(2,1)S(1)} %conv_late.1.late_ref), channel_id=1, source_target_pairs={{0,8},{1,9},{2,10},{3,11},{4,12},{5,13},{6,14},{7,15},{8,0},{9,1},... | collective-permute-start | bytes 786440 | tf_op jit(solution)/shard_map/ppermute | solution.py:114
  23.7 1.5 %collective-permute-start.7 = (bf16[3,64,1024]{2,1,0:T(8,128)(2,1)}, bf16[3,64,1024]{2,1,0:T(8,128)(2,1)S(1)}, u32[]{:S(2)}, u32[]{:S(2)}) collective-permute-start(bf16[3,64,1024]{2,1,0:T(8,128)(2,1)} %constant_dynamic-slice_fusion), channel_id=1, source_target_pairs={{0,16},{16,0},{1,17},{17,1},{2,18},{18,2},{3,19},{19,3},{4,20},{20... | collective-permute-start | bytes 1179656 | tf_op jit(solution)/shard_map/ppermute | solution.py:118
  26.9 1.9 %collective-permute-start.8 = (bf16[3,64,1024]{2,1,0:T(8,128)(2,1)}, bf16[3,64,1024]{2,1,0:T(8,128)(2,1)}, u32[]{:S(2)}, u32[]{:S(2)}) collective-permute-start(bf16[3,64,1024]{2,1,0:T(8,128)(2,1)} %constant_dynamic-slice_fusion), channel_id=1, source_target_pairs={{0,4},{1,5},{2,6},{3,7},{4,0},{5,1},{6,2},{7,3},{8,12},{9,13},{10,... | collective-permute-start | bytes 1179656 | tf_op jit(solution)/shard_map/ppermute | solution.py:114
  30.9 4.9 %collective-permute-done.13.refs_0_ = bf16[64,2048]{1,0:T(8,128)(2,1)S(1)} collective-permute-done((bf16[64,2048]{1,0:T(8,128)(2,1)S(1)}, bf16[64,2048]{1,0:T(8,128)(2,1)S(1)}, u32[]{:S(2)}, u32[]{:S(2)}) %collective-permute-start.13) | collective-permute-done | bytes 262176 | tf_op jit(solution)/shard_map/ppermute | solution.py:114
  39.2 4.5 %collective-permute-done.8 = bf16[3,64,1024]{2,1,0:T(8,128)(2,1)} collective-permute-done((bf16[3,64,1024]{2,1,0:T(8,128)(2,1)}, bf16[3,64,1024]{2,1,0:T(8,128)(2,1)}, u32[]{:S(2)}, u32[]{:S(2)}) %collective-permute-start.8) | collective-permute-done | bytes 393248 | tf_op jit(solution)/shard_map/ppermute | solution.py:114
  46.8 5.7 %collective-permute-done.16 = bf16[64,2048]{1,0:T(8,128)(2,1)S(1)} collective-permute-done((bf16[64,2048]{1,0:T(8,128)(2,1)}, bf16[64,2048]{1,0:T(8,128)(2,1)S(1)}, u32[]{:S(2)}, u32[]{:S(2)}) %collective-permute-start.16) | collective-permute-done | bytes 262176 | tf_op jit(solution)/shard_map/ppermute | solution.py:114
  53.2 1.5 %collective-permute-done.9.refs_1_ = bf16[3,64,1024]{2,1,0:T(8,128)(2,1)S(1)} collective-permute-done((bf16[3,64,1024]{2,1,0:T(8,128)(2,1)}, bf16[3,64,1024]{2,1,0:T(8,128)(2,1)S(1)}, u32[]{:S(2)}, u32[]{:S(2)}) %collective-permute-start.9) | collective-permute-done | bytes 393248 | tf_op jit(solution)/shard_map/ppermute | solution.py:118
  56.3 1.6 %copy.22 = bf16[3,2,64,2,1024]{4,3,2,1,0:T(2,128)(2,1)S(1)} copy(bf16[3,2,64,2,1024]{4,2,0,3,1:T(8,128)(2,1)S(1)} %pad_maximum_fusion) | data formatting | bytes 3145728 | tf_op jit(solution)/shard_map/stack | solution.py:188
  57.9 1.6 %copy.25 = bf16[48,8,2,1024]{3,1,2,0:T(8,128)(2,1)} copy(bf16[48,8,2,1024]{3,2,1,0:T(2,128)(2,1)S(1)} %bitcast.126) | data formatting | bytes 3145728
  59.6 2.2 %pad_maximum_fusion.2.refs_0_ = bf16[256,2048]{1,0:T(8,128)(2,1)} fusion(bf16[128,2048]{1,0:T(8,128)(2,1)} %collective-permute-done.15, bf16[64,2048]{1,0:T(8,128)(2,1)S(1)} %copy-done.13, bf16[64,2048]{1,0:T(8,128)(2,1)S(1)} %copy-done.7), kind=kLoop, calls=%fused_computation.17 | loop fusion | flops 3145728 | bytes 2097152 | tf_op jit(solution)/shard_map/concatenate | solution.py:245
  61.8 3.4 %fusion.8.refs_1_ = bf16[512,384]{1,0:T(8,128)(2,1)} fusion(bf16[384,2048]{1,0:T(8,128)(2,1)S(1)} %bitcast.129, bf16[256,2048]{1,0:T(8,128)(2,1)} %collective-permute-done.3, bf16[128,2048]{1,0:T(8,128)(2,1)} %collective-permute-done.2, bf16[128,2048]{1,0:T(8,128)(2,1)S(1)} %get-tuple-element.7), kind=kOutput, calls=%fused_computation.12 | convolution fusion | flops 811794432 | bytes 4063232 | tf_op jit(solution)/shard_map/dot_general | solution.py:246
  66.5 2.5 %convolution_convert_fusion.1 = bf16[256,384]{1,0:T(8,128)(2,1)S(1)} fusion(bf16[256,2048]{1,0:T(8,128)(2,1)} %after.9, bf16[384,2048]{1,0:T(8,128)(2,1)} %bitcast.127), kind=kOutput, calls=%fused_computation.15 | convolution fusion | flops 402751488 | bytes 2818048 | tf_op jit(solution)/shard_map/dot_general | solution.py:246
  72.2 2.5 %collective-permute-start.19 = (bf16[512,256]{1,0:T(8,128)(2,1)S(1)}, bf16[512,256]{1,0:T(8,128)(2,1)S(1)}, u32[]{:S(2)}, u32[]{:S(2)}) collective-permute-start(bf16[512,256]{1,0:T(8,128)(2,1)S(1)} %get-tuple-element.15), channel_id=1, source_target_pairs={{0,4},{1,5},{2,6},{3,7},{4,0},{5,1},{6,2},{7,3},{8,12},{9,13},{10,... | collective-permute-start | bytes 786440 | tf_op jit(solution)/shard_map/ppermute | solution.py:114
  76.3 3.4 %collective-permute-done.12 = s32[8,128]{1,0:T(8,128)S(1)} collective-permute-done((s32[8,128]{1,0:T(8,128)S(1)}, s32[8,128]{1,0:T(8,128)S(1)}, u32[]{:S(2)}, u32[]{:S(2)}) %collective-permute-start.12) | collective-permute-done | bytes 4128 | tf_op jit(solution)/shard_map/ppermute | solution.py:114
  80.6 2.0 %pad_maximum_fusion.3.refs_0_ = bf16[256,2048]{1,0:T(8,128)(2,1)} fusion(bf16[128,2048]{1,0:T(8,128)(2,1)S(1)} %collective-permute-done.18, bf16[64,2048]{1,0:T(8,128)(2,1)} %after.12, bf16[64,2048]{1,0:T(8,128)(2,1)S(1)} %collective-permute-done.16), kind=kLoop, calls=%fused_computation.18 | loop fusion | flops 3145728 | bytes 2097152 | tf_op jit(solution)/shard_map/concatenate | solution.py:245
  82.6 2.5 %convolution_convert_fusion = bf16[256,384]{1,0:T(8,128)(2,1)S(1)} fusion(bf16[256,2048]{1,0:T(8,128)(2,1)} %after.13, bf16[384,2048]{1,0:T(8,128)(2,1)} %bitcast.128), kind=kOutput, calls=%fused_computation.14 | convolution fusion | flops 402751488 | bytes 2818048 | tf_op jit(solution)/shard_map/dot_general | solution.py:246
  85.8 1.9 %collective-permute-start.21 = (bf16[256,256]{1,0:T(8,128)(2,1)S(1)}, bf16[256,256]{1,0:T(8,128)(2,1)S(1)}, u32[]{:S(2)}, u32[]{:S(2)}) collective-permute-start(bf16[256,256]{1,0:T(8,128)(2,1)S(1)} %get-tuple-element.20), channel_id=1, source_target_pairs={{0,4},{1,5},{2,6},{3,7},{4,0},{5,1},{6,2},{7,3},{8,12},{9,13},{10,... | collective-permute-start | bytes 393224 | tf_op jit(solution)/shard_map/ppermute | solution.py:114
  89.1 1.7 %collective-permute-done.21 = bf16[256,256]{1,0:T(8,128)(2,1)S(1)} collective-permute-done((bf16[256,256]{1,0:T(8,128)(2,1)S(1)}, bf16[256,256]{1,0:T(8,128)(2,1)S(1)}, u32[]{:S(2)}, u32[]{:S(2)}) %collective-permute-start.21) | collective-permute-done | bytes 131104 | tf_op jit(solution)/shard_map/ppermute | solution.py:114
  91.4 3.3 %fusion.37 = (f32[1024]{0:T(1024)S(1)}, f32[1024,2048]{1,0:T(8,128)S(1)}) fusion(bf16[2048,256]{1,0:T(8,128)(2,1)} %constant_dynamic-update-slice_fusion, bf16[256,128]{1,0:T(8,128)(2,1)S(1)} %slice.203, bf16[256,128]{1,0:T(8,128)(2,1)S(1)} %slice-done.1, bf16[512,128]{1,0:T(8,128)(2,1)S(1)} %slice-done, s32[1024]{0:T(1024)S(1)} %concatenate.91, ...), kind=kOutput, calls=%fused_computation.133 | convolution fusion | flops 550239232 | bytes 9203712 | tf_op jit(solution)/shard_map/dot_general | solution.py:284
  96.0 2.6 %fusion.11 = bf16[1024,128]{1,0:T(8,128)(2,1)S(1)} fusion(f32[1024,2048]{1,0:T(8,128)S(1)} %get-tuple-element.49, f32[1024]{0:T(1024)S(1)} %fusion, f32[1024]{0:T(1024)S(1)} %get-tuple-element.48, bf16[2048,256]{1,0:T(8,128)(2,1)} %constant_dynamic-update-slice_fusion), kind=kOutput, calls=%fused_computation.13 | convolution fusion | flops 543293440 | bytes 9183232 | tf_op jit(solution)/shard_map/dot_general | solution.py:293
  98.9 13.3 %all_to_all.5 = bf16[8,128,128]{2,1,0:T(8,128)(2,1)S(1)} all-to-all(bf16[8,128,128]{2,1,0:T(8,128)(2,1)S(1)} %fusion.23), channel_id=1, replica_groups=mesh['grp'=2,'far'=2,'near'=2,'quad'=4] {'far','quad'}, dimensions={0} | all-to-all | bytes 524288 | tf_op jit(solution)/shard_map/all_to_all | solution.py:303
  (142 shorter events, 33.0 us)
Async XLA Ops:
  0.0 18.9 %copy-start.1 = (bf16[128,2048]{1,0:T(8,128)(2,1)S(1)}, bf16[128,2048]{1,0:T(8,128)(2,1)}, u32[]{:S(2)}) copy-start(bf16[128,2048]{1,0:T(8,128)(2,1)} %frames_ref.3) | copy-start | bytes 1572868
  1.2 24.6 %copy-start.4 = (bf16[4,2048]{1,0:T(4,128)(2,1)S(1)}, bf16[4,2048]{1,0:T(4,128)(2,1)}, u32[]{:S(2)}) copy-start(bf16[4,2048]{1,0:T(4,128)(2,1)} %taps_ref.3) | copy-start | bytes 49156
  1.2 18.7 %collective-permute-start.4 = (bf16[64,1024]{1,0:T(8,128)(2,1)S(1)}, bf16[64,1024]{1,0:T(8,128)(2,1)S(1)}, u32[]{:S(2)}, u32[]{:S(2)}) collective-permute-start(bf16[64,1024]{1,0:T(8,128)(2,1)S(1)} %get-tuple-element.19), channel_id=1, source_target_pairs={{0,0},{1,5},{2,3},{3,12},{4,10},{5,15},{6,1},{7,6},{8,8},{9,13},{1... | collective-permute-start | bytes 393224 | tf_op jit(solution)/shard_map/ppermute | solution.py:210
  1.9 20.9 %collective-permute-start.5 = (bf16[64,1024]{1,0:T(8,128)(2,1)S(1)}, bf16[64,1024]{1,0:T(8,128)(2,1)S(1)}, u32[]{:S(2)}, u32[]{:S(2)}) collective-permute-start(bf16[64,1024]{1,0:T(8,128)(2,1)S(1)} %get-tuple-element.18), channel_id=1, source_target_pairs={{0,4},{1,2},{2,7},{3,9},{4,14},{5,0},{6,5},{7,3},{8,12},{9,10},{10... | collective-permute-start | bytes 393224 | tf_op jit(solution)/shard_map/ppermute | solution.py:210
  8.7 14.1 %collective-permute-start.6 = (bf16[64,1024]{1,0:T(8,128)(2,1)S(1)}, bf16[64,1024]{1,0:T(8,128)(2,1)S(1)}, u32[]{:S(2)}, u32[]{:S(2)}) collective-permute-start(bf16[64,1024]{1,0:T(8,128)(2,1)S(1)} %get-tuple-element.17), channel_id=1, source_target_pairs={{0,1},{1,6},{2,8},{3,13},{4,11},{5,4},{6,2},{7,7},{8,9},{9,14},{10... | collective-permute-start | bytes 393224 | tf_op jit(solution)/shard_map/ppermute | solution.py:210
  11.5 14.3 %collective-permute-start.1 = (bf16[16,2048]{1,0:T(8,128)(2,1)S(1)}, bf16[16,2048]{1,0:T(8,128)(2,1)S(1)}, u32[]{:S(2)}, u32[]{:S(2)}) collective-permute-start(bf16[16,2048]{1,0:T(8,128)(2,1)S(1)} %slice.150), channel_id=1, source_target_pairs={{0,1},{1,2},{2,3},{3,4},{4,5},{5,6},{6,7},{7,8},{8,9},{9,10},{10,1... | collective-permute-start | bytes 196616 | tf_op jit(solution)/shard_map/ppermute | solution.py:222
  16.5 13.1 %collective-permute-start = (s32[1,128]{1,0:T(1,128)}, s32[1,128]{1,0:T(1,128)}, u32[]{:S(2)}, u32[]{:S(2)}) collective-permute-start(s32[1,128]{1,0:T(1,128)} %bitcast), channel_id=1, source_target_pairs={{0,4},{1,5},{2,6},{3,7},{4,0},{5,1},{6,2},{7,3},{8,12},{9,13},{10,... | collective-permute-start | bytes 1544 | tf_op jit(solution)/shard_map/ppermute | solution.py:114
  20.0 15.8 %collective-permute-start.13 = (bf16[64,2048]{1,0:T(8,128)(2,1)S(1)}, bf16[64,2048]{1,0:T(8,128)(2,1)S(1)}, u32[]{:S(2)}, u32[]{:S(2)}) collective-permute-start(bf16[64,2048]{1,0:T(8,128)(2,1)S(1)} %conv_late.1.late_ref), channel_id=1, source_target_pairs={{0,8},{1,9},{2,10},{3,11},{4,12},{5,13},{6,14},{7,15},{8,0},{9,1},... | collective-permute-start | bytes 786440 | tf_op jit(solution)/shard_map/ppermute | solution.py:114
  23.7 12.0 %collective-permute-start.7 = (bf16[3,64,1024]{2,1,0:T(8,128)(2,1)}, bf16[3,64,1024]{2,1,0:T(8,128)(2,1)S(1)}, u32[]{:S(2)}, u32[]{:S(2)}) collective-permute-start(bf16[3,64,1024]{2,1,0:T(8,128)(2,1)} %constant_dynamic-slice_fusion), channel_id=1, source_target_pairs={{0,16},{16,0},{1,17},{17,1},{2,18},{18,2},{3,19},{19,3},{4,20},{20... | collective-permute-start | bytes 1179656 | tf_op jit(solution)/shard_map/ppermute | solution.py:118
  26.8 17.4 %collective-permute-start.2 = (bf16[128,2048]{1,0:T(8,128)(2,1)S(1)}, bf16[128,2048]{1,0:T(8,128)(2,1)}, u32[]{:S(2)}, u32[]{:S(2)}) collective-permute-start(bf16[128,2048]{1,0:T(8,128)(2,1)S(1)} %get-tuple-element.7), channel_id=1, source_target_pairs={{0,2},{1,3},{2,0},{3,1},{4,6},{5,7},{6,4},{7,5},{8,10},{9,11},{10,... | collective-permute-start | bytes 1572872 | tf_op jit(solution)/shard_map/ppermute | solution.py:114
  26.9 16.8 %collective-permute-start.8 = (bf16[3,64,1024]{2,1,0:T(8,128)(2,1)}, bf16[3,64,1024]{2,1,0:T(8,128)(2,1)}, u32[]{:S(2)}, u32[]{:S(2)}) collective-permute-start(bf16[3,64,1024]{2,1,0:T(8,128)(2,1)} %constant_dynamic-slice_fusion), channel_id=1, source_target_pairs={{0,4},{1,5},{2,6},{3,7},{4,0},{5,1},{6,2},{7,3},{8,12},{9,13},{10,... | collective-permute-start | bytes 1179656 | tf_op jit(solution)/shard_map/ppermute | solution.py:114
  37.2 8.5 %collective-permute-start.14 = (bf16[64,2048]{1,0:T(8,128)(2,1)}, bf16[64,2048]{1,0:T(8,128)(2,1)S(1)}, u32[]{:S(2)}, u32[]{:S(2)}) collective-permute-start(bf16[64,2048]{1,0:T(8,128)(2,1)} %after.8.refs_1_), channel_id=1, source_target_pairs={{0,2},{1,3},{2,0},{3,1},{4,6},{5,7},{6,4},{7,5},{8,10},{9,11},{10,... | collective-permute-start | bytes 786440 | tf_op jit(solution)/shard_map/ppermute | solution.py:114
  38.1 14.5 %collective-permute-start.16 = (bf16[64,2048]{1,0:T(8,128)(2,1)}, bf16[64,2048]{1,0:T(8,128)(2,1)S(1)}, u32[]{:S(2)}, u32[]{:S(2)}) collective-permute-start(bf16[64,2048]{1,0:T(8,128)(2,1)} %after.10), channel_id=1, source_target_pairs={{0,8},{1,9},{2,10},{3,11},{4,12},{5,13},{6,14},{7,15},{8,0},{9,1},... | collective-permute-start | bytes 786440 | tf_op jit(solution)/shard_map/ppermute | solution.py:114
  43.7 11.1 %collective-permute-start.9 = (bf16[3,64,1024]{2,1,0:T(8,128)(2,1)}, bf16[3,64,1024]{2,1,0:T(8,128)(2,1)S(1)}, u32[]{:S(2)}, u32[]{:S(2)}) collective-permute-start(bf16[3,64,1024]{2,1,0:T(8,128)(2,1)} %collective-permute-done.8), channel_id=1, source_target_pairs={{0,16},{16,0},{1,17},{17,1},{2,18},{18,2},{3,19},{19,3},{4,20},{20... | collective-permute-start | bytes 1179656 | tf_op jit(solution)/shard_map/ppermute | solution.py:118
  45.3 16.5 %collective-permute-start.3 = (bf16[256,2048]{1,0:T(8,128)(2,1)S(1)}, bf16[256,2048]{1,0:T(8,128)(2,1)}, u32[]{:S(2)}, u32[]{:S(2)}) collective-permute-start(bf16[256,2048]{1,0:T(8,128)(2,1)S(1)} %pad_maximum_fusion.1), channel_id=1, source_target_pairs={{0,1},{1,0},{2,3},{3,2},{4,5},{5,4},{6,7},{7,6},{8,9},{9,8},{10,11... | collective-permute-start | bytes 3145736 | tf_op jit(solution)/shard_map/ppermute | solution.py:114
  46.6 13.0 %collective-permute-start.15 = (bf16[128,2048]{1,0:T(8,128)(2,1)}, bf16[128,2048]{1,0:T(8,128)(2,1)}, u32[]{:S(2)}, u32[]{:S(2)}) collective-permute-start(bf16[128,2048]{1,0:T(8,128)(2,1)} %pad_maximum_fusion.6), channel_id=1, source_target_pairs={{0,1},{1,0},{2,3},{3,2},{4,5},{5,4},{6,7},{7,6},{8,9},{9,8},{10,11... | collective-permute-start | bytes 1572872 | tf_op jit(solution)/shard_map/ppermute | solution.py:114
  59.6 10.8 %collective-permute-start.17 = (bf16[64,2048]{1,0:T(8,128)(2,1)}, bf16[64,2048]{1,0:T(8,128)(2,1)S(1)}, u32[]{:S(2)}, u32[]{:S(2)}) collective-permute-start(bf16[64,2048]{1,0:T(8,128)(2,1)} %after.11), channel_id=1, source_target_pairs={{0,2},{1,3},{2,0},{3,1},{4,6},{5,7},{6,4},{7,5},{8,10},{9,11},{10,... | collective-permute-start | bytes 786440 | tf_op jit(solution)/shard_map/ppermute | solution.py:114
  65.2 9.6 %collective-permute-start.10 = (s32[2,128]{1,0:T(2,128)}, s32[2,128]{1,0:T(2,128)S(1)}, u32[]{:S(2)}, u32[]{:S(2)}) collective-permute-start(s32[2,128]{1,0:T(2,128)} %after.7), channel_id=1, source_target_pairs={{0,8},{1,9},{2,10},{3,11},{4,12},{5,13},{6,14},{7,15},{8,0},{9,1},... | collective-permute-start | bytes 3080 | tf_op jit(solution)/shard_map/ppermute | solution.py:114
  72.1 8.5 %collective-permute-start.18 = (bf16[128,2048]{1,0:T(8,128)(2,1)S(1)}, bf16[128,2048]{1,0:T(8,128)(2,1)S(1)}, u32[]{:S(2)}, u32[]{:S(2)}) collective-permute-start(bf16[128,2048]{1,0:T(8,128)(2,1)S(1)} %pad_maximum_fusion.7), channel_id=1, source_target_pairs={{0,1},{1,0},{2,3},{3,2},{4,5},{5,4},{6,7},{7,6},{8,9},{9,8},{10,11... | collective-permute-start | bytes 1572872 | tf_op jit(solution)/shard_map/ppermute | solution.py:114
  72.2 15.6 %collective-permute-start.19 = (bf16[512,256]{1,0:T(8,128)(2,1)S(1)}, bf16[512,256]{1,0:T(8,128)(2,1)S(1)}, u32[]{:S(2)}, u32[]{:S(2)}) collective-permute-start(bf16[512,256]{1,0:T(8,128)(2,1)S(1)} %get-tuple-element.15), channel_id=1, source_target_pairs={{0,4},{1,5},{2,6},{3,7},{4,0},{5,1},{6,2},{7,3},{8,12},{9,13},{10,... | collective-permute-start | bytes 786440 | tf_op jit(solution)/shard_map/ppermute | solution.py:114
  74.7 13.7 %collective-permute-start.20 = (bf16[256,256]{1,0:T(8,128)(2,1)S(1)}, bf16[256,256]{1,0:T(8,128)(2,1)S(1)}, u32[]{:S(2)}, u32[]{:S(2)}) collective-permute-start(bf16[256,256]{1,0:T(8,128)(2,1)S(1)} %get-tuple-element.22), channel_id=1, source_target_pairs={{0,4},{1,5},{2,6},{3,7},{4,0},{5,1},{6,2},{7,3},{8,12},{9,13},{10,... | collective-permute-start | bytes 393224 | tf_op jit(solution)/shard_map/ppermute | solution.py:114
  74.8 1.2 %collective-permute-start.11 = (s32[4,128]{1,0:T(4,128)S(1)}, s32[4,128]{1,0:T(4,128)S(1)}, u32[]{:S(2)}, u32[]{:S(2)}) collective-permute-start(s32[4,128]{1,0:T(4,128)S(1)} %pad_add_fusion.2), channel_id=1, source_target_pairs={{0,1},{1,0},{2,3},{3,2},{4,5},{5,4},{6,7},{7,6},{8,9},{9,8},{10,11... | collective-permute-start | bytes 6152 | tf_op jit(solution)/shard_map/ppermute | solution.py:114
  76.0 3.7 %collective-permute-start.12 = (s32[8,128]{1,0:T(8,128)S(1)}, s32[8,128]{1,0:T(8,128)S(1)}, u32[]{:S(2)}, u32[]{:S(2)}) collective-permute-start(s32[8,128]{1,0:T(8,128)S(1)} %pad_add_fusion.1), channel_id=1, source_target_pairs={{0,2},{1,3},{2,0},{3,1},{4,6},{5,7},{6,4},{7,5},{8,10},{9,11},{10,... | collective-permute-start | bytes 12296 | tf_op jit(solution)/shard_map/ppermute | solution.py:114
  85.8 5.0 %collective-permute-start.21 = (bf16[256,256]{1,0:T(8,128)(2,1)S(1)}, bf16[256,256]{1,0:T(8,128)(2,1)S(1)}, u32[]{:S(2)}, u32[]{:S(2)}) collective-permute-start(bf16[256,256]{1,0:T(8,128)(2,1)S(1)} %get-tuple-element.20), channel_id=1, source_target_pairs={{0,4},{1,5},{2,6},{3,7},{4,0},{5,1},{6,2},{7,3},{8,12},{9,13},{10,... | collective-permute-start | bytes 393224 | tf_op jit(solution)/shard_map/ppermute | solution.py:114
  (16 other events, 66.2 us)

commit v7 on v6

--- a/solution.py
+++ b/solution.py
@@ -106,7 +106,7 @@
 CORE, Y, NEAR, FAR = 1, 2, 4, 8
 QUADS = (0, Y, CORE, Y | CORE)
 RIM = 16
-VMEM_LIMIT = 40 * 2**20
+VMEM_LIMIT = 6 * 2**20
 
 
 def swap_seq(value, bit):
@@ -156,6 +156,7 @@
         in_specs=[anywhere] * (1 + len(others)),
         out_specs=anywhere,
         input_output_aliases={0: 0},
+        compiler_params=pltpu.CompilerParams(vmem_limit_bytes=2**20),
         name="after",
     )(value, *others)
 

time: 114 us -> 102 us (0.89)
  waiting for transfers between devices: 23 us -> 34.7 us
  matrix products: 14.3 us -> 6.62 us
  other arithmetic: 17.3 us -> 10.6 us
  local copies, waits for them, and re-layouts: 17.1 us -> 12.8 us
  starting transfers between devices: 27.2 us -> 23.8 us
  blocking collectives: 13.3 us -> 11.9 us
    ppermute x16, waiting for transfers between devices: 21.4 us -> 30.7 us  [swap_seq(): return lax.ppermute(value, FOUR, [(d, d ^ bit) for d in range(count)])]
    dot_general x3, matrix products: 8.33 us -> 2.72 us  [project(): lax.dot_general(after(rows, *others) if others else rows, head_weight, ((...]
    unnamed x40 -> x38, local copies, waits for them, and re-layouts: 8.51 us -> 3.71 us
    concatenate x2, other arithmetic: 4.23 us -> 0.14 us  [project(): rows = jnp.concatenate([rows, swap_seq(rows, CORE)], axis=0)]
    ppermute x16, starting transfers between devices: 12.1 us -> 8.76 us  [swap_seq(): return lax.ppermute(value, FOUR, [(d, d ^ bit) for d in range(count)])]
    concatenate x3, other arithmetic: 3 us -> 0.15 us  [project(): rows = jnp.concatenate(rows, axis=0)]
    ppermute x2, waiting for transfers between devices: 1.54 us -> 3.99 us  [swap_grp(): return lax.ppermute(value, 'grp', [(0, 1), (1, 0)])]
    slice x8, local copies, waits for them, and re-layouts: 2.12 us -> 0.09 us  [project(): parts.append((done[:, :HD], done[:, HD:], swap_seq(done[:, HD:], NEAR)))]
  transfers between devices with their start and end apart: 22 -> 22, of which waited for: 8 -> 10; matrix products, arithmetic and copies ran while one was open for 31% -> 20% of each run, Pallas kernels for 1% -> 1%
where the time goes in v7:
time: 102 us
  waiting for transfers between devices  34.7 us (34%)
  starting transfers between devices  23.8 us (23%)
  local copies, waits for them, and re-layouts  12.8 us (13%)
  blocking collectives  11.9 us (12%)
  other arithmetic  10.6 us (10%)
  matrix products  6.62 us (6%)
    ppermute x16, waiting for transfers between devices, swap_seq(): return lax.ppermute(value, FOUR, [(d, d ^ bit) for d in range(count)])  30.7 us
    all_to_all x1, blocking collectives, body_by_head(): lax.all_to_all(sent, ('far', 'quad'), split_axis=0, concat_axis=0, tiled=...  11.9 us
    ppermute x3, starting transfers between devices, body_by_head(): lax.ppermute(held[j], FOUR, [(d, home(3 * d + j)) for d in range(devices)])  9.43 us
    ppermute x16, starting transfers between devices, swap_seq(): return lax.ppermute(value, FOUR, [(d, d ^ bit) for d in range(count)])  8.76 us
    add x12, other arithmetic, of_rows(): (me ^ hop ^ bit) * tok_rows + start + jnp.arange(count, dtype=jnp.int32)  4.65 us
    ppermute x2, waiting for transfers between devices, swap_grp(): return lax.ppermute(value, 'grp', [(0, 1), (1, 0)])  3.99 us
    unnamed x38, local copies, waits for them, and re-layouts  3.71 us
    ppermute x1, starting transfers between devices, body_by_head(): lax.ppermute(frames[tok_rows - RIM:], FOUR, [(i, i + 1) for i in range(de...  3.63 us
  transfers between devices with their start and end apart: 22, of which 10 were waited for; matrix products, arithmetic and copies ran while one was open for 20% of the time, Pallas kernels for 1%

profile of v7, /device:TPU:0, one launch (start us, length us, event | category | flops | bytes accessed | tf_op | source)
XLA Modules:
  0.0 101.9 jit_solution(6468562880222210758)
XLA Ops:
  0.0 1.1 %copy-done = bf16[2048,192]{0,1:T(8,128)(2,1)S(1)} copy-done((bf16[2048,192]{0,1:T(8,128)(2,1)S(1)}, bf16[2048,192]{0,1:T(8,128)(2,1)}, u32[]{:S(2)}) %copy-start) | copy-done | bytes 786456
  1.9 6.9 %collective-permute-start.5 = (bf16[64,1024]{1,0:T(8,128)(2,1)S(1)}, bf16[64,1024]{1,0:T(8,128)(2,1)S(1)}, u32[]{:S(2)}, u32[]{:S(2)}) collective-permute-start(bf16[64,1024]{1,0:T(8,128)(2,1)S(1)} %get-tuple-element.18), channel_id=1, source_target_pairs={{0,4},{1,2},{2,7},{3,9},{4,14},{5,0},{6,5},{7,3},{8,12},{9,10},{10... | collective-permute-start | bytes 393224 | tf_op jit(solution)/shard_map/ppermute | solution.py:211
  8.7 1.9 %collective-permute-start.6 = (bf16[64,1024]{1,0:T(8,128)(2,1)S(1)}, bf16[64,1024]{1,0:T(8,128)(2,1)S(1)}, u32[]{:S(2)}, u32[]{:S(2)}) collective-permute-start(bf16[64,1024]{1,0:T(8,128)(2,1)S(1)} %get-tuple-element.17), channel_id=1, source_target_pairs={{0,1},{1,6},{2,8},{3,13},{4,11},{5,4},{6,2},{7,7},{8,9},{9,14},{10... | collective-permute-start | bytes 393224 | tf_op jit(solution)/shard_map/ppermute | solution.py:211
  11.5 3.6 %collective-permute-start.1 = (bf16[16,2048]{1,0:T(8,128)(2,1)S(1)}, bf16[16,2048]{1,0:T(8,128)(2,1)S(1)}, u32[]{:S(2)}, u32[]{:S(2)}) collective-permute-start(bf16[16,2048]{1,0:T(8,128)(2,1)S(1)} %slice.150), channel_id=1, source_target_pairs={{0,1},{1,2},{2,3},{3,4},{4,5},{5,6},{6,7},{7,8},{8,9},{9,10},{10,1... | collective-permute-start | bytes 196616 | tf_op jit(solution)/shard_map/ppermute | solution.py:223
  15.2 1.3 %select_reduce_fusion = s32[128]{0:T(128)} fusion(s32[64]{0:T(128)} %param.9, s32[128]{0:T(128)} %param.8), kind=kLoop, calls=%fused_computation.50 | loop fusion | flops 24448 | bytes 1280 | tf_op jit(solution)/shard_map/reduce_sum | solution.py:21
  21.6 2.8 %collective-permute-start.13 = (bf16[64,2048]{1,0:T(8,128)(2,1)S(1)}, bf16[64,2048]{1,0:T(8,128)(2,1)S(1)}, u32[]{:S(2)}, u32[]{:S(2)}) collective-permute-start(bf16[64,2048]{1,0:T(8,128)(2,1)S(1)} %conv_late.1.late_ref), channel_id=1, source_target_pairs={{0,8},{1,9},{2,10},{3,11},{4,12},{5,13},{6,14},{7,15},{8,0},{9,1},... | collective-permute-start | bytes 786440 | tf_op jit(solution)/shard_map/ppermute | solution.py:114
  25.3 1.5 %collective-permute-start.7 = (bf16[3,64,1024]{2,1,0:T(8,128)(2,1)}, bf16[3,64,1024]{2,1,0:T(8,128)(2,1)S(1)}, u32[]{:S(2)}, u32[]{:S(2)}) collective-permute-start(bf16[3,64,1024]{2,1,0:T(8,128)(2,1)} %constant_dynamic-slice_fusion), channel_id=1, source_target_pairs={{0,16},{16,0},{1,17},{17,1},{2,18},{18,2},{3,19},{19,3},{4,20},{20... | collective-permute-start | bytes 1179656 | tf_op jit(solution)/shard_map/ppermute | solution.py:118
  27.9 1.9 %collective-permute-start.8 = (bf16[3,64,1024]{2,1,0:T(8,128)(2,1)}, bf16[3,64,1024]{2,1,0:T(8,128)(2,1)}, u32[]{:S(2)}, u32[]{:S(2)}) collective-permute-start(bf16[3,64,1024]{2,1,0:T(8,128)(2,1)} %constant_dynamic-slice_fusion), channel_id=1, source_target_pairs={{0,4},{1,5},{2,6},{3,7},{4,0},{5,1},{6,2},{7,3},{8,12},{9,13},{10,... | collective-permute-start | bytes 1179656 | tf_op jit(solution)/shard_map/ppermute | solution.py:114
  29.8 1.4 %concatenate.84 = s32[1024]{0:T(1024)} concatenate(s32[128]{0:T(128)S(1)} %get-tuple-element.61, s32[128]{0:T(128)S(1)} %get-tuple-element.60, s32[128]{0:T(128)} %get-tuple-element.59, s32[128]{0:T(128)} %get-tuple-element.58, s32[64]{0:T(128)} %get-tuple-element.57, s32[64]{0:T(128)} %get-tuple-element.56, s32[64]{0:T(128)} %get-tuple-element.55, s32[64]{0:T(128)} %get-tuple-element.54, ...), dimensions={0} | concatenate | bytes 8192 | tf_op jit(solution)/shard_map/concatenate | solution.py:279
  32.7 4.6 %collective-permute-done.13.refs_0_ = bf16[64,2048]{1,0:T(8,128)(2,1)S(1)} collective-permute-done((bf16[64,2048]{1,0:T(8,128)(2,1)S(1)}, bf16[64,2048]{1,0:T(8,128)(2,1)S(1)}, u32[]{:S(2)}, u32[]{:S(2)}) %collective-permute-start.13) | collective-permute-done | bytes 262176 | tf_op jit(solution)/shard_map/ppermute | solution.py:114
  39.2 6.2 %collective-permute-done.8 = bf16[3,64,1024]{2,1,0:T(8,128)(2,1)} collective-permute-done((bf16[3,64,1024]{2,1,0:T(8,128)(2,1)}, bf16[3,64,1024]{2,1,0:T(8,128)(2,1)}, u32[]{:S(2)}, u32[]{:S(2)}) %collective-permute-start.8) | collective-permute-done | bytes 393248 | tf_op jit(solution)/shard_map/ppermute | solution.py:114
  46.9 5.6 %collective-permute-done.16 = bf16[64,2048]{1,0:T(8,128)(2,1)S(1)} collective-permute-done((bf16[64,2048]{1,0:T(8,128)(2,1)S(1)}, bf16[64,2048]{1,0:T(8,128)(2,1)S(1)}, u32[]{:S(2)}, u32[]{:S(2)}) %collective-permute-start.16) | collective-permute-done | bytes 262176 | tf_op jit(solution)/shard_map/ppermute | solution.py:114
  52.5 4.0 %collective-permute-done.9.refs_1_ = bf16[3,64,1024]{2,1,0:T(8,128)(2,1)S(1)} collective-permute-done((bf16[3,64,1024]{2,1,0:T(8,128)(2,1)}, bf16[3,64,1024]{2,1,0:T(8,128)(2,1)S(1)}, u32[]{:S(2)}, u32[]{:S(2)}) %collective-permute-start.9) | collective-permute-done | bytes 393248 | tf_op jit(solution)/shard_map/ppermute | solution.py:118
  57.8 1.6 %copy.22 = bf16[3,2,64,2,1024]{4,3,2,1,0:T(2,128)(2,1)S(1)} copy(bf16[3,2,64,2,1024]{4,2,0,3,1:T(8,128)(2,1)S(1)} %pad_maximum_fusion) | data formatting | bytes 3145728 | tf_op jit(solution)/shard_map/stack | solution.py:189
  60.1 1.3 %fusion.8.refs_1_ = bf16[512,384]{1,0:T(8,128)(2,1)S(1)} fusion(bf16[384,2048]{1,0:T(8,128)(2,1)S(1)} %bitcast.127, bf16[256,2048]{1,0:T(8,128)(2,1)S(1)} %collective-permute-done.3, bf16[128,2048]{1,0:T(8,128)(2,1)S(1)} %collective-permute-done.2, bf16[128,2048]{1,0:T(8,128)(2,1)S(1)} %get-tuple-element.7), kind=kOutput, calls=%fused_computation.12 | convolution fusion | flops 811794432 | bytes 4063232 | tf_op jit(solution)/shard_map/dot_general | solution.py:247
  62.6 4.5 %collective-permute-done.17.refs_0_ = bf16[64,2048]{1,0:T(8,128)(2,1)S(1)} collective-permute-done((bf16[64,2048]{1,0:T(8,128)(2,1)S(1)}, bf16[64,2048]{1,0:T(8,128)(2,1)S(1)}, u32[]{:S(2)}, u32[]{:S(2)}) %collective-permute-start.17) | collective-permute-done | bytes 262176 | tf_op jit(solution)/shard_map/ppermute | solution.py:114
  67.8 2.0 %collective-permute-start.20 = (bf16[256,256]{1,0:T(8,128)(2,1)S(1)}, bf16[256,256]{1,0:T(8,128)(2,1)S(1)}, u32[]{:S(2)}, u32[]{:S(2)}) collective-permute-start(bf16[256,256]{1,0:T(8,128)(2,1)S(1)} %get-tuple-element.22), channel_id=1, source_target_pairs={{0,4},{1,5},{2,6},{3,7},{4,0},{5,1},{6,2},{7,3},{8,12},{9,13},{10,... | collective-permute-start | bytes 393224 | tf_op jit(solution)/shard_map/ppermute | solution.py:114
  71.4 3.2 %collective-permute-done.12 = s32[8,128]{1,0:T(8,128)S(1)} collective-permute-done((s32[8,128]{1,0:T(8,128)S(1)}, s32[8,128]{1,0:T(8,128)S(1)}, u32[]{:S(2)}, u32[]{:S(2)}) %collective-permute-start.12) | collective-permute-done | bytes 4128 | tf_op jit(solution)/shard_map/ppermute | solution.py:114
  76.3 1.3 %copy-done.6 = bf16[48,8,2,1024]{3,1,2,0:T(8,128)(2,1)S(1)} copy-done((bf16[48,8,2,1024]{3,1,2,0:T(8,128)(2,1)S(1)}, bf16[48,8,2,1024]{3,1,2,0:T(8,128)(2,1)}, u32[]{:S(2)}) %copy-start.6) | copy-done | bytes 1572888
  79.3 4.1 %collective-permute-done.21 = bf16[256,256]{1,0:T(8,128)(2,1)S(1)} collective-permute-done((bf16[256,256]{1,0:T(8,128)(2,1)S(1)}, bf16[256,256]{1,0:T(8,128)(2,1)S(1)}, u32[]{:S(2)}, u32[]{:S(2)}) %collective-permute-start.21) | collective-permute-done | bytes 131104 | tf_op jit(solution)/shard_map/ppermute | solution.py:114
  83.5 2.3 %fusion.37 = (f32[1024]{0:T(1024)S(1)}, f32[1024,2048]{1,0:T(8,128)S(1)}) fusion(bf16[2048,256]{1,0:T(8,128)(2,1)S(1)} %constant_dynamic-update-slice_fusion, bf16[256,128]{1,0:T(8,128)(2,1)S(1)} %slice.203, bf16[256,128]{1,0:T(8,128)(2,1)S(1)} %slice-done.1, bf16[512,128]{1,0:T(8,128)(2,1)S(1)} %slice-done, s32[1024]{0:T(1024)S(1)} %copy-done.14, ...), kind=kOutput, calls=%fused_computation.133 | convolution fusion | flops 550239232 | bytes 9203712 | tf_op jit(solution)/shard_map/dot_general | solution.py:285
  85.8 1.3 %fusion = f32[1024]{0:T(1024)S(1)} fusion(f32[1024,2048]{1,0:T(8,128)S(1)} %get-tuple-element.49, f32[1024]{0:T(1024)S(1)} %get-tuple-element.48), kind=kLoop, calls=%fused_computation.3 | loop fusion | flops 4193280 | bytes 8396800 | tf_op jit(solution)/shard_map/reduce_sum | solution.py:293
  87.0 1.6 %fusion.11 = bf16[1024,128]{1,0:T(8,128)(2,1)S(1)} fusion(f32[1024,2048]{1,0:T(8,128)S(1)} %get-tuple-element.49, f32[1024]{0:T(1024)S(1)} %fusion, f32[1024]{0:T(1024)S(1)} %get-tuple-element.48, bf16[2048,256]{1,0:T(8,128)(2,1)S(1)} %constant_dynamic-update-slice_fusion), kind=kOutput, calls=%fused_computation.13 | convolution fusion | flops 543293440 | bytes 9183232 | tf_op jit(solution)/shard_map/dot_general | solution.py:294
  88.9 11.9 %all_to_all.5 = bf16[8,128,128]{2,1,0:T(8,128)(2,1)S(1)} all-to-all(bf16[8,128,128]{2,1,0:T(8,128)(2,1)S(1)} %fusion.23), channel_id=1, replica_groups=mesh['grp'=2,'far'=2,'near'=2,'quad'=4] {'far','quad'}, dimensions={0} | all-to-all | bytes 524288 | tf_op jit(solution)/shard_map/all_to_all | solution.py:304
  (140 shorter events, 23.4 us)
Async XLA Ops:
  0.0 19.9 %copy-start.2 = (bf16[128,2048]{1,0:T(8,128)(2,1)S(1)}, bf16[128,2048]{1,0:T(8,128)(2,1)}, u32[]{:S(2)}) copy-start(bf16[128,2048]{1,0:T(8,128)(2,1)} %frames_ref.3) | copy-start | bytes 1572868
  1.2 26.3 %copy-start.4 = (bf16[4,2048]{1,0:T(4,128)(2,1)S(1)}, bf16[4,2048]{1,0:T(4,128)(2,1)}, u32[]{:S(2)}) copy-start(bf16[4,2048]{1,0:T(4,128)(2,1)} %taps_ref.3) | copy-start | bytes 49156
  1.2 20.4 %collective-permute-start.4 = (bf16[64,1024]{1,0:T(8,128)(2,1)S(1)}, bf16[64,1024]{1,0:T(8,128)(2,1)S(1)}, u32[]{:S(2)}, u32[]{:S(2)}) collective-permute-start(bf16[64,1024]{1,0:T(8,128)(2,1)S(1)} %get-tuple-element.19), channel_id=1, source_target_pairs={{0,0},{1,5},{2,3},{3,12},{4,10},{5,15},{6,1},{7,6},{8,8},{9,13},{1... | collective-permute-start | bytes 393224 | tf_op jit(solution)/shard_map/ppermute | solution.py:211
  1.9 22.5 %collective-permute-start.5 = (bf16[64,1024]{1,0:T(8,128)(2,1)S(1)}, bf16[64,1024]{1,0:T(8,128)(2,1)S(1)}, u32[]{:S(2)}, u32[]{:S(2)}) collective-permute-start(bf16[64,1024]{1,0:T(8,128)(2,1)S(1)} %get-tuple-element.18), channel_id=1, source_target_pairs={{0,4},{1,2},{2,7},{3,9},{4,14},{5,0},{6,5},{7,3},{8,12},{9,10},{10... | collective-permute-start | bytes 393224 | tf_op jit(solution)/shard_map/ppermute | solution.py:211
  8.7 15.7 %collective-permute-start.6 = (bf16[64,1024]{1,0:T(8,128)(2,1)S(1)}, bf16[64,1024]{1,0:T(8,128)(2,1)S(1)}, u32[]{:S(2)}, u32[]{:S(2)}) collective-permute-start(bf16[64,1024]{1,0:T(8,128)(2,1)S(1)} %get-tuple-element.17), channel_id=1, source_target_pairs={{0,1},{1,6},{2,8},{3,13},{4,11},{5,4},{6,2},{7,7},{8,9},{9,14},{10... | collective-permute-start | bytes 393224 | tf_op jit(solution)/shard_map/ppermute | solution.py:211
  11.5 15.9 %collective-permute-start.1 = (bf16[16,2048]{1,0:T(8,128)(2,1)S(1)}, bf16[16,2048]{1,0:T(8,128)(2,1)S(1)}, u32[]{:S(2)}, u32[]{:S(2)}) collective-permute-start(bf16[16,2048]{1,0:T(8,128)(2,1)S(1)} %slice.150), channel_id=1, source_target_pairs={{0,1},{1,2},{2,3},{3,4},{4,5},{5,6},{6,7},{7,8},{8,9},{9,10},{10,1... | collective-permute-start | bytes 196616 | tf_op jit(solution)/shard_map/ppermute | solution.py:223
  16.4 15.5 %collective-permute-start = (s32[1,128]{1,0:T(1,128)}, s32[1,128]{1,0:T(1,128)}, u32[]{:S(2)}, u32[]{:S(2)}) collective-permute-start(s32[1,128]{1,0:T(1,128)} %bitcast), channel_id=1, source_target_pairs={{0,4},{1,5},{2,6},{3,7},{4,0},{5,1},{6,2},{7,3},{8,12},{9,13},{10,... | collective-permute-start | bytes 1544 | tf_op jit(solution)/shard_map/ppermute | solution.py:114
  21.6 15.7 %collective-permute-start.13 = (bf16[64,2048]{1,0:T(8,128)(2,1)S(1)}, bf16[64,2048]{1,0:T(8,128)(2,1)S(1)}, u32[]{:S(2)}, u32[]{:S(2)}) collective-permute-start(bf16[64,2048]{1,0:T(8,128)(2,1)S(1)} %conv_late.1.late_ref), channel_id=1, source_target_pairs={{0,8},{1,9},{2,10},{3,11},{4,12},{5,13},{6,14},{7,15},{8,0},{9,1},... | collective-permute-start | bytes 786440 | tf_op jit(solution)/shard_map/ppermute | solution.py:114
  25.3 11.9 %collective-permute-start.7 = (bf16[3,64,1024]{2,1,0:T(8,128)(2,1)}, bf16[3,64,1024]{2,1,0:T(8,128)(2,1)S(1)}, u32[]{:S(2)}, u32[]{:S(2)}) collective-permute-start(bf16[3,64,1024]{2,1,0:T(8,128)(2,1)} %constant_dynamic-slice_fusion), channel_id=1, source_target_pairs={{0,16},{16,0},{1,17},{17,1},{2,18},{18,2},{3,19},{19,3},{4,20},{20... | collective-permute-start | bytes 1179656 | tf_op jit(solution)/shard_map/ppermute | solution.py:118
  27.8 18.2 %collective-permute-start.2 = (bf16[128,2048]{1,0:T(8,128)(2,1)S(1)}, bf16[128,2048]{1,0:T(8,128)(2,1)S(1)}, u32[]{:S(2)}, u32[]{:S(2)}) collective-permute-start(bf16[128,2048]{1,0:T(8,128)(2,1)S(1)} %get-tuple-element.7), channel_id=1, source_target_pairs={{0,2},{1,3},{2,0},{3,1},{4,6},{5,7},{6,4},{7,5},{8,10},{9,11},{10,... | collective-permute-start | bytes 1572872 | tf_op jit(solution)/shard_map/ppermute | solution.py:114
  27.9 17.5 %collective-permute-start.8 = (bf16[3,64,1024]{2,1,0:T(8,128)(2,1)}, bf16[3,64,1024]{2,1,0:T(8,128)(2,1)}, u32[]{:S(2)}, u32[]{:S(2)}) collective-permute-start(bf16[3,64,1024]{2,1,0:T(8,128)(2,1)} %constant_dynamic-slice_fusion), channel_id=1, source_target_pairs={{0,4},{1,5},{2,6},{3,7},{4,0},{5,1},{6,2},{7,3},{8,12},{9,13},{10,... | collective-permute-start | bytes 1179656 | tf_op jit(solution)/shard_map/ppermute | solution.py:114
  37.3 9.4 %collective-permute-start.14 = (bf16[64,2048]{1,0:T(8,128)(2,1)S(1)}, bf16[64,2048]{1,0:T(8,128)(2,1)S(1)}, u32[]{:S(2)}, u32[]{:S(2)}) collective-permute-start(bf16[64,2048]{1,0:T(8,128)(2,1)S(1)} %after.8.refs_1_), channel_id=1, source_target_pairs={{0,2},{1,3},{2,0},{3,1},{4,6},{5,7},{6,4},{7,5},{8,10},{9,11},{10,... | collective-permute-start | bytes 786440 | tf_op jit(solution)/shard_map/ppermute | solution.py:114
  38.2 14.3 %collective-permute-start.16 = (bf16[64,2048]{1,0:T(8,128)(2,1)S(1)}, bf16[64,2048]{1,0:T(8,128)(2,1)S(1)}, u32[]{:S(2)}, u32[]{:S(2)}) collective-permute-start(bf16[64,2048]{1,0:T(8,128)(2,1)S(1)} %after.10), channel_id=1, source_target_pairs={{0,8},{1,9},{2,10},{3,11},{4,12},{5,13},{6,14},{7,15},{8,0},{9,1},... | collective-permute-start | bytes 786440 | tf_op jit(solution)/shard_map/ppermute | solution.py:114
  45.4 11.0 %collective-permute-start.9 = (bf16[3,64,1024]{2,1,0:T(8,128)(2,1)}, bf16[3,64,1024]{2,1,0:T(8,128)(2,1)S(1)}, u32[]{:S(2)}, u32[]{:S(2)}) collective-permute-start(bf16[3,64,1024]{2,1,0:T(8,128)(2,1)} %collective-permute-done.8), channel_id=1, source_target_pairs={{0,16},{16,0},{1,17},{17,1},{2,18},{18,2},{3,19},{19,3},{4,20},{20... | collective-permute-start | bytes 1179656 | tf_op jit(solution)/shard_map/ppermute | solution.py:118
  46.0 14.0 %collective-permute-start.3 = (bf16[256,2048]{1,0:T(8,128)(2,1)S(1)}, bf16[256,2048]{1,0:T(8,128)(2,1)S(1)}, u32[]{:S(2)}, u32[]{:S(2)}) collective-permute-start(bf16[256,2048]{1,0:T(8,128)(2,1)S(1)} %pad_maximum_fusion.1), channel_id=1, source_target_pairs={{0,1},{1,0},{2,3},{3,2},{4,5},{5,4},{6,7},{7,6},{8,9},{9,8},{10,11... | collective-permute-start | bytes 3145736 | tf_op jit(solution)/shard_map/ppermute | solution.py:114
  46.8 13.2 %collective-permute-start.15 = (bf16[128,2048]{1,0:T(8,128)(2,1)S(1)}, bf16[128,2048]{1,0:T(8,128)(2,1)S(1)}, u32[]{:S(2)}, u32[]{:S(2)}) collective-permute-start(bf16[128,2048]{1,0:T(8,128)(2,1)S(1)} %pad_maximum_fusion.6), channel_id=1, source_target_pairs={{0,1},{1,0},{2,3},{3,2},{4,5},{5,4},{6,7},{7,6},{8,9},{9,8},{10,11... | collective-permute-start | bytes 1572872 | tf_op jit(solution)/shard_map/ppermute | solution.py:114
  59.9 7.2 %collective-permute-start.17 = (bf16[64,2048]{1,0:T(8,128)(2,1)S(1)}, bf16[64,2048]{1,0:T(8,128)(2,1)S(1)}, u32[]{:S(2)}, u32[]{:S(2)}) collective-permute-start(bf16[64,2048]{1,0:T(8,128)(2,1)S(1)} %after.11), channel_id=1, source_target_pairs={{0,2},{1,3},{2,0},{3,1},{4,6},{5,7},{6,4},{7,5},{8,10},{9,11},{10,... | collective-permute-start | bytes 786440 | tf_op jit(solution)/shard_map/ppermute | solution.py:114
  61.4 8.4 %collective-permute-start.10 = (s32[2,128]{1,0:T(2,128)S(1)}, s32[2,128]{1,0:T(2,128)S(1)}, u32[]{:S(2)}, u32[]{:S(2)}) collective-permute-start(s32[2,128]{1,0:T(2,128)S(1)} %after.7), channel_id=1, source_target_pairs={{0,8},{1,9},{2,10},{3,11},{4,12},{5,13},{6,14},{7,15},{8,0},{9,1},... | collective-permute-start | bytes 3080 | tf_op jit(solution)/shard_map/ppermute | solution.py:114
  67.7 8.5 %collective-permute-start.18 = (bf16[128,2048]{1,0:T(8,128)(2,1)S(1)}, bf16[128,2048]{1,0:T(8,128)(2,1)S(1)}, u32[]{:S(2)}, u32[]{:S(2)}) collective-permute-start(bf16[128,2048]{1,0:T(8,128)(2,1)S(1)} %pad_maximum_fusion.7), channel_id=1, source_target_pairs={{0,1},{1,0},{2,3},{3,2},{4,5},{5,4},{6,7},{7,6},{8,9},{9,8},{10,11... | collective-permute-start | bytes 1572872 | tf_op jit(solution)/shard_map/ppermute | solution.py:114
  67.7 10.8 %collective-permute-start.19 = (bf16[512,256]{1,0:T(8,128)(2,1)S(1)}, bf16[512,256]{1,0:T(8,128)(2,1)S(1)}, u32[]{:S(2)}, u32[]{:S(2)}) collective-permute-start(bf16[512,256]{1,0:T(8,128)(2,1)S(1)} %get-tuple-element.15), channel_id=1, source_target_pairs={{0,4},{1,5},{2,6},{3,7},{4,0},{5,1},{6,2},{7,3},{8,12},{9,13},{10,... | collective-permute-start | bytes 786440 | tf_op jit(solution)/shard_map/ppermute | solution.py:114
  67.8 11.5 %collective-permute-start.20 = (bf16[256,256]{1,0:T(8,128)(2,1)S(1)}, bf16[256,256]{1,0:T(8,128)(2,1)S(1)}, u32[]{:S(2)}, u32[]{:S(2)}) collective-permute-start(bf16[256,256]{1,0:T(8,128)(2,1)S(1)} %get-tuple-element.22), channel_id=1, source_target_pairs={{0,4},{1,5},{2,6},{3,7},{4,0},{5,1},{6,2},{7,3},{8,12},{9,13},{10,... | collective-permute-start | bytes 393224 | tf_op jit(solution)/shard_map/ppermute | solution.py:114
  69.8 1.2 %collective-permute-start.11 = (s32[4,128]{1,0:T(4,128)S(1)}, s32[4,128]{1,0:T(4,128)S(1)}, u32[]{:S(2)}, u32[]{:S(2)}) collective-permute-start(s32[4,128]{1,0:T(4,128)S(1)} %pad_add_fusion.2), channel_id=1, source_target_pairs={{0,1},{1,0},{2,3},{3,2},{4,5},{5,4},{6,7},{7,6},{8,9},{9,8},{10,11... | collective-permute-start | bytes 6152 | tf_op jit(solution)/shard_map/ppermute | solution.py:114
  71.0 3.7 %collective-permute-start.12 = (s32[8,128]{1,0:T(8,128)S(1)}, s32[8,128]{1,0:T(8,128)S(1)}, u32[]{:S(2)}, u32[]{:S(2)}) collective-permute-start(s32[8,128]{1,0:T(8,128)S(1)} %pad_add_fusion.1), channel_id=1, source_target_pairs={{0,2},{1,3},{2,0},{3,1},{4,6},{5,7},{6,4},{7,5},{8,10},{9,11},{10,... | collective-permute-start | bytes 12296 | tf_op jit(solution)/shard_map/ppermute | solution.py:114
  78.4 5.0 %collective-permute-start.21 = (bf16[256,256]{1,0:T(8,128)(2,1)S(1)}, bf16[256,256]{1,0:T(8,128)(2,1)S(1)}, u32[]{:S(2)}, u32[]{:S(2)}) collective-permute-start(bf16[256,256]{1,0:T(8,128)(2,1)S(1)} %get-tuple-element.20), channel_id=1, source_target_pairs={{0,4},{1,5},{2,6},{3,7},{4,0},{5,1},{6,2},{7,3},{8,12},{9,13},{10,... | collective-permute-start | bytes 393224 | tf_op jit(solution)/shard_map/ppermute | solution.py:114
  (15 other events, 87.6 us)

commit v8 on v7

--- a/solution.py
+++ b/solution.py
@@ -106,7 +106,6 @@
 CORE, Y, NEAR, FAR = 1, 2, 4, 8
 QUADS = (0, Y, CORE, Y | CORE)
 RIM = 16
-VMEM_LIMIT = 6 * 2**20
 
 
 def swap_seq(value, bit):
@@ -118,24 +117,22 @@
     return lax.ppermute(value, "grp", [(0, 1), (1, 0)])
 
 
-def call(kernel, out_shape, operands, name, scalars=None, scratch=(), flops=0, anywhere=0):
-    in_specs = [pl.BlockSpec(memory_space=pltpu.VMEM)] * (len(operands) - anywhere)
-    in_specs += [pl.BlockSpec(memory_space=pl.ANY)] * anywhere
-    if scalars is not None:
-        operands = [scalars] + list(operands)
-        in_specs = [pl.BlockSpec(memory_space=pltpu.SMEM)] + in_specs
+def call(kernel, out_shape, operands, name, smem=0, flops=0, limit=6):
+    whole = pl.BlockSpec(memory_space=pltpu.VMEM)
+    scalars = pl.BlockSpec(memory_space=pltpu.SMEM)
     many = isinstance(out_shape, (list, tuple))
     shapes = list(out_shape) if many else [out_shape]
-    size = sum(2 * o.size for o in list(operands) + shapes)
-    whole = pl.BlockSpec(memory_space=pltpu.VMEM)
     return pl.pallas_call(
         kernel,
         out_shape=out_shape,
-        in_specs=in_specs,
+        in_specs=[scalars] * smem + [whole] * (len(operands) - smem),
         out_specs=[whole] * len(shapes) if many else whole,
-        scratch_shapes=list(scratch),
-        cost_estimate=pl.CostEstimate(flops=flops, bytes_accessed=size, transcendentals=0),
-        compiler_params=pltpu.CompilerParams(vmem_limit_bytes=VMEM_LIMIT),
+        cost_estimate=pl.CostEstimate(
+            flops=flops,
+            bytes_accessed=sum(2 * o.size for o in list(operands) + shapes),
+            transcendentals=0,
+        ),
+        compiler_params=pltpu.CompilerParams(vmem_limit_bytes=limit * 2**20),
         name=name,
     )(*operands)
 
@@ -172,23 +169,47 @@
     return total.astype(jnp.bfloat16)
 
 
-def conv_late_kernel(frames_ref, taps_ref, late_ref):
-    part = late_ref.shape[0]
-    late_ref[...] = convolved(frames_ref[part - RIM : part], frames_ref[part:], taps_ref[...])
-
-
-def conv_early_kernel(rim_ref, frames_ref, taps_ref, late_ref, early_ref, own_ref):
-    part = late_ref.shape[0]
-    early = convolved(rim_ref[...], frames_ref[:part], taps_ref[...])
-    early_ref[...] = early
-    own_ref[:part] = early
-    own_ref[part:] = late_ref[...]
-
-
-def by_bit(bit, mine, theirs, axis):
-    return jnp.stack(
-        [jnp.where(bit == 0, mine, theirs), jnp.where(bit == 0, theirs, mine)], axis=axis
-    )
+ME, SIDE, GRP, TURN, TURN_PAIRED = range(5)
+
+
+def first_kernel(scalars, owner, ids, frames, weight, taps, late, rim, block0, block1, block2, code):
+    tok_rows = frames.shape[0]
+    part = late.shape[0]
+    half = block0.shape[1]
+    tracks = owner.shape[0]
+    span = 16 * tok_rows
+    late[...] = convolved(frames[part - RIM : part], frames[part:], taps[...])
+    rim[...] = frames[tok_rows - RIM :]
+    lanes = pl.ds(pl.multiple_of(scalars[GRP] * half, half), half)
+    for j, block in enumerate((block0, block1, block2)):
+        block[...] = weight[j * (HD // 2) : (j + 1) * (HD // 2), lanes]
+    group = jnp.zeros(ids.shape, jnp.int32)
+    for track in range(tracks):
+        group = jnp.where(ids[...] == track, owner[track], group)
+    time = scalars[ME] * tok_rows + lax.broadcasted_iota(jnp.int32, ids.shape, 1)
+    code[...] = group * span + time
+
+
+def early_kernel(rim, frames, taps, late, early, own):
+    part = late.shape[0]
+    rows = convolved(rim[...], frames[:part], taps[...])
+    early[...] = rows
+    own[:part] = rows
+    own[part:] = late[...]
+
+
+def assemble_kernel(scalars, *refs):
+    pieces, weight = refs[:4], refs[4]
+    side, grp = scalars[SIDE], scalars[GRP]
+    half = pieces[0].shape[2]
+    for n, piece in enumerate(pieces):
+        column = side if n < 2 else 1 - side
+        feature = grp if n % 2 == 0 else 1 - grp
+        turn = scalars[TURN if n < 2 else TURN_PAIRED]
+        for j in range(3):
+            start = lax.rem(j + 3 - turn, 3) * HD + column * (HD // 2)
+            rows = pl.ds(pl.multiple_of(start, HD // 2), HD // 2)
+            weight[rows, pl.ds(pl.multiple_of(feature * half, half), half)] = piece[j]
 
 
 def body_by_head(frames, conv_weight, qkv_weight, track_ids, track_owner):
@@ -200,44 +221,61 @@
     head = far * 4 + quad
     part = tok_rows // 2
 
+    half = features // 2
+    turn = lax.rem(2 * head + near, 3)
+    turn_paired = lax.rem(2 * head + 1 - near, 3)
+    scalars = jnp.stack([me, near, grp, turn, turn_paired]).astype(jnp.int32)
+
+    late, rim_rows, *blocks, code = call(
+        first_kernel,
+        [bf16(part, features), bf16(RIM, features)]
+        + [bf16(HD // 2, half)] * 3
+        + [jax.ShapeDtypeStruct((1, tok_rows), jnp.int32)],
+        [scalars, track_owner, track_ids[None, :], frames, qkv_weight.T, conv_weight],
+        "first",
+        smem=2,
+        limit=10,
+    )
+
     def home(block):
         of_head, side = block % devices // 2, block % 2
         return of_head // 4 * FAR + side * NEAR + of_head % 4
 
-    half = features // 2
-    held = lax.dynamic_slice_in_dim(qkv_weight.T, grp * half, half, 1)
-    held = held.reshape(3, HD // 2, half)
-    moved = [
-        lax.ppermute(held[j], FOUR, [(d, home(3 * d + j)) for d in range(devices)])
-        for j in range(3)
-    ]
-    turn = lax.rem(2 * head + near, 3)
-    mine = lax.dynamic_slice_in_dim(jnp.stack(moved + moved[:2]), turn, 3, 0)
+    mine = jnp.stack(
+        [
+            lax.ppermute(block, FOUR, [(d, home(3 * d + j)) for d in range(devices)])
+            for j, block in enumerate(blocks)
+        ]
+    )
     mine_too = swap_grp(mine)
     paired = swap_seq(mine, NEAR)
     paired_too = swap_grp(paired)
-    head_weight = by_bit(
-        near, by_bit(grp, mine, mine_too, 2), by_bit(grp, paired, paired_too, 2), 1
-    ).reshape(3 * HD, features)
-
-    rim_rows = lax.ppermute(
-        frames[tok_rows - RIM :], FOUR, [(i, i + 1) for i in range(devices - 1)]
-    )
-    late = call(conv_late_kernel, bf16(part, features), [frames, conv_weight], "conv_late")
+    head_weight = call(
+        assemble_kernel,
+        bf16(3 * HD, features),
+        [scalars, mine, mine_too, paired, paired_too],
+        "assemble",
+        smem=1,
+    )
+
+    rim_rows = lax.ppermute(rim_rows, FOUR, [(i, i + 1) for i in range(devices - 1)])
     early, own = call(
-        conv_early_kernel,
+        early_kernel,
         [bf16(part, features), bf16(tok_rows, features)],
         [rim_rows, frames, conv_weight, late],
-        "conv_early",
+        "early",
     )
     beside = swap_seq(own, Y)
     far_late = after(swap_seq(late, FAR), mine_too)
     far_late_beside = swap_seq(far_late, Y)
     far_early = swap_seq(after(early, far_late), FAR)
-    far_early_beside = swap_seq(after(far_early, paired_too), Y)
-
-    groups = track_groups(track_ids, track_owner)[None, :]
-    groups = jnp.concatenate([groups, swap_seq(groups, NEAR)], axis=0)
+
+    seen = [0]
+    codes = after(code, far_late)
+    for bit in (Y, CORE, NEAR, FAR):
+        seen += [hop ^ bit for hop in seen]
+        codes = jnp.concatenate([codes, swap_seq(codes, bit)], axis=0)
+    far_early_beside = swap_seq(after(far_early, paired_too, codes), Y)
 
     parts = []
 
@@ -254,40 +292,28 @@
         return done
 
     done = project([own, beside])
-    groups = after(groups, done)
-    for bit in (FAR, CORE, Y):
-        groups = jnp.concatenate([groups, swap_seq(groups, bit)], axis=0)
     project([far_late, far_late_beside], done)
-    project([far_early, after(far_early_beside, done)], groups)
+    project([far_early, after(far_early_beside, done)])
     query = jnp.concatenate([p[0] for p in parts], axis=0)
     keyed = jnp.concatenate([p[1] for p in parts] + [p[2] for p in parts], axis=0)
-
-    row_of = {}
-    for bit in (0, NEAR, FAR, CORE, Y):
-        row_of.update({seen ^ bit: len(row_of) + n for n, seen in enumerate(list(row_of) or [0])})
 
     order = [(hop, 0, tok_rows) for hop in QUADS]
     order += [(hop | FAR, part, part) for hop in QUADS]
     order += [(hop | FAR, 0, part) for hop in QUADS]
 
-    def of_rows(bit):
-        times = [
-            (me ^ hop ^ bit) * tok_rows + start + jnp.arange(count, dtype=jnp.int32)
-            for hop, start, count in order
-        ]
-        marks = [groups[row_of[hop ^ bit], start : start + count] for hop, start, count in order]
-        return jnp.concatenate(times), jnp.concatenate(marks)
-
-    own_times, own_groups = of_rows(0)
-    other_times, other_groups = of_rows(NEAR)
-    key_times = jnp.concatenate([own_times, other_times])
-    key_groups = jnp.concatenate([own_groups, other_groups])
+    def codes_at(bit):
+        return jnp.concatenate(
+            [codes[seen.index(hop ^ bit), start : start + count] for hop, start, count in order]
+        )
+
+    asking = codes_at(0)
+    keys = jnp.concatenate([asking, codes_at(NEAR)])
+    span = devices * tok_rows
+    least = asking // span * span
     scores = lax.dot_general(
         query, keyed[:, :HD], (((1,), (1,)), ((), ())), preferred_element_type=jnp.float32
     ) * (1.0 / HD**0.5)
-    allowed = (key_times[None, :] <= own_times[:, None]) & (
-        key_groups[None, :] == own_groups[:, None]
-    )
+    allowed = (keys[None, :] <= asking[:, None]) & (keys[None, :] >= least[:, None])
     scores = jnp.where(allowed, scores, jnp.float32(-1e30))
     expd = jnp.exp(scores - jnp.max(scores, axis=-1, keepdims=True))
     weights = (expd / jnp.sum(expd, axis=-1, keepdims=True)).astype(jnp.bfloat16)

time: 102 us -> 103 us (level)
  local copies, waits for them, and re-layouts: 12.8 us -> 5.95 us
  starting transfers between devices: 23.8 us -> 30.4 us
  other arithmetic: 10.6 us -> 5.43 us
  blocking collectives: 11.9 us -> 13.9 us
  waiting for transfers between devices: 34.7 us -> 36.2 us
  matrix products: 6.62 us -> 7.97 us
  Pallas kernels: 0.72 us -> 1.98 us
    ppermute x16, starting transfers between devices: 8.76 us -> 17.6 us  [swap_seq(): return lax.ppermute(value, FOUR, [(d, d ^ bit) for d in range(count)])]
    ppermute x4, waiting for transfers between devices: 0.01 us -> 6.73 us  [the longest x3 6.72 us: body_by_head(): lax.ppermute(block, FOUR, [(d, home(3 * d + j)) for d in range(devices)])]
    add x12 -> x0, other arithmetic: 4.65 us -> none  [of_rows(): (me ^ hop ^ bit) * tok_rows + start + jnp.arange(count, dtype=jnp.int32)]
    ppermute x2, waiting for transfers between devices: 3.99 us -> 0.01 us  [swap_grp(): return lax.ppermute(value, 'grp', [(0, 1), (1, 0)])]
    concatenate x4 -> x3, local copies, waits for them, and re-layouts: 3.59 us -> 0.19 us  [the longest x1 0.09 us: body_by_head(): keys = jnp.concatenate([asking, codes_at(NEAR)])]
    concatenate x3, other arithmetic: 0.15 us -> 2.96 us  [project(): rows = jnp.concatenate(rows, axis=0)]
    ppermute x4, starting transfers between devices: 13.1 us -> 10.7 us  [the longest x3 9.43 us: body_by_head(): lax.ppermute(block, FOUR, [(d, home(3 * d + j)) for d in range(devices)])]
    another operation x3 -> x1, other arithmetic: 2.25 us -> 0.05 us  [body_by_head(): jnp.stack([lax.ppermute(block, FOUR, [(d, home(3 * d + j)) for d in range...]
  transfers between devices with their start and end apart: 22 -> 22, of which waited for: 10 -> 12; matrix products, arithmetic and copies ran while one was open for 20% -> 8% of each run, Pallas kernels for 1% -> 1%
where the time goes in v8:
time: 103 us; the launch traced here: 102 us
  waiting for transfers between devices  36.2 us (35%)
  starting transfers between devices  30.4 us (30%)
  blocking collectives  13.9 us (13%)
  matrix products  7.97 us (8%)
  local copies, waits for them, and re-layouts  5.95 us (6%)
  other arithmetic  5.43 us (5%)
  Pallas kernels  1.98 us (2%)
    ppermute x16, waiting for transfers between devices, swap_seq(): return lax.ppermute(value, FOUR, [(d, d ^ bit) for d in range(count)])  29.4 us
    ppermute x16, starting transfers between devices, swap_seq(): return lax.ppermute(value, FOUR, [(d, d ^ bit) for d in range(count)])  17.6 us
    all_to_all x1, blocking collectives, body_by_head(): lax.all_to_all(sent, ('far', 'quad'), split_axis=0, concat_axis=0, tiled=...  13.9 us
    ppermute x3, starting transfers between devices, body_by_head(): lax.ppermute(block, FOUR, [(d, home(3 * d + j)) for d in range(devices)])  9.43 us
    ppermute x3, waiting for transfers between devices, body_by_head(): lax.ppermute(block, FOUR, [(d, home(3 * d + j)) for d in range(devices)])  6.72 us
    unnamed x19, local copies, waits for them, and re-layouts  4.26 us
    dot_general x3, matrix products, project(): lax.dot_general(after(rows, *others) if others else rows, head_weight, ((...  4.09 us
    concatenate x3, other arithmetic, project(): rows = jnp.concatenate(rows, axis=0)  2.96 us
  transfers between devices with their start and end apart: 22, of which 12 were waited for; matrix products, arithmetic and copies ran while one was open for 8% of the time, Pallas kernels for 1%

profile of v8, /device:TPU:0, one launch (start us, length us, event | category | flops | bytes accessed | tf_op | source)
XLA Modules:
  0.0 102.2 jit_solution(3429171981353080367)
XLA Ops:
  5.9 6.9 %collective-permute-start.2 = (bf16[64,1024]{1,0:T(8,128)(2,1)S(1)}, bf16[64,1024]{1,0:T(8,128)(2,1)S(1)}, u32[]{:S(2)}, u32[]{:S(2)}) collective-permute-start(bf16[64,1024]{1,0:T(8,128)(2,1)S(1)} %get-tuple-element.16), channel_id=1, source_target_pairs={{0,4},{1,2},{2,7},{3,9},{4,14},{5,0},{6,5},{7,3},{8,12},{9,10},{10... | collective-permute-start | bytes 393224 | tf_op jit(solution)/shard_map/ppermute | solution.py:246
  12.8 1.9 %collective-permute-start.3 = (bf16[64,1024]{1,0:T(8,128)(2,1)S(1)}, bf16[64,1024]{1,0:T(8,128)(2,1)S(1)}, u32[]{:S(2)}, u32[]{:S(2)}) collective-permute-start(bf16[64,1024]{1,0:T(8,128)(2,1)S(1)} %get-tuple-element.17), channel_id=1, source_target_pairs={{0,1},{1,6},{2,8},{3,13},{4,11},{5,4},{6,2},{7,7},{8,9},{9,14},{10... | collective-permute-start | bytes 393224 | tf_op jit(solution)/shard_map/ppermute | solution.py:246
  14.7 1.6 %collective-permute-done.2 = bf16[64,1024]{1,0:T(8,128)(2,1)S(1)} collective-permute-done((bf16[64,1024]{1,0:T(8,128)(2,1)S(1)}, bf16[64,1024]{1,0:T(8,128)(2,1)S(1)}, u32[]{:S(2)}, u32[]{:S(2)}) %collective-permute-start.2) | collective-permute-done | bytes 131104 | tf_op jit(solution)/shard_map/ppermute | solution.py:246
  16.3 5.1 %collective-permute-done.3 = bf16[64,1024]{1,0:T(8,128)(2,1)S(1)} collective-permute-done((bf16[64,1024]{1,0:T(8,128)(2,1)S(1)}, bf16[64,1024]{1,0:T(8,128)(2,1)S(1)}, u32[]{:S(2)}, u32[]{:S(2)}) %collective-permute-start.3) | collective-permute-done | bytes 131104 | tf_op jit(solution)/shard_map/ppermute | solution.py:246
  21.5 1.6 %collective-permute-start.4 = (bf16[3,64,1024]{2,1,0:T(8,128)(2,1)S(1)}, bf16[3,64,1024]{2,1,0:T(8,128)(2,1)S(1)}, u32[]{:S(2)}, u32[]{:S(2)}) collective-permute-start(bf16[3,64,1024]{2,1,0:T(8,128)(2,1)S(1)} %pad_maximum_fusion.4.refs_0_), channel_id=1, source_target_pairs={{0,16},{16,0},{1,17},{17,1},{2,18},{18,2},{3,19},{19,3},{4,20},{20... | collective-permute-start | bytes 1179656 | tf_op jit(solution)/shard_map/ppermute | solution.py:117
  23.0 1.4 %collective-permute-start = (bf16[64,2048]{1,0:T(8,128)(2,1)S(1)}, bf16[64,2048]{1,0:T(8,128)(2,1)S(1)}, u32[]{:S(2)}, u32[]{:S(2)}) collective-permute-start(bf16[64,2048]{1,0:T(8,128)(2,1)S(1)} %get-tuple-element.14.late), channel_id=1, source_target_pairs={{0,8},{1,9},{2,10},{3,11},{4,12},{5,13},{6,14},{7,15},{8,0},{9,1},... | collective-permute-start | bytes 786440 | tf_op jit(solution)/shard_map/ppermute | solution.py:113
  24.5 1.3 %collective-permute-start.9 = (bf16[16,2048]{1,0:T(8,128)(2,1)S(1)}, bf16[16,2048]{1,0:T(8,128)(2,1)S(1)}, u32[]{:S(2)}, u32[]{:S(2)}) collective-permute-start(bf16[16,2048]{1,0:T(8,128)(2,1)S(1)} %get-tuple-element.18), channel_id=1, source_target_pairs={{0,1},{1,2},{2,3},{3,4},{4,5},{5,6},{6,7},{7,8},{8,9},{9,10},{10,1... | collective-permute-start | bytes 196616 | tf_op jit(solution)/shard_map/ppermute | solution.py:261
  25.8 9.7 %collective-permute-done.refs_0_ = bf16[64,2048]{1,0:T(8,128)(2,1)S(1)} collective-permute-done((bf16[64,2048]{1,0:T(8,128)(2,1)S(1)}, bf16[64,2048]{1,0:T(8,128)(2,1)S(1)}, u32[]{:S(2)}, u32[]{:S(2)}) %collective-permute-start) | collective-permute-done | bytes 262176 | tf_op jit(solution)/shard_map/ppermute | solution.py:113
  35.5 3.9 %collective-permute-start.5 = (s32[1,128]{1,0:T(1,128)S(1)}, s32[1,128]{1,0:T(1,128)S(1)}, u32[]{:S(2)}, u32[]{:S(2)}) collective-permute-start(s32[1,128]{1,0:T(1,128)S(1)} %after.7), channel_id=1, source_target_pairs={{0,2},{1,3},{2,0},{3,1},{4,6},{5,7},{6,4},{7,5},{8,10},{9,11},{10,... | collective-permute-start | bytes 1544 | tf_op jit(solution)/shard_map/ppermute | solution.py:113
  40.9 2.1 %collective-permute-start.14 = (bf16[64,2048]{1,0:T(8,128)(2,1)S(1)}, bf16[64,2048]{1,0:T(8,128)(2,1)S(1)}, u32[]{:S(2)}, u32[]{:S(2)}) collective-permute-start(bf16[64,2048]{1,0:T(8,128)(2,1)S(1)} %after.6.refs_1_), channel_id=1, source_target_pairs={{0,2},{1,3},{2,0},{3,1},{4,6},{5,7},{6,4},{7,5},{8,10},{9,11},{10,... | collective-permute-start | bytes 786440 | tf_op jit(solution)/shard_map/ppermute | solution.py:113
  43.0 3.4 %collective-permute-start.16 = (bf16[64,2048]{1,0:T(8,128)(2,1)S(1)}, bf16[64,2048]{1,0:T(8,128)(2,1)S(1)}, u32[]{:S(2)}, u32[]{:S(2)}) collective-permute-start(bf16[64,2048]{1,0:T(8,128)(2,1)S(1)} %after.9), channel_id=1, source_target_pairs={{0,8},{1,9},{2,10},{3,11},{4,12},{5,13},{6,14},{7,15},{8,0},{9,1},... | collective-permute-start | bytes 786440 | tf_op jit(solution)/shard_map/ppermute | solution.py:113
  47.1 5.3 %collective-permute-done.7 = s32[4,128]{1,0:T(4,128)S(1)} collective-permute-done((s32[4,128]{1,0:T(4,128)S(1)}, s32[4,128]{1,0:T(4,128)S(1)}, u32[]{:S(2)}, u32[]{:S(2)}) %collective-permute-start.7) | collective-permute-done | bytes 2080 | tf_op jit(solution)/shard_map/ppermute | solution.py:113
  54.6 2.1 %pad_maximum_fusion = bf16[256,2048]{1,0:T(8,128)(2,1)} fusion(bf16[128,2048]{1,0:T(8,128)(2,1)} %collective-permute-done.10, bf16[128,2048]{1,0:T(8,128)(2,1)S(1)} %get-tuple-element.19), kind=kLoop, calls=%fused_computation.15 | loop fusion | flops 2097152 | bytes 2097152 | tf_op jit(solution)/shard_map/concatenate | solution.py:283
  62.0 2.6 %fusion.8.refs_1_ = bf16[512,384]{1,0:T(8,128)(2,1)S(1)} fusion(bf16[384,2048]{1,0:T(8,128)(2,1)S(1)} %assemble.1, bf16[256,2048]{1,0:T(8,128)(2,1)} %collective-permute-done.11, bf16[128,2048]{1,0:T(8,128)(2,1)} %collective-permute-done.10, bf16[128,2048]{1,0:T(8,128)(2,1)S(1)} %get-tuple-element.19), kind=kOutput, calls=%fused_computation.11 | convolution fusion | flops 811794432 | bytes 4063232 | tf_op jit(solution)/shard_map/dot_general | solution.py:285
  64.7 2.6 %collective-permute-done.17.refs_0_ = bf16[64,2048]{1,0:T(8,128)(2,1)S(1)} collective-permute-done((bf16[64,2048]{1,0:T(8,128)(2,1)S(1)}, bf16[64,2048]{1,0:T(8,128)(2,1)S(1)}, u32[]{:S(2)}, u32[]{:S(2)}) %collective-permute-start.17) | collective-permute-done | bytes 262176 | tf_op jit(solution)/shard_map/ppermute | solution.py:113
  67.4 1.9 %collective-permute-start.19 = (bf16[512,256]{1,0:T(8,128)(2,1)S(1)}, bf16[512,256]{1,0:T(8,128)(2,1)S(1)}, u32[]{:S(2)}, u32[]{:S(2)}) collective-permute-start(bf16[512,256]{1,0:T(8,128)(2,1)S(1)} %get-tuple-element.21), channel_id=1, source_target_pairs={{0,4},{1,5},{2,6},{3,7},{4,0},{5,1},{6,2},{7,3},{8,12},{9,13},{10,... | collective-permute-start | bytes 786440 | tf_op jit(solution)/shard_map/ppermute | solution.py:113
  71.1 1.9 %collective-permute-start.21 = (bf16[256,256]{1,0:T(8,128)(2,1)S(1)}, bf16[256,256]{1,0:T(8,128)(2,1)S(1)}, u32[]{:S(2)}, u32[]{:S(2)}) collective-permute-start(bf16[256,256]{1,0:T(8,128)(2,1)S(1)} %get-tuple-element.23), channel_id=1, source_target_pairs={{0,4},{1,5},{2,6},{3,7},{4,0},{5,1},{6,2},{7,3},{8,12},{9,13},{10,... | collective-permute-start | bytes 393224 | tf_op jit(solution)/shard_map/ppermute | solution.py:113
  73.0 3.5 %collective-permute-done.19 = bf16[512,256]{1,0:T(8,128)(2,1)S(1)} collective-permute-done((bf16[512,256]{1,0:T(8,128)(2,1)S(1)}, bf16[512,256]{1,0:T(8,128)(2,1)S(1)}, u32[]{:S(2)}, u32[]{:S(2)}) %collective-permute-start.19) | collective-permute-done | bytes 262176 | tf_op jit(solution)/shard_map/ppermute | solution.py:113
  76.6 2.8 %collective-permute-done.20 = bf16[256,256]{1,0:T(8,128)(2,1)S(1)} collective-permute-done((bf16[256,256]{1,0:T(8,128)(2,1)S(1)}, bf16[256,256]{1,0:T(8,128)(2,1)S(1)}, u32[]{:S(2)}, u32[]{:S(2)}) %collective-permute-start.20) | collective-permute-done | bytes 131104 | tf_op jit(solution)/shard_map/ppermute | solution.py:113
  79.4 2.5 %collective-permute-done.21 = bf16[256,256]{1,0:T(8,128)(2,1)S(1)} collective-permute-done((bf16[256,256]{1,0:T(8,128)(2,1)S(1)}, bf16[256,256]{1,0:T(8,128)(2,1)S(1)}, u32[]{:S(2)}, u32[]{:S(2)}) %collective-permute-start.21) | collective-permute-done | bytes 131104 | tf_op jit(solution)/shard_map/ppermute | solution.py:113
  81.9 2.3 %fusion.45 = (f32[1024]{0:T(1024)S(1)}, f32[1024,2048]{1,0:T(8,128)S(1)}) fusion(bf16[2048,256]{1,0:T(8,128)(2,1)S(1)} %constant_dynamic-update-slice_fusion, bf16[256,128]{1,0:T(8,128)(2,1)S(1)} %slice.173, bf16[256,128]{1,0:T(8,128)(2,1)S(1)} %slice.172, bf16[512,128]{1,0:T(8,128)(2,1)S(1)} %slice-done, s32[1024]{0:T(1024)S(1)} %fusion.37, ...), kind=kOutput, calls=%fused_computation.101 | convolution fusion | flops 550239232 | bytes 9195520 | tf_op jit(solution)/shard_map/dot_general | solution.py:313
  84.2 1.3 %fusion = f32[1024]{0:T(1024)S(1)} fusion(f32[1024,2048]{1,0:T(8,128)S(1)} %get-tuple-element.50, f32[1024]{0:T(1024)S(1)} %get-tuple-element.49), kind=kLoop, calls=%fused_computation.3 | loop fusion | flops 4193280 | bytes 8396800 | tf_op jit(solution)/shard_map/reduce_sum | solution.py:319
  85.4 1.6 %fusion.11 = bf16[1024,128]{1,0:T(8,128)(2,1)S(1)} fusion(f32[1024,2048]{1,0:T(8,128)S(1)} %get-tuple-element.50, f32[1024]{0:T(1024)S(1)} %fusion, f32[1024]{0:T(1024)S(1)} %get-tuple-element.49, bf16[2048,256]{1,0:T(8,128)(2,1)S(1)} %constant_dynamic-update-slice_fusion), kind=kOutput, calls=%fused_computation.12 | convolution fusion | flops 543293440 | bytes 9183232 | tf_op jit(solution)/shard_map/dot_general | solution.py:320
  87.3 13.9 %all_to_all.5 = bf16[8,128,128]{2,1,0:T(8,128)(2,1)S(1)} all-to-all(bf16[8,128,128]{2,1,0:T(8,128)(2,1)S(1)} %fusion.28), channel_id=1, replica_groups=mesh['grp'=2,'far'=2,'near'=2,'quad'=4] {'far','quad'}, dimensions={0} | all-to-all | bytes 524288 | tf_op jit(solution)/shard_map/all_to_all | solution.py:330
  (94 shorter events, 18.8 us)
Async XLA Ops:
  0.0 39.3 %copy-start.5 = (bf16[4,2048]{1,0:T(4,128)(2,1)S(1)}, bf16[4,2048]{1,0:T(4,128)(2,1)}, u32[]{:S(2)}) copy-start(bf16[4,2048]{1,0:T(4,128)(2,1)} %taps.3) | copy-start | bytes 49156
  4.3 35.0 %copy-start.2 = (bf16[128,2048]{1,0:T(8,128)(2,1)S(1)}, bf16[128,2048]{1,0:T(8,128)(2,1)}, u32[]{:S(2)}) copy-start(bf16[128,2048]{1,0:T(8,128)(2,1)} %frames.3) | copy-start | bytes 1572868
  5.2 9.4 %collective-permute-start.1 = (bf16[64,1024]{1,0:T(8,128)(2,1)S(1)}, bf16[64,1024]{1,0:T(8,128)(2,1)S(1)}, u32[]{:S(2)}, u32[]{:S(2)}) collective-permute-start(bf16[64,1024]{1,0:T(8,128)(2,1)S(1)} %get-tuple-element.15), channel_id=1, source_target_pairs={{0,0},{1,5},{2,3},{3,12},{4,10},{5,15},{6,1},{7,6},{8,8},{9,13},{1... | collective-permute-start | bytes 393224 | tf_op jit(solution)/shard_map/ppermute | solution.py:246
  5.9 10.4 %collective-permute-start.2 = (bf16[64,1024]{1,0:T(8,128)(2,1)S(1)}, bf16[64,1024]{1,0:T(8,128)(2,1)S(1)}, u32[]{:S(2)}, u32[]{:S(2)}) collective-permute-start(bf16[64,1024]{1,0:T(8,128)(2,1)S(1)} %get-tuple-element.16), channel_id=1, source_target_pairs={{0,4},{1,2},{2,7},{3,9},{4,14},{5,0},{6,5},{7,3},{8,12},{9,10},{10... | collective-permute-start | bytes 393224 | tf_op jit(solution)/shard_map/ppermute | solution.py:246
  12.8 8.6 %collective-permute-start.3 = (bf16[64,1024]{1,0:T(8,128)(2,1)S(1)}, bf16[64,1024]{1,0:T(8,128)(2,1)S(1)}, u32[]{:S(2)}, u32[]{:S(2)}) collective-permute-start(bf16[64,1024]{1,0:T(8,128)(2,1)S(1)} %get-tuple-element.17), channel_id=1, source_target_pairs={{0,1},{1,6},{2,8},{3,13},{4,11},{5,4},{6,2},{7,7},{8,9},{9,14},{10... | collective-permute-start | bytes 393224 | tf_op jit(solution)/shard_map/ppermute | solution.py:246
  21.5 14.0 %collective-permute-start.4 = (bf16[3,64,1024]{2,1,0:T(8,128)(2,1)S(1)}, bf16[3,64,1024]{2,1,0:T(8,128)(2,1)S(1)}, u32[]{:S(2)}, u32[]{:S(2)}) collective-permute-start(bf16[3,64,1024]{2,1,0:T(8,128)(2,1)S(1)} %pad_maximum_fusion.4.refs_0_), channel_id=1, source_target_pairs={{0,16},{16,0},{1,17},{17,1},{2,18},{18,2},{3,19},{19,3},{4,20},{20... | collective-permute-start | bytes 1179656 | tf_op jit(solution)/shard_map/ppermute | solution.py:117
  23.0 23.4 %collective-permute-start.12 = (bf16[3,64,1024]{2,1,0:T(8,128)(2,1)S(1)}, bf16[3,64,1024]{2,1,0:T(8,128)(2,1)S(1)}, u32[]{:S(2)}, u32[]{:S(2)}) collective-permute-start(bf16[3,64,1024]{2,1,0:T(8,128)(2,1)S(1)} %pad_maximum_fusion.4.refs_0_), channel_id=1, source_target_pairs={{0,4},{1,5},{2,6},{3,7},{4,0},{5,1},{6,2},{7,3},{8,12},{9,13},{10,... | collective-permute-start | bytes 1179656 | tf_op jit(solution)/shard_map/ppermute | solution.py:113
  23.0 12.4 %collective-permute-start = (bf16[64,2048]{1,0:T(8,128)(2,1)S(1)}, bf16[64,2048]{1,0:T(8,128)(2,1)S(1)}, u32[]{:S(2)}, u32[]{:S(2)}) collective-permute-start(bf16[64,2048]{1,0:T(8,128)(2,1)S(1)} %get-tuple-element.14.late), channel_id=1, source_target_pairs={{0,8},{1,9},{2,10},{3,11},{4,12},{5,13},{6,14},{7,15},{8,0},{9,1},... | collective-permute-start | bytes 786440 | tf_op jit(solution)/shard_map/ppermute | solution.py:113
  24.5 14.9 %collective-permute-start.9 = (bf16[16,2048]{1,0:T(8,128)(2,1)S(1)}, bf16[16,2048]{1,0:T(8,128)(2,1)S(1)}, u32[]{:S(2)}, u32[]{:S(2)}) collective-permute-start(bf16[16,2048]{1,0:T(8,128)(2,1)S(1)} %get-tuple-element.18), channel_id=1, source_target_pairs={{0,1},{1,2},{2,3},{3,4},{4,5},{5,6},{6,7},{7,8},{8,9},{9,10},{10,1... | collective-permute-start | bytes 196616 | tf_op jit(solution)/shard_map/ppermute | solution.py:261
  35.5 5.4 %collective-permute-start.5 = (s32[1,128]{1,0:T(1,128)S(1)}, s32[1,128]{1,0:T(1,128)S(1)}, u32[]{:S(2)}, u32[]{:S(2)}) collective-permute-start(s32[1,128]{1,0:T(1,128)S(1)} %after.7), channel_id=1, source_target_pairs={{0,2},{1,3},{2,0},{3,1},{4,6},{5,7},{6,4},{7,5},{8,10},{9,11},{10,... | collective-permute-start | bytes 1544 | tf_op jit(solution)/shard_map/ppermute | solution.py:113
  39.7 14.9 %collective-permute-start.10 = (bf16[128,2048]{1,0:T(8,128)(2,1)S(1)}, bf16[128,2048]{1,0:T(8,128)(2,1)}, u32[]{:S(2)}, u32[]{:S(2)}) collective-permute-start(bf16[128,2048]{1,0:T(8,128)(2,1)S(1)} %get-tuple-element.19), channel_id=1, source_target_pairs={{0,2},{1,3},{2,0},{3,1},{4,6},{5,7},{6,4},{7,5},{8,10},{9,11},{10,... | collective-permute-start | bytes 1572872 | tf_op jit(solution)/shard_map/ppermute | solution.py:113
  40.8 6.2 %collective-permute-start.6 = (s32[2,128]{1,0:T(2,128)S(1)}, s32[2,128]{1,0:T(2,128)S(1)}, u32[]{:S(2)}, u32[]{:S(2)}) collective-permute-start(s32[2,128]{1,0:T(2,128)S(1)} %pad_add_fusion.2), channel_id=1, source_target_pairs={{0,1},{1,0},{2,3},{3,2},{4,5},{5,4},{6,7},{7,6},{8,9},{9,8},{10,11... | collective-permute-start | bytes 3080 | tf_op jit(solution)/shard_map/ppermute | solution.py:113
  40.9 16.4 %collective-permute-start.14 = (bf16[64,2048]{1,0:T(8,128)(2,1)S(1)}, bf16[64,2048]{1,0:T(8,128)(2,1)S(1)}, u32[]{:S(2)}, u32[]{:S(2)}) collective-permute-start(bf16[64,2048]{1,0:T(8,128)(2,1)S(1)} %after.6.refs_1_), channel_id=1, source_target_pairs={{0,2},{1,3},{2,0},{3,1},{4,6},{5,7},{6,4},{7,5},{8,10},{9,11},{10,... | collective-permute-start | bytes 786440 | tf_op jit(solution)/shard_map/ppermute | solution.py:113
  43.0 15.9 %collective-permute-start.16 = (bf16[64,2048]{1,0:T(8,128)(2,1)S(1)}, bf16[64,2048]{1,0:T(8,128)(2,1)S(1)}, u32[]{:S(2)}, u32[]{:S(2)}) collective-permute-start(bf16[64,2048]{1,0:T(8,128)(2,1)S(1)} %after.9), channel_id=1, source_target_pairs={{0,8},{1,9},{2,10},{3,11},{4,12},{5,13},{6,14},{7,15},{8,0},{9,1},... | collective-permute-start | bytes 786440 | tf_op jit(solution)/shard_map/ppermute | solution.py:113
  46.5 12.5 %collective-permute-start.13 = (bf16[3,64,1024]{2,1,0:T(8,128)(2,1)S(1)}, bf16[3,64,1024]{2,1,0:T(8,128)(2,1)S(1)}, u32[]{:S(2)}, u32[]{:S(2)}) collective-permute-start(bf16[3,64,1024]{2,1,0:T(8,128)(2,1)S(1)} %collective-permute-done.12.refs_2_), channel_id=1, source_target_pairs={{0,16},{16,0},{1,17},{17,1},{2,18},{18,2},{3,19},{19,3},{4,20},{20... | collective-permute-start | bytes 1179656 | tf_op jit(solution)/shard_map/ppermute | solution.py:117
  47.0 5.4 %collective-permute-start.7 = (s32[4,128]{1,0:T(4,128)S(1)}, s32[4,128]{1,0:T(4,128)S(1)}, u32[]{:S(2)}, u32[]{:S(2)}) collective-permute-start(s32[4,128]{1,0:T(4,128)S(1)} %pad_add_fusion.1), channel_id=1, source_target_pairs={{0,4},{1,5},{2,6},{3,7},{4,0},{5,1},{6,2},{7,3},{8,12},{9,13},{10,... | collective-permute-start | bytes 6152 | tf_op jit(solution)/shard_map/ppermute | solution.py:113
  52.4 6.2 %collective-permute-start.8 = (s32[8,128]{1,0:T(8,128)S(1)}, s32[8,128]{1,0:T(8,128)S(1)}, u32[]{:S(2)}, u32[]{:S(2)}) collective-permute-start(s32[8,128]{1,0:T(8,128)S(1)} %pad_add_fusion), channel_id=1, source_target_pairs={{0,8},{1,9},{2,10},{3,11},{4,12},{5,13},{6,14},{7,15},{8,0},{9,1},... | collective-permute-start | bytes 12296 | tf_op jit(solution)/shard_map/ppermute | solution.py:113
  56.7 5.3 %collective-permute-start.11 = (bf16[256,2048]{1,0:T(8,128)(2,1)}, bf16[256,2048]{1,0:T(8,128)(2,1)}, u32[]{:S(2)}, u32[]{:S(2)}) collective-permute-start(bf16[256,2048]{1,0:T(8,128)(2,1)} %pad_maximum_fusion), channel_id=1, source_target_pairs={{0,1},{1,0},{2,3},{3,2},{4,5},{5,4},{6,7},{7,6},{8,9},{9,8},{10,11... | collective-permute-start | bytes 3145736 | tf_op jit(solution)/shard_map/ppermute | solution.py:113
  58.1 2.8 %collective-permute-start.15 = (bf16[128,2048]{1,0:T(8,128)(2,1)}, bf16[128,2048]{1,0:T(8,128)(2,1)}, u32[]{:S(2)}, u32[]{:S(2)}) collective-permute-start(bf16[128,2048]{1,0:T(8,128)(2,1)} %pad_maximum_fusion.2), channel_id=1, source_target_pairs={{0,1},{1,0},{2,3},{3,2},{4,5},{5,4},{6,7},{7,6},{8,9},{9,8},{10,11... | collective-permute-start | bytes 1572872 | tf_op jit(solution)/shard_map/ppermute | solution.py:113
  59.0 8.3 %collective-permute-start.17 = (bf16[64,2048]{1,0:T(8,128)(2,1)S(1)}, bf16[64,2048]{1,0:T(8,128)(2,1)S(1)}, u32[]{:S(2)}, u32[]{:S(2)}) collective-permute-start(bf16[64,2048]{1,0:T(8,128)(2,1)S(1)} %after.10), channel_id=1, source_target_pairs={{0,2},{1,3},{2,0},{3,1},{4,6},{5,7},{6,4},{7,5},{8,10},{9,11},{10,... | collective-permute-start | bytes 786440 | tf_op jit(solution)/shard_map/ppermute | solution.py:113
  67.3 3.0 %collective-permute-start.18 = (bf16[128,2048]{1,0:T(8,128)(2,1)S(1)}, bf16[128,2048]{1,0:T(8,128)(2,1)S(1)}, u32[]{:S(2)}, u32[]{:S(2)}) collective-permute-start(bf16[128,2048]{1,0:T(8,128)(2,1)S(1)} %pad_maximum_fusion.3), channel_id=1, source_target_pairs={{0,1},{1,0},{2,3},{3,2},{4,5},{5,4},{6,7},{7,6},{8,9},{9,8},{10,11... | collective-permute-start | bytes 1572872 | tf_op jit(solution)/shard_map/ppermute | solution.py:113
  67.4 9.2 %collective-permute-start.19 = (bf16[512,256]{1,0:T(8,128)(2,1)S(1)}, bf16[512,256]{1,0:T(8,128)(2,1)S(1)}, u32[]{:S(2)}, u32[]{:S(2)}) collective-permute-start(bf16[512,256]{1,0:T(8,128)(2,1)S(1)} %get-tuple-element.21), channel_id=1, source_target_pairs={{0,4},{1,5},{2,6},{3,7},{4,0},{5,1},{6,2},{7,3},{8,12},{9,13},{10,... | collective-permute-start | bytes 786440 | tf_op jit(solution)/shard_map/ppermute | solution.py:113
  70.1 9.3 %collective-permute-start.20 = (bf16[256,256]{1,0:T(8,128)(2,1)S(1)}, bf16[256,256]{1,0:T(8,128)(2,1)S(1)}, u32[]{:S(2)}, u32[]{:S(2)}) collective-permute-start(bf16[256,256]{1,0:T(8,128)(2,1)S(1)} %get-tuple-element.25), channel_id=1, source_target_pairs={{0,4},{1,5},{2,6},{3,7},{4,0},{5,1},{6,2},{7,3},{8,12},{9,13},{10,... | collective-permute-start | bytes 393224 | tf_op jit(solution)/shard_map/ppermute | solution.py:113
  71.1 10.7 %collective-permute-start.21 = (bf16[256,256]{1,0:T(8,128)(2,1)S(1)}, bf16[256,256]{1,0:T(8,128)(2,1)S(1)}, u32[]{:S(2)}, u32[]{:S(2)}) collective-permute-start(bf16[256,256]{1,0:T(8,128)(2,1)S(1)} %get-tuple-element.23), channel_id=1, source_target_pairs={{0,4},{1,5},{2,6},{3,7},{4,0},{5,1},{6,2},{7,3},{8,12},{9,13},{10,... | collective-permute-start | bytes 393224 | tf_op jit(solution)/shard_map/ppermute | solution.py:113
  (7 other events, 18.6 us)

commit v9 on v3

--- a/solution.py
+++ b/solution.py
@@ -1,6 +1,8 @@
 import jax
 import jax.numpy as jnp
 from jax import lax
+from jax.experimental import pallas as pl
+from jax.experimental.pallas import tpu as pltpu
 from jax.sharding import Mesh
 from jax.sharding import PartitionSpec as P
 
@@ -111,6 +113,23 @@
     )
 
 
+def after_kernel(*refs):
+    del refs
+
+
+def after(value, *others):
+    anywhere = pl.BlockSpec(memory_space=pl.ANY)
+    return pl.pallas_call(
+        after_kernel,
+        out_shape=jax.ShapeDtypeStruct(value.shape, value.dtype),
+        in_specs=[anywhere] * (1 + len(others)),
+        out_specs=anywhere,
+        input_output_aliases={0: 0},
+        compiler_params=pltpu.CompilerParams(vmem_limit_bytes=2**20),
+        name="after",
+    )(value, *others)
+
+
 def body_by_head(frames, conv_weight, qkv_weight, track_ids, track_owner):
     tok_rows = frames.shape[0]
     chips = lax.axis_size("chip")
@@ -158,10 +177,10 @@
         done = lax.dot_general(
             rows, two_heads, (((1,), (1,)), ((), ())), preferred_element_type=jnp.float32
         ).astype(jnp.bfloat16)
-        return jnp.concatenate([done[:, : 3 * HD], xor_swap(done[:, 3 * HD :], Z0)], axis=0)
-
-    first = project(jnp.concatenate([own, beside, far_late, far_beside_late], axis=0))
-    second = project(jnp.concatenate([far_early, far_beside_early], axis=0))
+        return done, jnp.concatenate([done[:, : 3 * HD], xor_swap(done[:, 3 * HD :], Z0)], axis=0)
+
+    raw, first = project(jnp.concatenate([own, beside, far_late, far_beside_late], axis=0))
+    _, second = project(jnp.concatenate([far_early, far_beside_early], axis=0))
 
     first_rows = [(0, 0, tok_rows), (Y, 0, tok_rows), (Z1, part, part), (Z1 | Y, part, part)]
     second_rows = [(Z1, 0, part), (Z1 | Y, 0, part)]
@@ -169,33 +188,30 @@
     for pieces in (first_rows, second_rows):
         order += pieces + [(far ^ Z0, start, count) for far, start, count in pieces]
 
-    groups = track_groups(track_ids, track_owner)[None, :]
+    span = devices * tok_rows
+    times = me * tok_rows + jnp.arange(tok_rows, dtype=jnp.int32)
+    codes = (track_groups(track_ids, track_owner) * span + times)[None, :]
+    codes = after(codes, raw)
     for bit in (CORE, Y, Z0, Z1):
-        groups = jnp.concatenate([groups, xor_swap(groups, bit)], axis=0)
-
-    def of_rows(bit):
-        times = [
-            (me ^ far ^ bit) * tok_rows + start + jnp.arange(count, dtype=jnp.int32)
-            for far, start, count in order
-        ]
-        marks = [groups[far ^ bit, start : start + count] for far, start, count in order]
-        return jnp.concatenate(times), jnp.concatenate(marks)
-
+        codes = jnp.concatenate([codes, xor_swap(codes, bit)], axis=0)
+
+    def codes_at(bit):
+        return jnp.concatenate(
+            [codes[far ^ bit, start : start + count] for far, start, count in order]
+        )
+
+    asking = codes_at(0)
+    keys = jnp.concatenate([asking, codes_at(CORE)])
+    least = asking // span * span
     projected = jnp.concatenate([first, second], axis=0)
     query = projected[:, :HD]
     keyed = jnp.concatenate(
         [projected[:, HD:], xor_swap(first[:, HD:], CORE), xor_swap(second[:, HD:], CORE)], axis=0
     )
-    own_times, own_groups = of_rows(0)
-    other_times, other_groups = of_rows(CORE)
-    key_times = jnp.concatenate([own_times, other_times])
-    key_groups = jnp.concatenate([own_groups, other_groups])
     scores = lax.dot_general(
         query, keyed[:, :HD], (((1,), (1,)), ((), ())), preferred_element_type=jnp.float32
     ) * (1.0 / HD**0.5)
-    allowed = (key_times[None, :] <= own_times[:, None]) & (
-        key_groups[None, :] == own_groups[:, None]
-    )
+    allowed = (keys[None, :] <= asking[:, None]) & (keys[None, :] >= least[:, None])
     scores = jnp.where(allowed, scores, jnp.float32(-1e30))
     expd = jnp.exp(scores - jnp.max(scores, axis=-1, keepdims=True))
     weights = (expd / jnp.sum(expd, axis=-1, keepdims=True)).astype(jnp.bfloat16)

time: 93.9 us -> 101 us (1.076)
  waiting for transfers between devices: 39.5 us -> 34.1 us
  local copies, waits for them, and re-layouts: 4.2 us -> 9.57 us
  starting transfers between devices: 25.9 us -> 31.1 us
  other arithmetic: 3.74 us -> 5.4 us
    ppermute x18, waiting for transfers between devices: 39.5 us -> 34 us  [xor_swap(): return lax.ppermute(value, axes, [(d, d ^ bit) for d in range(count)])]
    ppermute x18, starting transfers between devices: 14.2 us -> 19.5 us  [xor_swap(): return lax.ppermute(value, axes, [(d, d ^ bit) for d in range(count)])]
    unnamed x12 -> x20, local copies, waits for them, and re-layouts: 1.24 us -> 6.07 us
    another operation x5, other arithmetic: 0.62 us -> 2.03 us  [by_bit(): jnp.stack([jnp.where(bit == 0, mine, theirs), jnp.where(bit == 0, theirs,...]
  transfers between devices with their start and end apart: 22 -> 22, of which waited for: 10 -> 9; matrix products, arithmetic and copies ran while one was open for 7% -> 13% of each run, Pallas kernels for 0% -> 0%
where the time goes in v9:
time: 101 us; the launch traced here: 100 us
  waiting for transfers between devices  34.1 us (34%)
  starting transfers between devices  31.1 us (31%)
  blocking collectives  12.1 us (12%)
  local copies, waits for them, and re-layouts  9.57 us (9%)
  matrix products  7.44 us (7%)
  other arithmetic  5.4 us (5%)
    ppermute x18, waiting for transfers between devices, xor_swap(): return lax.ppermute(value, axes, [(d, d ^ bit) for d in range(count)])  34 us
    ppermute x18, starting transfers between devices, xor_swap(): return lax.ppermute(value, axes, [(d, d ^ bit) for d in range(count)])  19.5 us
    all_to_all x1, blocking collectives, body_by_head(): lax.all_to_all(sent, 'chip', split_axis=0, concat_axis=0, tiled=True)  12.1 us
    ppermute x3, starting transfers between devices, body_by_head(): lax.ppermute(held[j], both, [(d, (3 * d + j) % devices) for d in range(de...  8.43 us
    unnamed x20, local copies, waits for them, and re-layouts  6.07 us
    dot_general x2, matrix products, project(): lax.dot_general(rows, two_heads, (((1,), (1,)), ((), ())), preferred_elem...  3.56 us
    ppermute x1, starting transfers between devices, body_by_head(): lax.ppermute(frames[tok_rows - (KW - 1):], both, [(i, i + 1) for i in ran...  3.2 us
    dot_general x1, matrix products, body_by_head(): lax.dot_general(query, keyed[:, :HD], (((1,), (1,)), ((), ())), preferred...  2.28 us
  transfers between devices with their start and end apart: 22, of which 9 were waited for; matrix products, arithmetic and copies ran while one was open for 13% of the time, Pallas kernels for 0%

profile of v9, /device:TPU:0, one launch (start us, length us, event | category | flops | bytes accessed | tf_op | source)
XLA Modules:
  0.0 100.3 jit_solution(2714190054963115702)
XLA Ops:
  1.9 3.8 %collective-permute-start.5 = (bf16[64,1024]{1,0:T(8,128)(2,1)S(1)}, bf16[64,1024]{1,0:T(8,128)(2,1)S(1)}, u32[]{:S(2)}, u32[]{:S(2)}) collective-permute-start(bf16[64,1024]{1,0:T(8,128)(2,1)S(1)} %get-tuple-element.20), channel_id=1, source_target_pairs={{0,1},{1,4},{2,7},{3,10},{4,13},{5,0},{6,3},{7,6},{8,9},{9,12},{10... | collective-permute-start | bytes 393224 | tf_op jit(solution)/shard_map/ppermute | solution.py:163
  5.7 3.9 %collective-permute-start.6 = (bf16[64,1024]{1,0:T(8,128)(2,1)S(1)}, bf16[64,1024]{1,0:T(8,128)(2,1)S(1)}, u32[]{:S(2)}, u32[]{:S(2)}) collective-permute-start(bf16[64,1024]{1,0:T(8,128)(2,1)S(1)} %get-tuple-element.19), channel_id=1, source_target_pairs={{0,2},{1,5},{2,8},{3,11},{4,14},{5,1},{6,4},{7,7},{8,10},{9,13},{1... | collective-permute-start | bytes 393224 | tf_op jit(solution)/shard_map/ppermute | solution.py:163
  10.5 3.2 %collective-permute-start = (bf16[3,2048]{1,0:T(4,128)(2,1)S(1)}, bf16[3,2048]{1,0:T(4,128)(2,1)S(1)}, u32[]{:S(2)}, u32[]{:S(2)}) collective-permute-start(bf16[3,2048]{1,0:T(4,128)(2,1)S(1)} %slice.197), channel_id=1, source_target_pairs={{0,1},{1,2},{2,3},{3,4},{4,5},{5,6},{6,7},{7,8},{8,9},{9,10},{10,1... | collective-permute-start | bytes 36872 | tf_op jit(solution)/shard_map/ppermute | solution.py:147
  15.4 1.6 %collective-permute-start.7 = (bf16[3,64,1024]{2,1,0:T(8,128)(2,1)S(1)}, bf16[3,64,1024]{2,1,0:T(8,128)(2,1)S(1)}, u32[]{:S(2)}, u32[]{:S(2)}) collective-permute-start(bf16[3,64,1024]{2,1,0:T(8,128)(2,1)S(1)} %constant_dynamic-slice_fusion), channel_id=1, source_target_pairs={{0,16},{1,17},{2,18},{3,19},{4,20},{5,21},{6,22},{7,23},{8,24},{9,... | collective-permute-start | bytes 1179656 | tf_op jit(solution)/shard_map/ppermute | solution.py:107
  17.0 4.2 %collective-permute-start.9 = (bf16[3,64,1024]{2,1,0:T(8,128)(2,1)S(1)}, bf16[3,64,1024]{2,1,0:T(8,128)(2,1)S(1)}, u32[]{:S(2)}, u32[]{:S(2)}) collective-permute-start(bf16[3,64,1024]{2,1,0:T(8,128)(2,1)S(1)} %constant_dynamic-slice_fusion), channel_id=1, source_target_pairs={{0,4},{1,5},{2,6},{3,7},{4,0},{5,1},{6,2},{7,3},{8,12},{9,13},{10,... | collective-permute-start | bytes 1179656 | tf_op jit(solution)/shard_map/ppermute | solution.py:107
  21.5 1.9 %collective-permute-start.2 = (bf16[64,2048]{1,0:T(8,128)(2,1)S(1)}, bf16[64,2048]{1,0:T(8,128)(2,1)}, u32[]{:S(2)}, u32[]{:S(2)}) collective-permute-start(bf16[64,2048]{1,0:T(8,128)(2,1)S(1)} %get-tuple-element.6), channel_id=1, source_target_pairs={{0,8},{1,9},{2,10},{3,11},{4,12},{5,13},{6,14},{7,15},{8,0},{9,1},... | collective-permute-start | bytes 786440 | tf_op jit(solution)/shard_map/ppermute | solution.py:107
  23.3 10.8 %collective-permute-done.9 = bf16[3,64,1024]{2,1,0:T(8,128)(2,1)S(1)} collective-permute-done((bf16[3,64,1024]{2,1,0:T(8,128)(2,1)S(1)}, bf16[3,64,1024]{2,1,0:T(8,128)(2,1)S(1)}, u32[]{:S(2)}, u32[]{:S(2)}) %collective-permute-start.9) | collective-permute-done | bytes 393248 | tf_op jit(solution)/shard_map/ppermute | solution.py:107
  34.8 2.1 %collective-permute-start.17 = (bf16[64,2048]{1,0:T(8,128)(2,1)S(1)}, bf16[64,2048]{1,0:T(8,128)(2,1)}, u32[]{:S(2)}, u32[]{:S(2)}) collective-permute-start(bf16[64,2048]{1,0:T(8,128)(2,1)S(1)} %get-tuple-element.8), channel_id=1, source_target_pairs={{0,8},{1,9},{2,10},{3,11},{4,12},{5,13},{6,14},{7,15},{8,0},{9,1},... | collective-permute-start | bytes 786440 | tf_op jit(solution)/shard_map/ppermute | solution.py:107
  37.2 5.5 %collective-permute-done.10 = bf16[3,64,1024]{2,1,0:T(8,128)(2,1)S(1)} collective-permute-done((bf16[3,64,1024]{2,1,0:T(8,128)(2,1)S(1)}, bf16[3,64,1024]{2,1,0:T(8,128)(2,1)S(1)}, u32[]{:S(2)}, u32[]{:S(2)}) %collective-permute-start.10) | collective-permute-done | bytes 393248 | tf_op jit(solution)/shard_map/ppermute | solution.py:107
  43.0 3.2 %collective-permute-start.3 = (bf16[64,2048]{1,0:T(8,128)(2,1)}, bf16[64,2048]{1,0:T(8,128)(2,1)S(1)}, u32[]{:S(2)}, u32[]{:S(2)}) collective-permute-start(bf16[64,2048]{1,0:T(8,128)(2,1)} %collective-permute-done.2), channel_id=1, source_target_pairs={{0,2},{1,3},{2,0},{3,1},{4,6},{5,7},{6,4},{7,5},{8,10},{9,11},{10,... | collective-permute-start | bytes 786440 | tf_op jit(solution)/shard_map/ppermute | solution.py:107
  46.2 1.6 %collective-permute-done.17 = bf16[64,2048]{1,0:T(8,128)(2,1)} collective-permute-done((bf16[64,2048]{1,0:T(8,128)(2,1)S(1)}, bf16[64,2048]{1,0:T(8,128)(2,1)}, u32[]{:S(2)}, u32[]{:S(2)}) %collective-permute-start.17) | collective-permute-done | bytes 262176 | tf_op jit(solution)/shard_map/ppermute | solution.py:107
  50.2 1.9 %constant_dynamic-update-slice_fusion.2 = bf16[384,2048]{1,0:T(8,128)(2,1)} fusion(bf16[384,2048]{1,0:T(8,128)(2,1)} %copy-done.3, bf16[128,2048]{1,0:T(8,128)(2,1)} %collective-permute-done.1), kind=kLoop, calls=%fused_computation.81 | loop fusion | bytes 1048576
  52.0 1.7 %constant_dynamic-update-slice_fusion.1 = bf16[384,2048]{1,0:T(8,128)(2,1)} fusion(bf16[384,2048]{1,0:T(8,128)(2,1)} %constant_dynamic-update-slice_fusion.2, bf16[64,2048]{1,0:T(8,128)(2,1)} %collective-permute-done.2), kind=kLoop, calls=%fused_computation.80 | loop fusion | bytes 524288
  53.7 1.9 %collective-permute-done.3 = bf16[64,2048]{1,0:T(8,128)(2,1)S(1)} collective-permute-done((bf16[64,2048]{1,0:T(8,128)(2,1)}, bf16[64,2048]{1,0:T(8,128)(2,1)S(1)}, u32[]{:S(2)}, u32[]{:S(2)}) %collective-permute-start.3) | collective-permute-done | bytes 262176 | tf_op jit(solution)/shard_map/ppermute | solution.py:107
  56.4 1.6 %select_bitcast_fusion.1 = (bf16[3,1,64,2048]{3,2,0,1:T(8,128)(2,1)S(1)}, bf16[3,1,64,2048]{3,2,0,1:T(8,128)(2,1)S(1)}, bf16[3,1,64,2048]{3,2,0,1:T(8,128)(2,1)S(1)}, bf16[3,1,64,2048]{3,2,0,1:T(8,128)(2,1)S(1)}) fusion(bf16[3,64,2048]{2,1,0:T(8,128)(2,1)S(1)} %bitcast.143, bf16[3,64,2048]{2,1,0:T(8,128)(2,1)} %collective-permute-done.11, pred[]{:T(512)S(6)} %eq.13, ...), kind=kLoop, calls=%fused_computation.21 | loop fusion | flops 1572864 | bytes 6291457 | tf_op jit(solution)/shard_map/stack | solution.py:111
  59.9 1.4 %fusion.4.refs_1_ = bf16[384,768]{1,0:T(8,128)(2,1)S(1)} fusion(bf16[384,2048]{1,0:T(8,128)(2,1)S(1)} %copy-done.4, bf16[384,2048]{1,0:T(8,128)(2,1)S(1)} %bitcast.146, bf16[384,2048]{1,0:T(8,128)(2,1)S(1)} %bitcast.144), kind=kOutput, calls=%fused_computation.10 | convolution fusion | flops 1214545920 | bytes 5308416 | tf_op jit(solution)/shard_map/dot_general | solution.py:177
  61.5 4.2 %collective-permute-start.16 = (bf16[384,384]{1,0:T(8,128)(2,1)S(1)}, bf16[384,384]{1,0:T(8,128)(2,1)S(1)}, u32[]{:S(2)}, u32[]{:S(2)}) collective-permute-start(bf16[384,384]{1,0:T(8,128)(2,1)S(1)} %get-tuple-element.18), channel_id=1, source_target_pairs={{0,4},{1,5},{2,6},{3,7},{4,0},{5,1},{6,2},{7,3},{8,12},{9,13},{10,... | collective-permute-start | bytes 884744 | tf_op jit(solution)/shard_map/ppermute | solution.py:107
  65.6 2.1 %fusion.6 = bf16[128,768]{1,0:T(8,128)(2,1)S(1)} fusion(bf16[384,2048]{1,0:T(8,128)(2,1)S(1)} %bitcast.147, bf16[384,2048]{1,0:T(8,128)(2,1)S(1)} %bitcast.145, bf16[64,2048]{1,0:T(8,128)(2,1)S(1)} %collective-permute-done.18, bf16[64,2048]{1,0:T(8,128)(2,1)} %collective-permute-done.17), kind=kOutput, calls=%fused_computation.12 | convolution fusion | flops 410091520 | bytes 3866624 | tf_op jit(solution)/shard_map/dot_general | solution.py:177
  68.0 3.4 %collective-permute-done.13 = s32[2,128]{1,0:T(2,128)S(1)} collective-permute-done((s32[2,128]{1,0:T(2,128)S(1)}, s32[2,128]{1,0:T(2,128)S(1)}, u32[]{:S(2)}, u32[]{:S(2)}) %collective-permute-start.13) | collective-permute-done | bytes 1056 | tf_op jit(solution)/shard_map/ppermute | solution.py:107
  71.5 3.9 %collective-permute-done.14 = s32[4,128]{1,0:T(4,128)S(1)} collective-permute-done((s32[4,128]{1,0:T(4,128)S(1)}, s32[4,128]{1,0:T(4,128)S(1)}, u32[]{:S(2)}, u32[]{:S(2)}) %collective-permute-start.14) | collective-permute-done | bytes 2080 | tf_op jit(solution)/shard_map/ppermute | solution.py:107
  75.7 4.4 %collective-permute-done.15 = s32[8,128]{1,0:T(8,128)S(1)} collective-permute-done((s32[8,128]{1,0:T(8,128)S(1)}, s32[8,128]{1,0:T(8,128)S(1)}, u32[]{:S(2)}, u32[]{:S(2)}) %collective-permute-start.15) | collective-permute-done | bytes 4128 | tf_op jit(solution)/shard_map/ppermute | solution.py:107
  81.8 2.3 %fusion.54 = (f32[1024]{0:T(1024)S(1)}, f32[1024,2048]{1,0:T(8,128)S(1)}) fusion(bf16[2048,256]{1,0:T(8,128)(2,1)S(1)} %fusion.8, bf16[128,384]{1,0:T(8,128)(2,1)S(1)} %collective-permute-done.19, bf16[128,384]{1,0:T(8,128)(2,1)S(1)} %get-tuple-element.22, bf16[384,384]{1,0:T(8,128)(2,1)S(1)} %collective-permute-done.16, ...), kind=kOutput, calls=%fused_computation.145 | convolution fusion | flops 550501376 | bytes 9719808 | tf_op jit(solution)/shard_map/dot_general | solution.py:211
  85.3 1.6 %fusion.5 = bf16[1024,128]{1,0:T(8,128)(2,1)S(1)} fusion(f32[1024,2048]{1,0:T(8,128)S(1)} %get-tuple-element.51, f32[1024]{0:T(1024)S(1)} %fusion, f32[1024]{0:T(1024)S(1)} %get-tuple-element.50, bf16[2048,256]{1,0:T(8,128)(2,1)S(1)} %fusion.8), kind=kOutput, calls=%fused_computation.11 | convolution fusion | flops 543293440 | bytes 9183232 | tf_op jit(solution)/shard_map/dot_general | solution.py:218
  87.2 12.1 %all_to_all.5 = bf16[8,128,128]{2,1,0:T(8,128)(2,1)S(1)} all-to-all(bf16[8,128,128]{2,1,0:T(8,128)(2,1)S(1)} %fusion.35), channel_id=1, replica_groups=mesh['grp'=2,'chip'=8,'core'=2] {'chip'}, dimensions={0} | all-to-all | bytes 524288 | tf_op jit(solution)/shard_map/all_to_all | solution.py:227
  (103 shorter events, 15.5 us)
Async XLA Ops:
  0.0 15.0 %copy-start.1 = (bf16[128,2048]{1,0:T(8,128)(2,1)S(1)}, bf16[128,2048]{1,0:T(8,128)(2,1)}, u32[]{:S(2)}) copy-start(bf16[128,2048]{1,0:T(8,128)(2,1)} %param.5) | copy-start | bytes 1572868
  1.3 14.0 %collective-permute-start.4 = (bf16[64,1024]{1,0:T(8,128)(2,1)S(1)}, bf16[64,1024]{1,0:T(8,128)(2,1)S(1)}, u32[]{:S(2)}, u32[]{:S(2)}) collective-permute-start(bf16[64,1024]{1,0:T(8,128)(2,1)S(1)} %get-tuple-element.21), channel_id=1, source_target_pairs={{0,0},{1,3},{2,6},{3,9},{4,12},{5,15},{6,2},{7,5},{8,8},{9,11},{10... | collective-permute-start | bytes 393224 | tf_op jit(solution)/shard_map/ppermute | solution.py:163
  1.9 13.4 %collective-permute-start.5 = (bf16[64,1024]{1,0:T(8,128)(2,1)S(1)}, bf16[64,1024]{1,0:T(8,128)(2,1)S(1)}, u32[]{:S(2)}, u32[]{:S(2)}) collective-permute-start(bf16[64,1024]{1,0:T(8,128)(2,1)S(1)} %get-tuple-element.20), channel_id=1, source_target_pairs={{0,1},{1,4},{2,7},{3,10},{4,13},{5,0},{6,3},{7,6},{8,9},{9,12},{10... | collective-permute-start | bytes 393224 | tf_op jit(solution)/shard_map/ppermute | solution.py:163
  5.7 9.6 %collective-permute-start.6 = (bf16[64,1024]{1,0:T(8,128)(2,1)S(1)}, bf16[64,1024]{1,0:T(8,128)(2,1)S(1)}, u32[]{:S(2)}, u32[]{:S(2)}) collective-permute-start(bf16[64,1024]{1,0:T(8,128)(2,1)S(1)} %get-tuple-element.19), channel_id=1, source_target_pairs={{0,2},{1,5},{2,8},{3,11},{4,14},{5,1},{6,4},{7,7},{8,10},{9,13},{1... | collective-permute-start | bytes 393224 | tf_op jit(solution)/shard_map/ppermute | solution.py:163
  10.5 4.4 %collective-permute-start = (bf16[3,2048]{1,0:T(4,128)(2,1)S(1)}, bf16[3,2048]{1,0:T(4,128)(2,1)S(1)}, u32[]{:S(2)}, u32[]{:S(2)}) collective-permute-start(bf16[3,2048]{1,0:T(4,128)(2,1)S(1)} %slice.197), channel_id=1, source_target_pairs={{0,1},{1,2},{2,3},{3,4},{4,5},{5,6},{6,7},{7,8},{8,9},{9,10},{10,1... | collective-permute-start | bytes 36872 | tf_op jit(solution)/shard_map/ppermute | solution.py:147
  15.4 21.4 %collective-permute-start.7 = (bf16[3,64,1024]{2,1,0:T(8,128)(2,1)S(1)}, bf16[3,64,1024]{2,1,0:T(8,128)(2,1)S(1)}, u32[]{:S(2)}, u32[]{:S(2)}) collective-permute-start(bf16[3,64,1024]{2,1,0:T(8,128)(2,1)S(1)} %constant_dynamic-slice_fusion), channel_id=1, source_target_pairs={{0,16},{1,17},{2,18},{3,19},{4,20},{5,21},{6,22},{7,23},{8,24},{9,... | collective-permute-start | bytes 1179656 | tf_op jit(solution)/shard_map/ppermute | solution.py:107
  17.0 17.2 %collective-permute-start.9 = (bf16[3,64,1024]{2,1,0:T(8,128)(2,1)S(1)}, bf16[3,64,1024]{2,1,0:T(8,128)(2,1)S(1)}, u32[]{:S(2)}, u32[]{:S(2)}) collective-permute-start(bf16[3,64,1024]{2,1,0:T(8,128)(2,1)S(1)} %constant_dynamic-slice_fusion), channel_id=1, source_target_pairs={{0,4},{1,5},{2,6},{3,7},{4,0},{5,1},{6,2},{7,3},{8,12},{9,13},{10,... | collective-permute-start | bytes 1179656 | tf_op jit(solution)/shard_map/ppermute | solution.py:107
  21.5 15.6 %copy-start.3 = (bf16[384,2048]{1,0:T(8,128)(2,1)}, bf16[384,2048]{1,0:T(8,128)(2,1)S(1)}, u32[]{:S(2)}) copy-start(bf16[384,2048]{1,0:T(8,128)(2,1)S(1)} %get-tuple-element.5) | copy-start | bytes 4718596
  21.5 21.5 %collective-permute-start.2 = (bf16[64,2048]{1,0:T(8,128)(2,1)S(1)}, bf16[64,2048]{1,0:T(8,128)(2,1)}, u32[]{:S(2)}, u32[]{:S(2)}) collective-permute-start(bf16[64,2048]{1,0:T(8,128)(2,1)S(1)} %get-tuple-element.6), channel_id=1, source_target_pairs={{0,8},{1,9},{2,10},{3,11},{4,12},{5,13},{6,14},{7,15},{8,0},{9,1},... | collective-permute-start | bytes 786440 | tf_op jit(solution)/shard_map/ppermute | solution.py:107
  34.2 8.5 %collective-permute-start.10 = (bf16[3,64,1024]{2,1,0:T(8,128)(2,1)S(1)}, bf16[3,64,1024]{2,1,0:T(8,128)(2,1)S(1)}, u32[]{:S(2)}, u32[]{:S(2)}) collective-permute-start(bf16[3,64,1024]{2,1,0:T(8,128)(2,1)S(1)} %collective-permute-done.9), channel_id=1, source_target_pairs={{0,16},{1,17},{2,18},{3,19},{4,20},{5,21},{6,22},{7,23},{8,24},{9,... | collective-permute-start | bytes 1179656 | tf_op jit(solution)/shard_map/ppermute | solution.py:107
  34.8 13.0 %collective-permute-start.17 = (bf16[64,2048]{1,0:T(8,128)(2,1)S(1)}, bf16[64,2048]{1,0:T(8,128)(2,1)}, u32[]{:S(2)}, u32[]{:S(2)}) collective-permute-start(bf16[64,2048]{1,0:T(8,128)(2,1)S(1)} %get-tuple-element.8), channel_id=1, source_target_pairs={{0,8},{1,9},{2,10},{3,11},{4,12},{5,13},{6,14},{7,15},{8,0},{9,1},... | collective-permute-start | bytes 786440 | tf_op jit(solution)/shard_map/ppermute | solution.py:107
  36.9 13.3 %collective-permute-start.1 = (bf16[128,2048]{1,0:T(8,128)(2,1)S(1)}, bf16[128,2048]{1,0:T(8,128)(2,1)}, u32[]{:S(2)}, u32[]{:S(2)}) collective-permute-start(bf16[128,2048]{1,0:T(8,128)(2,1)S(1)} %pad_maximum_fusion.12), channel_id=1, source_target_pairs={{0,2},{1,3},{2,0},{3,1},{4,6},{5,7},{6,4},{7,5},{8,10},{9,11},{10,... | collective-permute-start | bytes 1572872 | tf_op jit(solution)/shard_map/ppermute | solution.py:107
  37.1 19.3 %collective-permute-start.8 = (bf16[3,64,2048]{2,1,0:T(8,128)(2,1)S(1)}, bf16[3,64,2048]{2,1,0:T(8,128)(2,1)}, u32[]{:S(2)}, u32[]{:S(2)}) collective-permute-start(bf16[3,64,2048]{2,1,0:T(8,128)(2,1)S(1)} %bitcast.140), channel_id=1, source_target_pairs={{0,1},{1,0},{2,3},{3,2},{4,5},{5,4},{6,7},{7,6},{8,9},{9,8},{10,11... | collective-permute-start | bytes 2359304 | tf_op jit(solution)/shard_map/ppermute | solution.py:107
  42.9 13.5 %collective-permute-start.11 = (bf16[3,64,2048]{2,1,0:T(8,128)(2,1)S(1)}, bf16[3,64,2048]{2,1,0:T(8,128)(2,1)}, u32[]{:S(2)}, u32[]{:S(2)}) collective-permute-start(bf16[3,64,2048]{2,1,0:T(8,128)(2,1)S(1)} %bitcast.142), channel_id=1, source_target_pairs={{0,1},{1,0},{2,3},{3,2},{4,5},{5,4},{6,7},{7,6},{8,9},{9,8},{10,11... | collective-permute-start | bytes 2359304 | tf_op jit(solution)/shard_map/ppermute | solution.py:107
  43.0 12.7 %collective-permute-start.3 = (bf16[64,2048]{1,0:T(8,128)(2,1)}, bf16[64,2048]{1,0:T(8,128)(2,1)S(1)}, u32[]{:S(2)}, u32[]{:S(2)}) collective-permute-start(bf16[64,2048]{1,0:T(8,128)(2,1)} %collective-permute-done.2), channel_id=1, source_target_pairs={{0,2},{1,3},{2,0},{3,1},{4,6},{5,7},{6,4},{7,5},{8,10},{9,11},{10,... | collective-permute-start | bytes 786440 | tf_op jit(solution)/shard_map/ppermute | solution.py:107
  47.7 17.9 %collective-permute-start.18 = (bf16[64,2048]{1,0:T(8,128)(2,1)}, bf16[64,2048]{1,0:T(8,128)(2,1)S(1)}, u32[]{:S(2)}, u32[]{:S(2)}) collective-permute-start(bf16[64,2048]{1,0:T(8,128)(2,1)} %collective-permute-done.17), channel_id=1, source_target_pairs={{0,2},{1,3},{2,0},{3,1},{4,6},{5,7},{6,4},{7,5},{8,10},{9,11},{10,... | collective-permute-start | bytes 786440 | tf_op jit(solution)/shard_map/ppermute | solution.py:107
  61.3 6.4 %collective-permute-start.12 = (s32[1,128]{1,0:T(1,128)S(1)}, s32[1,128]{1,0:T(1,128)S(1)}, u32[]{:S(2)}, u32[]{:S(2)}) collective-permute-start(s32[1,128]{1,0:T(1,128)S(1)} %after.1), channel_id=1, source_target_pairs={{0,1},{1,0},{2,3},{3,2},{4,5},{5,4},{6,7},{7,6},{8,9},{9,8},{10,11... | collective-permute-start | bytes 1544 | tf_op jit(solution)/shard_map/ppermute | solution.py:107
  61.5 14.1 %collective-permute-start.16 = (bf16[384,384]{1,0:T(8,128)(2,1)S(1)}, bf16[384,384]{1,0:T(8,128)(2,1)S(1)}, u32[]{:S(2)}, u32[]{:S(2)}) collective-permute-start(bf16[384,384]{1,0:T(8,128)(2,1)S(1)} %get-tuple-element.18), channel_id=1, source_target_pairs={{0,4},{1,5},{2,6},{3,7},{4,0},{5,1},{6,2},{7,3},{8,12},{9,13},{10,... | collective-permute-start | bytes 884744 | tf_op jit(solution)/shard_map/ppermute | solution.py:107
  67.8 3.6 %collective-permute-start.13 = (s32[2,128]{1,0:T(2,128)S(1)}, s32[2,128]{1,0:T(2,128)S(1)}, u32[]{:S(2)}, u32[]{:S(2)}) collective-permute-start(s32[2,128]{1,0:T(2,128)S(1)} %pad_add_fusion.2), channel_id=1, source_target_pairs={{0,2},{1,3},{2,0},{3,1},{4,6},{5,7},{6,4},{7,5},{8,10},{9,11},{10,... | collective-permute-start | bytes 3080 | tf_op jit(solution)/shard_map/ppermute | solution.py:107
  67.9 12.3 %collective-permute-start.19 = (bf16[128,384]{1,0:T(8,128)(2,1)S(1)}, bf16[128,384]{1,0:T(8,128)(2,1)S(1)}, u32[]{:S(2)}, u32[]{:S(2)}) collective-permute-start(bf16[128,384]{1,0:T(8,128)(2,1)S(1)} %get-tuple-element.23), channel_id=1, source_target_pairs={{0,4},{1,5},{2,6},{3,7},{4,0},{5,1},{6,2},{7,3},{8,12},{9,13},{10,... | collective-permute-start | bytes 294920 | tf_op jit(solution)/shard_map/ppermute | solution.py:107
  71.4 4.0 %collective-permute-start.14 = (s32[4,128]{1,0:T(4,128)S(1)}, s32[4,128]{1,0:T(4,128)S(1)}, u32[]{:S(2)}, u32[]{:S(2)}) collective-permute-start(s32[4,128]{1,0:T(4,128)S(1)} %pad_add_fusion.1), channel_id=1, source_target_pairs={{0,4},{1,5},{2,6},{3,7},{4,0},{5,1},{6,2},{7,3},{8,12},{9,13},{10,... | collective-permute-start | bytes 6152 | tf_op jit(solution)/shard_map/ppermute | solution.py:107
  75.4 4.6 %collective-permute-start.15 = (s32[8,128]{1,0:T(8,128)S(1)}, s32[8,128]{1,0:T(8,128)S(1)}, u32[]{:S(2)}, u32[]{:S(2)}) collective-permute-start(s32[8,128]{1,0:T(8,128)S(1)} %pad_add_fusion), channel_id=1, source_target_pairs={{0,8},{1,9},{2,10},{3,11},{4,12},{5,13},{6,14},{7,15},{8,0},{9,1},... | collective-permute-start | bytes 12296 | tf_op jit(solution)/shard_map/ppermute | solution.py:107
  75.6 6.1 %collective-permute-start.20 = (bf16[768,256]{1,0:T(8,128)(2,1)S(1)}, bf16[768,256]{1,0:T(8,128)(2,1)S(1)}, u32[]{:S(2)}, u32[]{:S(2)}) collective-permute-start(bf16[768,256]{1,0:T(8,128)(2,1)S(1)} %pad_maximum_fusion.13), channel_id=1, source_target_pairs={{0,1},{1,0},{2,3},{3,2},{4,5},{5,4},{6,7},{7,6},{8,9},{9,8},{10,11... | collective-permute-start | bytes 1179656 | tf_op jit(solution)/shard_map/ppermute | solution.py:107
  80.3 1.4 %collective-permute-start.21 = (bf16[256,256]{1,0:T(8,128)(2,1)S(1)}, bf16[256,256]{1,0:T(8,128)(2,1)S(1)}, u32[]{:S(2)}, u32[]{:S(2)}) collective-permute-start(bf16[256,256]{1,0:T(8,128)(2,1)S(1)} %pad_maximum_fusion.14), channel_id=1, source_target_pairs={{0,1},{1,0},{2,3},{3,2},{4,5},{5,4},{6,7},{7,6},{8,9},{9,8},{10,11... | collective-permute-start | bytes 393224 | tf_op jit(solution)/shard_map/ppermute | solution.py:107
  (6 other events, 61.7 us)

commit v10 on v9

--- a/solution.py
+++ b/solution.py
@@ -1,8 +1,6 @@
 import jax
 import jax.numpy as jnp
 from jax import lax
-from jax.experimental import pallas as pl
-from jax.experimental.pallas import tpu as pltpu
 from jax.sharding import Mesh
 from jax.sharding import PartitionSpec as P
 
@@ -113,21 +111,13 @@
     )
 
 
-def after_kernel(*refs):
-    del refs
-
-
-def after(value, *others):
-    anywhere = pl.BlockSpec(memory_space=pl.ANY)
-    return pl.pallas_call(
-        after_kernel,
-        out_shape=jax.ShapeDtypeStruct(value.shape, value.dtype),
-        in_specs=[anywhere] * (1 + len(others)),
-        out_specs=anywhere,
-        input_output_aliases={0: 0},
-        compiler_params=pltpu.CompilerParams(vmem_limit_bytes=2**20),
-        name="after",
-    )(value, *others)
+def zero_after(*arrays):
+    total = jnp.zeros((), jnp.bfloat16)
+    for array in arrays:
+        last = array[(-1,) * array.ndim]
+        absent = last < 0 if array.dtype == jnp.int32 else last != last
+        total = total + jnp.where(absent, 1.0, 0.0).astype(jnp.bfloat16)
+    return total
 
 
 def body_by_head(frames, conv_weight, qkv_weight, track_ids, track_owner):
@@ -151,7 +141,7 @@
     early = convolve(frames[:part], conv_weight, rim_rows)
 
     far_late = xor_swap(late, Z1)
-    far_early = xor_swap(early, Z1)
+    far_early = xor_swap(early + zero_after(far_late), Z1)
     own = jnp.concatenate([early, late], axis=0)
     beside = xor_swap(own, Y)
     far_beside_late = xor_swap(far_late, Y)
@@ -164,36 +154,49 @@
         for j in range(3)
     ]
     mine = lax.dynamic_slice_in_dim(jnp.stack(moved + moved[:2]), lax.rem(me, 3), 3, 0)
+    mine_too = xor_swap(mine, devices, every)
     paired = xor_swap(mine, Z0)
 
-    def whole_head(quarter):
-        wide = by_bit(grp, quarter, xor_swap(quarter, devices, every), 2)
-        wide = wide.reshape(3, HD // 2, features)
+    cut = half // 2
+    fourth = jnp.concatenate(
+        [
+            xor_swap(paired[:, :, :cut], devices, every),
+            xor_swap(mine_too[:, :, cut:], Z0),
+        ],
+        axis=2,
+    )
+
+    span = devices * tok_rows
+    times = me * tok_rows + jnp.arange(tok_rows, dtype=jnp.int32)
+    codes = (track_groups(track_ids, track_owner) * span + times)[None, :]
+    codes = codes + zero_after(fourth).astype(jnp.int32)
+    for bit in (CORE, Y, Z0, Z1):
+        codes = jnp.concatenate([codes, xor_swap(codes, bit)], axis=0)
+
+    def whole_head(quarter, quarter_too):
+        wide = by_bit(grp, quarter, quarter_too, 2).reshape(3, HD // 2, features)
         return by_bit(core, wide, xor_swap(wide, CORE), 1).reshape(3 * HD, features)
 
-    two_heads = jnp.concatenate([whole_head(mine), whole_head(paired)], axis=0)
+    two_heads = jnp.concatenate(
+        [whole_head(mine, mine_too), whole_head(paired, fourth)], axis=0
+    )
 
     def project(rows):
         done = lax.dot_general(
             rows, two_heads, (((1,), (1,)), ((), ())), preferred_element_type=jnp.float32
         ).astype(jnp.bfloat16)
-        return done, jnp.concatenate([done[:, : 3 * HD], xor_swap(done[:, 3 * HD :], Z0)], axis=0)
-
-    raw, first = project(jnp.concatenate([own, beside, far_late, far_beside_late], axis=0))
-    _, second = project(jnp.concatenate([far_early, far_beside_early], axis=0))
+        return jnp.concatenate([done[:, : 3 * HD], xor_swap(done[:, 3 * HD :], Z0)], axis=0)
+
+    first = project(jnp.concatenate([own, beside, far_late, far_beside_late], axis=0))
+    second = project(
+        jnp.concatenate([far_early, far_beside_early], axis=0) + zero_after(codes)
+    )
 
     first_rows = [(0, 0, tok_rows), (Y, 0, tok_rows), (Z1, part, part), (Z1 | Y, part, part)]
     second_rows = [(Z1, 0, part), (Z1 | Y, 0, part)]
     order = []
     for pieces in (first_rows, second_rows):
         order += pieces + [(far ^ Z0, start, count) for far, start, count in pieces]
-
-    span = devices * tok_rows
-    times = me * tok_rows + jnp.arange(tok_rows, dtype=jnp.int32)
-    codes = (track_groups(track_ids, track_owner) * span + times)[None, :]
-    codes = after(codes, raw)
-    for bit in (CORE, Y, Z0, Z1):
-        codes = jnp.concatenate([codes, xor_swap(codes, bit)], axis=0)
 
     def codes_at(bit):
         return jnp.concatenate(

time: 101 us -> 97.4 us (0.964)
  waiting for transfers between devices: 34.1 us -> 29.5 us
  between operations: 0.63 us -> 3.99 us
  other arithmetic: 5.4 us -> 4.02 us
  local copies, waits for them, and re-layouts: 9.57 us -> 8.31 us
    ppermute x18 -> x19, waiting for transfers between devices: 34 us -> 29.5 us  [xor_swap(): return lax.ppermute(value, axes, [(d, d ^ bit) for d in range(count)])]
    unnamed x20 -> x21, local copies, waits for them, and re-layouts: 6.07 us -> 3.72 us
    slice x0 -> x5, local copies, waits for them, and re-layouts: none -> 1.78 us  [the longest x3 1.75 us: zero_after(): last = array[(-1,) * array.ndim]]
    another operation x5, other arithmetic: 2.03 us -> 0.62 us  [by_bit(): jnp.stack([jnp.where(bit == 0, mine, theirs), jnp.where(bit == 0, theirs,...]
    ppermute x18 -> x19, starting transfers between devices: 19.5 us -> 19.9 us  [xor_swap(): return lax.ppermute(value, axes, [(d, d ^ bit) for d in range(count)])]
  transfers between devices with their start and end apart: 22 -> 23, of which waited for: 9 -> 9; matrix products, arithmetic and copies ran while one was open for 13% -> 10% of each run, Pallas kernels for 0% -> 0%
where the time goes in v10:
time: 97.4 us; the launch traced here: 97 us
  starting transfers between devices  31.5 us (32%)
  waiting for transfers between devices  29.5 us (30%)
  blocking collectives  12.1 us (12%)
  local copies, waits for them, and re-layouts  8.31 us (9%)
  matrix products  7.51 us (8%)
  other arithmetic  4.02 us (4%)
  between operations  3.99 us (4%)
    ppermute x19, waiting for transfers between devices, xor_swap(): return lax.ppermute(value, axes, [(d, d ^ bit) for d in range(count)])  29.5 us
    ppermute x19, starting transfers between devices, xor_swap(): return lax.ppermute(value, axes, [(d, d ^ bit) for d in range(count)])  19.9 us
    all_to_all x1, blocking collectives, body_by_head(): lax.all_to_all(sent, 'chip', split_axis=0, concat_axis=0, tiled=True)  12.1 us
    ppermute x3, starting transfers between devices, body_by_head(): lax.ppermute(held[j], both, [(d, (3 * d + j) % devices) for d in range(de...  8.43 us
    unnamed x21, local copies, waits for them, and re-layouts  3.72 us
    dot_general x2, matrix products, project(): lax.dot_general(rows, two_heads, (((1,), (1,)), ((), ())), preferred_elem...  3.64 us
    ppermute x1, starting transfers between devices, body_by_head(): lax.ppermute(frames[tok_rows - (KW - 1):], both, [(i, i + 1) for i in ran...  3.2 us
    dot_general x1, matrix products, body_by_head(): lax.dot_general(query, keyed[:, :HD], (((1,), (1,)), ((), ())), preferred...  2.28 us
  transfers between devices with their start and end apart: 23, of which 9 were waited for; matrix products, arithmetic and copies ran while one was open for 10% of the time, Pallas kernels for 0%

profile of v10, /device:TPU:0, one launch (start us, length us, event | category | flops | bytes accessed | tf_op | source)
XLA Modules:
  0.0 97.0 jit_solution(17421528368623099362)
XLA Ops:
  1.9 3.8 %collective-permute-start.1 = (bf16[64,1024]{1,0:T(8,128)(2,1)S(1)}, bf16[64,1024]{1,0:T(8,128)(2,1)S(1)}, u32[]{:S(2)}, u32[]{:S(2)}) collective-permute-start(bf16[64,1024]{1,0:T(8,128)(2,1)S(1)} %get-tuple-element.20), channel_id=1, source_target_pairs={{0,1},{1,4},{2,7},{3,10},{4,13},{5,0},{6,3},{7,6},{8,9},{9,12},{10... | collective-permute-start | bytes 393224 | tf_op jit(solution)/shard_map/ppermute | solution.py:153
  5.7 3.9 %collective-permute-start.2 = (bf16[64,1024]{1,0:T(8,128)(2,1)S(1)}, bf16[64,1024]{1,0:T(8,128)(2,1)S(1)}, u32[]{:S(2)}, u32[]{:S(2)}) collective-permute-start(bf16[64,1024]{1,0:T(8,128)(2,1)S(1)} %get-tuple-element.19), channel_id=1, source_target_pairs={{0,2},{1,5},{2,8},{3,11},{4,14},{5,1},{6,4},{7,7},{8,10},{9,13},{1... | collective-permute-start | bytes 393224 | tf_op jit(solution)/shard_map/ppermute | solution.py:153
  10.5 3.2 %collective-permute-start.9 = (bf16[3,2048]{1,0:T(4,128)(2,1)S(1)}, bf16[3,2048]{1,0:T(4,128)(2,1)S(1)}, u32[]{:S(2)}, u32[]{:S(2)}) collective-permute-start(bf16[3,2048]{1,0:T(4,128)(2,1)S(1)} %slice.239), channel_id=1, source_target_pairs={{0,1},{1,2},{2,3},{3,4},{4,5},{5,6},{6,7},{7,8},{8,9},{9,10},{10,1... | collective-permute-start | bytes 36872 | tf_op jit(solution)/shard_map/ppermute | solution.py:137
  15.6 5.1 %collective-permute-start.11 = (bf16[64,2048]{1,0:T(8,128)(2,1)S(1)}, bf16[64,2048]{1,0:T(8,128)(2,1)S(1)}, u32[]{:S(2)}, u32[]{:S(2)}) collective-permute-start(bf16[64,2048]{1,0:T(8,128)(2,1)S(1)} %get-tuple-element.6), channel_id=1, source_target_pairs={{0,8},{1,9},{2,10},{3,11},{4,12},{5,13},{6,14},{7,15},{8,0},{9,1},... | collective-permute-start | bytes 786440 | tf_op jit(solution)/shard_map/ppermute | solution.py:105
  21.0 1.6 %collective-permute-start.3 = (bf16[3,64,1024]{2,1,0:T(8,128)(2,1)S(1)}, bf16[3,64,1024]{2,1,0:T(8,128)(2,1)S(1)}, u32[]{:S(2)}, u32[]{:S(2)}) collective-permute-start(bf16[3,64,1024]{2,1,0:T(8,128)(2,1)S(1)} %constant_dynamic-slice_fusion), channel_id=1, source_target_pairs={{0,16},{1,17},{2,18},{3,19},{4,20},{5,21},{6,22},{7,23},{8,24},{9,... | collective-permute-start | bytes 1179656 | tf_op jit(solution)/shard_map/ppermute | solution.py:105
  22.6 1.6 %collective-permute-start.14 = (bf16[3,64,1024]{2,1,0:T(8,128)(2,1)S(1)}, bf16[3,64,1024]{2,1,0:T(8,128)(2,1)S(1)}, u32[]{:S(2)}, u32[]{:S(2)}) collective-permute-start(bf16[3,64,1024]{2,1,0:T(8,128)(2,1)S(1)} %constant_dynamic-slice_fusion), channel_id=1, source_target_pairs={{0,4},{1,5},{2,6},{3,7},{4,0},{5,1},{6,2},{7,3},{8,12},{9,13},{10,... | collective-permute-start | bytes 1179656 | tf_op jit(solution)/shard_map/ppermute | solution.py:105
  24.2 7.1 %collective-permute-done.11 = bf16[64,2048]{1,0:T(8,128)(2,1)S(1)} collective-permute-done((bf16[64,2048]{1,0:T(8,128)(2,1)S(1)}, bf16[64,2048]{1,0:T(8,128)(2,1)S(1)}, u32[]{:S(2)}, u32[]{:S(2)}) %collective-permute-start.11) | collective-permute-done | bytes 262176 | tf_op jit(solution)/shard_map/ppermute | solution.py:105
  33.3 2.0 %collective-permute-start.12 = (bf16[64,2048]{1,0:T(8,128)(2,1)S(1)}, bf16[64,2048]{1,0:T(8,128)(2,1)S(1)}, u32[]{:S(2)}, u32[]{:S(2)}) collective-permute-start(bf16[64,2048]{1,0:T(8,128)(2,1)S(1)} %collective-permute-done.11), channel_id=1, source_target_pairs={{0,2},{1,3},{2,0},{3,1},{4,6},{5,7},{6,4},{7,5},{8,10},{9,11},{10,... | collective-permute-start | bytes 786440 | tf_op jit(solution)/shard_map/ppermute | solution.py:105
  35.3 1.9 %collective-permute-start.4 = (bf16[3,64,512]{2,1,0:T(8,128)(2,1)S(1)}, bf16[3,64,512]{2,1,0:T(8,128)(2,1)S(1)}, u32[]{:S(2)}, u32[]{:S(2)}) collective-permute-start(bf16[3,64,512]{2,1,0:T(8,128)(2,1)S(1)} %slice.280), channel_id=1, source_target_pairs={{0,4},{1,5},{2,6},{3,7},{4,0},{5,1},{6,2},{7,3},{8,12},{9,13},{10,... | collective-permute-start | bytes 589832 | tf_op jit(solution)/shard_map/ppermute | solution.py:105
  37.6 1.6 %collective-permute-start.15 = (bf16[3,64,512]{2,1,0:T(8,128)(2,1)S(1)}, bf16[3,64,512]{2,1,0:T(8,128)(2,1)S(1)}, u32[]{:S(2)}, u32[]{:S(2)}) collective-permute-start(bf16[3,64,512]{2,1,0:T(8,128)(2,1)S(1)} %slice.290), channel_id=1, source_target_pairs={{0,16},{1,17},{2,18},{3,19},{4,20},{5,21},{6,22},{7,23},{8,24},{9,... | collective-permute-start | bytes 589832 | tf_op jit(solution)/shard_map/ppermute | solution.py:105
  39.2 7.3 %collective-permute-done.18 = bf16[64,2048]{1,0:T(8,128)(2,1)} collective-permute-done((bf16[64,2048]{1,0:T(8,128)(2,1)S(1)}, bf16[64,2048]{1,0:T(8,128)(2,1)}, u32[]{:S(2)}, u32[]{:S(2)}) %collective-permute-start.18) | collective-permute-done | bytes 262176 | tf_op jit(solution)/shard_map/ppermute | solution.py:105
  52.9 2.6 %collective-permute-done.6 = s32[2,128]{1,0:T(2,128)S(1)} collective-permute-done((s32[2,128]{1,0:T(2,128)S(1)}, s32[2,128]{1,0:T(2,128)S(1)}, u32[]{:S(2)}, u32[]{:S(2)}) %collective-permute-start.6) | collective-permute-done | bytes 1056 | tf_op jit(solution)/shard_map/ppermute | solution.py:105
  55.6 3.6 %collective-permute-done.7 = s32[4,128]{1,0:T(4,128)S(1)} collective-permute-done((s32[4,128]{1,0:T(4,128)S(1)}, s32[4,128]{1,0:T(4,128)S(1)}, u32[]{:S(2)}, u32[]{:S(2)}) %collective-permute-start.7) | collective-permute-done | bytes 2080 | tf_op jit(solution)/shard_map/ppermute | solution.py:105
  60.1 3.7 %collective-permute-done.8 = s32[8,128]{1,0:T(8,128)S(1)} collective-permute-done((s32[8,128]{1,0:T(8,128)S(1)}, s32[8,128]{1,0:T(8,128)S(1)}, u32[]{:S(2)}, u32[]{:S(2)}) %collective-permute-start.8) | collective-permute-done | bytes 4128 | tf_op jit(solution)/shard_map/ppermute | solution.py:105
  65.8 1.3 %copy-done.4 = bf16[384,2048]{1,0:T(8,128)(2,1)S(1)} copy-done((bf16[384,2048]{1,0:T(8,128)(2,1)S(1)}, bf16[384,2048]{1,0:T(8,128)(2,1)}, u32[]{:S(2)}) %copy-start.4) | copy-done | bytes 1572888
  67.1 1.4 %fusion.4 = bf16[384,768]{1,0:T(8,128)(2,1)S(1)} fusion(bf16[384,2048]{1,0:T(8,128)(2,1)S(1)} %copy-done.4, bf16[384,2048]{1,0:T(8,128)(2,1)S(1)} %bitcast.149, bf16[384,2048]{1,0:T(8,128)(2,1)S(1)} %bitcast.147), kind=kOutput, calls=%fused_computation.10 | convolution fusion | flops 1214545920 | bytes 5308416 | tf_op jit(solution)/shard_map/dot_general | solution.py:185
  68.7 2.2 %fusion.6 = bf16[128,768]{1,0:T(8,128)(2,1)S(1)} fusion(bf16[384,2048]{1,0:T(8,128)(2,1)S(1)} %bitcast.150, bf16[384,2048]{1,0:T(8,128)(2,1)S(1)} %bitcast.148, bf16[64,2048]{1,0:T(8,128)(2,1)} %collective-permute-done.19, bf16[64,2048]{1,0:T(8,128)(2,1)} %collective-permute-done.18, bf16[]{:T(256)} %bitcast.45), kind=kOutput, calls=%fused_computation.12 | convolution fusion | flops 410615808 | bytes 3866626 | tf_op jit(solution)/shard_map/dot_general | solution.py:185
  70.9 2.1 %collective-permute-start.20 = (bf16[128,384]{1,0:T(8,128)(2,1)S(1)}, bf16[128,384]{1,0:T(8,128)(2,1)S(1)}, u32[]{:S(2)}, u32[]{:S(2)}) collective-permute-start(bf16[128,384]{1,0:T(8,128)(2,1)S(1)} %get-tuple-element.23), channel_id=1, source_target_pairs={{0,4},{1,5},{2,6},{3,7},{4,0},{5,1},{6,2},{7,3},{8,12},{9,13},{10,... | collective-permute-start | bytes 294920 | tf_op jit(solution)/shard_map/ppermute | solution.py:105
  73.0 2.9 %collective-permute-done.17 = bf16[384,384]{1,0:T(8,128)(2,1)S(1)} collective-permute-done((bf16[384,384]{1,0:T(8,128)(2,1)S(1)}, bf16[384,384]{1,0:T(8,128)(2,1)S(1)}, u32[]{:S(2)}, u32[]{:S(2)}) %collective-permute-start.17) | collective-permute-done | bytes 294944 | tf_op jit(solution)/shard_map/ppermute | solution.py:105
  77.0 1.3 %collective-permute-done.22 = bf16[256,256]{1,0:T(8,128)(2,1)S(1)} collective-permute-done((bf16[256,256]{1,0:T(8,128)(2,1)S(1)}, bf16[256,256]{1,0:T(8,128)(2,1)S(1)}, u32[]{:S(2)}, u32[]{:S(2)}) %collective-permute-start.22) | collective-permute-done | bytes 131104 | tf_op jit(solution)/shard_map/ppermute | solution.py:105
  78.4 2.3 %fusion.55 = (f32[1024]{0:T(1024)S(1)}, f32[1024,2048]{1,0:T(8,128)S(1)}) fusion(bf16[2048,256]{1,0:T(8,128)(2,1)S(1)} %fusion.8, bf16[128,384]{1,0:T(8,128)(2,1)S(1)} %collective-permute-done.20, bf16[128,384]{1,0:T(8,128)(2,1)S(1)} %get-tuple-element.22, bf16[384,384]{1,0:T(8,128)(2,1)S(1)} %collective-permute-done.17, ...), kind=kOutput, calls=%fused_computation.151 | convolution fusion | flops 550501376 | bytes 9719808 | tf_op jit(solution)/shard_map/dot_general | solution.py:214
  80.7 1.3 %fusion = f32[1024]{0:T(1024)S(1)} fusion(f32[1024,2048]{1,0:T(8,128)S(1)} %get-tuple-element.51, f32[1024]{0:T(1024)S(1)} %get-tuple-element.50), kind=kLoop, calls=%fused_computation.3 | loop fusion | flops 4193280 | bytes 8396800 | tf_op jit(solution)/shard_map/reduce_sum | solution.py:220
  81.9 1.6 %fusion.5 = bf16[1024,128]{1,0:T(8,128)(2,1)S(1)} fusion(f32[1024,2048]{1,0:T(8,128)S(1)} %get-tuple-element.51, f32[1024]{0:T(1024)S(1)} %fusion, f32[1024]{0:T(1024)S(1)} %get-tuple-element.50, bf16[2048,256]{1,0:T(8,128)(2,1)S(1)} %fusion.8), kind=kOutput, calls=%fused_computation.11 | convolution fusion | flops 543293440 | bytes 9183232 | tf_op jit(solution)/shard_map/dot_general | solution.py:221
  83.8 12.1 %all_to_all.5 = bf16[8,128,128]{2,1,0:T(8,128)(2,1)S(1)} all-to-all(bf16[8,128,128]{2,1,0:T(8,128)(2,1)S(1)} %fusion.35), channel_id=1, replica_groups=mesh['grp'=2,'chip'=8,'core'=2] {'chip'}, dimensions={0} | all-to-all | bytes 524288 | tf_op jit(solution)/shard_map/all_to_all | solution.py:230
  (113 shorter events, 15.5 us)
Async XLA Ops:
  0.0 15.0 %copy-start.1 = (bf16[128,2048]{1,0:T(8,128)(2,1)S(1)}, bf16[128,2048]{1,0:T(8,128)(2,1)}, u32[]{:S(2)}) copy-start(bf16[128,2048]{1,0:T(8,128)(2,1)} %param.5) | copy-start | bytes 1572868
  1.3 19.6 %collective-permute-start = (bf16[64,1024]{1,0:T(8,128)(2,1)S(1)}, bf16[64,1024]{1,0:T(8,128)(2,1)S(1)}, u32[]{:S(2)}, u32[]{:S(2)}) collective-permute-start(bf16[64,1024]{1,0:T(8,128)(2,1)S(1)} %get-tuple-element.21), channel_id=1, source_target_pairs={{0,0},{1,3},{2,6},{3,9},{4,12},{5,15},{6,2},{7,5},{8,8},{9,11},{10... | collective-permute-start | bytes 393224 | tf_op jit(solution)/shard_map/ppermute | solution.py:153
  1.9 18.9 %collective-permute-start.1 = (bf16[64,1024]{1,0:T(8,128)(2,1)S(1)}, bf16[64,1024]{1,0:T(8,128)(2,1)S(1)}, u32[]{:S(2)}, u32[]{:S(2)}) collective-permute-start(bf16[64,1024]{1,0:T(8,128)(2,1)S(1)} %get-tuple-element.20), channel_id=1, source_target_pairs={{0,1},{1,4},{2,7},{3,10},{4,13},{5,0},{6,3},{7,6},{8,9},{9,12},{10... | collective-permute-start | bytes 393224 | tf_op jit(solution)/shard_map/ppermute | solution.py:153
  5.7 15.2 %collective-permute-start.2 = (bf16[64,1024]{1,0:T(8,128)(2,1)S(1)}, bf16[64,1024]{1,0:T(8,128)(2,1)S(1)}, u32[]{:S(2)}, u32[]{:S(2)}) collective-permute-start(bf16[64,1024]{1,0:T(8,128)(2,1)S(1)} %get-tuple-element.19), channel_id=1, source_target_pairs={{0,2},{1,5},{2,8},{3,11},{4,14},{5,1},{6,4},{7,7},{8,10},{9,13},{1... | collective-permute-start | bytes 393224 | tf_op jit(solution)/shard_map/ppermute | solution.py:153
  10.5 4.5 %collective-permute-start.9 = (bf16[3,2048]{1,0:T(4,128)(2,1)S(1)}, bf16[3,2048]{1,0:T(4,128)(2,1)S(1)}, u32[]{:S(2)}, u32[]{:S(2)}) collective-permute-start(bf16[3,2048]{1,0:T(4,128)(2,1)S(1)} %slice.239), channel_id=1, source_target_pairs={{0,1},{1,2},{2,3},{3,4},{4,5},{5,6},{6,7},{7,8},{8,9},{9,10},{10,1... | collective-permute-start | bytes 36872 | tf_op jit(solution)/shard_map/ppermute | solution.py:137
  15.6 15.7 %collective-permute-start.11 = (bf16[64,2048]{1,0:T(8,128)(2,1)S(1)}, bf16[64,2048]{1,0:T(8,128)(2,1)S(1)}, u32[]{:S(2)}, u32[]{:S(2)}) collective-permute-start(bf16[64,2048]{1,0:T(8,128)(2,1)S(1)} %get-tuple-element.6), channel_id=1, source_target_pairs={{0,8},{1,9},{2,10},{3,11},{4,12},{5,13},{6,14},{7,15},{8,0},{9,1},... | collective-permute-start | bytes 786440 | tf_op jit(solution)/shard_map/ppermute | solution.py:105
  20.8 16.9 %collective-permute-start.10 = (bf16[128,2048]{1,0:T(8,128)(2,1)S(1)}, bf16[128,2048]{1,0:T(8,128)(2,1)S(1)}, u32[]{:S(2)}, u32[]{:S(2)}) collective-permute-start(bf16[128,2048]{1,0:T(8,128)(2,1)S(1)} %pad_maximum_fusion.12), channel_id=1, source_target_pairs={{0,2},{1,3},{2,0},{3,1},{4,6},{5,7},{6,4},{7,5},{8,10},{9,11},{10,... | collective-permute-start | bytes 1572872 | tf_op jit(solution)/shard_map/ppermute | solution.py:105
  21.0 14.3 %collective-permute-start.3 = (bf16[3,64,1024]{2,1,0:T(8,128)(2,1)S(1)}, bf16[3,64,1024]{2,1,0:T(8,128)(2,1)S(1)}, u32[]{:S(2)}, u32[]{:S(2)}) collective-permute-start(bf16[3,64,1024]{2,1,0:T(8,128)(2,1)S(1)} %constant_dynamic-slice_fusion), channel_id=1, source_target_pairs={{0,16},{1,17},{2,18},{3,19},{4,20},{5,21},{6,22},{7,23},{8,24},{9,... | collective-permute-start | bytes 1179656 | tf_op jit(solution)/shard_map/ppermute | solution.py:105
  22.6 14.9 %collective-permute-start.14 = (bf16[3,64,1024]{2,1,0:T(8,128)(2,1)S(1)}, bf16[3,64,1024]{2,1,0:T(8,128)(2,1)S(1)}, u32[]{:S(2)}, u32[]{:S(2)}) collective-permute-start(bf16[3,64,1024]{2,1,0:T(8,128)(2,1)S(1)} %constant_dynamic-slice_fusion), channel_id=1, source_target_pairs={{0,4},{1,5},{2,6},{3,7},{4,0},{5,1},{6,2},{7,3},{8,12},{9,13},{10,... | collective-permute-start | bytes 1179656 | tf_op jit(solution)/shard_map/ppermute | solution.py:105
  33.2 13.2 %collective-permute-start.18 = (bf16[64,2048]{1,0:T(8,128)(2,1)S(1)}, bf16[64,2048]{1,0:T(8,128)(2,1)}, u32[]{:S(2)}, u32[]{:S(2)}) collective-permute-start(bf16[64,2048]{1,0:T(8,128)(2,1)S(1)} %broadcast_add_fusion), channel_id=1, source_target_pairs={{0,8},{1,9},{2,10},{3,11},{4,12},{5,13},{6,14},{7,15},{8,0},{9,1},... | collective-permute-start | bytes 786440 | tf_op jit(solution)/shard_map/ppermute | solution.py:105
  33.3 14.3 %collective-permute-start.12 = (bf16[64,2048]{1,0:T(8,128)(2,1)S(1)}, bf16[64,2048]{1,0:T(8,128)(2,1)S(1)}, u32[]{:S(2)}, u32[]{:S(2)}) collective-permute-start(bf16[64,2048]{1,0:T(8,128)(2,1)S(1)} %collective-permute-done.11), channel_id=1, source_target_pairs={{0,2},{1,3},{2,0},{3,1},{4,6},{5,7},{6,4},{7,5},{8,10},{9,11},{10,... | collective-permute-start | bytes 786440 | tf_op jit(solution)/shard_map/ppermute | solution.py:105
  35.3 12.3 %collective-permute-start.4 = (bf16[3,64,512]{2,1,0:T(8,128)(2,1)S(1)}, bf16[3,64,512]{2,1,0:T(8,128)(2,1)S(1)}, u32[]{:S(2)}, u32[]{:S(2)}) collective-permute-start(bf16[3,64,512]{2,1,0:T(8,128)(2,1)S(1)} %slice.280), channel_id=1, source_target_pairs={{0,4},{1,5},{2,6},{3,7},{4,0},{5,1},{6,2},{7,3},{8,12},{9,13},{10,... | collective-permute-start | bytes 589832 | tf_op jit(solution)/shard_map/ppermute | solution.py:105
  37.5 27.5 %collective-permute-start.13 = (bf16[3,64,2048]{2,1,0:T(8,128)(2,1)S(1)}, bf16[3,64,2048]{2,1,0:T(8,128)(2,1)S(1)}, u32[]{:S(2)}, u32[]{:S(2)}) collective-permute-start(bf16[3,64,2048]{2,1,0:T(8,128)(2,1)S(1)} %bitcast.143), channel_id=1, source_target_pairs={{0,1},{1,0},{2,3},{3,2},{4,5},{5,4},{6,7},{7,6},{8,9},{9,8},{10,11... | collective-permute-start | bytes 2359304 | tf_op jit(solution)/shard_map/ppermute | solution.py:105
  37.6 13.2 %collective-permute-start.15 = (bf16[3,64,512]{2,1,0:T(8,128)(2,1)S(1)}, bf16[3,64,512]{2,1,0:T(8,128)(2,1)S(1)}, u32[]{:S(2)}, u32[]{:S(2)}) collective-permute-start(bf16[3,64,512]{2,1,0:T(8,128)(2,1)S(1)} %slice.290), channel_id=1, source_target_pairs={{0,16},{1,17},{2,18},{3,19},{4,20},{5,21},{6,22},{7,23},{8,24},{9,... | collective-permute-start | bytes 589832 | tf_op jit(solution)/shard_map/ppermute | solution.py:105
  46.5 22.2 %collective-permute-start.19 = (bf16[64,2048]{1,0:T(8,128)(2,1)}, bf16[64,2048]{1,0:T(8,128)(2,1)}, u32[]{:S(2)}, u32[]{:S(2)}) collective-permute-start(bf16[64,2048]{1,0:T(8,128)(2,1)} %collective-permute-done.18), channel_id=1, source_target_pairs={{0,2},{1,3},{2,0},{3,1},{4,6},{5,7},{6,4},{7,5},{8,10},{9,11},{10,... | collective-permute-start | bytes 786440 | tf_op jit(solution)/shard_map/ppermute | solution.py:105
  50.7 1.2 %collective-permute-start.5 = (s32[1,128]{1,0:T(1,128)S(1)}, s32[1,128]{1,0:T(1,128)S(1)}, u32[]{:S(2)}, u32[]{:S(2)}) collective-permute-start(s32[1,128]{1,0:T(1,128)S(1)} %fusion.46), channel_id=1, source_target_pairs={{0,1},{1,0},{2,3},{3,2},{4,5},{5,4},{6,7},{7,6},{8,9},{9,8},{10,11... | collective-permute-start | bytes 1544 | tf_op jit(solution)/shard_map/ppermute | solution.py:105
  51.1 13.9 %collective-permute-start.16 = (bf16[3,64,2048]{2,1,0:T(8,128)(2,1)S(1)}, bf16[3,64,2048]{2,1,0:T(8,128)(2,1)S(1)}, u32[]{:S(2)}, u32[]{:S(2)}) collective-permute-start(bf16[3,64,2048]{2,1,0:T(8,128)(2,1)S(1)} %bitcast.145), channel_id=1, source_target_pairs={{0,1},{1,0},{2,3},{3,2},{4,5},{5,4},{6,7},{7,6},{8,9},{9,8},{10,11... | collective-permute-start | bytes 2359304 | tf_op jit(solution)/shard_map/ppermute | solution.py:105
  51.9 3.6 %collective-permute-start.6 = (s32[2,128]{1,0:T(2,128)S(1)}, s32[2,128]{1,0:T(2,128)S(1)}, u32[]{:S(2)}, u32[]{:S(2)}) collective-permute-start(s32[2,128]{1,0:T(2,128)S(1)} %pad_add_fusion.2), channel_id=1, source_target_pairs={{0,2},{1,3},{2,0},{3,1},{4,6},{5,7},{6,4},{7,5},{8,10},{9,11},{10,... | collective-permute-start | bytes 3080 | tf_op jit(solution)/shard_map/ppermute | solution.py:105
  55.5 3.6 %collective-permute-start.7 = (s32[4,128]{1,0:T(4,128)S(1)}, s32[4,128]{1,0:T(4,128)S(1)}, u32[]{:S(2)}, u32[]{:S(2)}) collective-permute-start(s32[4,128]{1,0:T(4,128)S(1)} %pad_add_fusion.1), channel_id=1, source_target_pairs={{0,4},{1,5},{2,6},{3,7},{4,0},{5,1},{6,2},{7,3},{8,12},{9,13},{10,... | collective-permute-start | bytes 6152 | tf_op jit(solution)/shard_map/ppermute | solution.py:105
  59.2 4.6 %collective-permute-start.8 = (s32[8,128]{1,0:T(8,128)S(1)}, s32[8,128]{1,0:T(8,128)S(1)}, u32[]{:S(2)}, u32[]{:S(2)}) collective-permute-start(s32[8,128]{1,0:T(8,128)S(1)} %pad_add_fusion), channel_id=1, source_target_pairs={{0,8},{1,9},{2,10},{3,11},{4,12},{5,13},{6,14},{7,15},{8,0},{9,1},... | collective-permute-start | bytes 12296 | tf_op jit(solution)/shard_map/ppermute | solution.py:105
  68.6 7.3 %collective-permute-start.17 = (bf16[384,384]{1,0:T(8,128)(2,1)S(1)}, bf16[384,384]{1,0:T(8,128)(2,1)S(1)}, u32[]{:S(2)}, u32[]{:S(2)}) collective-permute-start(bf16[384,384]{1,0:T(8,128)(2,1)S(1)} %get-tuple-element.18), channel_id=1, source_target_pairs={{0,4},{1,5},{2,6},{3,7},{4,0},{5,1},{6,2},{7,3},{8,12},{9,13},{10,... | collective-permute-start | bytes 884744 | tf_op jit(solution)/shard_map/ppermute | solution.py:105
  70.9 6.0 %collective-permute-start.20 = (bf16[128,384]{1,0:T(8,128)(2,1)S(1)}, bf16[128,384]{1,0:T(8,128)(2,1)S(1)}, u32[]{:S(2)}, u32[]{:S(2)}) collective-permute-start(bf16[128,384]{1,0:T(8,128)(2,1)S(1)} %get-tuple-element.23), channel_id=1, source_target_pairs={{0,4},{1,5},{2,6},{3,7},{4,0},{5,1},{6,2},{7,3},{8,12},{9,13},{10,... | collective-permute-start | bytes 294920 | tf_op jit(solution)/shard_map/ppermute | solution.py:105
  75.9 2.5 %collective-permute-start.21 = (bf16[768,256]{1,0:T(8,128)(2,1)S(1)}, bf16[768,256]{1,0:T(8,128)(2,1)S(1)}, u32[]{:S(2)}, u32[]{:S(2)}) collective-permute-start(bf16[768,256]{1,0:T(8,128)(2,1)S(1)} %pad_maximum_fusion.13), channel_id=1, source_target_pairs={{0,1},{1,0},{2,3},{3,2},{4,5},{5,4},{6,7},{7,6},{8,9},{9,8},{10,11... | collective-permute-start | bytes 1179656 | tf_op jit(solution)/shard_map/ppermute | solution.py:105
  76.9 1.4 %collective-permute-start.22 = (bf16[256,256]{1,0:T(8,128)(2,1)S(1)}, bf16[256,256]{1,0:T(8,128)(2,1)S(1)}, u32[]{:S(2)}, u32[]{:S(2)}) collective-permute-start(bf16[256,256]{1,0:T(8,128)(2,1)S(1)} %pad_maximum_fusion.14), channel_id=1, source_target_pairs={{0,1},{1,0},{2,3},{3,2},{4,5},{5,4},{6,7},{7,6},{8,9},{9,8},{10,11... | collective-permute-start | bytes 393224 | tf_op jit(solution)/shard_map/ppermute | solution.py:105
  (7 other events, 62.9 us)

commit v11 on v10

--- a/solution.py
+++ b/solution.py
@@ -145,8 +145,6 @@
     own = jnp.concatenate([early, late], axis=0)
     beside = xor_swap(own, Y)
     far_beside_late = xor_swap(far_late, Y)
-    far_beside_early = xor_swap(far_early, Y)
-
     half = features // 2
     held = lax.dynamic_slice_in_dim(qkv_weight.T, grp * half, half, 1).reshape(3, HD // 2, half)
     moved = [
@@ -157,6 +155,16 @@
     mine_too = xor_swap(mine, devices, every)
     paired = xor_swap(mine, Z0)
 
+    span = devices * tok_rows
+    times = me * tok_rows + jnp.arange(tok_rows, dtype=jnp.int32)
+    codes = (track_groups(track_ids, track_owner) * span + times)[None, :]
+    codes = codes + zero_after(mine_too, paired).astype(jnp.int32)
+    for bit in (CORE, Y, Z0, Z1):
+        codes = jnp.concatenate([codes, xor_swap(codes, bit)], axis=0)
+        if bit == Y:
+            codes = codes + zero_after(far_beside_late).astype(jnp.int32)
+    far_beside_early = xor_swap(far_early + zero_after(codes), Y)
+
     cut = half // 2
     fourth = jnp.concatenate(
         [
@@ -166,13 +174,6 @@
         axis=2,
     )
 
-    span = devices * tok_rows
-    times = me * tok_rows + jnp.arange(tok_rows, dtype=jnp.int32)
-    codes = (track_groups(track_ids, track_owner) * span + times)[None, :]
-    codes = codes + zero_after(fourth).astype(jnp.int32)
-    for bit in (CORE, Y, Z0, Z1):
-        codes = jnp.concatenate([codes, xor_swap(codes, bit)], axis=0)
-
     def whole_head(quarter, quarter_too):
         wide = by_bit(grp, quarter, quarter_too, 2).reshape(3, HD // 2, features)
         return by_bit(core, wide, xor_swap(wide, CORE), 1).reshape(3 * HD, features)
@@ -188,9 +189,7 @@
         return jnp.concatenate([done[:, : 3 * HD], xor_swap(done[:, 3 * HD :], Z0)], axis=0)
 
     first = project(jnp.concatenate([own, beside, far_late, far_beside_late], axis=0))
-    second = project(
-        jnp.concatenate([far_early, far_beside_early], axis=0) + zero_after(codes)
-    )
+    second = project(jnp.concatenate([far_early, far_beside_early], axis=0))
 
     first_rows = [(0, 0, tok_rows), (Y, 0, tok_rows), (Z1, part, part), (Z1 | Y, part, part)]
     second_rows = [(Z1, 0, part), (Z1 | Y, 0, part)]

time: 97.4 us -> 99.1 us (1.017)
  waiting for transfers between devices: 29.5 us -> 15.6 us
  local copies, waits for them, and re-layouts: 8.31 us -> 16.4 us
  starting transfers between devices: 31.5 us -> 34.6 us
  between operations: 3.99 us -> 6.76 us
  other arithmetic: 4.02 us -> 5.55 us
    ppermute x19, waiting for transfers between devices: 29.5 us -> 15.6 us  [xor_swap(): return lax.ppermute(value, axes, [(d, d ^ bit) for d in range(count)])]
    ppermute x19, starting transfers between devices: 19.9 us -> 23 us  [xor_swap(): return lax.ppermute(value, axes, [(d, d ^ bit) for d in range(count)])]
    slice x3 -> x5, local copies, waits for them, and re-layouts: 1.75 us -> 4.52 us  [zero_after(): last = array[(-1,) * array.ndim]]
    unnamed x21, local copies, waits for them, and re-layouts: 3.72 us -> 6.08 us
    concatenate x1, local copies, waits for them, and re-layouts: 0.02 us -> 1.67 us  [body_by_head(): jnp.concatenate([own, beside, far_late, far_beside_late], axis=0)]
    dot_general x2, matrix products: 3.64 us -> 2.64 us  [project(): lax.dot_general(rows, two_heads, (((1,), (1,)), ((), ())), preferred_elem...]
  transfers between devices with their start and end apart: 23 -> 23, of which waited for: 9 -> 8; matrix products, arithmetic and copies ran while one was open for 10% -> 20% of each run, Pallas kernels for 0% -> 0%
where the time goes in v11:
time: 99.1 us; the launch traced here: 98.5 us
  starting transfers between devices  34.6 us (35%)
  local copies, waits for them, and re-layouts  16.4 us (17%)
  waiting for transfers between devices  15.6 us (16%)
  blocking collectives  12.9 us (13%)
  between operations  6.76 us (7%)
  matrix products  6.52 us (7%)
  other arithmetic  5.55 us (6%)
    ppermute x19, starting transfers between devices, xor_swap(): return lax.ppermute(value, axes, [(d, d ^ bit) for d in range(count)])  23 us
    ppermute x19, waiting for transfers between devices, xor_swap(): return lax.ppermute(value, axes, [(d, d ^ bit) for d in range(count)])  15.6 us
    all_to_all x1, blocking collectives, body_by_head(): lax.all_to_all(sent, 'chip', split_axis=0, concat_axis=0, tiled=True)  12.9 us
    ppermute x3, starting transfers between devices, body_by_head(): lax.ppermute(held[j], both, [(d, (3 * d + j) % devices) for d in range(de...  8.43 us
    unnamed x21, local copies, waits for them, and re-layouts  6.08 us
    slice x5, local copies, waits for them, and re-layouts, zero_after(): last = array[(-1,) * array.ndim]  4.52 us
    ppermute x1, starting transfers between devices, body_by_head(): lax.ppermute(frames[tok_rows - (KW - 1):], both, [(i, i + 1) for i in ran...  3.2 us
    dot_general x2, matrix products, project(): lax.dot_general(rows, two_heads, (((1,), (1,)), ((), ())), preferred_elem...  2.64 us
  transfers between devices with their start and end apart: 23, of which 8 were waited for; matrix products, arithmetic and copies ran while one was open for 20% of the time, Pallas kernels for 0%

profile of v11, /device:TPU:0, one launch (start us, length us, event | category | flops | bytes accessed | tf_op | source)
XLA Modules:
  0.0 98.5 jit_solution(2172545245435084526)
XLA Ops:
  1.9 3.8 %collective-permute-start.1 = (bf16[64,1024]{1,0:T(8,128)(2,1)S(1)}, bf16[64,1024]{1,0:T(8,128)(2,1)S(1)}, u32[]{:S(2)}, u32[]{:S(2)}) collective-permute-start(bf16[64,1024]{1,0:T(8,128)(2,1)S(1)} %get-tuple-element.20), channel_id=1, source_target_pairs={{0,1},{1,4},{2,7},{3,10},{4,13},{5,0},{6,3},{7,6},{8,9},{9,12},{10... | collective-permute-start | bytes 393224 | tf_op jit(solution)/shard_map/ppermute | solution.py:151
  5.7 3.9 %collective-permute-start.2 = (bf16[64,1024]{1,0:T(8,128)(2,1)S(1)}, bf16[64,1024]{1,0:T(8,128)(2,1)S(1)}, u32[]{:S(2)}, u32[]{:S(2)}) collective-permute-start(bf16[64,1024]{1,0:T(8,128)(2,1)S(1)} %get-tuple-element.19), channel_id=1, source_target_pairs={{0,2},{1,5},{2,8},{3,11},{4,14},{5,1},{6,4},{7,7},{8,10},{9,13},{1... | collective-permute-start | bytes 393224 | tf_op jit(solution)/shard_map/ppermute | solution.py:151
  10.5 3.2 %collective-permute-start.11 = (bf16[3,2048]{1,0:T(4,128)(2,1)S(1)}, bf16[3,2048]{1,0:T(4,128)(2,1)S(1)}, u32[]{:S(2)}, u32[]{:S(2)}) collective-permute-start(bf16[3,2048]{1,0:T(4,128)(2,1)S(1)} %slice.262), channel_id=1, source_target_pairs={{0,1},{1,2},{2,3},{3,4},{4,5},{5,6},{6,7},{7,8},{8,9},{9,10},{10,1... | collective-permute-start | bytes 36872 | tf_op jit(solution)/shard_map/ppermute | solution.py:137
  15.6 5.1 %collective-permute-start.7 = (bf16[64,2048]{1,0:T(8,128)(2,1)S(1)}, bf16[64,2048]{1,0:T(8,128)(2,1)}, u32[]{:S(2)}, u32[]{:S(2)}) collective-permute-start(bf16[64,2048]{1,0:T(8,128)(2,1)S(1)} %get-tuple-element.6), channel_id=1, source_target_pairs={{0,8},{1,9},{2,10},{3,11},{4,12},{5,13},{6,14},{7,15},{8,0},{9,1},... | collective-permute-start | bytes 786440 | tf_op jit(solution)/shard_map/ppermute | solution.py:105
  21.7 1.6 %collective-permute-start.3 = (bf16[3,64,1024]{2,1,0:T(8,128)(2,1)S(1)}, bf16[3,64,1024]{2,1,0:T(8,128)(2,1)S(1)}, u32[]{:S(2)}, u32[]{:S(2)}) collective-permute-start(bf16[3,64,1024]{2,1,0:T(8,128)(2,1)S(1)} %constant_dynamic-slice_fusion), channel_id=1, source_target_pairs={{0,16},{1,17},{2,18},{3,19},{4,20},{5,21},{6,22},{7,23},{8,24},{9,... | collective-permute-start | bytes 1179656 | tf_op jit(solution)/shard_map/ppermute | solution.py:105
  23.3 1.6 %collective-permute-start.4 = (bf16[3,64,1024]{2,1,0:T(8,128)(2,1)S(1)}, bf16[3,64,1024]{2,1,0:T(8,128)(2,1)S(1)}, u32[]{:S(2)}, u32[]{:S(2)}) collective-permute-start(bf16[3,64,1024]{2,1,0:T(8,128)(2,1)S(1)} %constant_dynamic-slice_fusion), channel_id=1, source_target_pairs={{0,4},{1,5},{2,6},{3,7},{4,0},{5,1},{6,2},{7,3},{8,12},{9,13},{10,... | collective-permute-start | bytes 1179656 | tf_op jit(solution)/shard_map/ppermute | solution.py:105
  24.9 6.5 %collective-permute-done.7 = bf16[64,2048]{1,0:T(8,128)(2,1)} collective-permute-done((bf16[64,2048]{1,0:T(8,128)(2,1)S(1)}, bf16[64,2048]{1,0:T(8,128)(2,1)}, u32[]{:S(2)}, u32[]{:S(2)}) %collective-permute-start.7) | collective-permute-done | bytes 262176 | tf_op jit(solution)/shard_map/ppermute | solution.py:105
  34.7 1.9 %collective-permute-start.8 = (bf16[64,2048]{1,0:T(8,128)(2,1)}, bf16[64,2048]{1,0:T(8,128)(2,1)}, u32[]{:S(2)}, u32[]{:S(2)}) collective-permute-start(bf16[64,2048]{1,0:T(8,128)(2,1)} %collective-permute-done.7), channel_id=1, source_target_pairs={{0,2},{1,3},{2,0},{3,1},{4,6},{5,7},{6,4},{7,5},{8,10},{9,11},{10,... | collective-permute-start | bytes 786440 | tf_op jit(solution)/shard_map/ppermute | solution.py:105
  43.9 1.4 %collective-permute-start.14 = (bf16[3,64,512]{2,1,0:T(8,128)(2,1)}, bf16[3,64,512]{2,1,0:T(8,128)(2,1)S(1)}, u32[]{:S(2)}, u32[]{:S(2)}) collective-permute-start(bf16[3,64,512]{2,1,0:T(8,128)(2,1)} %slice.307), channel_id=1, source_target_pairs={{0,16},{1,17},{2,18},{3,19},{4,20},{5,21},{6,22},{7,23},{8,24},{9,... | collective-permute-start | bytes 589832 | tf_op jit(solution)/shard_map/ppermute | solution.py:105
  45.3 1.3 %slice.302 = bf16[1,1]{1,0:T(2,128)(2,1)} slice(bf16[64,2048]{1,0:T(8,128)(2,1)} %collective-permute-done.8), slice={[63:64], [2047:2048]} | slice | bytes 4 | tf_op jit(solution)/shard_map/slice | solution.py:117
  48.1 2.0 %collective-permute-start.15 = (bf16[3,64,512]{2,1,0:T(8,128)(2,1)}, bf16[3,64,512]{2,1,0:T(8,128)(2,1)S(1)}, u32[]{:S(2)}, u32[]{:S(2)}) collective-permute-start(bf16[3,64,512]{2,1,0:T(8,128)(2,1)} %slice.308), channel_id=1, source_target_pairs={{0,4},{1,5},{2,6},{3,7},{4,0},{5,1},{6,2},{7,3},{8,12},{9,13},{10,... | collective-permute-start | bytes 589832 | tf_op jit(solution)/shard_map/ppermute | solution.py:105
  50.3 1.9 %constant_dynamic-update-slice_fusion.2 = bf16[384,2048]{1,0:T(8,128)(2,1)} fusion(bf16[384,2048]{1,0:T(8,128)(2,1)} %copy-done.3, bf16[128,2048]{1,0:T(8,128)(2,1)} %collective-permute-done.12), kind=kLoop, calls=%fused_computation.83 | loop fusion | bytes 1048576
  52.2 1.7 %constant_dynamic-update-slice_fusion.1 = bf16[384,2048]{1,0:T(8,128)(2,1)} fusion(bf16[384,2048]{1,0:T(8,128)(2,1)} %constant_dynamic-update-slice_fusion.2, bf16[64,2048]{1,0:T(8,128)(2,1)} %collective-permute-done.7), kind=kLoop, calls=%fused_computation.82 | loop fusion | bytes 524288
  53.8 1.7 %constant_dynamic-update-slice_fusion = bf16[384,2048]{1,0:T(8,128)(2,1)} fusion(bf16[384,2048]{1,0:T(8,128)(2,1)} %constant_dynamic-update-slice_fusion.1, bf16[64,2048]{1,0:T(8,128)(2,1)} %collective-permute-done.8), kind=kLoop, calls=%fused_computation.81 | loop fusion | bytes 524288 | tf_op jit(solution)/shard_map/concatenate | solution.py:191
  55.9 2.9 %collective-permute-start.10 = (s32[8,128]{1,0:T(8,128)S(1)}, s32[8,128]{1,0:T(8,128)S(1)}, u32[]{:S(2)}, u32[]{:S(2)}) collective-permute-start(s32[8,128]{1,0:T(8,128)S(1)} %pad_add_fusion), channel_id=1, source_target_pairs={{0,8},{1,9},{2,10},{3,11},{4,12},{5,13},{6,14},{7,15},{8,0},{9,1},... | collective-permute-start | bytes 12296 | tf_op jit(solution)/shard_map/ppermute | solution.py:105
  58.9 1.6 %collective-permute-done.10 = s32[8,128]{1,0:T(8,128)S(1)} collective-permute-done((s32[8,128]{1,0:T(8,128)S(1)}, s32[8,128]{1,0:T(8,128)S(1)}, u32[]{:S(2)}, u32[]{:S(2)}) %collective-permute-start.10) | collective-permute-done | bytes 4128 | tf_op jit(solution)/shard_map/ppermute | solution.py:105
  61.8 1.9 %collective-permute-start.19 = (bf16[64,2048]{1,0:T(8,128)(2,1)S(1)}, bf16[64,2048]{1,0:T(8,128)(2,1)S(1)}, u32[]{:S(2)}, u32[]{:S(2)}) collective-permute-start(bf16[64,2048]{1,0:T(8,128)(2,1)S(1)} %broadcast_add_fusion), channel_id=1, source_target_pairs={{0,2},{1,3},{2,0},{3,1},{4,6},{5,7},{6,4},{7,5},{8,10},{9,11},{10,... | collective-permute-start | bytes 786440 | tf_op jit(solution)/shard_map/ppermute | solution.py:105
  65.8 1.4 %fusion.4 = bf16[384,768]{1,0:T(8,128)(2,1)S(1)} fusion(bf16[384,2048]{1,0:T(8,128)(2,1)S(1)} %copy-done.4, bf16[384,2048]{1,0:T(8,128)(2,1)S(1)} %bitcast.154, bf16[384,2048]{1,0:T(8,128)(2,1)S(1)} %bitcast.152), kind=kOutput, calls=%fused_computation.10 | convolution fusion | flops 1214545920 | bytes 5308416 | tf_op jit(solution)/shard_map/dot_general | solution.py:186
  67.3 1.9 %collective-permute-start.17 = (bf16[384,384]{1,0:T(8,128)(2,1)S(1)}, bf16[384,384]{1,0:T(8,128)(2,1)S(1)}, u32[]{:S(2)}, u32[]{:S(2)}) collective-permute-start(bf16[384,384]{1,0:T(8,128)(2,1)S(1)} %get-tuple-element.18), channel_id=1, source_target_pairs={{0,4},{1,5},{2,6},{3,7},{4,0},{5,1},{6,2},{7,3},{8,12},{9,13},{10,... | collective-permute-start | bytes 884744 | tf_op jit(solution)/shard_map/ppermute | solution.py:105
  70.9 1.7 %collective-permute-start.20 = (bf16[128,384]{1,0:T(8,128)(2,1)S(1)}, bf16[128,384]{1,0:T(8,128)(2,1)S(1)}, u32[]{:S(2)}, u32[]{:S(2)}) collective-permute-start(bf16[128,384]{1,0:T(8,128)(2,1)S(1)} %get-tuple-element.23), channel_id=1, source_target_pairs={{0,4},{1,5},{2,6},{3,7},{4,0},{5,1},{6,2},{7,3},{8,12},{9,13},{10,... | collective-permute-start | bytes 294920 | tf_op jit(solution)/shard_map/ppermute | solution.py:105
  72.7 3.9 %collective-permute-done.17 = bf16[384,384]{1,0:T(8,128)(2,1)S(1)} collective-permute-done((bf16[384,384]{1,0:T(8,128)(2,1)S(1)}, bf16[384,384]{1,0:T(8,128)(2,1)S(1)}, u32[]{:S(2)}, u32[]{:S(2)}) %collective-permute-start.17) | collective-permute-done | bytes 294944 | tf_op jit(solution)/shard_map/ppermute | solution.py:105
  79.1 2.3 %fusion.55 = (f32[1024]{0:T(1024)S(1)}, f32[1024,2048]{1,0:T(8,128)S(1)}) fusion(bf16[2048,256]{1,0:T(8,128)(2,1)S(1)} %fusion.8, bf16[128,384]{1,0:T(8,128)(2,1)S(1)} %collective-permute-done.20, bf16[128,384]{1,0:T(8,128)(2,1)S(1)} %get-tuple-element.22, bf16[384,384]{1,0:T(8,128)(2,1)S(1)} %collective-permute-done.17, ...), kind=kOutput, calls=%fused_computation.152 | convolution fusion | flops 550501376 | bytes 9719808 | tf_op jit(solution)/shard_map/dot_general | solution.py:213
  82.6 1.6 %fusion.5 = bf16[1024,128]{1,0:T(8,128)(2,1)S(1)} fusion(f32[1024,2048]{1,0:T(8,128)S(1)} %get-tuple-element.53, f32[1024]{0:T(1024)S(1)} %fusion, f32[1024]{0:T(1024)S(1)} %get-tuple-element.52, bf16[2048,256]{1,0:T(8,128)(2,1)S(1)} %fusion.8), kind=kOutput, calls=%fused_computation.11 | convolution fusion | flops 543293440 | bytes 9183232 | tf_op jit(solution)/shard_map/dot_general | solution.py:220
  84.5 12.9 %all_to_all.5 = bf16[8,128,128]{2,1,0:T(8,128)(2,1)S(1)} all-to-all(bf16[8,128,128]{2,1,0:T(8,128)(2,1)S(1)} %fusion.35), channel_id=1, replica_groups=mesh['grp'=2,'chip'=8,'core'=2] {'chip'}, dimensions={0} | all-to-all | bytes 524288 | tf_op jit(solution)/shard_map/all_to_all | solution.py:229
  (115 shorter events, 21.7 us)
Async XLA Ops:
  1.3 20.3 %collective-permute-start = (bf16[64,1024]{1,0:T(8,128)(2,1)S(1)}, bf16[64,1024]{1,0:T(8,128)(2,1)S(1)}, u32[]{:S(2)}, u32[]{:S(2)}) collective-permute-start(bf16[64,1024]{1,0:T(8,128)(2,1)S(1)} %get-tuple-element.21), channel_id=1, source_target_pairs={{0,0},{1,3},{2,6},{3,9},{4,12},{5,15},{6,2},{7,5},{8,8},{9,11},{10... | collective-permute-start | bytes 393224 | tf_op jit(solution)/shard_map/ppermute | solution.py:151
  1.9 19.7 %collective-permute-start.1 = (bf16[64,1024]{1,0:T(8,128)(2,1)S(1)}, bf16[64,1024]{1,0:T(8,128)(2,1)S(1)}, u32[]{:S(2)}, u32[]{:S(2)}) collective-permute-start(bf16[64,1024]{1,0:T(8,128)(2,1)S(1)} %get-tuple-element.20), channel_id=1, source_target_pairs={{0,1},{1,4},{2,7},{3,10},{4,13},{5,0},{6,3},{7,6},{8,9},{9,12},{10... | collective-permute-start | bytes 393224 | tf_op jit(solution)/shard_map/ppermute | solution.py:151
  5.7 15.9 %collective-permute-start.2 = (bf16[64,1024]{1,0:T(8,128)(2,1)S(1)}, bf16[64,1024]{1,0:T(8,128)(2,1)S(1)}, u32[]{:S(2)}, u32[]{:S(2)}) collective-permute-start(bf16[64,1024]{1,0:T(8,128)(2,1)S(1)} %get-tuple-element.19), channel_id=1, source_target_pairs={{0,2},{1,5},{2,8},{3,11},{4,14},{5,1},{6,4},{7,7},{8,10},{9,13},{1... | collective-permute-start | bytes 393224 | tf_op jit(solution)/shard_map/ppermute | solution.py:151
  10.5 4.5 %collective-permute-start.11 = (bf16[3,2048]{1,0:T(4,128)(2,1)S(1)}, bf16[3,2048]{1,0:T(4,128)(2,1)S(1)}, u32[]{:S(2)}, u32[]{:S(2)}) collective-permute-start(bf16[3,2048]{1,0:T(4,128)(2,1)S(1)} %slice.262), channel_id=1, source_target_pairs={{0,1},{1,2},{2,3},{3,4},{4,5},{5,6},{6,7},{7,8},{8,9},{9,10},{10,1... | collective-permute-start | bytes 36872 | tf_op jit(solution)/shard_map/ppermute | solution.py:137
  15.6 23.1 %copy-start.3 = (bf16[384,2048]{1,0:T(8,128)(2,1)}, bf16[384,2048]{1,0:T(8,128)(2,1)S(1)}, u32[]{:S(2)}) copy-start(bf16[384,2048]{1,0:T(8,128)(2,1)S(1)} %get-tuple-element.5) | copy-start | bytes 4718596
  15.6 15.8 %collective-permute-start.7 = (bf16[64,2048]{1,0:T(8,128)(2,1)S(1)}, bf16[64,2048]{1,0:T(8,128)(2,1)}, u32[]{:S(2)}, u32[]{:S(2)}) collective-permute-start(bf16[64,2048]{1,0:T(8,128)(2,1)S(1)} %get-tuple-element.6), channel_id=1, source_target_pairs={{0,8},{1,9},{2,10},{3,11},{4,12},{5,13},{6,14},{7,15},{8,0},{9,1},... | collective-permute-start | bytes 786440 | tf_op jit(solution)/shard_map/ppermute | solution.py:105
  21.6 28.6 %collective-permute-start.12 = (bf16[128,2048]{1,0:T(8,128)(2,1)}, bf16[128,2048]{1,0:T(8,128)(2,1)}, u32[]{:S(2)}, u32[]{:S(2)}) collective-permute-start(bf16[128,2048]{1,0:T(8,128)(2,1)} %pad_maximum_fusion.12), channel_id=1, source_target_pairs={{0,2},{1,3},{2,0},{3,1},{4,6},{5,7},{6,4},{7,5},{8,10},{9,11},{10,... | collective-permute-start | bytes 1572872 | tf_op jit(solution)/shard_map/ppermute | solution.py:105
  21.7 14.9 %collective-permute-start.3 = (bf16[3,64,1024]{2,1,0:T(8,128)(2,1)S(1)}, bf16[3,64,1024]{2,1,0:T(8,128)(2,1)S(1)}, u32[]{:S(2)}, u32[]{:S(2)}) collective-permute-start(bf16[3,64,1024]{2,1,0:T(8,128)(2,1)S(1)} %constant_dynamic-slice_fusion), channel_id=1, source_target_pairs={{0,16},{1,17},{2,18},{3,19},{4,20},{5,21},{6,22},{7,23},{8,24},{9,... | collective-permute-start | bytes 1179656 | tf_op jit(solution)/shard_map/ppermute | solution.py:105
  23.3 15.4 %collective-permute-start.4 = (bf16[3,64,1024]{2,1,0:T(8,128)(2,1)S(1)}, bf16[3,64,1024]{2,1,0:T(8,128)(2,1)S(1)}, u32[]{:S(2)}, u32[]{:S(2)}) collective-permute-start(bf16[3,64,1024]{2,1,0:T(8,128)(2,1)S(1)} %constant_dynamic-slice_fusion), channel_id=1, source_target_pairs={{0,4},{1,5},{2,6},{3,7},{4,0},{5,1},{6,2},{7,3},{8,12},{9,13},{10,... | collective-permute-start | bytes 1179656 | tf_op jit(solution)/shard_map/ppermute | solution.py:105
  34.7 27.0 %collective-permute-start.18 = (bf16[64,2048]{1,0:T(8,128)(2,1)}, bf16[64,2048]{1,0:T(8,128)(2,1)S(1)}, u32[]{:S(2)}, u32[]{:S(2)}) collective-permute-start(bf16[64,2048]{1,0:T(8,128)(2,1)} %broadcast_add_fusion.1), channel_id=1, source_target_pairs={{0,8},{1,9},{2,10},{3,11},{4,12},{5,13},{6,14},{7,15},{8,0},{9,1},... | collective-permute-start | bytes 786440 | tf_op jit(solution)/shard_map/ppermute | solution.py:105
  34.7 9.2 %collective-permute-start.8 = (bf16[64,2048]{1,0:T(8,128)(2,1)}, bf16[64,2048]{1,0:T(8,128)(2,1)}, u32[]{:S(2)}, u32[]{:S(2)}) collective-permute-start(bf16[64,2048]{1,0:T(8,128)(2,1)} %collective-permute-done.7), channel_id=1, source_target_pairs={{0,2},{1,3},{2,0},{3,1},{4,6},{5,7},{6,4},{7,5},{8,10},{9,11},{10,... | collective-permute-start | bytes 786440 | tf_op jit(solution)/shard_map/ppermute | solution.py:105
  40.8 1.2 %collective-permute-start.5 = (s32[1,128]{1,0:T(1,128)S(1)}, s32[1,128]{1,0:T(1,128)S(1)}, u32[]{:S(2)}, u32[]{:S(2)}) collective-permute-start(s32[1,128]{1,0:T(1,128)S(1)} %fusion.46), channel_id=1, source_target_pairs={{0,1},{1,0},{2,3},{3,2},{4,5},{5,4},{6,7},{7,6},{8,9},{9,8},{10,11... | collective-permute-start | bytes 1544 | tf_op jit(solution)/shard_map/ppermute | solution.py:105
  42.0 6.1 %collective-permute-start.6 = (s32[2,128]{1,0:T(2,128)S(1)}, s32[2,128]{1,0:T(2,128)S(1)}, u32[]{:S(2)}, u32[]{:S(2)}) collective-permute-start(s32[2,128]{1,0:T(2,128)S(1)} %pad_add_fusion.1), channel_id=1, source_target_pairs={{0,2},{1,3},{2,0},{3,1},{4,6},{5,7},{6,4},{7,5},{8,10},{9,11},{10,... | collective-permute-start | bytes 3080 | tf_op jit(solution)/shard_map/ppermute | solution.py:105
  42.5 21.2 %collective-permute-start.13 = (bf16[3,64,2048]{2,1,0:T(8,128)(2,1)S(1)}, bf16[3,64,2048]{2,1,0:T(8,128)(2,1)S(1)}, u32[]{:S(2)}, u32[]{:S(2)}) collective-permute-start(bf16[3,64,2048]{2,1,0:T(8,128)(2,1)S(1)} %bitcast.148), channel_id=1, source_target_pairs={{0,1},{1,0},{2,3},{3,2},{4,5},{5,4},{6,7},{7,6},{8,9},{9,8},{10,11... | collective-permute-start | bytes 2359304 | tf_op jit(solution)/shard_map/ppermute | solution.py:105
  43.9 11.6 %collective-permute-start.14 = (bf16[3,64,512]{2,1,0:T(8,128)(2,1)}, bf16[3,64,512]{2,1,0:T(8,128)(2,1)S(1)}, u32[]{:S(2)}, u32[]{:S(2)}) collective-permute-start(bf16[3,64,512]{2,1,0:T(8,128)(2,1)} %slice.307), channel_id=1, source_target_pairs={{0,16},{1,17},{2,18},{3,19},{4,20},{5,21},{6,22},{7,23},{8,24},{9,... | collective-permute-start | bytes 589832 | tf_op jit(solution)/shard_map/ppermute | solution.py:105
  48.1 7.5 %collective-permute-start.15 = (bf16[3,64,512]{2,1,0:T(8,128)(2,1)}, bf16[3,64,512]{2,1,0:T(8,128)(2,1)S(1)}, u32[]{:S(2)}, u32[]{:S(2)}) collective-permute-start(bf16[3,64,512]{2,1,0:T(8,128)(2,1)} %slice.308), channel_id=1, source_target_pairs={{0,4},{1,5},{2,6},{3,7},{4,0},{5,1},{6,2},{7,3},{8,12},{9,13},{10,... | collective-permute-start | bytes 589832 | tf_op jit(solution)/shard_map/ppermute | solution.py:105
  50.1 5.8 %collective-permute-start.9 = (s32[4,128]{1,0:T(4,128)S(1)}, s32[4,128]{1,0:T(4,128)S(1)}, u32[]{:S(2)}, u32[]{:S(2)}) collective-permute-start(s32[4,128]{1,0:T(4,128)S(1)} %add_add_fusion), channel_id=1, source_target_pairs={{0,4},{1,5},{2,6},{3,7},{4,0},{5,1},{6,2},{7,3},{8,12},{9,13},{10,... | collective-permute-start | bytes 6152 | tf_op jit(solution)/shard_map/ppermute | solution.py:105
  55.8 7.9 %collective-permute-start.16 = (bf16[3,64,2048]{2,1,0:T(8,128)(2,1)S(1)}, bf16[3,64,2048]{2,1,0:T(8,128)(2,1)S(1)}, u32[]{:S(2)}, u32[]{:S(2)}) collective-permute-start(bf16[3,64,2048]{2,1,0:T(8,128)(2,1)S(1)} %bitcast.150), channel_id=1, source_target_pairs={{0,1},{1,0},{2,3},{3,2},{4,5},{5,4},{6,7},{7,6},{8,9},{9,8},{10,11... | collective-permute-start | bytes 2359304 | tf_op jit(solution)/shard_map/ppermute | solution.py:105
  55.9 4.6 %collective-permute-start.10 = (s32[8,128]{1,0:T(8,128)S(1)}, s32[8,128]{1,0:T(8,128)S(1)}, u32[]{:S(2)}, u32[]{:S(2)}) collective-permute-start(s32[8,128]{1,0:T(8,128)S(1)} %pad_add_fusion), channel_id=1, source_target_pairs={{0,8},{1,9},{2,10},{3,11},{4,12},{5,13},{6,14},{7,15},{8,0},{9,1},... | collective-permute-start | bytes 12296 | tf_op jit(solution)/shard_map/ppermute | solution.py:105
  61.8 7.9 %collective-permute-start.19 = (bf16[64,2048]{1,0:T(8,128)(2,1)S(1)}, bf16[64,2048]{1,0:T(8,128)(2,1)S(1)}, u32[]{:S(2)}, u32[]{:S(2)}) collective-permute-start(bf16[64,2048]{1,0:T(8,128)(2,1)S(1)} %broadcast_add_fusion), channel_id=1, source_target_pairs={{0,2},{1,3},{2,0},{3,1},{4,6},{5,7},{6,4},{7,5},{8,10},{9,11},{10,... | collective-permute-start | bytes 786440 | tf_op jit(solution)/shard_map/ppermute | solution.py:105
  67.3 9.3 %collective-permute-start.17 = (bf16[384,384]{1,0:T(8,128)(2,1)S(1)}, bf16[384,384]{1,0:T(8,128)(2,1)S(1)}, u32[]{:S(2)}, u32[]{:S(2)}) collective-permute-start(bf16[384,384]{1,0:T(8,128)(2,1)S(1)} %get-tuple-element.18), channel_id=1, source_target_pairs={{0,4},{1,5},{2,6},{3,7},{4,0},{5,1},{6,2},{7,3},{8,12},{9,13},{10,... | collective-permute-start | bytes 884744 | tf_op jit(solution)/shard_map/ppermute | solution.py:105
  70.9 6.7 %collective-permute-start.20 = (bf16[128,384]{1,0:T(8,128)(2,1)S(1)}, bf16[128,384]{1,0:T(8,128)(2,1)S(1)}, u32[]{:S(2)}, u32[]{:S(2)}) collective-permute-start(bf16[128,384]{1,0:T(8,128)(2,1)S(1)} %get-tuple-element.23), channel_id=1, source_target_pairs={{0,4},{1,5},{2,6},{3,7},{4,0},{5,1},{6,2},{7,3},{8,12},{9,13},{10,... | collective-permute-start | bytes 294920 | tf_op jit(solution)/shard_map/ppermute | solution.py:105
  76.6 2.5 %collective-permute-start.21 = (bf16[768,256]{1,0:T(8,128)(2,1)S(1)}, bf16[768,256]{1,0:T(8,128)(2,1)S(1)}, u32[]{:S(2)}, u32[]{:S(2)}) collective-permute-start(bf16[768,256]{1,0:T(8,128)(2,1)S(1)} %pad_maximum_fusion.13), channel_id=1, source_target_pairs={{0,1},{1,0},{2,3},{3,2},{4,5},{5,4},{6,7},{7,6},{8,9},{9,8},{10,11... | collective-permute-start | bytes 1179656 | tf_op jit(solution)/shard_map/ppermute | solution.py:105
  77.6 1.4 %collective-permute-start.22 = (bf16[256,256]{1,0:T(8,128)(2,1)S(1)}, bf16[256,256]{1,0:T(8,128)(2,1)S(1)}, u32[]{:S(2)}, u32[]{:S(2)}) collective-permute-start(bf16[256,256]{1,0:T(8,128)(2,1)S(1)} %pad_maximum_fusion.14), channel_id=1, source_target_pairs={{0,1},{1,0},{2,3},{3,2},{4,5},{5,4},{6,7},{7,6},{8,9},{9,8},{10,11... | collective-permute-start | bytes 393224 | tf_op jit(solution)/shard_map/ppermute | solution.py:105
  (7 other events, 76.8 us)

commit v12 on v10

--- a/solution.py
+++ b/solution.py
@@ -105,6 +105,19 @@
     return lax.ppermute(value, axes, [(d, d ^ bit) for d in range(count)])
 
 
+MORE = 8
+
+
+def with_groups(rows, groups):
+    width = rows.shape[1]
+    flat = jnp.pad(groups.reshape(-1), (0, MORE * width - groups.size))
+    return jnp.concatenate([rows, flat.reshape(MORE, width)], axis=0)
+
+
+def groups_behind(rows, count, tok_rows):
+    return rows[-MORE:].reshape(-1)[: count * tok_rows].reshape(count, tok_rows)
+
+
 def by_bit(bit, mine, theirs, axis):
     return jnp.stack(
         [jnp.where(bit == 0, mine, theirs), jnp.where(bit == 0, theirs, mine)], axis=axis
@@ -140,12 +153,20 @@
     late = convolve(frames[part:], conv_weight, frames[part - (KW - 1) : part])
     early = convolve(frames[:part], conv_weight, rim_rows)
 
-    far_late = xor_swap(late, Z1)
+    group = track_groups(track_ids, track_owner).astype(jnp.bfloat16)
+    row = jnp.pad(group[None, :], ((0, MORE - 1), (0, features - tok_rows)))
+    own = jnp.concatenate([early, late], axis=0)
+    far_late_and = xor_swap(jnp.concatenate([late, row], axis=0), Z1)
+    far_late = far_late_and[:part]
     far_early = xor_swap(early + zero_after(far_late), Z1)
-    own = jnp.concatenate([early, late], axis=0)
-    beside = xor_swap(own, Y)
-    far_beside_late = xor_swap(far_late, Y)
+    beside_and = xor_swap(jnp.concatenate([own, row], axis=0), Y)
+    beside = beside_and[:tok_rows]
+    far_beside_late_and = xor_swap(far_late_and, Y)
+    far_beside_late = far_beside_late_and[:part]
     far_beside_early = xor_swap(far_early, Y)
+    groups = [group] + [
+        rows[-MORE, :tok_rows] for rows in (beside_and, far_late_and, far_beside_late_and)
+    ]
 
     half = features // 2
     held = lax.dynamic_slice_in_dim(qkv_weight.T, grp * half, half, 1).reshape(3, HD // 2, half)
@@ -166,13 +187,6 @@
         axis=2,
     )
 
-    span = devices * tok_rows
-    times = me * tok_rows + jnp.arange(tok_rows, dtype=jnp.int32)
-    codes = (track_groups(track_ids, track_owner) * span + times)[None, :]
-    codes = codes + zero_after(fourth).astype(jnp.int32)
-    for bit in (CORE, Y, Z0, Z1):
-        codes = jnp.concatenate([codes, xor_swap(codes, bit)], axis=0)
-
     def whole_head(quarter, quarter_too):
         wide = by_bit(grp, quarter, quarter_too, 2).reshape(3, HD // 2, features)
         return by_bit(core, wide, xor_swap(wide, CORE), 1).reshape(3 * HD, features)
@@ -185,12 +199,20 @@
         done = lax.dot_general(
             rows, two_heads, (((1,), (1,)), ((), ())), preferred_element_type=jnp.float32
         ).astype(jnp.bfloat16)
-        return jnp.concatenate([done[:, : 3 * HD], xor_swap(done[:, 3 * HD :], Z0)], axis=0)
-
-    first = project(jnp.concatenate([own, beside, far_late, far_beside_late], axis=0))
-    second = project(
-        jnp.concatenate([far_early, far_beside_early], axis=0) + zero_after(codes)
-    )
+        return done[:, : 3 * HD], done[:, 3 * HD :]
+
+    hops = [0, Y, Z1, Z1 | Y]
+    groups = jnp.stack(groups)
+    mine, theirs = project(
+        jnp.concatenate([own, beside, far_late, far_beside_late], axis=0)
+    )
+    count = mine.shape[0]
+    theirs = xor_swap(with_groups(theirs, groups), Z0)
+    first = jnp.concatenate([mine, theirs[:count]], axis=0)
+    groups = jnp.concatenate([groups, groups_behind(theirs, 4, tok_rows)], axis=0)
+    hops += [hop ^ Z0 for hop in hops]
+    mine, theirs = project(jnp.concatenate([far_early, far_beside_early], axis=0))
+    second = jnp.concatenate([mine, xor_swap(theirs, Z0)], axis=0)
 
     first_rows = [(0, 0, tok_rows), (Y, 0, tok_rows), (Z1, part, part), (Z1 | Y, part, part)]
     second_rows = [(Z1, 0, part), (Z1 | Y, 0, part)]
@@ -198,19 +220,26 @@
     for pieces in (first_rows, second_rows):
         order += pieces + [(far ^ Z0, start, count) for far, start, count in pieces]
 
-    def codes_at(bit):
-        return jnp.concatenate(
-            [codes[far ^ bit, start : start + count] for far, start, count in order]
-        )
-
-    asking = codes_at(0)
-    keys = jnp.concatenate([asking, codes_at(CORE)])
-    least = asking // span * span
     projected = jnp.concatenate([first, second], axis=0)
     query = projected[:, :HD]
-    keyed = jnp.concatenate(
-        [projected[:, HD:], xor_swap(first[:, HD:], CORE), xor_swap(second[:, HD:], CORE)], axis=0
-    )
+    first = xor_swap(with_groups(first[:, HD:], groups), CORE)
+    second = xor_swap(second[:, HD:], CORE)
+    keyed = jnp.concatenate([projected[:, HD:], first[:-MORE], second], axis=0)
+    other_groups = groups_behind(first, 8, tok_rows)
+
+    span = devices * tok_rows
+
+    def codes_of(groups, bit):
+        seen = jnp.array(hops, jnp.int32)[:, None] ^ (me ^ bit)
+        times = seen * tok_rows + jnp.arange(tok_rows, dtype=jnp.int32)[None, :]
+        codes = groups.astype(jnp.int32) * span + times
+        return jnp.concatenate(
+            [codes[hops.index(far), start : start + count] for far, start, count in order]
+        )
+
+    asking = codes_of(groups, 0)
+    keys = jnp.concatenate([asking, codes_of(other_groups, CORE)])
+    least = asking // span * span
     scores = lax.dot_general(
         query, keyed[:, :HD], (((1,), (1,)), ((), ())), preferred_element_type=jnp.float32
     ) * (1.0 / HD**0.5)

time: 97.4 us -> 101 us (1.037)
  waiting for transfers between devices: 29.5 us -> 34.7 us
  starting transfers between devices: 31.5 us -> 27.1 us
  local copies, waits for them, and re-layouts: 8.31 us -> 11.3 us
  between operations: 3.99 us -> 1.95 us
  other arithmetic: 4.02 us -> 5.4 us
    ppermute x19 -> x15, waiting for transfers between devices: 29.5 us -> 34.7 us  [xor_swap(): return lax.ppermute(value, axes, [(d, d ^ bit) for d in range(count)])]
    ppermute x19 -> x15, starting transfers between devices: 19.9 us -> 15.5 us  [xor_swap(): return lax.ppermute(value, axes, [(d, d ^ bit) for d in range(count)])]
    unnamed x21 -> x29, local copies, waits for them, and re-layouts: 3.72 us -> 5.99 us
    concatenate x1, local copies, waits for them, and re-layouts: 0.02 us -> 1.67 us  [body_by_head(): jnp.concatenate([own, beside, far_late, far_beside_late], axis=0)]
    another operation x5, other arithmetic: 0.62 us -> 1.79 us  [by_bit(): jnp.stack([jnp.where(bit == 0, mine, theirs), jnp.where(bit == 0, theirs,...]
    slice x3 -> x1, local copies, waits for them, and re-layouts: 1.75 us -> 0.58 us  [zero_after(): last = array[(-1,) * array.ndim]]
  transfers between devices with their start and end apart: 23 -> 19, of which waited for: 9 -> 5; matrix products, arithmetic and copies ran while one was open for 10% -> 14% of each run, Pallas kernels for 0% -> 0%
where the time goes in v12:
time: 101 us; the launch traced here: 100 us
  waiting for transfers between devices  34.7 us (34%)
  starting transfers between devices  27.1 us (27%)
  blocking collectives  12.2 us (12%)
  local copies, waits for them, and re-layouts  11.3 us (11%)
  matrix products  7.49 us (7%)
  other arithmetic  5.4 us (5%)
  between operations  1.95 us (2%)
    ppermute x15, waiting for transfers between devices, xor_swap(): return lax.ppermute(value, axes, [(d, d ^ bit) for d in range(count)])  34.7 us
    ppermute x15, starting transfers between devices, xor_swap(): return lax.ppermute(value, axes, [(d, d ^ bit) for d in range(count)])  15.5 us
    all_to_all x1, blocking collectives, body_by_head(): lax.all_to_all(sent, 'chip', split_axis=0, concat_axis=0, tiled=True)  12.2 us
    ppermute x3, starting transfers between devices, body_by_head(): lax.ppermute(held[j], both, [(d, (3 * d + j) % devices) for d in range(de...  8.43 us
    unnamed x29, local copies, waits for them, and re-layouts  5.99 us
    dot_general x2, matrix products, project(): lax.dot_general(rows, two_heads, (((1,), (1,)), ((), ())), preferred_elem...  3.63 us
    ppermute x1, starting transfers between devices, body_by_head(): lax.ppermute(frames[tok_rows - (KW - 1):], both, [(i, i + 1) for i in ran...  3.2 us
    dot_general x1, matrix products, body_by_head(): lax.dot_general(query, keyed[:, :HD], (((1,), (1,)), ((), ())), preferred...  2.26 us
  transfers between devices with their start and end apart: 19, of which 5 were waited for; matrix products, arithmetic and copies ran while one was open for 14% of the time, Pallas kernels for 0%

profile of v12, /device:TPU:0, one launch (start us, length us, event | category | flops | bytes accessed | tf_op | source)
XLA Modules:
  0.0 100.1 jit_solution(5470567551650940172)
XLA Ops:
  1.9 3.8 %collective-permute-start.5 = (bf16[64,1024]{1,0:T(8,128)(2,1)S(1)}, bf16[64,1024]{1,0:T(8,128)(2,1)S(1)}, u32[]{:S(2)}, u32[]{:S(2)}) collective-permute-start(bf16[64,1024]{1,0:T(8,128)(2,1)S(1)} %get-tuple-element.18), channel_id=1, source_target_pairs={{0,1},{1,4},{2,7},{3,10},{4,13},{5,0},{6,3},{7,6},{8,9},{9,12},{10... | collective-permute-start | bytes 393224 | tf_op jit(solution)/shard_map/ppermute | solution.py:174
  5.7 3.9 %collective-permute-start.6 = (bf16[64,1024]{1,0:T(8,128)(2,1)S(1)}, bf16[64,1024]{1,0:T(8,128)(2,1)S(1)}, u32[]{:S(2)}, u32[]{:S(2)}) collective-permute-start(bf16[64,1024]{1,0:T(8,128)(2,1)S(1)} %get-tuple-element.17), channel_id=1, source_target_pairs={{0,2},{1,5},{2,8},{3,11},{4,14},{5,1},{6,4},{7,7},{8,10},{9,13},{1... | collective-permute-start | bytes 393224 | tf_op jit(solution)/shard_map/ppermute | solution.py:174
  10.5 3.2 %collective-permute-start = (bf16[3,2048]{1,0:T(4,128)(2,1)S(1)}, bf16[3,2048]{1,0:T(4,128)(2,1)S(1)}, u32[]{:S(2)}, u32[]{:S(2)}) collective-permute-start(bf16[3,2048]{1,0:T(4,128)(2,1)S(1)} %slice.252), channel_id=1, source_target_pairs={{0,1},{1,2},{2,3},{3,4},{4,5},{5,6},{6,7},{7,8},{8,9},{9,10},{10,1... | collective-permute-start | bytes 36872 | tf_op jit(solution)/shard_map/ppermute | solution.py:150
  15.2 1.4 %collective-permute-start.2 = (bf16[72,2048]{1,0:T(8,128)(2,1)S(1)}, bf16[72,2048]{1,0:T(8,128)(2,1)S(1)}, u32[]{:S(2)}, u32[]{:S(2)}) collective-permute-start(bf16[72,2048]{1,0:T(8,128)(2,1)S(1)} %pad_maximum_fusion.15), channel_id=1, source_target_pairs={{0,8},{1,9},{2,10},{3,11},{4,12},{5,13},{6,14},{7,15},{8,0},{9,1},... | collective-permute-start | bytes 884744 | tf_op jit(solution)/shard_map/ppermute | solution.py:105
  16.8 1.6 %collective-permute-start.7 = (bf16[3,64,1024]{2,1,0:T(8,128)(2,1)S(1)}, bf16[3,64,1024]{2,1,0:T(8,128)(2,1)S(1)}, u32[]{:S(2)}, u32[]{:S(2)}) collective-permute-start(bf16[3,64,1024]{2,1,0:T(8,128)(2,1)S(1)} %constant_dynamic-slice_fusion), channel_id=1, source_target_pairs={{0,16},{1,17},{2,18},{3,19},{4,20},{5,21},{6,22},{7,23},{8,24},{9,... | collective-permute-start | bytes 1179656 | tf_op jit(solution)/shard_map/ppermute | solution.py:105
  18.4 2.5 %collective-permute-start.9 = (bf16[3,64,1024]{2,1,0:T(8,128)(2,1)S(1)}, bf16[3,64,1024]{2,1,0:T(8,128)(2,1)S(1)}, u32[]{:S(2)}, u32[]{:S(2)}) collective-permute-start(bf16[3,64,1024]{2,1,0:T(8,128)(2,1)S(1)} %constant_dynamic-slice_fusion), channel_id=1, source_target_pairs={{0,4},{1,5},{2,6},{3,7},{4,0},{5,1},{6,2},{7,3},{8,12},{9,13},{10,... | collective-permute-start | bytes 1179656 | tf_op jit(solution)/shard_map/ppermute | solution.py:105
  20.9 11.4 %collective-permute-done.2 = bf16[72,2048]{1,0:T(8,128)(2,1)S(1)} collective-permute-done((bf16[72,2048]{1,0:T(8,128)(2,1)S(1)}, bf16[72,2048]{1,0:T(8,128)(2,1)S(1)}, u32[]{:S(2)}, u32[]{:S(2)}) %collective-permute-start.2) | collective-permute-done | bytes 294944 | tf_op jit(solution)/shard_map/ppermute | solution.py:105
  34.6 1.3 %collective-permute-start.1 = (bf16[136,2048]{1,0:T(8,128)(2,1)S(1)}, bf16[136,2048]{1,0:T(8,128)(2,1)S(1)}, u32[]{:S(2)}, u32[]{:S(2)}) collective-permute-start(bf16[136,2048]{1,0:T(8,128)(2,1)S(1)} %pad_maximum_fusion.12), channel_id=1, source_target_pairs={{0,2},{1,3},{2,0},{3,1},{4,6},{5,7},{6,4},{7,5},{8,10},{9,11},{10,... | collective-permute-start | bytes 1671176 | tf_op jit(solution)/shard_map/ppermute | solution.py:105
  36.8 1.6 %collective-permute-start.10 = (bf16[3,64,512]{2,1,0:T(8,128)(2,1)S(1)}, bf16[3,64,512]{2,1,0:T(8,128)(2,1)S(1)}, u32[]{:S(2)}, u32[]{:S(2)}) collective-permute-start(bf16[3,64,512]{2,1,0:T(8,128)(2,1)S(1)} %slice.346), channel_id=1, source_target_pairs={{0,16},{1,17},{2,18},{3,19},{4,20},{5,21},{6,22},{7,23},{8,24},{9,... | collective-permute-start | bytes 589832 | tf_op jit(solution)/shard_map/ppermute | solution.py:105
  38.4 2.0 %collective-permute-start.11 = (bf16[3,64,512]{2,1,0:T(8,128)(2,1)S(1)}, bf16[3,64,512]{2,1,0:T(8,128)(2,1)S(1)}, u32[]{:S(2)}, u32[]{:S(2)}) collective-permute-start(bf16[3,64,512]{2,1,0:T(8,128)(2,1)S(1)} %slice.347), channel_id=1, source_target_pairs={{0,4},{1,5},{2,6},{3,7},{4,0},{5,1},{6,2},{7,3},{8,12},{9,13},{10,... | collective-permute-start | bytes 589832 | tf_op jit(solution)/shard_map/ppermute | solution.py:105
  40.6 7.9 %collective-permute-done.15 = bf16[64,2048]{1,0:T(8,128)(2,1)} collective-permute-done((bf16[64,2048]{1,0:T(8,128)(2,1)S(1)}, bf16[64,2048]{1,0:T(8,128)(2,1)}, u32[]{:S(2)}, u32[]{:S(2)}) %collective-permute-start.15) | collective-permute-done | bytes 262176 | tf_op jit(solution)/shard_map/ppermute | solution.py:105
  48.5 6.9 %collective-permute-done.3 = bf16[72,2048]{1,0:T(8,128)(2,1)S(1)} collective-permute-done((bf16[72,2048]{1,0:T(8,128)(2,1)S(1)}, bf16[72,2048]{1,0:T(8,128)(2,1)S(1)}, u32[]{:S(2)}, u32[]{:S(2)}) %collective-permute-start.3) | collective-permute-done | bytes 294944 | tf_op jit(solution)/shard_map/ppermute | solution.py:105
  55.4 1.5 %collective-permute-start.16 = (bf16[64,2048]{1,0:T(8,128)(2,1)}, bf16[64,2048]{1,0:T(8,128)(2,1)}, u32[]{:S(2)}, u32[]{:S(2)}) collective-permute-start(bf16[64,2048]{1,0:T(8,128)(2,1)} %collective-permute-done.15), channel_id=1, source_target_pairs={{0,2},{1,3},{2,0},{3,1},{4,6},{5,7},{6,4},{7,5},{8,10},{9,11},{10,... | collective-permute-start | bytes 786440 | tf_op jit(solution)/shard_map/ppermute | solution.py:105
  58.2 1.9 %slice_dynamic-update-slice_fusion = bf16[384,2048]{1,0:T(8,128)(2,1)} fusion(bf16[384,2048]{1,0:T(8,128)(2,1)} %copy-done.5, bf16[136,2048]{1,0:T(8,128)(2,1)} %copy-done.2), kind=kLoop, calls=%fused_computation.27 | loop fusion | bytes 1048576
  60.8 1.7 %slice_dynamic-update-slice_fusion.1 = bf16[384,2048]{1,0:T(8,128)(2,1)} fusion(bf16[384,2048]{1,0:T(8,128)(2,1)} %slice_dynamic-update-slice_fusion.2, bf16[72,2048]{1,0:T(8,128)(2,1)} %copy-done.3), kind=kLoop, calls=%fused_computation.67 | loop fusion | bytes 524288 | tf_op jit(solution)/shard_map/concatenate | solution.py:207
  62.5 1.3 %select_bitcast_fusion.1 = (bf16[3,1,64,2048]{3,2,0,1:T(8,128)(2,1)S(1)}, bf16[3,1,64,2048]{3,2,0,1:T(8,128)(2,1)S(1)}, bf16[3,1,64,2048]{3,2,0,1:T(8,128)(2,1)S(1)}, bf16[3,1,64,2048]{3,2,0,1:T(8,128)(2,1)S(1)}) fusion(bf16[3,64,2048]{2,1,0:T(8,128)(2,1)S(1)} %bitcast.147, bf16[3,64,2048]{2,1,0:T(8,128)(2,1)} %collective-permute-done.12, pred[]{:T(512)S(6)} %eq.13, ...), kind=kLoop, calls=%fused_computation.21 | loop fusion | flops 1572864 | bytes 6291457 | tf_op jit(solution)/shard_map/stack | solution.py:122
  64.4 1.3 %copy-done.6 = bf16[384,2048]{1,0:T(8,128)(2,1)S(1)} copy-done((bf16[384,2048]{1,0:T(8,128)(2,1)S(1)}, bf16[384,2048]{1,0:T(8,128)(2,1)}, u32[]{:S(2)}) %copy-start.6) | copy-done | bytes 1572888
  65.7 1.4 %fusion.4 = bf16[384,768]{1,0:T(8,128)(2,1)S(1)} fusion(bf16[384,2048]{1,0:T(8,128)(2,1)S(1)} %copy-done.6, bf16[384,2048]{1,0:T(8,128)(2,1)S(1)} %bitcast.150, bf16[384,2048]{1,0:T(8,128)(2,1)S(1)} %bitcast.148), kind=kOutput, calls=%fused_computation.10 | convolution fusion | flops 1214545920 | bytes 5308416 | tf_op jit(solution)/shard_map/dot_general | solution.py:199
  67.3 2.2 %fusion.6 = bf16[128,768]{1,0:T(8,128)(2,1)S(1)} fusion(bf16[384,2048]{1,0:T(8,128)(2,1)S(1)} %bitcast.151, bf16[384,2048]{1,0:T(8,128)(2,1)S(1)} %bitcast.149, bf16[64,2048]{1,0:T(8,128)(2,1)} %collective-permute-done.16, bf16[64,2048]{1,0:T(8,128)(2,1)} %collective-permute-done.15), kind=kOutput, calls=%fused_computation.12 | convolution fusion | flops 410091520 | bytes 3866624 | tf_op jit(solution)/shard_map/dot_general | solution.py:199
  69.6 2.1 %collective-permute-start.17 = (bf16[128,384]{1,0:T(8,128)(2,1)S(1)}, bf16[128,384]{1,0:T(8,128)(2,1)S(1)}, u32[]{:S(2)}, u32[]{:S(2)}) collective-permute-start(bf16[128,384]{1,0:T(8,128)(2,1)S(1)} %get-tuple-element.21), channel_id=1, source_target_pairs={{0,4},{1,5},{2,6},{3,7},{4,0},{5,1},{6,2},{7,3},{8,12},{9,13},{10,... | collective-permute-start | bytes 294920 | tf_op jit(solution)/shard_map/ppermute | solution.py:105
  71.6 7.3 %collective-permute-done.17 = bf16[128,384]{1,0:T(8,128)(2,1)S(1)} collective-permute-done((bf16[128,384]{1,0:T(8,128)(2,1)S(1)}, bf16[128,384]{1,0:T(8,128)(2,1)S(1)}, u32[]{:S(2)}, u32[]{:S(2)}) %collective-permute-start.17) | collective-permute-done | bytes 98336 | tf_op jit(solution)/shard_map/ppermute | solution.py:105
  81.5 2.3 %fusion.54 = (f32[1024]{0:T(1024)S(1)}, f32[1024,2048]{1,0:T(8,128)S(1)}) fusion(bf16[2048,256]{1,0:T(8,128)(2,1)S(1)} %fusion.8, bf16[128,384]{1,0:T(8,128)(2,1)S(1)} %collective-permute-done.17, bf16[128,384]{1,0:T(8,128)(2,1)S(1)} %get-tuple-element.20, bf16[384,384]{1,0:T(8,128)(2,1)S(1)} %slice.352, bf16[384,384]{1,0:T(8,128)(2,1)S(1)} %get-tuple-element.15, ...), kind=kOutput, calls=%fused_computation.156 | convolution fusion | flops 550501376 | bytes 9719808 | tf_op jit(solution)/shard_map/dot_general | solution.py:243
  85.0 1.6 %fusion.5 = bf16[1024,128]{1,0:T(8,128)(2,1)S(1)} fusion(f32[1024,2048]{1,0:T(8,128)S(1)} %get-tuple-element.53, f32[1024]{0:T(1024)S(1)} %fusion, f32[1024]{0:T(1024)S(1)} %get-tuple-element.52, bf16[2048,256]{1,0:T(8,128)(2,1)S(1)} %fusion.8), kind=kOutput, calls=%fused_computation.11 | convolution fusion | flops 543293440 | bytes 9183232 | tf_op jit(solution)/shard_map/dot_general | solution.py:250
  86.9 12.2 %all_to_all.5 = bf16[8,128,128]{2,1,0:T(8,128)(2,1)S(1)} all-to-all(bf16[8,128,128]{2,1,0:T(8,128)(2,1)S(1)} %fusion.36), channel_id=1, replica_groups=mesh['grp'=2,'chip'=8,'core'=2] {'chip'}, dimensions={0} | all-to-all | bytes 524288 | tf_op jit(solution)/shard_map/all_to_all | solution.py:259
  (129 shorter events, 13.9 us)
Async XLA Ops:
  0.0 14.9 %copy-start.1 = (bf16[128,2048]{1,0:T(8,128)(2,1)S(1)}, bf16[128,2048]{1,0:T(8,128)(2,1)}, u32[]{:S(2)}) copy-start(bf16[128,2048]{1,0:T(8,128)(2,1)} %param.7) | copy-start | bytes 1572868
  0.0 14.7 %copy-start.4 = (bf16[4,2048]{1,0:T(4,128)(2,1)S(1)}, bf16[4,2048]{1,0:T(4,128)(2,1)}, u32[]{:S(2)}) copy-start(bf16[4,2048]{1,0:T(4,128)(2,1)} %param.8) | copy-start | bytes 49156
  0.0 14.8 %copy-start.9 = (s32[128]{0:T(128)S(1)}, s32[128]{0:T(128)}, u32[]{:S(2)}) copy-start(s32[128]{0:T(128)} %param.10) | copy-start | bytes 1540
  0.0 14.8 %copy-start.8 = (s32[64]{0:T(128)S(1)}, s32[64]{0:T(128)}, u32[]{:S(2)}) copy-start(s32[64]{0:T(128)} %param.11) | copy-start | bytes 772
  1.3 15.4 %collective-permute-start.4 = (bf16[64,1024]{1,0:T(8,128)(2,1)S(1)}, bf16[64,1024]{1,0:T(8,128)(2,1)S(1)}, u32[]{:S(2)}, u32[]{:S(2)}) collective-permute-start(bf16[64,1024]{1,0:T(8,128)(2,1)S(1)} %get-tuple-element.19), channel_id=1, source_target_pairs={{0,0},{1,3},{2,6},{3,9},{4,12},{5,15},{6,2},{7,5},{8,8},{9,11},{10... | collective-permute-start | bytes 393224 | tf_op jit(solution)/shard_map/ppermute | solution.py:174
  1.9 14.8 %collective-permute-start.5 = (bf16[64,1024]{1,0:T(8,128)(2,1)S(1)}, bf16[64,1024]{1,0:T(8,128)(2,1)S(1)}, u32[]{:S(2)}, u32[]{:S(2)}) collective-permute-start(bf16[64,1024]{1,0:T(8,128)(2,1)S(1)} %get-tuple-element.18), channel_id=1, source_target_pairs={{0,1},{1,4},{2,7},{3,10},{4,13},{5,0},{6,3},{7,6},{8,9},{9,12},{10... | collective-permute-start | bytes 393224 | tf_op jit(solution)/shard_map/ppermute | solution.py:174
  5.7 11.0 %collective-permute-start.6 = (bf16[64,1024]{1,0:T(8,128)(2,1)S(1)}, bf16[64,1024]{1,0:T(8,128)(2,1)S(1)}, u32[]{:S(2)}, u32[]{:S(2)}) collective-permute-start(bf16[64,1024]{1,0:T(8,128)(2,1)S(1)} %get-tuple-element.17), channel_id=1, source_target_pairs={{0,2},{1,5},{2,8},{3,11},{4,14},{5,1},{6,4},{7,7},{8,10},{9,13},{1... | collective-permute-start | bytes 393224 | tf_op jit(solution)/shard_map/ppermute | solution.py:174
  10.5 6.1 %collective-permute-start = (bf16[3,2048]{1,0:T(4,128)(2,1)S(1)}, bf16[3,2048]{1,0:T(4,128)(2,1)S(1)}, u32[]{:S(2)}, u32[]{:S(2)}) collective-permute-start(bf16[3,2048]{1,0:T(4,128)(2,1)S(1)} %slice.252), channel_id=1, source_target_pairs={{0,1},{1,2},{2,3},{3,4},{4,5},{5,6},{6,7},{7,8},{8,9},{9,10},{10,1... | collective-permute-start | bytes 36872 | tf_op jit(solution)/shard_map/ppermute | solution.py:150
  15.2 17.1 %collective-permute-start.2 = (bf16[72,2048]{1,0:T(8,128)(2,1)S(1)}, bf16[72,2048]{1,0:T(8,128)(2,1)S(1)}, u32[]{:S(2)}, u32[]{:S(2)}) collective-permute-start(bf16[72,2048]{1,0:T(8,128)(2,1)S(1)} %pad_maximum_fusion.15), channel_id=1, source_target_pairs={{0,8},{1,9},{2,10},{3,11},{4,12},{5,13},{6,14},{7,15},{8,0},{9,1},... | collective-permute-start | bytes 884744 | tf_op jit(solution)/shard_map/ppermute | solution.py:105
  16.8 21.5 %collective-permute-start.7 = (bf16[3,64,1024]{2,1,0:T(8,128)(2,1)S(1)}, bf16[3,64,1024]{2,1,0:T(8,128)(2,1)S(1)}, u32[]{:S(2)}, u32[]{:S(2)}) collective-permute-start(bf16[3,64,1024]{2,1,0:T(8,128)(2,1)S(1)} %constant_dynamic-slice_fusion), channel_id=1, source_target_pairs={{0,16},{1,17},{2,18},{3,19},{4,20},{5,21},{6,22},{7,23},{8,24},{9,... | collective-permute-start | bytes 1179656 | tf_op jit(solution)/shard_map/ppermute | solution.py:105
  18.4 18.4 %collective-permute-start.9 = (bf16[3,64,1024]{2,1,0:T(8,128)(2,1)S(1)}, bf16[3,64,1024]{2,1,0:T(8,128)(2,1)S(1)}, u32[]{:S(2)}, u32[]{:S(2)}) collective-permute-start(bf16[3,64,1024]{2,1,0:T(8,128)(2,1)S(1)} %constant_dynamic-slice_fusion), channel_id=1, source_target_pairs={{0,4},{1,5},{2,6},{3,7},{4,0},{5,1},{6,2},{7,3},{8,12},{9,13},{10,... | collective-permute-start | bytes 1179656 | tf_op jit(solution)/shard_map/ppermute | solution.py:105
  34.6 22.7 %collective-permute-start.1 = (bf16[136,2048]{1,0:T(8,128)(2,1)S(1)}, bf16[136,2048]{1,0:T(8,128)(2,1)S(1)}, u32[]{:S(2)}, u32[]{:S(2)}) collective-permute-start(bf16[136,2048]{1,0:T(8,128)(2,1)S(1)} %pad_maximum_fusion.12), channel_id=1, source_target_pairs={{0,2},{1,3},{2,0},{3,1},{4,6},{5,7},{6,4},{7,5},{8,10},{9,11},{10,... | collective-permute-start | bytes 1671176 | tf_op jit(solution)/shard_map/ppermute | solution.py:105
  35.9 12.6 %collective-permute-start.15 = (bf16[64,2048]{1,0:T(8,128)(2,1)S(1)}, bf16[64,2048]{1,0:T(8,128)(2,1)}, u32[]{:S(2)}, u32[]{:S(2)}) collective-permute-start(bf16[64,2048]{1,0:T(8,128)(2,1)S(1)} %get-tuple-element.5), channel_id=1, source_target_pairs={{0,8},{1,9},{2,10},{3,11},{4,12},{5,13},{6,14},{7,15},{8,0},{9,1},... | collective-permute-start | bytes 786440 | tf_op jit(solution)/shard_map/ppermute | solution.py:105
  35.9 19.5 %collective-permute-start.3 = (bf16[72,2048]{1,0:T(8,128)(2,1)S(1)}, bf16[72,2048]{1,0:T(8,128)(2,1)S(1)}, u32[]{:S(2)}, u32[]{:S(2)}) collective-permute-start(bf16[72,2048]{1,0:T(8,128)(2,1)S(1)} %collective-permute-done.2), channel_id=1, source_target_pairs={{0,2},{1,3},{2,0},{3,1},{4,6},{5,7},{6,4},{7,5},{8,10},{9,11},{10,... | collective-permute-start | bytes 884744 | tf_op jit(solution)/shard_map/ppermute | solution.py:105
  36.8 20.1 %collective-permute-start.10 = (bf16[3,64,512]{2,1,0:T(8,128)(2,1)S(1)}, bf16[3,64,512]{2,1,0:T(8,128)(2,1)S(1)}, u32[]{:S(2)}, u32[]{:S(2)}) collective-permute-start(bf16[3,64,512]{2,1,0:T(8,128)(2,1)S(1)} %slice.346), channel_id=1, source_target_pairs={{0,16},{1,17},{2,18},{3,19},{4,20},{5,21},{6,22},{7,23},{8,24},{9,... | collective-permute-start | bytes 589832 | tf_op jit(solution)/shard_map/ppermute | solution.py:105
  38.4 18.6 %collective-permute-start.11 = (bf16[3,64,512]{2,1,0:T(8,128)(2,1)S(1)}, bf16[3,64,512]{2,1,0:T(8,128)(2,1)S(1)}, u32[]{:S(2)}, u32[]{:S(2)}) collective-permute-start(bf16[3,64,512]{2,1,0:T(8,128)(2,1)S(1)} %slice.347), channel_id=1, source_target_pairs={{0,4},{1,5},{2,6},{3,7},{4,0},{5,1},{6,2},{7,3},{8,12},{9,13},{10,... | collective-permute-start | bytes 589832 | tf_op jit(solution)/shard_map/ppermute | solution.py:105
  48.5 14.0 %collective-permute-start.8 = (bf16[3,64,2048]{2,1,0:T(8,128)(2,1)S(1)}, bf16[3,64,2048]{2,1,0:T(8,128)(2,1)S(1)}, u32[]{:S(2)}, u32[]{:S(2)}) collective-permute-start(bf16[3,64,2048]{2,1,0:T(8,128)(2,1)S(1)} %bitcast.144), channel_id=1, source_target_pairs={{0,1},{1,0},{2,3},{3,2},{4,5},{5,4},{6,7},{7,6},{8,9},{9,8},{10,11... | collective-permute-start | bytes 2359304 | tf_op jit(solution)/shard_map/ppermute | solution.py:105
  55.4 11.9 %collective-permute-start.16 = (bf16[64,2048]{1,0:T(8,128)(2,1)}, bf16[64,2048]{1,0:T(8,128)(2,1)}, u32[]{:S(2)}, u32[]{:S(2)}) collective-permute-start(bf16[64,2048]{1,0:T(8,128)(2,1)} %collective-permute-done.15), channel_id=1, source_target_pairs={{0,2},{1,3},{2,0},{3,1},{4,6},{5,7},{6,4},{7,5},{8,10},{9,11},{10,... | collective-permute-start | bytes 786440 | tf_op jit(solution)/shard_map/ppermute | solution.py:105
  57.2 5.2 %collective-permute-start.12 = (bf16[3,64,2048]{2,1,0:T(8,128)(2,1)S(1)}, bf16[3,64,2048]{2,1,0:T(8,128)(2,1)}, u32[]{:S(2)}, u32[]{:S(2)}) collective-permute-start(bf16[3,64,2048]{2,1,0:T(8,128)(2,1)S(1)} %bitcast.146), channel_id=1, source_target_pairs={{0,1},{1,0},{2,3},{3,2},{4,5},{5,4},{6,7},{7,6},{8,9},{9,8},{10,11... | collective-permute-start | bytes 2359304 | tf_op jit(solution)/shard_map/ppermute | solution.py:105
  67.2 4.4 %copy-start.7 = (s32[8]{0:T(128)S(1)}, s32[8]{0:T(128)}, u32[]{:S(2)}) copy-start(s32[8]{0:T(128)} %constant.75.clone) | copy-start | bytes 100
  67.2 11.8 %collective-permute-start.13 = (bf16[392,384]{1,0:T(8,128)(2,1)S(1)}, bf16[392,384]{1,0:T(8,128)(2,1)S(1)}, u32[]{:S(2)}, u32[]{:S(2)}) collective-permute-start(bf16[392,384]{1,0:T(8,128)(2,1)S(1)} %pad_maximum_fusion.14), channel_id=1, source_target_pairs={{0,4},{1,5},{2,6},{3,7},{4,0},{5,1},{6,2},{7,3},{8,12},{9,13},{10,... | collective-permute-start | bytes 903176 | tf_op jit(solution)/shard_map/ppermute | solution.py:105
  69.6 9.4 %collective-permute-start.17 = (bf16[128,384]{1,0:T(8,128)(2,1)S(1)}, bf16[128,384]{1,0:T(8,128)(2,1)S(1)}, u32[]{:S(2)}, u32[]{:S(2)}) collective-permute-start(bf16[128,384]{1,0:T(8,128)(2,1)S(1)} %get-tuple-element.21), channel_id=1, source_target_pairs={{0,4},{1,5},{2,6},{3,7},{4,0},{5,1},{6,2},{7,3},{8,12},{9,13},{10,... | collective-permute-start | bytes 294920 | tf_op jit(solution)/shard_map/ppermute | solution.py:105
  78.9 2.5 %collective-permute-start.18 = (bf16[256,256]{1,0:T(8,128)(2,1)S(1)}, bf16[256,256]{1,0:T(8,128)(2,1)S(1)}, u32[]{:S(2)}, u32[]{:S(2)}) collective-permute-start(bf16[256,256]{1,0:T(8,128)(2,1)S(1)} %pad_maximum_fusion.16), channel_id=1, source_target_pairs={{0,1},{1,0},{2,3},{3,2},{4,5},{5,4},{6,7},{7,6},{8,9},{9,8},{10,11... | collective-permute-start | bytes 393224 | tf_op jit(solution)/shard_map/ppermute | solution.py:105
  79.2 1.9 %collective-permute-start.14 = (bf16[776,256]{1,0:T(8,128)(2,1)S(1)}, bf16[776,256]{1,0:T(8,128)(2,1)S(1)}, u32[]{:S(2)}, u32[]{:S(2)}) collective-permute-start(bf16[776,256]{1,0:T(8,128)(2,1)S(1)} %fusion.24), channel_id=1, source_target_pairs={{0,1},{1,0},{2,3},{3,2},{4,5},{5,4},{6,7},{7,6},{8,9},{9,8},{10,11... | collective-permute-start | bytes 1191944 | tf_op jit(solution)/shard_map/ppermute | solution.py:105
  (6 other events, 8.6 us)

commit v13 on v12

--- a/solution.py
+++ b/solution.py
@@ -159,14 +159,12 @@
     far_late_and = xor_swap(jnp.concatenate([late, row], axis=0), Z1)
     far_late = far_late_and[:part]
     far_early = xor_swap(early + zero_after(far_late), Z1)
-    beside_and = xor_swap(jnp.concatenate([own, row], axis=0), Y)
-    beside = beside_and[:tok_rows]
-    far_beside_late_and = xor_swap(far_late_and, Y)
+    beside = xor_swap(own, Y)
+    far_beside_late_and = xor_swap(jnp.concatenate([far_late_and, row], axis=0), Y)
     far_beside_late = far_beside_late_and[:part]
     far_beside_early = xor_swap(far_early, Y)
-    groups = [group] + [
-        rows[-MORE, :tok_rows] for rows in (beside_and, far_late_and, far_beside_late_and)
-    ]
+    groups = [group, far_beside_late_and[-MORE, :tok_rows]]
+    groups += [rows[part, :tok_rows] for rows in (far_late_and, far_beside_late_and)]
 
     half = features // 2
     held = lax.dynamic_slice_in_dim(qkv_weight.T, grp * half, half, 1).reshape(3, HD // 2, half)

time: 101 us -> 96.2 us (0.952)
  starting transfers between devices: 27.1 us -> 24 us
  local copies, waits for them, and re-layouts: 11.3 us -> 8.78 us
  waiting for transfers between devices: 34.7 us -> 35.9 us
    ppermute x15, starting transfers between devices: 15.5 us -> 12.4 us  [xor_swap(): return lax.ppermute(value, axes, [(d, d ^ bit) for d in range(count)])]
    unnamed x29, local copies, waits for them, and re-layouts: 5.99 us -> 3.75 us
    concatenate x1, local copies, waits for them, and re-layouts: 1.67 us -> 0.02 us  [body_by_head(): jnp.concatenate([own, beside, far_late, far_beside_late], axis=0)]
    ppermute x15, waiting for transfers between devices: 34.7 us -> 35.9 us  [xor_swap(): return lax.ppermute(value, axes, [(d, d ^ bit) for d in range(count)])]
    another operation x5, other arithmetic: 1.79 us -> 0.62 us  [by_bit(): jnp.stack([jnp.where(bit == 0, mine, theirs), jnp.where(bit == 0, theirs,...]
  transfers between devices with their start and end apart: 19 -> 19, of which waited for: 5 -> 6; matrix products, arithmetic and copies ran while one was open for 14% -> 13% of each run, Pallas kernels for 0% -> 0%
where the time goes in v13:
time: 96.2 us; the launch traced here: 95.8 us
  waiting for transfers between devices  35.9 us (37%)
  starting transfers between devices  24 us (25%)
  blocking collectives  12.5 us (13%)
  local copies, waits for them, and re-layouts  8.78 us (9%)
  matrix products  7.51 us (8%)
  other arithmetic  5.05 us (5%)
  between operations  1.97 us (2%)
    ppermute x15, waiting for transfers between devices, xor_swap(): return lax.ppermute(value, axes, [(d, d ^ bit) for d in range(count)])  35.9 us
    all_to_all x1, blocking collectives, body_by_head(): lax.all_to_all(sent, 'chip', split_axis=0, concat_axis=0, tiled=True)  12.5 us
    ppermute x15, starting transfers between devices, xor_swap(): return lax.ppermute(value, axes, [(d, d ^ bit) for d in range(count)])  12.4 us
    ppermute x3, starting transfers between devices, body_by_head(): lax.ppermute(held[j], both, [(d, (3 * d + j) % devices) for d in range(de...  8.43 us
    unnamed x29, local copies, waits for them, and re-layouts  3.75 us
    dot_general x2, matrix products, project(): lax.dot_general(rows, two_heads, (((1,), (1,)), ((), ())), preferred_elem...  3.64 us
    ppermute x1, starting transfers between devices, body_by_head(): lax.ppermute(frames[tok_rows - (KW - 1):], both, [(i, i + 1) for i in ran...  3.2 us
    dot_general x1, matrix products, body_by_head(): lax.dot_general(query, keyed[:, :HD], (((1,), (1,)), ((), ())), preferred...  2.27 us
  transfers between devices with their start and end apart: 19, of which 6 were waited for; matrix products, arithmetic and copies ran while one was open for 13% of the time, Pallas kernels for 0%

profile of v13, /device:TPU:0, one launch (start us, length us, event | category | flops | bytes accessed | tf_op | source)
XLA Modules:
  0.0 95.8 jit_solution(54406905352289477)
XLA Ops:
  0.0 1.2 %copy-done = bf16[2048,192]{0,1:T(8,128)(2,1)S(1)} copy-done((bf16[2048,192]{0,1:T(8,128)(2,1)S(1)}, bf16[2048,192]{0,1:T(8,128)(2,1)}, u32[]{:S(2)}) %copy-start) | copy-done | bytes 786456
  1.9 3.8 %collective-permute-start.5 = (bf16[64,1024]{1,0:T(8,128)(2,1)S(1)}, bf16[64,1024]{1,0:T(8,128)(2,1)S(1)}, u32[]{:S(2)}, u32[]{:S(2)}) collective-permute-start(bf16[64,1024]{1,0:T(8,128)(2,1)S(1)} %get-tuple-element.18), channel_id=1, source_target_pairs={{0,1},{1,4},{2,7},{3,10},{4,13},{5,0},{6,3},{7,6},{8,9},{9,12},{10... | collective-permute-start | bytes 393224 | tf_op jit(solution)/shard_map/ppermute | solution.py:172
  5.7 3.9 %collective-permute-start.6 = (bf16[64,1024]{1,0:T(8,128)(2,1)S(1)}, bf16[64,1024]{1,0:T(8,128)(2,1)S(1)}, u32[]{:S(2)}, u32[]{:S(2)}) collective-permute-start(bf16[64,1024]{1,0:T(8,128)(2,1)S(1)} %get-tuple-element.17), channel_id=1, source_target_pairs={{0,2},{1,5},{2,8},{3,11},{4,14},{5,1},{6,4},{7,7},{8,10},{9,13},{1... | collective-permute-start | bytes 393224 | tf_op jit(solution)/shard_map/ppermute | solution.py:172
  10.5 3.2 %collective-permute-start.2 = (bf16[3,2048]{1,0:T(4,128)(2,1)S(1)}, bf16[3,2048]{1,0:T(4,128)(2,1)S(1)}, u32[]{:S(2)}, u32[]{:S(2)}) collective-permute-start(bf16[3,2048]{1,0:T(4,128)(2,1)S(1)} %slice.260), channel_id=1, source_target_pairs={{0,1},{1,2},{2,3},{3,4},{4,5},{5,6},{6,7},{7,8},{8,9},{9,10},{10,1... | collective-permute-start | bytes 36872 | tf_op jit(solution)/shard_map/ppermute | solution.py:150
  15.2 1.4 %collective-permute-start = (bf16[72,2048]{1,0:T(8,128)(2,1)S(1)}, bf16[72,2048]{1,0:T(8,128)(2,1)S(1)}, u32[]{:S(2)}, u32[]{:S(2)}) collective-permute-start(bf16[72,2048]{1,0:T(8,128)(2,1)S(1)} %pad_maximum_fusion.16), channel_id=1, source_target_pairs={{0,8},{1,9},{2,10},{3,11},{4,12},{5,13},{6,14},{7,15},{8,0},{9,1},... | collective-permute-start | bytes 884744 | tf_op jit(solution)/shard_map/ppermute | solution.py:105
  16.8 1.6 %collective-permute-start.7 = (bf16[3,64,1024]{2,1,0:T(8,128)(2,1)S(1)}, bf16[3,64,1024]{2,1,0:T(8,128)(2,1)S(1)}, u32[]{:S(2)}, u32[]{:S(2)}) collective-permute-start(bf16[3,64,1024]{2,1,0:T(8,128)(2,1)S(1)} %constant_dynamic-slice_fusion), channel_id=1, source_target_pairs={{0,16},{1,17},{2,18},{3,19},{4,20},{5,21},{6,22},{7,23},{8,24},{9,... | collective-permute-start | bytes 1179656 | tf_op jit(solution)/shard_map/ppermute | solution.py:105
  18.4 2.5 %collective-permute-start.9 = (bf16[3,64,1024]{2,1,0:T(8,128)(2,1)S(1)}, bf16[3,64,1024]{2,1,0:T(8,128)(2,1)S(1)}, u32[]{:S(2)}, u32[]{:S(2)}) collective-permute-start(bf16[3,64,1024]{2,1,0:T(8,128)(2,1)S(1)} %constant_dynamic-slice_fusion), channel_id=1, source_target_pairs={{0,4},{1,5},{2,6},{3,7},{4,0},{5,1},{6,2},{7,3},{8,12},{9,13},{10,... | collective-permute-start | bytes 1179656 | tf_op jit(solution)/shard_map/ppermute | solution.py:105
  20.9 11.4 %collective-permute-done = bf16[72,2048]{1,0:T(8,128)(2,1)S(1)} collective-permute-done((bf16[72,2048]{1,0:T(8,128)(2,1)S(1)}, bf16[72,2048]{1,0:T(8,128)(2,1)S(1)}, u32[]{:S(2)}, u32[]{:S(2)}) %collective-permute-start) | collective-permute-done | bytes 294944 | tf_op jit(solution)/shard_map/ppermute | solution.py:105
  35.4 1.2 %collective-permute-start.3 = (bf16[128,2048]{1,0:T(8,128)(2,1)}, bf16[128,2048]{1,0:T(8,128)(2,1)}, u32[]{:S(2)}, u32[]{:S(2)}) collective-permute-start(bf16[128,2048]{1,0:T(8,128)(2,1)} %pad_maximum_fusion.12), channel_id=1, source_target_pairs={{0,2},{1,3},{2,0},{3,1},{4,6},{5,7},{6,4},{7,5},{8,10},{9,11},{10,... | collective-permute-start | bytes 1572872 | tf_op jit(solution)/shard_map/ppermute | solution.py:105
  38.9 1.5 %collective-permute-start.10 = (bf16[3,64,512]{2,1,0:T(8,128)(2,1)}, bf16[3,64,512]{2,1,0:T(8,128)(2,1)S(1)}, u32[]{:S(2)}, u32[]{:S(2)}) collective-permute-start(bf16[3,64,512]{2,1,0:T(8,128)(2,1)} %slice.341), channel_id=1, source_target_pairs={{0,16},{1,17},{2,18},{3,19},{4,20},{5,21},{6,22},{7,23},{8,24},{9,... | collective-permute-start | bytes 589832 | tf_op jit(solution)/shard_map/ppermute | solution.py:105
  41.0 9.6 %collective-permute-done.15 = bf16[64,2048]{1,0:T(8,128)(2,1)} collective-permute-done((bf16[64,2048]{1,0:T(8,128)(2,1)S(1)}, bf16[64,2048]{1,0:T(8,128)(2,1)}, u32[]{:S(2)}, u32[]{:S(2)}) %collective-permute-start.15) | collective-permute-done | bytes 262176 | tf_op jit(solution)/shard_map/ppermute | solution.py:105
  50.7 5.7 %collective-permute-done.1 = bf16[80,2048]{1,0:T(8,128)(2,1)S(1)} collective-permute-done((bf16[80,2048]{1,0:T(8,128)(2,1)S(1)}, bf16[80,2048]{1,0:T(8,128)(2,1)S(1)}, u32[]{:S(2)}, u32[]{:S(2)}) %collective-permute-start.1) | collective-permute-done | bytes 327712 | tf_op jit(solution)/shard_map/ppermute | solution.py:105
  56.4 1.5 %collective-permute-start.16 = (bf16[64,2048]{1,0:T(8,128)(2,1)}, bf16[64,2048]{1,0:T(8,128)(2,1)}, u32[]{:S(2)}, u32[]{:S(2)}) collective-permute-start(bf16[64,2048]{1,0:T(8,128)(2,1)} %collective-permute-done.15), channel_id=1, source_target_pairs={{0,2},{1,3},{2,0},{3,1},{4,6},{5,7},{6,4},{7,5},{8,10},{9,11},{10,... | collective-permute-start | bytes 786440 | tf_op jit(solution)/shard_map/ppermute | solution.py:105
  58.3 1.1 %copy-done.6 = bf16[384,2048]{1,0:T(8,128)(2,1)S(1)} copy-done((bf16[384,2048]{1,0:T(8,128)(2,1)S(1)}, bf16[384,2048]{1,0:T(8,128)(2,1)}, u32[]{:S(2)}) %copy-start.6) | copy-done | bytes 1572888
  59.4 1.1 %constant_dynamic-update-slice_fusion = bf16[384,2048]{1,0:T(8,128)(2,1)S(1)} fusion(bf16[384,2048]{1,0:T(8,128)(2,1)S(1)} %copy-done.6, bf16[128,2048]{1,0:T(8,128)(2,1)} %collective-permute-done.3), kind=kLoop, calls=%fused_computation.86 | loop fusion | bytes 1048576
  61.3 1.4 %fusion.4 = bf16[384,768]{1,0:T(8,128)(2,1)S(1)} fusion(bf16[384,2048]{1,0:T(8,128)(2,1)S(1)} %slice_dynamic-update-slice_fusion, bf16[384,2048]{1,0:T(8,128)(2,1)S(1)} %bitcast.150, bf16[384,2048]{1,0:T(8,128)(2,1)S(1)} %bitcast.148), kind=kOutput, calls=%fused_computation.10 | convolution fusion | flops 1214545920 | bytes 5308416 | tf_op jit(solution)/shard_map/dot_general | solution.py:197
  64.0 2.2 %fusion.6 = bf16[128,768]{1,0:T(8,128)(2,1)S(1)} fusion(bf16[384,2048]{1,0:T(8,128)(2,1)S(1)} %bitcast.151, bf16[384,2048]{1,0:T(8,128)(2,1)S(1)} %bitcast.149, bf16[64,2048]{1,0:T(8,128)(2,1)} %collective-permute-done.16, bf16[64,2048]{1,0:T(8,128)(2,1)} %collective-permute-done.15), kind=kOutput, calls=%fused_computation.12 | convolution fusion | flops 410091520 | bytes 3866624 | tf_op jit(solution)/shard_map/dot_general | solution.py:197
  66.2 1.1 %collective-permute-start.17 = (bf16[128,384]{1,0:T(8,128)(2,1)S(1)}, bf16[128,384]{1,0:T(8,128)(2,1)S(1)}, u32[]{:S(2)}, u32[]{:S(2)}) collective-permute-start(bf16[128,384]{1,0:T(8,128)(2,1)S(1)} %get-tuple-element.23), channel_id=1, source_target_pairs={{0,4},{1,5},{2,6},{3,7},{4,0},{5,1},{6,2},{7,3},{8,12},{9,13},{10,... | collective-permute-start | bytes 294920 | tf_op jit(solution)/shard_map/ppermute | solution.py:105
  67.3 6.9 %collective-permute-done.17 = bf16[128,384]{1,0:T(8,128)(2,1)S(1)} collective-permute-done((bf16[128,384]{1,0:T(8,128)(2,1)S(1)}, bf16[128,384]{1,0:T(8,128)(2,1)S(1)}, u32[]{:S(2)}, u32[]{:S(2)}) %collective-permute-start.17) | collective-permute-done | bytes 98336 | tf_op jit(solution)/shard_map/ppermute | solution.py:105
  75.3 1.1 %collective-permute-done.14 = bf16[776,256]{1,0:T(8,128)(2,1)S(1)} collective-permute-done((bf16[776,256]{1,0:T(8,128)(2,1)S(1)}, bf16[776,256]{1,0:T(8,128)(2,1)S(1)}, u32[]{:S(2)}, u32[]{:S(2)}) %collective-permute-start.14) | collective-permute-done | bytes 397344 | tf_op jit(solution)/shard_map/ppermute | solution.py:105
  76.8 2.3 %fusion.55 = (f32[1024]{0:T(1024)S(1)}, f32[1024,2048]{1,0:T(8,128)S(1)}) fusion(bf16[2048,256]{1,0:T(8,128)(2,1)S(1)} %fusion.8, bf16[128,384]{1,0:T(8,128)(2,1)S(1)} %collective-permute-done.17, bf16[128,384]{1,0:T(8,128)(2,1)S(1)} %get-tuple-element.22, bf16[384,384]{1,0:T(8,128)(2,1)S(1)} %slice.347, bf16[384,384]{1,0:T(8,128)(2,1)S(1)} %get-tuple-element.15, ...), kind=kOutput, calls=%fused_computation.158 | convolution fusion | flops 550501376 | bytes 9719808 | tf_op jit(solution)/shard_map/dot_general | solution.py:241
  79.1 1.3 %fusion = f32[1024]{0:T(1024)S(1)} fusion(f32[1024,2048]{1,0:T(8,128)S(1)} %get-tuple-element.55, f32[1024]{0:T(1024)S(1)} %get-tuple-element.54), kind=kLoop, calls=%fused_computation.3 | loop fusion | flops 4193280 | bytes 8396800 | tf_op jit(solution)/shard_map/reduce_sum | solution.py:247
  80.4 1.6 %fusion.5 = bf16[1024,128]{1,0:T(8,128)(2,1)S(1)} fusion(f32[1024,2048]{1,0:T(8,128)S(1)} %get-tuple-element.55, f32[1024]{0:T(1024)S(1)} %fusion, f32[1024]{0:T(1024)S(1)} %get-tuple-element.54, bf16[2048,256]{1,0:T(8,128)(2,1)S(1)} %fusion.8), kind=kOutput, calls=%fused_computation.11 | convolution fusion | flops 543293440 | bytes 9183232 | tf_op jit(solution)/shard_map/dot_general | solution.py:248
  82.2 12.5 %all_to_all.5 = bf16[8,128,128]{2,1,0:T(8,128)(2,1)S(1)} all-to-all(bf16[8,128,128]{2,1,0:T(8,128)(2,1)S(1)} %fusion.36), channel_id=1, replica_groups=mesh['grp'=2,'chip'=8,'core'=2] {'chip'}, dimensions={0} | all-to-all | bytes 524288 | tf_op jit(solution)/shard_map/all_to_all | solution.py:257
  (129 shorter events, 12.7 us)
Async XLA Ops:
  0.0 14.9 %copy-start.1 = (bf16[128,2048]{1,0:T(8,128)(2,1)S(1)}, bf16[128,2048]{1,0:T(8,128)(2,1)}, u32[]{:S(2)}) copy-start(bf16[128,2048]{1,0:T(8,128)(2,1)} %param.7) | copy-start | bytes 1572868
  0.0 14.7 %copy-start.4 = (bf16[4,2048]{1,0:T(4,128)(2,1)S(1)}, bf16[4,2048]{1,0:T(4,128)(2,1)}, u32[]{:S(2)}) copy-start(bf16[4,2048]{1,0:T(4,128)(2,1)} %param.8) | copy-start | bytes 49156
  0.0 14.8 %copy-start.9 = (s32[128]{0:T(128)S(1)}, s32[128]{0:T(128)}, u32[]{:S(2)}) copy-start(s32[128]{0:T(128)} %param.10) | copy-start | bytes 1540
  0.0 14.8 %copy-start.8 = (s32[64]{0:T(128)S(1)}, s32[64]{0:T(128)}, u32[]{:S(2)}) copy-start(s32[64]{0:T(128)} %param.11) | copy-start | bytes 772
  1.3 15.4 %collective-permute-start.4 = (bf16[64,1024]{1,0:T(8,128)(2,1)S(1)}, bf16[64,1024]{1,0:T(8,128)(2,1)S(1)}, u32[]{:S(2)}, u32[]{:S(2)}) collective-permute-start(bf16[64,1024]{1,0:T(8,128)(2,1)S(1)} %get-tuple-element.19), channel_id=1, source_target_pairs={{0,0},{1,3},{2,6},{3,9},{4,12},{5,15},{6,2},{7,5},{8,8},{9,11},{10... | collective-permute-start | bytes 393224 | tf_op jit(solution)/shard_map/ppermute | solution.py:172
  1.9 14.8 %collective-permute-start.5 = (bf16[64,1024]{1,0:T(8,128)(2,1)S(1)}, bf16[64,1024]{1,0:T(8,128)(2,1)S(1)}, u32[]{:S(2)}, u32[]{:S(2)}) collective-permute-start(bf16[64,1024]{1,0:T(8,128)(2,1)S(1)} %get-tuple-element.18), channel_id=1, source_target_pairs={{0,1},{1,4},{2,7},{3,10},{4,13},{5,0},{6,3},{7,6},{8,9},{9,12},{10... | collective-permute-start | bytes 393224 | tf_op jit(solution)/shard_map/ppermute | solution.py:172
  5.7 11.0 %collective-permute-start.6 = (bf16[64,1024]{1,0:T(8,128)(2,1)S(1)}, bf16[64,1024]{1,0:T(8,128)(2,1)S(1)}, u32[]{:S(2)}, u32[]{:S(2)}) collective-permute-start(bf16[64,1024]{1,0:T(8,128)(2,1)S(1)} %get-tuple-element.17), channel_id=1, source_target_pairs={{0,2},{1,5},{2,8},{3,11},{4,14},{5,1},{6,4},{7,7},{8,10},{9,13},{1... | collective-permute-start | bytes 393224 | tf_op jit(solution)/shard_map/ppermute | solution.py:172
  10.5 6.1 %collective-permute-start.2 = (bf16[3,2048]{1,0:T(4,128)(2,1)S(1)}, bf16[3,2048]{1,0:T(4,128)(2,1)S(1)}, u32[]{:S(2)}, u32[]{:S(2)}) collective-permute-start(bf16[3,2048]{1,0:T(4,128)(2,1)S(1)} %slice.260), channel_id=1, source_target_pairs={{0,1},{1,2},{2,3},{3,4},{4,5},{5,6},{6,7},{7,8},{8,9},{9,10},{10,1... | collective-permute-start | bytes 36872 | tf_op jit(solution)/shard_map/ppermute | solution.py:150
  15.2 17.1 %collective-permute-start = (bf16[72,2048]{1,0:T(8,128)(2,1)S(1)}, bf16[72,2048]{1,0:T(8,128)(2,1)S(1)}, u32[]{:S(2)}, u32[]{:S(2)}) collective-permute-start(bf16[72,2048]{1,0:T(8,128)(2,1)S(1)} %pad_maximum_fusion.16), channel_id=1, source_target_pairs={{0,8},{1,9},{2,10},{3,11},{4,12},{5,13},{6,14},{7,15},{8,0},{9,1},... | collective-permute-start | bytes 884744 | tf_op jit(solution)/shard_map/ppermute | solution.py:105
  16.8 21.0 %collective-permute-start.7 = (bf16[3,64,1024]{2,1,0:T(8,128)(2,1)S(1)}, bf16[3,64,1024]{2,1,0:T(8,128)(2,1)S(1)}, u32[]{:S(2)}, u32[]{:S(2)}) collective-permute-start(bf16[3,64,1024]{2,1,0:T(8,128)(2,1)S(1)} %constant_dynamic-slice_fusion), channel_id=1, source_target_pairs={{0,16},{1,17},{2,18},{3,19},{4,20},{5,21},{6,22},{7,23},{8,24},{9,... | collective-permute-start | bytes 1179656 | tf_op jit(solution)/shard_map/ppermute | solution.py:105
  18.4 19.8 %collective-permute-start.9 = (bf16[3,64,1024]{2,1,0:T(8,128)(2,1)S(1)}, bf16[3,64,1024]{2,1,0:T(8,128)(2,1)S(1)}, u32[]{:S(2)}, u32[]{:S(2)}) collective-permute-start(bf16[3,64,1024]{2,1,0:T(8,128)(2,1)S(1)} %constant_dynamic-slice_fusion), channel_id=1, source_target_pairs={{0,4},{1,5},{2,6},{3,7},{4,0},{5,1},{6,2},{7,3},{8,12},{9,13},{10,... | collective-permute-start | bytes 1179656 | tf_op jit(solution)/shard_map/ppermute | solution.py:105
  35.4 22.9 %collective-permute-start.3 = (bf16[128,2048]{1,0:T(8,128)(2,1)}, bf16[128,2048]{1,0:T(8,128)(2,1)}, u32[]{:S(2)}, u32[]{:S(2)}) collective-permute-start(bf16[128,2048]{1,0:T(8,128)(2,1)} %pad_maximum_fusion.12), channel_id=1, source_target_pairs={{0,2},{1,3},{2,0},{3,1},{4,6},{5,7},{6,4},{7,5},{8,10},{9,11},{10,... | collective-permute-start | bytes 1572872 | tf_op jit(solution)/shard_map/ppermute | solution.py:105
  36.7 19.7 %collective-permute-start.1 = (bf16[80,2048]{1,0:T(8,128)(2,1)S(1)}, bf16[80,2048]{1,0:T(8,128)(2,1)S(1)}, u32[]{:S(2)}, u32[]{:S(2)}) collective-permute-start(bf16[80,2048]{1,0:T(8,128)(2,1)S(1)} %pad_maximum_fusion.14), channel_id=1, source_target_pairs={{0,2},{1,3},{2,0},{3,1},{4,6},{5,7},{6,4},{7,5},{8,10},{9,11},{10,... | collective-permute-start | bytes 983048 | tf_op jit(solution)/shard_map/ppermute | solution.py:105
  37.6 13.1 %collective-permute-start.15 = (bf16[64,2048]{1,0:T(8,128)(2,1)S(1)}, bf16[64,2048]{1,0:T(8,128)(2,1)}, u32[]{:S(2)}, u32[]{:S(2)}) collective-permute-start(bf16[64,2048]{1,0:T(8,128)(2,1)S(1)} %get-tuple-element.5), channel_id=1, source_target_pairs={{0,8},{1,9},{2,10},{3,11},{4,12},{5,13},{6,14},{7,15},{8,0},{9,1},... | collective-permute-start | bytes 786440 | tf_op jit(solution)/shard_map/ppermute | solution.py:105
  38.1 22.5 %collective-permute-start.8 = (bf16[3,64,2048]{2,1,0:T(8,128)(2,1)S(1)}, bf16[3,64,2048]{2,1,0:T(8,128)(2,1)S(1)}, u32[]{:S(2)}, u32[]{:S(2)}) collective-permute-start(bf16[3,64,2048]{2,1,0:T(8,128)(2,1)S(1)} %bitcast.144), channel_id=1, source_target_pairs={{0,1},{1,0},{2,3},{3,2},{4,5},{5,4},{6,7},{7,6},{8,9},{9,8},{10,11... | collective-permute-start | bytes 2359304 | tf_op jit(solution)/shard_map/ppermute | solution.py:105
  38.9 19.1 %collective-permute-start.10 = (bf16[3,64,512]{2,1,0:T(8,128)(2,1)}, bf16[3,64,512]{2,1,0:T(8,128)(2,1)S(1)}, u32[]{:S(2)}, u32[]{:S(2)}) collective-permute-start(bf16[3,64,512]{2,1,0:T(8,128)(2,1)} %slice.341), channel_id=1, source_target_pairs={{0,16},{1,17},{2,18},{3,19},{4,20},{5,21},{6,22},{7,23},{8,24},{9,... | collective-permute-start | bytes 589832 | tf_op jit(solution)/shard_map/ppermute | solution.py:105
  50.7 7.3 %collective-permute-start.11 = (bf16[3,64,512]{2,1,0:T(8,128)(2,1)}, bf16[3,64,512]{2,1,0:T(8,128)(2,1)S(1)}, u32[]{:S(2)}, u32[]{:S(2)}) collective-permute-start(bf16[3,64,512]{2,1,0:T(8,128)(2,1)} %slice.342), channel_id=1, source_target_pairs={{0,4},{1,5},{2,6},{3,7},{4,0},{5,1},{6,2},{7,3},{8,12},{9,13},{10,... | collective-permute-start | bytes 589832 | tf_op jit(solution)/shard_map/ppermute | solution.py:105
  56.4 7.6 %collective-permute-start.16 = (bf16[64,2048]{1,0:T(8,128)(2,1)}, bf16[64,2048]{1,0:T(8,128)(2,1)}, u32[]{:S(2)}, u32[]{:S(2)}) collective-permute-start(bf16[64,2048]{1,0:T(8,128)(2,1)} %collective-permute-done.15), channel_id=1, source_target_pairs={{0,2},{1,3},{2,0},{3,1},{4,6},{5,7},{6,4},{7,5},{8,10},{9,11},{10,... | collective-permute-start | bytes 786440 | tf_op jit(solution)/shard_map/ppermute | solution.py:105
  58.3 2.4 %collective-permute-start.12 = (bf16[3,64,2048]{2,1,0:T(8,128)(2,1)S(1)}, bf16[3,64,2048]{2,1,0:T(8,128)(2,1)S(1)}, u32[]{:S(2)}, u32[]{:S(2)}) collective-permute-start(bf16[3,64,2048]{2,1,0:T(8,128)(2,1)S(1)} %bitcast.146), channel_id=1, source_target_pairs={{0,1},{1,0},{2,3},{3,2},{4,5},{5,4},{6,7},{7,6},{8,9},{9,8},{10,11... | collective-permute-start | bytes 2359304 | tf_op jit(solution)/shard_map/ppermute | solution.py:105
  62.9 4.4 %copy-start.7 = (s32[8]{0:T(128)S(1)}, s32[8]{0:T(128)}, u32[]{:S(2)}) copy-start(s32[8]{0:T(128)} %constant.75.clone) | copy-start | bytes 100
  62.9 11.4 %collective-permute-start.13 = (bf16[392,384]{1,0:T(8,128)(2,1)S(1)}, bf16[392,384]{1,0:T(8,128)(2,1)S(1)}, u32[]{:S(2)}, u32[]{:S(2)}) collective-permute-start(bf16[392,384]{1,0:T(8,128)(2,1)S(1)} %pad_maximum_fusion.15), channel_id=1, source_target_pairs={{0,4},{1,5},{2,6},{3,7},{4,0},{5,1},{6,2},{7,3},{8,12},{9,13},{10,... | collective-permute-start | bytes 903176 | tf_op jit(solution)/shard_map/ppermute | solution.py:105
  66.2 8.0 %collective-permute-start.17 = (bf16[128,384]{1,0:T(8,128)(2,1)S(1)}, bf16[128,384]{1,0:T(8,128)(2,1)S(1)}, u32[]{:S(2)}, u32[]{:S(2)}) collective-permute-start(bf16[128,384]{1,0:T(8,128)(2,1)S(1)} %get-tuple-element.23), channel_id=1, source_target_pairs={{0,4},{1,5},{2,6},{3,7},{4,0},{5,1},{6,2},{7,3},{8,12},{9,13},{10,... | collective-permute-start | bytes 294920 | tf_op jit(solution)/shard_map/ppermute | solution.py:105
  74.3 2.5 %collective-permute-start.18 = (bf16[256,256]{1,0:T(8,128)(2,1)S(1)}, bf16[256,256]{1,0:T(8,128)(2,1)S(1)}, u32[]{:S(2)}, u32[]{:S(2)}) collective-permute-start(bf16[256,256]{1,0:T(8,128)(2,1)S(1)} %pad_maximum_fusion.17), channel_id=1, source_target_pairs={{0,1},{1,0},{2,3},{3,2},{4,5},{5,4},{6,7},{7,6},{8,9},{9,8},{10,11... | collective-permute-start | bytes 393224 | tf_op jit(solution)/shard_map/ppermute | solution.py:105
  74.5 1.9 %collective-permute-start.14 = (bf16[776,256]{1,0:T(8,128)(2,1)S(1)}, bf16[776,256]{1,0:T(8,128)(2,1)S(1)}, u32[]{:S(2)}, u32[]{:S(2)}) collective-permute-start(bf16[776,256]{1,0:T(8,128)(2,1)S(1)} %fusion.24), channel_id=1, source_target_pairs={{0,1},{1,0},{2,3},{3,2},{4,5},{5,4},{6,7},{7,6},{8,9},{9,8},{10,11... | collective-permute-start | bytes 1191944 | tf_op jit(solution)/shard_map/ppermute | solution.py:105
  (6 other events, 9.6 us)

commit v14 on v11

--- a/solution.py
+++ b/solution.py
@@ -105,19 +105,28 @@
     return lax.ppermute(value, axes, [(d, d ^ bit) for d in range(count)])
 
 
+MORE = 8
+
+
+def with_groups(rows, groups):
+    width = rows.shape[1]
+    flat = jnp.pad(groups.reshape(-1), (0, MORE * width - groups.size))
+    return jnp.concatenate([rows, flat.reshape(MORE, width)], axis=0)
+
+
+def groups_behind(rows, count, tok_rows):
+    return rows[-MORE:].reshape(-1)[: count * tok_rows].reshape(count, tok_rows)
+
+
 def by_bit(bit, mine, theirs, axis):
     return jnp.stack(
         [jnp.where(bit == 0, mine, theirs), jnp.where(bit == 0, theirs, mine)], axis=axis
     )
 
 
-def zero_after(*arrays):
-    total = jnp.zeros((), jnp.bfloat16)
-    for array in arrays:
-        last = array[(-1,) * array.ndim]
-        absent = last < 0 if array.dtype == jnp.int32 else last != last
-        total = total + jnp.where(absent, 1.0, 0.0).astype(jnp.bfloat16)
-    return total
+def zero_after(array):
+    last = array[(-1,) * array.ndim]
+    return jnp.where(last != last, 1.0, 0.0).astype(jnp.bfloat16)
 
 
 def body_by_head(frames, conv_weight, qkv_weight, track_ids, track_owner):
@@ -130,21 +139,20 @@
     me = 2 * chip + core
     both = ("chip", "core")
     every = ("grp", "chip", "core")
-    part = tok_rows // 2
     features = frames.shape[1]
     CORE, Y, Z0, Z1 = 1, 2, 4, 8
 
     rim_rows = lax.ppermute(
         frames[tok_rows - (KW - 1) :], both, [(i, i + 1) for i in range(devices - 1)]
     )
-    late = convolve(frames[part:], conv_weight, frames[part - (KW - 1) : part])
-    early = convolve(frames[:part], conv_weight, rim_rows)
-
-    far_late = xor_swap(late, Z1)
-    far_early = xor_swap(early + zero_after(far_late), Z1)
-    own = jnp.concatenate([early, late], axis=0)
+    hidden = convolve(frames, conv_weight, rim_rows)
+
+    group = track_groups(track_ids, track_owner).astype(jnp.bfloat16)
+    own = with_groups(hidden, group)
+    far = xor_swap(own, Z1)
     beside = xor_swap(own, Y)
-    far_beside_late = xor_swap(far_late, Y)
+    far_beside = xor_swap(far, Y)
+
     half = features // 2
     held = lax.dynamic_slice_in_dim(qkv_weight.T, grp * half, half, 1).reshape(3, HD // 2, half)
     moved = [
@@ -155,16 +163,6 @@
     mine_too = xor_swap(mine, devices, every)
     paired = xor_swap(mine, Z0)
 
-    span = devices * tok_rows
-    times = me * tok_rows + jnp.arange(tok_rows, dtype=jnp.int32)
-    codes = (track_groups(track_ids, track_owner) * span + times)[None, :]
-    codes = codes + zero_after(mine_too, paired).astype(jnp.int32)
-    for bit in (CORE, Y, Z0, Z1):
-        codes = jnp.concatenate([codes, xor_swap(codes, bit)], axis=0)
-        if bit == Y:
-            codes = codes + zero_after(far_beside_late).astype(jnp.int32)
-    far_beside_early = xor_swap(far_early + zero_after(codes), Y)
-
     cut = half // 2
     fourth = jnp.concatenate(
         [
@@ -174,42 +172,54 @@
         axis=2,
     )
 
-    def whole_head(quarter, quarter_too):
-        wide = by_bit(grp, quarter, quarter_too, 2).reshape(3, HD // 2, features)
+    def whole_head(quarter, quarter_too, zero):
+        wide = by_bit(grp, quarter, quarter_too, 2).reshape(3, HD // 2, features) + zero
         return by_bit(core, wide, xor_swap(wide, CORE), 1).reshape(3 * HD, features)
 
     two_heads = jnp.concatenate(
-        [whole_head(mine, mine_too), whole_head(paired, fourth)], axis=0
-    )
-
-    def project(rows):
+        [
+            whole_head(mine, mine_too, zero_after(beside)),
+            whole_head(paired, fourth, zero_after(far)),
+        ],
+        axis=0,
+    )
+
+    span = devices * tok_rows
+
+    def codes_of(groups, hops):
+        seen = jnp.array(hops, jnp.int32)[:, None] ^ me
+        times = seen * tok_rows + jnp.arange(tok_rows, dtype=jnp.int32)[None, :]
+        return (groups.astype(jnp.int32) * span + times).reshape(-1)
+
+    def project(blocks, hops):
+        groups = jnp.stack([rows[tok_rows, :tok_rows] for rows in blocks])
         done = lax.dot_general(
-            rows, two_heads, (((1,), (1,)), ((), ())), preferred_element_type=jnp.float32
+            jnp.concatenate([rows[:tok_rows] for rows in blocks], axis=0),
+            two_heads,
+            (((1,), (1,)), ((), ())),
+            preferred_element_type=jnp.float32,
         ).astype(jnp.bfloat16)
-        return jnp.concatenate([done[:, : 3 * HD], xor_swap(done[:, 3 * HD :], Z0)], axis=0)
-
-    first = project(jnp.concatenate([own, beside, far_late, far_beside_late], axis=0))
-    second = project(jnp.concatenate([far_early, far_beside_early], axis=0))
-
-    first_rows = [(0, 0, tok_rows), (Y, 0, tok_rows), (Z1, part, part), (Z1 | Y, part, part)]
-    second_rows = [(Z1, 0, part), (Z1 | Y, 0, part)]
-    order = []
-    for pieces in (first_rows, second_rows):
-        order += pieces + [(far ^ Z0, start, count) for far, start, count in pieces]
-
-    def codes_at(bit):
-        return jnp.concatenate(
-            [codes[far ^ bit, start : start + count] for far, start, count in order]
+        swapped = xor_swap(with_groups(done[:, 3 * HD :], groups), Z0)
+        done = jnp.concatenate([done[:, : 3 * HD], swapped[:-MORE]], axis=0)
+        groups = jnp.concatenate([groups, groups_behind(swapped, 2, tok_rows)], axis=0)
+        hops = hops + [hop ^ Z0 for hop in hops]
+        other = xor_swap(with_groups(done[:, HD:], groups), CORE)
+        other_groups = groups_behind(other, 4, tok_rows)
+        return (
+            (done[:, :HD], codes_of(groups, hops)),
+            (done[:, HD:], codes_of(groups, hops)),
+            (other[:-MORE], codes_of(other_groups, [hop ^ CORE for hop in hops])),
+            hops,
         )
 
-    asking = codes_at(0)
-    keys = jnp.concatenate([asking, codes_at(CORE)])
+    parts = [project([own, beside], [0, Y])]
+    zero = zero_after(parts[0][0][0])
+    parts.append(project([far, far_beside + zero], [Z1, Z1 | Y]))
+    query, asking = (jnp.concatenate([p[0][n] for p in parts], axis=0) for n in (0, 1))
+    keyed, keys = (
+        jnp.concatenate([p[side][n] for side in (1, 2) for p in parts], axis=0) for n in (0, 1)
+    )
     least = asking // span * span
-    projected = jnp.concatenate([first, second], axis=0)
-    query = projected[:, :HD]
-    keyed = jnp.concatenate(
-        [projected[:, HD:], xor_swap(first[:, HD:], CORE), xor_swap(second[:, HD:], CORE)], axis=0
-    )
     scores = lax.dot_general(
         query, keyed[:, :HD], (((1,), (1,)), ((), ())), preferred_element_type=jnp.float32
     ) * (1.0 / HD**0.5)
@@ -220,12 +230,10 @@
     mixed = jnp.dot(weights, keyed[:, HD:], preferred_element_type=jnp.float32)
     mixed = mixed.astype(jnp.bfloat16)
 
+    mixed = mixed.reshape(chips, tok_rows, HD)
     sent = jnp.zeros((chips, tok_rows, HD), jnp.bfloat16)
-    at = 0
-    for far, start, count in order:
-        rows = mixed[at : at + count]
-        sent = lax.dynamic_update_slice(sent, rows[None], ((me ^ far) >> 1, start, 0))
-        at += count
+    for n, hop in enumerate(parts[0][3] + parts[1][3]):
+        sent = lax.dynamic_update_slice(sent, mixed[n : n + 1], ((me ^ hop) >> 1, 0, 0))
     returned = lax.all_to_all(sent, "chip", split_axis=0, concat_axis=0, tiled=True)
     return returned.transpose(1, 0, 2).reshape(tok_rows, chips * HD)
 

time: 99.1 us -> 101 us (1.019)
  waiting for transfers between devices: 15.6 us -> 33.7 us
  starting transfers between devices: 34.6 us -> 21.6 us
  local copies, waits for them, and re-layouts: 16.4 us -> 13.5 us
  between operations: 6.76 us -> 4.54 us
  matrix products: 6.52 us -> 7.53 us
    ppermute x19 -> x13, waiting for transfers between devices: 15.6 us -> 33.7 us  [xor_swap(): return lax.ppermute(value, axes, [(d, d ^ bit) for d in range(count)])]
    ppermute x19 -> x13, starting transfers between devices: 23 us -> 9.96 us  [xor_swap(): return lax.ppermute(value, axes, [(d, d ^ bit) for d in range(count)])]
    slice x4 -> x19, local copies, waits for them, and re-layouts: 0.09 us -> 5.49 us  [the longest x3 3 us: project(): rows[:tok_rows]]
    unnamed x21, local copies, waits for them, and re-layouts: 6.08 us -> 1.59 us
    concatenate x3 -> x0, local copies, waits for them, and re-layouts: 1.84 us -> none  [the longest x1 1.67 us: body_by_head(): jnp.concatenate([own, beside, far_late, far_beside_late], axis=0)]
    slice x5 -> x3, local copies, waits for them, and re-layouts: 4.52 us -> 3.11 us  [zero_after(): last = array[(-1,) * array.ndim]]
    another operation x5, other arithmetic: 0.62 us -> 1.99 us  [by_bit(): jnp.stack([jnp.where(bit == 0, mine, theirs), jnp.where(bit == 0, theirs,...]
    dot_general x2, matrix products: 2.64 us -> 3.66 us  [project(): lax.dot_general(jnp.concatenate([rows[:tok_rows] for rows in blocks], axi...]
  transfers between devices with their start and end apart: 23 -> 17, of which waited for: 8 -> 6; matrix products, arithmetic and copies ran while one was open for 20% -> 15% of each run, Pallas kernels for 0% -> 0%
where the time goes in v14:
time: 101 us; the launch traced here: 100 us
  waiting for transfers between devices  33.7 us (33%)
  starting transfers between devices  21.6 us (21%)
  local copies, waits for them, and re-layouts  13.5 us (13%)
  blocking collectives  13.2 us (13%)
  matrix products  7.53 us (7%)
  other arithmetic  6.4 us (6%)
  between operations  4.54 us (4%)
    ppermute x13, waiting for transfers between devices, xor_swap(): return lax.ppermute(value, axes, [(d, d ^ bit) for d in range(count)])  33.7 us
    all_to_all x1, blocking collectives, body_by_head(): lax.all_to_all(sent, 'chip', split_axis=0, concat_axis=0, tiled=True)  13.2 us
    ppermute x13, starting transfers between devices, xor_swap(): return lax.ppermute(value, axes, [(d, d ^ bit) for d in range(count)])  9.96 us
    ppermute x3, starting transfers between devices, body_by_head(): lax.ppermute(held[j], both, [(d, (3 * d + j) % devices) for d in range(de...  8.43 us
    dot_general x2, matrix products, project(): lax.dot_general(jnp.concatenate([rows[:tok_rows] for rows in blocks], axi...  3.66 us
    ppermute x1, starting transfers between devices, body_by_head(): lax.ppermute(frames[tok_rows - (KW - 1):], both, [(i, i + 1) for i in ran...  3.2 us
    slice x3, local copies, waits for them, and re-layouts, zero_after(): last = array[(-1,) * array.ndim]  3.11 us
    slice x3, local copies, waits for them, and re-layouts, project(): rows[:tok_rows]  3 us
  transfers between devices with their start and end apart: 17, of which 6 were waited for; matrix products, arithmetic and copies ran while one was open for 15% of the time, Pallas kernels for 0%

profile of v14, /device:TPU:0, one launch (start us, length us, event | category | flops | bytes accessed | tf_op | source)
XLA Modules:
  0.0 100.5 jit_solution(16170853521621110761)
XLA Ops:
  0.0 1.1 %copy-done = bf16[2048,192]{0,1:T(8,128)(2,1)S(1)} copy-done((bf16[2048,192]{0,1:T(8,128)(2,1)S(1)}, bf16[2048,192]{0,1:T(8,128)(2,1)}, u32[]{:S(2)}) %copy-start) | copy-done | bytes 786456
  1.9 3.8 %collective-permute-start.3 = (bf16[64,1024]{1,0:T(8,128)(2,1)S(1)}, bf16[64,1024]{1,0:T(8,128)(2,1)S(1)}, u32[]{:S(2)}, u32[]{:S(2)}) collective-permute-start(bf16[64,1024]{1,0:T(8,128)(2,1)S(1)} %get-tuple-element.22), channel_id=1, source_target_pairs={{0,1},{1,4},{2,7},{3,10},{4,13},{5,0},{6,3},{7,6},{8,9},{9,12},{10... | collective-permute-start | bytes 393224 | tf_op jit(solution)/shard_map/ppermute | solution.py:159
  5.7 3.9 %collective-permute-start.4 = (bf16[64,1024]{1,0:T(8,128)(2,1)S(1)}, bf16[64,1024]{1,0:T(8,128)(2,1)S(1)}, u32[]{:S(2)}, u32[]{:S(2)}) collective-permute-start(bf16[64,1024]{1,0:T(8,128)(2,1)S(1)} %get-tuple-element.21), channel_id=1, source_target_pairs={{0,2},{1,5},{2,8},{3,11},{4,14},{5,1},{6,4},{7,7},{8,10},{9,13},{1... | collective-permute-start | bytes 393224 | tf_op jit(solution)/shard_map/ppermute | solution.py:159
  10.4 3.2 %collective-permute-start = (bf16[3,2048]{1,0:T(4,128)(2,1)S(1)}, bf16[3,2048]{1,0:T(4,128)(2,1)S(1)}, u32[]{:S(2)}, u32[]{:S(2)}) collective-permute-start(bf16[3,2048]{1,0:T(4,128)(2,1)S(1)} %slice.202), channel_id=1, source_target_pairs={{0,1},{1,2},{2,3},{3,4},{4,5},{5,6},{6,7},{7,8},{8,9},{9,10},{10,1... | collective-permute-start | bytes 36872 | tf_op jit(solution)/shard_map/ppermute | solution.py:145
  17.0 1.5 %collective-permute-start.5 = (bf16[3,64,1024]{2,1,0:T(8,128)(2,1)}, bf16[3,64,1024]{2,1,0:T(8,128)(2,1)S(1)}, u32[]{:S(2)}, u32[]{:S(2)}) collective-permute-start(bf16[3,64,1024]{2,1,0:T(8,128)(2,1)} %constant_dynamic-slice_fusion), channel_id=1, source_target_pairs={{0,16},{1,17},{2,18},{3,19},{4,20},{5,21},{6,22},{7,23},{8,24},{9,... | collective-permute-start | bytes 1179656 | tf_op jit(solution)/shard_map/ppermute | solution.py:105
  18.5 3.7 %collective-permute-start.7 = (bf16[3,64,1024]{2,1,0:T(8,128)(2,1)}, bf16[3,64,1024]{2,1,0:T(8,128)(2,1)S(1)}, u32[]{:S(2)}, u32[]{:S(2)}) collective-permute-start(bf16[3,64,1024]{2,1,0:T(8,128)(2,1)} %constant_dynamic-slice_fusion), channel_id=1, source_target_pairs={{0,4},{1,5},{2,6},{3,7},{4,0},{5,1},{6,2},{7,3},{8,12},{9,13},{10,... | collective-permute-start | bytes 1179656 | tf_op jit(solution)/shard_map/ppermute | solution.py:105
  22.7 2.1 %collective-permute-start.10 = (bf16[136,2048]{1,0:T(8,128)(2,1)S(1)}, bf16[136,2048]{1,0:T(8,128)(2,1)}, u32[]{:S(2)}, u32[]{:S(2)}) collective-permute-start(bf16[136,2048]{1,0:T(8,128)(2,1)S(1)} %pad_maximum_fusion.10), channel_id=1, source_target_pairs={{0,8},{1,9},{2,10},{3,11},{4,12},{5,13},{6,14},{7,15},{8,0},{9,1},... | collective-permute-start | bytes 1671176 | tf_op jit(solution)/shard_map/ppermute | solution.py:105
  24.8 12.9 %collective-permute-done.7 = bf16[3,64,1024]{2,1,0:T(8,128)(2,1)S(1)} collective-permute-done((bf16[3,64,1024]{2,1,0:T(8,128)(2,1)}, bf16[3,64,1024]{2,1,0:T(8,128)(2,1)S(1)}, u32[]{:S(2)}, u32[]{:S(2)}) %collective-permute-start.7) | collective-permute-done | bytes 393248 | tf_op jit(solution)/shard_map/ppermute | solution.py:105
  38.5 1.3 %slice.272 = bf16[1,1]{1,0:T(2,128)(2,1)} slice(bf16[136,2048]{1,0:T(8,128)(2,1)} %collective-permute-done.1), slice={[135:136], [2047:2048]} | slice | bytes 4 | tf_op jit(solution)/shard_map/slice | solution.py:128
  41.3 7.4 %collective-permute-done.10 = bf16[136,2048]{1,0:T(8,128)(2,1)} collective-permute-done((bf16[136,2048]{1,0:T(8,128)(2,1)S(1)}, bf16[136,2048]{1,0:T(8,128)(2,1)}, u32[]{:S(2)}, u32[]{:S(2)}) %collective-permute-start.10) | collective-permute-done | bytes 557088 | tf_op jit(solution)/shard_map/ppermute | solution.py:105
  48.7 1.3 %slice.275 = bf16[1,1]{1,0:T(2,128)(2,1)} slice(bf16[136,2048]{1,0:T(8,128)(2,1)} %collective-permute-done.10), slice={[135:136], [2047:2048]} | slice | bytes 4 | tf_op jit(solution)/shard_map/slice | solution.py:128
  52.7 1.1 %slice.268 = bf16[128,2048]{1,0:T(8,128)(2,1)S(1)} slice(bf16[136,2048]{1,0:T(8,128)(2,1)} %collective-permute-done.1), slice={[0:128], [0:2048]} | slice | bytes 1048576 | tf_op jit(solution)/shard_map/slice | solution.py:197
  53.8 1.1 %collective-permute-start.13 = (bf16[136,2048]{1,0:T(8,128)(2,1)}, bf16[136,2048]{1,0:T(8,128)(2,1)S(1)}, u32[]{:S(2)}, u32[]{:S(2)}) collective-permute-start(bf16[136,2048]{1,0:T(8,128)(2,1)} %collective-permute-done.10), channel_id=1, source_target_pairs={{0,2},{1,3},{2,0},{3,1},{4,6},{5,7},{6,4},{7,5},{8,10},{9,11},{10,... | collective-permute-start | bytes 1671176 | tf_op jit(solution)/shard_map/ppermute | solution.py:105
  54.9 1.6 %select_bitcast_fusion.1 = (bf16[3,1,64,2048]{3,2,0,1:T(8,128)(2,1)S(1)}, bf16[3,1,64,2048]{3,2,0,1:T(8,128)(2,1)S(1)}, bf16[3,1,64,2048]{3,2,0,1:T(8,128)(2,1)S(1)}, bf16[3,1,64,2048]{3,2,0,1:T(8,128)(2,1)S(1)}) fusion(bf16[3,64,2048]{2,1,0:T(8,128)(2,1)S(1)} %bitcast.103, bf16[3,64,2048]{2,1,0:T(8,128)(2,1)} %collective-permute-done.11, pred[]{:T(512)S(6)} %eq.13, ...), kind=kLoop, calls=%fused_computation.34 | loop fusion | flops 1572864 | bytes 6291457 | tf_op jit(solution)/shard_map/stack | solution.py:122
  58.5 1.1 %slice.282 = bf16[128,2048]{1,0:T(8,128)(2,1)S(1)} slice(bf16[136,2048]{1,0:T(8,128)(2,1)} %collective-permute-done.10), slice={[0:128], [0:2048]} | slice | bytes 1048576 | tf_op jit(solution)/shard_map/slice | solution.py:197
  60.2 5.0 %collective-permute-done.12 = bf16[264,384]{1,0:T(8,128)(2,1)S(1)} collective-permute-done((bf16[264,384]{1,0:T(8,128)(2,1)S(1)}, bf16[264,384]{1,0:T(8,128)(2,1)S(1)}, u32[]{:S(2)}, u32[]{:S(2)}) %collective-permute-start.12) | collective-permute-done | bytes 202784 | tf_op jit(solution)/shard_map/ppermute | solution.py:105
  67.0 1.8 %collective-permute-done.13 = bf16[136,2048]{1,0:T(8,128)(2,1)S(1)} collective-permute-done((bf16[136,2048]{1,0:T(8,128)(2,1)}, bf16[136,2048]{1,0:T(8,128)(2,1)S(1)}, u32[]{:S(2)}, u32[]{:S(2)}) %collective-permute-start.13) | collective-permute-done | bytes 557088 | tf_op jit(solution)/shard_map/ppermute | solution.py:105
  69.8 2.6 %fusion.5 = bf16[256,768]{1,0:T(8,128)(2,1)S(1)} fusion(bf16[384,2048]{1,0:T(8,128)(2,1)} %bitcast.107, bf16[384,2048]{1,0:T(8,128)(2,1)S(1)} %bitcast.105, bf16[128,2048]{1,0:T(8,128)(2,1)} %slice.283, bf16[128,2048]{1,0:T(8,128)(2,1)S(1)} %slice.282), kind=kOutput, calls=%fused_computation.11 | convolution fusion | flops 813891584 | bytes 4587520 | tf_op jit(solution)/shard_map/dot_general | solution.py:196
  73.7 5.2 %collective-permute-done.14 = bf16[264,384]{1,0:T(8,128)(2,1)S(1)} collective-permute-done((bf16[264,384]{1,0:T(8,128)(2,1)S(1)}, bf16[264,384]{1,0:T(8,128)(2,1)S(1)}, u32[]{:S(2)}, u32[]{:S(2)}) %collective-permute-start.14) | collective-permute-done | bytes 202784 | tf_op jit(solution)/shard_map/ppermute | solution.py:105
  79.4 1.4 %collective-permute-done.16 = bf16[520,256]{1,0:T(8,128)(2,1)S(1)} collective-permute-done((bf16[520,256]{1,0:T(8,128)(2,1)S(1)}, bf16[520,256]{1,0:T(8,128)(2,1)S(1)}, u32[]{:S(2)}, u32[]{:S(2)}) %collective-permute-start.16) | collective-permute-done | bytes 266272 | tf_op jit(solution)/shard_map/ppermute | solution.py:105
  80.9 2.3 %fusion.45 = (f32[1024]{0:T(1024)S(1)}, f32[1024,2048]{1,0:T(8,128)S(1)}) fusion(bf16[2048,256]{1,0:T(8,128)(2,1)S(1)} %pad_maximum_fusion.9, bf16[256,384]{1,0:T(8,128)(2,1)S(1)} %slice.293, bf16[256,384]{1,0:T(8,128)(2,1)S(1)} %get-tuple-element.19, bf16[256,384]{1,0:T(8,128)(2,1)S(1)} %slice.288, bf16[256,384]{1,0:T(8,128)(2,1)S(1)} %get-tuple-element.17, ...), kind=kOutput, calls=%fused_computation.122 | convolution fusion | flops 550501376 | bytes 9719808 | tf_op jit(solution)/shard_map/dot_general | solution.py:223
  83.2 1.3 %fusion = f32[1024]{0:T(1024)S(1)} fusion(f32[1024,2048]{1,0:T(8,128)S(1)} %get-tuple-element.31, f32[1024]{0:T(1024)S(1)} %get-tuple-element.30), kind=kLoop, calls=%fused_computation.3 | loop fusion | flops 4193280 | bytes 8396800 | tf_op jit(solution)/shard_map/reduce_sum | solution.py:229
  84.5 1.6 %fusion.6 = bf16[1024,128]{1,0:T(8,128)(2,1)S(1)} fusion(f32[1024,2048]{1,0:T(8,128)S(1)} %get-tuple-element.31, f32[1024]{0:T(1024)S(1)} %fusion, f32[1024]{0:T(1024)S(1)} %get-tuple-element.30, bf16[2048,256]{1,0:T(8,128)(2,1)S(1)} %pad_maximum_fusion.9), kind=kOutput, calls=%fused_computation.12 | convolution fusion | flops 543293440 | bytes 9183232 | tf_op jit(solution)/shard_map/dot_general | solution.py:230
  86.3 13.2 %all_to_all.5 = bf16[8,128,128]{2,1,0:T(8,128)(2,1)S(1)} all-to-all(bf16[8,128,128]{2,1,0:T(8,128)(2,1)S(1)} %fusion.28), channel_id=1, replica_groups=mesh['grp'=2,'chip'=8,'core'=2] {'chip'}, dimensions={0} | all-to-all | bytes 524288 | tf_op jit(solution)/shard_map/all_to_all | solution.py:237
  (126 shorter events, 14.7 us)
Async XLA Ops:
  0.0 1.1 %copy-start = (bf16[2048,192]{0,1:T(8,128)(2,1)S(1)}, bf16[2048,192]{0,1:T(8,128)(2,1)}, u32[]{:S(2)}) copy-start(bf16[2048,192]{0,1:T(8,128)(2,1)} %param.13) | copy-start | bytes 2359300
  0.0 15.4 %copy-start.1 = (bf16[128,2048]{1,0:T(8,128)(2,1)S(1)}, bf16[128,2048]{1,0:T(8,128)(2,1)}, u32[]{:S(2)}) copy-start(bf16[128,2048]{1,0:T(8,128)(2,1)} %param.11) | copy-start | bytes 1572868
  1.2 14.9 %collective-permute-start.2 = (bf16[64,1024]{1,0:T(8,128)(2,1)S(1)}, bf16[64,1024]{1,0:T(8,128)(2,1)S(1)}, u32[]{:S(2)}, u32[]{:S(2)}) collective-permute-start(bf16[64,1024]{1,0:T(8,128)(2,1)S(1)} %get-tuple-element.23), channel_id=1, source_target_pairs={{0,0},{1,3},{2,6},{3,9},{4,12},{5,15},{6,2},{7,5},{8,8},{9,11},{10... | collective-permute-start | bytes 393224 | tf_op jit(solution)/shard_map/ppermute | solution.py:159
  1.9 14.2 %collective-permute-start.3 = (bf16[64,1024]{1,0:T(8,128)(2,1)S(1)}, bf16[64,1024]{1,0:T(8,128)(2,1)S(1)}, u32[]{:S(2)}, u32[]{:S(2)}) collective-permute-start(bf16[64,1024]{1,0:T(8,128)(2,1)S(1)} %get-tuple-element.22), channel_id=1, source_target_pairs={{0,1},{1,4},{2,7},{3,10},{4,13},{5,0},{6,3},{7,6},{8,9},{9,12},{10... | collective-permute-start | bytes 393224 | tf_op jit(solution)/shard_map/ppermute | solution.py:159
  5.7 10.4 %collective-permute-start.4 = (bf16[64,1024]{1,0:T(8,128)(2,1)S(1)}, bf16[64,1024]{1,0:T(8,128)(2,1)S(1)}, u32[]{:S(2)}, u32[]{:S(2)}) collective-permute-start(bf16[64,1024]{1,0:T(8,128)(2,1)S(1)} %get-tuple-element.21), channel_id=1, source_target_pairs={{0,2},{1,5},{2,8},{3,11},{4,14},{5,1},{6,4},{7,7},{8,10},{9,13},{1... | collective-permute-start | bytes 393224 | tf_op jit(solution)/shard_map/ppermute | solution.py:159
  10.4 4.9 %collective-permute-start = (bf16[3,2048]{1,0:T(4,128)(2,1)S(1)}, bf16[3,2048]{1,0:T(4,128)(2,1)S(1)}, u32[]{:S(2)}, u32[]{:S(2)}) collective-permute-start(bf16[3,2048]{1,0:T(4,128)(2,1)S(1)} %slice.202), channel_id=1, source_target_pairs={{0,1},{1,2},{2,3},{3,4},{4,5},{5,6},{6,7},{7,8},{8,9},{9,10},{10,1... | collective-permute-start | bytes 36872 | tf_op jit(solution)/shard_map/ppermute | solution.py:145
  17.0 21.3 %collective-permute-start.5 = (bf16[3,64,1024]{2,1,0:T(8,128)(2,1)}, bf16[3,64,1024]{2,1,0:T(8,128)(2,1)S(1)}, u32[]{:S(2)}, u32[]{:S(2)}) collective-permute-start(bf16[3,64,1024]{2,1,0:T(8,128)(2,1)} %constant_dynamic-slice_fusion), channel_id=1, source_target_pairs={{0,16},{1,17},{2,18},{3,19},{4,20},{5,21},{6,22},{7,23},{8,24},{9,... | collective-permute-start | bytes 1179656 | tf_op jit(solution)/shard_map/ppermute | solution.py:105
  18.5 19.2 %collective-permute-start.7 = (bf16[3,64,1024]{2,1,0:T(8,128)(2,1)}, bf16[3,64,1024]{2,1,0:T(8,128)(2,1)S(1)}, u32[]{:S(2)}, u32[]{:S(2)}) collective-permute-start(bf16[3,64,1024]{2,1,0:T(8,128)(2,1)} %constant_dynamic-slice_fusion), channel_id=1, source_target_pairs={{0,4},{1,5},{2,6},{3,7},{4,0},{5,1},{6,2},{7,3},{8,12},{9,13},{10,... | collective-permute-start | bytes 1179656 | tf_op jit(solution)/shard_map/ppermute | solution.py:105
  22.2 16.3 %collective-permute-start.1 = (bf16[136,2048]{1,0:T(8,128)(2,1)S(1)}, bf16[136,2048]{1,0:T(8,128)(2,1)}, u32[]{:S(2)}, u32[]{:S(2)}) collective-permute-start(bf16[136,2048]{1,0:T(8,128)(2,1)S(1)} %pad_maximum_fusion.10), channel_id=1, source_target_pairs={{0,2},{1,3},{2,0},{3,1},{4,6},{5,7},{6,4},{7,5},{8,10},{9,11},{10,... | collective-permute-start | bytes 1671176 | tf_op jit(solution)/shard_map/ppermute | solution.py:105
  22.7 26.0 %collective-permute-start.10 = (bf16[136,2048]{1,0:T(8,128)(2,1)S(1)}, bf16[136,2048]{1,0:T(8,128)(2,1)}, u32[]{:S(2)}, u32[]{:S(2)}) collective-permute-start(bf16[136,2048]{1,0:T(8,128)(2,1)S(1)} %pad_maximum_fusion.10), channel_id=1, source_target_pairs={{0,8},{1,9},{2,10},{3,11},{4,12},{5,13},{6,14},{7,15},{8,0},{9,1},... | collective-permute-start | bytes 1671176 | tf_op jit(solution)/shard_map/ppermute | solution.py:105
  37.7 13.5 %collective-permute-start.8 = (bf16[3,64,512]{2,1,0:T(8,128)(2,1)S(1)}, bf16[3,64,512]{2,1,0:T(8,128)(2,1)S(1)}, u32[]{:S(2)}, u32[]{:S(2)}) collective-permute-start(bf16[3,64,512]{2,1,0:T(8,128)(2,1)S(1)} %slice.273), channel_id=1, source_target_pairs={{0,16},{1,17},{2,18},{3,19},{4,20},{5,21},{6,22},{7,23},{8,24},{9,... | collective-permute-start | bytes 589832 | tf_op jit(solution)/shard_map/ppermute | solution.py:105
  38.3 13.0 %collective-permute-start.9 = (bf16[3,64,512]{2,1,0:T(8,128)(2,1)S(1)}, bf16[3,64,512]{2,1,0:T(8,128)(2,1)S(1)}, u32[]{:S(2)}, u32[]{:S(2)}) collective-permute-start(bf16[3,64,512]{2,1,0:T(8,128)(2,1)S(1)} %slice.274), channel_id=1, source_target_pairs={{0,4},{1,5},{2,6},{3,7},{4,0},{5,1},{6,2},{7,3},{8,12},{9,13},{10,... | collective-permute-start | bytes 589832 | tf_op jit(solution)/shard_map/ppermute | solution.py:105
  41.2 13.7 %collective-permute-start.6 = (bf16[3,64,2048]{2,1,0:T(8,128)(2,1)S(1)}, bf16[3,64,2048]{2,1,0:T(8,128)(2,1)}, u32[]{:S(2)}, u32[]{:S(2)}) collective-permute-start(bf16[3,64,2048]{2,1,0:T(8,128)(2,1)S(1)} %bitcast.100), channel_id=1, source_target_pairs={{0,1},{1,0},{2,3},{3,2},{4,5},{5,4},{6,7},{7,6},{8,9},{9,8},{10,11... | collective-permute-start | bytes 2359304 | tf_op jit(solution)/shard_map/ppermute | solution.py:105
  51.3 0.7 copy-start.4
  51.4 0.7 copy-start.5
  51.6 3.4 %collective-permute-start.11 = (bf16[3,64,2048]{2,1,0:T(8,128)(2,1)S(1)}, bf16[3,64,2048]{2,1,0:T(8,128)(2,1)}, u32[]{:S(2)}, u32[]{:S(2)}) collective-permute-start(bf16[3,64,2048]{2,1,0:T(8,128)(2,1)S(1)} %bitcast.102), channel_id=1, source_target_pairs={{0,1},{1,0},{2,3},{3,2},{4,5},{5,4},{6,7},{7,6},{8,9},{9,8},{10,11... | collective-permute-start | bytes 2359304 | tf_op jit(solution)/shard_map/ppermute | solution.py:105
  53.8 15.0 %collective-permute-start.13 = (bf16[136,2048]{1,0:T(8,128)(2,1)}, bf16[136,2048]{1,0:T(8,128)(2,1)S(1)}, u32[]{:S(2)}, u32[]{:S(2)}) collective-permute-start(bf16[136,2048]{1,0:T(8,128)(2,1)} %collective-permute-done.10), channel_id=1, source_target_pairs={{0,2},{1,3},{2,0},{3,1},{4,6},{5,7},{6,4},{7,5},{8,10},{9,11},{10,... | collective-permute-start | bytes 1671176 | tf_op jit(solution)/shard_map/ppermute | solution.py:105
  57.1 1.2 %copy-start.2 = (bf16[3,2,64,2048]{3,2,1,0:T(8,128)(2,1)}, bf16[3,2,64,2048]{3,2,1,0:T(8,128)(2,1)S(1)}, u32[]{:S(2)}) copy-start(bf16[3,2,64,2048]{3,2,1,0:T(8,128)(2,1)S(1)} %copy.33) | copy-start | bytes 4718596
  57.1 1.3 %copy-start.6 = (s32[4]{0:T(128)S(1)}, s32[4]{0:T(128)}, u32[]{:S(2)}) copy-start(s32[4]{0:T(128)} %constant.86.clone) | copy-start | bytes 52
  58.4 6.9 %collective-permute-start.12 = (bf16[264,384]{1,0:T(8,128)(2,1)S(1)}, bf16[264,384]{1,0:T(8,128)(2,1)S(1)}, u32[]{:S(2)}, u32[]{:S(2)}) collective-permute-start(bf16[264,384]{1,0:T(8,128)(2,1)S(1)} %pad_maximum_fusion.16), channel_id=1, source_target_pairs={{0,4},{1,5},{2,6},{3,7},{4,0},{5,1},{6,2},{7,3},{8,12},{9,13},{10,... | collective-permute-start | bytes 608264 | tf_op jit(solution)/shard_map/ppermute | solution.py:105
  65.3 4.6 %copy-start.3 = (bf16[264,384]{1,0:T(8,128)(2,1)}, bf16[264,384]{1,0:T(8,128)(2,1)S(1)}, u32[]{:S(2)}) copy-start(bf16[264,384]{1,0:T(8,128)(2,1)S(1)} %collective-permute-done.12) | copy-start | bytes 608260
  72.6 6.4 %collective-permute-start.14 = (bf16[264,384]{1,0:T(8,128)(2,1)S(1)}, bf16[264,384]{1,0:T(8,128)(2,1)S(1)}, u32[]{:S(2)}, u32[]{:S(2)}) collective-permute-start(bf16[264,384]{1,0:T(8,128)(2,1)S(1)} %pad_maximum_fusion.17), channel_id=1, source_target_pairs={{0,4},{1,5},{2,6},{3,7},{4,0},{5,1},{6,2},{7,3},{8,12},{9,13},{10,... | collective-permute-start | bytes 608264 | tf_op jit(solution)/shard_map/ppermute | solution.py:105
  73.7 5.6 %collective-permute-start.15 = (bf16[520,256]{1,0:T(8,128)(2,1)S(1)}, bf16[520,256]{1,0:T(8,128)(2,1)S(1)}, u32[]{:S(2)}, u32[]{:S(2)}) collective-permute-start(bf16[520,256]{1,0:T(8,128)(2,1)S(1)} %pad_maximum_fusion.11), channel_id=1, source_target_pairs={{0,1},{1,0},{2,3},{3,2},{4,5},{5,4},{6,7},{7,6},{8,9},{9,8},{10,11... | collective-permute-start | bytes 798728 | tf_op jit(solution)/shard_map/ppermute | solution.py:105
  79.1 1.6 %collective-permute-start.16 = (bf16[520,256]{1,0:T(8,128)(2,1)S(1)}, bf16[520,256]{1,0:T(8,128)(2,1)S(1)}, u32[]{:S(2)}, u32[]{:S(2)}) collective-permute-start(bf16[520,256]{1,0:T(8,128)(2,1)S(1)} %pad_maximum_fusion.12), channel_id=1, source_target_pairs={{0,1},{1,0},{2,3},{3,2},{4,5},{5,4},{6,7},{7,6},{8,9},{9,8},{10,11... | collective-permute-start | bytes 798728 | tf_op jit(solution)/shard_map/ppermute | solution.py:105

commit v15 on v3

--- a/solution.py
+++ b/solution.py
@@ -111,6 +111,11 @@
     )
 
 
+def zero_after(array):
+    last = array[(-1,) * array.ndim]
+    return jnp.where(last != last, 1.0, 0.0).astype(jnp.bfloat16)
+
+
 def body_by_head(frames, conv_weight, qkv_weight, track_ids, track_owner):
     tok_rows = frames.shape[0]
     chips = lax.axis_size("chip")
@@ -135,24 +140,48 @@
     far_early = xor_swap(early, Z1)
     own = jnp.concatenate([early, late], axis=0)
     beside = xor_swap(own, Y)
-    far_beside_late = xor_swap(far_late, Y)
+
+    half = features // 2
+    held = qkv_weight.T.reshape(3, HD // 2, features)
+
+    def to_heads(block, j):
+        pairs = [
+            (g * devices + d, g * devices + (3 * d + j[g]) % devices)
+            for g in (0, 1)
+            for d in range(devices)
+        ]
+        return lax.ppermute(block, every, pairs)
+
+    outer = to_heads(lax.dynamic_index_in_dim(held, 2 * grp, 0, False), (0, 2))
+    middle = to_heads(lax.dynamic_slice_in_dim(held[1], grp * half, half, 1), (1, 1))
+    mine = jnp.concatenate([outer[:, :half], outer[:, half:], middle], axis=0)
+    paired = xor_swap(mine, Z0)
+
+    far_beside_late = xor_swap(far_late + zero_after(paired), Y)
     far_beside_early = xor_swap(far_early, Y)
 
-    half = features // 2
-    held = lax.dynamic_slice_in_dim(qkv_weight.T, grp * half, half, 1).reshape(3, HD // 2, half)
-    moved = [
-        lax.ppermute(held[j], both, [(d, (3 * d + j) % devices) for d in range(devices)])
-        for j in range(3)
-    ]
-    mine = lax.dynamic_slice_in_dim(jnp.stack(moved + moved[:2]), lax.rem(me, 3), 3, 0)
-    paired = xor_swap(mine, Z0)
-
-    def whole_head(quarter):
-        wide = by_bit(grp, quarter, xor_swap(quarter, devices, every), 2)
-        wide = wide.reshape(3, HD // 2, features)
+    def whole_head(pieces, index):
+        theirs = xor_swap(pieces, devices, every)
+        size = HD // 2
+
+        def block(values, n):
+            return values[n * size : (n + 1) * size]
+
+        first, last = (
+            jnp.concatenate(
+                [jnp.where(grp == g, block(pieces, n), block(theirs, n)) for n in (0, 1)], axis=1
+            )
+            for g in (0, 1)
+        )
+        low, high = block(pieces, 2), block(theirs, 2)
+        between = jnp.concatenate(
+            [jnp.where(grp == 0, low, high), jnp.where(grp == 0, high, low)], axis=1
+        )
+        turned = [first, between, last, first, between]
+        wide = lax.dynamic_slice_in_dim(jnp.stack(turned), lax.rem(index, 3), 3, 0)
         return by_bit(core, wide, xor_swap(wide, CORE), 1).reshape(3 * HD, features)
 
-    two_heads = jnp.concatenate([whole_head(mine), whole_head(paired)], axis=0)
+    two_heads = jnp.concatenate([whole_head(mine, me), whole_head(paired, me ^ Z0)], axis=0)
 
     def project(rows):
         done = lax.dot_general(

time: 93.9 us -> 93 us (level)
  waiting for transfers between devices: 39.5 us -> 35.8 us
  between operations: 0.75 us -> 2.07 us
  local copies, waits for them, and re-layouts: 4.2 us -> 5.48 us
  starting transfers between devices: 25.9 us -> 27.1 us
  blocking collectives: 13 us -> 11.9 us
    ppermute x18, starting transfers between devices: 14.2 us -> 18.9 us  [xor_swap(): return lax.ppermute(value, axes, [(d, d ^ bit) for d in range(count)])]
    ppermute x18, waiting for transfers between devices: 39.5 us -> 35.8 us  [xor_swap(): return lax.ppermute(value, axes, [(d, d ^ bit) for d in range(count)])]
    ppermute x3 -> x2, starting transfers between devices: 8.43 us -> 5.83 us  [to_heads(): return lax.ppermute(block, every, pairs)]
    slice x1 -> x3, local copies, waits for them, and re-layouts: 0.03 us -> 1.57 us  [the longest x1 0.97 us: body_by_head(): held[1]]
    unnamed x12 -> x5, local copies, waits for them, and re-layouts: 1.24 us -> 0.04 us
    all_to_all x1, blocking collectives: 13 us -> 11.9 us  [body_by_head(): lax.all_to_all(sent, 'chip', split_axis=0, concat_axis=0, tiled=True)]
    squeeze x0 -> x1, local copies, waits for them, and re-layouts: none -> 0.97 us  [body_by_head(): outer = to_heads(lax.dynamic_index_in_dim(held, 2 * grp, 0, False), (0, 2))]
  transfers between devices with their start and end apart: 22 -> 21, of which waited for: 10 -> 10; matrix products, arithmetic and copies ran while one was open for 7% -> 9% of each run, Pallas kernels for 0% -> 0%
where the time goes in v15:
time: 93 us; the launch traced here: 92.7 us
  waiting for transfers between devices  35.8 us (38%)
  starting transfers between devices  27.1 us (29%)
  blocking collectives  11.9 us (13%)
  matrix products  6.55 us (7%)
  local copies, waits for them, and re-layouts  5.48 us (6%)
  other arithmetic  3.86 us (4%)
  between operations  2.07 us (2%)
    ppermute x18, waiting for transfers between devices, xor_swap(): return lax.ppermute(value, axes, [(d, d ^ bit) for d in range(count)])  35.8 us
    ppermute x18, starting transfers between devices, xor_swap(): return lax.ppermute(value, axes, [(d, d ^ bit) for d in range(count)])  18.9 us
    all_to_all x1, blocking collectives, body_by_head(): lax.all_to_all(sent, 'chip', split_axis=0, concat_axis=0, tiled=True)  11.9 us
    ppermute x2, starting transfers between devices, to_heads(): return lax.ppermute(block, every, pairs)  5.83 us
    dot_general x2, matrix products, project(): lax.dot_general(rows, two_heads, (((1,), (1,)), ((), ())), preferred_elem...  2.62 us
    ppermute x1, starting transfers between devices, body_by_head(): lax.ppermute(frames[tok_rows - (KW - 1):], both, [(i, i + 1) for i in ran...  2.36 us
    dot_general x1, matrix products, body_by_head(): lax.dot_general(query, keyed[:, :HD], (((1,), (1,)), ((), ())), preferred...  2.33 us
  transfers between devices with their start and end apart: 21, of which 10 were waited for; matrix products, arithmetic and copies ran while one was open for 9% of the time, Pallas kernels for 0%

profile of v15, /device:TPU:0, one launch (start us, length us, event | category | flops | bytes accessed | tf_op | source)
XLA Modules:
  0.0 92.7 jit_solution(15097306420697305876)
XLA Ops:
  0.9 2.4 %collective-permute-start.4 = (bf16[3,2048]{1,0:T(4,128)(2,1)S(1)}, bf16[3,2048]{1,0:T(4,128)(2,1)S(1)}, u32[]{:S(2)}, u32[]{:S(2)}) collective-permute-start(bf16[3,2048]{1,0:T(4,128)(2,1)S(1)} %slice.253), channel_id=1, source_target_pairs={{0,1},{1,2},{2,3},{3,4},{4,5},{5,6},{6,7},{7,8},{8,9},{9,10},{10,1... | collective-permute-start | bytes 36872 | tf_op jit(solution)/shard_map/ppermute | solution.py:133
  5.9 5.2 %collective-permute-start.8 = (bf16[64,1024]{1,0:T(8,128)(2,1)S(1)}, bf16[64,1024]{1,0:T(8,128)(2,1)S(1)}, u32[]{:S(2)}, u32[]{:S(2)}) collective-permute-start(bf16[64,1024]{1,0:T(8,128)(2,1)S(1)} %constant_dynamic-slice_fusion.2), channel_id=1, source_target_pairs={{0,1},{1,4},{2,7},{3,10},{4,13},{5,0},{6,3},{7,6},{8,9},{9,12},{10... | collective-permute-start | bytes 393224 | tf_op jit(solution)/shard_map/ppermute | solution.py:153
  11.8 1.5 %collective-permute-start = (s32[1,128]{1,0:T(1,128)S(1)}, s32[1,128]{1,0:T(1,128)S(1)}, u32[]{:S(2)}, u32[]{:S(2)}) collective-permute-start(s32[1,128]{1,0:T(1,128)S(1)} %bitcast.167), channel_id=1, source_target_pairs={{0,1},{1,0},{2,3},{3,2},{4,5},{5,4},{6,7},{7,6},{8,9},{9,8},{10,11... | collective-permute-start | bytes 1544 | tf_op jit(solution)/shard_map/ppermute | solution.py:105
  14.1 1.5 %collective-permute-start.1 = (s32[2,128]{1,0:T(2,128)S(1)}, s32[2,128]{1,0:T(2,128)S(1)}, u32[]{:S(2)}, u32[]{:S(2)}) collective-permute-start(s32[2,128]{1,0:T(2,128)S(1)} %pad_add_fusion.2), channel_id=1, source_target_pairs={{0,2},{1,3},{2,0},{3,1},{4,6},{5,7},{6,4},{7,5},{8,10},{9,11},{10,... | collective-permute-start | bytes 3080 | tf_op jit(solution)/shard_map/ppermute | solution.py:105
  15.8 1.9 %collective-permute-done.1 = s32[2,128]{1,0:T(2,128)S(1)} collective-permute-done((s32[2,128]{1,0:T(2,128)S(1)}, s32[2,128]{1,0:T(2,128)S(1)}, u32[]{:S(2)}, u32[]{:S(2)}) %collective-permute-start.1) | collective-permute-done | bytes 1056 | tf_op jit(solution)/shard_map/ppermute | solution.py:105
  17.7 2.5 %collective-permute-start.2 = (s32[4,128]{1,0:T(4,128)S(1)}, s32[4,128]{1,0:T(4,128)S(1)}, u32[]{:S(2)}, u32[]{:S(2)}) collective-permute-start(s32[4,128]{1,0:T(4,128)S(1)} %pad_add_fusion.1), channel_id=1, source_target_pairs={{0,4},{1,5},{2,6},{3,7},{4,0},{5,1},{6,2},{7,3},{8,12},{9,13},{10,... | collective-permute-start | bytes 6152 | tf_op jit(solution)/shard_map/ppermute | solution.py:105
  22.0 1.9 %collective-permute-start.9 = (bf16[192,1024]{1,0:T(8,128)(2,1)S(1)}, bf16[192,1024]{1,0:T(8,128)(2,1)S(1)}, u32[]{:S(2)}, u32[]{:S(2)}) collective-permute-start(bf16[192,1024]{1,0:T(8,128)(2,1)S(1)} %pad_maximum_fusion.14), channel_id=1, source_target_pairs={{0,4},{1,5},{2,6},{3,7},{4,0},{5,1},{6,2},{7,3},{8,12},{9,13},{10,... | collective-permute-start | bytes 1179656 | tf_op jit(solution)/shard_map/ppermute | solution.py:105
  23.9 1.3 %collective-permute-start.6 = (bf16[64,2048]{1,0:T(8,128)(2,1)S(1)}, bf16[64,2048]{1,0:T(8,128)(2,1)S(1)}, u32[]{:S(2)}, u32[]{:S(2)}) collective-permute-start(bf16[64,2048]{1,0:T(8,128)(2,1)S(1)} %get-tuple-element.6), channel_id=1, source_target_pairs={{0,8},{1,9},{2,10},{3,11},{4,12},{5,13},{6,14},{7,15},{8,0},{9,1},... | collective-permute-start | bytes 786440 | tf_op jit(solution)/shard_map/ppermute | solution.py:105
  25.2 1.7 %collective-permute-start.3 = (s32[8,128]{1,0:T(8,128)S(1)}, s32[8,128]{1,0:T(8,128)S(1)}, u32[]{:S(2)}, u32[]{:S(2)}) collective-permute-start(s32[8,128]{1,0:T(8,128)S(1)} %pad_add_fusion), channel_id=1, source_target_pairs={{0,8},{1,9},{2,10},{3,11},{4,12},{5,13},{6,14},{7,15},{8,0},{9,1},... | collective-permute-start | bytes 12296 | tf_op jit(solution)/shard_map/ppermute | solution.py:105
  26.9 7.1 %collective-permute-done.16 = bf16[64,2048]{1,0:T(8,128)(2,1)S(1)} collective-permute-done((bf16[64,2048]{1,0:T(8,128)(2,1)S(1)}, bf16[64,2048]{1,0:T(8,128)(2,1)S(1)}, u32[]{:S(2)}, u32[]{:S(2)}) %collective-permute-start.16) | collective-permute-done | bytes 262176 | tf_op jit(solution)/shard_map/ppermute | solution.py:105
  34.1 1.9 %collective-permute-start.11 = (bf16[192,1024]{1,0:T(8,128)(2,1)S(1)}, bf16[192,1024]{1,0:T(8,128)(2,1)S(1)}, u32[]{:S(2)}, u32[]{:S(2)}) collective-permute-start(bf16[192,1024]{1,0:T(8,128)(2,1)S(1)} %pad_maximum_fusion.14), channel_id=1, source_target_pairs={{0,16},{1,17},{2,18},{3,19},{4,20},{5,21},{6,22},{7,23},{8,24},{9,... | collective-permute-start | bytes 1179656 | tf_op jit(solution)/shard_map/ppermute | solution.py:105
  36.6 3.4 %collective-permute-done.9 = bf16[192,1024]{1,0:T(8,128)(2,1)S(1)} collective-permute-done((bf16[192,1024]{1,0:T(8,128)(2,1)S(1)}, bf16[192,1024]{1,0:T(8,128)(2,1)S(1)}, u32[]{:S(2)}, u32[]{:S(2)}) %collective-permute-start.9) | collective-permute-done | bytes 393248 | tf_op jit(solution)/shard_map/ppermute | solution.py:105
  41.8 3.4 %collective-permute-done.6 = bf16[64,2048]{1,0:T(8,128)(2,1)S(1)} collective-permute-done((bf16[64,2048]{1,0:T(8,128)(2,1)S(1)}, bf16[64,2048]{1,0:T(8,128)(2,1)S(1)}, u32[]{:S(2)}, u32[]{:S(2)}) %collective-permute-start.6) | collective-permute-done | bytes 262176 | tf_op jit(solution)/shard_map/ppermute | solution.py:105
  46.5 1.6 %collective-permute-start.13 = (bf16[192,1024]{1,0:T(8,128)(2,1)S(1)}, bf16[192,1024]{1,0:T(8,128)(2,1)S(1)}, u32[]{:S(2)}, u32[]{:S(2)}) collective-permute-start(bf16[192,1024]{1,0:T(8,128)(2,1)S(1)} %collective-permute-done.9), channel_id=1, source_target_pairs={{0,16},{1,17},{2,18},{3,19},{4,20},{5,21},{6,22},{7,23},{8,24},{9,... | collective-permute-start | bytes 1179656 | tf_op jit(solution)/shard_map/ppermute | solution.py:105
  48.3 8.8 %collective-permute-done.13 = bf16[192,1024]{1,0:T(8,128)(2,1)S(1)} collective-permute-done((bf16[192,1024]{1,0:T(8,128)(2,1)S(1)}, bf16[192,1024]{1,0:T(8,128)(2,1)S(1)}, u32[]{:S(2)}, u32[]{:S(2)}) %collective-permute-start.13) | collective-permute-done | bytes 393248 | tf_op jit(solution)/shard_map/ppermute | solution.py:105
  57.8 1.9 %collective-permute-done.14 = bf16[3,64,2048]{2,1,0:T(8,128)(2,1)S(1)} collective-permute-done((bf16[3,64,2048]{2,1,0:T(8,128)(2,1)S(1)}, bf16[3,64,2048]{2,1,0:T(8,128)(2,1)S(1)}, u32[]{:S(2)}, u32[]{:S(2)}) %collective-permute-start.14) | collective-permute-done | bytes 786464 | tf_op jit(solution)/shard_map/ppermute | solution.py:105
  60.1 1.4 %fusion.4 = bf16[384,768]{1,0:T(8,128)(2,1)S(1)} fusion(bf16[384,2048]{1,0:T(8,128)(2,1)S(1)} %constant_dynamic-update-slice_fusion, bf16[384,2048]{1,0:T(8,128)(2,1)S(1)} %bitcast.154, bf16[384,2048]{1,0:T(8,128)(2,1)S(1)} %bitcast.152), kind=kOutput, calls=%fused_computation.10 | convolution fusion | flops 1214545920 | bytes 5308416 | tf_op jit(solution)/shard_map/dot_general | solution.py:187
  61.7 1.2 %fusion.6 = bf16[128,768]{1,0:T(8,128)(2,1)S(1)} fusion(bf16[384,2048]{1,0:T(8,128)(2,1)S(1)} %bitcast.155, bf16[384,2048]{1,0:T(8,128)(2,1)S(1)} %bitcast.153, bf16[64,2048]{1,0:T(8,128)(2,1)S(1)} %collective-permute-done.17, bf16[64,2048]{1,0:T(8,128)(2,1)S(1)} %collective-permute-done.16), kind=kOutput, calls=%fused_computation.12 | convolution fusion | flops 410091520 | bytes 3866624 | tf_op jit(solution)/shard_map/dot_general | solution.py:187
  62.9 2.1 %collective-permute-start.18 = (bf16[128,384]{1,0:T(8,128)(2,1)S(1)}, bf16[128,384]{1,0:T(8,128)(2,1)S(1)}, u32[]{:S(2)}, u32[]{:S(2)}) collective-permute-start(bf16[128,384]{1,0:T(8,128)(2,1)S(1)} %get-tuple-element.34), channel_id=1, source_target_pairs={{0,4},{1,5},{2,6},{3,7},{4,0},{5,1},{6,2},{7,3},{8,12},{9,13},{10,... | collective-permute-start | bytes 294920 | tf_op jit(solution)/shard_map/ppermute | solution.py:105
  65.0 6.5 %collective-permute-done.15 = bf16[384,384]{1,0:T(8,128)(2,1)S(1)} collective-permute-done((bf16[384,384]{1,0:T(8,128)(2,1)S(1)}, bf16[384,384]{1,0:T(8,128)(2,1)S(1)}, u32[]{:S(2)}, u32[]{:S(2)}) %collective-permute-start.15) | collective-permute-done | bytes 294944 | tf_op jit(solution)/shard_map/ppermute | solution.py:105
  74.3 2.3 %fusion.61 = (f32[1024]{0:T(1024)S(1)}, f32[1024,2048]{1,0:T(8,128)S(1)}) fusion(bf16[2048,256]{1,0:T(8,128)(2,1)S(1)} %fusion.8, bf16[128,384]{1,0:T(8,128)(2,1)S(1)} %collective-permute-done.18, bf16[128,384]{1,0:T(8,128)(2,1)S(1)} %get-tuple-element.33, bf16[384,384]{1,0:T(8,128)(2,1)S(1)} %collective-permute-done.15, ...), kind=kOutput, calls=%fused_computation.181 | convolution fusion | flops 550501376 | bytes 9728000 | tf_op jit(solution)/shard_map/dot_general | solution.py:222
  76.7 1.3 %fusion = f32[1024]{0:T(1024)S(1)} fusion(f32[1024,2048]{1,0:T(8,128)S(1)} %get-tuple-element.62, f32[1024]{0:T(1024)S(1)} %get-tuple-element.61), kind=kLoop, calls=%fused_computation.3 | loop fusion | flops 4193280 | bytes 8396800 | tf_op jit(solution)/shard_map/reduce_sum | solution.py:230
  77.9 1.6 %fusion.5 = bf16[1024,128]{1,0:T(8,128)(2,1)S(1)} fusion(f32[1024,2048]{1,0:T(8,128)S(1)} %get-tuple-element.62, f32[1024]{0:T(1024)S(1)} %fusion, f32[1024]{0:T(1024)S(1)} %get-tuple-element.61, bf16[2048,256]{1,0:T(8,128)(2,1)S(1)} %fusion.8), kind=kOutput, calls=%fused_computation.11 | convolution fusion | flops 543293440 | bytes 9183232 | tf_op jit(solution)/shard_map/dot_general | solution.py:231
  79.8 11.9 %all_to_all.5 = bf16[8,128,128]{2,1,0:T(8,128)(2,1)S(1)} all-to-all(bf16[8,128,128]{2,1,0:T(8,128)(2,1)S(1)} %fusion.45), channel_id=1, replica_groups=mesh['grp'=2,'chip'=8,'core'=2] {'chip'}, dimensions={0} | all-to-all | bytes 524288 | tf_op jit(solution)/shard_map/all_to_all | solution.py:240
  (109 shorter events, 14.4 us)
Async XLA Ops:
  0.0 13.3 %copy-start = (bf16[128,2048]{1,0:T(8,128)(2,1)S(1)}, bf16[128,2048]{1,0:T(8,128)(2,1)}, u32[]{:S(2)}) copy-start(bf16[128,2048]{1,0:T(8,128)(2,1)} %param.5) | copy-start | bytes 1572868
  0.0 20.2 %slice-start = ((bf16[128,2048]{1,0:T(8,128)(2,1)}), bf16[64,2048]{1,0:T(8,128)(2,1)S(1)}, s32[]{:S(2)}) async-start(bf16[128,2048]{1,0:T(8,128)(2,1)} %param.5), calls=%async_computation.1 | async-start | bytes 524288 | tf_op jit(solution)/shard_map/slice | solution.py:137
  0.0 13.5 %copy-start.1 = (bf16[4,2048]{1,0:T(4,128)(2,1)S(1)}, bf16[4,2048]{1,0:T(4,128)(2,1)}, u32[]{:S(2)}) copy-start(bf16[4,2048]{1,0:T(4,128)(2,1)} %param.6) | copy-start | bytes 49156
  0.9 19.3 %collective-permute-start.4 = (bf16[3,2048]{1,0:T(4,128)(2,1)S(1)}, bf16[3,2048]{1,0:T(4,128)(2,1)S(1)}, u32[]{:S(2)}, u32[]{:S(2)}) collective-permute-start(bf16[3,2048]{1,0:T(4,128)(2,1)S(1)} %slice.253), channel_id=1, source_target_pairs={{0,1},{1,2},{2,3},{3,4},{4,5},{5,6},{6,7},{7,8},{8,9},{9,10},{10,1... | collective-permute-start | bytes 36872 | tf_op jit(solution)/shard_map/ppermute | solution.py:133
  4.2 17.8 %collective-permute-start.7 = (bf16[64,2048]{1,0:T(8,128)(2,1)S(1)}, bf16[64,2048]{1,0:T(8,128)(2,1)S(1)}, u32[]{:S(2)}, u32[]{:S(2)}) collective-permute-start(bf16[64,2048]{1,0:T(8,128)(2,1)S(1)} %dynamic-slice_bitcast_fusion), channel_id=1, source_target_pairs={{0,0},{1,3},{2,6},{3,9},{4,12},{5,15},{6,2},{7,5},{8,8},{9,11},{10... | collective-permute-start | bytes 786440 | tf_op jit(solution)/shard_map/ppermute | solution.py:153
  5.9 16.1 %collective-permute-start.8 = (bf16[64,1024]{1,0:T(8,128)(2,1)S(1)}, bf16[64,1024]{1,0:T(8,128)(2,1)S(1)}, u32[]{:S(2)}, u32[]{:S(2)}) collective-permute-start(bf16[64,1024]{1,0:T(8,128)(2,1)S(1)} %constant_dynamic-slice_fusion.2), channel_id=1, source_target_pairs={{0,1},{1,4},{2,7},{3,10},{4,13},{5,0},{6,3},{7,6},{8,9},{9,12},{10... | collective-permute-start | bytes 393224 | tf_op jit(solution)/shard_map/ppermute | solution.py:153
  11.8 2.3 %collective-permute-start = (s32[1,128]{1,0:T(1,128)S(1)}, s32[1,128]{1,0:T(1,128)S(1)}, u32[]{:S(2)}, u32[]{:S(2)}) collective-permute-start(s32[1,128]{1,0:T(1,128)S(1)} %bitcast.167), channel_id=1, source_target_pairs={{0,1},{1,0},{2,3},{3,2},{4,5},{5,4},{6,7},{7,6},{8,9},{9,8},{10,11... | collective-permute-start | bytes 1544 | tf_op jit(solution)/shard_map/ppermute | solution.py:105
  14.1 3.6 %collective-permute-start.1 = (s32[2,128]{1,0:T(2,128)S(1)}, s32[2,128]{1,0:T(2,128)S(1)}, u32[]{:S(2)}, u32[]{:S(2)}) collective-permute-start(s32[2,128]{1,0:T(2,128)S(1)} %pad_add_fusion.2), channel_id=1, source_target_pairs={{0,2},{1,3},{2,0},{3,1},{4,6},{5,7},{6,4},{7,5},{8,10},{9,11},{10,... | collective-permute-start | bytes 3080 | tf_op jit(solution)/shard_map/ppermute | solution.py:105
  17.7 7.5 %collective-permute-start.2 = (s32[4,128]{1,0:T(4,128)S(1)}, s32[4,128]{1,0:T(4,128)S(1)}, u32[]{:S(2)}, u32[]{:S(2)}) collective-permute-start(s32[4,128]{1,0:T(4,128)S(1)} %pad_add_fusion.1), channel_id=1, source_target_pairs={{0,4},{1,5},{2,6},{3,7},{4,0},{5,1},{6,2},{7,3},{8,12},{9,13},{10,... | collective-permute-start | bytes 6152 | tf_op jit(solution)/shard_map/ppermute | solution.py:105
  20.5 13.5 %collective-permute-start.16 = (bf16[64,2048]{1,0:T(8,128)(2,1)S(1)}, bf16[64,2048]{1,0:T(8,128)(2,1)S(1)}, u32[]{:S(2)}, u32[]{:S(2)}) collective-permute-start(bf16[64,2048]{1,0:T(8,128)(2,1)S(1)} %get-tuple-element.8), channel_id=1, source_target_pairs={{0,8},{1,9},{2,10},{3,11},{4,12},{5,13},{6,14},{7,15},{8,0},{9,1},... | collective-permute-start | bytes 786440 | tf_op jit(solution)/shard_map/ppermute | solution.py:105
  21.1 14.9 %collective-permute-start.5 = (bf16[128,2048]{1,0:T(8,128)(2,1)S(1)}, bf16[128,2048]{1,0:T(8,128)(2,1)S(1)}, u32[]{:S(2)}, u32[]{:S(2)}) collective-permute-start(bf16[128,2048]{1,0:T(8,128)(2,1)S(1)} %pad_maximum_fusion.12), channel_id=1, source_target_pairs={{0,2},{1,3},{2,0},{3,1},{4,6},{5,7},{6,4},{7,5},{8,10},{9,11},{10,... | collective-permute-start | bytes 1572872 | tf_op jit(solution)/shard_map/ppermute | solution.py:105
  22.0 17.9 %collective-permute-start.9 = (bf16[192,1024]{1,0:T(8,128)(2,1)S(1)}, bf16[192,1024]{1,0:T(8,128)(2,1)S(1)}, u32[]{:S(2)}, u32[]{:S(2)}) collective-permute-start(bf16[192,1024]{1,0:T(8,128)(2,1)S(1)} %pad_maximum_fusion.14), channel_id=1, source_target_pairs={{0,4},{1,5},{2,6},{3,7},{4,0},{5,1},{6,2},{7,3},{8,12},{9,13},{10,... | collective-permute-start | bytes 1179656 | tf_op jit(solution)/shard_map/ppermute | solution.py:105
  23.9 21.4 %collective-permute-start.6 = (bf16[64,2048]{1,0:T(8,128)(2,1)S(1)}, bf16[64,2048]{1,0:T(8,128)(2,1)S(1)}, u32[]{:S(2)}, u32[]{:S(2)}) collective-permute-start(bf16[64,2048]{1,0:T(8,128)(2,1)S(1)} %get-tuple-element.6), channel_id=1, source_target_pairs={{0,8},{1,9},{2,10},{3,11},{4,12},{5,13},{6,14},{7,15},{8,0},{9,1},... | collective-permute-start | bytes 786440 | tf_op jit(solution)/shard_map/ppermute | solution.py:105
  25.2 47.7 %collective-permute-start.3 = (s32[8,128]{1,0:T(8,128)S(1)}, s32[8,128]{1,0:T(8,128)S(1)}, u32[]{:S(2)}, u32[]{:S(2)}) collective-permute-start(s32[8,128]{1,0:T(8,128)S(1)} %pad_add_fusion), channel_id=1, source_target_pairs={{0,8},{1,9},{2,10},{3,11},{4,12},{5,13},{6,14},{7,15},{8,0},{9,1},... | collective-permute-start | bytes 12296 | tf_op jit(solution)/shard_map/ppermute | solution.py:105
  34.1 12.2 %collective-permute-start.11 = (bf16[192,1024]{1,0:T(8,128)(2,1)S(1)}, bf16[192,1024]{1,0:T(8,128)(2,1)S(1)}, u32[]{:S(2)}, u32[]{:S(2)}) collective-permute-start(bf16[192,1024]{1,0:T(8,128)(2,1)S(1)} %pad_maximum_fusion.14), channel_id=1, source_target_pairs={{0,16},{1,17},{2,18},{3,19},{4,20},{5,21},{6,22},{7,23},{8,24},{9,... | collective-permute-start | bytes 1179656 | tf_op jit(solution)/shard_map/ppermute | solution.py:105
  36.0 25.7 %collective-permute-start.17 = (bf16[64,2048]{1,0:T(8,128)(2,1)S(1)}, bf16[64,2048]{1,0:T(8,128)(2,1)S(1)}, u32[]{:S(2)}, u32[]{:S(2)}) collective-permute-start(bf16[64,2048]{1,0:T(8,128)(2,1)S(1)} %collective-permute-done.16), channel_id=1, source_target_pairs={{0,2},{1,3},{2,0},{3,1},{4,6},{5,7},{6,4},{7,5},{8,10},{9,11},{10,... | collective-permute-start | bytes 786440 | tf_op jit(solution)/shard_map/ppermute | solution.py:105
  45.3 12.1 %collective-permute-start.10 = (bf16[64,2048]{1,0:T(8,128)(2,1)S(1)}, bf16[64,2048]{1,0:T(8,128)(2,1)S(1)}, u32[]{:S(2)}, u32[]{:S(2)}) collective-permute-start(bf16[64,2048]{1,0:T(8,128)(2,1)S(1)} %get-tuple-element.29), channel_id=1, source_target_pairs={{0,2},{1,3},{2,0},{3,1},{4,6},{5,7},{6,4},{7,5},{8,10},{9,11},{10,... | collective-permute-start | bytes 786440 | tf_op jit(solution)/shard_map/ppermute | solution.py:105
  46.5 10.6 %collective-permute-start.13 = (bf16[192,1024]{1,0:T(8,128)(2,1)S(1)}, bf16[192,1024]{1,0:T(8,128)(2,1)S(1)}, u32[]{:S(2)}, u32[]{:S(2)}) collective-permute-start(bf16[192,1024]{1,0:T(8,128)(2,1)S(1)} %collective-permute-done.9), channel_id=1, source_target_pairs={{0,16},{1,17},{2,18},{3,19},{4,20},{5,21},{6,22},{7,23},{8,24},{9,... | collective-permute-start | bytes 1179656 | tf_op jit(solution)/shard_map/ppermute | solution.py:105
  48.2 9.3 %collective-permute-start.12 = (bf16[3,64,2048]{2,1,0:T(8,128)(2,1)S(1)}, bf16[3,64,2048]{2,1,0:T(8,128)(2,1)S(1)}, u32[]{:S(2)}, u32[]{:S(2)}) collective-permute-start(bf16[3,64,2048]{2,1,0:T(8,128)(2,1)S(1)} %constant_dynamic-slice_fusion.1), channel_id=1, source_target_pairs={{0,1},{1,0},{2,3},{3,2},{4,5},{5,4},{6,7},{7,6},{8,9},{9,8},{10,11... | collective-permute-start | bytes 2359304 | tf_op jit(solution)/shard_map/ppermute | solution.py:105
  57.4 2.4 %collective-permute-start.14 = (bf16[3,64,2048]{2,1,0:T(8,128)(2,1)S(1)}, bf16[3,64,2048]{2,1,0:T(8,128)(2,1)S(1)}, u32[]{:S(2)}, u32[]{:S(2)}) collective-permute-start(bf16[3,64,2048]{2,1,0:T(8,128)(2,1)S(1)} %constant_dynamic-slice_fusion), channel_id=1, source_target_pairs={{0,1},{1,0},{2,3},{3,2},{4,5},{5,4},{6,7},{7,6},{8,9},{9,8},{10,11... | collective-permute-start | bytes 2359304 | tf_op jit(solution)/shard_map/ppermute | solution.py:105
  61.6 9.9 %collective-permute-start.15 = (bf16[384,384]{1,0:T(8,128)(2,1)S(1)}, bf16[384,384]{1,0:T(8,128)(2,1)S(1)}, u32[]{:S(2)}, u32[]{:S(2)}) collective-permute-start(bf16[384,384]{1,0:T(8,128)(2,1)S(1)} %get-tuple-element.24), channel_id=1, source_target_pairs={{0,4},{1,5},{2,6},{3,7},{4,0},{5,1},{6,2},{7,3},{8,12},{9,13},{10,... | collective-permute-start | bytes 884744 | tf_op jit(solution)/shard_map/ppermute | solution.py:105
  62.9 9.9 %collective-permute-start.18 = (bf16[128,384]{1,0:T(8,128)(2,1)S(1)}, bf16[128,384]{1,0:T(8,128)(2,1)S(1)}, u32[]{:S(2)}, u32[]{:S(2)}) collective-permute-start(bf16[128,384]{1,0:T(8,128)(2,1)S(1)} %get-tuple-element.34), channel_id=1, source_target_pairs={{0,4},{1,5},{2,6},{3,7},{4,0},{5,1},{6,2},{7,3},{8,12},{9,13},{10,... | collective-permute-start | bytes 294920 | tf_op jit(solution)/shard_map/ppermute | solution.py:105
  71.5 2.7 %collective-permute-start.19 = (bf16[768,256]{1,0:T(8,128)(2,1)S(1)}, bf16[768,256]{1,0:T(8,128)(2,1)S(1)}, u32[]{:S(2)}, u32[]{:S(2)}) collective-permute-start(bf16[768,256]{1,0:T(8,128)(2,1)S(1)} %pad_maximum_fusion.13), channel_id=1, source_target_pairs={{0,1},{1,0},{2,3},{3,2},{4,5},{5,4},{6,7},{7,6},{8,9},{9,8},{10,11... | collective-permute-start | bytes 1179656 | tf_op jit(solution)/shard_map/ppermute | solution.py:105
  72.8 1.4 %collective-permute-start.20 = (bf16[256,256]{1,0:T(8,128)(2,1)S(1)}, bf16[256,256]{1,0:T(8,128)(2,1)S(1)}, u32[]{:S(2)}, u32[]{:S(2)}) collective-permute-start(bf16[256,256]{1,0:T(8,128)(2,1)S(1)} %pad_maximum_fusion.15), channel_id=1, source_target_pairs={{0,1},{1,0},{2,3},{3,2},{4,5},{5,4},{6,7},{7,6},{8,9},{9,8},{10,11... | collective-permute-start | bytes 393224 | tf_op jit(solution)/shard_map/ppermute | solution.py:105

commit v16 on v15

--- a/solution.py
+++ b/solution.py
@@ -133,14 +133,6 @@
     rim_rows = lax.ppermute(
         frames[tok_rows - (KW - 1) :], both, [(i, i + 1) for i in range(devices - 1)]
     )
-    late = convolve(frames[part:], conv_weight, frames[part - (KW - 1) : part])
-    early = convolve(frames[:part], conv_weight, rim_rows)
-
-    far_late = xor_swap(late, Z1)
-    far_early = xor_swap(early, Z1)
-    own = jnp.concatenate([early, late], axis=0)
-    beside = xor_swap(own, Y)
-
     half = features // 2
     held = qkv_weight.T.reshape(3, HD // 2, features)
 
@@ -154,14 +146,28 @@
 
     outer = to_heads(lax.dynamic_index_in_dim(held, 2 * grp, 0, False), (0, 2))
     middle = to_heads(lax.dynamic_slice_in_dim(held[1], grp * half, half, 1), (1, 1))
+    zero = zero_after(middle)
+
+    late = convolve(frames[part:], conv_weight, frames[part - (KW - 1) : part]) + zero
+    early = convolve(frames[:part], conv_weight, rim_rows) + zero
+
+    far_late = xor_swap(late, Z1)
+    own = jnp.concatenate([early, late], axis=0)
+    beside = xor_swap(own, Y)
+
     mine = jnp.concatenate([outer[:, :half], outer[:, half:], middle], axis=0)
     paired = xor_swap(mine, Z0)
 
-    far_beside_late = xor_swap(far_late + zero_after(paired), Y)
+    mine_too = xor_swap(mine, devices, every)
+    far_early = xor_swap(early + zero_after(mine_too), Z1)
+
+    cut = half // 2
+    fourth = [xor_swap(paired[:, :cut], devices, every), xor_swap(mine_too[:, cut:], Z0)]
+
+    far_beside_late = xor_swap(far_late + zero_after(fourth[0]) + zero_after(fourth[1]), Y)
     far_beside_early = xor_swap(far_early, Y)
 
-    def whole_head(pieces, index):
-        theirs = xor_swap(pieces, devices, every)
+    def whole_head(pieces, theirs, index):
         size = HD // 2
 
         def block(values, n):
@@ -181,7 +187,10 @@
         wide = lax.dynamic_slice_in_dim(jnp.stack(turned), lax.rem(index, 3), 3, 0)
         return by_bit(core, wide, xor_swap(wide, CORE), 1).reshape(3 * HD, features)
 
-    two_heads = jnp.concatenate([whole_head(mine, me), whole_head(paired, me ^ Z0)], axis=0)
+    fourth = jnp.concatenate(fourth, axis=1)
+    two_heads = jnp.concatenate(
+        [whole_head(mine, mine_too, me), whole_head(paired, fourth, me ^ Z0)], axis=0
+    )
 
     def project(rows):
         done = lax.dot_general(

time: 93 us -> 96.3 us (1.035)
  between operations: 2.07 us -> 6.02 us
  starting transfers between devices: 27.1 us -> 23.5 us
  local copies, waits for them, and re-layouts: 5.48 us -> 7.32 us
    ppermute x2, starting transfers between devices: 5.83 us -> 1.18 us  [to_heads(): return lax.ppermute(block, every, pairs)]
    ppermute x1, starting transfers between devices: 2.36 us -> 4.59 us  [body_by_head(): lax.ppermute(frames[tok_rows - (KW - 1):], both, [(i, i + 1) for i in ran...]
    slice x1 -> x4, local copies, waits for them, and re-layouts: 0.58 us -> 2.37 us  [zero_after(): last = array[(-1,) * array.ndim]]
    ppermute x18 -> x19, starting transfers between devices: 18.9 us -> 17.8 us  [xor_swap(): return lax.ppermute(value, axes, [(d, d ^ bit) for d in range(count)])]
    ppermute x18 -> x19, waiting for transfers between devices: 35.8 us -> 35.9 us  [xor_swap(): return lax.ppermute(value, axes, [(d, d ^ bit) for d in range(count)])]
  transfers between devices with their start and end apart: 21 -> 22, of which waited for: 10 -> 10; matrix products, arithmetic and copies ran while one was open for 9% -> 11% of each run, Pallas kernels for 0% -> 0%
where the time goes in v16:
time: 96.3 us; the launch traced here: 95.9 us
  waiting for transfers between devices  35.9 us (37%)
  starting transfers between devices  23.5 us (24%)
  blocking collectives  12.6 us (13%)
  local copies, waits for them, and re-layouts  7.32 us (8%)
  matrix products  6.55 us (7%)
  between operations  6.02 us (6%)
  other arithmetic  3.99 us (4%)
    ppermute x19, waiting for transfers between devices, xor_swap(): return lax.ppermute(value, axes, [(d, d ^ bit) for d in range(count)])  35.9 us
    ppermute x19, starting transfers between devices, xor_swap(): return lax.ppermute(value, axes, [(d, d ^ bit) for d in range(count)])  17.8 us
    all_to_all x1, blocking collectives, body_by_head(): lax.all_to_all(sent, 'chip', split_axis=0, concat_axis=0, tiled=True)  12.6 us
    ppermute x1, starting transfers between devices, body_by_head(): lax.ppermute(frames[tok_rows - (KW - 1):], both, [(i, i + 1) for i in ran...  4.59 us
    dot_general x2, matrix products, project(): lax.dot_general(rows, two_heads, (((1,), (1,)), ((), ())), preferred_elem...  2.62 us
    slice x4, local copies, waits for them, and re-layouts, zero_after(): last = array[(-1,) * array.ndim]  2.37 us
    dot_general x1, matrix products, body_by_head(): lax.dot_general(query, keyed[:, :HD], (((1,), (1,)), ((), ())), preferred...  2.33 us
  transfers between devices with their start and end apart: 22, of which 10 were waited for; matrix products, arithmetic and copies ran while one was open for 11% of the time, Pallas kernels for 0%

profile of v16, /device:TPU:0, one launch (start us, length us, event | category | flops | bytes accessed | tf_op | source)
XLA Modules:
  0.0 95.9 jit_solution(7670190729802559785)
XLA Ops:
  0.0 1.1 %slice.325 = bf16[64,2048]{1,0:T(8,128)(2,1)S(1)} slice(bf16[192,2048]{1,0:T(8,128)(2,1)} %bitcast.160), slice={[64:128], [0:2048]} | slice | bytes 524288 | tf_op jit(solution)/shard_map/slice | solution.py:148
  2.4 4.6 %collective-permute-start.4 = (bf16[3,2048]{1,0:T(4,128)(2,1)S(1)}, bf16[3,2048]{1,0:T(4,128)(2,1)S(1)}, u32[]{:S(2)}, u32[]{:S(2)}) collective-permute-start(bf16[3,2048]{1,0:T(4,128)(2,1)S(1)} %slice.268), channel_id=1, source_target_pairs={{0,1},{1,2},{2,3},{3,4},{4,5},{5,6},{6,7},{7,8},{8,9},{9,10},{10,1... | collective-permute-start | bytes 36872 | tf_op jit(solution)/shard_map/ppermute | solution.py:133
  9.4 4.5 %collective-permute-start = (s32[1,128]{1,0:T(1,128)S(1)}, s32[1,128]{1,0:T(1,128)S(1)}, u32[]{:S(2)}, u32[]{:S(2)}) collective-permute-start(s32[1,128]{1,0:T(1,128)S(1)} %bitcast.170), channel_id=1, source_target_pairs={{0,1},{1,0},{2,3},{3,2},{4,5},{5,4},{6,7},{7,6},{8,9},{9,8},{10,11... | collective-permute-start | bytes 1544 | tf_op jit(solution)/shard_map/ppermute | solution.py:105
  14.7 1.5 %collective-permute-start.1 = (s32[2,128]{1,0:T(2,128)S(1)}, s32[2,128]{1,0:T(2,128)S(1)}, u32[]{:S(2)}, u32[]{:S(2)}) collective-permute-start(s32[2,128]{1,0:T(2,128)S(1)} %pad_add_fusion.2), channel_id=1, source_target_pairs={{0,2},{1,3},{2,0},{3,1},{4,6},{5,7},{6,4},{7,5},{8,10},{9,11},{10,... | collective-permute-start | bytes 3080 | tf_op jit(solution)/shard_map/ppermute | solution.py:105
  16.4 1.9 %collective-permute-done.1 = s32[2,128]{1,0:T(2,128)S(1)} collective-permute-done((s32[2,128]{1,0:T(2,128)S(1)}, s32[2,128]{1,0:T(2,128)S(1)}, u32[]{:S(2)}, u32[]{:S(2)}) %collective-permute-start.1) | collective-permute-done | bytes 1056 | tf_op jit(solution)/shard_map/ppermute | solution.py:105
  18.5 3.5 %collective-permute-done.2 = s32[4,128]{1,0:T(4,128)S(1)} collective-permute-done((s32[4,128]{1,0:T(4,128)S(1)}, s32[4,128]{1,0:T(4,128)S(1)}, u32[]{:S(2)}, u32[]{:S(2)}) %collective-permute-start.2) | collective-permute-done | bytes 2080 | tf_op jit(solution)/shard_map/ppermute | solution.py:105
  25.0 1.9 %collective-permute-start.11 = (bf16[192,1024]{1,0:T(8,128)(2,1)S(1)}, bf16[192,1024]{1,0:T(8,128)(2,1)S(1)}, u32[]{:S(2)}, u32[]{:S(2)}) collective-permute-start(bf16[192,1024]{1,0:T(8,128)(2,1)S(1)} %pad_maximum_fusion.14), channel_id=1, source_target_pairs={{0,16},{1,17},{2,18},{3,19},{4,20},{5,21},{6,22},{7,23},{8,24},{9,... | collective-permute-start | bytes 1179656 | tf_op jit(solution)/shard_map/ppermute | solution.py:105
  26.8 1.2 %collective-permute-start.9 = (bf16[192,1024]{1,0:T(8,128)(2,1)S(1)}, bf16[192,1024]{1,0:T(8,128)(2,1)S(1)}, u32[]{:S(2)}, u32[]{:S(2)}) collective-permute-start(bf16[192,1024]{1,0:T(8,128)(2,1)S(1)} %pad_maximum_fusion.14), channel_id=1, source_target_pairs={{0,4},{1,5},{2,6},{3,7},{4,0},{5,1},{6,2},{7,3},{8,12},{9,13},{10,... | collective-permute-start | bytes 1179656 | tf_op jit(solution)/shard_map/ppermute | solution.py:105
  28.3 1.9 %collective-permute-start.7 = (bf16[64,2048]{1,0:T(8,128)(2,1)S(1)}, bf16[64,2048]{1,0:T(8,128)(2,1)S(1)}, u32[]{:S(2)}, u32[]{:S(2)}) collective-permute-start(bf16[64,2048]{1,0:T(8,128)(2,1)S(1)} %get-tuple-element.6), channel_id=1, source_target_pairs={{0,8},{1,9},{2,10},{3,11},{4,12},{5,13},{6,14},{7,15},{8,0},{9,1},... | collective-permute-start | bytes 786440 | tf_op jit(solution)/shard_map/ppermute | solution.py:105
  30.5 4.2 %collective-permute-done.11 = bf16[192,1024]{1,0:T(8,128)(2,1)S(1)} collective-permute-done((bf16[192,1024]{1,0:T(8,128)(2,1)S(1)}, bf16[192,1024]{1,0:T(8,128)(2,1)S(1)}, u32[]{:S(2)}, u32[]{:S(2)}) %collective-permute-start.11) | collective-permute-done | bytes 393248 | tf_op jit(solution)/shard_map/ppermute | solution.py:105
  35.7 7.5 %collective-permute-done.9 = bf16[192,1024]{1,0:T(8,128)(2,1)S(1)} collective-permute-done((bf16[192,1024]{1,0:T(8,128)(2,1)S(1)}, bf16[192,1024]{1,0:T(8,128)(2,1)S(1)}, u32[]{:S(2)}, u32[]{:S(2)}) %collective-permute-start.9) | collective-permute-done | bytes 393248 | tf_op jit(solution)/shard_map/ppermute | solution.py:105
  51.0 1.6 %collective-permute-start.13 = (bf16[64,2048]{1,0:T(8,128)(2,1)S(1)}, bf16[64,2048]{1,0:T(8,128)(2,1)S(1)}, u32[]{:S(2)}, u32[]{:S(2)}) collective-permute-start(bf16[64,2048]{1,0:T(8,128)(2,1)S(1)} %get-tuple-element.29), channel_id=1, source_target_pairs={{0,2},{1,3},{2,0},{3,1},{4,6},{5,7},{6,4},{7,5},{8,10},{9,11},{10,... | collective-permute-start | bytes 786440 | tf_op jit(solution)/shard_map/ppermute | solution.py:105
  52.9 7.9 %collective-permute-done.17 = bf16[64,2048]{1,0:T(8,128)(2,1)S(1)} collective-permute-done((bf16[64,2048]{1,0:T(8,128)(2,1)S(1)}, bf16[64,2048]{1,0:T(8,128)(2,1)S(1)}, u32[]{:S(2)}, u32[]{:S(2)}) %collective-permute-start.17) | collective-permute-done | bytes 262176 | tf_op jit(solution)/shard_map/ppermute | solution.py:105
  60.9 1.3 %collective-permute-start.18 = (bf16[64,2048]{1,0:T(8,128)(2,1)S(1)}, bf16[64,2048]{1,0:T(8,128)(2,1)S(1)}, u32[]{:S(2)}, u32[]{:S(2)}) collective-permute-start(bf16[64,2048]{1,0:T(8,128)(2,1)S(1)} %collective-permute-done.17), channel_id=1, source_target_pairs={{0,2},{1,3},{2,0},{3,1},{4,6},{5,7},{6,4},{7,5},{8,10},{9,11},{10,... | collective-permute-start | bytes 786440 | tf_op jit(solution)/shard_map/ppermute | solution.py:105
  62.9 1.4 %fusion.4 = bf16[384,768]{1,0:T(8,128)(2,1)S(1)} fusion(bf16[384,2048]{1,0:T(8,128)(2,1)S(1)} %constant_dynamic-update-slice_fusion, bf16[384,2048]{1,0:T(8,128)(2,1)S(1)} %bitcast.157, bf16[384,2048]{1,0:T(8,128)(2,1)S(1)} %bitcast.155), kind=kOutput, calls=%fused_computation.10 | convolution fusion | flops 1214545920 | bytes 5308416 | tf_op jit(solution)/shard_map/dot_general | solution.py:196
  64.5 4.6 %collective-permute-done.18 = bf16[64,2048]{1,0:T(8,128)(2,1)S(1)} collective-permute-done((bf16[64,2048]{1,0:T(8,128)(2,1)S(1)}, bf16[64,2048]{1,0:T(8,128)(2,1)S(1)}, u32[]{:S(2)}, u32[]{:S(2)}) %collective-permute-start.18) | collective-permute-done | bytes 262176 | tf_op jit(solution)/shard_map/ppermute | solution.py:105
  69.2 1.2 %fusion.6 = bf16[128,768]{1,0:T(8,128)(2,1)S(1)} fusion(bf16[384,2048]{1,0:T(8,128)(2,1)S(1)} %bitcast.158, bf16[384,2048]{1,0:T(8,128)(2,1)S(1)} %bitcast.156, bf16[64,2048]{1,0:T(8,128)(2,1)S(1)} %collective-permute-done.18, bf16[64,2048]{1,0:T(8,128)(2,1)S(1)} %collective-permute-done.17), kind=kOutput, calls=%fused_computation.12 | convolution fusion | flops 410091520 | bytes 3866624 | tf_op jit(solution)/shard_map/dot_general | solution.py:196
  70.5 3.6 %collective-permute-done.16 = bf16[384,384]{1,0:T(8,128)(2,1)S(1)} collective-permute-done((bf16[384,384]{1,0:T(8,128)(2,1)S(1)}, bf16[384,384]{1,0:T(8,128)(2,1)S(1)}, u32[]{:S(2)}, u32[]{:S(2)}) %collective-permute-start.16) | collective-permute-done | bytes 294944 | tf_op jit(solution)/shard_map/ppermute | solution.py:105
  74.2 1.1 %collective-permute-done.19 = bf16[128,384]{1,0:T(8,128)(2,1)S(1)} collective-permute-done((bf16[128,384]{1,0:T(8,128)(2,1)S(1)}, bf16[128,384]{1,0:T(8,128)(2,1)S(1)}, u32[]{:S(2)}, u32[]{:S(2)}) %collective-permute-start.19) | collective-permute-done | bytes 98336 | tf_op jit(solution)/shard_map/ppermute | solution.py:105
  75.7 1.1 %collective-permute-done.21 = bf16[256,256]{1,0:T(8,128)(2,1)S(1)} collective-permute-done((bf16[256,256]{1,0:T(8,128)(2,1)S(1)}, bf16[256,256]{1,0:T(8,128)(2,1)S(1)}, u32[]{:S(2)}, u32[]{:S(2)}) %collective-permute-start.21) | collective-permute-done | bytes 131104 | tf_op jit(solution)/shard_map/ppermute | solution.py:105
  76.8 2.3 %fusion.63 = (f32[1024]{0:T(1024)S(1)}, f32[1024,2048]{1,0:T(8,128)S(1)}) fusion(bf16[2048,256]{1,0:T(8,128)(2,1)S(1)} %fusion.8, bf16[128,384]{1,0:T(8,128)(2,1)S(1)} %collective-permute-done.19, bf16[128,384]{1,0:T(8,128)(2,1)S(1)} %get-tuple-element.33, bf16[384,384]{1,0:T(8,128)(2,1)S(1)} %collective-permute-done.16, ...), kind=kOutput, calls=%fused_computation.186 | convolution fusion | flops 550501376 | bytes 9728000 | tf_op jit(solution)/shard_map/dot_general | solution.py:231
  79.2 1.3 %fusion = f32[1024]{0:T(1024)S(1)} fusion(f32[1024,2048]{1,0:T(8,128)S(1)} %get-tuple-element.62, f32[1024]{0:T(1024)S(1)} %get-tuple-element.61), kind=kLoop, calls=%fused_computation.3 | loop fusion | flops 4193280 | bytes 8396800 | tf_op jit(solution)/shard_map/reduce_sum | solution.py:239
  80.4 1.6 %fusion.5 = bf16[1024,128]{1,0:T(8,128)(2,1)S(1)} fusion(f32[1024,2048]{1,0:T(8,128)S(1)} %get-tuple-element.62, f32[1024]{0:T(1024)S(1)} %fusion, f32[1024]{0:T(1024)S(1)} %get-tuple-element.61, bf16[2048,256]{1,0:T(8,128)(2,1)S(1)} %fusion.8), kind=kOutput, calls=%fused_computation.11 | convolution fusion | flops 543293440 | bytes 9183232 | tf_op jit(solution)/shard_map/dot_general | solution.py:240
  82.3 12.6 %all_to_all.5 = bf16[8,128,128]{2,1,0:T(8,128)(2,1)S(1)} all-to-all(bf16[8,128,128]{2,1,0:T(8,128)(2,1)S(1)} %fusion.47), channel_id=1, replica_groups=mesh['grp'=2,'chip'=8,'core'=2] {'chip'}, dimensions={0} | all-to-all | bytes 524288 | tf_op jit(solution)/shard_map/all_to_all | solution.py:249
  (119 shorter events, 14.4 us)
Async XLA Ops:
  0.0 22.6 %slice-start = ((bf16[128,2048]{1,0:T(8,128)(2,1)}), bf16[64,2048]{1,0:T(8,128)(2,1)S(1)}, s32[]{:S(2)}) async-start(bf16[128,2048]{1,0:T(8,128)(2,1)} %param.5), calls=%async_computation.1 | async-start | bytes 524288 | tf_op jit(solution)/shard_map/slice | solution.py:152
  0.0 14.1 %copy-start.1 = (bf16[4,2048]{1,0:T(4,128)(2,1)S(1)}, bf16[4,2048]{1,0:T(4,128)(2,1)}, u32[]{:S(2)}) copy-start(bf16[4,2048]{1,0:T(4,128)(2,1)} %param.6) | copy-start | bytes 49156
  1.1 21.6 %collective-permute-start.5 = (bf16[64,1024]{1,0:T(8,128)(2,1)S(1)}, bf16[64,1024]{1,0:T(8,128)(2,1)S(1)}, u32[]{:S(2)}, u32[]{:S(2)}) collective-permute-start(bf16[64,1024]{1,0:T(8,128)(2,1)S(1)} %constant_dynamic-slice_fusion.2), channel_id=1, source_target_pairs={{0,1},{1,4},{2,7},{3,10},{4,13},{5,0},{6,3},{7,6},{8,9},{9,12},{10... | collective-permute-start | bytes 393224 | tf_op jit(solution)/shard_map/ppermute | solution.py:145
  2.4 20.2 %collective-permute-start.4 = (bf16[3,2048]{1,0:T(4,128)(2,1)S(1)}, bf16[3,2048]{1,0:T(4,128)(2,1)S(1)}, u32[]{:S(2)}, u32[]{:S(2)}) collective-permute-start(bf16[3,2048]{1,0:T(4,128)(2,1)S(1)} %slice.268), channel_id=1, source_target_pairs={{0,1},{1,2},{2,3},{3,4},{4,5},{5,6},{6,7},{7,8},{8,9},{9,10},{10,1... | collective-permute-start | bytes 36872 | tf_op jit(solution)/shard_map/ppermute | solution.py:133
  7.9 16.9 %collective-permute-start.8 = (bf16[64,2048]{1,0:T(8,128)(2,1)S(1)}, bf16[64,2048]{1,0:T(8,128)(2,1)S(1)}, u32[]{:S(2)}, u32[]{:S(2)}) collective-permute-start(bf16[64,2048]{1,0:T(8,128)(2,1)S(1)} %dynamic-slice_bitcast_fusion), channel_id=1, source_target_pairs={{0,0},{1,3},{2,6},{3,9},{4,12},{5,15},{6,2},{7,5},{8,8},{9,11},{10... | collective-permute-start | bytes 786440 | tf_op jit(solution)/shard_map/ppermute | solution.py:145
  9.4 5.3 %collective-permute-start = (s32[1,128]{1,0:T(1,128)S(1)}, s32[1,128]{1,0:T(1,128)S(1)}, u32[]{:S(2)}, u32[]{:S(2)}) collective-permute-start(s32[1,128]{1,0:T(1,128)S(1)} %bitcast.170), channel_id=1, source_target_pairs={{0,1},{1,0},{2,3},{3,2},{4,5},{5,4},{6,7},{7,6},{8,9},{9,8},{10,11... | collective-permute-start | bytes 1544 | tf_op jit(solution)/shard_map/ppermute | solution.py:105
  14.7 3.6 %collective-permute-start.1 = (s32[2,128]{1,0:T(2,128)S(1)}, s32[2,128]{1,0:T(2,128)S(1)}, u32[]{:S(2)}, u32[]{:S(2)}) collective-permute-start(s32[2,128]{1,0:T(2,128)S(1)} %pad_add_fusion.2), channel_id=1, source_target_pairs={{0,2},{1,3},{2,0},{3,1},{4,6},{5,7},{6,4},{7,5},{8,10},{9,11},{10,... | collective-permute-start | bytes 3080 | tf_op jit(solution)/shard_map/ppermute | solution.py:105
  18.3 3.6 %collective-permute-start.2 = (s32[4,128]{1,0:T(4,128)S(1)}, s32[4,128]{1,0:T(4,128)S(1)}, u32[]{:S(2)}, u32[]{:S(2)}) collective-permute-start(s32[4,128]{1,0:T(4,128)S(1)} %pad_add_fusion.1), channel_id=1, source_target_pairs={{0,4},{1,5},{2,6},{3,7},{4,0},{5,1},{6,2},{7,3},{8,12},{9,13},{10,... | collective-permute-start | bytes 6152 | tf_op jit(solution)/shard_map/ppermute | solution.py:105
  22.0 53.4 %collective-permute-start.3 = (s32[8,128]{1,0:T(8,128)S(1)}, s32[8,128]{1,0:T(8,128)S(1)}, u32[]{:S(2)}, u32[]{:S(2)}) collective-permute-start(s32[8,128]{1,0:T(8,128)S(1)} %pad_add_fusion), channel_id=1, source_target_pairs={{0,8},{1,9},{2,10},{3,11},{4,12},{5,13},{6,14},{7,15},{8,0},{9,1},... | collective-permute-start | bytes 12296 | tf_op jit(solution)/shard_map/ppermute | solution.py:105
  25.0 9.8 %collective-permute-start.11 = (bf16[192,1024]{1,0:T(8,128)(2,1)S(1)}, bf16[192,1024]{1,0:T(8,128)(2,1)S(1)}, u32[]{:S(2)}, u32[]{:S(2)}) collective-permute-start(bf16[192,1024]{1,0:T(8,128)(2,1)S(1)} %pad_maximum_fusion.14), channel_id=1, source_target_pairs={{0,16},{1,17},{2,18},{3,19},{4,20},{5,21},{6,22},{7,23},{8,24},{9,... | collective-permute-start | bytes 1179656 | tf_op jit(solution)/shard_map/ppermute | solution.py:105
  26.8 16.4 %collective-permute-start.9 = (bf16[192,1024]{1,0:T(8,128)(2,1)S(1)}, bf16[192,1024]{1,0:T(8,128)(2,1)S(1)}, u32[]{:S(2)}, u32[]{:S(2)}) collective-permute-start(bf16[192,1024]{1,0:T(8,128)(2,1)S(1)} %pad_maximum_fusion.14), channel_id=1, source_target_pairs={{0,4},{1,5},{2,6},{3,7},{4,0},{5,1},{6,2},{7,3},{8,12},{9,13},{10,... | collective-permute-start | bytes 1179656 | tf_op jit(solution)/shard_map/ppermute | solution.py:105
  28.3 22.6 %collective-permute-start.7 = (bf16[64,2048]{1,0:T(8,128)(2,1)S(1)}, bf16[64,2048]{1,0:T(8,128)(2,1)S(1)}, u32[]{:S(2)}, u32[]{:S(2)}) collective-permute-start(bf16[64,2048]{1,0:T(8,128)(2,1)S(1)} %get-tuple-element.6), channel_id=1, source_target_pairs={{0,8},{1,9},{2,10},{3,11},{4,12},{5,13},{6,14},{7,15},{8,0},{9,1},... | collective-permute-start | bytes 786440 | tf_op jit(solution)/shard_map/ppermute | solution.py:105
  30.3 16.1 %collective-permute-start.6 = (bf16[128,2048]{1,0:T(8,128)(2,1)S(1)}, bf16[128,2048]{1,0:T(8,128)(2,1)S(1)}, u32[]{:S(2)}, u32[]{:S(2)}) collective-permute-start(bf16[128,2048]{1,0:T(8,128)(2,1)S(1)} %pad_maximum_fusion.12), channel_id=1, source_target_pairs={{0,2},{1,3},{2,0},{3,1},{4,6},{5,7},{6,4},{7,5},{8,10},{9,11},{10,... | collective-permute-start | bytes 1572872 | tf_op jit(solution)/shard_map/ppermute | solution.py:105
  34.7 11.8 %collective-permute-start.12 = (bf16[192,512]{1,0:T(8,128)(2,1)S(1)}, bf16[192,512]{1,0:T(8,128)(2,1)S(1)}, u32[]{:S(2)}, u32[]{:S(2)}) collective-permute-start(bf16[192,512]{1,0:T(8,128)(2,1)S(1)} %slice.335), channel_id=1, source_target_pairs={{0,4},{1,5},{2,6},{3,7},{4,0},{5,1},{6,2},{7,3},{8,12},{9,13},{10,... | collective-permute-start | bytes 589832 | tf_op jit(solution)/shard_map/ppermute | solution.py:105
  43.3 5.7 %collective-permute-start.10 = (bf16[192,512]{1,0:T(8,128)(2,1)S(1)}, bf16[192,512]{1,0:T(8,128)(2,1)S(1)}, u32[]{:S(2)}, u32[]{:S(2)}) collective-permute-start(bf16[192,512]{1,0:T(8,128)(2,1)S(1)} %slice.333), channel_id=1, source_target_pairs={{0,16},{1,17},{2,18},{3,19},{4,20},{5,21},{6,22},{7,23},{8,24},{9,... | collective-permute-start | bytes 589832 | tf_op jit(solution)/shard_map/ppermute | solution.py:105
  46.4 15.8 %collective-permute-start.14 = (bf16[3,64,2048]{2,1,0:T(8,128)(2,1)S(1)}, bf16[3,64,2048]{2,1,0:T(8,128)(2,1)S(1)}, u32[]{:S(2)}, u32[]{:S(2)}) collective-permute-start(bf16[3,64,2048]{2,1,0:T(8,128)(2,1)S(1)} %constant_dynamic-slice_fusion.1), channel_id=1, source_target_pairs={{0,1},{1,0},{2,3},{3,2},{4,5},{5,4},{6,7},{7,6},{8,9},{9,8},{10,11... | collective-permute-start | bytes 2359304 | tf_op jit(solution)/shard_map/ppermute | solution.py:105
  46.6 14.3 %collective-permute-start.17 = (bf16[64,2048]{1,0:T(8,128)(2,1)S(1)}, bf16[64,2048]{1,0:T(8,128)(2,1)S(1)}, u32[]{:S(2)}, u32[]{:S(2)}) collective-permute-start(bf16[64,2048]{1,0:T(8,128)(2,1)S(1)} %broadcast_add_fusion), channel_id=1, source_target_pairs={{0,8},{1,9},{2,10},{3,11},{4,12},{5,13},{6,14},{7,15},{8,0},{9,1},... | collective-permute-start | bytes 786440 | tf_op jit(solution)/shard_map/ppermute | solution.py:105
  51.0 11.3 %collective-permute-start.13 = (bf16[64,2048]{1,0:T(8,128)(2,1)S(1)}, bf16[64,2048]{1,0:T(8,128)(2,1)S(1)}, u32[]{:S(2)}, u32[]{:S(2)}) collective-permute-start(bf16[64,2048]{1,0:T(8,128)(2,1)S(1)} %get-tuple-element.29), channel_id=1, source_target_pairs={{0,2},{1,3},{2,0},{3,1},{4,6},{5,7},{6,4},{7,5},{8,10},{9,11},{10,... | collective-permute-start | bytes 786440 | tf_op jit(solution)/shard_map/ppermute | solution.py:105
  52.9 9.7 %collective-permute-start.15 = (bf16[3,64,2048]{2,1,0:T(8,128)(2,1)S(1)}, bf16[3,64,2048]{2,1,0:T(8,128)(2,1)S(1)}, u32[]{:S(2)}, u32[]{:S(2)}) collective-permute-start(bf16[3,64,2048]{2,1,0:T(8,128)(2,1)S(1)} %constant_dynamic-slice_fusion), channel_id=1, source_target_pairs={{0,1},{1,0},{2,3},{3,2},{4,5},{5,4},{6,7},{7,6},{8,9},{9,8},{10,11... | collective-permute-start | bytes 2359304 | tf_op jit(solution)/shard_map/ppermute | solution.py:105
  60.9 8.3 %collective-permute-start.18 = (bf16[64,2048]{1,0:T(8,128)(2,1)S(1)}, bf16[64,2048]{1,0:T(8,128)(2,1)S(1)}, u32[]{:S(2)}, u32[]{:S(2)}) collective-permute-start(bf16[64,2048]{1,0:T(8,128)(2,1)S(1)} %collective-permute-done.17), channel_id=1, source_target_pairs={{0,2},{1,3},{2,0},{3,1},{4,6},{5,7},{6,4},{7,5},{8,10},{9,11},{10,... | collective-permute-start | bytes 786440 | tf_op jit(solution)/shard_map/ppermute | solution.py:105
  64.4 9.6 %collective-permute-start.16 = (bf16[384,384]{1,0:T(8,128)(2,1)S(1)}, bf16[384,384]{1,0:T(8,128)(2,1)S(1)}, u32[]{:S(2)}, u32[]{:S(2)}) collective-permute-start(bf16[384,384]{1,0:T(8,128)(2,1)S(1)} %get-tuple-element.24), channel_id=1, source_target_pairs={{0,4},{1,5},{2,6},{3,7},{4,0},{5,1},{6,2},{7,3},{8,12},{9,13},{10,... | collective-permute-start | bytes 884744 | tf_op jit(solution)/shard_map/ppermute | solution.py:105
  70.4 4.9 %collective-permute-start.19 = (bf16[128,384]{1,0:T(8,128)(2,1)S(1)}, bf16[128,384]{1,0:T(8,128)(2,1)S(1)}, u32[]{:S(2)}, u32[]{:S(2)}) collective-permute-start(bf16[128,384]{1,0:T(8,128)(2,1)S(1)} %get-tuple-element.34), channel_id=1, source_target_pairs={{0,4},{1,5},{2,6},{3,7},{4,0},{5,1},{6,2},{7,3},{8,12},{9,13},{10,... | collective-permute-start | bytes 294920 | tf_op jit(solution)/shard_map/ppermute | solution.py:105
  74.1 2.6 %collective-permute-start.20 = (bf16[768,256]{1,0:T(8,128)(2,1)S(1)}, bf16[768,256]{1,0:T(8,128)(2,1)S(1)}, u32[]{:S(2)}, u32[]{:S(2)}) collective-permute-start(bf16[768,256]{1,0:T(8,128)(2,1)S(1)} %pad_maximum_fusion.13), channel_id=1, source_target_pairs={{0,1},{1,0},{2,3},{3,2},{4,5},{5,4},{6,7},{7,6},{8,9},{9,8},{10,11... | collective-permute-start | bytes 1179656 | tf_op jit(solution)/shard_map/ppermute | solution.py:105
  75.3 1.4 %collective-permute-start.21 = (bf16[256,256]{1,0:T(8,128)(2,1)S(1)}, bf16[256,256]{1,0:T(8,128)(2,1)S(1)}, u32[]{:S(2)}, u32[]{:S(2)}) collective-permute-start(bf16[256,256]{1,0:T(8,128)(2,1)S(1)} %pad_maximum_fusion.15), channel_id=1, source_target_pairs={{0,1},{1,0},{2,3},{3,2},{4,5},{5,4},{6,7},{7,6},{8,9},{9,8},{10,11... | collective-permute-start | bytes 393224 | tf_op jit(solution)/shard_map/ppermute | solution.py:105
  (1 other events, 13.9 us)

commit v17 on v16

--- a/solution.py
+++ b/solution.py
@@ -133,6 +133,14 @@
     rim_rows = lax.ppermute(
         frames[tok_rows - (KW - 1) :], both, [(i, i + 1) for i in range(devices - 1)]
     )
+    late = convolve(frames[part:], conv_weight, frames[part - (KW - 1) : part])
+    early = convolve(frames[:part], conv_weight, rim_rows)
+
+    far_late = xor_swap(late, Z1)
+    far_early = xor_swap(early, Z1)
+    own = jnp.concatenate([early, late], axis=0)
+    beside = xor_swap(own, Y)
+
     half = features // 2
     held = qkv_weight.T.reshape(3, HD // 2, features)
 
@@ -146,26 +154,21 @@
 
     outer = to_heads(lax.dynamic_index_in_dim(held, 2 * grp, 0, False), (0, 2))
     middle = to_heads(lax.dynamic_slice_in_dim(held[1], grp * half, half, 1), (1, 1))
-    zero = zero_after(middle)
-
-    late = convolve(frames[part:], conv_weight, frames[part - (KW - 1) : part]) + zero
-    early = convolve(frames[:part], conv_weight, rim_rows) + zero
-
-    far_late = xor_swap(late, Z1)
-    own = jnp.concatenate([early, late], axis=0)
-    beside = xor_swap(own, Y)
-
     mine = jnp.concatenate([outer[:, :half], outer[:, half:], middle], axis=0)
     paired = xor_swap(mine, Z0)
 
     mine_too = xor_swap(mine, devices, every)
-    far_early = xor_swap(early + zero_after(mine_too), Z1)
 
     cut = half // 2
     fourth = [xor_swap(paired[:, :cut], devices, every), xor_swap(mine_too[:, cut:], Z0)]
 
     far_beside_late = xor_swap(far_late + zero_after(fourth[0]) + zero_after(fourth[1]), Y)
-    far_beside_early = xor_swap(far_early, Y)
+
+    groups = track_groups(track_ids, track_owner)[None, :] + zero_after(paired).astype(jnp.int32)
+    for bit in (CORE, Y, Z0, Z1):
+        groups = jnp.concatenate([groups, xor_swap(groups, bit)], axis=0)
+    zero = jnp.where(groups[-1, -1] < 0, 1.0, 0.0).astype(jnp.bfloat16)
+    far_beside_early = xor_swap(far_early + zero, Y)
 
     def whole_head(pieces, theirs, index):
         size = HD // 2
@@ -207,10 +210,6 @@
     for pieces in (first_rows, second_rows):
         order += pieces + [(far ^ Z0, start, count) for far, start, count in pieces]
 
-    groups = track_groups(track_ids, track_owner)[None, :]
-    for bit in (CORE, Y, Z0, Z1):
-        groups = jnp.concatenate([groups, xor_swap(groups, bit)], axis=0)
-
     def of_rows(bit):
         times = [
             (me ^ far ^ bit) * tok_rows + start + jnp.arange(count, dtype=jnp.int32)

time: 96.3 us -> 103 us (1.070)
  other arithmetic: 3.99 us -> 6.9 us
  starting transfers between devices: 23.5 us -> 26.1 us
    ppermute x2, starting transfers between devices: 1.18 us -> 4.48 us  [to_heads(): return lax.ppermute(block, every, pairs)]
    add x13, other arithmetic: 0.06 us -> 1.74 us  [of_rows(): (me ^ far ^ bit) * tok_rows + start + jnp.arange(count, dtype=jnp.int32)]
    ppermute x19, starting transfers between devices: 17.8 us -> 16.5 us  [xor_swap(): return lax.ppermute(value, axes, [(d, d ^ bit) for d in range(count)])]
    slice x4 -> x3, local copies, waits for them, and re-layouts: 2.37 us -> 1.75 us  [zero_after(): last = array[(-1,) * array.ndim]]
  transfers between devices with their start and end apart: 22 -> 22, of which waited for: 10 -> 11; matrix products, arithmetic and copies ran while one was open for 11% -> 15% of each run, Pallas kernels for 0% -> 0%
where the time goes in v17:
time: 103 us
  waiting for transfers between devices  35.7 us (35%)
  starting transfers between devices  26.1 us (25%)
  blocking collectives  13.1 us (13%)
  local copies, waits for them, and re-layouts  8.21 us (8%)
  matrix products  7.47 us (7%)
  other arithmetic  6.9 us (7%)
  between operations  5.13 us (5%)
    ppermute x19, waiting for transfers between devices, xor_swap(): return lax.ppermute(value, axes, [(d, d ^ bit) for d in range(count)])  35.7 us
    ppermute x19, starting transfers between devices, xor_swap(): return lax.ppermute(value, axes, [(d, d ^ bit) for d in range(count)])  16.5 us
    all_to_all x1, blocking collectives, body_by_head(): lax.all_to_all(sent, 'chip', split_axis=0, concat_axis=0, tiled=True)  13.1 us
    ppermute x1, starting transfers between devices, body_by_head(): lax.ppermute(frames[tok_rows - (KW - 1):], both, [(i, i + 1) for i in ran...  5.11 us
    ppermute x2, starting transfers between devices, to_heads(): return lax.ppermute(block, every, pairs)  4.48 us
    dot_general x2, matrix products, project(): lax.dot_general(rows, two_heads, (((1,), (1,)), ((), ())), preferred_elem...  3.56 us
    dot_general x1, matrix products, body_by_head(): lax.dot_general(query, keyed[:, :HD], (((1,), (1,)), ((), ())), preferred...  2.31 us
  transfers between devices with their start and end apart: 22, of which 11 were waited for; matrix products, arithmetic and copies ran while one was open for 15% of the time, Pallas kernels for 0%

profile of v17, /device:TPU:0, one launch (start us, length us, event | category | flops | bytes accessed | tf_op | source)
XLA Modules:
  0.0 102.6 jit_solution(1569489087702573043)
XLA Ops:
  2.8 3.8 %collective-permute-start.1 = (bf16[64,1024]{1,0:T(8,128)(2,1)S(1)}, bf16[64,1024]{1,0:T(8,128)(2,1)S(1)}, u32[]{:S(2)}, u32[]{:S(2)}) collective-permute-start(bf16[64,1024]{1,0:T(8,128)(2,1)S(1)} %constant_dynamic-slice_fusion.2), channel_id=1, source_target_pairs={{0,1},{1,4},{2,7},{3,10},{4,13},{5,0},{6,3},{7,6},{8,9},{9,12},{10... | collective-permute-start | bytes 393224 | tf_op jit(solution)/shard_map/ppermute | solution.py:153
  7.3 5.1 %collective-permute-start.7 = (bf16[3,2048]{1,0:T(4,128)(2,1)S(1)}, bf16[3,2048]{1,0:T(4,128)(2,1)S(1)}, u32[]{:S(2)}, u32[]{:S(2)}) collective-permute-start(bf16[3,2048]{1,0:T(4,128)(2,1)S(1)} %slice.272), channel_id=1, source_target_pairs={{0,1},{1,2},{2,3},{3,4},{4,5},{5,6},{6,7},{7,8},{8,9},{9,10},{10,1... | collective-permute-start | bytes 36872 | tf_op jit(solution)/shard_map/ppermute | solution.py:133
  15.2 1.6 %collective-permute-start.8 = (bf16[128,2048]{1,0:T(8,128)(2,1)S(1)}, bf16[128,2048]{1,0:T(8,128)(2,1)S(1)}, u32[]{:S(2)}, u32[]{:S(2)}) collective-permute-start(bf16[128,2048]{1,0:T(8,128)(2,1)S(1)} %pad_maximum_fusion.12), channel_id=1, source_target_pairs={{0,2},{1,3},{2,0},{3,1},{4,6},{5,7},{6,4},{7,5},{8,10},{9,11},{10,... | collective-permute-start | bytes 1572872 | tf_op jit(solution)/shard_map/ppermute | solution.py:105
  16.9 3.8 %collective-permute-start.2 = (bf16[192,1024]{1,0:T(8,128)(2,1)S(1)}, bf16[192,1024]{1,0:T(8,128)(2,1)S(1)}, u32[]{:S(2)}, u32[]{:S(2)}) collective-permute-start(bf16[192,1024]{1,0:T(8,128)(2,1)S(1)} %pad_maximum_fusion.14), channel_id=1, source_target_pairs={{0,4},{1,5},{2,6},{3,7},{4,0},{5,1},{6,2},{7,3},{8,12},{9,13},{10,... | collective-permute-start | bytes 1179656 | tf_op jit(solution)/shard_map/ppermute | solution.py:105
  21.8 2.3 %collective-permute-start.17 = (bf16[64,2048]{1,0:T(8,128)(2,1)S(1)}, bf16[64,2048]{1,0:T(8,128)(2,1)}, u32[]{:S(2)}, u32[]{:S(2)}) collective-permute-start(bf16[64,2048]{1,0:T(8,128)(2,1)S(1)} %get-tuple-element.8), channel_id=1, source_target_pairs={{0,8},{1,9},{2,10},{3,11},{4,12},{5,13},{6,14},{7,15},{8,0},{9,1},... | collective-permute-start | bytes 786440 | tf_op jit(solution)/shard_map/ppermute | solution.py:105
  24.7 5.4 %collective-permute-done.8 = bf16[128,2048]{1,0:T(8,128)(2,1)S(1)} collective-permute-done((bf16[128,2048]{1,0:T(8,128)(2,1)S(1)}, bf16[128,2048]{1,0:T(8,128)(2,1)S(1)}, u32[]{:S(2)}, u32[]{:S(2)}) %collective-permute-start.8) | collective-permute-done | bytes 524320 | tf_op jit(solution)/shard_map/ppermute | solution.py:105
  30.9 5.6 %collective-permute-done.2 = bf16[192,1024]{1,0:T(8,128)(2,1)S(1)} collective-permute-done((bf16[192,1024]{1,0:T(8,128)(2,1)S(1)}, bf16[192,1024]{1,0:T(8,128)(2,1)S(1)}, u32[]{:S(2)}, u32[]{:S(2)}) %collective-permute-start.2) | collective-permute-done | bytes 393248 | tf_op jit(solution)/shard_map/ppermute | solution.py:105
  39.6 1.7 %collective-permute-start.4 = (s32[2,128]{1,0:T(2,128)S(1)}, s32[2,128]{1,0:T(2,128)S(1)}, u32[]{:S(2)}, u32[]{:S(2)}) collective-permute-start(s32[2,128]{1,0:T(2,128)S(1)} %pad_add_fusion.2), channel_id=1, source_target_pairs={{0,2},{1,3},{2,0},{3,1},{4,6},{5,7},{6,4},{7,5},{8,10},{9,11},{10,... | collective-permute-start | bytes 3080 | tf_op jit(solution)/shard_map/ppermute | solution.py:105
  41.3 1.9 %collective-permute-done.4 = s32[2,128]{1,0:T(2,128)S(1)} collective-permute-done((s32[2,128]{1,0:T(2,128)S(1)}, s32[2,128]{1,0:T(2,128)S(1)}, u32[]{:S(2)}, u32[]{:S(2)}) %collective-permute-start.4) | collective-permute-done | bytes 1056 | tf_op jit(solution)/shard_map/ppermute | solution.py:105
  43.2 1.8 %collective-permute-start.5 = (s32[4,128]{1,0:T(4,128)S(1)}, s32[4,128]{1,0:T(4,128)S(1)}, u32[]{:S(2)}, u32[]{:S(2)}) collective-permute-start(s32[4,128]{1,0:T(4,128)S(1)} %pad_add_fusion.1), channel_id=1, source_target_pairs={{0,4},{1,5},{2,6},{3,7},{4,0},{5,1},{6,2},{7,3},{8,12},{9,13},{10,... | collective-permute-start | bytes 6152 | tf_op jit(solution)/shard_map/ppermute | solution.py:105
  45.1 4.2 %collective-permute-done.5 = s32[4,128]{1,0:T(4,128)S(1)} collective-permute-done((s32[4,128]{1,0:T(4,128)S(1)}, s32[4,128]{1,0:T(4,128)S(1)}, u32[]{:S(2)}, u32[]{:S(2)}) %collective-permute-start.5) | collective-permute-done | bytes 2080 | tf_op jit(solution)/shard_map/ppermute | solution.py:105
  49.6 4.3 %collective-permute-done.6 = s32[8,128]{1,0:T(8,128)S(1)} collective-permute-done((s32[8,128]{1,0:T(8,128)S(1)}, s32[8,128]{1,0:T(8,128)S(1)}, u32[]{:S(2)}, u32[]{:S(2)}) %collective-permute-start.6) | collective-permute-done | bytes 4128 | tf_op jit(solution)/shard_map/ppermute | solution.py:105
  59.6 1.1 %add_add_fusion = (bf16[64,2048]{1,0:T(8,128)(2,1)S(1)}, bf16[384,2048]{1,0:T(8,128)(2,1)S(1)}) fusion(bf16[64,2048]{1,0:T(8,128)(2,1)} %collective-permute-done.9, bf16[]{:T(256)} %bitcast.33, bf16[]{:T(256)} %bitcast.32, bf16[384,2048]{1,0:T(8,128)(2,1)S(1)} %copy-done.3), kind=kLoop, calls=%fused_computation.65 | loop fusion | flops 786432 | bytes 786436 | tf_op jit(solution)/shard_map/add | solution.py:165
  62.2 1.6 %collective-permute-start.18 = (bf16[64,2048]{1,0:T(8,128)(2,1)S(1)}, bf16[64,2048]{1,0:T(8,128)(2,1)S(1)}, u32[]{:S(2)}, u32[]{:S(2)}) collective-permute-start(bf16[64,2048]{1,0:T(8,128)(2,1)S(1)} %broadcast_add_fusion), channel_id=1, source_target_pairs={{0,2},{1,3},{2,0},{3,1},{4,6},{5,7},{6,4},{7,5},{8,10},{9,11},{10,... | collective-permute-start | bytes 786440 | tf_op jit(solution)/shard_map/ppermute | solution.py:105
  63.8 6.1 %collective-permute-done.13 = bf16[64,2048]{1,0:T(8,128)(2,1)S(1)} collective-permute-done((bf16[64,2048]{1,0:T(8,128)(2,1)S(1)}, bf16[64,2048]{1,0:T(8,128)(2,1)S(1)}, u32[]{:S(2)}, u32[]{:S(2)}) %collective-permute-start.13) | collective-permute-done | bytes 262176 | tf_op jit(solution)/shard_map/ppermute | solution.py:105
  70.7 1.4 %fusion.4 = bf16[384,768]{1,0:T(8,128)(2,1)S(1)} fusion(bf16[384,2048]{1,0:T(8,128)(2,1)S(1)} %constant_dynamic-update-slice_fusion, bf16[384,2048]{1,0:T(8,128)(2,1)S(1)} %bitcast.157, bf16[384,2048]{1,0:T(8,128)(2,1)S(1)} %bitcast.155), kind=kOutput, calls=%fused_computation.10 | convolution fusion | flops 1214545920 | bytes 5308416 | tf_op jit(solution)/shard_map/dot_general | solution.py:199
  72.3 2.3 %collective-permute-done.18 = bf16[64,2048]{1,0:T(8,128)(2,1)S(1)} collective-permute-done((bf16[64,2048]{1,0:T(8,128)(2,1)S(1)}, bf16[64,2048]{1,0:T(8,128)(2,1)S(1)}, u32[]{:S(2)}, u32[]{:S(2)}) %collective-permute-start.18) | collective-permute-done | bytes 262176 | tf_op jit(solution)/shard_map/ppermute | solution.py:105
  74.6 2.1 %fusion.6 = bf16[128,768]{1,0:T(8,128)(2,1)S(1)} fusion(bf16[384,2048]{1,0:T(8,128)(2,1)S(1)} %bitcast.158, bf16[384,2048]{1,0:T(8,128)(2,1)S(1)} %bitcast.156, bf16[64,2048]{1,0:T(8,128)(2,1)S(1)} %collective-permute-done.18, bf16[64,2048]{1,0:T(8,128)(2,1)} %collective-permute-done.17), kind=kOutput, calls=%fused_computation.12 | convolution fusion | flops 410091520 | bytes 3866624 | tf_op jit(solution)/shard_map/dot_general | solution.py:199
  76.8 3.4 %collective-permute-done.16 = bf16[384,384]{1,0:T(8,128)(2,1)S(1)} collective-permute-done((bf16[384,384]{1,0:T(8,128)(2,1)S(1)}, bf16[384,384]{1,0:T(8,128)(2,1)S(1)}, u32[]{:S(2)}, u32[]{:S(2)}) %collective-permute-start.16) | collective-permute-done | bytes 294944 | tf_op jit(solution)/shard_map/ppermute | solution.py:105
  80.3 1.2 %collective-permute-done.19 = bf16[128,384]{1,0:T(8,128)(2,1)S(1)} collective-permute-done((bf16[128,384]{1,0:T(8,128)(2,1)S(1)}, bf16[128,384]{1,0:T(8,128)(2,1)S(1)}, u32[]{:S(2)}, u32[]{:S(2)}) %collective-permute-start.19) | collective-permute-done | bytes 98336 | tf_op jit(solution)/shard_map/ppermute | solution.py:105
  83.1 2.3 %fusion.61 = (f32[1024]{0:T(1024)S(1)}, f32[1024,2048]{1,0:T(8,128)S(1)}) fusion(bf16[2048,256]{1,0:T(8,128)(2,1)S(1)} %fusion.8, bf16[128,384]{1,0:T(8,128)(2,1)S(1)} %collective-permute-done.19, bf16[128,384]{1,0:T(8,128)(2,1)S(1)} %get-tuple-element.33, bf16[384,384]{1,0:T(8,128)(2,1)S(1)} %collective-permute-done.16, ...), kind=kOutput, calls=%fused_computation.185 | convolution fusion | flops 550501376 | bytes 9728000 | tf_op jit(solution)/shard_map/dot_general | solution.py:230
  85.4 1.3 %fusion = f32[1024]{0:T(1024)S(1)} fusion(f32[1024,2048]{1,0:T(8,128)S(1)} %get-tuple-element.62, f32[1024]{0:T(1024)S(1)} %get-tuple-element.61), kind=kLoop, calls=%fused_computation.3 | loop fusion | flops 4193280 | bytes 8396800 | tf_op jit(solution)/shard_map/reduce_sum | solution.py:238
  86.6 1.6 %fusion.5 = bf16[1024,128]{1,0:T(8,128)(2,1)S(1)} fusion(f32[1024,2048]{1,0:T(8,128)S(1)} %get-tuple-element.62, f32[1024]{0:T(1024)S(1)} %fusion, f32[1024]{0:T(1024)S(1)} %get-tuple-element.61, bf16[2048,256]{1,0:T(8,128)(2,1)S(1)} %fusion.8), kind=kOutput, calls=%fused_computation.11 | convolution fusion | flops 543293440 | bytes 9183232 | tf_op jit(solution)/shard_map/dot_general | solution.py:239
  88.5 13.1 %all_to_all.5 = bf16[8,128,128]{2,1,0:T(8,128)(2,1)S(1)} all-to-all(bf16[8,128,128]{2,1,0:T(8,128)(2,1)S(1)} %fusion.45), channel_id=1, replica_groups=mesh['grp'=2,'chip'=8,'core'=2] {'chip'}, dimensions={0} | all-to-all | bytes 524288 | tf_op jit(solution)/shard_map/all_to_all | solution.py:248
  (141 shorter events, 18.6 us)
Async XLA Ops:
  0.0 14.4 %slice-start = ((bf16[128,2048]{1,0:T(8,128)(2,1)}), bf16[64,2048]{1,0:T(8,128)(2,1)S(1)}, s32[]{:S(2)}) async-start(bf16[128,2048]{1,0:T(8,128)(2,1)} %param.5), calls=%async_computation.1 | async-start | bytes 524288 | tf_op jit(solution)/shard_map/slice | solution.py:137
  0.0 12.6 %copy-start.1 = (bf16[4,2048]{1,0:T(4,128)(2,1)S(1)}, bf16[4,2048]{1,0:T(4,128)(2,1)}, u32[]{:S(2)}) copy-start(bf16[4,2048]{1,0:T(4,128)(2,1)} %param.6) | copy-start | bytes 49156
  1.1 15.7 %collective-permute-start = (bf16[64,2048]{1,0:T(8,128)(2,1)S(1)}, bf16[64,2048]{1,0:T(8,128)(2,1)S(1)}, u32[]{:S(2)}, u32[]{:S(2)}) collective-permute-start(bf16[64,2048]{1,0:T(8,128)(2,1)S(1)} %dynamic-slice_bitcast_fusion), channel_id=1, source_target_pairs={{0,0},{1,3},{2,6},{3,9},{4,12},{5,15},{6,2},{7,5},{8,8},{9,11},{10... | collective-permute-start | bytes 786440 | tf_op jit(solution)/shard_map/ppermute | solution.py:153
  2.8 14.1 %collective-permute-start.1 = (bf16[64,1024]{1,0:T(8,128)(2,1)S(1)}, bf16[64,1024]{1,0:T(8,128)(2,1)S(1)}, u32[]{:S(2)}, u32[]{:S(2)}) collective-permute-start(bf16[64,1024]{1,0:T(8,128)(2,1)S(1)} %constant_dynamic-slice_fusion.2), channel_id=1, source_target_pairs={{0,1},{1,4},{2,7},{3,10},{4,13},{5,0},{6,3},{7,6},{8,9},{9,12},{10... | collective-permute-start | bytes 393224 | tf_op jit(solution)/shard_map/ppermute | solution.py:153
  7.3 7.1 %collective-permute-start.7 = (bf16[3,2048]{1,0:T(4,128)(2,1)S(1)}, bf16[3,2048]{1,0:T(4,128)(2,1)S(1)}, u32[]{:S(2)}, u32[]{:S(2)}) collective-permute-start(bf16[3,2048]{1,0:T(4,128)(2,1)S(1)} %slice.272), channel_id=1, source_target_pairs={{0,1},{1,2},{2,3},{3,4},{4,5},{5,6},{6,7},{7,8},{8,9},{9,10},{10,1... | collective-permute-start | bytes 36872 | tf_op jit(solution)/shard_map/ppermute | solution.py:133
  15.2 14.8 %collective-permute-start.8 = (bf16[128,2048]{1,0:T(8,128)(2,1)S(1)}, bf16[128,2048]{1,0:T(8,128)(2,1)S(1)}, u32[]{:S(2)}, u32[]{:S(2)}) collective-permute-start(bf16[128,2048]{1,0:T(8,128)(2,1)S(1)} %pad_maximum_fusion.12), channel_id=1, source_target_pairs={{0,2},{1,3},{2,0},{3,1},{4,6},{5,7},{6,4},{7,5},{8,10},{9,11},{10,... | collective-permute-start | bytes 1572872 | tf_op jit(solution)/shard_map/ppermute | solution.py:105
  16.9 19.6 %collective-permute-start.2 = (bf16[192,1024]{1,0:T(8,128)(2,1)S(1)}, bf16[192,1024]{1,0:T(8,128)(2,1)S(1)}, u32[]{:S(2)}, u32[]{:S(2)}) collective-permute-start(bf16[192,1024]{1,0:T(8,128)(2,1)S(1)} %pad_maximum_fusion.14), channel_id=1, source_target_pairs={{0,4},{1,5},{2,6},{3,7},{4,0},{5,1},{6,2},{7,3},{8,12},{9,13},{10,... | collective-permute-start | bytes 1179656 | tf_op jit(solution)/shard_map/ppermute | solution.py:105
  21.0 38.5 %collective-permute-start.9 = (bf16[64,2048]{1,0:T(8,128)(2,1)S(1)}, bf16[64,2048]{1,0:T(8,128)(2,1)}, u32[]{:S(2)}, u32[]{:S(2)}) collective-permute-start(bf16[64,2048]{1,0:T(8,128)(2,1)S(1)} %get-tuple-element.6), channel_id=1, source_target_pairs={{0,8},{1,9},{2,10},{3,11},{4,12},{5,13},{6,14},{7,15},{8,0},{9,1},... | collective-permute-start | bytes 786440 | tf_op jit(solution)/shard_map/ppermute | solution.py:105
  21.8 39.5 %collective-permute-start.17 = (bf16[64,2048]{1,0:T(8,128)(2,1)S(1)}, bf16[64,2048]{1,0:T(8,128)(2,1)}, u32[]{:S(2)}, u32[]{:S(2)}) collective-permute-start(bf16[64,2048]{1,0:T(8,128)(2,1)S(1)} %get-tuple-element.8), channel_id=1, source_target_pairs={{0,8},{1,9},{2,10},{3,11},{4,12},{5,13},{6,14},{7,15},{8,0},{9,1},... | collective-permute-start | bytes 786440 | tf_op jit(solution)/shard_map/ppermute | solution.py:105
  24.0 15.0 %collective-permute-start.11 = (bf16[192,1024]{1,0:T(8,128)(2,1)S(1)}, bf16[192,1024]{1,0:T(8,128)(2,1)S(1)}, u32[]{:S(2)}, u32[]{:S(2)}) collective-permute-start(bf16[192,1024]{1,0:T(8,128)(2,1)S(1)} %pad_maximum_fusion.14), channel_id=1, source_target_pairs={{0,16},{1,17},{2,18},{3,19},{4,20},{5,21},{6,22},{7,23},{8,24},{9,... | collective-permute-start | bytes 1179656 | tf_op jit(solution)/shard_map/ppermute | solution.py:105
  38.4 1.2 %collective-permute-start.3 = (s32[1,128]{1,0:T(1,128)S(1)}, s32[1,128]{1,0:T(1,128)S(1)}, u32[]{:S(2)}, u32[]{:S(2)}) collective-permute-start(s32[1,128]{1,0:T(1,128)S(1)} %fusion.63), channel_id=1, source_target_pairs={{0,1},{1,0},{2,3},{3,2},{4,5},{5,4},{6,7},{7,6},{8,9},{9,8},{10,11... | collective-permute-start | bytes 1544 | tf_op jit(solution)/shard_map/ppermute | solution.py:105
  38.5 16.6 %collective-permute-start.10 = (bf16[192,512]{1,0:T(8,128)(2,1)S(1)}, bf16[192,512]{1,0:T(8,128)(2,1)S(1)}, u32[]{:S(2)}, u32[]{:S(2)}) collective-permute-start(bf16[192,512]{1,0:T(8,128)(2,1)S(1)} %slice.333), channel_id=1, source_target_pairs={{0,16},{1,17},{2,18},{3,19},{4,20},{5,21},{6,22},{7,23},{8,24},{9,... | collective-permute-start | bytes 589832 | tf_op jit(solution)/shard_map/ppermute | solution.py:105
  39.0 16.1 %collective-permute-start.12 = (bf16[192,512]{1,0:T(8,128)(2,1)S(1)}, bf16[192,512]{1,0:T(8,128)(2,1)S(1)}, u32[]{:S(2)}, u32[]{:S(2)}) collective-permute-start(bf16[192,512]{1,0:T(8,128)(2,1)S(1)} %slice.335), channel_id=1, source_target_pairs={{0,4},{1,5},{2,6},{3,7},{4,0},{5,1},{6,2},{7,3},{8,12},{9,13},{10,... | collective-permute-start | bytes 589832 | tf_op jit(solution)/shard_map/ppermute | solution.py:105
  39.6 3.6 %collective-permute-start.4 = (s32[2,128]{1,0:T(2,128)S(1)}, s32[2,128]{1,0:T(2,128)S(1)}, u32[]{:S(2)}, u32[]{:S(2)}) collective-permute-start(s32[2,128]{1,0:T(2,128)S(1)} %pad_add_fusion.2), channel_id=1, source_target_pairs={{0,2},{1,3},{2,0},{3,1},{4,6},{5,7},{6,4},{7,5},{8,10},{9,11},{10,... | collective-permute-start | bytes 3080 | tf_op jit(solution)/shard_map/ppermute | solution.py:105
  43.2 6.1 %collective-permute-start.5 = (s32[4,128]{1,0:T(4,128)S(1)}, s32[4,128]{1,0:T(4,128)S(1)}, u32[]{:S(2)}, u32[]{:S(2)}) collective-permute-start(s32[4,128]{1,0:T(4,128)S(1)} %pad_add_fusion.1), channel_id=1, source_target_pairs={{0,4},{1,5},{2,6},{3,7},{4,0},{5,1},{6,2},{7,3},{8,12},{9,13},{10,... | collective-permute-start | bytes 6152 | tf_op jit(solution)/shard_map/ppermute | solution.py:105
  49.3 4.6 %collective-permute-start.6 = (s32[8,128]{1,0:T(8,128)S(1)}, s32[8,128]{1,0:T(8,128)S(1)}, u32[]{:S(2)}, u32[]{:S(2)}) collective-permute-start(s32[8,128]{1,0:T(8,128)S(1)} %pad_add_fusion), channel_id=1, source_target_pairs={{0,8},{1,9},{2,10},{3,11},{4,12},{5,13},{6,14},{7,15},{8,0},{9,1},... | collective-permute-start | bytes 12296 | tf_op jit(solution)/shard_map/ppermute | solution.py:105
  53.8 16.1 %collective-permute-start.14 = (bf16[3,64,2048]{2,1,0:T(8,128)(2,1)S(1)}, bf16[3,64,2048]{2,1,0:T(8,128)(2,1)S(1)}, u32[]{:S(2)}, u32[]{:S(2)}) collective-permute-start(bf16[3,64,2048]{2,1,0:T(8,128)(2,1)S(1)} %constant_dynamic-slice_fusion.1), channel_id=1, source_target_pairs={{0,1},{1,0},{2,3},{3,2},{4,5},{5,4},{6,7},{7,6},{8,9},{9,8},{10,11... | collective-permute-start | bytes 2359304 | tf_op jit(solution)/shard_map/ppermute | solution.py:105
  59.0 10.9 %collective-permute-start.15 = (bf16[3,64,2048]{2,1,0:T(8,128)(2,1)S(1)}, bf16[3,64,2048]{2,1,0:T(8,128)(2,1)S(1)}, u32[]{:S(2)}, u32[]{:S(2)}) collective-permute-start(bf16[3,64,2048]{2,1,0:T(8,128)(2,1)S(1)} %constant_dynamic-slice_fusion), channel_id=1, source_target_pairs={{0,1},{1,0},{2,3},{3,2},{4,5},{5,4},{6,7},{7,6},{8,9},{9,8},{10,11... | collective-permute-start | bytes 2359304 | tf_op jit(solution)/shard_map/ppermute | solution.py:105
  60.7 9.2 %collective-permute-start.13 = (bf16[64,2048]{1,0:T(8,128)(2,1)S(1)}, bf16[64,2048]{1,0:T(8,128)(2,1)S(1)}, u32[]{:S(2)}, u32[]{:S(2)}) collective-permute-start(bf16[64,2048]{1,0:T(8,128)(2,1)S(1)} %get-tuple-element.29), channel_id=1, source_target_pairs={{0,2},{1,3},{2,0},{3,1},{4,6},{5,7},{6,4},{7,5},{8,10},{9,11},{10,... | collective-permute-start | bytes 786440 | tf_op jit(solution)/shard_map/ppermute | solution.py:105
  62.2 12.4 %collective-permute-start.18 = (bf16[64,2048]{1,0:T(8,128)(2,1)S(1)}, bf16[64,2048]{1,0:T(8,128)(2,1)S(1)}, u32[]{:S(2)}, u32[]{:S(2)}) collective-permute-start(bf16[64,2048]{1,0:T(8,128)(2,1)S(1)} %broadcast_add_fusion), channel_id=1, source_target_pairs={{0,2},{1,3},{2,0},{3,1},{4,6},{5,7},{6,4},{7,5},{8,10},{9,11},{10,... | collective-permute-start | bytes 786440 | tf_op jit(solution)/shard_map/ppermute | solution.py:105
  72.2 8.0 %collective-permute-start.16 = (bf16[384,384]{1,0:T(8,128)(2,1)S(1)}, bf16[384,384]{1,0:T(8,128)(2,1)S(1)}, u32[]{:S(2)}, u32[]{:S(2)}) collective-permute-start(bf16[384,384]{1,0:T(8,128)(2,1)S(1)} %get-tuple-element.24), channel_id=1, source_target_pairs={{0,4},{1,5},{2,6},{3,7},{4,0},{5,1},{6,2},{7,3},{8,12},{9,13},{10,... | collective-permute-start | bytes 884744 | tf_op jit(solution)/shard_map/ppermute | solution.py:105
  76.8 4.8 %collective-permute-start.19 = (bf16[128,384]{1,0:T(8,128)(2,1)S(1)}, bf16[128,384]{1,0:T(8,128)(2,1)S(1)}, u32[]{:S(2)}, u32[]{:S(2)}) collective-permute-start(bf16[128,384]{1,0:T(8,128)(2,1)S(1)} %get-tuple-element.34), channel_id=1, source_target_pairs={{0,4},{1,5},{2,6},{3,7},{4,0},{5,1},{6,2},{7,3},{8,12},{9,13},{10,... | collective-permute-start | bytes 294920 | tf_op jit(solution)/shard_map/ppermute | solution.py:105
  80.3 2.7 %collective-permute-start.20 = (bf16[768,256]{1,0:T(8,128)(2,1)S(1)}, bf16[768,256]{1,0:T(8,128)(2,1)S(1)}, u32[]{:S(2)}, u32[]{:S(2)}) collective-permute-start(bf16[768,256]{1,0:T(8,128)(2,1)S(1)} %pad_maximum_fusion.13), channel_id=1, source_target_pairs={{0,1},{1,0},{2,3},{3,2},{4,5},{5,4},{6,7},{7,6},{8,9},{9,8},{10,11... | collective-permute-start | bytes 1179656 | tf_op jit(solution)/shard_map/ppermute | solution.py:105
  81.6 1.4 %collective-permute-start.21 = (bf16[256,256]{1,0:T(8,128)(2,1)S(1)}, bf16[256,256]{1,0:T(8,128)(2,1)S(1)}, u32[]{:S(2)}, u32[]{:S(2)}) collective-permute-start(bf16[256,256]{1,0:T(8,128)(2,1)S(1)} %pad_maximum_fusion.15), channel_id=1, source_target_pairs={{0,1},{1,0},{2,3},{3,2},{4,5},{5,4},{6,7},{7,6},{8,9},{9,8},{10,11... | collective-permute-start | bytes 393224 | tf_op jit(solution)/shard_map/ppermute | solution.py:105
  (11 other events, 64.4 us)

commit v18 on v17

--- a/solution.py
+++ b/solution.py
@@ -162,13 +162,10 @@
     cut = half // 2
     fourth = [xor_swap(paired[:, :cut], devices, every), xor_swap(mine_too[:, cut:], Z0)]
 
-    far_beside_late = xor_swap(far_late + zero_after(fourth[0]) + zero_after(fourth[1]), Y)
-
-    groups = track_groups(track_ids, track_owner)[None, :] + zero_after(paired).astype(jnp.int32)
-    for bit in (CORE, Y, Z0, Z1):
-        groups = jnp.concatenate([groups, xor_swap(groups, bit)], axis=0)
-    zero = jnp.where(groups[-1, -1] < 0, 1.0, 0.0).astype(jnp.bfloat16)
-    far_beside_early = xor_swap(far_early + zero, Y)
+    far_beside_late = xor_swap(far_late + zero_after(fourth[0]), Y)
+    far_beside_early = xor_swap(far_early, Y)
+
+    fourth = jnp.concatenate(fourth, axis=1)
 
     def whole_head(pieces, theirs, index):
         size = HD // 2
@@ -190,7 +187,6 @@
         wide = lax.dynamic_slice_in_dim(jnp.stack(turned), lax.rem(index, 3), 3, 0)
         return by_bit(core, wide, xor_swap(wide, CORE), 1).reshape(3 * HD, features)
 
-    fourth = jnp.concatenate(fourth, axis=1)
     two_heads = jnp.concatenate(
         [whole_head(mine, mine_too, me), whole_head(paired, fourth, me ^ Z0)], axis=0
     )
@@ -209,6 +205,10 @@
     order = []
     for pieces in (first_rows, second_rows):
         order += pieces + [(far ^ Z0, start, count) for far, start, count in pieces]
+
+    groups = track_groups(track_ids, track_owner)[None, :]
+    for bit in (CORE, Y, Z0, Z1):
+        groups = jnp.concatenate([groups, xor_swap(groups, bit)], axis=0)
 
     def of_rows(bit):
         times = [

time: 103 us -> 89.1 us (0.87)
  waiting for transfers between devices: 35.7 us -> 31.6 us
  between operations: 5.13 us -> 2.09 us
  other arithmetic: 6.9 us -> 3.87 us
  local copies, waits for them, and re-layouts: 8.21 us -> 5.53 us
    ppermute x19, waiting for transfers between devices: 35.7 us -> 31.6 us  [xor_swap(): return lax.ppermute(value, axes, [(d, d ^ bit) for d in range(count)])]
    ppermute x1, starting transfers between devices: 5.11 us -> 2.36 us  [body_by_head(): lax.ppermute(frames[tok_rows - (KW - 1):], both, [(i, i + 1) for i in ran...]
    add x4 -> x1, other arithmetic: 2.07 us -> 0.05 us  [body_by_head(): far_beside_late = xor_swap(far_late + zero_after(fourth[0]), Y)]
    add x13, other arithmetic: 1.74 us -> 0.06 us  [of_rows(): (me ^ far ^ bit) * tok_rows + start + jnp.arange(count, dtype=jnp.int32)]
    ppermute x2, starting transfers between devices: 4.48 us -> 5.83 us  [to_heads(): return lax.ppermute(block, every, pairs)]
    slice x3 -> x1, local copies, waits for them, and re-layouts: 1.75 us -> 0.58 us  [zero_after(): last = array[(-1,) * array.ndim]]
  transfers between devices with their start and end apart: 22 -> 22, of which waited for: 11 -> 11; matrix products, arithmetic and copies ran while one was open for 15% -> 10% of each run, Pallas kernels for 0% -> 0%
where the time goes in v18:
time: 89.1 us; the launch traced here: 88.9 us
  waiting for transfers between devices  31.6 us (35%)
  starting transfers between devices  25.6 us (29%)
  blocking collectives  13.6 us (15%)
  matrix products  6.54 us (7%)
  local copies, waits for them, and re-layouts  5.53 us (6%)
  other arithmetic  3.87 us (4%)
  between operations  2.09 us (2%)
    ppermute x19, waiting for transfers between devices, xor_swap(): return lax.ppermute(value, axes, [(d, d ^ bit) for d in range(count)])  31.6 us
    ppermute x19, starting transfers between devices, xor_swap(): return lax.ppermute(value, axes, [(d, d ^ bit) for d in range(count)])  17.4 us
    all_to_all x1, blocking collectives, body_by_head(): lax.all_to_all(sent, 'chip', split_axis=0, concat_axis=0, tiled=True)  13.6 us
    ppermute x2, starting transfers between devices, to_heads(): return lax.ppermute(block, every, pairs)  5.83 us
    dot_general x2, matrix products, project(): lax.dot_general(rows, two_heads, (((1,), (1,)), ((), ())), preferred_elem...  2.62 us
    ppermute x1, starting transfers between devices, body_by_head(): lax.ppermute(frames[tok_rows - (KW - 1):], both, [(i, i + 1) for i in ran...  2.36 us
    dot_general x1, matrix products, body_by_head(): lax.dot_general(query, keyed[:, :HD], (((1,), (1,)), ((), ())), preferred...  2.33 us
  transfers between devices with their start and end apart: 22, of which 11 were waited for; matrix products, arithmetic and copies ran while one was open for 10% of the time, Pallas kernels for 0%

profile of v18, /device:TPU:0, one launch (start us, length us, event | category | flops | bytes accessed | tf_op | source)
XLA Modules:
  0.0 88.9 jit_solution(11121524591923875115)
XLA Ops:
  0.9 2.4 %collective-permute-start.4 = (bf16[3,2048]{1,0:T(4,128)(2,1)S(1)}, bf16[3,2048]{1,0:T(4,128)(2,1)S(1)}, u32[]{:S(2)}, u32[]{:S(2)}) collective-permute-start(bf16[3,2048]{1,0:T(4,128)(2,1)S(1)} %slice.259), channel_id=1, source_target_pairs={{0,1},{1,2},{2,3},{3,4},{4,5},{5,6},{6,7},{7,8},{8,9},{9,10},{10,1... | collective-permute-start | bytes 36872 | tf_op jit(solution)/shard_map/ppermute | solution.py:133
  5.9 5.2 %collective-permute-start.8 = (bf16[64,1024]{1,0:T(8,128)(2,1)S(1)}, bf16[64,1024]{1,0:T(8,128)(2,1)S(1)}, u32[]{:S(2)}, u32[]{:S(2)}) collective-permute-start(bf16[64,1024]{1,0:T(8,128)(2,1)S(1)} %constant_dynamic-slice_fusion.2), channel_id=1, source_target_pairs={{0,1},{1,4},{2,7},{3,10},{4,13},{5,0},{6,3},{7,6},{8,9},{9,12},{10... | collective-permute-start | bytes 393224 | tf_op jit(solution)/shard_map/ppermute | solution.py:153
  11.8 1.5 %collective-permute-start = (s32[1,128]{1,0:T(1,128)S(1)}, s32[1,128]{1,0:T(1,128)S(1)}, u32[]{:S(2)}, u32[]{:S(2)}) collective-permute-start(s32[1,128]{1,0:T(1,128)S(1)} %bitcast.167), channel_id=1, source_target_pairs={{0,1},{1,0},{2,3},{3,2},{4,5},{5,4},{6,7},{7,6},{8,9},{9,8},{10,11... | collective-permute-start | bytes 1544 | tf_op jit(solution)/shard_map/ppermute | solution.py:105
  14.1 1.5 %collective-permute-start.1 = (s32[2,128]{1,0:T(2,128)S(1)}, s32[2,128]{1,0:T(2,128)S(1)}, u32[]{:S(2)}, u32[]{:S(2)}) collective-permute-start(s32[2,128]{1,0:T(2,128)S(1)} %pad_add_fusion.2), channel_id=1, source_target_pairs={{0,2},{1,3},{2,0},{3,1},{4,6},{5,7},{6,4},{7,5},{8,10},{9,11},{10,... | collective-permute-start | bytes 3080 | tf_op jit(solution)/shard_map/ppermute | solution.py:105
  15.8 1.9 %collective-permute-done.1 = s32[2,128]{1,0:T(2,128)S(1)} collective-permute-done((s32[2,128]{1,0:T(2,128)S(1)}, s32[2,128]{1,0:T(2,128)S(1)}, u32[]{:S(2)}, u32[]{:S(2)}) %collective-permute-start.1) | collective-permute-done | bytes 1056 | tf_op jit(solution)/shard_map/ppermute | solution.py:105
  17.7 2.5 %collective-permute-start.2 = (s32[4,128]{1,0:T(4,128)S(1)}, s32[4,128]{1,0:T(4,128)S(1)}, u32[]{:S(2)}, u32[]{:S(2)}) collective-permute-start(s32[4,128]{1,0:T(4,128)S(1)} %pad_add_fusion.1), channel_id=1, source_target_pairs={{0,4},{1,5},{2,6},{3,7},{4,0},{5,1},{6,2},{7,3},{8,12},{9,13},{10,... | collective-permute-start | bytes 6152 | tf_op jit(solution)/shard_map/ppermute | solution.py:105
  22.0 1.9 %collective-permute-start.9 = (bf16[192,1024]{1,0:T(8,128)(2,1)S(1)}, bf16[192,1024]{1,0:T(8,128)(2,1)S(1)}, u32[]{:S(2)}, u32[]{:S(2)}) collective-permute-start(bf16[192,1024]{1,0:T(8,128)(2,1)S(1)} %pad_maximum_fusion.14), channel_id=1, source_target_pairs={{0,4},{1,5},{2,6},{3,7},{4,0},{5,1},{6,2},{7,3},{8,12},{9,13},{10,... | collective-permute-start | bytes 1179656 | tf_op jit(solution)/shard_map/ppermute | solution.py:105
  25.1 1.4 %collective-permute-start.3 = (s32[8,128]{1,0:T(8,128)S(1)}, s32[8,128]{1,0:T(8,128)S(1)}, u32[]{:S(2)}, u32[]{:S(2)}) collective-permute-start(s32[8,128]{1,0:T(8,128)S(1)} %pad_add_fusion), channel_id=1, source_target_pairs={{0,8},{1,9},{2,10},{3,11},{4,12},{5,13},{6,14},{7,15},{8,0},{9,1},... | collective-permute-start | bytes 12296 | tf_op jit(solution)/shard_map/ppermute | solution.py:105
  26.4 7.6 %collective-permute-done.17 = bf16[64,2048]{1,0:T(8,128)(2,1)S(1)} collective-permute-done((bf16[64,2048]{1,0:T(8,128)(2,1)S(1)}, bf16[64,2048]{1,0:T(8,128)(2,1)S(1)}, u32[]{:S(2)}, u32[]{:S(2)}) %collective-permute-start.17) | collective-permute-done | bytes 262176 | tf_op jit(solution)/shard_map/ppermute | solution.py:105
  34.9 2.2 %collective-permute-done.9 = bf16[192,1024]{1,0:T(8,128)(2,1)S(1)} collective-permute-done((bf16[192,1024]{1,0:T(8,128)(2,1)S(1)}, bf16[192,1024]{1,0:T(8,128)(2,1)S(1)}, u32[]{:S(2)}, u32[]{:S(2)}) %collective-permute-start.9) | collective-permute-done | bytes 393248 | tf_op jit(solution)/shard_map/ppermute | solution.py:105
  37.1 1.5 %collective-permute-start.10 = (bf16[192,512]{1,0:T(8,128)(2,1)S(1)}, bf16[192,512]{1,0:T(8,128)(2,1)S(1)}, u32[]{:S(2)}, u32[]{:S(2)}) collective-permute-start(bf16[192,512]{1,0:T(8,128)(2,1)S(1)} %slice.320), channel_id=1, source_target_pairs={{0,16},{1,17},{2,18},{3,19},{4,20},{5,21},{6,22},{7,23},{8,24},{9,... | collective-permute-start | bytes 589832 | tf_op jit(solution)/shard_map/ppermute | solution.py:105
  39.0 3.8 %collective-permute-done.10 = bf16[192,512]{1,0:T(8,128)(2,1)S(1)} collective-permute-done((bf16[192,512]{1,0:T(8,128)(2,1)S(1)}, bf16[192,512]{1,0:T(8,128)(2,1)S(1)}, u32[]{:S(2)}, u32[]{:S(2)}) %collective-permute-start.10) | collective-permute-done | bytes 196640 | tf_op jit(solution)/shard_map/ppermute | solution.py:105
  45.0 2.5 %collective-permute-done.6 = bf16[64,2048]{1,0:T(8,128)(2,1)S(1)} collective-permute-done((bf16[64,2048]{1,0:T(8,128)(2,1)S(1)}, bf16[64,2048]{1,0:T(8,128)(2,1)S(1)}, u32[]{:S(2)}, u32[]{:S(2)}) %collective-permute-start.6) | collective-permute-done | bytes 262176 | tf_op jit(solution)/shard_map/ppermute | solution.py:105
  47.6 1.4 %collective-permute-start.11 = (bf16[64,2048]{1,0:T(8,128)(2,1)S(1)}, bf16[64,2048]{1,0:T(8,128)(2,1)S(1)}, u32[]{:S(2)}, u32[]{:S(2)}) collective-permute-start(bf16[64,2048]{1,0:T(8,128)(2,1)S(1)} %get-tuple-element.29), channel_id=1, source_target_pairs={{0,2},{1,3},{2,0},{3,1},{4,6},{5,7},{6,4},{7,5},{8,10},{9,11},{10,... | collective-permute-start | bytes 786440 | tf_op jit(solution)/shard_map/ppermute | solution.py:105
  49.0 2.5 %collective-permute-done.14 = bf16[192,512]{1,0:T(8,128)(2,1)S(1)} collective-permute-done((bf16[192,512]{1,0:T(8,128)(2,1)S(1)}, bf16[192,512]{1,0:T(8,128)(2,1)S(1)}, u32[]{:S(2)}, u32[]{:S(2)}) %collective-permute-start.14) | collective-permute-done | bytes 196640 | tf_op jit(solution)/shard_map/ppermute | solution.py:105
  51.8 3.5 %collective-permute-done.11 = bf16[64,2048]{1,0:T(8,128)(2,1)S(1)} collective-permute-done((bf16[64,2048]{1,0:T(8,128)(2,1)S(1)}, bf16[64,2048]{1,0:T(8,128)(2,1)S(1)}, u32[]{:S(2)}, u32[]{:S(2)}) %collective-permute-start.11) | collective-permute-done | bytes 262176 | tf_op jit(solution)/shard_map/ppermute | solution.py:105
  56.1 1.4 %fusion.4 = bf16[384,768]{1,0:T(8,128)(2,1)S(1)} fusion(bf16[384,2048]{1,0:T(8,128)(2,1)S(1)} %constant_dynamic-update-slice_fusion, bf16[384,2048]{1,0:T(8,128)(2,1)S(1)} %bitcast.154, bf16[384,2048]{1,0:T(8,128)(2,1)S(1)} %bitcast.152), kind=kOutput, calls=%fused_computation.10 | convolution fusion | flops 1214545920 | bytes 5308416 | tf_op jit(solution)/shard_map/dot_general | solution.py:195
  57.7 1.2 %fusion.6 = bf16[128,768]{1,0:T(8,128)(2,1)S(1)} fusion(bf16[384,2048]{1,0:T(8,128)(2,1)S(1)} %bitcast.155, bf16[384,2048]{1,0:T(8,128)(2,1)S(1)} %bitcast.153, bf16[64,2048]{1,0:T(8,128)(2,1)S(1)} %collective-permute-done.18, bf16[64,2048]{1,0:T(8,128)(2,1)S(1)} %collective-permute-done.17), kind=kOutput, calls=%fused_computation.12 | convolution fusion | flops 410091520 | bytes 3866624 | tf_op jit(solution)/shard_map/dot_general | solution.py:195
  58.9 2.1 %collective-permute-start.19 = (bf16[128,384]{1,0:T(8,128)(2,1)S(1)}, bf16[128,384]{1,0:T(8,128)(2,1)S(1)}, u32[]{:S(2)}, u32[]{:S(2)}) collective-permute-start(bf16[128,384]{1,0:T(8,128)(2,1)S(1)} %get-tuple-element.34), channel_id=1, source_target_pairs={{0,4},{1,5},{2,6},{3,7},{4,0},{5,1},{6,2},{7,3},{8,12},{9,13},{10,... | collective-permute-start | bytes 294920 | tf_op jit(solution)/shard_map/ppermute | solution.py:105
  61.0 5.3 %collective-permute-done.16 = bf16[384,384]{1,0:T(8,128)(2,1)S(1)} collective-permute-done((bf16[384,384]{1,0:T(8,128)(2,1)S(1)}, bf16[384,384]{1,0:T(8,128)(2,1)S(1)}, u32[]{:S(2)}, u32[]{:S(2)}) %collective-permute-start.16) | collective-permute-done | bytes 294944 | tf_op jit(solution)/shard_map/ppermute | solution.py:105
  68.8 2.3 %fusion.61 = (f32[1024]{0:T(1024)S(1)}, f32[1024,2048]{1,0:T(8,128)S(1)}) fusion(bf16[2048,256]{1,0:T(8,128)(2,1)S(1)} %fusion.8, bf16[128,384]{1,0:T(8,128)(2,1)S(1)} %collective-permute-done.19, bf16[128,384]{1,0:T(8,128)(2,1)S(1)} %get-tuple-element.33, bf16[384,384]{1,0:T(8,128)(2,1)S(1)} %collective-permute-done.16, ...), kind=kOutput, calls=%fused_computation.183 | convolution fusion | flops 550501376 | bytes 9728000 | tf_op jit(solution)/shard_map/dot_general | solution.py:230
  71.1 1.3 %fusion = f32[1024]{0:T(1024)S(1)} fusion(f32[1024,2048]{1,0:T(8,128)S(1)} %get-tuple-element.62, f32[1024]{0:T(1024)S(1)} %get-tuple-element.61), kind=kLoop, calls=%fused_computation.3 | loop fusion | flops 4193280 | bytes 8396800 | tf_op jit(solution)/shard_map/reduce_sum | solution.py:238
  72.4 1.6 %fusion.5 = bf16[1024,128]{1,0:T(8,128)(2,1)S(1)} fusion(f32[1024,2048]{1,0:T(8,128)S(1)} %get-tuple-element.62, f32[1024]{0:T(1024)S(1)} %fusion, f32[1024]{0:T(1024)S(1)} %get-tuple-element.61, bf16[2048,256]{1,0:T(8,128)(2,1)S(1)} %fusion.8), kind=kOutput, calls=%fused_computation.11 | convolution fusion | flops 543293440 | bytes 9183232 | tf_op jit(solution)/shard_map/dot_general | solution.py:239
  74.2 13.6 %all_to_all.5 = bf16[8,128,128]{2,1,0:T(8,128)(2,1)S(1)} all-to-all(bf16[8,128,128]{2,1,0:T(8,128)(2,1)S(1)} %fusion.45), channel_id=1, replica_groups=mesh['grp'=2,'chip'=8,'core'=2] {'chip'}, dimensions={0} | all-to-all | bytes 524288 | tf_op jit(solution)/shard_map/all_to_all | solution.py:248
  (115 shorter events, 14.9 us)
Async XLA Ops:
  0.0 20.2 %slice-start = ((bf16[128,2048]{1,0:T(8,128)(2,1)}), bf16[64,2048]{1,0:T(8,128)(2,1)S(1)}, s32[]{:S(2)}) async-start(bf16[128,2048]{1,0:T(8,128)(2,1)} %param.5), calls=%async_computation.1 | async-start | bytes 524288 | tf_op jit(solution)/shard_map/slice | solution.py:137
  0.0 13.5 %copy-start.1 = (bf16[4,2048]{1,0:T(4,128)(2,1)S(1)}, bf16[4,2048]{1,0:T(4,128)(2,1)}, u32[]{:S(2)}) copy-start(bf16[4,2048]{1,0:T(4,128)(2,1)} %param.6) | copy-start | bytes 49156
  0.9 19.3 %collective-permute-start.4 = (bf16[3,2048]{1,0:T(4,128)(2,1)S(1)}, bf16[3,2048]{1,0:T(4,128)(2,1)S(1)}, u32[]{:S(2)}, u32[]{:S(2)}) collective-permute-start(bf16[3,2048]{1,0:T(4,128)(2,1)S(1)} %slice.259), channel_id=1, source_target_pairs={{0,1},{1,2},{2,3},{3,4},{4,5},{5,6},{6,7},{7,8},{8,9},{9,10},{10,1... | collective-permute-start | bytes 36872 | tf_op jit(solution)/shard_map/ppermute | solution.py:133
  4.2 17.8 %collective-permute-start.7 = (bf16[64,2048]{1,0:T(8,128)(2,1)S(1)}, bf16[64,2048]{1,0:T(8,128)(2,1)S(1)}, u32[]{:S(2)}, u32[]{:S(2)}) collective-permute-start(bf16[64,2048]{1,0:T(8,128)(2,1)S(1)} %dynamic-slice_bitcast_fusion), channel_id=1, source_target_pairs={{0,0},{1,3},{2,6},{3,9},{4,12},{5,15},{6,2},{7,5},{8,8},{9,11},{10... | collective-permute-start | bytes 786440 | tf_op jit(solution)/shard_map/ppermute | solution.py:153
  5.9 16.1 %collective-permute-start.8 = (bf16[64,1024]{1,0:T(8,128)(2,1)S(1)}, bf16[64,1024]{1,0:T(8,128)(2,1)S(1)}, u32[]{:S(2)}, u32[]{:S(2)}) collective-permute-start(bf16[64,1024]{1,0:T(8,128)(2,1)S(1)} %constant_dynamic-slice_fusion.2), channel_id=1, source_target_pairs={{0,1},{1,4},{2,7},{3,10},{4,13},{5,0},{6,3},{7,6},{8,9},{9,12},{10... | collective-permute-start | bytes 393224 | tf_op jit(solution)/shard_map/ppermute | solution.py:153
  11.8 2.3 %collective-permute-start = (s32[1,128]{1,0:T(1,128)S(1)}, s32[1,128]{1,0:T(1,128)S(1)}, u32[]{:S(2)}, u32[]{:S(2)}) collective-permute-start(s32[1,128]{1,0:T(1,128)S(1)} %bitcast.167), channel_id=1, source_target_pairs={{0,1},{1,0},{2,3},{3,2},{4,5},{5,4},{6,7},{7,6},{8,9},{9,8},{10,11... | collective-permute-start | bytes 1544 | tf_op jit(solution)/shard_map/ppermute | solution.py:105
  14.1 3.6 %collective-permute-start.1 = (s32[2,128]{1,0:T(2,128)S(1)}, s32[2,128]{1,0:T(2,128)S(1)}, u32[]{:S(2)}, u32[]{:S(2)}) collective-permute-start(s32[2,128]{1,0:T(2,128)S(1)} %pad_add_fusion.2), channel_id=1, source_target_pairs={{0,2},{1,3},{2,0},{3,1},{4,6},{5,7},{6,4},{7,5},{8,10},{9,11},{10,... | collective-permute-start | bytes 3080 | tf_op jit(solution)/shard_map/ppermute | solution.py:105
  17.7 7.3 %collective-permute-start.2 = (s32[4,128]{1,0:T(4,128)S(1)}, s32[4,128]{1,0:T(4,128)S(1)}, u32[]{:S(2)}, u32[]{:S(2)}) collective-permute-start(s32[4,128]{1,0:T(4,128)S(1)} %pad_add_fusion.1), channel_id=1, source_target_pairs={{0,4},{1,5},{2,6},{3,7},{4,0},{5,1},{6,2},{7,3},{8,12},{9,13},{10,... | collective-permute-start | bytes 6152 | tf_op jit(solution)/shard_map/ppermute | solution.py:105
  20.5 13.5 %collective-permute-start.17 = (bf16[64,2048]{1,0:T(8,128)(2,1)S(1)}, bf16[64,2048]{1,0:T(8,128)(2,1)S(1)}, u32[]{:S(2)}, u32[]{:S(2)}) collective-permute-start(bf16[64,2048]{1,0:T(8,128)(2,1)S(1)} %get-tuple-element.8), channel_id=1, source_target_pairs={{0,8},{1,9},{2,10},{3,11},{4,12},{5,13},{6,14},{7,15},{8,0},{9,1},... | collective-permute-start | bytes 786440 | tf_op jit(solution)/shard_map/ppermute | solution.py:105
  21.1 12.9 %collective-permute-start.5 = (bf16[128,2048]{1,0:T(8,128)(2,1)S(1)}, bf16[128,2048]{1,0:T(8,128)(2,1)S(1)}, u32[]{:S(2)}, u32[]{:S(2)}) collective-permute-start(bf16[128,2048]{1,0:T(8,128)(2,1)S(1)} %pad_maximum_fusion.12), channel_id=1, source_target_pairs={{0,2},{1,3},{2,0},{3,1},{4,6},{5,7},{6,4},{7,5},{8,10},{9,11},{10,... | collective-permute-start | bytes 1572872 | tf_op jit(solution)/shard_map/ppermute | solution.py:105
  22.0 15.1 %collective-permute-start.9 = (bf16[192,1024]{1,0:T(8,128)(2,1)S(1)}, bf16[192,1024]{1,0:T(8,128)(2,1)S(1)}, u32[]{:S(2)}, u32[]{:S(2)}) collective-permute-start(bf16[192,1024]{1,0:T(8,128)(2,1)S(1)} %pad_maximum_fusion.14), channel_id=1, source_target_pairs={{0,4},{1,5},{2,6},{3,7},{4,0},{5,1},{6,2},{7,3},{8,12},{9,13},{10,... | collective-permute-start | bytes 1179656 | tf_op jit(solution)/shard_map/ppermute | solution.py:105
  23.9 14.8 %collective-permute-start.12 = (bf16[192,1024]{1,0:T(8,128)(2,1)S(1)}, bf16[192,1024]{1,0:T(8,128)(2,1)S(1)}, u32[]{:S(2)}, u32[]{:S(2)}) collective-permute-start(bf16[192,1024]{1,0:T(8,128)(2,1)S(1)} %pad_maximum_fusion.14), channel_id=1, source_target_pairs={{0,16},{1,17},{2,18},{3,19},{4,20},{5,21},{6,22},{7,23},{8,24},{9,... | collective-permute-start | bytes 1179656 | tf_op jit(solution)/shard_map/ppermute | solution.py:105
  25.1 42.3 %collective-permute-start.3 = (s32[8,128]{1,0:T(8,128)S(1)}, s32[8,128]{1,0:T(8,128)S(1)}, u32[]{:S(2)}, u32[]{:S(2)}) collective-permute-start(s32[8,128]{1,0:T(8,128)S(1)} %pad_add_fusion), channel_id=1, source_target_pairs={{0,8},{1,9},{2,10},{3,11},{4,12},{5,13},{6,14},{7,15},{8,0},{9,1},... | collective-permute-start | bytes 12296 | tf_op jit(solution)/shard_map/ppermute | solution.py:105
  34.0 13.5 %collective-permute-start.6 = (bf16[64,2048]{1,0:T(8,128)(2,1)S(1)}, bf16[64,2048]{1,0:T(8,128)(2,1)S(1)}, u32[]{:S(2)}, u32[]{:S(2)}) collective-permute-start(bf16[64,2048]{1,0:T(8,128)(2,1)S(1)} %get-tuple-element.6), channel_id=1, source_target_pairs={{0,8},{1,9},{2,10},{3,11},{4,12},{5,13},{6,14},{7,15},{8,0},{9,1},... | collective-permute-start | bytes 786440 | tf_op jit(solution)/shard_map/ppermute | solution.py:105
  34.0 23.6 %collective-permute-start.18 = (bf16[64,2048]{1,0:T(8,128)(2,1)S(1)}, bf16[64,2048]{1,0:T(8,128)(2,1)S(1)}, u32[]{:S(2)}, u32[]{:S(2)}) collective-permute-start(bf16[64,2048]{1,0:T(8,128)(2,1)S(1)} %collective-permute-done.17), channel_id=1, source_target_pairs={{0,2},{1,3},{2,0},{3,1},{4,6},{5,7},{6,4},{7,5},{8,10},{9,11},{10,... | collective-permute-start | bytes 786440 | tf_op jit(solution)/shard_map/ppermute | solution.py:105
  37.1 5.7 %collective-permute-start.10 = (bf16[192,512]{1,0:T(8,128)(2,1)S(1)}, bf16[192,512]{1,0:T(8,128)(2,1)S(1)}, u32[]{:S(2)}, u32[]{:S(2)}) collective-permute-start(bf16[192,512]{1,0:T(8,128)(2,1)S(1)} %slice.320), channel_id=1, source_target_pairs={{0,16},{1,17},{2,18},{3,19},{4,20},{5,21},{6,22},{7,23},{8,24},{9,... | collective-permute-start | bytes 589832 | tf_op jit(solution)/shard_map/ppermute | solution.py:105
  38.9 16.4 %collective-permute-start.13 = (bf16[3,64,2048]{2,1,0:T(8,128)(2,1)S(1)}, bf16[3,64,2048]{2,1,0:T(8,128)(2,1)S(1)}, u32[]{:S(2)}, u32[]{:S(2)}) collective-permute-start(bf16[3,64,2048]{2,1,0:T(8,128)(2,1)S(1)} %constant_dynamic-slice_fusion.1), channel_id=1, source_target_pairs={{0,1},{1,0},{2,3},{3,2},{4,5},{5,4},{6,7},{7,6},{8,9},{9,8},{10,11... | collective-permute-start | bytes 2359304 | tf_op jit(solution)/shard_map/ppermute | solution.py:105
  42.9 8.6 %collective-permute-start.14 = (bf16[192,512]{1,0:T(8,128)(2,1)S(1)}, bf16[192,512]{1,0:T(8,128)(2,1)S(1)}, u32[]{:S(2)}, u32[]{:S(2)}) collective-permute-start(bf16[192,512]{1,0:T(8,128)(2,1)S(1)} %slice.326), channel_id=1, source_target_pairs={{0,4},{1,5},{2,6},{3,7},{4,0},{5,1},{6,2},{7,3},{8,12},{9,13},{10,... | collective-permute-start | bytes 589832 | tf_op jit(solution)/shard_map/ppermute | solution.py:105
  47.6 7.8 %collective-permute-start.11 = (bf16[64,2048]{1,0:T(8,128)(2,1)S(1)}, bf16[64,2048]{1,0:T(8,128)(2,1)S(1)}, u32[]{:S(2)}, u32[]{:S(2)}) collective-permute-start(bf16[64,2048]{1,0:T(8,128)(2,1)S(1)} %get-tuple-element.29), channel_id=1, source_target_pairs={{0,2},{1,3},{2,0},{3,1},{4,6},{5,7},{6,4},{7,5},{8,10},{9,11},{10,... | collective-permute-start | bytes 786440 | tf_op jit(solution)/shard_map/ppermute | solution.py:105
  51.8 3.9 %collective-permute-start.15 = (bf16[3,64,2048]{2,1,0:T(8,128)(2,1)S(1)}, bf16[3,64,2048]{2,1,0:T(8,128)(2,1)S(1)}, u32[]{:S(2)}, u32[]{:S(2)}) collective-permute-start(bf16[3,64,2048]{2,1,0:T(8,128)(2,1)S(1)} %constant_dynamic-slice_fusion), channel_id=1, source_target_pairs={{0,1},{1,0},{2,3},{3,2},{4,5},{5,4},{6,7},{7,6},{8,9},{9,8},{10,11... | collective-permute-start | bytes 2359304 | tf_op jit(solution)/shard_map/ppermute | solution.py:105
  57.6 8.6 %collective-permute-start.16 = (bf16[384,384]{1,0:T(8,128)(2,1)S(1)}, bf16[384,384]{1,0:T(8,128)(2,1)S(1)}, u32[]{:S(2)}, u32[]{:S(2)}) collective-permute-start(bf16[384,384]{1,0:T(8,128)(2,1)S(1)} %get-tuple-element.24), channel_id=1, source_target_pairs={{0,4},{1,5},{2,6},{3,7},{4,0},{5,1},{6,2},{7,3},{8,12},{9,13},{10,... | collective-permute-start | bytes 884744 | tf_op jit(solution)/shard_map/ppermute | solution.py:105
  58.9 8.4 %collective-permute-start.19 = (bf16[128,384]{1,0:T(8,128)(2,1)S(1)}, bf16[128,384]{1,0:T(8,128)(2,1)S(1)}, u32[]{:S(2)}, u32[]{:S(2)}) collective-permute-start(bf16[128,384]{1,0:T(8,128)(2,1)S(1)} %get-tuple-element.34), channel_id=1, source_target_pairs={{0,4},{1,5},{2,6},{3,7},{4,0},{5,1},{6,2},{7,3},{8,12},{9,13},{10,... | collective-permute-start | bytes 294920 | tf_op jit(solution)/shard_map/ppermute | solution.py:105
  66.2 2.5 %collective-permute-start.20 = (bf16[768,256]{1,0:T(8,128)(2,1)S(1)}, bf16[768,256]{1,0:T(8,128)(2,1)S(1)}, u32[]{:S(2)}, u32[]{:S(2)}) collective-permute-start(bf16[768,256]{1,0:T(8,128)(2,1)S(1)} %pad_maximum_fusion.13), channel_id=1, source_target_pairs={{0,1},{1,0},{2,3},{3,2},{4,5},{5,4},{6,7},{7,6},{8,9},{9,8},{10,11... | collective-permute-start | bytes 1179656 | tf_op jit(solution)/shard_map/ppermute | solution.py:105
  67.3 1.4 %collective-permute-start.21 = (bf16[256,256]{1,0:T(8,128)(2,1)S(1)}, bf16[256,256]{1,0:T(8,128)(2,1)S(1)}, u32[]{:S(2)}, u32[]{:S(2)}) collective-permute-start(bf16[256,256]{1,0:T(8,128)(2,1)S(1)} %pad_maximum_fusion.15), channel_id=1, source_target_pairs={{0,1},{1,0},{2,3},{3,2},{4,5},{5,4},{6,7},{7,6},{8,9},{9,8},{10,11... | collective-permute-start | bytes 393224 | tf_op jit(solution)/shard_map/ppermute | solution.py:105
  (1 other events, 13.3 us)

commit v19 on v18

--- a/solution.py
+++ b/solution.py
@@ -162,7 +162,7 @@
     cut = half // 2
     fourth = [xor_swap(paired[:, :cut], devices, every), xor_swap(mine_too[:, cut:], Z0)]
 
-    far_beside_late = xor_swap(far_late + zero_after(fourth[0]), Y)
+    far_beside_late = xor_swap(far_late + zero_after(fourth[0]) + zero_after(fourth[1]), Y)
     far_beside_early = xor_swap(far_early, Y)
 
     fourth = jnp.concatenate(fourth, axis=1)

time: 89.1 us -> 89 us (level)
  between operations: 2.09 us -> 3.41 us
  waiting for transfers between devices: 31.6 us -> 30.4 us
  blocking collectives: 13.6 us -> 12.7 us
    ppermute x19, waiting for transfers between devices: 31.6 us -> 30.4 us  [xor_swap(): return lax.ppermute(value, axes, [(d, d ^ bit) for d in range(count)])]
    all_to_all x1, blocking collectives: 13.6 us -> 12.7 us  [body_by_head(): lax.all_to_all(sent, 'chip', split_axis=0, concat_axis=0, tiled=True)]
  transfers between devices with their start and end apart: 22 -> 22, of which waited for: 11 -> 10; matrix products, arithmetic and copies ran while one was open for 10% -> 10% of each run, Pallas kernels for 0% -> 0%
where the time goes in v19:
time: 89 us; the launch traced here: 88.7 us
  waiting for transfers between devices  30.4 us (34%)
  starting transfers between devices  25.6 us (29%)
  blocking collectives  12.7 us (14%)
  matrix products  6.54 us (7%)
  local copies, waits for them, and re-layouts  6.12 us (7%)
  other arithmetic  3.91 us (4%)
  between operations  3.41 us (4%)
    ppermute x19, waiting for transfers between devices, xor_swap(): return lax.ppermute(value, axes, [(d, d ^ bit) for d in range(count)])  30.4 us
    ppermute x19, starting transfers between devices, xor_swap(): return lax.ppermute(value, axes, [(d, d ^ bit) for d in range(count)])  17.4 us
    all_to_all x1, blocking collectives, body_by_head(): lax.all_to_all(sent, 'chip', split_axis=0, concat_axis=0, tiled=True)  12.7 us
    ppermute x2, starting transfers between devices, to_heads(): return lax.ppermute(block, every, pairs)  5.83 us
    dot_general x2, matrix products, project(): lax.dot_general(rows, two_heads, (((1,), (1,)), ((), ())), preferred_elem...  2.61 us
    ppermute x1, starting transfers between devices, body_by_head(): lax.ppermute(frames[tok_rows - (KW - 1):], both, [(i, i + 1) for i in ran...  2.36 us
    dot_general x1, matrix products, body_by_head(): lax.dot_general(query, keyed[:, :HD], (((1,), (1,)), ((), ())), preferred...  2.33 us
  transfers between devices with their start and end apart: 22, of which 10 were waited for; matrix products, arithmetic and copies ran while one was open for 10% of the time, Pallas kernels for 0%

profile of v19, /device:TPU:0, one launch (start us, length us, event | category | flops | bytes accessed | tf_op | source)
XLA Modules:
  0.0 88.7 jit_solution(11447140855593405586)
XLA Ops:
  0.9 2.4 %collective-permute-start.4 = (bf16[3,2048]{1,0:T(4,128)(2,1)S(1)}, bf16[3,2048]{1,0:T(4,128)(2,1)S(1)}, u32[]{:S(2)}, u32[]{:S(2)}) collective-permute-start(bf16[3,2048]{1,0:T(4,128)(2,1)S(1)} %slice.262), channel_id=1, source_target_pairs={{0,1},{1,2},{2,3},{3,4},{4,5},{5,6},{6,7},{7,8},{8,9},{9,10},{10,1... | collective-permute-start | bytes 36872 | tf_op jit(solution)/shard_map/ppermute | solution.py:133
  5.9 5.2 %collective-permute-start.8 = (bf16[64,1024]{1,0:T(8,128)(2,1)S(1)}, bf16[64,1024]{1,0:T(8,128)(2,1)S(1)}, u32[]{:S(2)}, u32[]{:S(2)}) collective-permute-start(bf16[64,1024]{1,0:T(8,128)(2,1)S(1)} %constant_dynamic-slice_fusion.2), channel_id=1, source_target_pairs={{0,1},{1,4},{2,7},{3,10},{4,13},{5,0},{6,3},{7,6},{8,9},{9,12},{10... | collective-permute-start | bytes 393224 | tf_op jit(solution)/shard_map/ppermute | solution.py:153
  11.8 1.5 %collective-permute-start = (s32[1,128]{1,0:T(1,128)S(1)}, s32[1,128]{1,0:T(1,128)S(1)}, u32[]{:S(2)}, u32[]{:S(2)}) collective-permute-start(s32[1,128]{1,0:T(1,128)S(1)} %bitcast.168), channel_id=1, source_target_pairs={{0,1},{1,0},{2,3},{3,2},{4,5},{5,4},{6,7},{7,6},{8,9},{9,8},{10,11... | collective-permute-start | bytes 1544 | tf_op jit(solution)/shard_map/ppermute | solution.py:105
  14.1 1.5 %collective-permute-start.1 = (s32[2,128]{1,0:T(2,128)S(1)}, s32[2,128]{1,0:T(2,128)S(1)}, u32[]{:S(2)}, u32[]{:S(2)}) collective-permute-start(s32[2,128]{1,0:T(2,128)S(1)} %pad_add_fusion.2), channel_id=1, source_target_pairs={{0,2},{1,3},{2,0},{3,1},{4,6},{5,7},{6,4},{7,5},{8,10},{9,11},{10,... | collective-permute-start | bytes 3080 | tf_op jit(solution)/shard_map/ppermute | solution.py:105
  15.8 1.9 %collective-permute-done.1 = s32[2,128]{1,0:T(2,128)S(1)} collective-permute-done((s32[2,128]{1,0:T(2,128)S(1)}, s32[2,128]{1,0:T(2,128)S(1)}, u32[]{:S(2)}, u32[]{:S(2)}) %collective-permute-start.1) | collective-permute-done | bytes 1056 | tf_op jit(solution)/shard_map/ppermute | solution.py:105
  17.7 2.5 %collective-permute-start.2 = (s32[4,128]{1,0:T(4,128)S(1)}, s32[4,128]{1,0:T(4,128)S(1)}, u32[]{:S(2)}, u32[]{:S(2)}) collective-permute-start(s32[4,128]{1,0:T(4,128)S(1)} %pad_add_fusion.1), channel_id=1, source_target_pairs={{0,4},{1,5},{2,6},{3,7},{4,0},{5,1},{6,2},{7,3},{8,12},{9,13},{10,... | collective-permute-start | bytes 6152 | tf_op jit(solution)/shard_map/ppermute | solution.py:105
  22.0 1.9 %collective-permute-start.9 = (bf16[192,1024]{1,0:T(8,128)(2,1)S(1)}, bf16[192,1024]{1,0:T(8,128)(2,1)S(1)}, u32[]{:S(2)}, u32[]{:S(2)}) collective-permute-start(bf16[192,1024]{1,0:T(8,128)(2,1)S(1)} %pad_maximum_fusion.14), channel_id=1, source_target_pairs={{0,4},{1,5},{2,6},{3,7},{4,0},{5,1},{6,2},{7,3},{8,12},{9,13},{10,... | collective-permute-start | bytes 1179656 | tf_op jit(solution)/shard_map/ppermute | solution.py:105
  23.9 1.1 %collective-permute-start.11 = (bf16[192,1024]{1,0:T(8,128)(2,1)S(1)}, bf16[192,1024]{1,0:T(8,128)(2,1)S(1)}, u32[]{:S(2)}, u32[]{:S(2)}) collective-permute-start(bf16[192,1024]{1,0:T(8,128)(2,1)S(1)} %pad_maximum_fusion.14), channel_id=1, source_target_pairs={{0,16},{1,17},{2,18},{3,19},{4,20},{5,21},{6,22},{7,23},{8,24},{9,... | collective-permute-start | bytes 1179656 | tf_op jit(solution)/shard_map/ppermute | solution.py:105
  25.1 1.4 %collective-permute-start.3 = (s32[8,128]{1,0:T(8,128)S(1)}, s32[8,128]{1,0:T(8,128)S(1)}, u32[]{:S(2)}, u32[]{:S(2)}) collective-permute-start(s32[8,128]{1,0:T(8,128)S(1)} %pad_add_fusion), channel_id=1, source_target_pairs={{0,8},{1,9},{2,10},{3,11},{4,12},{5,13},{6,14},{7,15},{8,0},{9,1},... | collective-permute-start | bytes 12296 | tf_op jit(solution)/shard_map/ppermute | solution.py:105
  26.4 7.6 %collective-permute-done.17 = bf16[64,2048]{1,0:T(8,128)(2,1)S(1)} collective-permute-done((bf16[64,2048]{1,0:T(8,128)(2,1)S(1)}, bf16[64,2048]{1,0:T(8,128)(2,1)S(1)}, u32[]{:S(2)}, u32[]{:S(2)}) %collective-permute-start.17) | collective-permute-done | bytes 262176 | tf_op jit(solution)/shard_map/ppermute | solution.py:105
  34.9 2.2 %collective-permute-done.9 = bf16[192,1024]{1,0:T(8,128)(2,1)S(1)} collective-permute-done((bf16[192,1024]{1,0:T(8,128)(2,1)S(1)}, bf16[192,1024]{1,0:T(8,128)(2,1)S(1)}, u32[]{:S(2)}, u32[]{:S(2)}) %collective-permute-start.9) | collective-permute-done | bytes 393248 | tf_op jit(solution)/shard_map/ppermute | solution.py:105
  37.1 1.5 %collective-permute-start.10 = (bf16[192,512]{1,0:T(8,128)(2,1)S(1)}, bf16[192,512]{1,0:T(8,128)(2,1)S(1)}, u32[]{:S(2)}, u32[]{:S(2)}) collective-permute-start(bf16[192,512]{1,0:T(8,128)(2,1)S(1)} %slice.324), channel_id=1, source_target_pairs={{0,16},{1,17},{2,18},{3,19},{4,20},{5,21},{6,22},{7,23},{8,24},{9,... | collective-permute-start | bytes 589832 | tf_op jit(solution)/shard_map/ppermute | solution.py:105
  39.1 3.8 %collective-permute-done.10 = bf16[192,512]{1,0:T(8,128)(2,1)S(1)} collective-permute-done((bf16[192,512]{1,0:T(8,128)(2,1)S(1)}, bf16[192,512]{1,0:T(8,128)(2,1)S(1)}, u32[]{:S(2)}, u32[]{:S(2)}) %collective-permute-start.10) | collective-permute-done | bytes 196640 | tf_op jit(solution)/shard_map/ppermute | solution.py:105
  44.8 3.8 %collective-permute-done.12 = bf16[192,512]{1,0:T(8,128)(2,1)S(1)} collective-permute-done((bf16[192,512]{1,0:T(8,128)(2,1)S(1)}, bf16[192,512]{1,0:T(8,128)(2,1)S(1)}, u32[]{:S(2)}, u32[]{:S(2)}) %collective-permute-start.12) | collective-permute-done | bytes 196640 | tf_op jit(solution)/shard_map/ppermute | solution.py:105
  50.6 1.6 %collective-permute-start.13 = (bf16[64,2048]{1,0:T(8,128)(2,1)S(1)}, bf16[64,2048]{1,0:T(8,128)(2,1)S(1)}, u32[]{:S(2)}, u32[]{:S(2)}) collective-permute-start(bf16[64,2048]{1,0:T(8,128)(2,1)S(1)} %get-tuple-element.29), channel_id=1, source_target_pairs={{0,2},{1,3},{2,0},{3,1},{4,6},{5,7},{6,4},{7,5},{8,10},{9,11},{10,... | collective-permute-start | bytes 786440 | tf_op jit(solution)/shard_map/ppermute | solution.py:105
  52.6 4.4 %collective-permute-done.13 = bf16[64,2048]{1,0:T(8,128)(2,1)S(1)} collective-permute-done((bf16[64,2048]{1,0:T(8,128)(2,1)S(1)}, bf16[64,2048]{1,0:T(8,128)(2,1)S(1)}, u32[]{:S(2)}, u32[]{:S(2)}) %collective-permute-start.13) | collective-permute-done | bytes 262176 | tf_op jit(solution)/shard_map/ppermute | solution.py:105
  57.7 1.4 %fusion.4 = bf16[384,768]{1,0:T(8,128)(2,1)S(1)} fusion(bf16[384,2048]{1,0:T(8,128)(2,1)S(1)} %constant_dynamic-update-slice_fusion, bf16[384,2048]{1,0:T(8,128)(2,1)S(1)} %bitcast.155, bf16[384,2048]{1,0:T(8,128)(2,1)S(1)} %bitcast.153), kind=kOutput, calls=%fused_computation.10 | convolution fusion | flops 1214545920 | bytes 5308416 | tf_op jit(solution)/shard_map/dot_general | solution.py:195
  59.3 1.2 %fusion.6 = bf16[128,768]{1,0:T(8,128)(2,1)S(1)} fusion(bf16[384,2048]{1,0:T(8,128)(2,1)S(1)} %bitcast.156, bf16[384,2048]{1,0:T(8,128)(2,1)S(1)} %bitcast.154, bf16[64,2048]{1,0:T(8,128)(2,1)S(1)} %collective-permute-done.18, bf16[64,2048]{1,0:T(8,128)(2,1)S(1)} %collective-permute-done.17), kind=kOutput, calls=%fused_computation.12 | convolution fusion | flops 410091520 | bytes 3866624 | tf_op jit(solution)/shard_map/dot_general | solution.py:195
  60.6 2.1 %collective-permute-start.19 = (bf16[128,384]{1,0:T(8,128)(2,1)S(1)}, bf16[128,384]{1,0:T(8,128)(2,1)S(1)}, u32[]{:S(2)}, u32[]{:S(2)}) collective-permute-start(bf16[128,384]{1,0:T(8,128)(2,1)S(1)} %get-tuple-element.34), channel_id=1, source_target_pairs={{0,4},{1,5},{2,6},{3,7},{4,0},{5,1},{6,2},{7,3},{8,12},{9,13},{10,... | collective-permute-start | bytes 294920 | tf_op jit(solution)/shard_map/ppermute | solution.py:105
  62.6 4.3 %collective-permute-done.16 = bf16[384,384]{1,0:T(8,128)(2,1)S(1)} collective-permute-done((bf16[384,384]{1,0:T(8,128)(2,1)S(1)}, bf16[384,384]{1,0:T(8,128)(2,1)S(1)}, u32[]{:S(2)}, u32[]{:S(2)}) %collective-permute-start.16) | collective-permute-done | bytes 294944 | tf_op jit(solution)/shard_map/ppermute | solution.py:105
  69.5 2.3 %fusion.61 = (f32[1024]{0:T(1024)S(1)}, f32[1024,2048]{1,0:T(8,128)S(1)}) fusion(bf16[2048,256]{1,0:T(8,128)(2,1)S(1)} %fusion.8, bf16[128,384]{1,0:T(8,128)(2,1)S(1)} %collective-permute-done.19, bf16[128,384]{1,0:T(8,128)(2,1)S(1)} %get-tuple-element.33, bf16[384,384]{1,0:T(8,128)(2,1)S(1)} %collective-permute-done.16, ...), kind=kOutput, calls=%fused_computation.183 | convolution fusion | flops 550501376 | bytes 9728000 | tf_op jit(solution)/shard_map/dot_general | solution.py:230
  71.8 1.3 %fusion = f32[1024]{0:T(1024)S(1)} fusion(f32[1024,2048]{1,0:T(8,128)S(1)} %get-tuple-element.62, f32[1024]{0:T(1024)S(1)} %get-tuple-element.61), kind=kLoop, calls=%fused_computation.3 | loop fusion | flops 4193280 | bytes 8396800 | tf_op jit(solution)/shard_map/reduce_sum | solution.py:238
  73.1 1.6 %fusion.5 = bf16[1024,128]{1,0:T(8,128)(2,1)S(1)} fusion(f32[1024,2048]{1,0:T(8,128)S(1)} %get-tuple-element.62, f32[1024]{0:T(1024)S(1)} %fusion, f32[1024]{0:T(1024)S(1)} %get-tuple-element.61, bf16[2048,256]{1,0:T(8,128)(2,1)S(1)} %fusion.8), kind=kOutput, calls=%fused_computation.11 | convolution fusion | flops 543293440 | bytes 9183232 | tf_op jit(solution)/shard_map/dot_general | solution.py:239
  74.9 12.7 %all_to_all.5 = bf16[8,128,128]{2,1,0:T(8,128)(2,1)S(1)} all-to-all(bf16[8,128,128]{2,1,0:T(8,128)(2,1)S(1)} %fusion.45), channel_id=1, replica_groups=mesh['grp'=2,'chip'=8,'core'=2] {'chip'}, dimensions={0} | all-to-all | bytes 524288 | tf_op jit(solution)/shard_map/all_to_all | solution.py:248
  (116 shorter events, 14.2 us)
Async XLA Ops:
  0.0 20.2 %slice-start = ((bf16[128,2048]{1,0:T(8,128)(2,1)}), bf16[64,2048]{1,0:T(8,128)(2,1)S(1)}, s32[]{:S(2)}) async-start(bf16[128,2048]{1,0:T(8,128)(2,1)} %param.5), calls=%async_computation.1 | async-start | bytes 524288 | tf_op jit(solution)/shard_map/slice | solution.py:137
  0.0 13.5 %copy-start.1 = (bf16[4,2048]{1,0:T(4,128)(2,1)S(1)}, bf16[4,2048]{1,0:T(4,128)(2,1)}, u32[]{:S(2)}) copy-start(bf16[4,2048]{1,0:T(4,128)(2,1)} %param.6) | copy-start | bytes 49156
  0.9 19.3 %collective-permute-start.4 = (bf16[3,2048]{1,0:T(4,128)(2,1)S(1)}, bf16[3,2048]{1,0:T(4,128)(2,1)S(1)}, u32[]{:S(2)}, u32[]{:S(2)}) collective-permute-start(bf16[3,2048]{1,0:T(4,128)(2,1)S(1)} %slice.262), channel_id=1, source_target_pairs={{0,1},{1,2},{2,3},{3,4},{4,5},{5,6},{6,7},{7,8},{8,9},{9,10},{10,1... | collective-permute-start | bytes 36872 | tf_op jit(solution)/shard_map/ppermute | solution.py:133
  4.2 17.8 %collective-permute-start.7 = (bf16[64,2048]{1,0:T(8,128)(2,1)S(1)}, bf16[64,2048]{1,0:T(8,128)(2,1)S(1)}, u32[]{:S(2)}, u32[]{:S(2)}) collective-permute-start(bf16[64,2048]{1,0:T(8,128)(2,1)S(1)} %dynamic-slice_bitcast_fusion), channel_id=1, source_target_pairs={{0,0},{1,3},{2,6},{3,9},{4,12},{5,15},{6,2},{7,5},{8,8},{9,11},{10... | collective-permute-start | bytes 786440 | tf_op jit(solution)/shard_map/ppermute | solution.py:153
  5.9 16.1 %collective-permute-start.8 = (bf16[64,1024]{1,0:T(8,128)(2,1)S(1)}, bf16[64,1024]{1,0:T(8,128)(2,1)S(1)}, u32[]{:S(2)}, u32[]{:S(2)}) collective-permute-start(bf16[64,1024]{1,0:T(8,128)(2,1)S(1)} %constant_dynamic-slice_fusion.2), channel_id=1, source_target_pairs={{0,1},{1,4},{2,7},{3,10},{4,13},{5,0},{6,3},{7,6},{8,9},{9,12},{10... | collective-permute-start | bytes 393224 | tf_op jit(solution)/shard_map/ppermute | solution.py:153
  11.8 2.3 %collective-permute-start = (s32[1,128]{1,0:T(1,128)S(1)}, s32[1,128]{1,0:T(1,128)S(1)}, u32[]{:S(2)}, u32[]{:S(2)}) collective-permute-start(s32[1,128]{1,0:T(1,128)S(1)} %bitcast.168), channel_id=1, source_target_pairs={{0,1},{1,0},{2,3},{3,2},{4,5},{5,4},{6,7},{7,6},{8,9},{9,8},{10,11... | collective-permute-start | bytes 1544 | tf_op jit(solution)/shard_map/ppermute | solution.py:105
  14.1 3.6 %collective-permute-start.1 = (s32[2,128]{1,0:T(2,128)S(1)}, s32[2,128]{1,0:T(2,128)S(1)}, u32[]{:S(2)}, u32[]{:S(2)}) collective-permute-start(s32[2,128]{1,0:T(2,128)S(1)} %pad_add_fusion.2), channel_id=1, source_target_pairs={{0,2},{1,3},{2,0},{3,1},{4,6},{5,7},{6,4},{7,5},{8,10},{9,11},{10,... | collective-permute-start | bytes 3080 | tf_op jit(solution)/shard_map/ppermute | solution.py:105
  17.7 7.3 %collective-permute-start.2 = (s32[4,128]{1,0:T(4,128)S(1)}, s32[4,128]{1,0:T(4,128)S(1)}, u32[]{:S(2)}, u32[]{:S(2)}) collective-permute-start(s32[4,128]{1,0:T(4,128)S(1)} %pad_add_fusion.1), channel_id=1, source_target_pairs={{0,4},{1,5},{2,6},{3,7},{4,0},{5,1},{6,2},{7,3},{8,12},{9,13},{10,... | collective-permute-start | bytes 6152 | tf_op jit(solution)/shard_map/ppermute | solution.py:105
  20.5 13.5 %collective-permute-start.17 = (bf16[64,2048]{1,0:T(8,128)(2,1)S(1)}, bf16[64,2048]{1,0:T(8,128)(2,1)S(1)}, u32[]{:S(2)}, u32[]{:S(2)}) collective-permute-start(bf16[64,2048]{1,0:T(8,128)(2,1)S(1)} %get-tuple-element.8), channel_id=1, source_target_pairs={{0,8},{1,9},{2,10},{3,11},{4,12},{5,13},{6,14},{7,15},{8,0},{9,1},... | collective-permute-start | bytes 786440 | tf_op jit(solution)/shard_map/ppermute | solution.py:105
  21.1 12.9 %collective-permute-start.5 = (bf16[128,2048]{1,0:T(8,128)(2,1)S(1)}, bf16[128,2048]{1,0:T(8,128)(2,1)S(1)}, u32[]{:S(2)}, u32[]{:S(2)}) collective-permute-start(bf16[128,2048]{1,0:T(8,128)(2,1)S(1)} %pad_maximum_fusion.12), channel_id=1, source_target_pairs={{0,2},{1,3},{2,0},{3,1},{4,6},{5,7},{6,4},{7,5},{8,10},{9,11},{10,... | collective-permute-start | bytes 1572872 | tf_op jit(solution)/shard_map/ppermute | solution.py:105
  22.0 15.1 %collective-permute-start.9 = (bf16[192,1024]{1,0:T(8,128)(2,1)S(1)}, bf16[192,1024]{1,0:T(8,128)(2,1)S(1)}, u32[]{:S(2)}, u32[]{:S(2)}) collective-permute-start(bf16[192,1024]{1,0:T(8,128)(2,1)S(1)} %pad_maximum_fusion.14), channel_id=1, source_target_pairs={{0,4},{1,5},{2,6},{3,7},{4,0},{5,1},{6,2},{7,3},{8,12},{9,13},{10,... | collective-permute-start | bytes 1179656 | tf_op jit(solution)/shard_map/ppermute | solution.py:105
  23.9 14.8 %collective-permute-start.11 = (bf16[192,1024]{1,0:T(8,128)(2,1)S(1)}, bf16[192,1024]{1,0:T(8,128)(2,1)S(1)}, u32[]{:S(2)}, u32[]{:S(2)}) collective-permute-start(bf16[192,1024]{1,0:T(8,128)(2,1)S(1)} %pad_maximum_fusion.14), channel_id=1, source_target_pairs={{0,16},{1,17},{2,18},{3,19},{4,20},{5,21},{6,22},{7,23},{8,24},{9,... | collective-permute-start | bytes 1179656 | tf_op jit(solution)/shard_map/ppermute | solution.py:105
  25.1 43.0 %collective-permute-start.3 = (s32[8,128]{1,0:T(8,128)S(1)}, s32[8,128]{1,0:T(8,128)S(1)}, u32[]{:S(2)}, u32[]{:S(2)}) collective-permute-start(s32[8,128]{1,0:T(8,128)S(1)} %pad_add_fusion), channel_id=1, source_target_pairs={{0,8},{1,9},{2,10},{3,11},{4,12},{5,13},{6,14},{7,15},{8,0},{9,1},... | collective-permute-start | bytes 12296 | tf_op jit(solution)/shard_map/ppermute | solution.py:105
  34.0 16.5 %collective-permute-start.6 = (bf16[64,2048]{1,0:T(8,128)(2,1)S(1)}, bf16[64,2048]{1,0:T(8,128)(2,1)S(1)}, u32[]{:S(2)}, u32[]{:S(2)}) collective-permute-start(bf16[64,2048]{1,0:T(8,128)(2,1)S(1)} %get-tuple-element.6), channel_id=1, source_target_pairs={{0,8},{1,9},{2,10},{3,11},{4,12},{5,13},{6,14},{7,15},{8,0},{9,1},... | collective-permute-start | bytes 786440 | tf_op jit(solution)/shard_map/ppermute | solution.py:105
  34.0 25.3 %collective-permute-start.18 = (bf16[64,2048]{1,0:T(8,128)(2,1)S(1)}, bf16[64,2048]{1,0:T(8,128)(2,1)S(1)}, u32[]{:S(2)}, u32[]{:S(2)}) collective-permute-start(bf16[64,2048]{1,0:T(8,128)(2,1)S(1)} %collective-permute-done.17), channel_id=1, source_target_pairs={{0,2},{1,3},{2,0},{3,1},{4,6},{5,7},{6,4},{7,5},{8,10},{9,11},{10,... | collective-permute-start | bytes 786440 | tf_op jit(solution)/shard_map/ppermute | solution.py:105
  37.1 5.7 %collective-permute-start.10 = (bf16[192,512]{1,0:T(8,128)(2,1)S(1)}, bf16[192,512]{1,0:T(8,128)(2,1)S(1)}, u32[]{:S(2)}, u32[]{:S(2)}) collective-permute-start(bf16[192,512]{1,0:T(8,128)(2,1)S(1)} %slice.324), channel_id=1, source_target_pairs={{0,16},{1,17},{2,18},{3,19},{4,20},{5,21},{6,22},{7,23},{8,24},{9,... | collective-permute-start | bytes 589832 | tf_op jit(solution)/shard_map/ppermute | solution.py:105
  38.7 9.9 %collective-permute-start.12 = (bf16[192,512]{1,0:T(8,128)(2,1)S(1)}, bf16[192,512]{1,0:T(8,128)(2,1)S(1)}, u32[]{:S(2)}, u32[]{:S(2)}) collective-permute-start(bf16[192,512]{1,0:T(8,128)(2,1)S(1)} %slice.326), channel_id=1, source_target_pairs={{0,4},{1,5},{2,6},{3,7},{4,0},{5,1},{6,2},{7,3},{8,12},{9,13},{10,... | collective-permute-start | bytes 589832 | tf_op jit(solution)/shard_map/ppermute | solution.py:105
  42.9 14.2 %collective-permute-start.14 = (bf16[3,64,2048]{2,1,0:T(8,128)(2,1)S(1)}, bf16[3,64,2048]{2,1,0:T(8,128)(2,1)S(1)}, u32[]{:S(2)}, u32[]{:S(2)}) collective-permute-start(bf16[3,64,2048]{2,1,0:T(8,128)(2,1)S(1)} %constant_dynamic-slice_fusion.1), channel_id=1, source_target_pairs={{0,1},{1,0},{2,3},{3,2},{4,5},{5,4},{6,7},{7,6},{8,9},{9,8},{10,11... | collective-permute-start | bytes 2359304 | tf_op jit(solution)/shard_map/ppermute | solution.py:105
  50.6 6.4 %collective-permute-start.13 = (bf16[64,2048]{1,0:T(8,128)(2,1)S(1)}, bf16[64,2048]{1,0:T(8,128)(2,1)S(1)}, u32[]{:S(2)}, u32[]{:S(2)}) collective-permute-start(bf16[64,2048]{1,0:T(8,128)(2,1)S(1)} %get-tuple-element.29), channel_id=1, source_target_pairs={{0,2},{1,3},{2,0},{3,1},{4,6},{5,7},{6,4},{7,5},{8,10},{9,11},{10,... | collective-permute-start | bytes 786440 | tf_op jit(solution)/shard_map/ppermute | solution.py:105
  52.5 4.8 %collective-permute-start.15 = (bf16[3,64,2048]{2,1,0:T(8,128)(2,1)S(1)}, bf16[3,64,2048]{2,1,0:T(8,128)(2,1)S(1)}, u32[]{:S(2)}, u32[]{:S(2)}) collective-permute-start(bf16[3,64,2048]{2,1,0:T(8,128)(2,1)S(1)} %constant_dynamic-slice_fusion), channel_id=1, source_target_pairs={{0,1},{1,0},{2,3},{3,2},{4,5},{5,4},{6,7},{7,6},{8,9},{9,8},{10,11... | collective-permute-start | bytes 2359304 | tf_op jit(solution)/shard_map/ppermute | solution.py:105
  59.2 7.7 %collective-permute-start.16 = (bf16[384,384]{1,0:T(8,128)(2,1)S(1)}, bf16[384,384]{1,0:T(8,128)(2,1)S(1)}, u32[]{:S(2)}, u32[]{:S(2)}) collective-permute-start(bf16[384,384]{1,0:T(8,128)(2,1)S(1)} %get-tuple-element.24), channel_id=1, source_target_pairs={{0,4},{1,5},{2,6},{3,7},{4,0},{5,1},{6,2},{7,3},{8,12},{9,13},{10,... | collective-permute-start | bytes 884744 | tf_op jit(solution)/shard_map/ppermute | solution.py:105
  60.6 7.4 %collective-permute-start.19 = (bf16[128,384]{1,0:T(8,128)(2,1)S(1)}, bf16[128,384]{1,0:T(8,128)(2,1)S(1)}, u32[]{:S(2)}, u32[]{:S(2)}) collective-permute-start(bf16[128,384]{1,0:T(8,128)(2,1)S(1)} %get-tuple-element.34), channel_id=1, source_target_pairs={{0,4},{1,5},{2,6},{3,7},{4,0},{5,1},{6,2},{7,3},{8,12},{9,13},{10,... | collective-permute-start | bytes 294920 | tf_op jit(solution)/shard_map/ppermute | solution.py:105
  67.0 2.5 %collective-permute-start.20 = (bf16[768,256]{1,0:T(8,128)(2,1)S(1)}, bf16[768,256]{1,0:T(8,128)(2,1)S(1)}, u32[]{:S(2)}, u32[]{:S(2)}) collective-permute-start(bf16[768,256]{1,0:T(8,128)(2,1)S(1)} %pad_maximum_fusion.13), channel_id=1, source_target_pairs={{0,1},{1,0},{2,3},{3,2},{4,5},{5,4},{6,7},{7,6},{8,9},{9,8},{10,11... | collective-permute-start | bytes 1179656 | tf_op jit(solution)/shard_map/ppermute | solution.py:105
  68.0 1.4 %collective-permute-start.21 = (bf16[256,256]{1,0:T(8,128)(2,1)S(1)}, bf16[256,256]{1,0:T(8,128)(2,1)S(1)}, u32[]{:S(2)}, u32[]{:S(2)}) collective-permute-start(bf16[256,256]{1,0:T(8,128)(2,1)S(1)} %pad_maximum_fusion.15), channel_id=1, source_target_pairs={{0,1},{1,0},{2,3},{3,2},{4,5},{5,4},{6,7},{7,6},{8,9},{9,8},{10,11... | collective-permute-start | bytes 393224 | tf_op jit(solution)/shard_map/ppermute | solution.py:105
  (1 other events, 13.3 us)

commit v20 on v17

--- a/solution.py
+++ b/solution.py
@@ -162,13 +162,15 @@
     cut = half // 2
     fourth = [xor_swap(paired[:, :cut], devices, every), xor_swap(mine_too[:, cut:], Z0)]
 
-    far_beside_late = xor_swap(far_late + zero_after(fourth[0]) + zero_after(fourth[1]), Y)
-
-    groups = track_groups(track_ids, track_owner)[None, :] + zero_after(paired).astype(jnp.int32)
+    far_beside_late = xor_swap(far_late + zero_after(fourth[0]), Y)
+
+    groups = track_groups(track_ids, track_owner)[None, :] + zero_after(mine).astype(jnp.int32)
     for bit in (CORE, Y, Z0, Z1):
         groups = jnp.concatenate([groups, xor_swap(groups, bit)], axis=0)
     zero = jnp.where(groups[-1, -1] < 0, 1.0, 0.0).astype(jnp.bfloat16)
     far_beside_early = xor_swap(far_early + zero, Y)
+
+    fourth = jnp.concatenate(fourth, axis=1)
 
     def whole_head(pieces, theirs, index):
         size = HD // 2
@@ -190,7 +192,6 @@
         wide = lax.dynamic_slice_in_dim(jnp.stack(turned), lax.rem(index, 3), 3, 0)
         return by_bit(core, wide, xor_swap(wide, CORE), 1).reshape(3 * HD, features)
 
-    fourth = jnp.concatenate(fourth, axis=1)
     two_heads = jnp.concatenate(
         [whole_head(mine, mine_too, me), whole_head(paired, fourth, me ^ Z0)], axis=0
     )

time: 103 us -> 97.4 us (0.946)
  other arithmetic: 6.9 us -> 4.64 us
  waiting for transfers between devices: 35.7 us -> 37.6 us
  local copies, waits for them, and re-layouts: 8.21 us -> 6.83 us
  starting transfers between devices: 26.1 us -> 24.8 us
    ppermute x2, starting transfers between devices: 4.48 us -> 1.19 us  [to_heads(): return lax.ppermute(block, every, pairs)]
    ppermute x19, starting transfers between devices: 16.5 us -> 19 us  [xor_swap(): return lax.ppermute(value, axes, [(d, d ^ bit) for d in range(count)])]
    ppermute x19, waiting for transfers between devices: 35.7 us -> 37.6 us  [xor_swap(): return lax.ppermute(value, axes, [(d, d ^ bit) for d in range(count)])]
    add x13, other arithmetic: 1.74 us -> 0.07 us  [of_rows(): (me ^ far ^ bit) * tok_rows + start + jnp.arange(count, dtype=jnp.int32)]
    unnamed x10, other arithmetic: 0.7 us -> 2.11 us
    add x1, other arithmetic: 1.09 us -> 0.05 us  [body_by_head(): far_beside_late = xor_swap(far_late + zero_after(fourth[0]), Y)]
  transfers between devices with their start and end apart: 22 -> 22, of which waited for: 11 -> 11; matrix products, arithmetic and copies ran while one was open for 15% -> 11% of each run, Pallas kernels for 0% -> 0%
where the time goes in v20:
time: 97.4 us; the launch traced here: 97.1 us
  waiting for transfers between devices  37.6 us (39%)
  starting transfers between devices  24.8 us (25%)
  blocking collectives  12.5 us (13%)
  local copies, waits for them, and re-layouts  6.83 us (7%)
  matrix products  6.54 us (7%)
  other arithmetic  4.64 us (5%)
  between operations  4.15 us (4%)
    ppermute x19, waiting for transfers between devices, xor_swap(): return lax.ppermute(value, axes, [(d, d ^ bit) for d in range(count)])  37.6 us
    ppermute x19, starting transfers between devices, xor_swap(): return lax.ppermute(value, axes, [(d, d ^ bit) for d in range(count)])  19 us
    all_to_all x1, blocking collectives, body_by_head(): lax.all_to_all(sent, 'chip', split_axis=0, concat_axis=0, tiled=True)  12.5 us
    ppermute x1, starting transfers between devices, body_by_head(): lax.ppermute(frames[tok_rows - (KW - 1):], both, [(i, i + 1) for i in ran...  4.59 us
    dot_general x2, matrix products, project(): lax.dot_general(rows, two_heads, (((1,), (1,)), ((), ())), preferred_elem...  2.62 us
    dot_general x1, matrix products, body_by_head(): lax.dot_general(query, keyed[:, :HD], (((1,), (1,)), ((), ())), preferred...  2.32 us
    unnamed x10, other arithmetic  2.11 us
  transfers between devices with their start and end apart: 22, of which 11 were waited for; matrix products, arithmetic and copies ran while one was open for 11% of the time, Pallas kernels for 0%

profile of v20, /device:TPU:0, one launch (start us, length us, event | category | flops | bytes accessed | tf_op | source)
XLA Modules:
  0.0 97.1 jit_solution(1416887390588314084)
XLA Ops:
  2.4 4.6 %collective-permute-start.5 = (bf16[3,2048]{1,0:T(4,128)(2,1)S(1)}, bf16[3,2048]{1,0:T(4,128)(2,1)S(1)}, u32[]{:S(2)}, u32[]{:S(2)}) collective-permute-start(bf16[3,2048]{1,0:T(4,128)(2,1)S(1)} %slice.267), channel_id=1, source_target_pairs={{0,1},{1,2},{2,3},{3,4},{4,5},{5,6},{6,7},{7,8},{8,9},{9,10},{10,1... | collective-permute-start | bytes 36872 | tf_op jit(solution)/shard_map/ppermute | solution.py:133
  12.3 4.5 %collective-permute-start.1 = (s32[1,128]{1,0:T(1,128)S(1)}, s32[1,128]{1,0:T(1,128)S(1)}, u32[]{:S(2)}, u32[]{:S(2)}) collective-permute-start(s32[1,128]{1,0:T(1,128)S(1)} %fusion.63), channel_id=1, source_target_pairs={{0,1},{1,0},{2,3},{3,2},{4,5},{5,4},{6,7},{7,6},{8,9},{9,8},{10,11... | collective-permute-start | bytes 1544 | tf_op jit(solution)/shard_map/ppermute | solution.py:105
  18.4 1.3 %collective-permute-start.2 = (s32[2,128]{1,0:T(2,128)S(1)}, s32[2,128]{1,0:T(2,128)S(1)}, u32[]{:S(2)}, u32[]{:S(2)}) collective-permute-start(s32[2,128]{1,0:T(2,128)S(1)} %pad_add_fusion.2), channel_id=1, source_target_pairs={{0,2},{1,3},{2,0},{3,1},{4,6},{5,7},{6,4},{7,5},{8,10},{9,11},{10,... | collective-permute-start | bytes 3080 | tf_op jit(solution)/shard_map/ppermute | solution.py:105
  20.6 1.4 %collective-permute-done.2 = s32[2,128]{1,0:T(2,128)S(1)} collective-permute-done((s32[2,128]{1,0:T(2,128)S(1)}, s32[2,128]{1,0:T(2,128)S(1)}, u32[]{:S(2)}, u32[]{:S(2)}) %collective-permute-start.2) | collective-permute-done | bytes 1056 | tf_op jit(solution)/shard_map/ppermute | solution.py:105
  22.1 1.4 %collective-permute-start.3 = (s32[4,128]{1,0:T(4,128)S(1)}, s32[4,128]{1,0:T(4,128)S(1)}, u32[]{:S(2)}, u32[]{:S(2)}) collective-permute-start(s32[4,128]{1,0:T(4,128)S(1)} %pad_add_fusion.1), channel_id=1, source_target_pairs={{0,4},{1,5},{2,6},{3,7},{4,0},{5,1},{6,2},{7,3},{8,12},{9,13},{10,... | collective-permute-start | bytes 6152 | tf_op jit(solution)/shard_map/ppermute | solution.py:105
  23.5 2.2 %collective-permute-done.3 = s32[4,128]{1,0:T(4,128)S(1)} collective-permute-done((s32[4,128]{1,0:T(4,128)S(1)}, s32[4,128]{1,0:T(4,128)S(1)}, u32[]{:S(2)}, u32[]{:S(2)}) %collective-permute-start.3) | collective-permute-done | bytes 2080 | tf_op jit(solution)/shard_map/ppermute | solution.py:105
  25.7 2.4 %collective-permute-start.4 = (s32[8,128]{1,0:T(8,128)S(1)}, s32[8,128]{1,0:T(8,128)S(1)}, u32[]{:S(2)}, u32[]{:S(2)}) collective-permute-start(s32[8,128]{1,0:T(8,128)S(1)} %pad_add_fusion), channel_id=1, source_target_pairs={{0,8},{1,9},{2,10},{3,11},{4,12},{5,13},{6,14},{7,15},{8,0},{9,1},... | collective-permute-start | bytes 12296 | tf_op jit(solution)/shard_map/ppermute | solution.py:105
  28.3 2.2 %collective-permute-start.12 = (bf16[192,1024]{1,0:T(8,128)(2,1)S(1)}, bf16[192,1024]{1,0:T(8,128)(2,1)S(1)}, u32[]{:S(2)}, u32[]{:S(2)}) collective-permute-start(bf16[192,1024]{1,0:T(8,128)(2,1)S(1)} %pad_maximum_fusion.14), channel_id=1, source_target_pairs={{0,16},{1,17},{2,18},{3,19},{4,20},{5,21},{6,22},{7,23},{8,24},{9,... | collective-permute-start | bytes 1179656 | tf_op jit(solution)/shard_map/ppermute | solution.py:105
  30.5 2.1 %collective-permute-done.4 = s32[8,128]{1,0:T(8,128)S(1)} collective-permute-done((s32[8,128]{1,0:T(8,128)S(1)}, s32[8,128]{1,0:T(8,128)S(1)}, u32[]{:S(2)}, u32[]{:S(2)}) %collective-permute-start.4) | collective-permute-done | bytes 4128 | tf_op jit(solution)/shard_map/ppermute | solution.py:105
  34.1 9.1 %collective-permute-done.9 = bf16[192,1024]{1,0:T(8,128)(2,1)S(1)} collective-permute-done((bf16[192,1024]{1,0:T(8,128)(2,1)S(1)}, bf16[192,1024]{1,0:T(8,128)(2,1)S(1)}, u32[]{:S(2)}, u32[]{:S(2)}) %collective-permute-start.9) | collective-permute-done | bytes 393248 | tf_op jit(solution)/shard_map/ppermute | solution.py:105
  43.2 2.3 %collective-permute-start.10 = (bf16[192,512]{1,0:T(8,128)(2,1)S(1)}, bf16[192,512]{1,0:T(8,128)(2,1)S(1)}, u32[]{:S(2)}, u32[]{:S(2)}) collective-permute-start(bf16[192,512]{1,0:T(8,128)(2,1)S(1)} %slice.329), channel_id=1, source_target_pairs={{0,16},{1,17},{2,18},{3,19},{4,20},{5,21},{6,22},{7,23},{8,24},{9,... | collective-permute-start | bytes 589832 | tf_op jit(solution)/shard_map/ppermute | solution.py:105
  45.9 4.6 %collective-permute-done.10 = bf16[192,512]{1,0:T(8,128)(2,1)S(1)} collective-permute-done((bf16[192,512]{1,0:T(8,128)(2,1)S(1)}, bf16[192,512]{1,0:T(8,128)(2,1)S(1)}, u32[]{:S(2)}, u32[]{:S(2)}) %collective-permute-start.10) | collective-permute-done | bytes 196640 | tf_op jit(solution)/shard_map/ppermute | solution.py:105
  50.5 1.7 %collective-permute-done.14 = bf16[192,512]{1,0:T(8,128)(2,1)S(1)} collective-permute-done((bf16[192,512]{1,0:T(8,128)(2,1)S(1)}, bf16[192,512]{1,0:T(8,128)(2,1)S(1)}, u32[]{:S(2)}, u32[]{:S(2)}) %collective-permute-start.14) | collective-permute-done | bytes 196640 | tf_op jit(solution)/shard_map/ppermute | solution.py:105
  54.7 1.1 %collective-permute-start.11 = (bf16[64,2048]{1,0:T(8,128)(2,1)S(1)}, bf16[64,2048]{1,0:T(8,128)(2,1)S(1)}, u32[]{:S(2)}, u32[]{:S(2)}) collective-permute-start(bf16[64,2048]{1,0:T(8,128)(2,1)S(1)} %get-tuple-element.29), channel_id=1, source_target_pairs={{0,2},{1,3},{2,0},{3,1},{4,6},{5,7},{6,4},{7,5},{8,10},{9,11},{10,... | collective-permute-start | bytes 786440 | tf_op jit(solution)/shard_map/ppermute | solution.py:105
  56.9 7.0 %collective-permute-done.11 = bf16[64,2048]{1,0:T(8,128)(2,1)S(1)} collective-permute-done((bf16[64,2048]{1,0:T(8,128)(2,1)S(1)}, bf16[64,2048]{1,0:T(8,128)(2,1)S(1)}, u32[]{:S(2)}, u32[]{:S(2)}) %collective-permute-start.11) | collective-permute-done | bytes 262176 | tf_op jit(solution)/shard_map/ppermute | solution.py:105
  64.7 1.4 %fusion.4 = bf16[384,768]{1,0:T(8,128)(2,1)S(1)} fusion(bf16[384,2048]{1,0:T(8,128)(2,1)S(1)} %constant_dynamic-update-slice_fusion, bf16[384,2048]{1,0:T(8,128)(2,1)S(1)} %bitcast.156, bf16[384,2048]{1,0:T(8,128)(2,1)S(1)} %bitcast.154), kind=kOutput, calls=%fused_computation.10 | convolution fusion | flops 1214545920 | bytes 5308416 | tf_op jit(solution)/shard_map/dot_general | solution.py:200
  66.5 2.6 %collective-permute-done.18 = bf16[64,2048]{1,0:T(8,128)(2,1)S(1)} collective-permute-done((bf16[64,2048]{1,0:T(8,128)(2,1)S(1)}, bf16[64,2048]{1,0:T(8,128)(2,1)S(1)}, u32[]{:S(2)}, u32[]{:S(2)}) %collective-permute-start.18) | collective-permute-done | bytes 262176 | tf_op jit(solution)/shard_map/ppermute | solution.py:105
  69.1 1.2 %fusion.6 = bf16[128,768]{1,0:T(8,128)(2,1)S(1)} fusion(bf16[384,2048]{1,0:T(8,128)(2,1)S(1)} %bitcast.157, bf16[384,2048]{1,0:T(8,128)(2,1)S(1)} %bitcast.155, bf16[64,2048]{1,0:T(8,128)(2,1)S(1)} %collective-permute-done.18, bf16[64,2048]{1,0:T(8,128)(2,1)S(1)} %collective-permute-done.17), kind=kOutput, calls=%fused_computation.12 | convolution fusion | flops 410091520 | bytes 3866624 | tf_op jit(solution)/shard_map/dot_general | solution.py:200
  70.7 4.9 %collective-permute-done.16 = bf16[384,384]{1,0:T(8,128)(2,1)S(1)} collective-permute-done((bf16[384,384]{1,0:T(8,128)(2,1)S(1)}, bf16[384,384]{1,0:T(8,128)(2,1)S(1)}, u32[]{:S(2)}, u32[]{:S(2)}) %collective-permute-start.16) | collective-permute-done | bytes 294944 | tf_op jit(solution)/shard_map/ppermute | solution.py:105
  76.9 1.1 %collective-permute-done.21 = bf16[256,256]{1,0:T(8,128)(2,1)S(1)} collective-permute-done((bf16[256,256]{1,0:T(8,128)(2,1)S(1)}, bf16[256,256]{1,0:T(8,128)(2,1)S(1)}, u32[]{:S(2)}, u32[]{:S(2)}) %collective-permute-start.21) | collective-permute-done | bytes 131104 | tf_op jit(solution)/shard_map/ppermute | solution.py:105
  78.1 2.3 %fusion.61 = (f32[1024]{0:T(1024)S(1)}, f32[1024,2048]{1,0:T(8,128)S(1)}) fusion(bf16[2048,256]{1,0:T(8,128)(2,1)S(1)} %fusion.8, bf16[128,384]{1,0:T(8,128)(2,1)S(1)} %collective-permute-done.19, bf16[128,384]{1,0:T(8,128)(2,1)S(1)} %get-tuple-element.33, bf16[384,384]{1,0:T(8,128)(2,1)S(1)} %collective-permute-done.16, ...), kind=kOutput, calls=%fused_computation.185 | convolution fusion | flops 550501376 | bytes 9728000 | tf_op jit(solution)/shard_map/dot_general | solution.py:231
  80.4 1.3 %fusion = f32[1024]{0:T(1024)S(1)} fusion(f32[1024,2048]{1,0:T(8,128)S(1)} %get-tuple-element.62, f32[1024]{0:T(1024)S(1)} %get-tuple-element.61), kind=kLoop, calls=%fused_computation.3 | loop fusion | flops 4193280 | bytes 8396800 | tf_op jit(solution)/shard_map/reduce_sum | solution.py:239
  81.7 1.6 %fusion.5 = bf16[1024,128]{1,0:T(8,128)(2,1)S(1)} fusion(f32[1024,2048]{1,0:T(8,128)S(1)} %get-tuple-element.62, f32[1024]{0:T(1024)S(1)} %fusion, f32[1024]{0:T(1024)S(1)} %get-tuple-element.61, bf16[2048,256]{1,0:T(8,128)(2,1)S(1)} %fusion.8), kind=kOutput, calls=%fused_computation.11 | convolution fusion | flops 543293440 | bytes 9183232 | tf_op jit(solution)/shard_map/dot_general | solution.py:240
  83.5 12.5 %all_to_all.5 = bf16[8,128,128]{2,1,0:T(8,128)(2,1)S(1)} all-to-all(bf16[8,128,128]{2,1,0:T(8,128)(2,1)S(1)} %fusion.45), channel_id=1, replica_groups=mesh['grp'=2,'chip'=8,'core'=2] {'chip'}, dimensions={0} | all-to-all | bytes 524288 | tf_op jit(solution)/shard_map/all_to_all | solution.py:249
  (126 shorter events, 16.1 us)
Async XLA Ops:
  0.0 9.4 %slice-start = ((bf16[128,2048]{1,0:T(8,128)(2,1)}), bf16[64,2048]{1,0:T(8,128)(2,1)S(1)}, s32[]{:S(2)}) async-start(bf16[128,2048]{1,0:T(8,128)(2,1)} %param.5), calls=%async_computation.1 | async-start | bytes 524288 | tf_op jit(solution)/shard_map/slice | solution.py:137
  1.1 9.3 %collective-permute-start = (bf16[64,1024]{1,0:T(8,128)(2,1)S(1)}, bf16[64,1024]{1,0:T(8,128)(2,1)S(1)}, u32[]{:S(2)}, u32[]{:S(2)}) collective-permute-start(bf16[64,1024]{1,0:T(8,128)(2,1)S(1)} %constant_dynamic-slice_fusion.2), channel_id=1, source_target_pairs={{0,1},{1,4},{2,7},{3,10},{4,13},{5,0},{6,3},{7,6},{8,9},{9,12},{10... | collective-permute-start | bytes 393224 | tf_op jit(solution)/shard_map/ppermute | solution.py:153
  2.4 7.0 %collective-permute-start.5 = (bf16[3,2048]{1,0:T(4,128)(2,1)S(1)}, bf16[3,2048]{1,0:T(4,128)(2,1)S(1)}, u32[]{:S(2)}, u32[]{:S(2)}) collective-permute-start(bf16[3,2048]{1,0:T(4,128)(2,1)S(1)} %slice.267), channel_id=1, source_target_pairs={{0,1},{1,2},{2,3},{3,4},{4,5},{5,6},{6,7},{7,8},{8,9},{9,10},{10,1... | collective-permute-start | bytes 36872 | tf_op jit(solution)/shard_map/ppermute | solution.py:133
  8.0 20.2 %collective-permute-start.8 = (bf16[64,2048]{1,0:T(8,128)(2,1)S(1)}, bf16[64,2048]{1,0:T(8,128)(2,1)S(1)}, u32[]{:S(2)}, u32[]{:S(2)}) collective-permute-start(bf16[64,2048]{1,0:T(8,128)(2,1)S(1)} %dynamic-slice_bitcast_fusion), channel_id=1, source_target_pairs={{0,0},{1,3},{2,6},{3,9},{4,12},{5,15},{6,2},{7,5},{8,8},{9,11},{10... | collective-permute-start | bytes 786440 | tf_op jit(solution)/shard_map/ppermute | solution.py:153
  12.3 6.1 %collective-permute-start.1 = (s32[1,128]{1,0:T(1,128)S(1)}, s32[1,128]{1,0:T(1,128)S(1)}, u32[]{:S(2)}, u32[]{:S(2)}) collective-permute-start(s32[1,128]{1,0:T(1,128)S(1)} %fusion.63), channel_id=1, source_target_pairs={{0,1},{1,0},{2,3},{3,2},{4,5},{5,4},{6,7},{7,6},{8,9},{9,8},{10,11... | collective-permute-start | bytes 1544 | tf_op jit(solution)/shard_map/ppermute | solution.py:105
  17.8 16.2 %copy-start.2 = (bf16[384,2048]{1,0:T(8,128)(2,1)S(1)}, bf16[384,2048]{1,0:T(8,128)(2,1)}, u32[]{:S(2)}) copy-start(bf16[384,2048]{1,0:T(8,128)(2,1)} %get-tuple-element.5) | copy-start | bytes 4718596
  17.8 36.8 %collective-permute-start.7 = (bf16[64,2048]{1,0:T(8,128)(2,1)S(1)}, bf16[64,2048]{1,0:T(8,128)(2,1)S(1)}, u32[]{:S(2)}, u32[]{:S(2)}) collective-permute-start(bf16[64,2048]{1,0:T(8,128)(2,1)S(1)} %get-tuple-element.6), channel_id=1, source_target_pairs={{0,8},{1,9},{2,10},{3,11},{4,12},{5,13},{6,14},{7,15},{8,0},{9,1},... | collective-permute-start | bytes 786440 | tf_op jit(solution)/shard_map/ppermute | solution.py:105
  18.4 3.6 %collective-permute-start.2 = (s32[2,128]{1,0:T(2,128)S(1)}, s32[2,128]{1,0:T(2,128)S(1)}, u32[]{:S(2)}, u32[]{:S(2)}) collective-permute-start(s32[2,128]{1,0:T(2,128)S(1)} %pad_add_fusion.2), channel_id=1, source_target_pairs={{0,2},{1,3},{2,0},{3,1},{4,6},{5,7},{6,4},{7,5},{8,10},{9,11},{10,... | collective-permute-start | bytes 3080 | tf_op jit(solution)/shard_map/ppermute | solution.py:105
  19.8 14.2 %collective-permute-start.6 = (bf16[128,2048]{1,0:T(8,128)(2,1)S(1)}, bf16[128,2048]{1,0:T(8,128)(2,1)S(1)}, u32[]{:S(2)}, u32[]{:S(2)}) collective-permute-start(bf16[128,2048]{1,0:T(8,128)(2,1)S(1)} %pad_maximum_fusion.12), channel_id=1, source_target_pairs={{0,2},{1,3},{2,0},{3,1},{4,6},{5,7},{6,4},{7,5},{8,10},{9,11},{10,... | collective-permute-start | bytes 1572872 | tf_op jit(solution)/shard_map/ppermute | solution.py:105
  22.1 3.6 %collective-permute-start.3 = (s32[4,128]{1,0:T(4,128)S(1)}, s32[4,128]{1,0:T(4,128)S(1)}, u32[]{:S(2)}, u32[]{:S(2)}) collective-permute-start(s32[4,128]{1,0:T(4,128)S(1)} %pad_add_fusion.1), channel_id=1, source_target_pairs={{0,4},{1,5},{2,6},{3,7},{4,0},{5,1},{6,2},{7,3},{8,12},{9,13},{10,... | collective-permute-start | bytes 6152 | tf_op jit(solution)/shard_map/ppermute | solution.py:105
  25.7 6.8 %collective-permute-start.4 = (s32[8,128]{1,0:T(8,128)S(1)}, s32[8,128]{1,0:T(8,128)S(1)}, u32[]{:S(2)}, u32[]{:S(2)}) collective-permute-start(s32[8,128]{1,0:T(8,128)S(1)} %pad_add_fusion), channel_id=1, source_target_pairs={{0,8},{1,9},{2,10},{3,11},{4,12},{5,13},{6,14},{7,15},{8,0},{9,1},... | collective-permute-start | bytes 12296 | tf_op jit(solution)/shard_map/ppermute | solution.py:105
  28.2 15.0 %collective-permute-start.9 = (bf16[192,1024]{1,0:T(8,128)(2,1)S(1)}, bf16[192,1024]{1,0:T(8,128)(2,1)S(1)}, u32[]{:S(2)}, u32[]{:S(2)}) collective-permute-start(bf16[192,1024]{1,0:T(8,128)(2,1)S(1)} %pad_maximum_fusion.14), channel_id=1, source_target_pairs={{0,4},{1,5},{2,6},{3,7},{4,0},{5,1},{6,2},{7,3},{8,12},{9,13},{10,... | collective-permute-start | bytes 1179656 | tf_op jit(solution)/shard_map/ppermute | solution.py:105
  28.3 17.2 %collective-permute-start.12 = (bf16[192,1024]{1,0:T(8,128)(2,1)S(1)}, bf16[192,1024]{1,0:T(8,128)(2,1)S(1)}, u32[]{:S(2)}, u32[]{:S(2)}) collective-permute-start(bf16[192,1024]{1,0:T(8,128)(2,1)S(1)} %pad_maximum_fusion.14), channel_id=1, source_target_pairs={{0,16},{1,17},{2,18},{3,19},{4,20},{5,21},{6,22},{7,23},{8,24},{9,... | collective-permute-start | bytes 1179656 | tf_op jit(solution)/shard_map/ppermute | solution.py:105
  32.6 23.2 %collective-permute-start.17 = (bf16[64,2048]{1,0:T(8,128)(2,1)S(1)}, bf16[64,2048]{1,0:T(8,128)(2,1)S(1)}, u32[]{:S(2)}, u32[]{:S(2)}) collective-permute-start(bf16[64,2048]{1,0:T(8,128)(2,1)S(1)} %get-tuple-element.8), channel_id=1, source_target_pairs={{0,8},{1,9},{2,10},{3,11},{4,12},{5,13},{6,14},{7,15},{8,0},{9,1},... | collective-permute-start | bytes 786440 | tf_op jit(solution)/shard_map/ppermute | solution.py:105
  43.2 7.3 %collective-permute-start.10 = (bf16[192,512]{1,0:T(8,128)(2,1)S(1)}, bf16[192,512]{1,0:T(8,128)(2,1)S(1)}, u32[]{:S(2)}, u32[]{:S(2)}) collective-permute-start(bf16[192,512]{1,0:T(8,128)(2,1)S(1)} %slice.329), channel_id=1, source_target_pairs={{0,16},{1,17},{2,18},{3,19},{4,20},{5,21},{6,22},{7,23},{8,24},{9,... | collective-permute-start | bytes 589832 | tf_op jit(solution)/shard_map/ppermute | solution.py:105
  45.7 6.6 %collective-permute-start.14 = (bf16[192,512]{1,0:T(8,128)(2,1)S(1)}, bf16[192,512]{1,0:T(8,128)(2,1)S(1)}, u32[]{:S(2)}, u32[]{:S(2)}) collective-permute-start(bf16[192,512]{1,0:T(8,128)(2,1)S(1)} %slice.335), channel_id=1, source_target_pairs={{0,4},{1,5},{2,6},{3,7},{4,0},{5,1},{6,2},{7,3},{8,12},{9,13},{10,... | collective-permute-start | bytes 589832 | tf_op jit(solution)/shard_map/ppermute | solution.py:105
  45.8 18.1 %collective-permute-start.13 = (bf16[3,64,2048]{2,1,0:T(8,128)(2,1)S(1)}, bf16[3,64,2048]{2,1,0:T(8,128)(2,1)S(1)}, u32[]{:S(2)}, u32[]{:S(2)}) collective-permute-start(bf16[3,64,2048]{2,1,0:T(8,128)(2,1)S(1)} %constant_dynamic-slice_fusion.1), channel_id=1, source_target_pairs={{0,1},{1,0},{2,3},{3,2},{4,5},{5,4},{6,7},{7,6},{8,9},{9,8},{10,11... | collective-permute-start | bytes 2359304 | tf_op jit(solution)/shard_map/ppermute | solution.py:105
  54.6 9.3 %collective-permute-start.15 = (bf16[3,64,2048]{2,1,0:T(8,128)(2,1)S(1)}, bf16[3,64,2048]{2,1,0:T(8,128)(2,1)S(1)}, u32[]{:S(2)}, u32[]{:S(2)}) collective-permute-start(bf16[3,64,2048]{2,1,0:T(8,128)(2,1)S(1)} %constant_dynamic-slice_fusion), channel_id=1, source_target_pairs={{0,1},{1,0},{2,3},{3,2},{4,5},{5,4},{6,7},{7,6},{8,9},{9,8},{10,11... | collective-permute-start | bytes 2359304 | tf_op jit(solution)/shard_map/ppermute | solution.py:105
  54.7 9.2 %collective-permute-start.11 = (bf16[64,2048]{1,0:T(8,128)(2,1)S(1)}, bf16[64,2048]{1,0:T(8,128)(2,1)S(1)}, u32[]{:S(2)}, u32[]{:S(2)}) collective-permute-start(bf16[64,2048]{1,0:T(8,128)(2,1)S(1)} %get-tuple-element.29), channel_id=1, source_target_pairs={{0,2},{1,3},{2,0},{3,1},{4,6},{5,7},{6,4},{7,5},{8,10},{9,11},{10,... | collective-permute-start | bytes 786440 | tf_op jit(solution)/shard_map/ppermute | solution.py:105
  55.8 13.3 %collective-permute-start.18 = (bf16[64,2048]{1,0:T(8,128)(2,1)S(1)}, bf16[64,2048]{1,0:T(8,128)(2,1)S(1)}, u32[]{:S(2)}, u32[]{:S(2)}) collective-permute-start(bf16[64,2048]{1,0:T(8,128)(2,1)S(1)} %broadcast_add_fusion), channel_id=1, source_target_pairs={{0,2},{1,3},{2,0},{3,1},{4,6},{5,7},{6,4},{7,5},{8,10},{9,11},{10,... | collective-permute-start | bytes 786440 | tf_op jit(solution)/shard_map/ppermute | solution.py:105
  66.2 9.3 %collective-permute-start.16 = (bf16[384,384]{1,0:T(8,128)(2,1)S(1)}, bf16[384,384]{1,0:T(8,128)(2,1)S(1)}, u32[]{:S(2)}, u32[]{:S(2)}) collective-permute-start(bf16[384,384]{1,0:T(8,128)(2,1)S(1)} %get-tuple-element.24), channel_id=1, source_target_pairs={{0,4},{1,5},{2,6},{3,7},{4,0},{5,1},{6,2},{7,3},{8,12},{9,13},{10,... | collective-permute-start | bytes 884744 | tf_op jit(solution)/shard_map/ppermute | solution.py:105
  70.3 6.3 %collective-permute-start.19 = (bf16[128,384]{1,0:T(8,128)(2,1)S(1)}, bf16[128,384]{1,0:T(8,128)(2,1)S(1)}, u32[]{:S(2)}, u32[]{:S(2)}) collective-permute-start(bf16[128,384]{1,0:T(8,128)(2,1)S(1)} %get-tuple-element.34), channel_id=1, source_target_pairs={{0,4},{1,5},{2,6},{3,7},{4,0},{5,1},{6,2},{7,3},{8,12},{9,13},{10,... | collective-permute-start | bytes 294920 | tf_op jit(solution)/shard_map/ppermute | solution.py:105
  75.6 2.5 %collective-permute-start.20 = (bf16[768,256]{1,0:T(8,128)(2,1)S(1)}, bf16[768,256]{1,0:T(8,128)(2,1)S(1)}, u32[]{:S(2)}, u32[]{:S(2)}) collective-permute-start(bf16[768,256]{1,0:T(8,128)(2,1)S(1)} %pad_maximum_fusion.13), channel_id=1, source_target_pairs={{0,1},{1,0},{2,3},{3,2},{4,5},{5,4},{6,7},{7,6},{8,9},{9,8},{10,11... | collective-permute-start | bytes 1179656 | tf_op jit(solution)/shard_map/ppermute | solution.py:105
  76.6 1.4 %collective-permute-start.21 = (bf16[256,256]{1,0:T(8,128)(2,1)S(1)}, bf16[256,256]{1,0:T(8,128)(2,1)S(1)}, u32[]{:S(2)}, u32[]{:S(2)}) collective-permute-start(bf16[256,256]{1,0:T(8,128)(2,1)S(1)} %pad_maximum_fusion.15), channel_id=1, source_target_pairs={{0,1},{1,0},{2,3},{3,2},{4,5},{5,4},{6,7},{7,6},{8,9},{9,8},{10,11... | collective-permute-start | bytes 393224 | tf_op jit(solution)/shard_map/ppermute | solution.py:105
  (4 other events, 35.3 us)

commit v21 on v19

--- a/solution.py
+++ b/solution.py
@@ -162,8 +162,9 @@
     cut = half // 2
     fourth = [xor_swap(paired[:, :cut], devices, every), xor_swap(mine_too[:, cut:], Z0)]
 
-    far_beside_late = xor_swap(far_late + zero_after(fourth[0]) + zero_after(fourth[1]), Y)
-    far_beside_early = xor_swap(far_early, Y)
+    zero = zero_after(fourth[0]) + zero_after(fourth[1])
+    far_beside_late = xor_swap(far_late + zero, Y)
+    far_beside_early = xor_swap(far_early + zero, Y)
 
     fourth = jnp.concatenate(fourth, axis=1)
 
@@ -195,13 +196,14 @@
         done = lax.dot_general(
             rows, two_heads, (((1,), (1,)), ((), ())), preferred_element_type=jnp.float32
         ).astype(jnp.bfloat16)
-        return jnp.concatenate([done[:, : 3 * HD], xor_swap(done[:, 3 * HD :], Z0)], axis=0)
-
-    first = project(jnp.concatenate([own, beside, far_late, far_beside_late], axis=0))
-    second = project(jnp.concatenate([far_early, far_beside_early], axis=0))
-
-    first_rows = [(0, 0, tok_rows), (Y, 0, tok_rows), (Z1, part, part), (Z1 | Y, part, part)]
-    second_rows = [(Z1, 0, part), (Z1 | Y, 0, part)]
+        swapped = xor_swap(done[:, 3 * HD :], Z0)
+        return jnp.concatenate([done[:, : 3 * HD], swapped], axis=0), zero_after(done)
+
+    first, _ = project(jnp.concatenate([own, beside, far_early, far_beside_early], axis=0))
+    second, _ = project(jnp.concatenate([far_late, far_beside_late], axis=0))
+
+    first_rows = [(0, 0, tok_rows), (Y, 0, tok_rows), (Z1, 0, part), (Z1 | Y, 0, part)]
+    second_rows = [(Z1, part, part), (Z1 | Y, part, part)]
     order = []
     for pieces in (first_rows, second_rows):
         order += pieces + [(far ^ Z0, start, count) for far, start, count in pieces]

time: 89 us -> 92.3 us (1.037)
  blocking collectives: 12.7 us -> 16.5 us
  waiting for transfers between devices: 30.4 us -> 28 us
  starting transfers between devices: 25.6 us -> 27.5 us
    all_to_all x1, blocking collectives: 12.7 us -> 16.5 us  [body_by_head(): lax.all_to_all(sent, 'chip', split_axis=0, concat_axis=0, tiled=True)]
    ppermute x1, starting transfers between devices: 2.36 us -> 5.11 us  [body_by_head(): lax.ppermute(frames[tok_rows - (KW - 1):], both, [(i, i + 1) for i in ran...]
    ppermute x19, waiting for transfers between devices: 30.4 us -> 27.9 us  [xor_swap(): return lax.ppermute(value, axes, [(d, d ^ bit) for d in range(count)])]
    ppermute x2, starting transfers between devices: 5.83 us -> 4.48 us  [to_heads(): return lax.ppermute(block, every, pairs)]
  transfers between devices with their start and end apart: 22 -> 22, of which waited for: 10 -> 11; matrix products, arithmetic and copies ran while one was open for 10% -> 10% of each run, Pallas kernels for 0% -> 0%
where the time goes in v21:
time: 92.3 us; the launch traced here: 92 us
  waiting for transfers between devices  28 us (30%)
  starting transfers between devices  27.5 us (30%)
  blocking collectives  16.5 us (18%)
  matrix products  6.53 us (7%)
  local copies, waits for them, and re-layouts  6.11 us (7%)
  other arithmetic  3.9 us (4%)
  between operations  3.41 us (4%)
    ppermute x19, waiting for transfers between devices, xor_swap(): return lax.ppermute(value, axes, [(d, d ^ bit) for d in range(count)])  27.9 us
    ppermute x19, starting transfers between devices, xor_swap(): return lax.ppermute(value, axes, [(d, d ^ bit) for d in range(count)])  17.9 us
    all_to_all x1, blocking collectives, body_by_head(): lax.all_to_all(sent, 'chip', split_axis=0, concat_axis=0, tiled=True)  16.5 us
    ppermute x1, starting transfers between devices, body_by_head(): lax.ppermute(frames[tok_rows - (KW - 1):], both, [(i, i + 1) for i in ran...  5.11 us
    ppermute x2, starting transfers between devices, to_heads(): return lax.ppermute(block, every, pairs)  4.48 us
    dot_general x2, matrix products, project(): lax.dot_general(rows, two_heads, (((1,), (1,)), ((), ())), preferred_elem...  2.61 us
    dot_general x1, matrix products, body_by_head(): lax.dot_general(query, keyed[:, :HD], (((1,), (1,)), ((), ())), preferred...  2.33 us
  transfers between devices with their start and end apart: 22, of which 11 were waited for; matrix products, arithmetic and copies ran while one was open for 10% of the time, Pallas kernels for 0%

profile of v21, /device:TPU:0, one launch (start us, length us, event | category | flops | bytes accessed | tf_op | source)
XLA Modules:
  0.0 92.0 jit_solution(15685358914037891009)
XLA Ops:
  0.0 1.1 %dynamic-slice_bitcast_fusion = bf16[64,2048]{1,0:T(8,128)(2,1)S(1)} fusion(bf16[3,64,2048]{2,1,0:T(8,128)(2,1)} %bitcast.157, s32[]{:T(128)S(6)} %select_n.133), kind=kLoop, calls=%fused_computation.65 | loop fusion | bytes 524292 | tf_op jit(solution)/shard_map/jit(dynamic_index_in_dim)/squeeze | solution.py:155
  2.8 3.8 %collective-permute-start.8 = (bf16[64,1024]{1,0:T(8,128)(2,1)S(1)}, bf16[64,1024]{1,0:T(8,128)(2,1)S(1)}, u32[]{:S(2)}, u32[]{:S(2)}) collective-permute-start(bf16[64,1024]{1,0:T(8,128)(2,1)S(1)} %constant_dynamic-slice_fusion.2), channel_id=1, source_target_pairs={{0,1},{1,4},{2,7},{3,10},{4,13},{5,0},{6,3},{7,6},{8,9},{9,12},{10... | collective-permute-start | bytes 393224 | tf_op jit(solution)/shard_map/ppermute | solution.py:153
  7.3 5.1 %collective-permute-start.4 = (bf16[3,2048]{1,0:T(4,128)(2,1)S(1)}, bf16[3,2048]{1,0:T(4,128)(2,1)S(1)}, u32[]{:S(2)}, u32[]{:S(2)}) collective-permute-start(bf16[3,2048]{1,0:T(4,128)(2,1)S(1)} %slice.262), channel_id=1, source_target_pairs={{0,1},{1,2},{2,3},{3,4},{4,5},{5,6},{6,7},{7,8},{8,9},{9,10},{10,1... | collective-permute-start | bytes 36872 | tf_op jit(solution)/shard_map/ppermute | solution.py:133
  14.4 1.6 %collective-permute-start.1 = (s32[2,128]{1,0:T(2,128)S(1)}, s32[2,128]{1,0:T(2,128)S(1)}, u32[]{:S(2)}, u32[]{:S(2)}) collective-permute-start(s32[2,128]{1,0:T(2,128)S(1)} %pad_add_fusion.2), channel_id=1, source_target_pairs={{0,2},{1,3},{2,0},{3,1},{4,6},{5,7},{6,4},{7,5},{8,10},{9,11},{10,... | collective-permute-start | bytes 3080 | tf_op jit(solution)/shard_map/ppermute | solution.py:105
  16.2 1.8 %collective-permute-done.1 = s32[2,128]{1,0:T(2,128)S(1)} collective-permute-done((s32[2,128]{1,0:T(2,128)S(1)}, s32[2,128]{1,0:T(2,128)S(1)}, u32[]{:S(2)}, u32[]{:S(2)}) %collective-permute-start.1) | collective-permute-done | bytes 1056 | tf_op jit(solution)/shard_map/ppermute | solution.py:105
  20.5 2.1 %collective-permute-start.9 = (bf16[192,1024]{1,0:T(8,128)(2,1)S(1)}, bf16[192,1024]{1,0:T(8,128)(2,1)S(1)}, u32[]{:S(2)}, u32[]{:S(2)}) collective-permute-start(bf16[192,1024]{1,0:T(8,128)(2,1)S(1)} %pad_maximum_fusion.14), channel_id=1, source_target_pairs={{0,4},{1,5},{2,6},{3,7},{4,0},{5,1},{6,2},{7,3},{8,12},{9,13},{10,... | collective-permute-start | bytes 1179656 | tf_op jit(solution)/shard_map/ppermute | solution.py:105
  22.6 2.0 %collective-permute-start.11 = (bf16[192,1024]{1,0:T(8,128)(2,1)S(1)}, bf16[192,1024]{1,0:T(8,128)(2,1)S(1)}, u32[]{:S(2)}, u32[]{:S(2)}) collective-permute-start(bf16[192,1024]{1,0:T(8,128)(2,1)S(1)} %pad_maximum_fusion.14), channel_id=1, source_target_pairs={{0,16},{1,17},{2,18},{3,19},{4,20},{5,21},{6,22},{7,23},{8,24},{9,... | collective-permute-start | bytes 1179656 | tf_op jit(solution)/shard_map/ppermute | solution.py:105
  25.3 2.2 %collective-permute-start.6 = (bf16[64,2048]{1,0:T(8,128)(2,1)S(1)}, bf16[64,2048]{1,0:T(8,128)(2,1)S(1)}, u32[]{:S(2)}, u32[]{:S(2)}) collective-permute-start(bf16[64,2048]{1,0:T(8,128)(2,1)S(1)} %get-tuple-element.8), channel_id=1, source_target_pairs={{0,8},{1,9},{2,10},{3,11},{4,12},{5,13},{6,14},{7,15},{8,0},{9,1},... | collective-permute-start | bytes 786440 | tf_op jit(solution)/shard_map/ppermute | solution.py:105
  27.6 4.7 %collective-permute-done.5 = bf16[128,2048]{1,0:T(8,128)(2,1)S(1)} collective-permute-done((bf16[128,2048]{1,0:T(8,128)(2,1)S(1)}, bf16[128,2048]{1,0:T(8,128)(2,1)S(1)}, u32[]{:S(2)}, u32[]{:S(2)}) %collective-permute-start.5) | collective-permute-done | bytes 524320 | tf_op jit(solution)/shard_map/ppermute | solution.py:105
  32.3 2.4 %collective-permute-start.17 = (bf16[64,2048]{1,0:T(8,128)(2,1)S(1)}, bf16[64,2048]{1,0:T(8,128)(2,1)S(1)}, u32[]{:S(2)}, u32[]{:S(2)}) collective-permute-start(bf16[64,2048]{1,0:T(8,128)(2,1)S(1)} %get-tuple-element.6), channel_id=1, source_target_pairs={{0,8},{1,9},{2,10},{3,11},{4,12},{5,13},{6,14},{7,15},{8,0},{9,1},... | collective-permute-start | bytes 786440 | tf_op jit(solution)/shard_map/ppermute | solution.py:105
  34.7 1.5 %collective-permute-done.9 = bf16[192,1024]{1,0:T(8,128)(2,1)S(1)} collective-permute-done((bf16[192,1024]{1,0:T(8,128)(2,1)S(1)}, bf16[192,1024]{1,0:T(8,128)(2,1)S(1)}, u32[]{:S(2)}, u32[]{:S(2)}) %collective-permute-start.9) | collective-permute-done | bytes 393248 | tf_op jit(solution)/shard_map/ppermute | solution.py:105
  37.1 4.8 %collective-permute-done.10 = bf16[192,512]{1,0:T(8,128)(2,1)S(1)} collective-permute-done((bf16[192,512]{1,0:T(8,128)(2,1)S(1)}, bf16[192,512]{1,0:T(8,128)(2,1)S(1)}, u32[]{:S(2)}, u32[]{:S(2)}) %collective-permute-start.10) | collective-permute-done | bytes 196640 | tf_op jit(solution)/shard_map/ppermute | solution.py:105
  43.8 1.5 %collective-permute-done.12 = bf16[192,512]{1,0:T(8,128)(2,1)S(1)} collective-permute-done((bf16[192,512]{1,0:T(8,128)(2,1)S(1)}, bf16[192,512]{1,0:T(8,128)(2,1)S(1)}, u32[]{:S(2)}, u32[]{:S(2)}) %collective-permute-start.12) | collective-permute-done | bytes 196640 | tf_op jit(solution)/shard_map/ppermute | solution.py:105
  48.1 1.4 %collective-permute-done.17 = bf16[64,2048]{1,0:T(8,128)(2,1)S(1)} collective-permute-done((bf16[64,2048]{1,0:T(8,128)(2,1)S(1)}, bf16[64,2048]{1,0:T(8,128)(2,1)S(1)}, u32[]{:S(2)}, u32[]{:S(2)}) %collective-permute-start.17) | collective-permute-done | bytes 262176 | tf_op jit(solution)/shard_map/ppermute | solution.py:105
  50.2 6.4 %collective-permute-done.13 = bf16[64,2048]{1,0:T(8,128)(2,1)S(1)} collective-permute-done((bf16[64,2048]{1,0:T(8,128)(2,1)S(1)}, bf16[64,2048]{1,0:T(8,128)(2,1)S(1)}, u32[]{:S(2)}, u32[]{:S(2)}) %collective-permute-start.13) | collective-permute-done | bytes 262176 | tf_op jit(solution)/shard_map/ppermute | solution.py:105
  57.3 1.4 %fusion.4 = bf16[384,768]{1,0:T(8,128)(2,1)S(1)} fusion(bf16[384,2048]{1,0:T(8,128)(2,1)S(1)} %constant_dynamic-update-slice_fusion, bf16[384,2048]{1,0:T(8,128)(2,1)S(1)} %bitcast.154, bf16[384,2048]{1,0:T(8,128)(2,1)S(1)} %bitcast.152), kind=kOutput, calls=%fused_computation.10 | convolution fusion | flops 1214545920 | bytes 5308416 | tf_op jit(solution)/shard_map/dot_general | solution.py:196
  58.8 2.2 %collective-permute-start.16 = (bf16[384,384]{1,0:T(8,128)(2,1)S(1)}, bf16[384,384]{1,0:T(8,128)(2,1)S(1)}, u32[]{:S(2)}, u32[]{:S(2)}) collective-permute-start(bf16[384,384]{1,0:T(8,128)(2,1)S(1)} %get-tuple-element.24), channel_id=1, source_target_pairs={{0,4},{1,5},{2,6},{3,7},{4,0},{5,1},{6,2},{7,3},{8,12},{9,13},{10,... | collective-permute-start | bytes 884744 | tf_op jit(solution)/shard_map/ppermute | solution.py:105
  61.0 1.2 %fusion.6 = bf16[128,768]{1,0:T(8,128)(2,1)S(1)} fusion(bf16[384,2048]{1,0:T(8,128)(2,1)S(1)} %bitcast.155, bf16[384,2048]{1,0:T(8,128)(2,1)S(1)} %bitcast.153, bf16[64,2048]{1,0:T(8,128)(2,1)S(1)} %collective-permute-done.18, bf16[64,2048]{1,0:T(8,128)(2,1)S(1)} %collective-permute-done.17), kind=kOutput, calls=%fused_computation.12 | convolution fusion | flops 410091520 | bytes 3866624 | tf_op jit(solution)/shard_map/dot_general | solution.py:196
  63.1 3.3 %collective-permute-done.16 = bf16[384,384]{1,0:T(8,128)(2,1)S(1)} collective-permute-done((bf16[384,384]{1,0:T(8,128)(2,1)S(1)}, bf16[384,384]{1,0:T(8,128)(2,1)S(1)}, u32[]{:S(2)}, u32[]{:S(2)}) %collective-permute-start.16) | collective-permute-done | bytes 294944 | tf_op jit(solution)/shard_map/ppermute | solution.py:105
  67.8 1.1 %collective-permute-done.21 = bf16[256,256]{1,0:T(8,128)(2,1)S(1)} collective-permute-done((bf16[256,256]{1,0:T(8,128)(2,1)S(1)}, bf16[256,256]{1,0:T(8,128)(2,1)S(1)}, u32[]{:S(2)}, u32[]{:S(2)}) %collective-permute-start.21) | collective-permute-done | bytes 131104 | tf_op jit(solution)/shard_map/ppermute | solution.py:105
  68.9 2.3 %fusion.61 = (f32[1024]{0:T(1024)S(1)}, f32[1024,2048]{1,0:T(8,128)S(1)}) fusion(bf16[2048,256]{1,0:T(8,128)(2,1)S(1)} %fusion.8, bf16[128,384]{1,0:T(8,128)(2,1)S(1)} %collective-permute-done.19, bf16[128,384]{1,0:T(8,128)(2,1)S(1)} %get-tuple-element.33, bf16[384,384]{1,0:T(8,128)(2,1)S(1)} %collective-permute-done.16, ...), kind=kOutput, calls=%fused_computation.184 | convolution fusion | flops 550501376 | bytes 9728000 | tf_op jit(solution)/shard_map/dot_general | solution.py:232
  71.2 1.3 %fusion = f32[1024]{0:T(1024)S(1)} fusion(f32[1024,2048]{1,0:T(8,128)S(1)} %get-tuple-element.62, f32[1024]{0:T(1024)S(1)} %get-tuple-element.61), kind=kLoop, calls=%fused_computation.3 | loop fusion | flops 4193280 | bytes 8396800 | tf_op jit(solution)/shard_map/reduce_sum | solution.py:240
  72.5 1.6 %fusion.5 = bf16[1024,128]{1,0:T(8,128)(2,1)S(1)} fusion(f32[1024,2048]{1,0:T(8,128)S(1)} %get-tuple-element.62, f32[1024]{0:T(1024)S(1)} %fusion, f32[1024]{0:T(1024)S(1)} %get-tuple-element.61, bf16[2048,256]{1,0:T(8,128)(2,1)S(1)} %fusion.8), kind=kOutput, calls=%fused_computation.11 | convolution fusion | flops 543293440 | bytes 9183232 | tf_op jit(solution)/shard_map/dot_general | solution.py:241
  74.4 16.5 %all_to_all.5 = bf16[8,128,128]{2,1,0:T(8,128)(2,1)S(1)} all-to-all(bf16[8,128,128]{2,1,0:T(8,128)(2,1)S(1)} %fusion.45), channel_id=1, replica_groups=mesh['grp'=2,'chip'=8,'core'=2] {'chip'}, dimensions={0} | all-to-all | bytes 524288 | tf_op jit(solution)/shard_map/all_to_all | solution.py:250
  (117 shorter events, 15.3 us)
Async XLA Ops:
  0.0 18.8 %slice-start = ((bf16[128,2048]{1,0:T(8,128)(2,1)}), bf16[64,2048]{1,0:T(8,128)(2,1)S(1)}, s32[]{:S(2)}) async-start(bf16[128,2048]{1,0:T(8,128)(2,1)} %param.5), calls=%async_computation.1 | async-start | bytes 524288 | tf_op jit(solution)/shard_map/slice | solution.py:137
  0.0 13.5 %copy-start.1 = (bf16[4,2048]{1,0:T(4,128)(2,1)S(1)}, bf16[4,2048]{1,0:T(4,128)(2,1)}, u32[]{:S(2)}) copy-start(bf16[4,2048]{1,0:T(4,128)(2,1)} %param.6) | copy-start | bytes 49156
  1.1 19.4 %collective-permute-start.7 = (bf16[64,2048]{1,0:T(8,128)(2,1)S(1)}, bf16[64,2048]{1,0:T(8,128)(2,1)S(1)}, u32[]{:S(2)}, u32[]{:S(2)}) collective-permute-start(bf16[64,2048]{1,0:T(8,128)(2,1)S(1)} %dynamic-slice_bitcast_fusion), channel_id=1, source_target_pairs={{0,0},{1,3},{2,6},{3,9},{4,12},{5,15},{6,2},{7,5},{8,8},{9,11},{10... | collective-permute-start | bytes 786440 | tf_op jit(solution)/shard_map/ppermute | solution.py:153
  2.8 17.7 %collective-permute-start.8 = (bf16[64,1024]{1,0:T(8,128)(2,1)S(1)}, bf16[64,1024]{1,0:T(8,128)(2,1)S(1)}, u32[]{:S(2)}, u32[]{:S(2)}) collective-permute-start(bf16[64,1024]{1,0:T(8,128)(2,1)S(1)} %constant_dynamic-slice_fusion.2), channel_id=1, source_target_pairs={{0,1},{1,4},{2,7},{3,10},{4,13},{5,0},{6,3},{7,6},{8,9},{9,12},{10... | collective-permute-start | bytes 393224 | tf_op jit(solution)/shard_map/ppermute | solution.py:153
  7.3 11.5 %collective-permute-start.4 = (bf16[3,2048]{1,0:T(4,128)(2,1)S(1)}, bf16[3,2048]{1,0:T(4,128)(2,1)S(1)}, u32[]{:S(2)}, u32[]{:S(2)}) collective-permute-start(bf16[3,2048]{1,0:T(4,128)(2,1)S(1)} %slice.262), channel_id=1, source_target_pairs={{0,1},{1,2},{2,3},{3,4},{4,5},{5,6},{6,7},{7,8},{8,9},{9,10},{10,1... | collective-permute-start | bytes 36872 | tf_op jit(solution)/shard_map/ppermute | solution.py:133
  13.2 1.2 %collective-permute-start = (s32[1,128]{1,0:T(1,128)S(1)}, s32[1,128]{1,0:T(1,128)S(1)}, u32[]{:S(2)}, u32[]{:S(2)}) collective-permute-start(s32[1,128]{1,0:T(1,128)S(1)} %bitcast.167), channel_id=1, source_target_pairs={{0,1},{1,0},{2,3},{3,2},{4,5},{5,4},{6,7},{7,6},{8,9},{9,8},{10,11... | collective-permute-start | bytes 1544 | tf_op jit(solution)/shard_map/ppermute | solution.py:105
  14.4 3.6 %collective-permute-start.1 = (s32[2,128]{1,0:T(2,128)S(1)}, s32[2,128]{1,0:T(2,128)S(1)}, u32[]{:S(2)}, u32[]{:S(2)}) collective-permute-start(s32[2,128]{1,0:T(2,128)S(1)} %pad_add_fusion.2), channel_id=1, source_target_pairs={{0,2},{1,3},{2,0},{3,1},{4,6},{5,7},{6,4},{7,5},{8,10},{9,11},{10,... | collective-permute-start | bytes 3080 | tf_op jit(solution)/shard_map/ppermute | solution.py:105
  18.0 6.6 %collective-permute-start.2 = (s32[4,128]{1,0:T(4,128)S(1)}, s32[4,128]{1,0:T(4,128)S(1)}, u32[]{:S(2)}, u32[]{:S(2)}) collective-permute-start(s32[4,128]{1,0:T(4,128)S(1)} %pad_add_fusion.1), channel_id=1, source_target_pairs={{0,4},{1,5},{2,6},{3,7},{4,0},{5,1},{6,2},{7,3},{8,12},{9,13},{10,... | collective-permute-start | bytes 6152 | tf_op jit(solution)/shard_map/ppermute | solution.py:105
  19.5 12.8 %collective-permute-start.5 = (bf16[128,2048]{1,0:T(8,128)(2,1)S(1)}, bf16[128,2048]{1,0:T(8,128)(2,1)S(1)}, u32[]{:S(2)}, u32[]{:S(2)}) collective-permute-start(bf16[128,2048]{1,0:T(8,128)(2,1)S(1)} %pad_maximum_fusion.12), channel_id=1, source_target_pairs={{0,2},{1,3},{2,0},{3,1},{4,6},{5,7},{6,4},{7,5},{8,10},{9,11},{10,... | collective-permute-start | bytes 1572872 | tf_op jit(solution)/shard_map/ppermute | solution.py:105
  20.5 15.6 %collective-permute-start.9 = (bf16[192,1024]{1,0:T(8,128)(2,1)S(1)}, bf16[192,1024]{1,0:T(8,128)(2,1)S(1)}, u32[]{:S(2)}, u32[]{:S(2)}) collective-permute-start(bf16[192,1024]{1,0:T(8,128)(2,1)S(1)} %pad_maximum_fusion.14), channel_id=1, source_target_pairs={{0,4},{1,5},{2,6},{3,7},{4,0},{5,1},{6,2},{7,3},{8,12},{9,13},{10,... | collective-permute-start | bytes 1179656 | tf_op jit(solution)/shard_map/ppermute | solution.py:105
  22.6 14.1 %collective-permute-start.11 = (bf16[192,1024]{1,0:T(8,128)(2,1)S(1)}, bf16[192,1024]{1,0:T(8,128)(2,1)S(1)}, u32[]{:S(2)}, u32[]{:S(2)}) collective-permute-start(bf16[192,1024]{1,0:T(8,128)(2,1)S(1)} %pad_maximum_fusion.14), channel_id=1, source_target_pairs={{0,16},{1,17},{2,18},{3,19},{4,20},{5,21},{6,22},{7,23},{8,24},{9,... | collective-permute-start | bytes 1179656 | tf_op jit(solution)/shard_map/ppermute | solution.py:105
  24.6 42.9 %collective-permute-start.3 = (s32[8,128]{1,0:T(8,128)S(1)}, s32[8,128]{1,0:T(8,128)S(1)}, u32[]{:S(2)}, u32[]{:S(2)}) collective-permute-start(s32[8,128]{1,0:T(8,128)S(1)} %pad_add_fusion), channel_id=1, source_target_pairs={{0,8},{1,9},{2,10},{3,11},{4,12},{5,13},{6,14},{7,15},{8,0},{9,1},... | collective-permute-start | bytes 12296 | tf_op jit(solution)/shard_map/ppermute | solution.py:105
  25.3 21.9 %collective-permute-start.6 = (bf16[64,2048]{1,0:T(8,128)(2,1)S(1)}, bf16[64,2048]{1,0:T(8,128)(2,1)S(1)}, u32[]{:S(2)}, u32[]{:S(2)}) collective-permute-start(bf16[64,2048]{1,0:T(8,128)(2,1)S(1)} %get-tuple-element.8), channel_id=1, source_target_pairs={{0,8},{1,9},{2,10},{3,11},{4,12},{5,13},{6,14},{7,15},{8,0},{9,1},... | collective-permute-start | bytes 786440 | tf_op jit(solution)/shard_map/ppermute | solution.py:105
  32.3 17.3 %collective-permute-start.17 = (bf16[64,2048]{1,0:T(8,128)(2,1)S(1)}, bf16[64,2048]{1,0:T(8,128)(2,1)S(1)}, u32[]{:S(2)}, u32[]{:S(2)}) collective-permute-start(bf16[64,2048]{1,0:T(8,128)(2,1)S(1)} %get-tuple-element.6), channel_id=1, source_target_pairs={{0,8},{1,9},{2,10},{3,11},{4,12},{5,13},{6,14},{7,15},{8,0},{9,1},... | collective-permute-start | bytes 786440 | tf_op jit(solution)/shard_map/ppermute | solution.py:105
  36.2 5.7 %collective-permute-start.10 = (bf16[192,512]{1,0:T(8,128)(2,1)S(1)}, bf16[192,512]{1,0:T(8,128)(2,1)S(1)}, u32[]{:S(2)}, u32[]{:S(2)}) collective-permute-start(bf16[192,512]{1,0:T(8,128)(2,1)S(1)} %slice.324), channel_id=1, source_target_pairs={{0,16},{1,17},{2,18},{3,19},{4,20},{5,21},{6,22},{7,23},{8,24},{9,... | collective-permute-start | bytes 589832 | tf_op jit(solution)/shard_map/ppermute | solution.py:105
  36.7 8.6 %collective-permute-start.12 = (bf16[192,512]{1,0:T(8,128)(2,1)S(1)}, bf16[192,512]{1,0:T(8,128)(2,1)S(1)}, u32[]{:S(2)}, u32[]{:S(2)}) collective-permute-start(bf16[192,512]{1,0:T(8,128)(2,1)S(1)} %slice.326), channel_id=1, source_target_pairs={{0,4},{1,5},{2,6},{3,7},{4,0},{5,1},{6,2},{7,3},{8,12},{9,13},{10,... | collective-permute-start | bytes 589832 | tf_op jit(solution)/shard_map/ppermute | solution.py:105
  41.9 14.7 %collective-permute-start.14 = (bf16[3,64,2048]{2,1,0:T(8,128)(2,1)S(1)}, bf16[3,64,2048]{2,1,0:T(8,128)(2,1)S(1)}, u32[]{:S(2)}, u32[]{:S(2)}) collective-permute-start(bf16[3,64,2048]{2,1,0:T(8,128)(2,1)S(1)} %constant_dynamic-slice_fusion.1), channel_id=1, source_target_pairs={{0,1},{1,0},{2,3},{3,2},{4,5},{5,4},{6,7},{7,6},{8,9},{9,8},{10,11... | collective-permute-start | bytes 2359304 | tf_op jit(solution)/shard_map/ppermute | solution.py:105
  47.3 9.3 %collective-permute-start.13 = (bf16[64,2048]{1,0:T(8,128)(2,1)S(1)}, bf16[64,2048]{1,0:T(8,128)(2,1)S(1)}, u32[]{:S(2)}, u32[]{:S(2)}) collective-permute-start(bf16[64,2048]{1,0:T(8,128)(2,1)S(1)} %get-tuple-element.29), channel_id=1, source_target_pairs={{0,2},{1,3},{2,0},{3,1},{4,6},{5,7},{6,4},{7,5},{8,10},{9,11},{10,... | collective-permute-start | bytes 786440 | tf_op jit(solution)/shard_map/ppermute | solution.py:105
  48.1 8.8 %collective-permute-start.15 = (bf16[3,64,2048]{2,1,0:T(8,128)(2,1)S(1)}, bf16[3,64,2048]{2,1,0:T(8,128)(2,1)S(1)}, u32[]{:S(2)}, u32[]{:S(2)}) collective-permute-start(bf16[3,64,2048]{2,1,0:T(8,128)(2,1)S(1)} %constant_dynamic-slice_fusion), channel_id=1, source_target_pairs={{0,1},{1,0},{2,3},{3,2},{4,5},{5,4},{6,7},{7,6},{8,9},{9,8},{10,11... | collective-permute-start | bytes 2359304 | tf_op jit(solution)/shard_map/ppermute | solution.py:105
  49.6 11.4 %collective-permute-start.18 = (bf16[64,2048]{1,0:T(8,128)(2,1)S(1)}, bf16[64,2048]{1,0:T(8,128)(2,1)S(1)}, u32[]{:S(2)}, u32[]{:S(2)}) collective-permute-start(bf16[64,2048]{1,0:T(8,128)(2,1)S(1)} %broadcast_add_fusion), channel_id=1, source_target_pairs={{0,2},{1,3},{2,0},{3,1},{4,6},{5,7},{6,4},{7,5},{8,10},{9,11},{10,... | collective-permute-start | bytes 786440 | tf_op jit(solution)/shard_map/ppermute | solution.py:105
  58.8 7.6 %collective-permute-start.16 = (bf16[384,384]{1,0:T(8,128)(2,1)S(1)}, bf16[384,384]{1,0:T(8,128)(2,1)S(1)}, u32[]{:S(2)}, u32[]{:S(2)}) collective-permute-start(bf16[384,384]{1,0:T(8,128)(2,1)S(1)} %get-tuple-element.24), channel_id=1, source_target_pairs={{0,4},{1,5},{2,6},{3,7},{4,0},{5,1},{6,2},{7,3},{8,12},{9,13},{10,... | collective-permute-start | bytes 884744 | tf_op jit(solution)/shard_map/ppermute | solution.py:105
  62.2 5.2 %collective-permute-start.19 = (bf16[128,384]{1,0:T(8,128)(2,1)S(1)}, bf16[128,384]{1,0:T(8,128)(2,1)S(1)}, u32[]{:S(2)}, u32[]{:S(2)}) collective-permute-start(bf16[128,384]{1,0:T(8,128)(2,1)S(1)} %get-tuple-element.34), channel_id=1, source_target_pairs={{0,4},{1,5},{2,6},{3,7},{4,0},{5,1},{6,2},{7,3},{8,12},{9,13},{10,... | collective-permute-start | bytes 294920 | tf_op jit(solution)/shard_map/ppermute | solution.py:105
  66.4 2.5 %collective-permute-start.20 = (bf16[768,256]{1,0:T(8,128)(2,1)S(1)}, bf16[768,256]{1,0:T(8,128)(2,1)S(1)}, u32[]{:S(2)}, u32[]{:S(2)}) collective-permute-start(bf16[768,256]{1,0:T(8,128)(2,1)S(1)} %pad_maximum_fusion.13), channel_id=1, source_target_pairs={{0,1},{1,0},{2,3},{3,2},{4,5},{5,4},{6,7},{7,6},{8,9},{9,8},{10,11... | collective-permute-start | bytes 1179656 | tf_op jit(solution)/shard_map/ppermute | solution.py:105
  67.4 1.4 %collective-permute-start.21 = (bf16[256,256]{1,0:T(8,128)(2,1)S(1)}, bf16[256,256]{1,0:T(8,128)(2,1)S(1)}, u32[]{:S(2)}, u32[]{:S(2)}) collective-permute-start(bf16[256,256]{1,0:T(8,128)(2,1)S(1)} %pad_maximum_fusion.15), channel_id=1, source_target_pairs={{0,1},{1,0},{2,3},{3,2},{4,5},{5,4},{6,7},{7,6},{8,9},{9,8},{10,11... | collective-permute-start | bytes 393224 | tf_op jit(solution)/shard_map/ppermute | solution.py:105
  (1 other events, 13.3 us)

commit v22 on v19

--- a/solution.py
+++ b/solution.py
@@ -126,7 +126,8 @@
     me = 2 * chip + core
     both = ("chip", "core")
     every = ("grp", "chip", "core")
-    part = tok_rows // 2
+    part = tok_rows // 4
+    rest = tok_rows - part
     features = frames.shape[1]
     CORE, Y, Z0, Z1 = 1, 2, 4, 8
 
@@ -200,7 +201,7 @@
     first = project(jnp.concatenate([own, beside, far_late, far_beside_late], axis=0))
     second = project(jnp.concatenate([far_early, far_beside_early], axis=0))
 
-    first_rows = [(0, 0, tok_rows), (Y, 0, tok_rows), (Z1, part, part), (Z1 | Y, part, part)]
+    first_rows = [(0, 0, tok_rows), (Y, 0, tok_rows), (Z1, part, rest), (Z1 | Y, part, rest)]
     second_rows = [(Z1, 0, part), (Z1 | Y, 0, part)]
     order = []
     for pieces in (first_rows, second_rows):

time: 89 us -> 100 us (1.12)
  waiting for transfers between devices: 30.4 us -> 35.9 us
  starting transfers between devices: 25.6 us -> 29.1 us
  blocking collectives: 12.7 us -> 14.8 us
    ppermute x19, waiting for transfers between devices: 30.4 us -> 35.9 us  [xor_swap(): return lax.ppermute(value, axes, [(d, d ^ bit) for d in range(count)])]
    ppermute x19, starting transfers between devices: 17.4 us -> 20.9 us  [xor_swap(): return lax.ppermute(value, axes, [(d, d ^ bit) for d in range(count)])]
    all_to_all x1, blocking collectives: 12.7 us -> 14.8 us  [body_by_head(): lax.all_to_all(sent, 'chip', split_axis=0, concat_axis=0, tiled=True)]
  transfers between devices with their start and end apart: 22 -> 22, of which waited for: 10 -> 12; matrix products, arithmetic and copies ran while one was open for 10% -> 9% of each run, Pallas kernels for 0% -> 0%
where the time goes in v22:
time: 100 us; the launch traced here: 99.9 us
  waiting for transfers between devices  35.9 us (36%)
  starting transfers between devices  29.1 us (29%)
  blocking collectives  14.8 us (15%)
  matrix products  6.66 us (7%)
  local copies, waits for them, and re-layouts  6.14 us (6%)
  other arithmetic  3.94 us (4%)
  between operations  3.4 us (3%)
    ppermute x19, waiting for transfers between devices, xor_swap(): return lax.ppermute(value, axes, [(d, d ^ bit) for d in range(count)])  35.9 us
    ppermute x19, starting transfers between devices, xor_swap(): return lax.ppermute(value, axes, [(d, d ^ bit) for d in range(count)])  20.9 us
    all_to_all x1, blocking collectives, body_by_head(): lax.all_to_all(sent, 'chip', split_axis=0, concat_axis=0, tiled=True)  14.8 us
    ppermute x2, starting transfers between devices, to_heads(): return lax.ppermute(block, every, pairs)  5.83 us
    dot_general x2, matrix products, project(): lax.dot_general(rows, two_heads, (((1,), (1,)), ((), ())), preferred_elem...  2.71 us
    dot_general x1, matrix products, body_by_head(): lax.dot_general(query, keyed[:, :HD], (((1,), (1,)), ((), ())), preferred...  2.36 us
    ppermute x1, starting transfers between devices, body_by_head(): lax.ppermute(frames[tok_rows - (KW - 1):], both, [(i, i + 1) for i in ran...  2.36 us
  transfers between devices with their start and end apart: 22, of which 12 were waited for; matrix products, arithmetic and copies ran while one was open for 9% of the time, Pallas kernels for 0%

profile of v22, /device:TPU:0, one launch (start us, length us, event | category | flops | bytes accessed | tf_op | source)
XLA Modules:
  0.0 99.9 jit_solution(3031767083649082395)
XLA Ops:
  0.9 2.4 %collective-permute-start.4 = (bf16[3,2048]{1,0:T(4,128)(2,1)S(1)}, bf16[3,2048]{1,0:T(4,128)(2,1)S(1)}, u32[]{:S(2)}, u32[]{:S(2)}) collective-permute-start(bf16[3,2048]{1,0:T(4,128)(2,1)S(1)} %slice.262), channel_id=1, source_target_pairs={{0,1},{1,2},{2,3},{3,4},{4,5},{5,6},{6,7},{7,8},{8,9},{9,10},{10,1... | collective-permute-start | bytes 36872 | tf_op jit(solution)/shard_map/ppermute | solution.py:134
  5.9 5.2 %collective-permute-start.8 = (bf16[64,1024]{1,0:T(8,128)(2,1)S(1)}, bf16[64,1024]{1,0:T(8,128)(2,1)S(1)}, u32[]{:S(2)}, u32[]{:S(2)}) collective-permute-start(bf16[64,1024]{1,0:T(8,128)(2,1)S(1)} %constant_dynamic-slice_fusion.2), channel_id=1, source_target_pairs={{0,1},{1,4},{2,7},{3,10},{4,13},{5,0},{6,3},{7,6},{8,9},{9,12},{10... | collective-permute-start | bytes 393224 | tf_op jit(solution)/shard_map/ppermute | solution.py:154
  11.8 1.5 %collective-permute-start = (s32[1,128]{1,0:T(1,128)S(1)}, s32[1,128]{1,0:T(1,128)S(1)}, u32[]{:S(2)}, u32[]{:S(2)}) collective-permute-start(s32[1,128]{1,0:T(1,128)S(1)} %bitcast.168), channel_id=1, source_target_pairs={{0,1},{1,0},{2,3},{3,2},{4,5},{5,4},{6,7},{7,6},{8,9},{9,8},{10,11... | collective-permute-start | bytes 1544 | tf_op jit(solution)/shard_map/ppermute | solution.py:105
  14.1 1.5 %collective-permute-start.1 = (s32[2,128]{1,0:T(2,128)S(1)}, s32[2,128]{1,0:T(2,128)S(1)}, u32[]{:S(2)}, u32[]{:S(2)}) collective-permute-start(s32[2,128]{1,0:T(2,128)S(1)} %pad_add_fusion.2), channel_id=1, source_target_pairs={{0,2},{1,3},{2,0},{3,1},{4,6},{5,7},{6,4},{7,5},{8,10},{9,11},{10,... | collective-permute-start | bytes 3080 | tf_op jit(solution)/shard_map/ppermute | solution.py:105
  15.8 1.9 %collective-permute-done.1 = s32[2,128]{1,0:T(2,128)S(1)} collective-permute-done((s32[2,128]{1,0:T(2,128)S(1)}, s32[2,128]{1,0:T(2,128)S(1)}, u32[]{:S(2)}, u32[]{:S(2)}) %collective-permute-start.1) | collective-permute-done | bytes 1056 | tf_op jit(solution)/shard_map/ppermute | solution.py:105
  17.7 2.5 %collective-permute-start.2 = (s32[4,128]{1,0:T(4,128)S(1)}, s32[4,128]{1,0:T(4,128)S(1)}, u32[]{:S(2)}, u32[]{:S(2)}) collective-permute-start(s32[4,128]{1,0:T(4,128)S(1)} %pad_add_fusion.1), channel_id=1, source_target_pairs={{0,4},{1,5},{2,6},{3,7},{4,0},{5,1},{6,2},{7,3},{8,12},{9,13},{10,... | collective-permute-start | bytes 6152 | tf_op jit(solution)/shard_map/ppermute | solution.py:105
  20.2 1.6 %collective-permute-done.2 = s32[4,128]{1,0:T(4,128)S(1)} collective-permute-done((s32[4,128]{1,0:T(4,128)S(1)}, s32[4,128]{1,0:T(4,128)S(1)}, u32[]{:S(2)}, u32[]{:S(2)}) %collective-permute-start.2) | collective-permute-done | bytes 2080 | tf_op jit(solution)/shard_map/ppermute | solution.py:105
  23.1 1.9 %collective-permute-start.17 = (bf16[32,2048]{1,0:T(8,128)(2,1)S(1)}, bf16[32,2048]{1,0:T(8,128)(2,1)S(1)}, u32[]{:S(2)}, u32[]{:S(2)}) collective-permute-start(bf16[32,2048]{1,0:T(8,128)(2,1)S(1)} %get-tuple-element.8), channel_id=1, source_target_pairs={{0,8},{1,9},{2,10},{3,11},{4,12},{5,13},{6,14},{7,15},{8,0},{9,1},... | collective-permute-start | bytes 393224 | tf_op jit(solution)/shard_map/ppermute | solution.py:105
  25.5 1.2 %collective-permute-start.5 = (bf16[128,2048]{1,0:T(8,128)(2,1)S(1)}, bf16[128,2048]{1,0:T(8,128)(2,1)S(1)}, u32[]{:S(2)}, u32[]{:S(2)}) collective-permute-start(bf16[128,2048]{1,0:T(8,128)(2,1)S(1)} %pad_maximum_fusion.12), channel_id=1, source_target_pairs={{0,2},{1,3},{2,0},{3,1},{4,6},{5,7},{6,4},{7,5},{8,10},{9,11},{10,... | collective-permute-start | bytes 1572872 | tf_op jit(solution)/shard_map/ppermute | solution.py:105
  26.7 1.6 %collective-permute-start.9 = (bf16[192,1024]{1,0:T(8,128)(2,1)S(1)}, bf16[192,1024]{1,0:T(8,128)(2,1)S(1)}, u32[]{:S(2)}, u32[]{:S(2)}) collective-permute-start(bf16[192,1024]{1,0:T(8,128)(2,1)S(1)} %pad_maximum_fusion.14), channel_id=1, source_target_pairs={{0,4},{1,5},{2,6},{3,7},{4,0},{5,1},{6,2},{7,3},{8,12},{9,13},{10,... | collective-permute-start | bytes 1179656 | tf_op jit(solution)/shard_map/ppermute | solution.py:105
  28.3 1.5 %collective-permute-start.11 = (bf16[192,1024]{1,0:T(8,128)(2,1)S(1)}, bf16[192,1024]{1,0:T(8,128)(2,1)S(1)}, u32[]{:S(2)}, u32[]{:S(2)}) collective-permute-start(bf16[192,1024]{1,0:T(8,128)(2,1)S(1)} %pad_maximum_fusion.14), channel_id=1, source_target_pairs={{0,16},{1,17},{2,18},{3,19},{4,20},{5,21},{6,22},{7,23},{8,24},{9,... | collective-permute-start | bytes 1179656 | tf_op jit(solution)/shard_map/ppermute | solution.py:105
  30.8 1.4 %collective-permute-start.6 = (bf16[96,2048]{1,0:T(8,128)(2,1)S(1)}, bf16[96,2048]{1,0:T(8,128)(2,1)S(1)}, u32[]{:S(2)}, u32[]{:S(2)}) collective-permute-start(bf16[96,2048]{1,0:T(8,128)(2,1)S(1)} %get-tuple-element.6), channel_id=1, source_target_pairs={{0,8},{1,9},{2,10},{3,11},{4,12},{5,13},{6,14},{7,15},{8,0},{9,1},... | collective-permute-start | bytes 1179656 | tf_op jit(solution)/shard_map/ppermute | solution.py:105
  32.2 5.4 %collective-permute-done.5 = bf16[128,2048]{1,0:T(8,128)(2,1)S(1)} collective-permute-done((bf16[128,2048]{1,0:T(8,128)(2,1)S(1)}, bf16[128,2048]{1,0:T(8,128)(2,1)S(1)}, u32[]{:S(2)}, u32[]{:S(2)}) %collective-permute-start.5) | collective-permute-done | bytes 524320 | tf_op jit(solution)/shard_map/ppermute | solution.py:105
  38.8 4.0 %collective-permute-done.9 = bf16[192,1024]{1,0:T(8,128)(2,1)S(1)} collective-permute-done((bf16[192,1024]{1,0:T(8,128)(2,1)S(1)}, bf16[192,1024]{1,0:T(8,128)(2,1)S(1)}, u32[]{:S(2)}, u32[]{:S(2)}) %collective-permute-start.9) | collective-permute-done | bytes 393248 | tf_op jit(solution)/shard_map/ppermute | solution.py:105
  43.6 5.0 %collective-permute-done.10 = bf16[192,512]{1,0:T(8,128)(2,1)S(1)} collective-permute-done((bf16[192,512]{1,0:T(8,128)(2,1)S(1)}, bf16[192,512]{1,0:T(8,128)(2,1)S(1)}, u32[]{:S(2)}, u32[]{:S(2)}) %collective-permute-start.10) | collective-permute-done | bytes 196640 | tf_op jit(solution)/shard_map/ppermute | solution.py:105
  52.8 2.6 %collective-permute-start.13 = (bf16[96,2048]{1,0:T(8,128)(2,1)S(1)}, bf16[96,2048]{1,0:T(8,128)(2,1)S(1)}, u32[]{:S(2)}, u32[]{:S(2)}) collective-permute-start(bf16[96,2048]{1,0:T(8,128)(2,1)S(1)} %get-tuple-element.27), channel_id=1, source_target_pairs={{0,2},{1,3},{2,0},{3,1},{4,6},{5,7},{6,4},{7,5},{8,10},{9,11},{10,... | collective-permute-start | bytes 1179656 | tf_op jit(solution)/shard_map/ppermute | solution.py:105
  55.9 8.5 %collective-permute-done.13 = bf16[96,2048]{1,0:T(8,128)(2,1)S(1)} collective-permute-done((bf16[96,2048]{1,0:T(8,128)(2,1)S(1)}, bf16[96,2048]{1,0:T(8,128)(2,1)S(1)}, u32[]{:S(2)}, u32[]{:S(2)}) %collective-permute-start.13) | collective-permute-done | bytes 393248 | tf_op jit(solution)/shard_map/ppermute | solution.py:105
  65.1 1.6 %fusion.4 = bf16[448,768]{1,0:T(8,128)(2,1)S(1)} fusion(bf16[448,2048]{1,0:T(8,128)(2,1)S(1)} %constant_dynamic-update-slice_fusion, bf16[384,2048]{1,0:T(8,128)(2,1)S(1)} %bitcast.155, bf16[384,2048]{1,0:T(8,128)(2,1)S(1)} %bitcast.153), kind=kOutput, calls=%fused_computation.10 | convolution fusion | flops 1415921664 | bytes 5668864 | tf_op jit(solution)/shard_map/dot_general | solution.py:196
  68.0 2.1 %collective-permute-start.19 = (bf16[64,384]{1,0:T(8,128)(2,1)S(1)}, bf16[64,384]{1,0:T(8,128)(2,1)S(1)}, u32[]{:S(2)}, u32[]{:S(2)}) collective-permute-start(bf16[64,384]{1,0:T(8,128)(2,1)S(1)} %get-tuple-element.34), channel_id=1, source_target_pairs={{0,4},{1,5},{2,6},{3,7},{4,0},{5,1},{6,2},{7,3},{8,12},{9,13},{10,... | collective-permute-start | bytes 147464 | tf_op jit(solution)/shard_map/ppermute | solution.py:105
  70.1 6.4 %collective-permute-done.16 = bf16[448,384]{1,0:T(8,128)(2,1)S(1)} collective-permute-done((bf16[448,384]{1,0:T(8,128)(2,1)S(1)}, bf16[448,384]{1,0:T(8,128)(2,1)S(1)}, u32[]{:S(2)}, u32[]{:S(2)}) %collective-permute-start.16) | collective-permute-done | bytes 344096 | tf_op jit(solution)/shard_map/ppermute | solution.py:105
  78.5 2.4 %fusion.61 = (f32[1024]{0:T(1024)S(1)}, f32[1024,2048]{1,0:T(8,128)S(1)}) fusion(bf16[2048,256]{1,0:T(8,128)(2,1)S(1)} %fusion.8, bf16[64,384]{1,0:T(8,128)(2,1)S(1)} %collective-permute-done.19, bf16[64,384]{1,0:T(8,128)(2,1)S(1)} %get-tuple-element.33, bf16[448,384]{1,0:T(8,128)(2,1)S(1)} %collective-permute-done.16, ...), kind=kOutput, calls=%fused_computation.183 | convolution fusion | flops 550501376 | bytes 9728000 | tf_op jit(solution)/shard_map/dot_general | solution.py:231
  80.9 1.3 %fusion = f32[1024]{0:T(1024)S(1)} fusion(f32[1024,2048]{1,0:T(8,128)S(1)} %get-tuple-element.62, f32[1024]{0:T(1024)S(1)} %get-tuple-element.61), kind=kLoop, calls=%fused_computation.3 | loop fusion | flops 4193280 | bytes 8396800 | tf_op jit(solution)/shard_map/reduce_sum | solution.py:239
  82.2 1.6 %fusion.5 = bf16[1024,128]{1,0:T(8,128)(2,1)S(1)} fusion(f32[1024,2048]{1,0:T(8,128)S(1)} %get-tuple-element.62, f32[1024]{0:T(1024)S(1)} %fusion, f32[1024]{0:T(1024)S(1)} %get-tuple-element.61, bf16[2048,256]{1,0:T(8,128)(2,1)S(1)} %fusion.8), kind=kOutput, calls=%fused_computation.11 | convolution fusion | flops 543293440 | bytes 9183232 | tf_op jit(solution)/shard_map/dot_general | solution.py:240
  84.0 14.8 %all_to_all.5 = bf16[8,128,128]{2,1,0:T(8,128)(2,1)S(1)} all-to-all(bf16[8,128,128]{2,1,0:T(8,128)(2,1)S(1)} %fusion.49), channel_id=1, replica_groups=mesh['grp'=2,'chip'=8,'core'=2] {'chip'}, dimensions={0} | all-to-all | bytes 524288 | tf_op jit(solution)/shard_map/all_to_all | solution.py:249
  (117 shorter events, 16.8 us)
Async XLA Ops:
  0.0 22.9 %slice-start = ((bf16[128,2048]{1,0:T(8,128)(2,1)}), bf16[32,2048]{1,0:T(8,128)(2,1)S(1)}, s32[]{:S(2)}) async-start(bf16[128,2048]{1,0:T(8,128)(2,1)} %param.5), calls=%async_computation.1 | async-start | bytes 262144 | tf_op jit(solution)/shard_map/slice | solution.py:138
  0.0 13.6 %copy-start.1 = (bf16[4,2048]{1,0:T(4,128)(2,1)S(1)}, bf16[4,2048]{1,0:T(4,128)(2,1)}, u32[]{:S(2)}) copy-start(bf16[4,2048]{1,0:T(4,128)(2,1)} %param.6) | copy-start | bytes 49156
  0.9 22.0 %collective-permute-start.4 = (bf16[3,2048]{1,0:T(4,128)(2,1)S(1)}, bf16[3,2048]{1,0:T(4,128)(2,1)S(1)}, u32[]{:S(2)}, u32[]{:S(2)}) collective-permute-start(bf16[3,2048]{1,0:T(4,128)(2,1)S(1)} %slice.262), channel_id=1, source_target_pairs={{0,1},{1,2},{2,3},{3,4},{4,5},{5,6},{6,7},{7,8},{8,9},{9,10},{10,1... | collective-permute-start | bytes 36872 | tf_op jit(solution)/shard_map/ppermute | solution.py:134
  4.2 22.4 %collective-permute-start.7 = (bf16[64,2048]{1,0:T(8,128)(2,1)S(1)}, bf16[64,2048]{1,0:T(8,128)(2,1)S(1)}, u32[]{:S(2)}, u32[]{:S(2)}) collective-permute-start(bf16[64,2048]{1,0:T(8,128)(2,1)S(1)} %dynamic-slice_bitcast_fusion), channel_id=1, source_target_pairs={{0,0},{1,3},{2,6},{3,9},{4,12},{5,15},{6,2},{7,5},{8,8},{9,11},{10... | collective-permute-start | bytes 786440 | tf_op jit(solution)/shard_map/ppermute | solution.py:154
  5.9 20.8 %collective-permute-start.8 = (bf16[64,1024]{1,0:T(8,128)(2,1)S(1)}, bf16[64,1024]{1,0:T(8,128)(2,1)S(1)}, u32[]{:S(2)}, u32[]{:S(2)}) collective-permute-start(bf16[64,1024]{1,0:T(8,128)(2,1)S(1)} %constant_dynamic-slice_fusion.2), channel_id=1, source_target_pairs={{0,1},{1,4},{2,7},{3,10},{4,13},{5,0},{6,3},{7,6},{8,9},{9,12},{10... | collective-permute-start | bytes 393224 | tf_op jit(solution)/shard_map/ppermute | solution.py:154
  11.8 2.3 %collective-permute-start = (s32[1,128]{1,0:T(1,128)S(1)}, s32[1,128]{1,0:T(1,128)S(1)}, u32[]{:S(2)}, u32[]{:S(2)}) collective-permute-start(s32[1,128]{1,0:T(1,128)S(1)} %bitcast.168), channel_id=1, source_target_pairs={{0,1},{1,0},{2,3},{3,2},{4,5},{5,4},{6,7},{7,6},{8,9},{9,8},{10,11... | collective-permute-start | bytes 1544 | tf_op jit(solution)/shard_map/ppermute | solution.py:105
  14.1 3.6 %collective-permute-start.1 = (s32[2,128]{1,0:T(2,128)S(1)}, s32[2,128]{1,0:T(2,128)S(1)}, u32[]{:S(2)}, u32[]{:S(2)}) collective-permute-start(s32[2,128]{1,0:T(2,128)S(1)} %pad_add_fusion.2), channel_id=1, source_target_pairs={{0,2},{1,3},{2,0},{3,1},{4,6},{5,7},{6,4},{7,5},{8,10},{9,11},{10,... | collective-permute-start | bytes 3080 | tf_op jit(solution)/shard_map/ppermute | solution.py:105
  17.7 4.0 %collective-permute-start.2 = (s32[4,128]{1,0:T(4,128)S(1)}, s32[4,128]{1,0:T(4,128)S(1)}, u32[]{:S(2)}, u32[]{:S(2)}) collective-permute-start(s32[4,128]{1,0:T(4,128)S(1)} %pad_add_fusion.1), channel_id=1, source_target_pairs={{0,4},{1,5},{2,6},{3,7},{4,0},{5,1},{6,2},{7,3},{8,12},{9,13},{10,... | collective-permute-start | bytes 6152 | tf_op jit(solution)/shard_map/ppermute | solution.py:105
  21.8 54.8 %collective-permute-start.3 = (s32[8,128]{1,0:T(8,128)S(1)}, s32[8,128]{1,0:T(8,128)S(1)}, u32[]{:S(2)}, u32[]{:S(2)}) collective-permute-start(s32[8,128]{1,0:T(8,128)S(1)} %pad_add_fusion), channel_id=1, source_target_pairs={{0,8},{1,9},{2,10},{3,11},{4,12},{5,13},{6,14},{7,15},{8,0},{9,1},... | collective-permute-start | bytes 12296 | tf_op jit(solution)/shard_map/ppermute | solution.py:105
  23.1 7.7 %collective-permute-start.17 = (bf16[32,2048]{1,0:T(8,128)(2,1)S(1)}, bf16[32,2048]{1,0:T(8,128)(2,1)S(1)}, u32[]{:S(2)}, u32[]{:S(2)}) collective-permute-start(bf16[32,2048]{1,0:T(8,128)(2,1)S(1)} %get-tuple-element.8), channel_id=1, source_target_pairs={{0,8},{1,9},{2,10},{3,11},{4,12},{5,13},{6,14},{7,15},{8,0},{9,1},... | collective-permute-start | bytes 393224 | tf_op jit(solution)/shard_map/ppermute | solution.py:105
  25.5 12.2 %collective-permute-start.5 = (bf16[128,2048]{1,0:T(8,128)(2,1)S(1)}, bf16[128,2048]{1,0:T(8,128)(2,1)S(1)}, u32[]{:S(2)}, u32[]{:S(2)}) collective-permute-start(bf16[128,2048]{1,0:T(8,128)(2,1)S(1)} %pad_maximum_fusion.12), channel_id=1, source_target_pairs={{0,2},{1,3},{2,0},{3,1},{4,6},{5,7},{6,4},{7,5},{8,10},{9,11},{10,... | collective-permute-start | bytes 1572872 | tf_op jit(solution)/shard_map/ppermute | solution.py:105
  26.7 16.1 %collective-permute-start.9 = (bf16[192,1024]{1,0:T(8,128)(2,1)S(1)}, bf16[192,1024]{1,0:T(8,128)(2,1)S(1)}, u32[]{:S(2)}, u32[]{:S(2)}) collective-permute-start(bf16[192,1024]{1,0:T(8,128)(2,1)S(1)} %pad_maximum_fusion.14), channel_id=1, source_target_pairs={{0,4},{1,5},{2,6},{3,7},{4,0},{5,1},{6,2},{7,3},{8,12},{9,13},{10,... | collective-permute-start | bytes 1179656 | tf_op jit(solution)/shard_map/ppermute | solution.py:105
  28.3 14.9 %collective-permute-start.11 = (bf16[192,1024]{1,0:T(8,128)(2,1)S(1)}, bf16[192,1024]{1,0:T(8,128)(2,1)S(1)}, u32[]{:S(2)}, u32[]{:S(2)}) collective-permute-start(bf16[192,1024]{1,0:T(8,128)(2,1)S(1)} %pad_maximum_fusion.14), channel_id=1, source_target_pairs={{0,16},{1,17},{2,18},{3,19},{4,20},{5,21},{6,22},{7,23},{8,24},{9,... | collective-permute-start | bytes 1179656 | tf_op jit(solution)/shard_map/ppermute | solution.py:105
  30.8 21.9 %collective-permute-start.6 = (bf16[96,2048]{1,0:T(8,128)(2,1)S(1)}, bf16[96,2048]{1,0:T(8,128)(2,1)S(1)}, u32[]{:S(2)}, u32[]{:S(2)}) collective-permute-start(bf16[96,2048]{1,0:T(8,128)(2,1)S(1)} %get-tuple-element.6), channel_id=1, source_target_pairs={{0,8},{1,9},{2,10},{3,11},{4,12},{5,13},{6,14},{7,15},{8,0},{9,1},... | collective-permute-start | bytes 1179656 | tf_op jit(solution)/shard_map/ppermute | solution.py:105
  37.6 29.3 %collective-permute-start.18 = (bf16[32,2048]{1,0:T(8,128)(2,1)S(1)}, bf16[32,2048]{1,0:T(8,128)(2,1)S(1)}, u32[]{:S(2)}, u32[]{:S(2)}) collective-permute-start(bf16[32,2048]{1,0:T(8,128)(2,1)S(1)} %collective-permute-done.17), channel_id=1, source_target_pairs={{0,2},{1,3},{2,0},{3,1},{4,6},{5,7},{6,4},{7,5},{8,10},{9,11},{10,... | collective-permute-start | bytes 393224 | tf_op jit(solution)/shard_map/ppermute | solution.py:105
  42.8 5.7 %collective-permute-start.10 = (bf16[192,512]{1,0:T(8,128)(2,1)S(1)}, bf16[192,512]{1,0:T(8,128)(2,1)S(1)}, u32[]{:S(2)}, u32[]{:S(2)}) collective-permute-start(bf16[192,512]{1,0:T(8,128)(2,1)S(1)} %slice.324), channel_id=1, source_target_pairs={{0,16},{1,17},{2,18},{3,19},{4,20},{5,21},{6,22},{7,23},{8,24},{9,... | collective-permute-start | bytes 589832 | tf_op jit(solution)/shard_map/ppermute | solution.py:105
  43.2 7.6 %collective-permute-start.12 = (bf16[192,512]{1,0:T(8,128)(2,1)S(1)}, bf16[192,512]{1,0:T(8,128)(2,1)S(1)}, u32[]{:S(2)}, u32[]{:S(2)}) collective-permute-start(bf16[192,512]{1,0:T(8,128)(2,1)S(1)} %slice.326), channel_id=1, source_target_pairs={{0,4},{1,5},{2,6},{3,7},{4,0},{5,1},{6,2},{7,3},{8,12},{9,13},{10,... | collective-permute-start | bytes 589832 | tf_op jit(solution)/shard_map/ppermute | solution.py:105
  48.6 15.9 %collective-permute-start.14 = (bf16[3,64,2048]{2,1,0:T(8,128)(2,1)S(1)}, bf16[3,64,2048]{2,1,0:T(8,128)(2,1)S(1)}, u32[]{:S(2)}, u32[]{:S(2)}) collective-permute-start(bf16[3,64,2048]{2,1,0:T(8,128)(2,1)S(1)} %constant_dynamic-slice_fusion.1), channel_id=1, source_target_pairs={{0,1},{1,0},{2,3},{3,2},{4,5},{5,4},{6,7},{7,6},{8,9},{9,8},{10,11... | collective-permute-start | bytes 2359304 | tf_op jit(solution)/shard_map/ppermute | solution.py:105
  52.8 11.5 %collective-permute-start.13 = (bf16[96,2048]{1,0:T(8,128)(2,1)S(1)}, bf16[96,2048]{1,0:T(8,128)(2,1)S(1)}, u32[]{:S(2)}, u32[]{:S(2)}) collective-permute-start(bf16[96,2048]{1,0:T(8,128)(2,1)S(1)} %get-tuple-element.27), channel_id=1, source_target_pairs={{0,2},{1,3},{2,0},{3,1},{4,6},{5,7},{6,4},{7,5},{8,10},{9,11},{10,... | collective-permute-start | bytes 1179656 | tf_op jit(solution)/shard_map/ppermute | solution.py:105
  55.8 8.9 %collective-permute-start.15 = (bf16[3,64,2048]{2,1,0:T(8,128)(2,1)S(1)}, bf16[3,64,2048]{2,1,0:T(8,128)(2,1)S(1)}, u32[]{:S(2)}, u32[]{:S(2)}) collective-permute-start(bf16[3,64,2048]{2,1,0:T(8,128)(2,1)S(1)} %constant_dynamic-slice_fusion), channel_id=1, source_target_pairs={{0,1},{1,0},{2,3},{3,2},{4,5},{5,4},{6,7},{7,6},{8,9},{9,8},{10,11... | collective-permute-start | bytes 2359304 | tf_op jit(solution)/shard_map/ppermute | solution.py:105
  66.8 9.6 %collective-permute-start.16 = (bf16[448,384]{1,0:T(8,128)(2,1)S(1)}, bf16[448,384]{1,0:T(8,128)(2,1)S(1)}, u32[]{:S(2)}, u32[]{:S(2)}) collective-permute-start(bf16[448,384]{1,0:T(8,128)(2,1)S(1)} %get-tuple-element.20), channel_id=1, source_target_pairs={{0,4},{1,5},{2,6},{3,7},{4,0},{5,1},{6,2},{7,3},{8,12},{9,13},{10,... | collective-permute-start | bytes 1032200 | tf_op jit(solution)/shard_map/ppermute | solution.py:105
  68.0 9.0 %collective-permute-start.19 = (bf16[64,384]{1,0:T(8,128)(2,1)S(1)}, bf16[64,384]{1,0:T(8,128)(2,1)S(1)}, u32[]{:S(2)}, u32[]{:S(2)}) collective-permute-start(bf16[64,384]{1,0:T(8,128)(2,1)S(1)} %get-tuple-element.34), channel_id=1, source_target_pairs={{0,4},{1,5},{2,6},{3,7},{4,0},{5,1},{6,2},{7,3},{8,12},{9,13},{10,... | collective-permute-start | bytes 147464 | tf_op jit(solution)/shard_map/ppermute | solution.py:105
  76.5 2.0 %collective-permute-start.20 = (bf16[896,256]{1,0:T(8,128)(2,1)S(1)}, bf16[896,256]{1,0:T(8,128)(2,1)S(1)}, u32[]{:S(2)}, u32[]{:S(2)}) collective-permute-start(bf16[896,256]{1,0:T(8,128)(2,1)S(1)} %pad_maximum_fusion.13), channel_id=1, source_target_pairs={{0,1},{1,0},{2,3},{3,2},{4,5},{5,4},{6,7},{7,6},{8,9},{9,8},{10,11... | collective-permute-start | bytes 1376264 | tf_op jit(solution)/shard_map/ppermute | solution.py:105
  77.0 1.5 %collective-permute-start.21 = (bf16[128,256]{1,0:T(8,128)(2,1)S(1)}, bf16[128,256]{1,0:T(8,128)(2,1)S(1)}, u32[]{:S(2)}, u32[]{:S(2)}) collective-permute-start(bf16[128,256]{1,0:T(8,128)(2,1)S(1)} %pad_maximum_fusion.15), channel_id=1, source_target_pairs={{0,1},{1,0},{2,3},{3,2},{4,5},{5,4},{6,7},{7,6},{8,9},{9,8},{10,11... | collective-permute-start | bytes 196616 | tf_op jit(solution)/shard_map/ppermute | solution.py:105
  (1 other events, 13.3 us)

commit v23 on v22

--- a/solution.py
+++ b/solution.py
@@ -126,7 +126,7 @@
     me = 2 * chip + core
     both = ("chip", "core")
     every = ("grp", "chip", "core")
-    part = tok_rows // 4
+    part = 3 * tok_rows // 4
     rest = tok_rows - part
     features = frames.shape[1]
     CORE, Y, Z0, Z1 = 1, 2, 4, 8

time: 100 us -> 95.3 us (0.953)
  waiting for transfers between devices: 35.9 us -> 31.5 us
  blocking collectives: 14.8 us -> 13.6 us
  starting transfers between devices: 29.1 us -> 30.2 us
    ppermute x19, waiting for transfers between devices: 35.9 us -> 31.5 us  [xor_swap(): return lax.ppermute(value, axes, [(d, d ^ bit) for d in range(count)])]
    all_to_all x1, blocking collectives: 14.8 us -> 13.6 us  [body_by_head(): lax.all_to_all(sent, 'chip', split_axis=0, concat_axis=0, tiled=True)]
    ppermute x19, starting transfers between devices: 20.9 us -> 22 us  [xor_swap(): return lax.ppermute(value, axes, [(d, d ^ bit) for d in range(count)])]
  transfers between devices with their start and end apart: 22 -> 22, of which waited for: 12 -> 10; matrix products, arithmetic and copies ran while one was open for 9% -> 9% of each run, Pallas kernels for 0% -> 0%
where the time goes in v23:
time: 95.3 us; the launch traced here: 95 us
  waiting for transfers between devices  31.5 us (33%)
  starting transfers between devices  30.2 us (32%)
  blocking collectives  13.6 us (14%)
  matrix products  6.36 us (7%)
  local copies, waits for them, and re-layouts  6.14 us (6%)
  other arithmetic  3.87 us (4%)
  between operations  3.4 us (4%)
    ppermute x19, waiting for transfers between devices, xor_swap(): return lax.ppermute(value, axes, [(d, d ^ bit) for d in range(count)])  31.5 us
    ppermute x19, starting transfers between devices, xor_swap(): return lax.ppermute(value, axes, [(d, d ^ bit) for d in range(count)])  22 us
    all_to_all x1, blocking collectives, body_by_head(): lax.all_to_all(sent, 'chip', split_axis=0, concat_axis=0, tiled=True)  13.6 us
    ppermute x2, starting transfers between devices, to_heads(): return lax.ppermute(block, every, pairs)  5.83 us
    dot_general x2, matrix products, project(): lax.dot_general(rows, two_heads, (((1,), (1,)), ((), ())), preferred_elem...  2.42 us
    ppermute x1, starting transfers between devices, body_by_head(): lax.ppermute(frames[tok_rows - (KW - 1):], both, [(i, i + 1) for i in ran...  2.36 us
    dot_general x1, matrix products, body_by_head(): lax.dot_general(query, keyed[:, :HD], (((1,), (1,)), ((), ())), preferred...  2.34 us
  transfers between devices with their start and end apart: 22, of which 10 were waited for; matrix products, arithmetic and copies ran while one was open for 9% of the time, Pallas kernels for 0%

profile of v23, /device:TPU:0, one launch (start us, length us, event | category | flops | bytes accessed | tf_op | source)
XLA Modules:
  0.0 95.0 jit_solution(10779518475934513358)
XLA Ops:
  0.9 2.4 %collective-permute-start.4 = (bf16[3,2048]{1,0:T(4,128)(2,1)S(1)}, bf16[3,2048]{1,0:T(4,128)(2,1)S(1)}, u32[]{:S(2)}, u32[]{:S(2)}) collective-permute-start(bf16[3,2048]{1,0:T(4,128)(2,1)S(1)} %slice.262), channel_id=1, source_target_pairs={{0,1},{1,2},{2,3},{3,4},{4,5},{5,6},{6,7},{7,8},{8,9},{9,10},{10,1... | collective-permute-start | bytes 36872 | tf_op jit(solution)/shard_map/ppermute | solution.py:134
  5.9 5.2 %collective-permute-start.8 = (bf16[64,1024]{1,0:T(8,128)(2,1)S(1)}, bf16[64,1024]{1,0:T(8,128)(2,1)S(1)}, u32[]{:S(2)}, u32[]{:S(2)}) collective-permute-start(bf16[64,1024]{1,0:T(8,128)(2,1)S(1)} %constant_dynamic-slice_fusion.2), channel_id=1, source_target_pairs={{0,1},{1,4},{2,7},{3,10},{4,13},{5,0},{6,3},{7,6},{8,9},{9,12},{10... | collective-permute-start | bytes 393224 | tf_op jit(solution)/shard_map/ppermute | solution.py:154
  11.8 1.5 %collective-permute-start = (s32[1,128]{1,0:T(1,128)S(1)}, s32[1,128]{1,0:T(1,128)S(1)}, u32[]{:S(2)}, u32[]{:S(2)}) collective-permute-start(s32[1,128]{1,0:T(1,128)S(1)} %bitcast.168), channel_id=1, source_target_pairs={{0,1},{1,0},{2,3},{3,2},{4,5},{5,4},{6,7},{7,6},{8,9},{9,8},{10,11... | collective-permute-start | bytes 1544 | tf_op jit(solution)/shard_map/ppermute | solution.py:105
  14.1 1.5 %collective-permute-start.1 = (s32[2,128]{1,0:T(2,128)S(1)}, s32[2,128]{1,0:T(2,128)S(1)}, u32[]{:S(2)}, u32[]{:S(2)}) collective-permute-start(s32[2,128]{1,0:T(2,128)S(1)} %pad_add_fusion.2), channel_id=1, source_target_pairs={{0,2},{1,3},{2,0},{3,1},{4,6},{5,7},{6,4},{7,5},{8,10},{9,11},{10,... | collective-permute-start | bytes 3080 | tf_op jit(solution)/shard_map/ppermute | solution.py:105
  15.8 1.9 %collective-permute-done.1 = s32[2,128]{1,0:T(2,128)S(1)} collective-permute-done((s32[2,128]{1,0:T(2,128)S(1)}, s32[2,128]{1,0:T(2,128)S(1)}, u32[]{:S(2)}, u32[]{:S(2)}) %collective-permute-start.1) | collective-permute-done | bytes 1056 | tf_op jit(solution)/shard_map/ppermute | solution.py:105
  17.7 2.5 %collective-permute-start.2 = (s32[4,128]{1,0:T(4,128)S(1)}, s32[4,128]{1,0:T(4,128)S(1)}, u32[]{:S(2)}, u32[]{:S(2)}) collective-permute-start(s32[4,128]{1,0:T(4,128)S(1)} %pad_add_fusion.1), channel_id=1, source_target_pairs={{0,4},{1,5},{2,6},{3,7},{4,0},{5,1},{6,2},{7,3},{8,12},{9,13},{10,... | collective-permute-start | bytes 6152 | tf_op jit(solution)/shard_map/ppermute | solution.py:105
  20.2 1.6 %collective-permute-done.2 = s32[4,128]{1,0:T(4,128)S(1)} collective-permute-done((s32[4,128]{1,0:T(4,128)S(1)}, s32[4,128]{1,0:T(4,128)S(1)}, u32[]{:S(2)}, u32[]{:S(2)}) %collective-permute-start.2) | collective-permute-done | bytes 2080 | tf_op jit(solution)/shard_map/ppermute | solution.py:105
  23.4 1.9 %collective-permute-start.17 = (bf16[96,2048]{1,0:T(8,128)(2,1)S(1)}, bf16[96,2048]{1,0:T(8,128)(2,1)S(1)}, u32[]{:S(2)}, u32[]{:S(2)}) collective-permute-start(bf16[96,2048]{1,0:T(8,128)(2,1)S(1)} %get-tuple-element.8), channel_id=1, source_target_pairs={{0,8},{1,9},{2,10},{3,11},{4,12},{5,13},{6,14},{7,15},{8,0},{9,1},... | collective-permute-start | bytes 1179656 | tf_op jit(solution)/shard_map/ppermute | solution.py:105
  26.8 1.6 %collective-permute-start.9 = (bf16[192,1024]{1,0:T(8,128)(2,1)S(1)}, bf16[192,1024]{1,0:T(8,128)(2,1)S(1)}, u32[]{:S(2)}, u32[]{:S(2)}) collective-permute-start(bf16[192,1024]{1,0:T(8,128)(2,1)S(1)} %pad_maximum_fusion.13), channel_id=1, source_target_pairs={{0,4},{1,5},{2,6},{3,7},{4,0},{5,1},{6,2},{7,3},{8,12},{9,13},{10,... | collective-permute-start | bytes 1179656 | tf_op jit(solution)/shard_map/ppermute | solution.py:105
  28.4 1.5 %collective-permute-start.11 = (bf16[192,1024]{1,0:T(8,128)(2,1)S(1)}, bf16[192,1024]{1,0:T(8,128)(2,1)S(1)}, u32[]{:S(2)}, u32[]{:S(2)}) collective-permute-start(bf16[192,1024]{1,0:T(8,128)(2,1)S(1)} %pad_maximum_fusion.13), channel_id=1, source_target_pairs={{0,16},{1,17},{2,18},{3,19},{4,20},{5,21},{6,22},{7,23},{8,24},{9,... | collective-permute-start | bytes 1179656 | tf_op jit(solution)/shard_map/ppermute | solution.py:105
  29.9 12.6 %collective-permute-done.17 = bf16[96,2048]{1,0:T(8,128)(2,1)S(1)} collective-permute-done((bf16[96,2048]{1,0:T(8,128)(2,1)S(1)}, bf16[96,2048]{1,0:T(8,128)(2,1)S(1)}, u32[]{:S(2)}, u32[]{:S(2)}) %collective-permute-start.17) | collective-permute-done | bytes 393248 | tf_op jit(solution)/shard_map/ppermute | solution.py:105
  43.2 1.9 %collective-permute-start.10 = (bf16[192,512]{1,0:T(8,128)(2,1)S(1)}, bf16[192,512]{1,0:T(8,128)(2,1)S(1)}, u32[]{:S(2)}, u32[]{:S(2)}) collective-permute-start(bf16[192,512]{1,0:T(8,128)(2,1)S(1)} %slice.324), channel_id=1, source_target_pairs={{0,16},{1,17},{2,18},{3,19},{4,20},{5,21},{6,22},{7,23},{8,24},{9,... | collective-permute-start | bytes 589832 | tf_op jit(solution)/shard_map/ppermute | solution.py:105
  45.1 3.0 %collective-permute-start.12 = (bf16[192,512]{1,0:T(8,128)(2,1)S(1)}, bf16[192,512]{1,0:T(8,128)(2,1)S(1)}, u32[]{:S(2)}, u32[]{:S(2)}) collective-permute-start(bf16[192,512]{1,0:T(8,128)(2,1)S(1)} %slice.326), channel_id=1, source_target_pairs={{0,4},{1,5},{2,6},{3,7},{4,0},{5,1},{6,2},{7,3},{8,12},{9,13},{10,... | collective-permute-start | bytes 589832 | tf_op jit(solution)/shard_map/ppermute | solution.py:105
  48.3 1.4 %collective-permute-done.10 = bf16[192,512]{1,0:T(8,128)(2,1)S(1)} collective-permute-done((bf16[192,512]{1,0:T(8,128)(2,1)S(1)}, bf16[192,512]{1,0:T(8,128)(2,1)S(1)}, u32[]{:S(2)}, u32[]{:S(2)}) %collective-permute-start.10) | collective-permute-done | bytes 196640 | tf_op jit(solution)/shard_map/ppermute | solution.py:105
  51.6 2.7 %collective-permute-done.12 = bf16[192,512]{1,0:T(8,128)(2,1)S(1)} collective-permute-done((bf16[192,512]{1,0:T(8,128)(2,1)S(1)}, bf16[192,512]{1,0:T(8,128)(2,1)S(1)}, u32[]{:S(2)}, u32[]{:S(2)}) %collective-permute-start.12) | collective-permute-done | bytes 196640 | tf_op jit(solution)/shard_map/ppermute | solution.py:105
  56.2 1.3 %collective-permute-start.13 = (bf16[32,2048]{1,0:T(8,128)(2,1)S(1)}, bf16[32,2048]{1,0:T(8,128)(2,1)S(1)}, u32[]{:S(2)}, u32[]{:S(2)}) collective-permute-start(bf16[32,2048]{1,0:T(8,128)(2,1)S(1)} %get-tuple-element.33), channel_id=1, source_target_pairs={{0,2},{1,3},{2,0},{3,1},{4,6},{5,7},{6,4},{7,5},{8,10},{9,11},{10,... | collective-permute-start | bytes 393224 | tf_op jit(solution)/shard_map/ppermute | solution.py:105
  58.0 3.3 %collective-permute-done.13 = bf16[32,2048]{1,0:T(8,128)(2,1)S(1)} collective-permute-done((bf16[32,2048]{1,0:T(8,128)(2,1)S(1)}, bf16[32,2048]{1,0:T(8,128)(2,1)S(1)}, u32[]{:S(2)}, u32[]{:S(2)}) %collective-permute-start.13) | collective-permute-done | bytes 131104 | tf_op jit(solution)/shard_map/ppermute | solution.py:105
  61.9 1.2 %fusion.4 = bf16[320,768]{1,0:T(8,128)(2,1)S(1)} fusion(bf16[320,2048]{1,0:T(8,128)(2,1)S(1)} %constant_dynamic-update-slice_fusion, bf16[384,2048]{1,0:T(8,128)(2,1)S(1)} %bitcast.155, bf16[384,2048]{1,0:T(8,128)(2,1)S(1)} %bitcast.153), kind=kOutput, calls=%fused_computation.10 | convolution fusion | flops 1013170176 | bytes 4947968 | tf_op jit(solution)/shard_map/dot_general | solution.py:196
  66.6 5.2 %collective-permute-done.16 = bf16[320,384]{1,0:T(8,128)(2,1)S(1)} collective-permute-done((bf16[320,384]{1,0:T(8,128)(2,1)S(1)}, bf16[320,384]{1,0:T(8,128)(2,1)S(1)}, u32[]{:S(2)}, u32[]{:S(2)}) %collective-permute-start.16) | collective-permute-done | bytes 245792 | tf_op jit(solution)/shard_map/ppermute | solution.py:105
  71.9 1.5 %collective-permute-done.19 = bf16[192,384]{1,0:T(8,128)(2,1)S(1)} collective-permute-done((bf16[192,384]{1,0:T(8,128)(2,1)S(1)}, bf16[192,384]{1,0:T(8,128)(2,1)S(1)}, u32[]{:S(2)}, u32[]{:S(2)}) %collective-permute-start.19) | collective-permute-done | bytes 147488 | tf_op jit(solution)/shard_map/ppermute | solution.py:105
  75.0 2.3 %fusion.61 = (f32[1024]{0:T(1024)S(1)}, f32[1024,2048]{1,0:T(8,128)S(1)}) fusion(bf16[2048,256]{1,0:T(8,128)(2,1)S(1)} %fusion.8, bf16[192,384]{1,0:T(8,128)(2,1)S(1)} %collective-permute-done.19, bf16[192,384]{1,0:T(8,128)(2,1)S(1)} %get-tuple-element.29, bf16[320,384]{1,0:T(8,128)(2,1)S(1)} %collective-permute-done.16, ...), kind=kOutput, calls=%fused_computation.183 | convolution fusion | flops 550501376 | bytes 9728000 | tf_op jit(solution)/shard_map/dot_general | solution.py:231
  77.3 1.3 %fusion = f32[1024]{0:T(1024)S(1)} fusion(f32[1024,2048]{1,0:T(8,128)S(1)} %get-tuple-element.62, f32[1024]{0:T(1024)S(1)} %get-tuple-element.61), kind=kLoop, calls=%fused_computation.3 | loop fusion | flops 4193280 | bytes 8396800 | tf_op jit(solution)/shard_map/reduce_sum | solution.py:239
  78.6 1.6 %fusion.6 = bf16[1024,128]{1,0:T(8,128)(2,1)S(1)} fusion(f32[1024,2048]{1,0:T(8,128)S(1)} %get-tuple-element.62, f32[1024]{0:T(1024)S(1)} %fusion, f32[1024]{0:T(1024)S(1)} %get-tuple-element.61, bf16[2048,256]{1,0:T(8,128)(2,1)S(1)} %fusion.8), kind=kOutput, calls=%fused_computation.12 | convolution fusion | flops 543293440 | bytes 9183232 | tf_op jit(solution)/shard_map/dot_general | solution.py:240
  80.4 13.6 %all_to_all.5 = bf16[8,128,128]{2,1,0:T(8,128)(2,1)S(1)} all-to-all(bf16[8,128,128]{2,1,0:T(8,128)(2,1)S(1)} %fusion.45), channel_id=1, replica_groups=mesh['grp'=2,'chip'=8,'core'=2] {'chip'}, dimensions={0} | all-to-all | bytes 524288 | tf_op jit(solution)/shard_map/all_to_all | solution.py:249
  (117 shorter events, 17.4 us)
Async XLA Ops:
  0.0 22.9 %slice-start = ((bf16[128,2048]{1,0:T(8,128)(2,1)}), bf16[96,2048]{1,0:T(8,128)(2,1)S(1)}, s32[]{:S(2)}) async-start(bf16[128,2048]{1,0:T(8,128)(2,1)} %param.5), calls=%async_computation.1 | async-start | bytes 786432 | tf_op jit(solution)/shard_map/slice | solution.py:138
  0.0 13.5 %copy-start.1 = (bf16[4,2048]{1,0:T(4,128)(2,1)S(1)}, bf16[4,2048]{1,0:T(4,128)(2,1)}, u32[]{:S(2)}) copy-start(bf16[4,2048]{1,0:T(4,128)(2,1)} %param.6) | copy-start | bytes 49156
  0.9 22.0 %collective-permute-start.4 = (bf16[3,2048]{1,0:T(4,128)(2,1)S(1)}, bf16[3,2048]{1,0:T(4,128)(2,1)S(1)}, u32[]{:S(2)}, u32[]{:S(2)}) collective-permute-start(bf16[3,2048]{1,0:T(4,128)(2,1)S(1)} %slice.262), channel_id=1, source_target_pairs={{0,1},{1,2},{2,3},{3,4},{4,5},{5,6},{6,7},{7,8},{8,9},{9,10},{10,1... | collective-permute-start | bytes 36872 | tf_op jit(solution)/shard_map/ppermute | solution.py:134
  4.2 22.5 %collective-permute-start.7 = (bf16[64,2048]{1,0:T(8,128)(2,1)S(1)}, bf16[64,2048]{1,0:T(8,128)(2,1)S(1)}, u32[]{:S(2)}, u32[]{:S(2)}) collective-permute-start(bf16[64,2048]{1,0:T(8,128)(2,1)S(1)} %dynamic-slice_bitcast_fusion), channel_id=1, source_target_pairs={{0,0},{1,3},{2,6},{3,9},{4,12},{5,15},{6,2},{7,5},{8,8},{9,11},{10... | collective-permute-start | bytes 786440 | tf_op jit(solution)/shard_map/ppermute | solution.py:154
  5.9 20.8 %collective-permute-start.8 = (bf16[64,1024]{1,0:T(8,128)(2,1)S(1)}, bf16[64,1024]{1,0:T(8,128)(2,1)S(1)}, u32[]{:S(2)}, u32[]{:S(2)}) collective-permute-start(bf16[64,1024]{1,0:T(8,128)(2,1)S(1)} %constant_dynamic-slice_fusion.2), channel_id=1, source_target_pairs={{0,1},{1,4},{2,7},{3,10},{4,13},{5,0},{6,3},{7,6},{8,9},{9,12},{10... | collective-permute-start | bytes 393224 | tf_op jit(solution)/shard_map/ppermute | solution.py:154
  11.8 2.3 %collective-permute-start = (s32[1,128]{1,0:T(1,128)S(1)}, s32[1,128]{1,0:T(1,128)S(1)}, u32[]{:S(2)}, u32[]{:S(2)}) collective-permute-start(s32[1,128]{1,0:T(1,128)S(1)} %bitcast.168), channel_id=1, source_target_pairs={{0,1},{1,0},{2,3},{3,2},{4,5},{5,4},{6,7},{7,6},{8,9},{9,8},{10,11... | collective-permute-start | bytes 1544 | tf_op jit(solution)/shard_map/ppermute | solution.py:105
  14.1 3.6 %collective-permute-start.1 = (s32[2,128]{1,0:T(2,128)S(1)}, s32[2,128]{1,0:T(2,128)S(1)}, u32[]{:S(2)}, u32[]{:S(2)}) collective-permute-start(s32[2,128]{1,0:T(2,128)S(1)} %pad_add_fusion.2), channel_id=1, source_target_pairs={{0,2},{1,3},{2,0},{3,1},{4,6},{5,7},{6,4},{7,5},{8,10},{9,11},{10,... | collective-permute-start | bytes 3080 | tf_op jit(solution)/shard_map/ppermute | solution.py:105
  17.7 4.0 %collective-permute-start.2 = (s32[4,128]{1,0:T(4,128)S(1)}, s32[4,128]{1,0:T(4,128)S(1)}, u32[]{:S(2)}, u32[]{:S(2)}) collective-permute-start(s32[4,128]{1,0:T(4,128)S(1)} %pad_add_fusion.1), channel_id=1, source_target_pairs={{0,4},{1,5},{2,6},{3,7},{4,0},{5,1},{6,2},{7,3},{8,12},{9,13},{10,... | collective-permute-start | bytes 6152 | tf_op jit(solution)/shard_map/ppermute | solution.py:105
  21.8 44.8 %collective-permute-start.3 = (s32[8,128]{1,0:T(8,128)S(1)}, s32[8,128]{1,0:T(8,128)S(1)}, u32[]{:S(2)}, u32[]{:S(2)}) collective-permute-start(s32[8,128]{1,0:T(8,128)S(1)} %pad_add_fusion), channel_id=1, source_target_pairs={{0,8},{1,9},{2,10},{3,11},{4,12},{5,13},{6,14},{7,15},{8,0},{9,1},... | collective-permute-start | bytes 12296 | tf_op jit(solution)/shard_map/ppermute | solution.py:105
  23.4 19.1 %collective-permute-start.17 = (bf16[96,2048]{1,0:T(8,128)(2,1)S(1)}, bf16[96,2048]{1,0:T(8,128)(2,1)S(1)}, u32[]{:S(2)}, u32[]{:S(2)}) collective-permute-start(bf16[96,2048]{1,0:T(8,128)(2,1)S(1)} %get-tuple-element.8), channel_id=1, source_target_pairs={{0,8},{1,9},{2,10},{3,11},{4,12},{5,13},{6,14},{7,15},{8,0},{9,1},... | collective-permute-start | bytes 1179656 | tf_op jit(solution)/shard_map/ppermute | solution.py:105
  25.5 17.0 %collective-permute-start.5 = (bf16[128,2048]{1,0:T(8,128)(2,1)S(1)}, bf16[128,2048]{1,0:T(8,128)(2,1)S(1)}, u32[]{:S(2)}, u32[]{:S(2)}) collective-permute-start(bf16[128,2048]{1,0:T(8,128)(2,1)S(1)} %pad_maximum_fusion.12), channel_id=1, source_target_pairs={{0,2},{1,3},{2,0},{3,1},{4,6},{5,7},{6,4},{7,5},{8,10},{9,11},{10,... | collective-permute-start | bytes 1572872 | tf_op jit(solution)/shard_map/ppermute | solution.py:105
  26.8 16.3 %collective-permute-start.9 = (bf16[192,1024]{1,0:T(8,128)(2,1)S(1)}, bf16[192,1024]{1,0:T(8,128)(2,1)S(1)}, u32[]{:S(2)}, u32[]{:S(2)}) collective-permute-start(bf16[192,1024]{1,0:T(8,128)(2,1)S(1)} %pad_maximum_fusion.13), channel_id=1, source_target_pairs={{0,4},{1,5},{2,6},{3,7},{4,0},{5,1},{6,2},{7,3},{8,12},{9,13},{10,... | collective-permute-start | bytes 1179656 | tf_op jit(solution)/shard_map/ppermute | solution.py:105
  28.4 16.7 %collective-permute-start.11 = (bf16[192,1024]{1,0:T(8,128)(2,1)S(1)}, bf16[192,1024]{1,0:T(8,128)(2,1)S(1)}, u32[]{:S(2)}, u32[]{:S(2)}) collective-permute-start(bf16[192,1024]{1,0:T(8,128)(2,1)S(1)} %pad_maximum_fusion.13), channel_id=1, source_target_pairs={{0,16},{1,17},{2,18},{3,19},{4,20},{5,21},{6,22},{7,23},{8,24},{9,... | collective-permute-start | bytes 1179656 | tf_op jit(solution)/shard_map/ppermute | solution.py:105
  42.5 13.6 %collective-permute-start.6 = (bf16[32,2048]{1,0:T(8,128)(2,1)S(1)}, bf16[32,2048]{1,0:T(8,128)(2,1)S(1)}, u32[]{:S(2)}, u32[]{:S(2)}) collective-permute-start(bf16[32,2048]{1,0:T(8,128)(2,1)S(1)} %get-tuple-element.6), channel_id=1, source_target_pairs={{0,8},{1,9},{2,10},{3,11},{4,12},{5,13},{6,14},{7,15},{8,0},{9,1},... | collective-permute-start | bytes 393224 | tf_op jit(solution)/shard_map/ppermute | solution.py:105
  42.5 21.8 %collective-permute-start.18 = (bf16[96,2048]{1,0:T(8,128)(2,1)S(1)}, bf16[96,2048]{1,0:T(8,128)(2,1)S(1)}, u32[]{:S(2)}, u32[]{:S(2)}) collective-permute-start(bf16[96,2048]{1,0:T(8,128)(2,1)S(1)} %collective-permute-done.17), channel_id=1, source_target_pairs={{0,2},{1,3},{2,0},{3,1},{4,6},{5,7},{6,4},{7,5},{8,10},{9,11},{10,... | collective-permute-start | bytes 1179656 | tf_op jit(solution)/shard_map/ppermute | solution.py:105
  43.2 6.5 %collective-permute-start.10 = (bf16[192,512]{1,0:T(8,128)(2,1)S(1)}, bf16[192,512]{1,0:T(8,128)(2,1)S(1)}, u32[]{:S(2)}, u32[]{:S(2)}) collective-permute-start(bf16[192,512]{1,0:T(8,128)(2,1)S(1)} %slice.324), channel_id=1, source_target_pairs={{0,16},{1,17},{2,18},{3,19},{4,20},{5,21},{6,22},{7,23},{8,24},{9,... | collective-permute-start | bytes 589832 | tf_op jit(solution)/shard_map/ppermute | solution.py:105
  45.1 9.2 %collective-permute-start.12 = (bf16[192,512]{1,0:T(8,128)(2,1)S(1)}, bf16[192,512]{1,0:T(8,128)(2,1)S(1)}, u32[]{:S(2)}, u32[]{:S(2)}) collective-permute-start(bf16[192,512]{1,0:T(8,128)(2,1)S(1)} %slice.326), channel_id=1, source_target_pairs={{0,4},{1,5},{2,6},{3,7},{4,0},{5,1},{6,2},{7,3},{8,12},{9,13},{10,... | collective-permute-start | bytes 589832 | tf_op jit(solution)/shard_map/ppermute | solution.py:105
  49.7 11.5 %collective-permute-start.14 = (bf16[3,64,2048]{2,1,0:T(8,128)(2,1)S(1)}, bf16[3,64,2048]{2,1,0:T(8,128)(2,1)S(1)}, u32[]{:S(2)}, u32[]{:S(2)}) collective-permute-start(bf16[3,64,2048]{2,1,0:T(8,128)(2,1)S(1)} %constant_dynamic-slice_fusion.1), channel_id=1, source_target_pairs={{0,1},{1,0},{2,3},{3,2},{4,5},{5,4},{6,7},{7,6},{8,9},{9,8},{10,11... | collective-permute-start | bytes 2359304 | tf_op jit(solution)/shard_map/ppermute | solution.py:105
  56.2 5.0 %collective-permute-start.13 = (bf16[32,2048]{1,0:T(8,128)(2,1)S(1)}, bf16[32,2048]{1,0:T(8,128)(2,1)S(1)}, u32[]{:S(2)}, u32[]{:S(2)}) collective-permute-start(bf16[32,2048]{1,0:T(8,128)(2,1)S(1)} %get-tuple-element.33), channel_id=1, source_target_pairs={{0,2},{1,3},{2,0},{3,1},{4,6},{5,7},{6,4},{7,5},{8,10},{9,11},{10,... | collective-permute-start | bytes 393224 | tf_op jit(solution)/shard_map/ppermute | solution.py:105
  57.9 3.7 %collective-permute-start.15 = (bf16[3,64,2048]{2,1,0:T(8,128)(2,1)S(1)}, bf16[3,64,2048]{2,1,0:T(8,128)(2,1)S(1)}, u32[]{:S(2)}, u32[]{:S(2)}) collective-permute-start(bf16[3,64,2048]{2,1,0:T(8,128)(2,1)S(1)} %constant_dynamic-slice_fusion), channel_id=1, source_target_pairs={{0,1},{1,0},{2,3},{3,2},{4,5},{5,4},{6,7},{7,6},{8,9},{9,8},{10,11... | collective-permute-start | bytes 2359304 | tf_op jit(solution)/shard_map/ppermute | solution.py:105
  63.2 8.6 %collective-permute-start.16 = (bf16[320,384]{1,0:T(8,128)(2,1)S(1)}, bf16[320,384]{1,0:T(8,128)(2,1)S(1)}, u32[]{:S(2)}, u32[]{:S(2)}) collective-permute-start(bf16[320,384]{1,0:T(8,128)(2,1)S(1)} %get-tuple-element.26), channel_id=1, source_target_pairs={{0,4},{1,5},{2,6},{3,7},{4,0},{5,1},{6,2},{7,3},{8,12},{9,13},{10,... | collective-permute-start | bytes 737288 | tf_op jit(solution)/shard_map/ppermute | solution.py:105
  65.6 7.8 %collective-permute-start.19 = (bf16[192,384]{1,0:T(8,128)(2,1)S(1)}, bf16[192,384]{1,0:T(8,128)(2,1)S(1)}, u32[]{:S(2)}, u32[]{:S(2)}) collective-permute-start(bf16[192,384]{1,0:T(8,128)(2,1)S(1)} %get-tuple-element.30), channel_id=1, source_target_pairs={{0,4},{1,5},{2,6},{3,7},{4,0},{5,1},{6,2},{7,3},{8,12},{9,13},{10,... | collective-permute-start | bytes 442376 | tf_op jit(solution)/shard_map/ppermute | solution.py:105
  71.8 3.1 %collective-permute-start.20 = (bf16[640,256]{1,0:T(8,128)(2,1)S(1)}, bf16[640,256]{1,0:T(8,128)(2,1)S(1)}, u32[]{:S(2)}, u32[]{:S(2)}) collective-permute-start(bf16[640,256]{1,0:T(8,128)(2,1)S(1)} %pad_maximum_fusion.14), channel_id=1, source_target_pairs={{0,1},{1,0},{2,3},{3,2},{4,5},{5,4},{6,7},{7,6},{8,9},{9,8},{10,11... | collective-permute-start | bytes 983048 | tf_op jit(solution)/shard_map/ppermute | solution.py:105
  73.4 1.5 %collective-permute-start.21 = (bf16[384,256]{1,0:T(8,128)(2,1)S(1)}, bf16[384,256]{1,0:T(8,128)(2,1)S(1)}, u32[]{:S(2)}, u32[]{:S(2)}) collective-permute-start(bf16[384,256]{1,0:T(8,128)(2,1)S(1)} %pad_maximum_fusion.15), channel_id=1, source_target_pairs={{0,1},{1,0},{2,3},{3,2},{4,5},{5,4},{6,7},{7,6},{8,9},{9,8},{10,11... | collective-permute-start | bytes 589832 | tf_op jit(solution)/shard_map/ppermute | solution.py:105
  (1 other events, 13.3 us)

commit v24 on v21

--- a/solution.py
+++ b/solution.py
@@ -162,9 +162,8 @@
     cut = half // 2
     fourth = [xor_swap(paired[:, :cut], devices, every), xor_swap(mine_too[:, cut:], Z0)]
 
-    zero = zero_after(fourth[0]) + zero_after(fourth[1])
-    far_beside_late = xor_swap(far_late + zero, Y)
-    far_beside_early = xor_swap(far_early + zero, Y)
+    far_beside_late = xor_swap(far_late + zero_after(fourth[0]) + zero_after(fourth[1]), Y)
+    far_beside_early = xor_swap(far_early, Y)
 
     fourth = jnp.concatenate(fourth, axis=1)
 

time: 92.3 us -> 104 us (1.13)
  waiting for transfers between devices: 28 us -> 48.3 us
  starting transfers between devices: 27.5 us -> 22.3 us
  blocking collectives: 16.5 us -> 13.3 us
    ppermute x19, waiting for transfers between devices: 27.9 us -> 48.3 us  [xor_swap(): return lax.ppermute(value, axes, [(d, d ^ bit) for d in range(count)])]
    ppermute x19, starting transfers between devices: 17.9 us -> 12.8 us  [xor_swap(): return lax.ppermute(value, axes, [(d, d ^ bit) for d in range(count)])]
    all_to_all x1, blocking collectives: 16.5 us -> 13.3 us  [body_by_head(): lax.all_to_all(sent, 'chip', split_axis=0, concat_axis=0, tiled=True)]
  transfers between devices with their start and end apart: 22 -> 22, of which waited for: 11 -> 12; matrix products, arithmetic and copies ran while one was open for 10% -> 9% of each run, Pallas kernels for 0% -> 0%
where the time goes in v24:
time: 104 us
  waiting for transfers between devices  48.3 us (46%)
  starting transfers between devices  22.3 us (21%)
  blocking collectives  13.3 us (13%)
  matrix products  6.54 us (6%)
  local copies, waits for them, and re-layouts  6.13 us (6%)
  other arithmetic  3.86 us (4%)
  between operations  3.42 us (3%)
    ppermute x19, waiting for transfers between devices, xor_swap(): return lax.ppermute(value, axes, [(d, d ^ bit) for d in range(count)])  48.3 us
    all_to_all x1, blocking collectives, body_by_head(): lax.all_to_all(sent, 'chip', split_axis=0, concat_axis=0, tiled=True)  13.3 us
    ppermute x19, starting transfers between devices, xor_swap(): return lax.ppermute(value, axes, [(d, d ^ bit) for d in range(count)])  12.8 us
    ppermute x1, starting transfers between devices, body_by_head(): lax.ppermute(frames[tok_rows - (KW - 1):], both, [(i, i + 1) for i in ran...  5.11 us
    ppermute x2, starting transfers between devices, to_heads(): return lax.ppermute(block, every, pairs)  4.48 us
    dot_general x2, matrix products, project(): lax.dot_general(rows, two_heads, (((1,), (1,)), ((), ())), preferred_elem...  2.61 us
    dot_general x1, matrix products, body_by_head(): lax.dot_general(query, keyed[:, :HD], (((1,), (1,)), ((), ())), preferred...  2.33 us
  transfers between devices with their start and end apart: 22, of which 12 were waited for; matrix products, arithmetic and copies ran while one was open for 9% of the time, Pallas kernels for 0%

profile of v24, /device:TPU:0, one launch (start us, length us, event | category | flops | bytes accessed | tf_op | source)
XLA Modules:
  0.0 103.9 jit_solution(16399015330942848047)
XLA Ops:
  0.0 1.1 %dynamic-slice_bitcast_fusion = bf16[64,2048]{1,0:T(8,128)(2,1)S(1)} fusion(bf16[3,64,2048]{2,1,0:T(8,128)(2,1)} %bitcast.158, s32[]{:T(128)S(6)} %select_n.135), kind=kLoop, calls=%fused_computation.66 | loop fusion | bytes 524292 | tf_op jit(solution)/shard_map/jit(dynamic_index_in_dim)/squeeze | solution.py:155
  1.7 1.0 slice.323
  2.8 3.8 %collective-permute-start.9 = (bf16[64,1024]{1,0:T(8,128)(2,1)S(1)}, bf16[64,1024]{1,0:T(8,128)(2,1)S(1)}, u32[]{:S(2)}, u32[]{:S(2)}) collective-permute-start(bf16[64,1024]{1,0:T(8,128)(2,1)S(1)} %constant_dynamic-slice_fusion.2), channel_id=1, source_target_pairs={{0,1},{1,4},{2,7},{3,10},{4,13},{5,0},{6,3},{7,6},{8,9},{9,12},{10... | collective-permute-start | bytes 393224 | tf_op jit(solution)/shard_map/ppermute | solution.py:153
  7.3 5.1 %collective-permute-start.4 = (bf16[3,2048]{1,0:T(4,128)(2,1)S(1)}, bf16[3,2048]{1,0:T(4,128)(2,1)S(1)}, u32[]{:S(2)}, u32[]{:S(2)}) collective-permute-start(bf16[3,2048]{1,0:T(4,128)(2,1)S(1)} %slice.262), channel_id=1, source_target_pairs={{0,1},{1,2},{2,3},{3,4},{4,5},{5,6},{6,7},{7,8},{8,9},{9,10},{10,1... | collective-permute-start | bytes 36872 | tf_op jit(solution)/shard_map/ppermute | solution.py:133
  14.4 1.6 %collective-permute-start.1 = (s32[2,128]{1,0:T(2,128)S(1)}, s32[2,128]{1,0:T(2,128)S(1)}, u32[]{:S(2)}, u32[]{:S(2)}) collective-permute-start(s32[2,128]{1,0:T(2,128)S(1)} %pad_add_fusion.2), channel_id=1, source_target_pairs={{0,2},{1,3},{2,0},{3,1},{4,6},{5,7},{6,4},{7,5},{8,10},{9,11},{10,... | collective-permute-start | bytes 3080 | tf_op jit(solution)/shard_map/ppermute | solution.py:105
  16.2 1.8 %collective-permute-done.1 = s32[2,128]{1,0:T(2,128)S(1)} collective-permute-done((s32[2,128]{1,0:T(2,128)S(1)}, s32[2,128]{1,0:T(2,128)S(1)}, u32[]{:S(2)}, u32[]{:S(2)}) %collective-permute-start.1) | collective-permute-done | bytes 1056 | tf_op jit(solution)/shard_map/ppermute | solution.py:105
  20.4 1.2 %collective-permute-done.2 = s32[4,128]{1,0:T(4,128)S(1)} collective-permute-done((s32[4,128]{1,0:T(4,128)S(1)}, s32[4,128]{1,0:T(4,128)S(1)}, u32[]{:S(2)}, u32[]{:S(2)}) %collective-permute-start.2) | collective-permute-done | bytes 2080 | tf_op jit(solution)/shard_map/ppermute | solution.py:105
  21.6 2.2 %collective-permute-start.3 = (s32[8,128]{1,0:T(8,128)S(1)}, s32[8,128]{1,0:T(8,128)S(1)}, u32[]{:S(2)}, u32[]{:S(2)}) collective-permute-start(s32[8,128]{1,0:T(8,128)S(1)} %pad_add_fusion), channel_id=1, source_target_pairs={{0,8},{1,9},{2,10},{3,11},{4,12},{5,13},{6,14},{7,15},{8,0},{9,1},... | collective-permute-start | bytes 12296 | tf_op jit(solution)/shard_map/ppermute | solution.py:105
  24.6 2.2 %collective-permute-start.17 = (bf16[64,2048]{1,0:T(8,128)(2,1)S(1)}, bf16[64,2048]{1,0:T(8,128)(2,1)S(1)}, u32[]{:S(2)}, u32[]{:S(2)}) collective-permute-start(bf16[64,2048]{1,0:T(8,128)(2,1)S(1)} %get-tuple-element.6), channel_id=1, source_target_pairs={{0,8},{1,9},{2,10},{3,11},{4,12},{5,13},{6,14},{7,15},{8,0},{9,1},... | collective-permute-start | bytes 786440 | tf_op jit(solution)/shard_map/ppermute | solution.py:105
  27.6 15.8 %collective-permute-done.6 = bf16[64,2048]{1,0:T(8,128)(2,1)S(1)} collective-permute-done((bf16[64,2048]{1,0:T(8,128)(2,1)S(1)}, bf16[64,2048]{1,0:T(8,128)(2,1)S(1)}, u32[]{:S(2)}, u32[]{:S(2)}) %collective-permute-start.6) | collective-permute-done | bytes 262176 | tf_op jit(solution)/shard_map/ppermute | solution.py:105
  44.0 6.3 %collective-permute-done.7 = bf16[64,2048]{1,0:T(8,128)(2,1)S(1)} collective-permute-done((bf16[64,2048]{1,0:T(8,128)(2,1)S(1)}, bf16[64,2048]{1,0:T(8,128)(2,1)S(1)}, u32[]{:S(2)}, u32[]{:S(2)}) %collective-permute-start.7) | collective-permute-done | bytes 262176 | tf_op jit(solution)/shard_map/ppermute | solution.py:105
  50.5 5.9 %collective-permute-done.12 = bf16[192,1024]{1,0:T(8,128)(2,1)S(1)} collective-permute-done((bf16[192,1024]{1,0:T(8,128)(2,1)S(1)}, bf16[192,1024]{1,0:T(8,128)(2,1)S(1)}, u32[]{:S(2)}, u32[]{:S(2)}) %collective-permute-start.12) | collective-permute-done | bytes 393248 | tf_op jit(solution)/shard_map/ppermute | solution.py:105
  57.1 6.2 %collective-permute-done.13 = bf16[192,512]{1,0:T(8,128)(2,1)S(1)} collective-permute-done((bf16[192,512]{1,0:T(8,128)(2,1)S(1)}, bf16[192,512]{1,0:T(8,128)(2,1)S(1)}, u32[]{:S(2)}, u32[]{:S(2)}) %collective-permute-start.13) | collective-permute-done | bytes 196640 | tf_op jit(solution)/shard_map/ppermute | solution.py:105
  67.7 1.5 %collective-permute-start.18 = (bf16[64,2048]{1,0:T(8,128)(2,1)S(1)}, bf16[64,2048]{1,0:T(8,128)(2,1)S(1)}, u32[]{:S(2)}, u32[]{:S(2)}) collective-permute-start(bf16[64,2048]{1,0:T(8,128)(2,1)S(1)} %add_add_fusion), channel_id=1, source_target_pairs={{0,2},{1,3},{2,0},{3,1},{4,6},{5,7},{6,4},{7,5},{8,10},{9,11},{10,... | collective-permute-start | bytes 786440 | tf_op jit(solution)/shard_map/ppermute | solution.py:105
  69.8 1.4 %fusion.4 = bf16[384,768]{1,0:T(8,128)(2,1)S(1)} fusion(bf16[384,2048]{1,0:T(8,128)(2,1)S(1)} %constant_dynamic-update-slice_fusion, bf16[384,2048]{1,0:T(8,128)(2,1)S(1)} %bitcast.155, bf16[384,2048]{1,0:T(8,128)(2,1)S(1)} %bitcast.153), kind=kOutput, calls=%fused_computation.10 | convolution fusion | flops 1214545920 | bytes 5308416 | tf_op jit(solution)/shard_map/dot_general | solution.py:195
  71.6 4.8 %collective-permute-done.18 = bf16[64,2048]{1,0:T(8,128)(2,1)S(1)} collective-permute-done((bf16[64,2048]{1,0:T(8,128)(2,1)S(1)}, bf16[64,2048]{1,0:T(8,128)(2,1)S(1)}, u32[]{:S(2)}, u32[]{:S(2)}) %collective-permute-start.18) | collective-permute-done | bytes 262176 | tf_op jit(solution)/shard_map/ppermute | solution.py:105
  76.4 1.2 %fusion.6 = bf16[128,768]{1,0:T(8,128)(2,1)S(1)} fusion(bf16[384,2048]{1,0:T(8,128)(2,1)S(1)} %bitcast.156, bf16[384,2048]{1,0:T(8,128)(2,1)S(1)} %bitcast.154, bf16[64,2048]{1,0:T(8,128)(2,1)S(1)} %collective-permute-done.18, bf16[64,2048]{1,0:T(8,128)(2,1)S(1)} %collective-permute-done.17), kind=kOutput, calls=%fused_computation.12 | convolution fusion | flops 410091520 | bytes 3866624 | tf_op jit(solution)/shard_map/dot_general | solution.py:195
  78.0 2.9 %collective-permute-done.16 = bf16[384,384]{1,0:T(8,128)(2,1)S(1)} collective-permute-done((bf16[384,384]{1,0:T(8,128)(2,1)S(1)}, bf16[384,384]{1,0:T(8,128)(2,1)S(1)}, u32[]{:S(2)}, u32[]{:S(2)}) %collective-permute-start.16) | collective-permute-done | bytes 294944 | tf_op jit(solution)/shard_map/ppermute | solution.py:105
  81.0 1.6 %collective-permute-done.19 = bf16[128,384]{1,0:T(8,128)(2,1)S(1)} collective-permute-done((bf16[128,384]{1,0:T(8,128)(2,1)S(1)}, bf16[128,384]{1,0:T(8,128)(2,1)S(1)}, u32[]{:S(2)}, u32[]{:S(2)}) %collective-permute-start.19) | collective-permute-done | bytes 98336 | tf_op jit(solution)/shard_map/ppermute | solution.py:105
  82.9 1.1 %collective-permute-done.21 = bf16[256,256]{1,0:T(8,128)(2,1)S(1)} collective-permute-done((bf16[256,256]{1,0:T(8,128)(2,1)S(1)}, bf16[256,256]{1,0:T(8,128)(2,1)S(1)}, u32[]{:S(2)}, u32[]{:S(2)}) %collective-permute-start.21) | collective-permute-done | bytes 131104 | tf_op jit(solution)/shard_map/ppermute | solution.py:105
  84.1 2.3 %fusion.61 = (f32[1024]{0:T(1024)S(1)}, f32[1024,2048]{1,0:T(8,128)S(1)}) fusion(bf16[2048,256]{1,0:T(8,128)(2,1)S(1)} %fusion.8, bf16[128,384]{1,0:T(8,128)(2,1)S(1)} %collective-permute-done.19, bf16[128,384]{1,0:T(8,128)(2,1)S(1)} %get-tuple-element.31, bf16[384,384]{1,0:T(8,128)(2,1)S(1)} %collective-permute-done.16, ...), kind=kOutput, calls=%fused_computation.183 | convolution fusion | flops 550501376 | bytes 9728000 | tf_op jit(solution)/shard_map/dot_general | solution.py:231
  86.4 1.3 %fusion = f32[1024]{0:T(1024)S(1)} fusion(f32[1024,2048]{1,0:T(8,128)S(1)} %get-tuple-element.60, f32[1024]{0:T(1024)S(1)} %get-tuple-element.59), kind=kLoop, calls=%fused_computation.3 | loop fusion | flops 4193280 | bytes 8396800 | tf_op jit(solution)/shard_map/reduce_sum | solution.py:239
  87.7 1.6 %fusion.5 = bf16[1024,128]{1,0:T(8,128)(2,1)S(1)} fusion(f32[1024,2048]{1,0:T(8,128)S(1)} %get-tuple-element.60, f32[1024]{0:T(1024)S(1)} %fusion, f32[1024]{0:T(1024)S(1)} %get-tuple-element.59, bf16[2048,256]{1,0:T(8,128)(2,1)S(1)} %fusion.8), kind=kOutput, calls=%fused_computation.11 | convolution fusion | flops 543293440 | bytes 9183232 | tf_op jit(solution)/shard_map/dot_general | solution.py:240
  89.6 13.3 %all_to_all.5 = bf16[8,128,128]{2,1,0:T(8,128)(2,1)S(1)} all-to-all(bf16[8,128,128]{2,1,0:T(8,128)(2,1)S(1)} %fusion.45), channel_id=1, replica_groups=mesh['grp'=2,'chip'=8,'core'=2] {'chip'}, dimensions={0} | all-to-all | bytes 524288 | tf_op jit(solution)/shard_map/all_to_all | solution.py:249
  (117 shorter events, 13.4 us)
Async XLA Ops:
  0.0 18.8 %slice-start = ((bf16[128,2048]{1,0:T(8,128)(2,1)}), bf16[64,2048]{1,0:T(8,128)(2,1)S(1)}, s32[]{:S(2)}) async-start(bf16[128,2048]{1,0:T(8,128)(2,1)} %param.5), calls=%async_computation.1 | async-start | bytes 524288 | tf_op jit(solution)/shard_map/slice | solution.py:137
  0.0 13.5 %copy-start.1 = (bf16[4,2048]{1,0:T(4,128)(2,1)S(1)}, bf16[4,2048]{1,0:T(4,128)(2,1)}, u32[]{:S(2)}) copy-start(bf16[4,2048]{1,0:T(4,128)(2,1)} %param.6) | copy-start | bytes 49156
  1.1 23.6 %collective-permute-start.8 = (bf16[64,2048]{1,0:T(8,128)(2,1)S(1)}, bf16[64,2048]{1,0:T(8,128)(2,1)S(1)}, u32[]{:S(2)}, u32[]{:S(2)}) collective-permute-start(bf16[64,2048]{1,0:T(8,128)(2,1)S(1)} %dynamic-slice_bitcast_fusion), channel_id=1, source_target_pairs={{0,0},{1,3},{2,6},{3,9},{4,12},{5,15},{6,2},{7,5},{8,8},{9,11},{10... | collective-permute-start | bytes 786440 | tf_op jit(solution)/shard_map/ppermute | solution.py:153
  2.8 24.1 %collective-permute-start.9 = (bf16[64,1024]{1,0:T(8,128)(2,1)S(1)}, bf16[64,1024]{1,0:T(8,128)(2,1)S(1)}, u32[]{:S(2)}, u32[]{:S(2)}) collective-permute-start(bf16[64,1024]{1,0:T(8,128)(2,1)S(1)} %constant_dynamic-slice_fusion.2), channel_id=1, source_target_pairs={{0,1},{1,4},{2,7},{3,10},{4,13},{5,0},{6,3},{7,6},{8,9},{9,12},{10... | collective-permute-start | bytes 393224 | tf_op jit(solution)/shard_map/ppermute | solution.py:153
  7.3 11.5 %collective-permute-start.4 = (bf16[3,2048]{1,0:T(4,128)(2,1)S(1)}, bf16[3,2048]{1,0:T(4,128)(2,1)S(1)}, u32[]{:S(2)}, u32[]{:S(2)}) collective-permute-start(bf16[3,2048]{1,0:T(4,128)(2,1)S(1)} %slice.262), channel_id=1, source_target_pairs={{0,1},{1,2},{2,3},{3,4},{4,5},{5,6},{6,7},{7,8},{8,9},{9,10},{10,1... | collective-permute-start | bytes 36872 | tf_op jit(solution)/shard_map/ppermute | solution.py:133
  13.2 1.2 %collective-permute-start = (s32[1,128]{1,0:T(1,128)S(1)}, s32[1,128]{1,0:T(1,128)S(1)}, u32[]{:S(2)}, u32[]{:S(2)}) collective-permute-start(s32[1,128]{1,0:T(1,128)S(1)} %bitcast.168), channel_id=1, source_target_pairs={{0,1},{1,0},{2,3},{3,2},{4,5},{5,4},{6,7},{7,6},{8,9},{9,8},{10,11... | collective-permute-start | bytes 1544 | tf_op jit(solution)/shard_map/ppermute | solution.py:105
  14.4 3.6 %collective-permute-start.1 = (s32[2,128]{1,0:T(2,128)S(1)}, s32[2,128]{1,0:T(2,128)S(1)}, u32[]{:S(2)}, u32[]{:S(2)}) collective-permute-start(s32[2,128]{1,0:T(2,128)S(1)} %pad_add_fusion.2), channel_id=1, source_target_pairs={{0,2},{1,3},{2,0},{3,1},{4,6},{5,7},{6,4},{7,5},{8,10},{9,11},{10,... | collective-permute-start | bytes 3080 | tf_op jit(solution)/shard_map/ppermute | solution.py:105
  18.0 3.6 %collective-permute-start.2 = (s32[4,128]{1,0:T(4,128)S(1)}, s32[4,128]{1,0:T(4,128)S(1)}, u32[]{:S(2)}, u32[]{:S(2)}) collective-permute-start(s32[4,128]{1,0:T(4,128)S(1)} %pad_add_fusion.1), channel_id=1, source_target_pairs={{0,4},{1,5},{2,6},{3,7},{4,0},{5,1},{6,2},{7,3},{8,12},{9,13},{10,... | collective-permute-start | bytes 6152 | tf_op jit(solution)/shard_map/ppermute | solution.py:105
  19.5 23.9 %collective-permute-start.5 = (bf16[128,2048]{1,0:T(8,128)(2,1)S(1)}, bf16[128,2048]{1,0:T(8,128)(2,1)S(1)}, u32[]{:S(2)}, u32[]{:S(2)}) collective-permute-start(bf16[128,2048]{1,0:T(8,128)(2,1)S(1)} %pad_maximum_fusion.12), channel_id=1, source_target_pairs={{0,2},{1,3},{2,0},{3,1},{4,6},{5,7},{6,4},{7,5},{8,10},{9,11},{10,... | collective-permute-start | bytes 1572872 | tf_op jit(solution)/shard_map/ppermute | solution.py:105
  21.6 61.1 %collective-permute-start.3 = (s32[8,128]{1,0:T(8,128)S(1)}, s32[8,128]{1,0:T(8,128)S(1)}, u32[]{:S(2)}, u32[]{:S(2)}) collective-permute-start(s32[8,128]{1,0:T(8,128)S(1)} %pad_add_fusion), channel_id=1, source_target_pairs={{0,8},{1,9},{2,10},{3,11},{4,12},{5,13},{6,14},{7,15},{8,0},{9,1},... | collective-permute-start | bytes 12296 | tf_op jit(solution)/shard_map/ppermute | solution.py:105
  23.9 19.5 %collective-permute-start.6 = (bf16[64,2048]{1,0:T(8,128)(2,1)S(1)}, bf16[64,2048]{1,0:T(8,128)(2,1)S(1)}, u32[]{:S(2)}, u32[]{:S(2)}) collective-permute-start(bf16[64,2048]{1,0:T(8,128)(2,1)S(1)} %get-tuple-element.8), channel_id=1, source_target_pairs={{0,8},{1,9},{2,10},{3,11},{4,12},{5,13},{6,14},{7,15},{8,0},{9,1},... | collective-permute-start | bytes 786440 | tf_op jit(solution)/shard_map/ppermute | solution.py:105
  24.6 43.0 %collective-permute-start.17 = (bf16[64,2048]{1,0:T(8,128)(2,1)S(1)}, bf16[64,2048]{1,0:T(8,128)(2,1)S(1)}, u32[]{:S(2)}, u32[]{:S(2)}) collective-permute-start(bf16[64,2048]{1,0:T(8,128)(2,1)S(1)} %get-tuple-element.6), channel_id=1, source_target_pairs={{0,8},{1,9},{2,10},{3,11},{4,12},{5,13},{6,14},{7,15},{8,0},{9,1},... | collective-permute-start | bytes 786440 | tf_op jit(solution)/shard_map/ppermute | solution.py:105
  26.9 23.4 %collective-permute-start.10 = (bf16[192,1024]{1,0:T(8,128)(2,1)S(1)}, bf16[192,1024]{1,0:T(8,128)(2,1)S(1)}, u32[]{:S(2)}, u32[]{:S(2)}) collective-permute-start(bf16[192,1024]{1,0:T(8,128)(2,1)S(1)} %pad_maximum_fusion.14), channel_id=1, source_target_pairs={{0,16},{1,17},{2,18},{3,19},{4,20},{5,21},{6,22},{7,23},{8,24},{9,... | collective-permute-start | bytes 1179656 | tf_op jit(solution)/shard_map/ppermute | solution.py:105
  43.4 13.0 %collective-permute-start.12 = (bf16[192,1024]{1,0:T(8,128)(2,1)S(1)}, bf16[192,1024]{1,0:T(8,128)(2,1)S(1)}, u32[]{:S(2)}, u32[]{:S(2)}) collective-permute-start(bf16[192,1024]{1,0:T(8,128)(2,1)S(1)} %pad_maximum_fusion.14), channel_id=1, source_target_pairs={{0,4},{1,5},{2,6},{3,7},{4,0},{5,1},{6,2},{7,3},{8,12},{9,13},{10,... | collective-permute-start | bytes 1179656 | tf_op jit(solution)/shard_map/ppermute | solution.py:105
  43.4 6.9 %collective-permute-start.7 = (bf16[64,2048]{1,0:T(8,128)(2,1)S(1)}, bf16[64,2048]{1,0:T(8,128)(2,1)S(1)}, u32[]{:S(2)}, u32[]{:S(2)}) collective-permute-start(bf16[64,2048]{1,0:T(8,128)(2,1)S(1)} %collective-permute-done.6), channel_id=1, source_target_pairs={{0,2},{1,3},{2,0},{3,1},{4,6},{5,7},{6,4},{7,5},{8,10},{9,11},{10,... | collective-permute-start | bytes 786440 | tf_op jit(solution)/shard_map/ppermute | solution.py:105
  56.4 6.9 %collective-permute-start.13 = (bf16[192,512]{1,0:T(8,128)(2,1)S(1)}, bf16[192,512]{1,0:T(8,128)(2,1)S(1)}, u32[]{:S(2)}, u32[]{:S(2)}) collective-permute-start(bf16[192,512]{1,0:T(8,128)(2,1)S(1)} %slice.328), channel_id=1, source_target_pairs={{0,16},{1,17},{2,18},{3,19},{4,20},{5,21},{6,22},{7,23},{8,24},{9,... | collective-permute-start | bytes 589832 | tf_op jit(solution)/shard_map/ppermute | solution.py:105
  56.8 6.6 %collective-permute-start.14 = (bf16[192,512]{1,0:T(8,128)(2,1)S(1)}, bf16[192,512]{1,0:T(8,128)(2,1)S(1)}, u32[]{:S(2)}, u32[]{:S(2)}) collective-permute-start(bf16[192,512]{1,0:T(8,128)(2,1)S(1)} %slice.329), channel_id=1, source_target_pairs={{0,4},{1,5},{2,6},{3,7},{4,0},{5,1},{6,2},{7,3},{8,12},{9,13},{10,... | collective-permute-start | bytes 589832 | tf_op jit(solution)/shard_map/ppermute | solution.py:105
  57.0 12.1 %collective-permute-start.11 = (bf16[3,64,2048]{2,1,0:T(8,128)(2,1)S(1)}, bf16[3,64,2048]{2,1,0:T(8,128)(2,1)S(1)}, u32[]{:S(2)}, u32[]{:S(2)}) collective-permute-start(bf16[3,64,2048]{2,1,0:T(8,128)(2,1)S(1)} %constant_dynamic-slice_fusion.1), channel_id=1, source_target_pairs={{0,1},{1,0},{2,3},{3,2},{4,5},{5,4},{6,7},{7,6},{8,9},{9,8},{10,11... | collective-permute-start | bytes 2359304 | tf_op jit(solution)/shard_map/ppermute | solution.py:105
  63.7 5.7 %collective-permute-start.15 = (bf16[3,64,2048]{2,1,0:T(8,128)(2,1)S(1)}, bf16[3,64,2048]{2,1,0:T(8,128)(2,1)S(1)}, u32[]{:S(2)}, u32[]{:S(2)}) collective-permute-start(bf16[3,64,2048]{2,1,0:T(8,128)(2,1)S(1)} %constant_dynamic-slice_fusion), channel_id=1, source_target_pairs={{0,1},{1,0},{2,3},{3,2},{4,5},{5,4},{6,7},{7,6},{8,9},{9,8},{10,11... | collective-permute-start | bytes 2359304 | tf_op jit(solution)/shard_map/ppermute | solution.py:105
  67.7 8.8 %collective-permute-start.18 = (bf16[64,2048]{1,0:T(8,128)(2,1)S(1)}, bf16[64,2048]{1,0:T(8,128)(2,1)S(1)}, u32[]{:S(2)}, u32[]{:S(2)}) collective-permute-start(bf16[64,2048]{1,0:T(8,128)(2,1)S(1)} %add_add_fusion), channel_id=1, source_target_pairs={{0,2},{1,3},{2,0},{3,1},{4,6},{5,7},{6,4},{7,5},{8,10},{9,11},{10,... | collective-permute-start | bytes 786440 | tf_op jit(solution)/shard_map/ppermute | solution.py:105
  71.3 9.6 %collective-permute-start.16 = (bf16[384,384]{1,0:T(8,128)(2,1)S(1)}, bf16[384,384]{1,0:T(8,128)(2,1)S(1)}, u32[]{:S(2)}, u32[]{:S(2)}) collective-permute-start(bf16[384,384]{1,0:T(8,128)(2,1)S(1)} %get-tuple-element.24), channel_id=1, source_target_pairs={{0,4},{1,5},{2,6},{3,7},{4,0},{5,1},{6,2},{7,3},{8,12},{9,13},{10,... | collective-permute-start | bytes 884744 | tf_op jit(solution)/shard_map/ppermute | solution.py:105
  77.6 5.0 %collective-permute-start.19 = (bf16[128,384]{1,0:T(8,128)(2,1)S(1)}, bf16[128,384]{1,0:T(8,128)(2,1)S(1)}, u32[]{:S(2)}, u32[]{:S(2)}) collective-permute-start(bf16[128,384]{1,0:T(8,128)(2,1)S(1)} %get-tuple-element.32), channel_id=1, source_target_pairs={{0,4},{1,5},{2,6},{3,7},{4,0},{5,1},{6,2},{7,3},{8,12},{9,13},{10,... | collective-permute-start | bytes 294920 | tf_op jit(solution)/shard_map/ppermute | solution.py:105
  80.9 3.1 %collective-permute-start.20 = (bf16[768,256]{1,0:T(8,128)(2,1)S(1)}, bf16[768,256]{1,0:T(8,128)(2,1)S(1)}, u32[]{:S(2)}, u32[]{:S(2)}) collective-permute-start(bf16[768,256]{1,0:T(8,128)(2,1)S(1)} %pad_maximum_fusion.13), channel_id=1, source_target_pairs={{0,1},{1,0},{2,3},{3,2},{4,5},{5,4},{6,7},{7,6},{8,9},{9,8},{10,11... | collective-permute-start | bytes 1179656 | tf_op jit(solution)/shard_map/ppermute | solution.py:105
  82.6 1.4 %collective-permute-start.21 = (bf16[256,256]{1,0:T(8,128)(2,1)S(1)}, bf16[256,256]{1,0:T(8,128)(2,1)S(1)}, u32[]{:S(2)}, u32[]{:S(2)}) collective-permute-start(bf16[256,256]{1,0:T(8,128)(2,1)S(1)} %pad_maximum_fusion.15), channel_id=1, source_target_pairs={{0,1},{1,0},{2,3},{3,2},{4,5},{5,4},{6,7},{7,6},{8,9},{9,8},{10,11... | collective-permute-start | bytes 393224 | tf_op jit(solution)/shard_map/ppermute | solution.py:105
  (1 other events, 13.3 us)

commit v25 on v19

--- a/solution.py
+++ b/solution.py
@@ -235,7 +235,8 @@
     )
     scores = jnp.where(allowed, scores, jnp.float32(-1e30))
     expd = jnp.exp(scores - jnp.max(scores, axis=-1, keepdims=True))
-    weights = (expd / jnp.sum(expd, axis=-1, keepdims=True)).astype(jnp.bfloat16)
+    share = 1.0 / jnp.sum(expd, axis=-1, keepdims=True)
+    weights = (expd * share).astype(jnp.bfloat16)
     mixed = jnp.dot(weights, keyed[:, HD:], preferred_element_type=jnp.float32)
     mixed = mixed.astype(jnp.bfloat16)
 

time: 89 us -> 88.9 us (level)
  no operation moved by 1% of the time
where the time goes in v25:
time: 88.9 us; the launch traced here: 88.6 us
  waiting for transfers between devices  30.4 us (34%)
  starting transfers between devices  25.6 us (29%)
  blocking collectives  12.7 us (14%)
  matrix products  6.49 us (7%)
  local copies, waits for them, and re-layouts  6.12 us (7%)
  other arithmetic  3.91 us (4%)
  between operations  3.42 us (4%)
    ppermute x19, waiting for transfers between devices, xor_swap(): return lax.ppermute(value, axes, [(d, d ^ bit) for d in range(count)])  30.4 us
    ppermute x19, starting transfers between devices, xor_swap(): return lax.ppermute(value, axes, [(d, d ^ bit) for d in range(count)])  17.4 us
    all_to_all x1, blocking collectives, body_by_head(): lax.all_to_all(sent, 'chip', split_axis=0, concat_axis=0, tiled=True)  12.7 us
    ppermute x2, starting transfers between devices, to_heads(): return lax.ppermute(block, every, pairs)  5.83 us
    dot_general x2, matrix products, project(): lax.dot_general(rows, two_heads, (((1,), (1,)), ((), ())), preferred_elem...  2.61 us
    ppermute x1, starting transfers between devices, body_by_head(): lax.ppermute(frames[tok_rows - (KW - 1):], both, [(i, i + 1) for i in ran...  2.36 us
    dot_general x1, matrix products, body_by_head(): lax.dot_general(query, keyed[:, :HD], (((1,), (1,)), ((), ())), preferred...  2.33 us
  transfers between devices with their start and end apart: 22, of which 10 were waited for; matrix products, arithmetic and copies ran while one was open for 10% of the time, Pallas kernels for 0%

profile of v25, /device:TPU:0, one launch (start us, length us, event | category | flops | bytes accessed | tf_op | source)
XLA Modules:
  0.0 88.6 jit_solution(944808386445203545)
XLA Ops:
  0.9 2.4 %collective-permute-start.4 = (bf16[3,2048]{1,0:T(4,128)(2,1)S(1)}, bf16[3,2048]{1,0:T(4,128)(2,1)S(1)}, u32[]{:S(2)}, u32[]{:S(2)}) collective-permute-start(bf16[3,2048]{1,0:T(4,128)(2,1)S(1)} %slice.262), channel_id=1, source_target_pairs={{0,1},{1,2},{2,3},{3,4},{4,5},{5,6},{6,7},{7,8},{8,9},{9,10},{10,1... | collective-permute-start | bytes 36872 | tf_op jit(solution)/shard_map/ppermute | solution.py:133
  5.9 5.2 %collective-permute-start.8 = (bf16[64,1024]{1,0:T(8,128)(2,1)S(1)}, bf16[64,1024]{1,0:T(8,128)(2,1)S(1)}, u32[]{:S(2)}, u32[]{:S(2)}) collective-permute-start(bf16[64,1024]{1,0:T(8,128)(2,1)S(1)} %constant_dynamic-slice_fusion.2), channel_id=1, source_target_pairs={{0,1},{1,4},{2,7},{3,10},{4,13},{5,0},{6,3},{7,6},{8,9},{9,12},{10... | collective-permute-start | bytes 393224 | tf_op jit(solution)/shard_map/ppermute | solution.py:153
  11.8 1.5 %collective-permute-start = (s32[1,128]{1,0:T(1,128)S(1)}, s32[1,128]{1,0:T(1,128)S(1)}, u32[]{:S(2)}, u32[]{:S(2)}) collective-permute-start(s32[1,128]{1,0:T(1,128)S(1)} %bitcast.168), channel_id=1, source_target_pairs={{0,1},{1,0},{2,3},{3,2},{4,5},{5,4},{6,7},{7,6},{8,9},{9,8},{10,11... | collective-permute-start | bytes 1544 | tf_op jit(solution)/shard_map/ppermute | solution.py:105
  14.1 1.5 %collective-permute-start.1 = (s32[2,128]{1,0:T(2,128)S(1)}, s32[2,128]{1,0:T(2,128)S(1)}, u32[]{:S(2)}, u32[]{:S(2)}) collective-permute-start(s32[2,128]{1,0:T(2,128)S(1)} %pad_add_fusion.2), channel_id=1, source_target_pairs={{0,2},{1,3},{2,0},{3,1},{4,6},{5,7},{6,4},{7,5},{8,10},{9,11},{10,... | collective-permute-start | bytes 3080 | tf_op jit(solution)/shard_map/ppermute | solution.py:105
  15.8 1.9 %collective-permute-done.1 = s32[2,128]{1,0:T(2,128)S(1)} collective-permute-done((s32[2,128]{1,0:T(2,128)S(1)}, s32[2,128]{1,0:T(2,128)S(1)}, u32[]{:S(2)}, u32[]{:S(2)}) %collective-permute-start.1) | collective-permute-done | bytes 1056 | tf_op jit(solution)/shard_map/ppermute | solution.py:105
  17.7 2.5 %collective-permute-start.2 = (s32[4,128]{1,0:T(4,128)S(1)}, s32[4,128]{1,0:T(4,128)S(1)}, u32[]{:S(2)}, u32[]{:S(2)}) collective-permute-start(s32[4,128]{1,0:T(4,128)S(1)} %pad_add_fusion.1), channel_id=1, source_target_pairs={{0,4},{1,5},{2,6},{3,7},{4,0},{5,1},{6,2},{7,3},{8,12},{9,13},{10,... | collective-permute-start | bytes 6152 | tf_op jit(solution)/shard_map/ppermute | solution.py:105
  22.0 1.9 %collective-permute-start.9 = (bf16[192,1024]{1,0:T(8,128)(2,1)S(1)}, bf16[192,1024]{1,0:T(8,128)(2,1)S(1)}, u32[]{:S(2)}, u32[]{:S(2)}) collective-permute-start(bf16[192,1024]{1,0:T(8,128)(2,1)S(1)} %pad_maximum_fusion.14), channel_id=1, source_target_pairs={{0,4},{1,5},{2,6},{3,7},{4,0},{5,1},{6,2},{7,3},{8,12},{9,13},{10,... | collective-permute-start | bytes 1179656 | tf_op jit(solution)/shard_map/ppermute | solution.py:105
  23.9 1.1 %collective-permute-start.11 = (bf16[192,1024]{1,0:T(8,128)(2,1)S(1)}, bf16[192,1024]{1,0:T(8,128)(2,1)S(1)}, u32[]{:S(2)}, u32[]{:S(2)}) collective-permute-start(bf16[192,1024]{1,0:T(8,128)(2,1)S(1)} %pad_maximum_fusion.14), channel_id=1, source_target_pairs={{0,16},{1,17},{2,18},{3,19},{4,20},{5,21},{6,22},{7,23},{8,24},{9,... | collective-permute-start | bytes 1179656 | tf_op jit(solution)/shard_map/ppermute | solution.py:105
  25.1 1.4 %collective-permute-start.3 = (s32[8,128]{1,0:T(8,128)S(1)}, s32[8,128]{1,0:T(8,128)S(1)}, u32[]{:S(2)}, u32[]{:S(2)}) collective-permute-start(s32[8,128]{1,0:T(8,128)S(1)} %pad_add_fusion), channel_id=1, source_target_pairs={{0,8},{1,9},{2,10},{3,11},{4,12},{5,13},{6,14},{7,15},{8,0},{9,1},... | collective-permute-start | bytes 12296 | tf_op jit(solution)/shard_map/ppermute | solution.py:105
  26.4 7.6 %collective-permute-done.17 = bf16[64,2048]{1,0:T(8,128)(2,1)S(1)} collective-permute-done((bf16[64,2048]{1,0:T(8,128)(2,1)S(1)}, bf16[64,2048]{1,0:T(8,128)(2,1)S(1)}, u32[]{:S(2)}, u32[]{:S(2)}) %collective-permute-start.17) | collective-permute-done | bytes 262176 | tf_op jit(solution)/shard_map/ppermute | solution.py:105
  34.9 2.2 %collective-permute-done.9 = bf16[192,1024]{1,0:T(8,128)(2,1)S(1)} collective-permute-done((bf16[192,1024]{1,0:T(8,128)(2,1)S(1)}, bf16[192,1024]{1,0:T(8,128)(2,1)S(1)}, u32[]{:S(2)}, u32[]{:S(2)}) %collective-permute-start.9) | collective-permute-done | bytes 393248 | tf_op jit(solution)/shard_map/ppermute | solution.py:105
  37.1 1.5 %collective-permute-start.10 = (bf16[192,512]{1,0:T(8,128)(2,1)S(1)}, bf16[192,512]{1,0:T(8,128)(2,1)S(1)}, u32[]{:S(2)}, u32[]{:S(2)}) collective-permute-start(bf16[192,512]{1,0:T(8,128)(2,1)S(1)} %slice.324), channel_id=1, source_target_pairs={{0,16},{1,17},{2,18},{3,19},{4,20},{5,21},{6,22},{7,23},{8,24},{9,... | collective-permute-start | bytes 589832 | tf_op jit(solution)/shard_map/ppermute | solution.py:105
  39.1 3.8 %collective-permute-done.10 = bf16[192,512]{1,0:T(8,128)(2,1)S(1)} collective-permute-done((bf16[192,512]{1,0:T(8,128)(2,1)S(1)}, bf16[192,512]{1,0:T(8,128)(2,1)S(1)}, u32[]{:S(2)}, u32[]{:S(2)}) %collective-permute-start.10) | collective-permute-done | bytes 196640 | tf_op jit(solution)/shard_map/ppermute | solution.py:105
  44.8 3.8 %collective-permute-done.12 = bf16[192,512]{1,0:T(8,128)(2,1)S(1)} collective-permute-done((bf16[192,512]{1,0:T(8,128)(2,1)S(1)}, bf16[192,512]{1,0:T(8,128)(2,1)S(1)}, u32[]{:S(2)}, u32[]{:S(2)}) %collective-permute-start.12) | collective-permute-done | bytes 196640 | tf_op jit(solution)/shard_map/ppermute | solution.py:105
  50.6 1.6 %collective-permute-start.13 = (bf16[64,2048]{1,0:T(8,128)(2,1)S(1)}, bf16[64,2048]{1,0:T(8,128)(2,1)S(1)}, u32[]{:S(2)}, u32[]{:S(2)}) collective-permute-start(bf16[64,2048]{1,0:T(8,128)(2,1)S(1)} %get-tuple-element.29), channel_id=1, source_target_pairs={{0,2},{1,3},{2,0},{3,1},{4,6},{5,7},{6,4},{7,5},{8,10},{9,11},{10,... | collective-permute-start | bytes 786440 | tf_op jit(solution)/shard_map/ppermute | solution.py:105
  52.6 4.4 %collective-permute-done.13 = bf16[64,2048]{1,0:T(8,128)(2,1)S(1)} collective-permute-done((bf16[64,2048]{1,0:T(8,128)(2,1)S(1)}, bf16[64,2048]{1,0:T(8,128)(2,1)S(1)}, u32[]{:S(2)}, u32[]{:S(2)}) %collective-permute-start.13) | collective-permute-done | bytes 262176 | tf_op jit(solution)/shard_map/ppermute | solution.py:105
  57.7 1.4 %fusion.4 = bf16[384,768]{1,0:T(8,128)(2,1)S(1)} fusion(bf16[384,2048]{1,0:T(8,128)(2,1)S(1)} %constant_dynamic-update-slice_fusion, bf16[384,2048]{1,0:T(8,128)(2,1)S(1)} %bitcast.155, bf16[384,2048]{1,0:T(8,128)(2,1)S(1)} %bitcast.153), kind=kOutput, calls=%fused_computation.10 | convolution fusion | flops 1214545920 | bytes 5308416 | tf_op jit(solution)/shard_map/dot_general | solution.py:195
  59.3 1.2 %fusion.6 = bf16[128,768]{1,0:T(8,128)(2,1)S(1)} fusion(bf16[384,2048]{1,0:T(8,128)(2,1)S(1)} %bitcast.156, bf16[384,2048]{1,0:T(8,128)(2,1)S(1)} %bitcast.154, bf16[64,2048]{1,0:T(8,128)(2,1)S(1)} %collective-permute-done.18, bf16[64,2048]{1,0:T(8,128)(2,1)S(1)} %collective-permute-done.17), kind=kOutput, calls=%fused_computation.12 | convolution fusion | flops 410091520 | bytes 3866624 | tf_op jit(solution)/shard_map/dot_general | solution.py:195
  60.6 2.1 %collective-permute-start.19 = (bf16[128,384]{1,0:T(8,128)(2,1)S(1)}, bf16[128,384]{1,0:T(8,128)(2,1)S(1)}, u32[]{:S(2)}, u32[]{:S(2)}) collective-permute-start(bf16[128,384]{1,0:T(8,128)(2,1)S(1)} %get-tuple-element.34), channel_id=1, source_target_pairs={{0,4},{1,5},{2,6},{3,7},{4,0},{5,1},{6,2},{7,3},{8,12},{9,13},{10,... | collective-permute-start | bytes 294920 | tf_op jit(solution)/shard_map/ppermute | solution.py:105
  62.6 4.3 %collective-permute-done.16 = bf16[384,384]{1,0:T(8,128)(2,1)S(1)} collective-permute-done((bf16[384,384]{1,0:T(8,128)(2,1)S(1)}, bf16[384,384]{1,0:T(8,128)(2,1)S(1)}, u32[]{:S(2)}, u32[]{:S(2)}) %collective-permute-start.16) | collective-permute-done | bytes 294944 | tf_op jit(solution)/shard_map/ppermute | solution.py:105
  69.5 2.3 %fusion.61 = (f32[1024]{0:T(1024)S(1)}, f32[1024,2048]{1,0:T(8,128)S(1)}) fusion(bf16[2048,256]{1,0:T(8,128)(2,1)S(1)} %fusion.8, bf16[128,384]{1,0:T(8,128)(2,1)S(1)} %collective-permute-done.19, bf16[128,384]{1,0:T(8,128)(2,1)S(1)} %get-tuple-element.33, bf16[384,384]{1,0:T(8,128)(2,1)S(1)} %collective-permute-done.16, ...), kind=kOutput, calls=%fused_computation.184 | convolution fusion | flops 550501376 | bytes 9728000 | tf_op jit(solution)/shard_map/dot_general | solution.py:230
  71.8 1.3 %fusion = f32[1024]{0:T(1024)S(1)} fusion(f32[1024,2048]{1,0:T(8,128)S(1)} %get-tuple-element.62, f32[1024]{0:T(1024)S(1)} %get-tuple-element.61), kind=kLoop, calls=%fused_computation.3 | loop fusion | flops 4193280 | bytes 8396800 | tf_op jit(solution)/shard_map/reduce_sum | solution.py:238
  73.1 1.5 %fusion.5 = bf16[1024,128]{1,0:T(8,128)(2,1)S(1)} fusion(f32[1024,2048]{1,0:T(8,128)S(1)} %get-tuple-element.62, f32[1024]{0:T(1024)S(1)} %broadcast_divide_fusion, f32[1024]{0:T(1024)S(1)} %get-tuple-element.61, bf16[2048,256]{1,0:T(8,128)(2,1)S(1)} %fusion.8), kind=kOutput, calls=%fused_computation.11 | convolution fusion | flops 543293440 | bytes 9183232 | tf_op jit(solution)/shard_map/dot_general | solution.py:240
  74.9 12.7 %all_to_all.5 = bf16[8,128,128]{2,1,0:T(8,128)(2,1)S(1)} all-to-all(bf16[8,128,128]{2,1,0:T(8,128)(2,1)S(1)} %fusion.45), channel_id=1, replica_groups=mesh['grp'=2,'chip'=8,'core'=2] {'chip'}, dimensions={0} | all-to-all | bytes 524288 | tf_op jit(solution)/shard_map/all_to_all | solution.py:249
  (117 shorter events, 14.2 us)
Async XLA Ops:
  0.0 20.2 %slice-start = ((bf16[128,2048]{1,0:T(8,128)(2,1)}), bf16[64,2048]{1,0:T(8,128)(2,1)S(1)}, s32[]{:S(2)}) async-start(bf16[128,2048]{1,0:T(8,128)(2,1)} %param.5), calls=%async_computation.1 | async-start | bytes 524288 | tf_op jit(solution)/shard_map/slice | solution.py:137
  0.0 13.5 %copy-start.1 = (bf16[4,2048]{1,0:T(4,128)(2,1)S(1)}, bf16[4,2048]{1,0:T(4,128)(2,1)}, u32[]{:S(2)}) copy-start(bf16[4,2048]{1,0:T(4,128)(2,1)} %param.6) | copy-start | bytes 49156
  0.9 19.3 %collective-permute-start.4 = (bf16[3,2048]{1,0:T(4,128)(2,1)S(1)}, bf16[3,2048]{1,0:T(4,128)(2,1)S(1)}, u32[]{:S(2)}, u32[]{:S(2)}) collective-permute-start(bf16[3,2048]{1,0:T(4,128)(2,1)S(1)} %slice.262), channel_id=1, source_target_pairs={{0,1},{1,2},{2,3},{3,4},{4,5},{5,6},{6,7},{7,8},{8,9},{9,10},{10,1... | collective-permute-start | bytes 36872 | tf_op jit(solution)/shard_map/ppermute | solution.py:133
  4.2 17.8 %collective-permute-start.7 = (bf16[64,2048]{1,0:T(8,128)(2,1)S(1)}, bf16[64,2048]{1,0:T(8,128)(2,1)S(1)}, u32[]{:S(2)}, u32[]{:S(2)}) collective-permute-start(bf16[64,2048]{1,0:T(8,128)(2,1)S(1)} %dynamic-slice_bitcast_fusion), channel_id=1, source_target_pairs={{0,0},{1,3},{2,6},{3,9},{4,12},{5,15},{6,2},{7,5},{8,8},{9,11},{10... | collective-permute-start | bytes 786440 | tf_op jit(solution)/shard_map/ppermute | solution.py:153
  5.9 16.1 %collective-permute-start.8 = (bf16[64,1024]{1,0:T(8,128)(2,1)S(1)}, bf16[64,1024]{1,0:T(8,128)(2,1)S(1)}, u32[]{:S(2)}, u32[]{:S(2)}) collective-permute-start(bf16[64,1024]{1,0:T(8,128)(2,1)S(1)} %constant_dynamic-slice_fusion.2), channel_id=1, source_target_pairs={{0,1},{1,4},{2,7},{3,10},{4,13},{5,0},{6,3},{7,6},{8,9},{9,12},{10... | collective-permute-start | bytes 393224 | tf_op jit(solution)/shard_map/ppermute | solution.py:153
  11.8 2.3 %collective-permute-start = (s32[1,128]{1,0:T(1,128)S(1)}, s32[1,128]{1,0:T(1,128)S(1)}, u32[]{:S(2)}, u32[]{:S(2)}) collective-permute-start(s32[1,128]{1,0:T(1,128)S(1)} %bitcast.168), channel_id=1, source_target_pairs={{0,1},{1,0},{2,3},{3,2},{4,5},{5,4},{6,7},{7,6},{8,9},{9,8},{10,11... | collective-permute-start | bytes 1544 | tf_op jit(solution)/shard_map/ppermute | solution.py:105
  14.1 3.6 %collective-permute-start.1 = (s32[2,128]{1,0:T(2,128)S(1)}, s32[2,128]{1,0:T(2,128)S(1)}, u32[]{:S(2)}, u32[]{:S(2)}) collective-permute-start(s32[2,128]{1,0:T(2,128)S(1)} %pad_add_fusion.2), channel_id=1, source_target_pairs={{0,2},{1,3},{2,0},{3,1},{4,6},{5,7},{6,4},{7,5},{8,10},{9,11},{10,... | collective-permute-start | bytes 3080 | tf_op jit(solution)/shard_map/ppermute | solution.py:105
  17.7 7.3 %collective-permute-start.2 = (s32[4,128]{1,0:T(4,128)S(1)}, s32[4,128]{1,0:T(4,128)S(1)}, u32[]{:S(2)}, u32[]{:S(2)}) collective-permute-start(s32[4,128]{1,0:T(4,128)S(1)} %pad_add_fusion.1), channel_id=1, source_target_pairs={{0,4},{1,5},{2,6},{3,7},{4,0},{5,1},{6,2},{7,3},{8,12},{9,13},{10,... | collective-permute-start | bytes 6152 | tf_op jit(solution)/shard_map/ppermute | solution.py:105
  20.5 13.5 %collective-permute-start.17 = (bf16[64,2048]{1,0:T(8,128)(2,1)S(1)}, bf16[64,2048]{1,0:T(8,128)(2,1)S(1)}, u32[]{:S(2)}, u32[]{:S(2)}) collective-permute-start(bf16[64,2048]{1,0:T(8,128)(2,1)S(1)} %get-tuple-element.8), channel_id=1, source_target_pairs={{0,8},{1,9},{2,10},{3,11},{4,12},{5,13},{6,14},{7,15},{8,0},{9,1},... | collective-permute-start | bytes 786440 | tf_op jit(solution)/shard_map/ppermute | solution.py:105
  21.1 12.9 %collective-permute-start.5 = (bf16[128,2048]{1,0:T(8,128)(2,1)S(1)}, bf16[128,2048]{1,0:T(8,128)(2,1)S(1)}, u32[]{:S(2)}, u32[]{:S(2)}) collective-permute-start(bf16[128,2048]{1,0:T(8,128)(2,1)S(1)} %pad_maximum_fusion.12), channel_id=1, source_target_pairs={{0,2},{1,3},{2,0},{3,1},{4,6},{5,7},{6,4},{7,5},{8,10},{9,11},{10,... | collective-permute-start | bytes 1572872 | tf_op jit(solution)/shard_map/ppermute | solution.py:105
  22.0 15.1 %collective-permute-start.9 = (bf16[192,1024]{1,0:T(8,128)(2,1)S(1)}, bf16[192,1024]{1,0:T(8,128)(2,1)S(1)}, u32[]{:S(2)}, u32[]{:S(2)}) collective-permute-start(bf16[192,1024]{1,0:T(8,128)(2,1)S(1)} %pad_maximum_fusion.14), channel_id=1, source_target_pairs={{0,4},{1,5},{2,6},{3,7},{4,0},{5,1},{6,2},{7,3},{8,12},{9,13},{10,... | collective-permute-start | bytes 1179656 | tf_op jit(solution)/shard_map/ppermute | solution.py:105
  23.9 14.8 %collective-permute-start.11 = (bf16[192,1024]{1,0:T(8,128)(2,1)S(1)}, bf16[192,1024]{1,0:T(8,128)(2,1)S(1)}, u32[]{:S(2)}, u32[]{:S(2)}) collective-permute-start(bf16[192,1024]{1,0:T(8,128)(2,1)S(1)} %pad_maximum_fusion.14), channel_id=1, source_target_pairs={{0,16},{1,17},{2,18},{3,19},{4,20},{5,21},{6,22},{7,23},{8,24},{9,... | collective-permute-start | bytes 1179656 | tf_op jit(solution)/shard_map/ppermute | solution.py:105
  25.1 43.0 %collective-permute-start.3 = (s32[8,128]{1,0:T(8,128)S(1)}, s32[8,128]{1,0:T(8,128)S(1)}, u32[]{:S(2)}, u32[]{:S(2)}) collective-permute-start(s32[8,128]{1,0:T(8,128)S(1)} %pad_add_fusion), channel_id=1, source_target_pairs={{0,8},{1,9},{2,10},{3,11},{4,12},{5,13},{6,14},{7,15},{8,0},{9,1},... | collective-permute-start | bytes 12296 | tf_op jit(solution)/shard_map/ppermute | solution.py:105
  34.0 16.5 %collective-permute-start.6 = (bf16[64,2048]{1,0:T(8,128)(2,1)S(1)}, bf16[64,2048]{1,0:T(8,128)(2,1)S(1)}, u32[]{:S(2)}, u32[]{:S(2)}) collective-permute-start(bf16[64,2048]{1,0:T(8,128)(2,1)S(1)} %get-tuple-element.6), channel_id=1, source_target_pairs={{0,8},{1,9},{2,10},{3,11},{4,12},{5,13},{6,14},{7,15},{8,0},{9,1},... | collective-permute-start | bytes 786440 | tf_op jit(solution)/shard_map/ppermute | solution.py:105
  34.0 25.3 %collective-permute-start.18 = (bf16[64,2048]{1,0:T(8,128)(2,1)S(1)}, bf16[64,2048]{1,0:T(8,128)(2,1)S(1)}, u32[]{:S(2)}, u32[]{:S(2)}) collective-permute-start(bf16[64,2048]{1,0:T(8,128)(2,1)S(1)} %collective-permute-done.17), channel_id=1, source_target_pairs={{0,2},{1,3},{2,0},{3,1},{4,6},{5,7},{6,4},{7,5},{8,10},{9,11},{10,... | collective-permute-start | bytes 786440 | tf_op jit(solution)/shard_map/ppermute | solution.py:105
  37.1 5.7 %collective-permute-start.10 = (bf16[192,512]{1,0:T(8,128)(2,1)S(1)}, bf16[192,512]{1,0:T(8,128)(2,1)S(1)}, u32[]{:S(2)}, u32[]{:S(2)}) collective-permute-start(bf16[192,512]{1,0:T(8,128)(2,1)S(1)} %slice.324), channel_id=1, source_target_pairs={{0,16},{1,17},{2,18},{3,19},{4,20},{5,21},{6,22},{7,23},{8,24},{9,... | collective-permute-start | bytes 589832 | tf_op jit(solution)/shard_map/ppermute | solution.py:105
  38.7 9.9 %collective-permute-start.12 = (bf16[192,512]{1,0:T(8,128)(2,1)S(1)}, bf16[192,512]{1,0:T(8,128)(2,1)S(1)}, u32[]{:S(2)}, u32[]{:S(2)}) collective-permute-start(bf16[192,512]{1,0:T(8,128)(2,1)S(1)} %slice.326), channel_id=1, source_target_pairs={{0,4},{1,5},{2,6},{3,7},{4,0},{5,1},{6,2},{7,3},{8,12},{9,13},{10,... | collective-permute-start | bytes 589832 | tf_op jit(solution)/shard_map/ppermute | solution.py:105
  42.9 14.2 %collective-permute-start.14 = (bf16[3,64,2048]{2,1,0:T(8,128)(2,1)S(1)}, bf16[3,64,2048]{2,1,0:T(8,128)(2,1)S(1)}, u32[]{:S(2)}, u32[]{:S(2)}) collective-permute-start(bf16[3,64,2048]{2,1,0:T(8,128)(2,1)S(1)} %constant_dynamic-slice_fusion.1), channel_id=1, source_target_pairs={{0,1},{1,0},{2,3},{3,2},{4,5},{5,4},{6,7},{7,6},{8,9},{9,8},{10,11... | collective-permute-start | bytes 2359304 | tf_op jit(solution)/shard_map/ppermute | solution.py:105
  50.6 6.4 %collective-permute-start.13 = (bf16[64,2048]{1,0:T(8,128)(2,1)S(1)}, bf16[64,2048]{1,0:T(8,128)(2,1)S(1)}, u32[]{:S(2)}, u32[]{:S(2)}) collective-permute-start(bf16[64,2048]{1,0:T(8,128)(2,1)S(1)} %get-tuple-element.29), channel_id=1, source_target_pairs={{0,2},{1,3},{2,0},{3,1},{4,6},{5,7},{6,4},{7,5},{8,10},{9,11},{10,... | collective-permute-start | bytes 786440 | tf_op jit(solution)/shard_map/ppermute | solution.py:105
  52.5 4.8 %collective-permute-start.15 = (bf16[3,64,2048]{2,1,0:T(8,128)(2,1)S(1)}, bf16[3,64,2048]{2,1,0:T(8,128)(2,1)S(1)}, u32[]{:S(2)}, u32[]{:S(2)}) collective-permute-start(bf16[3,64,2048]{2,1,0:T(8,128)(2,1)S(1)} %constant_dynamic-slice_fusion), channel_id=1, source_target_pairs={{0,1},{1,0},{2,3},{3,2},{4,5},{5,4},{6,7},{7,6},{8,9},{9,8},{10,11... | collective-permute-start | bytes 2359304 | tf_op jit(solution)/shard_map/ppermute | solution.py:105
  59.2 7.7 %collective-permute-start.16 = (bf16[384,384]{1,0:T(8,128)(2,1)S(1)}, bf16[384,384]{1,0:T(8,128)(2,1)S(1)}, u32[]{:S(2)}, u32[]{:S(2)}) collective-permute-start(bf16[384,384]{1,0:T(8,128)(2,1)S(1)} %get-tuple-element.24), channel_id=1, source_target_pairs={{0,4},{1,5},{2,6},{3,7},{4,0},{5,1},{6,2},{7,3},{8,12},{9,13},{10,... | collective-permute-start | bytes 884744 | tf_op jit(solution)/shard_map/ppermute | solution.py:105
  60.6 7.4 %collective-permute-start.19 = (bf16[128,384]{1,0:T(8,128)(2,1)S(1)}, bf16[128,384]{1,0:T(8,128)(2,1)S(1)}, u32[]{:S(2)}, u32[]{:S(2)}) collective-permute-start(bf16[128,384]{1,0:T(8,128)(2,1)S(1)} %get-tuple-element.34), channel_id=1, source_target_pairs={{0,4},{1,5},{2,6},{3,7},{4,0},{5,1},{6,2},{7,3},{8,12},{9,13},{10,... | collective-permute-start | bytes 294920 | tf_op jit(solution)/shard_map/ppermute | solution.py:105
  67.0 2.5 %collective-permute-start.20 = (bf16[768,256]{1,0:T(8,128)(2,1)S(1)}, bf16[768,256]{1,0:T(8,128)(2,1)S(1)}, u32[]{:S(2)}, u32[]{:S(2)}) collective-permute-start(bf16[768,256]{1,0:T(8,128)(2,1)S(1)} %pad_maximum_fusion.13), channel_id=1, source_target_pairs={{0,1},{1,0},{2,3},{3,2},{4,5},{5,4},{6,7},{7,6},{8,9},{9,8},{10,11... | collective-permute-start | bytes 1179656 | tf_op jit(solution)/shard_map/ppermute | solution.py:105
  68.0 1.4 %collective-permute-start.21 = (bf16[256,256]{1,0:T(8,128)(2,1)S(1)}, bf16[256,256]{1,0:T(8,128)(2,1)S(1)}, u32[]{:S(2)}, u32[]{:S(2)}) collective-permute-start(bf16[256,256]{1,0:T(8,128)(2,1)S(1)} %pad_maximum_fusion.15), channel_id=1, source_target_pairs={{0,1},{1,0},{2,3},{3,2},{4,5},{5,4},{6,7},{7,6},{8,9},{9,8},{10,11... | collective-permute-start | bytes 393224 | tf_op jit(solution)/shard_map/ppermute | solution.py:105
  (1 other events, 13.3 us)

commit v26 on v25

--- a/solution.py
+++ b/solution.py
@@ -206,9 +206,10 @@
     for pieces in (first_rows, second_rows):
         order += pieces + [(far ^ Z0, start, count) for far, start, count in pieces]
 
-    groups = track_groups(track_ids, track_owner)[None, :]
+    groups = track_ids[None, :]
     for bit in (CORE, Y, Z0, Z1):
         groups = jnp.concatenate([groups, xor_swap(groups, bit)], axis=0)
+    groups = track_groups(groups.reshape(-1), track_owner).reshape(groups.shape)
 
     def of_rows(bit):
         times = [

time: 88.9 us -> 94.8 us (1.066)
  other arithmetic: 3.91 us -> 6.55 us
  waiting for transfers between devices: 30.4 us -> 31.7 us
    add x13, other arithmetic: 0.06 us -> 3.32 us  [of_rows(): (me ^ far ^ bit) * tok_rows + start + jnp.arange(count, dtype=jnp.int32)]
    ppermute x19, waiting for transfers between devices: 30.4 us -> 31.7 us  [xor_swap(): return lax.ppermute(value, axes, [(d, d ^ bit) for d in range(count)])]
    dot_general x2, matrix products: 2.61 us -> 3.57 us  [project(): lax.dot_general(rows, two_heads, (((1,), (1,)), ((), ())), preferred_elem...]
  transfers between devices with their start and end apart: 22 -> 22, of which waited for: 10 -> 9; matrix products, arithmetic and copies ran while one was open for 10% -> 14% of each run, Pallas kernels for 0% -> 0%
where the time goes in v26:
time: 94.8 us; the launch traced here: 94.5 us
  waiting for transfers between devices  31.7 us (33%)
  starting transfers between devices  25.9 us (27%)
  blocking collectives  12.4 us (13%)
  matrix products  7.43 us (8%)
  local copies, waits for them, and re-layouts  7.05 us (7%)
  other arithmetic  6.55 us (7%)
  between operations  3.41 us (4%)
    ppermute x19, waiting for transfers between devices, xor_swap(): return lax.ppermute(value, axes, [(d, d ^ bit) for d in range(count)])  31.7 us
    ppermute x19, starting transfers between devices, xor_swap(): return lax.ppermute(value, axes, [(d, d ^ bit) for d in range(count)])  17.7 us
    all_to_all x1, blocking collectives, body_by_head(): lax.all_to_all(sent, 'chip', split_axis=0, concat_axis=0, tiled=True)  12.4 us
    ppermute x2, starting transfers between devices, to_heads(): return lax.ppermute(block, every, pairs)  5.83 us
    dot_general x2, matrix products, project(): lax.dot_general(rows, two_heads, (((1,), (1,)), ((), ())), preferred_elem...  3.57 us
    add x13, other arithmetic, of_rows(): (me ^ far ^ bit) * tok_rows + start + jnp.arange(count, dtype=jnp.int32)  3.32 us
    ppermute x1, starting transfers between devices, body_by_head(): lax.ppermute(frames[tok_rows - (KW - 1):], both, [(i, i + 1) for i in ran...  2.36 us
    dot_general x1, matrix products, body_by_head(): lax.dot_general(query, keyed[:, :HD], (((1,), (1,)), ((), ())), preferred...  2.33 us
  transfers between devices with their start and end apart: 22, of which 9 were waited for; matrix products, arithmetic and copies ran while one was open for 14% of the time, Pallas kernels for 0%

profile of v26, /device:TPU:0, one launch (start us, length us, event | category | flops | bytes accessed | tf_op | source)
XLA Modules:
  0.0 94.5 jit_solution(1241628341346225852)
XLA Ops:
  0.9 2.4 %collective-permute-start.4 = (bf16[3,2048]{1,0:T(4,128)(2,1)S(1)}, bf16[3,2048]{1,0:T(4,128)(2,1)S(1)}, u32[]{:S(2)}, u32[]{:S(2)}) collective-permute-start(bf16[3,2048]{1,0:T(4,128)(2,1)S(1)} %slice.278), channel_id=1, source_target_pairs={{0,1},{1,2},{2,3},{3,4},{4,5},{5,6},{6,7},{7,8},{8,9},{9,10},{10,1... | collective-permute-start | bytes 36872 | tf_op jit(solution)/shard_map/ppermute | solution.py:133
  5.9 5.2 %collective-permute-start.8 = (bf16[64,1024]{1,0:T(8,128)(2,1)S(1)}, bf16[64,1024]{1,0:T(8,128)(2,1)S(1)}, u32[]{:S(2)}, u32[]{:S(2)}) collective-permute-start(bf16[64,1024]{1,0:T(8,128)(2,1)S(1)} %constant_dynamic-slice_fusion.2), channel_id=1, source_target_pairs={{0,1},{1,4},{2,7},{3,10},{4,13},{5,0},{6,3},{7,6},{8,9},{9,12},{10... | collective-permute-start | bytes 393224 | tf_op jit(solution)/shard_map/ppermute | solution.py:153
  11.1 1.4 %collective-permute-start = (s32[1,128]{1,0:T(1,128)}, s32[1,128]{1,0:T(1,128)S(1)}, u32[]{:S(2)}, u32[]{:S(2)}) collective-permute-start(s32[1,128]{1,0:T(1,128)} %bitcast.159), channel_id=1, source_target_pairs={{0,1},{1,0},{2,3},{3,2},{4,5},{5,4},{6,7},{7,6},{8,9},{9,8},{10,11... | collective-permute-start | bytes 1544 | tf_op jit(solution)/shard_map/ppermute | solution.py:105
  15.5 1.6 %collective-permute-start.1 = (s32[2,128]{1,0:T(2,128)S(1)}, s32[2,128]{1,0:T(2,128)S(1)}, u32[]{:S(2)}, u32[]{:S(2)}) collective-permute-start(s32[2,128]{1,0:T(2,128)S(1)} %pad_add_fusion.2), channel_id=1, source_target_pairs={{0,2},{1,3},{2,0},{3,1},{4,6},{5,7},{6,4},{7,5},{8,10},{9,11},{10,... | collective-permute-start | bytes 3080 | tf_op jit(solution)/shard_map/ppermute | solution.py:105
  17.6 1.5 %collective-permute-done.1 = s32[2,128]{1,0:T(2,128)S(1)} collective-permute-done((s32[2,128]{1,0:T(2,128)S(1)}, s32[2,128]{1,0:T(2,128)S(1)}, u32[]{:S(2)}, u32[]{:S(2)}) %collective-permute-start.1) | collective-permute-done | bytes 1056 | tf_op jit(solution)/shard_map/ppermute | solution.py:105
  19.1 2.2 %collective-permute-start.2 = (s32[4,128]{1,0:T(4,128)S(1)}, s32[4,128]{1,0:T(4,128)S(1)}, u32[]{:S(2)}, u32[]{:S(2)}) collective-permute-start(s32[4,128]{1,0:T(4,128)S(1)} %pad_add_fusion.1), channel_id=1, source_target_pairs={{0,4},{1,5},{2,6},{3,7},{4,0},{5,1},{6,2},{7,3},{8,12},{9,13},{10,... | collective-permute-start | bytes 6152 | tf_op jit(solution)/shard_map/ppermute | solution.py:105
  21.3 1.6 %collective-permute-done.2 = s32[4,128]{1,0:T(4,128)S(1)} collective-permute-done((s32[4,128]{1,0:T(4,128)S(1)}, s32[4,128]{1,0:T(4,128)S(1)}, u32[]{:S(2)}, u32[]{:S(2)}) %collective-permute-start.2) | collective-permute-done | bytes 2080 | tf_op jit(solution)/shard_map/ppermute | solution.py:105
  24.5 1.8 %collective-permute-start.17 = (bf16[64,2048]{1,0:T(8,128)(2,1)S(1)}, bf16[64,2048]{1,0:T(8,128)(2,1)}, u32[]{:S(2)}, u32[]{:S(2)}) collective-permute-start(bf16[64,2048]{1,0:T(8,128)(2,1)S(1)} %get-tuple-element.8), channel_id=1, source_target_pairs={{0,8},{1,9},{2,10},{3,11},{4,12},{5,13},{6,14},{7,15},{8,0},{9,1},... | collective-permute-start | bytes 786440 | tf_op jit(solution)/shard_map/ppermute | solution.py:105
  26.8 1.5 %collective-permute-start.5 = (bf16[128,2048]{1,0:T(8,128)(2,1)S(1)}, bf16[128,2048]{1,0:T(8,128)(2,1)S(1)}, u32[]{:S(2)}, u32[]{:S(2)}) collective-permute-start(bf16[128,2048]{1,0:T(8,128)(2,1)S(1)} %pad_maximum_fusion.12), channel_id=1, source_target_pairs={{0,2},{1,3},{2,0},{3,1},{4,6},{5,7},{6,4},{7,5},{8,10},{9,11},{10,... | collective-permute-start | bytes 1572872 | tf_op jit(solution)/shard_map/ppermute | solution.py:105
  28.3 1.3 %collective-permute-start.9 = (bf16[192,1024]{1,0:T(8,128)(2,1)S(1)}, bf16[192,1024]{1,0:T(8,128)(2,1)S(1)}, u32[]{:S(2)}, u32[]{:S(2)}) collective-permute-start(bf16[192,1024]{1,0:T(8,128)(2,1)S(1)} %pad_maximum_fusion.14), channel_id=1, source_target_pairs={{0,4},{1,5},{2,6},{3,7},{4,0},{5,1},{6,2},{7,3},{8,12},{9,13},{10,... | collective-permute-start | bytes 1179656 | tf_op jit(solution)/shard_map/ppermute | solution.py:105
  29.6 1.5 %collective-permute-start.11 = (bf16[192,1024]{1,0:T(8,128)(2,1)S(1)}, bf16[192,1024]{1,0:T(8,128)(2,1)S(1)}, u32[]{:S(2)}, u32[]{:S(2)}) collective-permute-start(bf16[192,1024]{1,0:T(8,128)(2,1)S(1)} %pad_maximum_fusion.14), channel_id=1, source_target_pairs={{0,16},{1,17},{2,18},{3,19},{4,20},{5,21},{6,22},{7,23},{8,24},{9,... | collective-permute-start | bytes 1179656 | tf_op jit(solution)/shard_map/ppermute | solution.py:105
  32.0 6.7 %collective-permute-done.17 = bf16[64,2048]{1,0:T(8,128)(2,1)} collective-permute-done((bf16[64,2048]{1,0:T(8,128)(2,1)S(1)}, bf16[64,2048]{1,0:T(8,128)(2,1)}, u32[]{:S(2)}, u32[]{:S(2)}) %collective-permute-start.17) | collective-permute-done | bytes 262176 | tf_op jit(solution)/shard_map/ppermute | solution.py:105
  38.8 1.2 %collective-permute-start.18 = (bf16[64,2048]{1,0:T(8,128)(2,1)}, bf16[64,2048]{1,0:T(8,128)(2,1)S(1)}, u32[]{:S(2)}, u32[]{:S(2)}) collective-permute-start(bf16[64,2048]{1,0:T(8,128)(2,1)} %collective-permute-done.17), channel_id=1, source_target_pairs={{0,2},{1,3},{2,0},{3,1},{4,6},{5,7},{6,4},{7,5},{8,10},{9,11},{10,... | collective-permute-start | bytes 786440 | tf_op jit(solution)/shard_map/ppermute | solution.py:105
  40.9 7.1 %collective-permute-done.9 = bf16[192,1024]{1,0:T(8,128)(2,1)S(1)} collective-permute-done((bf16[192,1024]{1,0:T(8,128)(2,1)S(1)}, bf16[192,1024]{1,0:T(8,128)(2,1)S(1)}, u32[]{:S(2)}, u32[]{:S(2)}) %collective-permute-start.9) | collective-permute-done | bytes 393248 | tf_op jit(solution)/shard_map/ppermute | solution.py:105
  49.4 4.3 %collective-permute-done.10 = bf16[192,512]{1,0:T(8,128)(2,1)S(1)} collective-permute-done((bf16[192,512]{1,0:T(8,128)(2,1)S(1)}, bf16[192,512]{1,0:T(8,128)(2,1)S(1)}, u32[]{:S(2)}, u32[]{:S(2)}) %collective-permute-start.10) | collective-permute-done | bytes 196640 | tf_op jit(solution)/shard_map/ppermute | solution.py:105
  58.1 5.9 %collective-permute-done.13 = bf16[64,2048]{1,0:T(8,128)(2,1)S(1)} collective-permute-done((bf16[64,2048]{1,0:T(8,128)(2,1)S(1)}, bf16[64,2048]{1,0:T(8,128)(2,1)S(1)}, u32[]{:S(2)}, u32[]{:S(2)}) %collective-permute-start.13) | collective-permute-done | bytes 262176 | tf_op jit(solution)/shard_map/ppermute | solution.py:105
  64.7 1.4 %fusion.4 = bf16[384,768]{1,0:T(8,128)(2,1)S(1)} fusion(bf16[384,2048]{1,0:T(8,128)(2,1)S(1)} %constant_dynamic-update-slice_fusion, bf16[384,2048]{1,0:T(8,128)(2,1)S(1)} %bitcast.144, bf16[384,2048]{1,0:T(8,128)(2,1)S(1)} %bitcast.142), kind=kOutput, calls=%fused_computation.10 | convolution fusion | flops 1214545920 | bytes 5308416 | tf_op jit(solution)/shard_map/dot_general | solution.py:195
  66.4 2.1 %fusion.6 = bf16[128,768]{1,0:T(8,128)(2,1)S(1)} fusion(bf16[384,2048]{1,0:T(8,128)(2,1)S(1)} %bitcast.145, bf16[384,2048]{1,0:T(8,128)(2,1)S(1)} %bitcast.143, bf16[64,2048]{1,0:T(8,128)(2,1)S(1)} %collective-permute-done.18, bf16[64,2048]{1,0:T(8,128)(2,1)} %collective-permute-done.17), kind=kOutput, calls=%fused_computation.12 | convolution fusion | flops 410091520 | bytes 3866624 | tf_op jit(solution)/shard_map/dot_general | solution.py:195
  68.5 2.0 %collective-permute-start.19 = (bf16[128,384]{1,0:T(8,128)(2,1)S(1)}, bf16[128,384]{1,0:T(8,128)(2,1)S(1)}, u32[]{:S(2)}, u32[]{:S(2)}) collective-permute-start(bf16[128,384]{1,0:T(8,128)(2,1)S(1)} %get-tuple-element.34), channel_id=1, source_target_pairs={{0,4},{1,5},{2,6},{3,7},{4,0},{5,1},{6,2},{7,3},{8,12},{9,13},{10,... | collective-permute-start | bytes 294920 | tf_op jit(solution)/shard_map/ppermute | solution.py:105
  70.6 2.5 %collective-permute-done.16 = bf16[384,384]{1,0:T(8,128)(2,1)S(1)} collective-permute-done((bf16[384,384]{1,0:T(8,128)(2,1)S(1)}, bf16[384,384]{1,0:T(8,128)(2,1)S(1)}, u32[]{:S(2)}, u32[]{:S(2)}) %collective-permute-start.16) | collective-permute-done | bytes 294944 | tf_op jit(solution)/shard_map/ppermute | solution.py:105
  75.6 2.3 %fusion.62 = (f32[1024]{0:T(1024)S(1)}, f32[1024,2048]{1,0:T(8,128)S(1)}) fusion(bf16[2048,256]{1,0:T(8,128)(2,1)S(1)} %fusion.8, bf16[128,384]{1,0:T(8,128)(2,1)S(1)} %collective-permute-done.19, bf16[128,384]{1,0:T(8,128)(2,1)S(1)} %get-tuple-element.33, bf16[384,384]{1,0:T(8,128)(2,1)S(1)} %collective-permute-done.16, ...), kind=kOutput, calls=%fused_computation.179 | convolution fusion | flops 550501376 | bytes 9728000 | tf_op jit(solution)/shard_map/dot_general | solution.py:231
  78.0 1.3 %fusion = f32[1024]{0:T(1024)S(1)} fusion(f32[1024,2048]{1,0:T(8,128)S(1)} %get-tuple-element.64, f32[1024]{0:T(1024)S(1)} %get-tuple-element.63), kind=kLoop, calls=%fused_computation.3 | loop fusion | flops 4193280 | bytes 8396800 | tf_op jit(solution)/shard_map/reduce_sum | solution.py:239
  79.2 1.5 %fusion.5 = bf16[1024,128]{1,0:T(8,128)(2,1)S(1)} fusion(f32[1024,2048]{1,0:T(8,128)S(1)} %get-tuple-element.64, f32[1024]{0:T(1024)S(1)} %broadcast_divide_fusion, f32[1024]{0:T(1024)S(1)} %get-tuple-element.63, bf16[2048,256]{1,0:T(8,128)(2,1)S(1)} %fusion.8), kind=kOutput, calls=%fused_computation.11 | convolution fusion | flops 543293440 | bytes 9183232 | tf_op jit(solution)/shard_map/dot_general | solution.py:241
  81.0 12.4 %all_to_all.5 = bf16[8,128,128]{2,1,0:T(8,128)(2,1)S(1)} all-to-all(bf16[8,128,128]{2,1,0:T(8,128)(2,1)S(1)} %fusion.45), channel_id=1, replica_groups=mesh['grp'=2,'chip'=8,'core'=2] {'chip'}, dimensions={0} | all-to-all | bytes 524288 | tf_op jit(solution)/shard_map/all_to_all | solution.py:250
  (149 shorter events, 18.2 us)
Async XLA Ops:
  0.0 24.1 %slice-start = ((bf16[128,2048]{1,0:T(8,128)(2,1)}), bf16[64,2048]{1,0:T(8,128)(2,1)S(1)}, s32[]{:S(2)}) async-start(bf16[128,2048]{1,0:T(8,128)(2,1)} %param.5), calls=%async_computation.1 | async-start | bytes 524288 | tf_op jit(solution)/shard_map/slice | solution.py:137
  0.0 15.5 %copy-start.4 = (s32[128]{0:T(128)S(1)}, s32[128]{0:T(128)}, u32[]{:S(2)}) copy-start(s32[128]{0:T(128)} %param.8) | copy-start | bytes 1540
  0.9 23.2 %collective-permute-start.4 = (bf16[3,2048]{1,0:T(4,128)(2,1)S(1)}, bf16[3,2048]{1,0:T(4,128)(2,1)S(1)}, u32[]{:S(2)}, u32[]{:S(2)}) collective-permute-start(bf16[3,2048]{1,0:T(4,128)(2,1)S(1)} %slice.278), channel_id=1, source_target_pairs={{0,1},{1,2},{2,3},{3,4},{4,5},{5,6},{6,7},{7,8},{8,9},{9,10},{10,1... | collective-permute-start | bytes 36872 | tf_op jit(solution)/shard_map/ppermute | solution.py:133
  4.2 24.0 %collective-permute-start.7 = (bf16[64,2048]{1,0:T(8,128)(2,1)S(1)}, bf16[64,2048]{1,0:T(8,128)(2,1)S(1)}, u32[]{:S(2)}, u32[]{:S(2)}) collective-permute-start(bf16[64,2048]{1,0:T(8,128)(2,1)S(1)} %dynamic-slice_bitcast_fusion), channel_id=1, source_target_pairs={{0,0},{1,3},{2,6},{3,9},{4,12},{5,15},{6,2},{7,5},{8,8},{9,11},{10... | collective-permute-start | bytes 786440 | tf_op jit(solution)/shard_map/ppermute | solution.py:153
  5.9 22.4 %collective-permute-start.8 = (bf16[64,1024]{1,0:T(8,128)(2,1)S(1)}, bf16[64,1024]{1,0:T(8,128)(2,1)S(1)}, u32[]{:S(2)}, u32[]{:S(2)}) collective-permute-start(bf16[64,1024]{1,0:T(8,128)(2,1)S(1)} %constant_dynamic-slice_fusion.2), channel_id=1, source_target_pairs={{0,1},{1,4},{2,7},{3,10},{4,13},{5,0},{6,3},{7,6},{8,9},{9,12},{10... | collective-permute-start | bytes 393224 | tf_op jit(solution)/shard_map/ppermute | solution.py:153
  11.1 4.4 %collective-permute-start = (s32[1,128]{1,0:T(1,128)}, s32[1,128]{1,0:T(1,128)S(1)}, u32[]{:S(2)}, u32[]{:S(2)}) collective-permute-start(s32[1,128]{1,0:T(1,128)} %bitcast.159), channel_id=1, source_target_pairs={{0,1},{1,0},{2,3},{3,2},{4,5},{5,4},{6,7},{7,6},{8,9},{9,8},{10,11... | collective-permute-start | bytes 1544 | tf_op jit(solution)/shard_map/ppermute | solution.py:105
  15.5 3.6 %collective-permute-start.1 = (s32[2,128]{1,0:T(2,128)S(1)}, s32[2,128]{1,0:T(2,128)S(1)}, u32[]{:S(2)}, u32[]{:S(2)}) collective-permute-start(s32[2,128]{1,0:T(2,128)S(1)} %pad_add_fusion.2), channel_id=1, source_target_pairs={{0,2},{1,3},{2,0},{3,1},{4,6},{5,7},{6,4},{7,5},{8,10},{9,11},{10,... | collective-permute-start | bytes 3080 | tf_op jit(solution)/shard_map/ppermute | solution.py:105
  19.1 3.8 %collective-permute-start.2 = (s32[4,128]{1,0:T(4,128)S(1)}, s32[4,128]{1,0:T(4,128)S(1)}, u32[]{:S(2)}, u32[]{:S(2)}) collective-permute-start(s32[4,128]{1,0:T(4,128)S(1)} %pad_add_fusion.1), channel_id=1, source_target_pairs={{0,4},{1,5},{2,6},{3,7},{4,0},{5,1},{6,2},{7,3},{8,12},{9,13},{10,... | collective-permute-start | bytes 6152 | tf_op jit(solution)/shard_map/ppermute | solution.py:105
  22.9 8.5 %collective-permute-start.3 = (s32[8,128]{1,0:T(8,128)S(1)}, s32[8,128]{1,0:T(8,128)S(1)}, u32[]{:S(2)}, u32[]{:S(2)}) collective-permute-start(s32[8,128]{1,0:T(8,128)S(1)} %pad_add_fusion), channel_id=1, source_target_pairs={{0,8},{1,9},{2,10},{3,11},{4,12},{5,13},{6,14},{7,15},{8,0},{9,1},... | collective-permute-start | bytes 12296 | tf_op jit(solution)/shard_map/ppermute | solution.py:105
  24.5 14.3 %collective-permute-start.17 = (bf16[64,2048]{1,0:T(8,128)(2,1)S(1)}, bf16[64,2048]{1,0:T(8,128)(2,1)}, u32[]{:S(2)}, u32[]{:S(2)}) collective-permute-start(bf16[64,2048]{1,0:T(8,128)(2,1)S(1)} %get-tuple-element.8), channel_id=1, source_target_pairs={{0,8},{1,9},{2,10},{3,11},{4,12},{5,13},{6,14},{7,15},{8,0},{9,1},... | collective-permute-start | bytes 786440 | tf_op jit(solution)/shard_map/ppermute | solution.py:105
  26.8 13.2 %collective-permute-start.5 = (bf16[128,2048]{1,0:T(8,128)(2,1)S(1)}, bf16[128,2048]{1,0:T(8,128)(2,1)S(1)}, u32[]{:S(2)}, u32[]{:S(2)}) collective-permute-start(bf16[128,2048]{1,0:T(8,128)(2,1)S(1)} %pad_maximum_fusion.12), channel_id=1, source_target_pairs={{0,2},{1,3},{2,0},{3,1},{4,6},{5,7},{6,4},{7,5},{8,10},{9,11},{10,... | collective-permute-start | bytes 1572872 | tf_op jit(solution)/shard_map/ppermute | solution.py:105
  28.3 19.6 %collective-permute-start.9 = (bf16[192,1024]{1,0:T(8,128)(2,1)S(1)}, bf16[192,1024]{1,0:T(8,128)(2,1)S(1)}, u32[]{:S(2)}, u32[]{:S(2)}) collective-permute-start(bf16[192,1024]{1,0:T(8,128)(2,1)S(1)} %pad_maximum_fusion.14), channel_id=1, source_target_pairs={{0,4},{1,5},{2,6},{3,7},{4,0},{5,1},{6,2},{7,3},{8,12},{9,13},{10,... | collective-permute-start | bytes 1179656 | tf_op jit(solution)/shard_map/ppermute | solution.py:105
  29.6 19.3 %collective-permute-start.11 = (bf16[192,1024]{1,0:T(8,128)(2,1)S(1)}, bf16[192,1024]{1,0:T(8,128)(2,1)S(1)}, u32[]{:S(2)}, u32[]{:S(2)}) collective-permute-start(bf16[192,1024]{1,0:T(8,128)(2,1)S(1)} %pad_maximum_fusion.14), channel_id=1, source_target_pairs={{0,16},{1,17},{2,18},{3,19},{4,20},{5,21},{6,22},{7,23},{8,24},{9,... | collective-permute-start | bytes 1179656 | tf_op jit(solution)/shard_map/ppermute | solution.py:105
  31.6 25.9 %collective-permute-start.6 = (bf16[64,2048]{1,0:T(8,128)(2,1)S(1)}, bf16[64,2048]{1,0:T(8,128)(2,1)S(1)}, u32[]{:S(2)}, u32[]{:S(2)}) collective-permute-start(bf16[64,2048]{1,0:T(8,128)(2,1)S(1)} %get-tuple-element.6), channel_id=1, source_target_pairs={{0,8},{1,9},{2,10},{3,11},{4,12},{5,13},{6,14},{7,15},{8,0},{9,1},... | collective-permute-start | bytes 786440 | tf_op jit(solution)/shard_map/ppermute | solution.py:105
  38.8 27.6 %collective-permute-start.18 = (bf16[64,2048]{1,0:T(8,128)(2,1)}, bf16[64,2048]{1,0:T(8,128)(2,1)S(1)}, u32[]{:S(2)}, u32[]{:S(2)}) collective-permute-start(bf16[64,2048]{1,0:T(8,128)(2,1)} %collective-permute-done.17), channel_id=1, source_target_pairs={{0,2},{1,3},{2,0},{3,1},{4,6},{5,7},{6,4},{7,5},{8,10},{9,11},{10,... | collective-permute-start | bytes 786440 | tf_op jit(solution)/shard_map/ppermute | solution.py:105
  48.0 5.7 %collective-permute-start.10 = (bf16[192,512]{1,0:T(8,128)(2,1)S(1)}, bf16[192,512]{1,0:T(8,128)(2,1)S(1)}, u32[]{:S(2)}, u32[]{:S(2)}) collective-permute-start(bf16[192,512]{1,0:T(8,128)(2,1)S(1)} %slice.364), channel_id=1, source_target_pairs={{0,16},{1,17},{2,18},{3,19},{4,20},{5,21},{6,22},{7,23},{8,24},{9,... | collective-permute-start | bytes 589832 | tf_op jit(solution)/shard_map/ppermute | solution.py:105
  48.9 6.6 %collective-permute-start.12 = (bf16[192,512]{1,0:T(8,128)(2,1)S(1)}, bf16[192,512]{1,0:T(8,128)(2,1)S(1)}, u32[]{:S(2)}, u32[]{:S(2)}) collective-permute-start(bf16[192,512]{1,0:T(8,128)(2,1)S(1)} %slice.366), channel_id=1, source_target_pairs={{0,4},{1,5},{2,6},{3,7},{4,0},{5,1},{6,2},{7,3},{8,12},{9,13},{10,... | collective-permute-start | bytes 589832 | tf_op jit(solution)/shard_map/ppermute | solution.py:105
  49.3 14.7 %collective-permute-start.14 = (bf16[3,64,2048]{2,1,0:T(8,128)(2,1)S(1)}, bf16[3,64,2048]{2,1,0:T(8,128)(2,1)S(1)}, u32[]{:S(2)}, u32[]{:S(2)}) collective-permute-start(bf16[3,64,2048]{2,1,0:T(8,128)(2,1)S(1)} %constant_dynamic-slice_fusion.1), channel_id=1, source_target_pairs={{0,1},{1,0},{2,3},{3,2},{4,5},{5,4},{6,7},{7,6},{8,9},{9,8},{10,11... | collective-permute-start | bytes 2359304 | tf_op jit(solution)/shard_map/ppermute | solution.py:105
  57.6 6.4 %collective-permute-start.13 = (bf16[64,2048]{1,0:T(8,128)(2,1)S(1)}, bf16[64,2048]{1,0:T(8,128)(2,1)S(1)}, u32[]{:S(2)}, u32[]{:S(2)}) collective-permute-start(bf16[64,2048]{1,0:T(8,128)(2,1)S(1)} %get-tuple-element.29), channel_id=1, source_target_pairs={{0,2},{1,3},{2,0},{3,1},{4,6},{5,7},{6,4},{7,5},{8,10},{9,11},{10,... | collective-permute-start | bytes 786440 | tf_op jit(solution)/shard_map/ppermute | solution.py:105
  58.0 6.3 %collective-permute-start.15 = (bf16[3,64,2048]{2,1,0:T(8,128)(2,1)S(1)}, bf16[3,64,2048]{2,1,0:T(8,128)(2,1)S(1)}, u32[]{:S(2)}, u32[]{:S(2)}) collective-permute-start(bf16[3,64,2048]{2,1,0:T(8,128)(2,1)S(1)} %constant_dynamic-slice_fusion), channel_id=1, source_target_pairs={{0,1},{1,0},{2,3},{3,2},{4,5},{5,4},{6,7},{7,6},{8,9},{9,8},{10,11... | collective-permute-start | bytes 2359304 | tf_op jit(solution)/shard_map/ppermute | solution.py:105
  66.2 6.8 %collective-permute-start.16 = (bf16[384,384]{1,0:T(8,128)(2,1)S(1)}, bf16[384,384]{1,0:T(8,128)(2,1)S(1)}, u32[]{:S(2)}, u32[]{:S(2)}) collective-permute-start(bf16[384,384]{1,0:T(8,128)(2,1)S(1)} %get-tuple-element.24), channel_id=1, source_target_pairs={{0,4},{1,5},{2,6},{3,7},{4,0},{5,1},{6,2},{7,3},{8,12},{9,13},{10,... | collective-permute-start | bytes 884744 | tf_op jit(solution)/shard_map/ppermute | solution.py:105
  68.5 5.6 %collective-permute-start.19 = (bf16[128,384]{1,0:T(8,128)(2,1)S(1)}, bf16[128,384]{1,0:T(8,128)(2,1)S(1)}, u32[]{:S(2)}, u32[]{:S(2)}) collective-permute-start(bf16[128,384]{1,0:T(8,128)(2,1)S(1)} %get-tuple-element.34), channel_id=1, source_target_pairs={{0,4},{1,5},{2,6},{3,7},{4,0},{5,1},{6,2},{7,3},{8,12},{9,13},{10,... | collective-permute-start | bytes 294920 | tf_op jit(solution)/shard_map/ppermute | solution.py:105
  73.1 2.5 %collective-permute-start.20 = (bf16[768,256]{1,0:T(8,128)(2,1)S(1)}, bf16[768,256]{1,0:T(8,128)(2,1)S(1)}, u32[]{:S(2)}, u32[]{:S(2)}) collective-permute-start(bf16[768,256]{1,0:T(8,128)(2,1)S(1)} %pad_maximum_fusion.13), channel_id=1, source_target_pairs={{0,1},{1,0},{2,3},{3,2},{4,5},{5,4},{6,7},{7,6},{8,9},{9,8},{10,11... | collective-permute-start | bytes 1179656 | tf_op jit(solution)/shard_map/ppermute | solution.py:105
  74.1 1.4 %collective-permute-start.21 = (bf16[256,256]{1,0:T(8,128)(2,1)S(1)}, bf16[256,256]{1,0:T(8,128)(2,1)S(1)}, u32[]{:S(2)}, u32[]{:S(2)}) collective-permute-start(bf16[256,256]{1,0:T(8,128)(2,1)S(1)} %pad_maximum_fusion.15), channel_id=1, source_target_pairs={{0,1},{1,0},{2,3},{3,2},{4,5},{5,4},{6,7},{7,6},{8,9},{9,8},{10,11... | collective-permute-start | bytes 393224 | tf_op jit(solution)/shard_map/ppermute | solution.py:105
  (17 other events, 99.6 us)

commit v27 on v25

--- a/solution.py
+++ b/solution.py
@@ -197,8 +197,8 @@
         ).astype(jnp.bfloat16)
         return jnp.concatenate([done[:, : 3 * HD], xor_swap(done[:, 3 * HD :], Z0)], axis=0)
 
-    first = project(jnp.concatenate([own, beside, far_late, far_beside_late], axis=0))
     second = project(jnp.concatenate([far_early, far_beside_early], axis=0))
+    first = project(jnp.concatenate([own, beside, far_late, far_beside_late + zero_after(second[:part])], axis=0))
 
     first_rows = [(0, 0, tok_rows), (Y, 0, tok_rows), (Z1, part, part), (Z1 | Y, part, part)]
     second_rows = [(Z1, 0, part), (Z1 | Y, 0, part)]

time: 88.9 us -> 101 us (1.14)
  waiting for transfers between devices: 30.4 us -> 41.9 us
  between operations: 3.42 us -> 4.72 us
  starting transfers between devices: 25.6 us -> 24.4 us
    ppermute x19, waiting for transfers between devices: 30.4 us -> 41.9 us  [xor_swap(): return lax.ppermute(value, axes, [(d, d ^ bit) for d in range(count)])]
    ppermute x1, starting transfers between devices: 2.36 us -> 5.11 us  [body_by_head(): lax.ppermute(frames[tok_rows - (KW - 1):], both, [(i, i + 1) for i in ran...]
    ppermute x19, starting transfers between devices: 17.4 us -> 14.8 us  [xor_swap(): return lax.ppermute(value, axes, [(d, d ^ bit) for d in range(count)])]
    ppermute x2, starting transfers between devices: 5.83 us -> 4.48 us  [to_heads(): return lax.ppermute(block, every, pairs)]
  transfers between devices with their start and end apart: 22 -> 22, of which waited for: 10 -> 11; matrix products, arithmetic and copies ran while one was open for 10% -> 10% of each run, Pallas kernels for 0% -> 0%
where the time goes in v27:
time: 101 us; the launch traced here: 100 us
  waiting for transfers between devices  41.9 us (41%)
  starting transfers between devices  24.4 us (24%)
  blocking collectives  12.1 us (12%)
  local copies, waits for them, and re-layouts  6.75 us (7%)
  matrix products  6.49 us (6%)
  between operations  4.72 us (5%)
  other arithmetic  3.94 us (4%)
    ppermute x19, waiting for transfers between devices, xor_swap(): return lax.ppermute(value, axes, [(d, d ^ bit) for d in range(count)])  41.9 us
    ppermute x19, starting transfers between devices, xor_swap(): return lax.ppermute(value, axes, [(d, d ^ bit) for d in range(count)])  14.8 us
    all_to_all x1, blocking collectives, body_by_head(): lax.all_to_all(sent, 'chip', split_axis=0, concat_axis=0, tiled=True)  12.1 us
    ppermute x1, starting transfers between devices, body_by_head(): lax.ppermute(frames[tok_rows - (KW - 1):], both, [(i, i + 1) for i in ran...  5.11 us
    ppermute x2, starting transfers between devices, to_heads(): return lax.ppermute(block, every, pairs)  4.48 us
    dot_general x2, matrix products, project(): lax.dot_general(rows, two_heads, (((1,), (1,)), ((), ())), preferred_elem...  2.62 us
    dot_general x1, matrix products, body_by_head(): lax.dot_general(query, keyed[:, :HD], (((1,), (1,)), ((), ())), preferred...  2.34 us
  transfers between devices with their start and end apart: 22, of which 11 were waited for; matrix products, arithmetic and copies ran while one was open for 10% of the time, Pallas kernels for 0%

profile of v27, /device:TPU:0, one launch (start us, length us, event | category | flops | bytes accessed | tf_op | source)
XLA Modules:
  0.0 100.3 jit_solution(14401173920277453574)
XLA Ops:
  0.0 1.1 %dynamic-slice_bitcast_fusion = bf16[64,2048]{1,0:T(8,128)(2,1)S(1)} fusion(bf16[3,64,2048]{2,1,0:T(8,128)(2,1)} %bitcast.157, s32[]{:T(128)S(6)} %select_n.137), kind=kLoop, calls=%fused_computation.67 | loop fusion | bytes 524292 | tf_op jit(solution)/shard_map/jit(dynamic_index_in_dim)/squeeze | solution.py:155
  2.8 3.8 %collective-permute-start.8 = (bf16[64,1024]{1,0:T(8,128)(2,1)S(1)}, bf16[64,1024]{1,0:T(8,128)(2,1)S(1)}, u32[]{:S(2)}, u32[]{:S(2)}) collective-permute-start(bf16[64,1024]{1,0:T(8,128)(2,1)S(1)} %constant_dynamic-slice_fusion.2), channel_id=1, source_target_pairs={{0,1},{1,4},{2,7},{3,10},{4,13},{5,0},{6,3},{7,6},{8,9},{9,12},{10... | collective-permute-start | bytes 393224 | tf_op jit(solution)/shard_map/ppermute | solution.py:153
  7.3 5.1 %collective-permute-start.4 = (bf16[3,2048]{1,0:T(4,128)(2,1)S(1)}, bf16[3,2048]{1,0:T(4,128)(2,1)S(1)}, u32[]{:S(2)}, u32[]{:S(2)}) collective-permute-start(bf16[3,2048]{1,0:T(4,128)(2,1)S(1)} %slice.268), channel_id=1, source_target_pairs={{0,1},{1,2},{2,3},{3,4},{4,5},{5,6},{6,7},{7,8},{8,9},{9,10},{10,1... | collective-permute-start | bytes 36872 | tf_op jit(solution)/shard_map/ppermute | solution.py:133
  14.4 1.6 %collective-permute-start.1 = (s32[2,128]{1,0:T(2,128)S(1)}, s32[2,128]{1,0:T(2,128)S(1)}, u32[]{:S(2)}, u32[]{:S(2)}) collective-permute-start(s32[2,128]{1,0:T(2,128)S(1)} %pad_add_fusion.2), channel_id=1, source_target_pairs={{0,2},{1,3},{2,0},{3,1},{4,6},{5,7},{6,4},{7,5},{8,10},{9,11},{10,... | collective-permute-start | bytes 3080 | tf_op jit(solution)/shard_map/ppermute | solution.py:105
  16.2 1.8 %collective-permute-done.1 = s32[2,128]{1,0:T(2,128)S(1)} collective-permute-done((s32[2,128]{1,0:T(2,128)S(1)}, s32[2,128]{1,0:T(2,128)S(1)}, u32[]{:S(2)}, u32[]{:S(2)}) %collective-permute-start.1) | collective-permute-done | bytes 1056 | tf_op jit(solution)/shard_map/ppermute | solution.py:105
  18.3 2.2 %collective-permute-start.14 = (bf16[64,2048]{1,0:T(8,128)(2,1)S(1)}, bf16[64,2048]{1,0:T(8,128)(2,1)S(1)}, u32[]{:S(2)}, u32[]{:S(2)}) collective-permute-start(bf16[64,2048]{1,0:T(8,128)(2,1)S(1)} %get-tuple-element.8), channel_id=1, source_target_pairs={{0,8},{1,9},{2,10},{3,11},{4,12},{5,13},{6,14},{7,15},{8,0},{9,1},... | collective-permute-start | bytes 786440 | tf_op jit(solution)/shard_map/ppermute | solution.py:105
  21.6 2.6 %collective-permute-start.6 = (bf16[64,2048]{1,0:T(8,128)(2,1)S(1)}, bf16[64,2048]{1,0:T(8,128)(2,1)S(1)}, u32[]{:S(2)}, u32[]{:S(2)}) collective-permute-start(bf16[64,2048]{1,0:T(8,128)(2,1)S(1)} %get-tuple-element.6), channel_id=1, source_target_pairs={{0,8},{1,9},{2,10},{3,11},{4,12},{5,13},{6,14},{7,15},{8,0},{9,1},... | collective-permute-start | bytes 786440 | tf_op jit(solution)/shard_map/ppermute | solution.py:105
  24.3 1.2 %collective-permute-start.5 = (bf16[128,2048]{1,0:T(8,128)(2,1)S(1)}, bf16[128,2048]{1,0:T(8,128)(2,1)S(1)}, u32[]{:S(2)}, u32[]{:S(2)}) collective-permute-start(bf16[128,2048]{1,0:T(8,128)(2,1)S(1)} %pad_maximum_fusion.12), channel_id=1, source_target_pairs={{0,2},{1,3},{2,0},{3,1},{4,6},{5,7},{6,4},{7,5},{8,10},{9,11},{10,... | collective-permute-start | bytes 1572872 | tf_op jit(solution)/shard_map/ppermute | solution.py:105
  25.5 5.3 %collective-permute-done.11 = bf16[192,1024]{1,0:T(8,128)(2,1)S(1)} collective-permute-done((bf16[192,1024]{1,0:T(8,128)(2,1)S(1)}, bf16[192,1024]{1,0:T(8,128)(2,1)S(1)}, u32[]{:S(2)}, u32[]{:S(2)}) %collective-permute-start.11) | collective-permute-done | bytes 393248 | tf_op jit(solution)/shard_map/ppermute | solution.py:105
  31.1 16.2 %collective-permute-done.9 = bf16[192,1024]{1,0:T(8,128)(2,1)S(1)} collective-permute-done((bf16[192,1024]{1,0:T(8,128)(2,1)S(1)}, bf16[192,1024]{1,0:T(8,128)(2,1)S(1)}, u32[]{:S(2)}, u32[]{:S(2)}) %collective-permute-start.9) | collective-permute-done | bytes 393248 | tf_op jit(solution)/shard_map/ppermute | solution.py:105
  47.5 5.5 %collective-permute-done.10 = bf16[192,512]{1,0:T(8,128)(2,1)S(1)} collective-permute-done((bf16[192,512]{1,0:T(8,128)(2,1)S(1)}, bf16[192,512]{1,0:T(8,128)(2,1)S(1)}, u32[]{:S(2)}, u32[]{:S(2)}) %collective-permute-start.10) | collective-permute-done | bytes 196640 | tf_op jit(solution)/shard_map/ppermute | solution.py:105
  54.0 1.4 %collective-permute-start.15 = (bf16[64,2048]{1,0:T(8,128)(2,1)S(1)}, bf16[64,2048]{1,0:T(8,128)(2,1)S(1)}, u32[]{:S(2)}, u32[]{:S(2)}) collective-permute-start(bf16[64,2048]{1,0:T(8,128)(2,1)S(1)} %collective-permute-done.14), channel_id=1, source_target_pairs={{0,2},{1,3},{2,0},{3,1},{4,6},{5,7},{6,4},{7,5},{8,10},{9,11},{10,... | collective-permute-start | bytes 786440 | tf_op jit(solution)/shard_map/ppermute | solution.py:105
  60.8 2.1 %collective-permute-done.15 = bf16[64,2048]{1,0:T(8,128)(2,1)S(1)} collective-permute-done((bf16[64,2048]{1,0:T(8,128)(2,1)S(1)}, bf16[64,2048]{1,0:T(8,128)(2,1)S(1)}, u32[]{:S(2)}, u32[]{:S(2)}) %collective-permute-start.15) | collective-permute-done | bytes 262176 | tf_op jit(solution)/shard_map/ppermute | solution.py:105
  62.9 1.2 %fusion.6 = bf16[128,768]{1,0:T(8,128)(2,1)S(1)} fusion(bf16[384,2048]{1,0:T(8,128)(2,1)S(1)} %bitcast.154, bf16[384,2048]{1,0:T(8,128)(2,1)S(1)} %bitcast.152, bf16[64,2048]{1,0:T(8,128)(2,1)S(1)} %collective-permute-done.15, bf16[64,2048]{1,0:T(8,128)(2,1)S(1)} %collective-permute-done.14), kind=kOutput, calls=%fused_computation.12 | convolution fusion | flops 410091520 | bytes 3866624 | tf_op jit(solution)/shard_map/dot_general | solution.py:195
  66.0 2.0 %collective-permute-done.13 = bf16[64,2048]{1,0:T(8,128)(2,1)S(1)} collective-permute-done((bf16[64,2048]{1,0:T(8,128)(2,1)S(1)}, bf16[64,2048]{1,0:T(8,128)(2,1)S(1)}, u32[]{:S(2)}, u32[]{:S(2)}) %collective-permute-start.13) | collective-permute-done | bytes 262176 | tf_op jit(solution)/shard_map/ppermute | solution.py:105
  68.0 1.4 %fusion.4 = bf16[384,768]{1,0:T(8,128)(2,1)S(1)} fusion(bf16[384,2048]{1,0:T(8,128)(2,1)S(1)} %add_dynamic-update-slice_fusion, bf16[384,2048]{1,0:T(8,128)(2,1)S(1)} %bitcast.155, bf16[384,2048]{1,0:T(8,128)(2,1)S(1)} %bitcast.153), kind=kOutput, calls=%fused_computation.10 | convolution fusion | flops 1214545920 | bytes 5308416 | tf_op jit(solution)/shard_map/dot_general | solution.py:195
  69.5 1.7 %collective-permute-start.18 = (bf16[384,384]{1,0:T(8,128)(2,1)S(1)}, bf16[384,384]{1,0:T(8,128)(2,1)S(1)}, u32[]{:S(2)}, u32[]{:S(2)}) collective-permute-start(bf16[384,384]{1,0:T(8,128)(2,1)S(1)} %get-tuple-element.24), channel_id=1, source_target_pairs={{0,4},{1,5},{2,6},{3,7},{4,0},{5,1},{6,2},{7,3},{8,12},{9,13},{10,... | collective-permute-start | bytes 884744 | tf_op jit(solution)/shard_map/ppermute | solution.py:105
  71.4 1.5 %collective-permute-start.19 = (bf16[128,384]{1,0:T(8,128)(2,1)S(1)}, bf16[128,384]{1,0:T(8,128)(2,1)S(1)}, u32[]{:S(2)}, u32[]{:S(2)}) collective-permute-start(bf16[128,384]{1,0:T(8,128)(2,1)S(1)} %get-tuple-element.34), channel_id=1, source_target_pairs={{0,4},{1,5},{2,6},{3,7},{4,0},{5,1},{6,2},{7,3},{8,12},{9,13},{10,... | collective-permute-start | bytes 294920 | tf_op jit(solution)/shard_map/ppermute | solution.py:105
  72.9 6.3 %collective-permute-done.18 = bf16[384,384]{1,0:T(8,128)(2,1)S(1)} collective-permute-done((bf16[384,384]{1,0:T(8,128)(2,1)S(1)}, bf16[384,384]{1,0:T(8,128)(2,1)S(1)}, u32[]{:S(2)}, u32[]{:S(2)}) %collective-permute-start.18) | collective-permute-done | bytes 294944 | tf_op jit(solution)/shard_map/ppermute | solution.py:105
  80.6 1.1 %collective-permute-done.21 = bf16[256,256]{1,0:T(8,128)(2,1)S(1)} collective-permute-done((bf16[256,256]{1,0:T(8,128)(2,1)S(1)}, bf16[256,256]{1,0:T(8,128)(2,1)S(1)}, u32[]{:S(2)}, u32[]{:S(2)}) %collective-permute-start.21) | collective-permute-done | bytes 131104 | tf_op jit(solution)/shard_map/ppermute | solution.py:105
  81.7 2.3 %fusion.61 = (f32[1024]{0:T(1024)S(1)}, f32[1024,2048]{1,0:T(8,128)S(1)}) fusion(bf16[2048,256]{1,0:T(8,128)(2,1)S(1)} %fusion.8, bf16[128,384]{1,0:T(8,128)(2,1)S(1)} %collective-permute-done.19, bf16[128,384]{1,0:T(8,128)(2,1)S(1)} %get-tuple-element.33, bf16[384,384]{1,0:T(8,128)(2,1)S(1)} %collective-permute-done.18, ...), kind=kOutput, calls=%fused_computation.184 | convolution fusion | flops 550501376 | bytes 9728000 | tf_op jit(solution)/shard_map/dot_general | solution.py:230
  84.1 1.3 %fusion = f32[1024]{0:T(1024)S(1)} fusion(f32[1024,2048]{1,0:T(8,128)S(1)} %get-tuple-element.62, f32[1024]{0:T(1024)S(1)} %get-tuple-element.61), kind=kLoop, calls=%fused_computation.3 | loop fusion | flops 4193280 | bytes 8396800 | tf_op jit(solution)/shard_map/reduce_sum | solution.py:238
  85.3 1.5 %fusion.5 = bf16[1024,128]{1,0:T(8,128)(2,1)S(1)} fusion(f32[1024,2048]{1,0:T(8,128)S(1)} %get-tuple-element.62, f32[1024]{0:T(1024)S(1)} %broadcast_divide_fusion, f32[1024]{0:T(1024)S(1)} %get-tuple-element.61, bf16[2048,256]{1,0:T(8,128)(2,1)S(1)} %fusion.8), kind=kOutput, calls=%fused_computation.11 | convolution fusion | flops 543293440 | bytes 9183232 | tf_op jit(solution)/shard_map/dot_general | solution.py:240
  87.2 12.1 %all_to_all.5 = bf16[8,128,128]{2,1,0:T(8,128)(2,1)S(1)} all-to-all(bf16[8,128,128]{2,1,0:T(8,128)(2,1)S(1)} %fusion.45), channel_id=1, replica_groups=mesh['grp'=2,'chip'=8,'core'=2] {'chip'}, dimensions={0} | all-to-all | bytes 524288 | tf_op jit(solution)/shard_map/all_to_all | solution.py:249
  (118 shorter events, 13.2 us)
Async XLA Ops:
  0.0 18.0 %slice-start = ((bf16[128,2048]{1,0:T(8,128)(2,1)}), bf16[64,2048]{1,0:T(8,128)(2,1)S(1)}, s32[]{:S(2)}) async-start(bf16[128,2048]{1,0:T(8,128)(2,1)} %param.5), calls=%async_computation.1 | async-start | bytes 524288 | tf_op jit(solution)/shard_map/slice | solution.py:137
  0.0 13.5 %copy-start.1 = (bf16[4,2048]{1,0:T(4,128)(2,1)S(1)}, bf16[4,2048]{1,0:T(4,128)(2,1)}, u32[]{:S(2)}) copy-start(bf16[4,2048]{1,0:T(4,128)(2,1)} %param.6) | copy-start | bytes 49156
  1.1 19.5 %collective-permute-start.7 = (bf16[64,2048]{1,0:T(8,128)(2,1)S(1)}, bf16[64,2048]{1,0:T(8,128)(2,1)S(1)}, u32[]{:S(2)}, u32[]{:S(2)}) collective-permute-start(bf16[64,2048]{1,0:T(8,128)(2,1)S(1)} %dynamic-slice_bitcast_fusion), channel_id=1, source_target_pairs={{0,0},{1,3},{2,6},{3,9},{4,12},{5,15},{6,2},{7,5},{8,8},{9,11},{10... | collective-permute-start | bytes 786440 | tf_op jit(solution)/shard_map/ppermute | solution.py:153
  2.8 17.9 %collective-permute-start.8 = (bf16[64,1024]{1,0:T(8,128)(2,1)S(1)}, bf16[64,1024]{1,0:T(8,128)(2,1)S(1)}, u32[]{:S(2)}, u32[]{:S(2)}) collective-permute-start(bf16[64,1024]{1,0:T(8,128)(2,1)S(1)} %constant_dynamic-slice_fusion.2), channel_id=1, source_target_pairs={{0,1},{1,4},{2,7},{3,10},{4,13},{5,0},{6,3},{7,6},{8,9},{9,12},{10... | collective-permute-start | bytes 393224 | tf_op jit(solution)/shard_map/ppermute | solution.py:153
  7.3 10.7 %collective-permute-start.4 = (bf16[3,2048]{1,0:T(4,128)(2,1)S(1)}, bf16[3,2048]{1,0:T(4,128)(2,1)S(1)}, u32[]{:S(2)}, u32[]{:S(2)}) collective-permute-start(bf16[3,2048]{1,0:T(4,128)(2,1)S(1)} %slice.268), channel_id=1, source_target_pairs={{0,1},{1,2},{2,3},{3,4},{4,5},{5,6},{6,7},{7,8},{8,9},{9,10},{10,1... | collective-permute-start | bytes 36872 | tf_op jit(solution)/shard_map/ppermute | solution.py:133
  13.2 1.2 %collective-permute-start = (s32[1,128]{1,0:T(1,128)S(1)}, s32[1,128]{1,0:T(1,128)S(1)}, u32[]{:S(2)}, u32[]{:S(2)}) collective-permute-start(s32[1,128]{1,0:T(1,128)S(1)} %bitcast.167), channel_id=1, source_target_pairs={{0,1},{1,0},{2,3},{3,2},{4,5},{5,4},{6,7},{7,6},{8,9},{9,8},{10,11... | collective-permute-start | bytes 1544 | tf_op jit(solution)/shard_map/ppermute | solution.py:105
  14.4 3.6 %collective-permute-start.1 = (s32[2,128]{1,0:T(2,128)S(1)}, s32[2,128]{1,0:T(2,128)S(1)}, u32[]{:S(2)}, u32[]{:S(2)}) collective-permute-start(s32[2,128]{1,0:T(2,128)S(1)} %pad_add_fusion.2), channel_id=1, source_target_pairs={{0,2},{1,3},{2,0},{3,1},{4,6},{5,7},{6,4},{7,5},{8,10},{9,11},{10,... | collective-permute-start | bytes 3080 | tf_op jit(solution)/shard_map/ppermute | solution.py:105
  18.3 35.6 %collective-permute-start.14 = (bf16[64,2048]{1,0:T(8,128)(2,1)S(1)}, bf16[64,2048]{1,0:T(8,128)(2,1)S(1)}, u32[]{:S(2)}, u32[]{:S(2)}) collective-permute-start(bf16[64,2048]{1,0:T(8,128)(2,1)S(1)} %get-tuple-element.8), channel_id=1, source_target_pairs={{0,8},{1,9},{2,10},{3,11},{4,12},{5,13},{6,14},{7,15},{8,0},{9,1},... | collective-permute-start | bytes 786440 | tf_op jit(solution)/shard_map/ppermute | solution.py:105
  20.7 10.2 %collective-permute-start.11 = (bf16[192,1024]{1,0:T(8,128)(2,1)S(1)}, bf16[192,1024]{1,0:T(8,128)(2,1)S(1)}, u32[]{:S(2)}, u32[]{:S(2)}) collective-permute-start(bf16[192,1024]{1,0:T(8,128)(2,1)S(1)} %pad_maximum_fusion.14), channel_id=1, source_target_pairs={{0,16},{1,17},{2,18},{3,19},{4,20},{5,21},{6,22},{7,23},{8,24},{9,... | collective-permute-start | bytes 1179656 | tf_op jit(solution)/shard_map/ppermute | solution.py:105
  21.6 37.6 %collective-permute-start.6 = (bf16[64,2048]{1,0:T(8,128)(2,1)S(1)}, bf16[64,2048]{1,0:T(8,128)(2,1)S(1)}, u32[]{:S(2)}, u32[]{:S(2)}) collective-permute-start(bf16[64,2048]{1,0:T(8,128)(2,1)S(1)} %get-tuple-element.6), channel_id=1, source_target_pairs={{0,8},{1,9},{2,10},{3,11},{4,12},{5,13},{6,14},{7,15},{8,0},{9,1},... | collective-permute-start | bytes 786440 | tf_op jit(solution)/shard_map/ppermute | solution.py:105
  24.3 29.7 %collective-permute-start.5 = (bf16[128,2048]{1,0:T(8,128)(2,1)S(1)}, bf16[128,2048]{1,0:T(8,128)(2,1)S(1)}, u32[]{:S(2)}, u32[]{:S(2)}) collective-permute-start(bf16[128,2048]{1,0:T(8,128)(2,1)S(1)} %pad_maximum_fusion.12), channel_id=1, source_target_pairs={{0,2},{1,3},{2,0},{3,1},{4,6},{5,7},{6,4},{7,5},{8,10},{9,11},{10,... | collective-permute-start | bytes 1572872 | tf_op jit(solution)/shard_map/ppermute | solution.py:105
  25.5 21.7 %collective-permute-start.9 = (bf16[192,1024]{1,0:T(8,128)(2,1)S(1)}, bf16[192,1024]{1,0:T(8,128)(2,1)S(1)}, u32[]{:S(2)}, u32[]{:S(2)}) collective-permute-start(bf16[192,1024]{1,0:T(8,128)(2,1)S(1)} %pad_maximum_fusion.14), channel_id=1, source_target_pairs={{0,4},{1,5},{2,6},{3,7},{4,0},{5,1},{6,2},{7,3},{8,12},{9,13},{10,... | collective-permute-start | bytes 1179656 | tf_op jit(solution)/shard_map/ppermute | solution.py:105
  47.3 5.7 %collective-permute-start.10 = (bf16[192,512]{1,0:T(8,128)(2,1)S(1)}, bf16[192,512]{1,0:T(8,128)(2,1)S(1)}, u32[]{:S(2)}, u32[]{:S(2)}) collective-permute-start(bf16[192,512]{1,0:T(8,128)(2,1)S(1)} %slice.331), channel_id=1, source_target_pairs={{0,16},{1,17},{2,18},{3,19},{4,20},{5,21},{6,22},{7,23},{8,24},{9,... | collective-permute-start | bytes 589832 | tf_op jit(solution)/shard_map/ppermute | solution.py:105
  47.4 5.7 %collective-permute-start.12 = (bf16[192,512]{1,0:T(8,128)(2,1)S(1)}, bf16[192,512]{1,0:T(8,128)(2,1)S(1)}, u32[]{:S(2)}, u32[]{:S(2)}) collective-permute-start(bf16[192,512]{1,0:T(8,128)(2,1)S(1)} %slice.333), channel_id=1, source_target_pairs={{0,4},{1,5},{2,6},{3,7},{4,0},{5,1},{6,2},{7,3},{8,12},{9,13},{10,... | collective-permute-start | bytes 589832 | tf_op jit(solution)/shard_map/ppermute | solution.py:105
  53.0 7.1 %collective-permute-start.16 = (bf16[3,64,2048]{2,1,0:T(8,128)(2,1)S(1)}, bf16[3,64,2048]{2,1,0:T(8,128)(2,1)S(1)}, u32[]{:S(2)}, u32[]{:S(2)}) collective-permute-start(bf16[3,64,2048]{2,1,0:T(8,128)(2,1)S(1)} %constant_dynamic-slice_fusion.1), channel_id=1, source_target_pairs={{0,1},{1,0},{2,3},{3,2},{4,5},{5,4},{6,7},{7,6},{8,9},{9,8},{10,11... | collective-permute-start | bytes 2359304 | tf_op jit(solution)/shard_map/ppermute | solution.py:105
  53.4 6.7 %collective-permute-start.17 = (bf16[3,64,2048]{2,1,0:T(8,128)(2,1)S(1)}, bf16[3,64,2048]{2,1,0:T(8,128)(2,1)S(1)}, u32[]{:S(2)}, u32[]{:S(2)}) collective-permute-start(bf16[3,64,2048]{2,1,0:T(8,128)(2,1)S(1)} %constant_dynamic-slice_fusion), channel_id=1, source_target_pairs={{0,1},{1,0},{2,3},{3,2},{4,5},{5,4},{6,7},{7,6},{8,9},{9,8},{10,11... | collective-permute-start | bytes 2359304 | tf_op jit(solution)/shard_map/ppermute | solution.py:105
  53.9 17.3 %collective-permute-start.2 = (s32[4,128]{1,0:T(4,128)S(1)}, s32[4,128]{1,0:T(4,128)S(1)}, u32[]{:S(2)}, u32[]{:S(2)}) collective-permute-start(s32[4,128]{1,0:T(4,128)S(1)} %pad_add_fusion.1), channel_id=1, source_target_pairs={{0,4},{1,5},{2,6},{3,7},{4,0},{5,1},{6,2},{7,3},{8,12},{9,13},{10,... | collective-permute-start | bytes 6152 | tf_op jit(solution)/shard_map/ppermute | solution.py:105
  54.0 8.9 %collective-permute-start.15 = (bf16[64,2048]{1,0:T(8,128)(2,1)S(1)}, bf16[64,2048]{1,0:T(8,128)(2,1)S(1)}, u32[]{:S(2)}, u32[]{:S(2)}) collective-permute-start(bf16[64,2048]{1,0:T(8,128)(2,1)S(1)} %collective-permute-done.14), channel_id=1, source_target_pairs={{0,2},{1,3},{2,0},{3,1},{4,6},{5,7},{6,4},{7,5},{8,10},{9,11},{10,... | collective-permute-start | bytes 786440 | tf_op jit(solution)/shard_map/ppermute | solution.py:105
  59.3 8.7 %collective-permute-start.13 = (bf16[64,2048]{1,0:T(8,128)(2,1)S(1)}, bf16[64,2048]{1,0:T(8,128)(2,1)S(1)}, u32[]{:S(2)}, u32[]{:S(2)}) collective-permute-start(bf16[64,2048]{1,0:T(8,128)(2,1)S(1)} %get-tuple-element.29), channel_id=1, source_target_pairs={{0,2},{1,3},{2,0},{3,1},{4,6},{5,7},{6,4},{7,5},{8,10},{9,11},{10,... | collective-permute-start | bytes 786440 | tf_op jit(solution)/shard_map/ppermute | solution.py:105
  69.5 9.6 %collective-permute-start.18 = (bf16[384,384]{1,0:T(8,128)(2,1)S(1)}, bf16[384,384]{1,0:T(8,128)(2,1)S(1)}, u32[]{:S(2)}, u32[]{:S(2)}) collective-permute-start(bf16[384,384]{1,0:T(8,128)(2,1)S(1)} %get-tuple-element.24), channel_id=1, source_target_pairs={{0,4},{1,5},{2,6},{3,7},{4,0},{5,1},{6,2},{7,3},{8,12},{9,13},{10,... | collective-permute-start | bytes 884744 | tf_op jit(solution)/shard_map/ppermute | solution.py:105
  71.3 9.0 %collective-permute-start.3 = (s32[8,128]{1,0:T(8,128)S(1)}, s32[8,128]{1,0:T(8,128)S(1)}, u32[]{:S(2)}, u32[]{:S(2)}) collective-permute-start(s32[8,128]{1,0:T(8,128)S(1)} %pad_add_fusion), channel_id=1, source_target_pairs={{0,8},{1,9},{2,10},{3,11},{4,12},{5,13},{6,14},{7,15},{8,0},{9,1},... | collective-permute-start | bytes 12296 | tf_op jit(solution)/shard_map/ppermute | solution.py:105
  71.4 8.8 %collective-permute-start.19 = (bf16[128,384]{1,0:T(8,128)(2,1)S(1)}, bf16[128,384]{1,0:T(8,128)(2,1)S(1)}, u32[]{:S(2)}, u32[]{:S(2)}) collective-permute-start(bf16[128,384]{1,0:T(8,128)(2,1)S(1)} %get-tuple-element.34), channel_id=1, source_target_pairs={{0,4},{1,5},{2,6},{3,7},{4,0},{5,1},{6,2},{7,3},{8,12},{9,13},{10,... | collective-permute-start | bytes 294920 | tf_op jit(solution)/shard_map/ppermute | solution.py:105
  79.2 2.5 %collective-permute-start.20 = (bf16[768,256]{1,0:T(8,128)(2,1)S(1)}, bf16[768,256]{1,0:T(8,128)(2,1)S(1)}, u32[]{:S(2)}, u32[]{:S(2)}) collective-permute-start(bf16[768,256]{1,0:T(8,128)(2,1)S(1)} %pad_maximum_fusion.13), channel_id=1, source_target_pairs={{0,1},{1,0},{2,3},{3,2},{4,5},{5,4},{6,7},{7,6},{8,9},{9,8},{10,11... | collective-permute-start | bytes 1179656 | tf_op jit(solution)/shard_map/ppermute | solution.py:105
  80.2 1.4 %collective-permute-start.21 = (bf16[256,256]{1,0:T(8,128)(2,1)S(1)}, bf16[256,256]{1,0:T(8,128)(2,1)S(1)}, u32[]{:S(2)}, u32[]{:S(2)}) collective-permute-start(bf16[256,256]{1,0:T(8,128)(2,1)S(1)} %pad_maximum_fusion.15), channel_id=1, source_target_pairs={{0,1},{1,0},{2,3},{3,2},{4,5},{5,4},{6,7},{7,6},{8,9},{9,8},{10,11... | collective-permute-start | bytes 393224 | tf_op jit(solution)/shard_map/ppermute | solution.py:105
  (1 other events, 13.3 us)

commit v28 on v25

--- a/solution.py
+++ b/solution.py
@@ -159,7 +159,7 @@
 
     mine_too = xor_swap(mine, devices, every)
 
-    cut = half // 2
+    cut = 3 * half // 4
     fourth = [xor_swap(paired[:, :cut], devices, every), xor_swap(mine_too[:, cut:], Z0)]
 
     far_beside_late = xor_swap(far_late + zero_after(fourth[0]) + zero_after(fourth[1]), Y)

time: 88.9 us -> 95.1 us (1.070)
  waiting for transfers between devices: 30.4 us -> 35.5 us
    ppermute x19, waiting for transfers between devices: 30.4 us -> 35.5 us  [xor_swap(): return lax.ppermute(value, axes, [(d, d ^ bit) for d in range(count)])]
  transfers between devices with their start and end apart: 22 -> 22, of which waited for: 10 -> 9; matrix products, arithmetic and copies ran while one was open for 10% -> 10% of each run, Pallas kernels for 0% -> 0%
where the time goes in v28:
time: 95.1 us; the launch traced here: 94.8 us
  waiting for transfers between devices  35.5 us (37%)
  starting transfers between devices  25.8 us (27%)
  blocking collectives  13.6 us (14%)
  matrix products  6.49 us (7%)
  local copies, waits for them, and re-layouts  6.16 us (6%)
  other arithmetic  3.91 us (4%)
  between operations  3.38 us (4%)
    ppermute x19, waiting for transfers between devices, xor_swap(): return lax.ppermute(value, axes, [(d, d ^ bit) for d in range(count)])  35.5 us
    ppermute x19, starting transfers between devices, xor_swap(): return lax.ppermute(value, axes, [(d, d ^ bit) for d in range(count)])  17.6 us
    all_to_all x1, blocking collectives, body_by_head(): lax.all_to_all(sent, 'chip', split_axis=0, concat_axis=0, tiled=True)  13.6 us
    ppermute x2, starting transfers between devices, to_heads(): return lax.ppermute(block, every, pairs)  5.83 us
    dot_general x2, matrix products, project(): lax.dot_general(rows, two_heads, (((1,), (1,)), ((), ())), preferred_elem...  2.62 us
    ppermute x1, starting transfers between devices, body_by_head(): lax.ppermute(frames[tok_rows - (KW - 1):], both, [(i, i + 1) for i in ran...  2.36 us
    dot_general x1, matrix products, body_by_head(): lax.dot_general(query, keyed[:, :HD], (((1,), (1,)), ((), ())), preferred...  2.33 us
  transfers between devices with their start and end apart: 22, of which 9 were waited for; matrix products, arithmetic and copies ran while one was open for 10% of the time, Pallas kernels for 0%

profile of v28, /device:TPU:0, one launch (start us, length us, event | category | flops | bytes accessed | tf_op | source)
XLA Modules:
  0.0 94.8 jit_solution(5094912500207694305)
XLA Ops:
  0.9 2.4 %collective-permute-start.4 = (bf16[3,2048]{1,0:T(4,128)(2,1)S(1)}, bf16[3,2048]{1,0:T(4,128)(2,1)S(1)}, u32[]{:S(2)}, u32[]{:S(2)}) collective-permute-start(bf16[3,2048]{1,0:T(4,128)(2,1)S(1)} %slice.262), channel_id=1, source_target_pairs={{0,1},{1,2},{2,3},{3,4},{4,5},{5,6},{6,7},{7,8},{8,9},{9,10},{10,1... | collective-permute-start | bytes 36872 | tf_op jit(solution)/shard_map/ppermute | solution.py:133
  5.9 5.2 %collective-permute-start.8 = (bf16[64,1024]{1,0:T(8,128)(2,1)S(1)}, bf16[64,1024]{1,0:T(8,128)(2,1)S(1)}, u32[]{:S(2)}, u32[]{:S(2)}) collective-permute-start(bf16[64,1024]{1,0:T(8,128)(2,1)S(1)} %constant_dynamic-slice_fusion.2), channel_id=1, source_target_pairs={{0,1},{1,4},{2,7},{3,10},{4,13},{5,0},{6,3},{7,6},{8,9},{9,12},{10... | collective-permute-start | bytes 393224 | tf_op jit(solution)/shard_map/ppermute | solution.py:153
  11.8 1.5 %collective-permute-start = (s32[1,128]{1,0:T(1,128)S(1)}, s32[1,128]{1,0:T(1,128)S(1)}, u32[]{:S(2)}, u32[]{:S(2)}) collective-permute-start(s32[1,128]{1,0:T(1,128)S(1)} %bitcast.168), channel_id=1, source_target_pairs={{0,1},{1,0},{2,3},{3,2},{4,5},{5,4},{6,7},{7,6},{8,9},{9,8},{10,11... | collective-permute-start | bytes 1544 | tf_op jit(solution)/shard_map/ppermute | solution.py:105
  14.1 1.5 %collective-permute-start.1 = (s32[2,128]{1,0:T(2,128)S(1)}, s32[2,128]{1,0:T(2,128)S(1)}, u32[]{:S(2)}, u32[]{:S(2)}) collective-permute-start(s32[2,128]{1,0:T(2,128)S(1)} %pad_add_fusion.2), channel_id=1, source_target_pairs={{0,2},{1,3},{2,0},{3,1},{4,6},{5,7},{6,4},{7,5},{8,10},{9,11},{10,... | collective-permute-start | bytes 3080 | tf_op jit(solution)/shard_map/ppermute | solution.py:105
  15.8 1.9 %collective-permute-done.1 = s32[2,128]{1,0:T(2,128)S(1)} collective-permute-done((s32[2,128]{1,0:T(2,128)S(1)}, s32[2,128]{1,0:T(2,128)S(1)}, u32[]{:S(2)}, u32[]{:S(2)}) %collective-permute-start.1) | collective-permute-done | bytes 1056 | tf_op jit(solution)/shard_map/ppermute | solution.py:105
  17.7 2.5 %collective-permute-start.2 = (s32[4,128]{1,0:T(4,128)S(1)}, s32[4,128]{1,0:T(4,128)S(1)}, u32[]{:S(2)}, u32[]{:S(2)}) collective-permute-start(s32[4,128]{1,0:T(4,128)S(1)} %pad_add_fusion.1), channel_id=1, source_target_pairs={{0,4},{1,5},{2,6},{3,7},{4,0},{5,1},{6,2},{7,3},{8,12},{9,13},{10,... | collective-permute-start | bytes 6152 | tf_op jit(solution)/shard_map/ppermute | solution.py:105
  22.0 1.9 %collective-permute-start.9 = (bf16[192,1024]{1,0:T(8,128)(2,1)S(1)}, bf16[192,1024]{1,0:T(8,128)(2,1)S(1)}, u32[]{:S(2)}, u32[]{:S(2)}) collective-permute-start(bf16[192,1024]{1,0:T(8,128)(2,1)S(1)} %pad_maximum_fusion.14), channel_id=1, source_target_pairs={{0,4},{1,5},{2,6},{3,7},{4,0},{5,1},{6,2},{7,3},{8,12},{9,13},{10,... | collective-permute-start | bytes 1179656 | tf_op jit(solution)/shard_map/ppermute | solution.py:105
  23.9 1.1 %collective-permute-start.11 = (bf16[192,1024]{1,0:T(8,128)(2,1)S(1)}, bf16[192,1024]{1,0:T(8,128)(2,1)S(1)}, u32[]{:S(2)}, u32[]{:S(2)}) collective-permute-start(bf16[192,1024]{1,0:T(8,128)(2,1)S(1)} %pad_maximum_fusion.14), channel_id=1, source_target_pairs={{0,16},{1,17},{2,18},{3,19},{4,20},{5,21},{6,22},{7,23},{8,24},{9,... | collective-permute-start | bytes 1179656 | tf_op jit(solution)/shard_map/ppermute | solution.py:105
  25.1 1.4 %collective-permute-start.3 = (s32[8,128]{1,0:T(8,128)S(1)}, s32[8,128]{1,0:T(8,128)S(1)}, u32[]{:S(2)}, u32[]{:S(2)}) collective-permute-start(s32[8,128]{1,0:T(8,128)S(1)} %pad_add_fusion), channel_id=1, source_target_pairs={{0,8},{1,9},{2,10},{3,11},{4,12},{5,13},{6,14},{7,15},{8,0},{9,1},... | collective-permute-start | bytes 12296 | tf_op jit(solution)/shard_map/ppermute | solution.py:105
  26.4 7.6 %collective-permute-done.17 = bf16[64,2048]{1,0:T(8,128)(2,1)S(1)} collective-permute-done((bf16[64,2048]{1,0:T(8,128)(2,1)S(1)}, bf16[64,2048]{1,0:T(8,128)(2,1)S(1)}, u32[]{:S(2)}, u32[]{:S(2)}) %collective-permute-start.17) | collective-permute-done | bytes 262176 | tf_op jit(solution)/shard_map/ppermute | solution.py:105
  34.9 2.2 %collective-permute-done.9 = bf16[192,1024]{1,0:T(8,128)(2,1)S(1)} collective-permute-done((bf16[192,1024]{1,0:T(8,128)(2,1)S(1)}, bf16[192,1024]{1,0:T(8,128)(2,1)S(1)}, u32[]{:S(2)}, u32[]{:S(2)}) %collective-permute-start.9) | collective-permute-done | bytes 393248 | tf_op jit(solution)/shard_map/ppermute | solution.py:105
  37.1 1.5 %collective-permute-start.10 = (bf16[192,768]{1,0:T(8,128)(2,1)S(1)}, bf16[192,768]{1,0:T(8,128)(2,1)S(1)}, u32[]{:S(2)}, u32[]{:S(2)}) collective-permute-start(bf16[192,768]{1,0:T(8,128)(2,1)S(1)} %slice.324), channel_id=1, source_target_pairs={{0,16},{1,17},{2,18},{3,19},{4,20},{5,21},{6,22},{7,23},{8,24},{9,... | collective-permute-start | bytes 884744 | tf_op jit(solution)/shard_map/ppermute | solution.py:105
  39.1 8.5 %collective-permute-done.12 = bf16[192,256]{1,0:T(8,128)(2,1)S(1)} collective-permute-done((bf16[192,256]{1,0:T(8,128)(2,1)S(1)}, bf16[192,256]{1,0:T(8,128)(2,1)S(1)}, u32[]{:S(2)}, u32[]{:S(2)}) %collective-permute-start.12) | collective-permute-done | bytes 98336 | tf_op jit(solution)/shard_map/ppermute | solution.py:105
  51.4 1.6 %collective-permute-start.13 = (bf16[64,2048]{1,0:T(8,128)(2,1)S(1)}, bf16[64,2048]{1,0:T(8,128)(2,1)S(1)}, u32[]{:S(2)}, u32[]{:S(2)}) collective-permute-start(bf16[64,2048]{1,0:T(8,128)(2,1)S(1)} %get-tuple-element.29), channel_id=1, source_target_pairs={{0,2},{1,3},{2,0},{3,1},{4,6},{5,7},{6,4},{7,5},{8,10},{9,11},{10,... | collective-permute-start | bytes 786440 | tf_op jit(solution)/shard_map/ppermute | solution.py:105
  53.7 6.6 %collective-permute-done.13 = bf16[64,2048]{1,0:T(8,128)(2,1)S(1)} collective-permute-done((bf16[64,2048]{1,0:T(8,128)(2,1)S(1)}, bf16[64,2048]{1,0:T(8,128)(2,1)S(1)}, u32[]{:S(2)}, u32[]{:S(2)}) %collective-permute-start.13) | collective-permute-done | bytes 262176 | tf_op jit(solution)/shard_map/ppermute | solution.py:105
  60.9 1.4 %fusion.4 = bf16[384,768]{1,0:T(8,128)(2,1)S(1)} fusion(bf16[384,2048]{1,0:T(8,128)(2,1)S(1)} %constant_dynamic-update-slice_fusion, bf16[384,2048]{1,0:T(8,128)(2,1)S(1)} %bitcast.155, bf16[384,2048]{1,0:T(8,128)(2,1)S(1)} %bitcast.153), kind=kOutput, calls=%fused_computation.10 | convolution fusion | flops 1214545920 | bytes 5308416 | tf_op jit(solution)/shard_map/dot_general | solution.py:195
  62.5 1.2 %fusion.6 = bf16[128,768]{1,0:T(8,128)(2,1)S(1)} fusion(bf16[384,2048]{1,0:T(8,128)(2,1)S(1)} %bitcast.156, bf16[384,2048]{1,0:T(8,128)(2,1)S(1)} %bitcast.154, bf16[64,2048]{1,0:T(8,128)(2,1)S(1)} %collective-permute-done.18, bf16[64,2048]{1,0:T(8,128)(2,1)S(1)} %collective-permute-done.17), kind=kOutput, calls=%fused_computation.12 | convolution fusion | flops 410091520 | bytes 3866624 | tf_op jit(solution)/shard_map/dot_general | solution.py:195
  63.8 2.1 %collective-permute-start.19 = (bf16[128,384]{1,0:T(8,128)(2,1)S(1)}, bf16[128,384]{1,0:T(8,128)(2,1)S(1)}, u32[]{:S(2)}, u32[]{:S(2)}) collective-permute-start(bf16[128,384]{1,0:T(8,128)(2,1)S(1)} %get-tuple-element.34), channel_id=1, source_target_pairs={{0,4},{1,5},{2,6},{3,7},{4,0},{5,1},{6,2},{7,3},{8,12},{9,13},{10,... | collective-permute-start | bytes 294920 | tf_op jit(solution)/shard_map/ppermute | solution.py:105
  65.8 6.4 %collective-permute-done.16 = bf16[384,384]{1,0:T(8,128)(2,1)S(1)} collective-permute-done((bf16[384,384]{1,0:T(8,128)(2,1)S(1)}, bf16[384,384]{1,0:T(8,128)(2,1)S(1)}, u32[]{:S(2)}, u32[]{:S(2)}) %collective-permute-start.16) | collective-permute-done | bytes 294944 | tf_op jit(solution)/shard_map/ppermute | solution.py:105
  73.6 1.1 %collective-permute-done.21 = bf16[256,256]{1,0:T(8,128)(2,1)S(1)} collective-permute-done((bf16[256,256]{1,0:T(8,128)(2,1)S(1)}, bf16[256,256]{1,0:T(8,128)(2,1)S(1)}, u32[]{:S(2)}, u32[]{:S(2)}) %collective-permute-start.21) | collective-permute-done | bytes 131104 | tf_op jit(solution)/shard_map/ppermute | solution.py:105
  74.8 2.3 %fusion.61 = (f32[1024]{0:T(1024)S(1)}, f32[1024,2048]{1,0:T(8,128)S(1)}) fusion(bf16[2048,256]{1,0:T(8,128)(2,1)S(1)} %fusion.8, bf16[128,384]{1,0:T(8,128)(2,1)S(1)} %collective-permute-done.19, bf16[128,384]{1,0:T(8,128)(2,1)S(1)} %get-tuple-element.33, bf16[384,384]{1,0:T(8,128)(2,1)S(1)} %collective-permute-done.16, ...), kind=kOutput, calls=%fused_computation.184 | convolution fusion | flops 550501376 | bytes 9728000 | tf_op jit(solution)/shard_map/dot_general | solution.py:230
  77.1 1.3 %fusion = f32[1024]{0:T(1024)S(1)} fusion(f32[1024,2048]{1,0:T(8,128)S(1)} %get-tuple-element.62, f32[1024]{0:T(1024)S(1)} %get-tuple-element.61), kind=kLoop, calls=%fused_computation.3 | loop fusion | flops 4193280 | bytes 8396800 | tf_op jit(solution)/shard_map/reduce_sum | solution.py:238
  78.4 1.5 %fusion.5 = bf16[1024,128]{1,0:T(8,128)(2,1)S(1)} fusion(f32[1024,2048]{1,0:T(8,128)S(1)} %get-tuple-element.62, f32[1024]{0:T(1024)S(1)} %broadcast_divide_fusion, f32[1024]{0:T(1024)S(1)} %get-tuple-element.61, bf16[2048,256]{1,0:T(8,128)(2,1)S(1)} %fusion.8), kind=kOutput, calls=%fused_computation.11 | convolution fusion | flops 543293440 | bytes 9183232 | tf_op jit(solution)/shard_map/dot_general | solution.py:240
  80.2 13.6 %all_to_all.5 = bf16[8,128,128]{2,1,0:T(8,128)(2,1)S(1)} all-to-all(bf16[8,128,128]{2,1,0:T(8,128)(2,1)S(1)} %fusion.45), channel_id=1, replica_groups=mesh['grp'=2,'chip'=8,'core'=2] {'chip'}, dimensions={0} | all-to-all | bytes 524288 | tf_op jit(solution)/shard_map/all_to_all | solution.py:249
  (117 shorter events, 13.4 us)
Async XLA Ops:
  0.0 20.2 %slice-start = ((bf16[128,2048]{1,0:T(8,128)(2,1)}), bf16[64,2048]{1,0:T(8,128)(2,1)S(1)}, s32[]{:S(2)}) async-start(bf16[128,2048]{1,0:T(8,128)(2,1)} %param.5), calls=%async_computation.1 | async-start | bytes 524288 | tf_op jit(solution)/shard_map/slice | solution.py:137
  0.0 13.5 %copy-start.1 = (bf16[4,2048]{1,0:T(4,128)(2,1)S(1)}, bf16[4,2048]{1,0:T(4,128)(2,1)}, u32[]{:S(2)}) copy-start(bf16[4,2048]{1,0:T(4,128)(2,1)} %param.6) | copy-start | bytes 49156
  0.9 19.3 %collective-permute-start.4 = (bf16[3,2048]{1,0:T(4,128)(2,1)S(1)}, bf16[3,2048]{1,0:T(4,128)(2,1)S(1)}, u32[]{:S(2)}, u32[]{:S(2)}) collective-permute-start(bf16[3,2048]{1,0:T(4,128)(2,1)S(1)} %slice.262), channel_id=1, source_target_pairs={{0,1},{1,2},{2,3},{3,4},{4,5},{5,6},{6,7},{7,8},{8,9},{9,10},{10,1... | collective-permute-start | bytes 36872 | tf_op jit(solution)/shard_map/ppermute | solution.py:133
  4.2 17.8 %collective-permute-start.7 = (bf16[64,2048]{1,0:T(8,128)(2,1)S(1)}, bf16[64,2048]{1,0:T(8,128)(2,1)S(1)}, u32[]{:S(2)}, u32[]{:S(2)}) collective-permute-start(bf16[64,2048]{1,0:T(8,128)(2,1)S(1)} %dynamic-slice_bitcast_fusion), channel_id=1, source_target_pairs={{0,0},{1,3},{2,6},{3,9},{4,12},{5,15},{6,2},{7,5},{8,8},{9,11},{10... | collective-permute-start | bytes 786440 | tf_op jit(solution)/shard_map/ppermute | solution.py:153
  5.9 16.1 %collective-permute-start.8 = (bf16[64,1024]{1,0:T(8,128)(2,1)S(1)}, bf16[64,1024]{1,0:T(8,128)(2,1)S(1)}, u32[]{:S(2)}, u32[]{:S(2)}) collective-permute-start(bf16[64,1024]{1,0:T(8,128)(2,1)S(1)} %constant_dynamic-slice_fusion.2), channel_id=1, source_target_pairs={{0,1},{1,4},{2,7},{3,10},{4,13},{5,0},{6,3},{7,6},{8,9},{9,12},{10... | collective-permute-start | bytes 393224 | tf_op jit(solution)/shard_map/ppermute | solution.py:153
  11.8 2.3 %collective-permute-start = (s32[1,128]{1,0:T(1,128)S(1)}, s32[1,128]{1,0:T(1,128)S(1)}, u32[]{:S(2)}, u32[]{:S(2)}) collective-permute-start(s32[1,128]{1,0:T(1,128)S(1)} %bitcast.168), channel_id=1, source_target_pairs={{0,1},{1,0},{2,3},{3,2},{4,5},{5,4},{6,7},{7,6},{8,9},{9,8},{10,11... | collective-permute-start | bytes 1544 | tf_op jit(solution)/shard_map/ppermute | solution.py:105
  14.1 3.6 %collective-permute-start.1 = (s32[2,128]{1,0:T(2,128)S(1)}, s32[2,128]{1,0:T(2,128)S(1)}, u32[]{:S(2)}, u32[]{:S(2)}) collective-permute-start(s32[2,128]{1,0:T(2,128)S(1)} %pad_add_fusion.2), channel_id=1, source_target_pairs={{0,2},{1,3},{2,0},{3,1},{4,6},{5,7},{6,4},{7,5},{8,10},{9,11},{10,... | collective-permute-start | bytes 3080 | tf_op jit(solution)/shard_map/ppermute | solution.py:105
  17.7 7.3 %collective-permute-start.2 = (s32[4,128]{1,0:T(4,128)S(1)}, s32[4,128]{1,0:T(4,128)S(1)}, u32[]{:S(2)}, u32[]{:S(2)}) collective-permute-start(s32[4,128]{1,0:T(4,128)S(1)} %pad_add_fusion.1), channel_id=1, source_target_pairs={{0,4},{1,5},{2,6},{3,7},{4,0},{5,1},{6,2},{7,3},{8,12},{9,13},{10,... | collective-permute-start | bytes 6152 | tf_op jit(solution)/shard_map/ppermute | solution.py:105
  20.5 13.5 %collective-permute-start.17 = (bf16[64,2048]{1,0:T(8,128)(2,1)S(1)}, bf16[64,2048]{1,0:T(8,128)(2,1)S(1)}, u32[]{:S(2)}, u32[]{:S(2)}) collective-permute-start(bf16[64,2048]{1,0:T(8,128)(2,1)S(1)} %get-tuple-element.8), channel_id=1, source_target_pairs={{0,8},{1,9},{2,10},{3,11},{4,12},{5,13},{6,14},{7,15},{8,0},{9,1},... | collective-permute-start | bytes 786440 | tf_op jit(solution)/shard_map/ppermute | solution.py:105
  21.1 12.9 %collective-permute-start.5 = (bf16[128,2048]{1,0:T(8,128)(2,1)S(1)}, bf16[128,2048]{1,0:T(8,128)(2,1)S(1)}, u32[]{:S(2)}, u32[]{:S(2)}) collective-permute-start(bf16[128,2048]{1,0:T(8,128)(2,1)S(1)} %pad_maximum_fusion.12), channel_id=1, source_target_pairs={{0,2},{1,3},{2,0},{3,1},{4,6},{5,7},{6,4},{7,5},{8,10},{9,11},{10,... | collective-permute-start | bytes 1572872 | tf_op jit(solution)/shard_map/ppermute | solution.py:105
  22.0 15.1 %collective-permute-start.9 = (bf16[192,1024]{1,0:T(8,128)(2,1)S(1)}, bf16[192,1024]{1,0:T(8,128)(2,1)S(1)}, u32[]{:S(2)}, u32[]{:S(2)}) collective-permute-start(bf16[192,1024]{1,0:T(8,128)(2,1)S(1)} %pad_maximum_fusion.14), channel_id=1, source_target_pairs={{0,4},{1,5},{2,6},{3,7},{4,0},{5,1},{6,2},{7,3},{8,12},{9,13},{10,... | collective-permute-start | bytes 1179656 | tf_op jit(solution)/shard_map/ppermute | solution.py:105
  23.9 14.8 %collective-permute-start.11 = (bf16[192,1024]{1,0:T(8,128)(2,1)S(1)}, bf16[192,1024]{1,0:T(8,128)(2,1)S(1)}, u32[]{:S(2)}, u32[]{:S(2)}) collective-permute-start(bf16[192,1024]{1,0:T(8,128)(2,1)S(1)} %pad_maximum_fusion.14), channel_id=1, source_target_pairs={{0,16},{1,17},{2,18},{3,19},{4,20},{5,21},{6,22},{7,23},{8,24},{9,... | collective-permute-start | bytes 1179656 | tf_op jit(solution)/shard_map/ppermute | solution.py:105
  25.1 48.3 %collective-permute-start.3 = (s32[8,128]{1,0:T(8,128)S(1)}, s32[8,128]{1,0:T(8,128)S(1)}, u32[]{:S(2)}, u32[]{:S(2)}) collective-permute-start(s32[8,128]{1,0:T(8,128)S(1)} %pad_add_fusion), channel_id=1, source_target_pairs={{0,8},{1,9},{2,10},{3,11},{4,12},{5,13},{6,14},{7,15},{8,0},{9,1},... | collective-permute-start | bytes 12296 | tf_op jit(solution)/shard_map/ppermute | solution.py:105
  34.0 17.4 %collective-permute-start.6 = (bf16[64,2048]{1,0:T(8,128)(2,1)S(1)}, bf16[64,2048]{1,0:T(8,128)(2,1)S(1)}, u32[]{:S(2)}, u32[]{:S(2)}) collective-permute-start(bf16[64,2048]{1,0:T(8,128)(2,1)S(1)} %get-tuple-element.6), channel_id=1, source_target_pairs={{0,8},{1,9},{2,10},{3,11},{4,12},{5,13},{6,14},{7,15},{8,0},{9,1},... | collective-permute-start | bytes 786440 | tf_op jit(solution)/shard_map/ppermute | solution.py:105
  34.0 28.5 %collective-permute-start.18 = (bf16[64,2048]{1,0:T(8,128)(2,1)S(1)}, bf16[64,2048]{1,0:T(8,128)(2,1)S(1)}, u32[]{:S(2)}, u32[]{:S(2)}) collective-permute-start(bf16[64,2048]{1,0:T(8,128)(2,1)S(1)} %collective-permute-done.17), channel_id=1, source_target_pairs={{0,2},{1,3},{2,0},{3,1},{4,6},{5,7},{6,4},{7,5},{8,10},{9,11},{10,... | collective-permute-start | bytes 786440 | tf_op jit(solution)/shard_map/ppermute | solution.py:105
  37.1 12.3 %collective-permute-start.10 = (bf16[192,768]{1,0:T(8,128)(2,1)S(1)}, bf16[192,768]{1,0:T(8,128)(2,1)S(1)}, u32[]{:S(2)}, u32[]{:S(2)}) collective-permute-start(bf16[192,768]{1,0:T(8,128)(2,1)S(1)} %slice.324), channel_id=1, source_target_pairs={{0,16},{1,17},{2,18},{3,19},{4,20},{5,21},{6,22},{7,23},{8,24},{9,... | collective-permute-start | bytes 884744 | tf_op jit(solution)/shard_map/ppermute | solution.py:105
  38.7 8.9 %collective-permute-start.12 = (bf16[192,256]{1,0:T(8,128)(2,1)S(1)}, bf16[192,256]{1,0:T(8,128)(2,1)S(1)}, u32[]{:S(2)}, u32[]{:S(2)}) collective-permute-start(bf16[192,256]{1,0:T(8,128)(2,1)S(1)} %slice.326), channel_id=1, source_target_pairs={{0,4},{1,5},{2,6},{3,7},{4,0},{5,1},{6,2},{7,3},{8,12},{9,13},{10,... | collective-permute-start | bytes 294920 | tf_op jit(solution)/shard_map/ppermute | solution.py:105
  47.6 12.7 %collective-permute-start.14 = (bf16[3,64,2048]{2,1,0:T(8,128)(2,1)S(1)}, bf16[3,64,2048]{2,1,0:T(8,128)(2,1)S(1)}, u32[]{:S(2)}, u32[]{:S(2)}) collective-permute-start(bf16[3,64,2048]{2,1,0:T(8,128)(2,1)S(1)} %constant_dynamic-slice_fusion.1), channel_id=1, source_target_pairs={{0,1},{1,0},{2,3},{3,2},{4,5},{5,4},{6,7},{7,6},{8,9},{9,8},{10,11... | collective-permute-start | bytes 2359304 | tf_op jit(solution)/shard_map/ppermute | solution.py:105
  51.4 8.8 %collective-permute-start.13 = (bf16[64,2048]{1,0:T(8,128)(2,1)S(1)}, bf16[64,2048]{1,0:T(8,128)(2,1)S(1)}, u32[]{:S(2)}, u32[]{:S(2)}) collective-permute-start(bf16[64,2048]{1,0:T(8,128)(2,1)S(1)} %get-tuple-element.29), channel_id=1, source_target_pairs={{0,2},{1,3},{2,0},{3,1},{4,6},{5,7},{6,4},{7,5},{8,10},{9,11},{10,... | collective-permute-start | bytes 786440 | tf_op jit(solution)/shard_map/ppermute | solution.py:105
  53.4 7.2 %collective-permute-start.15 = (bf16[3,64,2048]{2,1,0:T(8,128)(2,1)S(1)}, bf16[3,64,2048]{2,1,0:T(8,128)(2,1)S(1)}, u32[]{:S(2)}, u32[]{:S(2)}) collective-permute-start(bf16[3,64,2048]{2,1,0:T(8,128)(2,1)S(1)} %constant_dynamic-slice_fusion), channel_id=1, source_target_pairs={{0,1},{1,0},{2,3},{3,2},{4,5},{5,4},{6,7},{7,6},{8,9},{9,8},{10,11... | collective-permute-start | bytes 2359304 | tf_op jit(solution)/shard_map/ppermute | solution.py:105
  62.4 9.8 %collective-permute-start.16 = (bf16[384,384]{1,0:T(8,128)(2,1)S(1)}, bf16[384,384]{1,0:T(8,128)(2,1)S(1)}, u32[]{:S(2)}, u32[]{:S(2)}) collective-permute-start(bf16[384,384]{1,0:T(8,128)(2,1)S(1)} %get-tuple-element.24), channel_id=1, source_target_pairs={{0,4},{1,5},{2,6},{3,7},{4,0},{5,1},{6,2},{7,3},{8,12},{9,13},{10,... | collective-permute-start | bytes 884744 | tf_op jit(solution)/shard_map/ppermute | solution.py:105
  63.8 9.5 %collective-permute-start.19 = (bf16[128,384]{1,0:T(8,128)(2,1)S(1)}, bf16[128,384]{1,0:T(8,128)(2,1)S(1)}, u32[]{:S(2)}, u32[]{:S(2)}) collective-permute-start(bf16[128,384]{1,0:T(8,128)(2,1)S(1)} %get-tuple-element.34), channel_id=1, source_target_pairs={{0,4},{1,5},{2,6},{3,7},{4,0},{5,1},{6,2},{7,3},{8,12},{9,13},{10,... | collective-permute-start | bytes 294920 | tf_op jit(solution)/shard_map/ppermute | solution.py:105
  72.2 2.5 %collective-permute-start.20 = (bf16[768,256]{1,0:T(8,128)(2,1)S(1)}, bf16[768,256]{1,0:T(8,128)(2,1)S(1)}, u32[]{:S(2)}, u32[]{:S(2)}) collective-permute-start(bf16[768,256]{1,0:T(8,128)(2,1)S(1)} %pad_maximum_fusion.13), channel_id=1, source_target_pairs={{0,1},{1,0},{2,3},{3,2},{4,5},{5,4},{6,7},{7,6},{8,9},{9,8},{10,11... | collective-permute-start | bytes 1179656 | tf_op jit(solution)/shard_map/ppermute | solution.py:105
  73.3 1.4 %collective-permute-start.21 = (bf16[256,256]{1,0:T(8,128)(2,1)S(1)}, bf16[256,256]{1,0:T(8,128)(2,1)S(1)}, u32[]{:S(2)}, u32[]{:S(2)}) collective-permute-start(bf16[256,256]{1,0:T(8,128)(2,1)S(1)} %pad_maximum_fusion.15), channel_id=1, source_target_pairs={{0,1},{1,0},{2,3},{3,2},{4,5},{5,4},{6,7},{7,6},{8,9},{9,8},{10,11... | collective-permute-start | bytes 393224 | tf_op jit(solution)/shard_map/ppermute | solution.py:105
  (1 other events, 13.3 us)

commit v29 on v28

--- a/solution.py
+++ b/solution.py
@@ -159,7 +159,7 @@
 
     mine_too = xor_swap(mine, devices, every)
 
-    cut = 3 * half // 4
+    cut = 5 * half // 8
     fourth = [xor_swap(paired[:, :cut], devices, every), xor_swap(mine_too[:, cut:], Z0)]
 
     far_beside_late = xor_swap(far_late + zero_after(fourth[0]) + zero_after(fourth[1]), Y)

time: 95.1 us -> 95.6 us (level)
  no operation moved by 1% of the time
where the time goes in v29:
time: 95.6 us; the launch traced here: 95.3 us
  waiting for transfers between devices  36 us (38%)
  starting transfers between devices  25.8 us (27%)
  blocking collectives  13.6 us (14%)
  matrix products  6.49 us (7%)
  local copies, waits for them, and re-layouts  6.19 us (6%)
  other arithmetic  3.91 us (4%)
  between operations  3.38 us (4%)
    ppermute x19, waiting for transfers between devices, xor_swap(): return lax.ppermute(value, axes, [(d, d ^ bit) for d in range(count)])  36 us
    ppermute x19, starting transfers between devices, xor_swap(): return lax.ppermute(value, axes, [(d, d ^ bit) for d in range(count)])  17.6 us
    all_to_all x1, blocking collectives, body_by_head(): lax.all_to_all(sent, 'chip', split_axis=0, concat_axis=0, tiled=True)  13.6 us
    ppermute x2, starting transfers between devices, to_heads(): return lax.ppermute(block, every, pairs)  5.83 us
    dot_general x2, matrix products, project(): lax.dot_general(rows, two_heads, (((1,), (1,)), ((), ())), preferred_elem...  2.62 us
    ppermute x1, starting transfers between devices, body_by_head(): lax.ppermute(frames[tok_rows - (KW - 1):], both, [(i, i + 1) for i in ran...  2.36 us
    dot_general x1, matrix products, body_by_head(): lax.dot_general(query, keyed[:, :HD], (((1,), (1,)), ((), ())), preferred...  2.33 us
  transfers between devices with their start and end apart: 22, of which 9 were waited for; matrix products, arithmetic and copies ran while one was open for 10% of the time, Pallas kernels for 0%

profile of v29, /device:TPU:0, one launch (start us, length us, event | category | flops | bytes accessed | tf_op | source)
XLA Modules:
  0.0 95.3 jit_solution(10283291516524028233)
XLA Ops:
  0.9 2.4 %collective-permute-start.4 = (bf16[3,2048]{1,0:T(4,128)(2,1)S(1)}, bf16[3,2048]{1,0:T(4,128)(2,1)S(1)}, u32[]{:S(2)}, u32[]{:S(2)}) collective-permute-start(bf16[3,2048]{1,0:T(4,128)(2,1)S(1)} %slice.262), channel_id=1, source_target_pairs={{0,1},{1,2},{2,3},{3,4},{4,5},{5,6},{6,7},{7,8},{8,9},{9,10},{10,1... | collective-permute-start | bytes 36872 | tf_op jit(solution)/shard_map/ppermute | solution.py:133
  5.9 5.2 %collective-permute-start.8 = (bf16[64,1024]{1,0:T(8,128)(2,1)S(1)}, bf16[64,1024]{1,0:T(8,128)(2,1)S(1)}, u32[]{:S(2)}, u32[]{:S(2)}) collective-permute-start(bf16[64,1024]{1,0:T(8,128)(2,1)S(1)} %constant_dynamic-slice_fusion.2), channel_id=1, source_target_pairs={{0,1},{1,4},{2,7},{3,10},{4,13},{5,0},{6,3},{7,6},{8,9},{9,12},{10... | collective-permute-start | bytes 393224 | tf_op jit(solution)/shard_map/ppermute | solution.py:153
  11.8 1.5 %collective-permute-start = (s32[1,128]{1,0:T(1,128)S(1)}, s32[1,128]{1,0:T(1,128)S(1)}, u32[]{:S(2)}, u32[]{:S(2)}) collective-permute-start(s32[1,128]{1,0:T(1,128)S(1)} %bitcast.168), channel_id=1, source_target_pairs={{0,1},{1,0},{2,3},{3,2},{4,5},{5,4},{6,7},{7,6},{8,9},{9,8},{10,11... | collective-permute-start | bytes 1544 | tf_op jit(solution)/shard_map/ppermute | solution.py:105
  14.1 1.5 %collective-permute-start.1 = (s32[2,128]{1,0:T(2,128)S(1)}, s32[2,128]{1,0:T(2,128)S(1)}, u32[]{:S(2)}, u32[]{:S(2)}) collective-permute-start(s32[2,128]{1,0:T(2,128)S(1)} %pad_add_fusion.2), channel_id=1, source_target_pairs={{0,2},{1,3},{2,0},{3,1},{4,6},{5,7},{6,4},{7,5},{8,10},{9,11},{10,... | collective-permute-start | bytes 3080 | tf_op jit(solution)/shard_map/ppermute | solution.py:105
  15.8 1.9 %collective-permute-done.1 = s32[2,128]{1,0:T(2,128)S(1)} collective-permute-done((s32[2,128]{1,0:T(2,128)S(1)}, s32[2,128]{1,0:T(2,128)S(1)}, u32[]{:S(2)}, u32[]{:S(2)}) %collective-permute-start.1) | collective-permute-done | bytes 1056 | tf_op jit(solution)/shard_map/ppermute | solution.py:105
  17.7 2.5 %collective-permute-start.2 = (s32[4,128]{1,0:T(4,128)S(1)}, s32[4,128]{1,0:T(4,128)S(1)}, u32[]{:S(2)}, u32[]{:S(2)}) collective-permute-start(s32[4,128]{1,0:T(4,128)S(1)} %pad_add_fusion.1), channel_id=1, source_target_pairs={{0,4},{1,5},{2,6},{3,7},{4,0},{5,1},{6,2},{7,3},{8,12},{9,13},{10,... | collective-permute-start | bytes 6152 | tf_op jit(solution)/shard_map/ppermute | solution.py:105
  22.0 1.9 %collective-permute-start.9 = (bf16[192,1024]{1,0:T(8,128)(2,1)S(1)}, bf16[192,1024]{1,0:T(8,128)(2,1)S(1)}, u32[]{:S(2)}, u32[]{:S(2)}) collective-permute-start(bf16[192,1024]{1,0:T(8,128)(2,1)S(1)} %pad_maximum_fusion.14), channel_id=1, source_target_pairs={{0,4},{1,5},{2,6},{3,7},{4,0},{5,1},{6,2},{7,3},{8,12},{9,13},{10,... | collective-permute-start | bytes 1179656 | tf_op jit(solution)/shard_map/ppermute | solution.py:105
  23.9 1.1 %collective-permute-start.11 = (bf16[192,1024]{1,0:T(8,128)(2,1)S(1)}, bf16[192,1024]{1,0:T(8,128)(2,1)S(1)}, u32[]{:S(2)}, u32[]{:S(2)}) collective-permute-start(bf16[192,1024]{1,0:T(8,128)(2,1)S(1)} %pad_maximum_fusion.14), channel_id=1, source_target_pairs={{0,16},{1,17},{2,18},{3,19},{4,20},{5,21},{6,22},{7,23},{8,24},{9,... | collective-permute-start | bytes 1179656 | tf_op jit(solution)/shard_map/ppermute | solution.py:105
  25.1 1.4 %collective-permute-start.3 = (s32[8,128]{1,0:T(8,128)S(1)}, s32[8,128]{1,0:T(8,128)S(1)}, u32[]{:S(2)}, u32[]{:S(2)}) collective-permute-start(s32[8,128]{1,0:T(8,128)S(1)} %pad_add_fusion), channel_id=1, source_target_pairs={{0,8},{1,9},{2,10},{3,11},{4,12},{5,13},{6,14},{7,15},{8,0},{9,1},... | collective-permute-start | bytes 12296 | tf_op jit(solution)/shard_map/ppermute | solution.py:105
  26.4 7.6 %collective-permute-done.17 = bf16[64,2048]{1,0:T(8,128)(2,1)S(1)} collective-permute-done((bf16[64,2048]{1,0:T(8,128)(2,1)S(1)}, bf16[64,2048]{1,0:T(8,128)(2,1)S(1)}, u32[]{:S(2)}, u32[]{:S(2)}) %collective-permute-start.17) | collective-permute-done | bytes 262176 | tf_op jit(solution)/shard_map/ppermute | solution.py:105
  34.9 2.2 %collective-permute-done.9 = bf16[192,1024]{1,0:T(8,128)(2,1)S(1)} collective-permute-done((bf16[192,1024]{1,0:T(8,128)(2,1)S(1)}, bf16[192,1024]{1,0:T(8,128)(2,1)S(1)}, u32[]{:S(2)}, u32[]{:S(2)}) %collective-permute-start.9) | collective-permute-done | bytes 393248 | tf_op jit(solution)/shard_map/ppermute | solution.py:105
  37.1 1.5 %collective-permute-start.10 = (bf16[192,640]{1,0:T(8,128)(2,1)S(1)}, bf16[192,640]{1,0:T(8,128)(2,1)S(1)}, u32[]{:S(2)}, u32[]{:S(2)}) collective-permute-start(bf16[192,640]{1,0:T(8,128)(2,1)S(1)} %slice.324), channel_id=1, source_target_pairs={{0,16},{1,17},{2,18},{3,19},{4,20},{5,21},{6,22},{7,23},{8,24},{9,... | collective-permute-start | bytes 737288 | tf_op jit(solution)/shard_map/ppermute | solution.py:105
  39.1 9.0 %collective-permute-done.12 = bf16[192,384]{1,0:T(8,128)(2,1)S(1)} collective-permute-done((bf16[192,384]{1,0:T(8,128)(2,1)S(1)}, bf16[192,384]{1,0:T(8,128)(2,1)S(1)}, u32[]{:S(2)}, u32[]{:S(2)}) %collective-permute-start.12) | collective-permute-done | bytes 147488 | tf_op jit(solution)/shard_map/ppermute | solution.py:105
  52.0 1.6 %collective-permute-start.13 = (bf16[64,2048]{1,0:T(8,128)(2,1)S(1)}, bf16[64,2048]{1,0:T(8,128)(2,1)S(1)}, u32[]{:S(2)}, u32[]{:S(2)}) collective-permute-start(bf16[64,2048]{1,0:T(8,128)(2,1)S(1)} %get-tuple-element.29), channel_id=1, source_target_pairs={{0,2},{1,3},{2,0},{3,1},{4,6},{5,7},{6,4},{7,5},{8,10},{9,11},{10,... | collective-permute-start | bytes 786440 | tf_op jit(solution)/shard_map/ppermute | solution.py:105
  54.2 6.5 %collective-permute-done.13 = bf16[64,2048]{1,0:T(8,128)(2,1)S(1)} collective-permute-done((bf16[64,2048]{1,0:T(8,128)(2,1)S(1)}, bf16[64,2048]{1,0:T(8,128)(2,1)S(1)}, u32[]{:S(2)}, u32[]{:S(2)}) %collective-permute-start.13) | collective-permute-done | bytes 262176 | tf_op jit(solution)/shard_map/ppermute | solution.py:105
  61.5 1.4 %fusion.4 = bf16[384,768]{1,0:T(8,128)(2,1)S(1)} fusion(bf16[384,2048]{1,0:T(8,128)(2,1)S(1)} %constant_dynamic-update-slice_fusion, bf16[384,2048]{1,0:T(8,128)(2,1)S(1)} %bitcast.155, bf16[384,2048]{1,0:T(8,128)(2,1)S(1)} %bitcast.153), kind=kOutput, calls=%fused_computation.10 | convolution fusion | flops 1214545920 | bytes 5308416 | tf_op jit(solution)/shard_map/dot_general | solution.py:195
  63.1 1.2 %fusion.6 = bf16[128,768]{1,0:T(8,128)(2,1)S(1)} fusion(bf16[384,2048]{1,0:T(8,128)(2,1)S(1)} %bitcast.156, bf16[384,2048]{1,0:T(8,128)(2,1)S(1)} %bitcast.154, bf16[64,2048]{1,0:T(8,128)(2,1)S(1)} %collective-permute-done.18, bf16[64,2048]{1,0:T(8,128)(2,1)S(1)} %collective-permute-done.17), kind=kOutput, calls=%fused_computation.12 | convolution fusion | flops 410091520 | bytes 3866624 | tf_op jit(solution)/shard_map/dot_general | solution.py:195
  64.3 2.1 %collective-permute-start.19 = (bf16[128,384]{1,0:T(8,128)(2,1)S(1)}, bf16[128,384]{1,0:T(8,128)(2,1)S(1)}, u32[]{:S(2)}, u32[]{:S(2)}) collective-permute-start(bf16[128,384]{1,0:T(8,128)(2,1)S(1)} %get-tuple-element.34), channel_id=1, source_target_pairs={{0,4},{1,5},{2,6},{3,7},{4,0},{5,1},{6,2},{7,3},{8,12},{9,13},{10,... | collective-permute-start | bytes 294920 | tf_op jit(solution)/shard_map/ppermute | solution.py:105
  66.4 6.4 %collective-permute-done.16 = bf16[384,384]{1,0:T(8,128)(2,1)S(1)} collective-permute-done((bf16[384,384]{1,0:T(8,128)(2,1)S(1)}, bf16[384,384]{1,0:T(8,128)(2,1)S(1)}, u32[]{:S(2)}, u32[]{:S(2)}) %collective-permute-start.16) | collective-permute-done | bytes 294944 | tf_op jit(solution)/shard_map/ppermute | solution.py:105
  74.1 1.1 %collective-permute-done.21 = bf16[256,256]{1,0:T(8,128)(2,1)S(1)} collective-permute-done((bf16[256,256]{1,0:T(8,128)(2,1)S(1)}, bf16[256,256]{1,0:T(8,128)(2,1)S(1)}, u32[]{:S(2)}, u32[]{:S(2)}) %collective-permute-start.21) | collective-permute-done | bytes 131104 | tf_op jit(solution)/shard_map/ppermute | solution.py:105
  75.3 2.3 %fusion.61 = (f32[1024]{0:T(1024)S(1)}, f32[1024,2048]{1,0:T(8,128)S(1)}) fusion(bf16[2048,256]{1,0:T(8,128)(2,1)S(1)} %fusion.8, bf16[128,384]{1,0:T(8,128)(2,1)S(1)} %collective-permute-done.19, bf16[128,384]{1,0:T(8,128)(2,1)S(1)} %get-tuple-element.33, bf16[384,384]{1,0:T(8,128)(2,1)S(1)} %collective-permute-done.16, ...), kind=kOutput, calls=%fused_computation.184 | convolution fusion | flops 550501376 | bytes 9728000 | tf_op jit(solution)/shard_map/dot_general | solution.py:230
  77.6 1.3 %fusion = f32[1024]{0:T(1024)S(1)} fusion(f32[1024,2048]{1,0:T(8,128)S(1)} %get-tuple-element.62, f32[1024]{0:T(1024)S(1)} %get-tuple-element.61), kind=kLoop, calls=%fused_computation.3 | loop fusion | flops 4193280 | bytes 8396800 | tf_op jit(solution)/shard_map/reduce_sum | solution.py:238
  78.9 1.5 %fusion.5 = bf16[1024,128]{1,0:T(8,128)(2,1)S(1)} fusion(f32[1024,2048]{1,0:T(8,128)S(1)} %get-tuple-element.62, f32[1024]{0:T(1024)S(1)} %broadcast_divide_fusion, f32[1024]{0:T(1024)S(1)} %get-tuple-element.61, bf16[2048,256]{1,0:T(8,128)(2,1)S(1)} %fusion.8), kind=kOutput, calls=%fused_computation.11 | convolution fusion | flops 543293440 | bytes 9183232 | tf_op jit(solution)/shard_map/dot_general | solution.py:240
  80.7 13.6 %all_to_all.5 = bf16[8,128,128]{2,1,0:T(8,128)(2,1)S(1)} all-to-all(bf16[8,128,128]{2,1,0:T(8,128)(2,1)S(1)} %fusion.45), channel_id=1, replica_groups=mesh['grp'=2,'chip'=8,'core'=2] {'chip'}, dimensions={0} | all-to-all | bytes 524288 | tf_op jit(solution)/shard_map/all_to_all | solution.py:249
  (117 shorter events, 13.4 us)
Async XLA Ops:
  0.0 20.2 %slice-start = ((bf16[128,2048]{1,0:T(8,128)(2,1)}), bf16[64,2048]{1,0:T(8,128)(2,1)S(1)}, s32[]{:S(2)}) async-start(bf16[128,2048]{1,0:T(8,128)(2,1)} %param.5), calls=%async_computation.1 | async-start | bytes 524288 | tf_op jit(solution)/shard_map/slice | solution.py:137
  0.0 13.5 %copy-start.1 = (bf16[4,2048]{1,0:T(4,128)(2,1)S(1)}, bf16[4,2048]{1,0:T(4,128)(2,1)}, u32[]{:S(2)}) copy-start(bf16[4,2048]{1,0:T(4,128)(2,1)} %param.6) | copy-start | bytes 49156
  0.9 19.3 %collective-permute-start.4 = (bf16[3,2048]{1,0:T(4,128)(2,1)S(1)}, bf16[3,2048]{1,0:T(4,128)(2,1)S(1)}, u32[]{:S(2)}, u32[]{:S(2)}) collective-permute-start(bf16[3,2048]{1,0:T(4,128)(2,1)S(1)} %slice.262), channel_id=1, source_target_pairs={{0,1},{1,2},{2,3},{3,4},{4,5},{5,6},{6,7},{7,8},{8,9},{9,10},{10,1... | collective-permute-start | bytes 36872 | tf_op jit(solution)/shard_map/ppermute | solution.py:133
  4.2 17.8 %collective-permute-start.7 = (bf16[64,2048]{1,0:T(8,128)(2,1)S(1)}, bf16[64,2048]{1,0:T(8,128)(2,1)S(1)}, u32[]{:S(2)}, u32[]{:S(2)}) collective-permute-start(bf16[64,2048]{1,0:T(8,128)(2,1)S(1)} %dynamic-slice_bitcast_fusion), channel_id=1, source_target_pairs={{0,0},{1,3},{2,6},{3,9},{4,12},{5,15},{6,2},{7,5},{8,8},{9,11},{10... | collective-permute-start | bytes 786440 | tf_op jit(solution)/shard_map/ppermute | solution.py:153
  5.9 16.1 %collective-permute-start.8 = (bf16[64,1024]{1,0:T(8,128)(2,1)S(1)}, bf16[64,1024]{1,0:T(8,128)(2,1)S(1)}, u32[]{:S(2)}, u32[]{:S(2)}) collective-permute-start(bf16[64,1024]{1,0:T(8,128)(2,1)S(1)} %constant_dynamic-slice_fusion.2), channel_id=1, source_target_pairs={{0,1},{1,4},{2,7},{3,10},{4,13},{5,0},{6,3},{7,6},{8,9},{9,12},{10... | collective-permute-start | bytes 393224 | tf_op jit(solution)/shard_map/ppermute | solution.py:153
  11.8 2.3 %collective-permute-start = (s32[1,128]{1,0:T(1,128)S(1)}, s32[1,128]{1,0:T(1,128)S(1)}, u32[]{:S(2)}, u32[]{:S(2)}) collective-permute-start(s32[1,128]{1,0:T(1,128)S(1)} %bitcast.168), channel_id=1, source_target_pairs={{0,1},{1,0},{2,3},{3,2},{4,5},{5,4},{6,7},{7,6},{8,9},{9,8},{10,11... | collective-permute-start | bytes 1544 | tf_op jit(solution)/shard_map/ppermute | solution.py:105
  14.1 3.6 %collective-permute-start.1 = (s32[2,128]{1,0:T(2,128)S(1)}, s32[2,128]{1,0:T(2,128)S(1)}, u32[]{:S(2)}, u32[]{:S(2)}) collective-permute-start(s32[2,128]{1,0:T(2,128)S(1)} %pad_add_fusion.2), channel_id=1, source_target_pairs={{0,2},{1,3},{2,0},{3,1},{4,6},{5,7},{6,4},{7,5},{8,10},{9,11},{10,... | collective-permute-start | bytes 3080 | tf_op jit(solution)/shard_map/ppermute | solution.py:105
  17.7 7.3 %collective-permute-start.2 = (s32[4,128]{1,0:T(4,128)S(1)}, s32[4,128]{1,0:T(4,128)S(1)}, u32[]{:S(2)}, u32[]{:S(2)}) collective-permute-start(s32[4,128]{1,0:T(4,128)S(1)} %pad_add_fusion.1), channel_id=1, source_target_pairs={{0,4},{1,5},{2,6},{3,7},{4,0},{5,1},{6,2},{7,3},{8,12},{9,13},{10,... | collective-permute-start | bytes 6152 | tf_op jit(solution)/shard_map/ppermute | solution.py:105
  20.5 13.5 %collective-permute-start.17 = (bf16[64,2048]{1,0:T(8,128)(2,1)S(1)}, bf16[64,2048]{1,0:T(8,128)(2,1)S(1)}, u32[]{:S(2)}, u32[]{:S(2)}) collective-permute-start(bf16[64,2048]{1,0:T(8,128)(2,1)S(1)} %get-tuple-element.8), channel_id=1, source_target_pairs={{0,8},{1,9},{2,10},{3,11},{4,12},{5,13},{6,14},{7,15},{8,0},{9,1},... | collective-permute-start | bytes 786440 | tf_op jit(solution)/shard_map/ppermute | solution.py:105
  21.1 12.9 %collective-permute-start.5 = (bf16[128,2048]{1,0:T(8,128)(2,1)S(1)}, bf16[128,2048]{1,0:T(8,128)(2,1)S(1)}, u32[]{:S(2)}, u32[]{:S(2)}) collective-permute-start(bf16[128,2048]{1,0:T(8,128)(2,1)S(1)} %pad_maximum_fusion.12), channel_id=1, source_target_pairs={{0,2},{1,3},{2,0},{3,1},{4,6},{5,7},{6,4},{7,5},{8,10},{9,11},{10,... | collective-permute-start | bytes 1572872 | tf_op jit(solution)/shard_map/ppermute | solution.py:105
  22.0 15.1 %collective-permute-start.9 = (bf16[192,1024]{1,0:T(8,128)(2,1)S(1)}, bf16[192,1024]{1,0:T(8,128)(2,1)S(1)}, u32[]{:S(2)}, u32[]{:S(2)}) collective-permute-start(bf16[192,1024]{1,0:T(8,128)(2,1)S(1)} %pad_maximum_fusion.14), channel_id=1, source_target_pairs={{0,4},{1,5},{2,6},{3,7},{4,0},{5,1},{6,2},{7,3},{8,12},{9,13},{10,... | collective-permute-start | bytes 1179656 | tf_op jit(solution)/shard_map/ppermute | solution.py:105
  23.9 14.8 %collective-permute-start.11 = (bf16[192,1024]{1,0:T(8,128)(2,1)S(1)}, bf16[192,1024]{1,0:T(8,128)(2,1)S(1)}, u32[]{:S(2)}, u32[]{:S(2)}) collective-permute-start(bf16[192,1024]{1,0:T(8,128)(2,1)S(1)} %pad_maximum_fusion.14), channel_id=1, source_target_pairs={{0,16},{1,17},{2,18},{3,19},{4,20},{5,21},{6,22},{7,23},{8,24},{9,... | collective-permute-start | bytes 1179656 | tf_op jit(solution)/shard_map/ppermute | solution.py:105
  25.1 48.8 %collective-permute-start.3 = (s32[8,128]{1,0:T(8,128)S(1)}, s32[8,128]{1,0:T(8,128)S(1)}, u32[]{:S(2)}, u32[]{:S(2)}) collective-permute-start(s32[8,128]{1,0:T(8,128)S(1)} %pad_add_fusion), channel_id=1, source_target_pairs={{0,8},{1,9},{2,10},{3,11},{4,12},{5,13},{6,14},{7,15},{8,0},{9,1},... | collective-permute-start | bytes 12296 | tf_op jit(solution)/shard_map/ppermute | solution.py:105
  34.0 17.9 %collective-permute-start.6 = (bf16[64,2048]{1,0:T(8,128)(2,1)S(1)}, bf16[64,2048]{1,0:T(8,128)(2,1)S(1)}, u32[]{:S(2)}, u32[]{:S(2)}) collective-permute-start(bf16[64,2048]{1,0:T(8,128)(2,1)S(1)} %get-tuple-element.6), channel_id=1, source_target_pairs={{0,8},{1,9},{2,10},{3,11},{4,12},{5,13},{6,14},{7,15},{8,0},{9,1},... | collective-permute-start | bytes 786440 | tf_op jit(solution)/shard_map/ppermute | solution.py:105
  34.0 29.0 %collective-permute-start.18 = (bf16[64,2048]{1,0:T(8,128)(2,1)S(1)}, bf16[64,2048]{1,0:T(8,128)(2,1)S(1)}, u32[]{:S(2)}, u32[]{:S(2)}) collective-permute-start(bf16[64,2048]{1,0:T(8,128)(2,1)S(1)} %collective-permute-done.17), channel_id=1, source_target_pairs={{0,2},{1,3},{2,0},{3,1},{4,6},{5,7},{6,4},{7,5},{8,10},{9,11},{10,... | collective-permute-start | bytes 786440 | tf_op jit(solution)/shard_map/ppermute | solution.py:105
  37.1 12.8 %collective-permute-start.10 = (bf16[192,640]{1,0:T(8,128)(2,1)S(1)}, bf16[192,640]{1,0:T(8,128)(2,1)S(1)}, u32[]{:S(2)}, u32[]{:S(2)}) collective-permute-start(bf16[192,640]{1,0:T(8,128)(2,1)S(1)} %slice.324), channel_id=1, source_target_pairs={{0,16},{1,17},{2,18},{3,19},{4,20},{5,21},{6,22},{7,23},{8,24},{9,... | collective-permute-start | bytes 737288 | tf_op jit(solution)/shard_map/ppermute | solution.py:105
  38.7 9.4 %collective-permute-start.12 = (bf16[192,384]{1,0:T(8,128)(2,1)S(1)}, bf16[192,384]{1,0:T(8,128)(2,1)S(1)}, u32[]{:S(2)}, u32[]{:S(2)}) collective-permute-start(bf16[192,384]{1,0:T(8,128)(2,1)S(1)} %slice.326), channel_id=1, source_target_pairs={{0,4},{1,5},{2,6},{3,7},{4,0},{5,1},{6,2},{7,3},{8,12},{9,13},{10,... | collective-permute-start | bytes 442376 | tf_op jit(solution)/shard_map/ppermute | solution.py:105
  48.1 12.7 %collective-permute-start.14 = (bf16[3,64,2048]{2,1,0:T(8,128)(2,1)S(1)}, bf16[3,64,2048]{2,1,0:T(8,128)(2,1)S(1)}, u32[]{:S(2)}, u32[]{:S(2)}) collective-permute-start(bf16[3,64,2048]{2,1,0:T(8,128)(2,1)S(1)} %constant_dynamic-slice_fusion.1), channel_id=1, source_target_pairs={{0,1},{1,0},{2,3},{3,2},{4,5},{5,4},{6,7},{7,6},{8,9},{9,8},{10,11... | collective-permute-start | bytes 2359304 | tf_op jit(solution)/shard_map/ppermute | solution.py:105
  52.0 8.8 %collective-permute-start.13 = (bf16[64,2048]{1,0:T(8,128)(2,1)S(1)}, bf16[64,2048]{1,0:T(8,128)(2,1)S(1)}, u32[]{:S(2)}, u32[]{:S(2)}) collective-permute-start(bf16[64,2048]{1,0:T(8,128)(2,1)S(1)} %get-tuple-element.29), channel_id=1, source_target_pairs={{0,2},{1,3},{2,0},{3,1},{4,6},{5,7},{6,4},{7,5},{8,10},{9,11},{10,... | collective-permute-start | bytes 786440 | tf_op jit(solution)/shard_map/ppermute | solution.py:105
  53.9 7.1 %collective-permute-start.15 = (bf16[3,64,2048]{2,1,0:T(8,128)(2,1)S(1)}, bf16[3,64,2048]{2,1,0:T(8,128)(2,1)S(1)}, u32[]{:S(2)}, u32[]{:S(2)}) collective-permute-start(bf16[3,64,2048]{2,1,0:T(8,128)(2,1)S(1)} %constant_dynamic-slice_fusion), channel_id=1, source_target_pairs={{0,1},{1,0},{2,3},{3,2},{4,5},{5,4},{6,7},{7,6},{8,9},{9,8},{10,11... | collective-permute-start | bytes 2359304 | tf_op jit(solution)/shard_map/ppermute | solution.py:105
  63.0 9.7 %collective-permute-start.16 = (bf16[384,384]{1,0:T(8,128)(2,1)S(1)}, bf16[384,384]{1,0:T(8,128)(2,1)S(1)}, u32[]{:S(2)}, u32[]{:S(2)}) collective-permute-start(bf16[384,384]{1,0:T(8,128)(2,1)S(1)} %get-tuple-element.24), channel_id=1, source_target_pairs={{0,4},{1,5},{2,6},{3,7},{4,0},{5,1},{6,2},{7,3},{8,12},{9,13},{10,... | collective-permute-start | bytes 884744 | tf_op jit(solution)/shard_map/ppermute | solution.py:105
  64.3 9.5 %collective-permute-start.19 = (bf16[128,384]{1,0:T(8,128)(2,1)S(1)}, bf16[128,384]{1,0:T(8,128)(2,1)S(1)}, u32[]{:S(2)}, u32[]{:S(2)}) collective-permute-start(bf16[128,384]{1,0:T(8,128)(2,1)S(1)} %get-tuple-element.34), channel_id=1, source_target_pairs={{0,4},{1,5},{2,6},{3,7},{4,0},{5,1},{6,2},{7,3},{8,12},{9,13},{10,... | collective-permute-start | bytes 294920 | tf_op jit(solution)/shard_map/ppermute | solution.py:105
  72.8 2.5 %collective-permute-start.20 = (bf16[768,256]{1,0:T(8,128)(2,1)S(1)}, bf16[768,256]{1,0:T(8,128)(2,1)S(1)}, u32[]{:S(2)}, u32[]{:S(2)}) collective-permute-start(bf16[768,256]{1,0:T(8,128)(2,1)S(1)} %pad_maximum_fusion.13), channel_id=1, source_target_pairs={{0,1},{1,0},{2,3},{3,2},{4,5},{5,4},{6,7},{7,6},{8,9},{9,8},{10,11... | collective-permute-start | bytes 1179656 | tf_op jit(solution)/shard_map/ppermute | solution.py:105
  73.8 1.4 %collective-permute-start.21 = (bf16[256,256]{1,0:T(8,128)(2,1)S(1)}, bf16[256,256]{1,0:T(8,128)(2,1)S(1)}, u32[]{:S(2)}, u32[]{:S(2)}) collective-permute-start(bf16[256,256]{1,0:T(8,128)(2,1)S(1)} %pad_maximum_fusion.15), channel_id=1, source_target_pairs={{0,1},{1,0},{2,3},{3,2},{4,5},{5,4},{6,7},{7,6},{8,9},{9,8},{10,11... | collective-permute-start | bytes 393224 | tf_op jit(solution)/shard_map/ppermute | solution.py:105
  (1 other events, 13.3 us)
